TPU v7x, 32 devices: a whole 2x2x4 slice. The times are simulated.
32 devices in a mesh: groups: 2 (over y), resi: 4 (over z), resj: 2 (over core), seq: 2 (over x).
Axes of the slice: x: 2, y: 2, z: 4, core: 2. Of those that a mesh axis runs over, the one named last changes fastest.
Arguments:
- homolog_matrix: bfloat16 [256, 128, 256], P(('groups', 'resj', 'seq'), 'resi'), parts along dimension 0, may hold values from -6 to 6
- sequence_pad_mask: int32 [256, 128], P(('groups', 'resj', 'seq'), 'resi'), parts along dimension 0, may hold values 0 or 1
- pair_features: bfloat16 [256, 128, 128], P(('groups', 'resi'), ('resj', 'seq')), parts along dimension 0, may hold values from -6 to 6
- residue_pad_mask: int32 [256], P('groups'), parts along dimension 0, may hold values 0 or 1
- residue_chain_index: int32 [256], P('groups'), parts along dimension 0, may hold values from 0 to 3, never falling along the last dimension, each value on 1 to 64 neighbouring positions
- homolog_standard_factor: float32 [256], replicated, may hold values from 0.5 to 1.5
- homolog_standard_offset: float32 [256], replicated, may hold values from -0.3 to 0.3
- factor_mapping_matrices: bfloat16 [256, 64], replicated, may hold values from -0.375 to 0.375
- outer_side_biases: float32 [64], replicated, may hold values from -0.3 to 0.3
- outer_pair_projection: bfloat16 [1024, 128], replicated, may hold values from -2.390625 to 2.390625
- relative_position_table: bfloat16 [66, 128], replicated, may hold values from -3 to 3
- pair_norm_gain: float32 [128], replicated, may hold values from 0.5 to 1.5
- pair_norm_bias: float32 [128], replicated, may hold values from -3 to 3
- triangle_projection_weights: bfloat16 [128, 640], replicated, may hold values from -0.5 to 0.5
- triangle_projection_biases: float32 [640], replicated, may hold values from -2 to 2
- triangle_sum_norm_gain: float32 [128], replicated, may hold values from 0.5 to 1.5
- triangle_sum_norm_bias: float32 [128], replicated, may hold values from -3 to 3
- triangle_output_weight: bfloat16 [128, 128], replicated, may hold values from -0.5 to 0.5
- outer_pair_bias: float32 [128], replicated, may hold values from -3 to 3
Outputs:
- new_pair: bfloat16 [256, 128, 128], P(('groups', 'resi'), ('resj', 'seq')), parts along dimension 0
There are 2 independent parts, one for each index of `groups`. A program takes and returns all parts, laid end to end along the dimension named above; an argument that names none is the same for every part. Nothing has to cross between parts.
Inputs may be any that keep to these rules, and one draw needn't show every extreme that they name: residue_chain_index never falls along the residues; each chain holds 1 to 64 residues, one exactly 64.
All inputs are finite; a program needn't handle non-finite values. No bound on the sum of `sequence_pad_mask` on one device may be relied on, other than what follows from the above.
Results may differ from a plain program's by a relative error of at most 0.0085.
Values may be sent and summed in bfloat16 or wider, within the bound.
No kernel may reach another device: no remote copies, remote signals or barrier semaphores. Data moves between devices by JAX's collectives and lax.ppermute only.
A program may use at most 64 MiB of HBM per device.

v0:
```python
import jax
import jax.numpy as jnp
from jax import lax
from jax.sharding import PartitionSpec as P

RELMAX = 32


def broadcast(block, axis, holder):
    block = jnp.where(lax.axis_index(axis) == holder, block, jnp.zeros_like(block))
    return lax.psum(block, axis)


def apply_layer_norm(values, gain_vec, shift_vec):
    average = jnp.mean(values, axis=-1, keepdims=True)
    centred = values - average
    variance = jnp.mean(centred * centred, axis=-1, keepdims=True)
    return centred * lax.rsqrt(variance + 1e-05) * gain_vec + shift_vec


def body(
    homolog_matrix,
    sequence_pad_mask,
    pair_features,
    residue_pad_mask,
    residue_chain_index,
    homolog_standard_factor,
    homolog_standard_offset,
    factor_mapping_matrices,
    outer_side_biases,
    outer_pair_projection,
    relative_position_table,
    pair_norm_gain,
    pair_norm_bias,
    triangle_projection_weights,
    triangle_projection_biases,
    triangle_sum_norm_gain,
    triangle_sum_norm_bias,
    triangle_output_weight,
    outer_pair_bias,
):
    row_count = pair_features.shape[0]
    col_count = pair_features.shape[1]
    channels = pair_features.shape[2]
    seq_local = homolog_matrix.shape[0]
    narrow = factor_mapping_matrices.shape[1] // 2
    row_start = lax.axis_index("resi") * row_count
    col_index = lax.axis_index(("resj", "seq"))
    col_start = col_index * col_count
    residue_live = residue_pad_mask.astype(jnp.float32)
    row_live = lax.dynamic_slice_in_dim(residue_live, row_start, row_count)
    col_live = lax.dynamic_slice_in_dim(residue_live, col_start, col_count)
    seq_live = sequence_pad_mask.astype(jnp.float32) * row_live[None, :]
    standardized_homologs = apply_layer_norm(
        homolog_matrix.astype(jnp.float32), homolog_standard_factor, homolog_standard_offset
    ).astype(jnp.bfloat16)
    mapped_factors = jnp.dot(
        standardized_homologs.reshape(seq_local * row_count, -1),
        factor_mapping_matrices,
        preferred_element_type=jnp.float32,
    )
    mapped_factors = (
        mapped_factors.reshape(seq_local, row_count, 2 * narrow) + outer_side_biases
    ) * seq_live[:, :, None]
    mapped_factors = mapped_factors.astype(jnp.bfloat16)
    live_bf = seq_live.astype(jnp.bfloat16)
    left_rows = (
        mapped_factors[:, :, :narrow].transpose(1, 0, 2).reshape(row_count, seq_local * narrow)
    )
    live_rows = live_bf.T
    right_rows = (
        mapped_factors[:, :, narrow:].transpose(1, 0, 2).reshape(row_count, seq_local * narrow)
    )
    left_all, right_all, live_all = (
        lax.all_gather(left_rows, ("resj", "seq"), axis=1, tiled=True),
        lax.all_gather(right_rows, ("resj", "seq"), axis=1, tiled=True),
        lax.all_gather(live_rows, ("resj", "seq"), axis=1, tiled=True),
    )
    right_cols, live_cols = (
        broadcast(right_all, "resi", col_index),
        broadcast(live_all, "resi", col_index),
    )
    total_seqs = live_all.shape[1]
    products = jnp.einsum(
        "isc,jsd->ijcd",
        left_all.reshape(row_count, total_seqs, narrow),
        right_cols.reshape(col_count, total_seqs, narrow),
        preferred_element_type=jnp.float32,
    )
    counts = jnp.dot(live_all, live_cols.T, preferred_element_type=jnp.float32)
    flattened = products.astype(jnp.bfloat16).reshape(row_count * col_count, narrow * narrow)
    outer_sum = jnp.dot(
        flattened, outer_pair_projection, preferred_element_type=jnp.float32
    ).reshape(row_count, col_count, channels)
    outer_mean = outer_sum / jnp.maximum(counts, 1.0)[:, :, None]
    row_pos = row_start + jnp.arange(row_count, dtype=jnp.int32)
    col_pos = col_start + jnp.arange(col_count, dtype=jnp.int32)
    offsets = jnp.clip(col_pos[None, :] - row_pos[:, None] + RELMAX, 0, 2 * RELMAX)
    chain_rows = lax.dynamic_slice_in_dim(residue_chain_index, row_start, row_count)
    chain_cols = lax.dynamic_slice_in_dim(residue_chain_index, col_start, col_count)
    same_chain = chain_rows[:, None] == chain_cols[None, :]
    bin_index = jnp.where(same_chain, offsets, 2 * RELMAX + 1)
    one_hot = (
        bin_index[:, :, None] == jnp.arange(relative_position_table.shape[0], dtype=jnp.int32)
    ).astype(jnp.bfloat16)
    embedded = jnp.einsum(
        "ijb,bc->ijc", one_hot, relative_position_table, preferred_element_type=jnp.float32
    )
    updated = (pair_features.astype(jnp.float32) + embedded + outer_mean).astype(jnp.bfloat16)
    normed_pair = apply_layer_norm(
        updated.astype(jnp.float32), pair_norm_gain, pair_norm_bias
    ).astype(jnp.bfloat16)
    mixture = jnp.dot(
        normed_pair.reshape(row_count * col_count, channels),
        triangle_projection_weights,
        preferred_element_type=jnp.float32,
    )
    mixture = mixture.reshape(row_count, col_count, 5 * channels) + triangle_projection_biases
    pair_live = (row_live[:, None] * col_live[None, :])[:, :, None]
    left_edge = (
        jax.nn.sigmoid(mixture[:, :, :channels])
        * mixture[:, :, channels : 2 * channels]
        * pair_live
    ).astype(jnp.bfloat16)
    right_edge = (
        jax.nn.sigmoid(mixture[:, :, 2 * channels : 3 * channels])
        * mixture[:, :, 3 * channels : 4 * channels]
        * pair_live
    ).astype(jnp.bfloat16)
    gating = jax.nn.sigmoid(mixture[:, :, 4 * channels :])
    left_panel, right_panel = (
        lax.all_gather(left_edge, ("resj", "seq"), axis=1, tiled=True),
        lax.all_gather(right_edge, ("resj", "seq"), axis=1, tiled=True),
    )
    right_match = broadcast(right_panel, "resi", col_index)
    triangle = jnp.einsum(
        "ikc,jkc->ijc", left_panel, right_match, preferred_element_type=jnp.float32
    )
    normed_tri = apply_layer_norm(triangle, triangle_sum_norm_gain, triangle_sum_norm_bias).astype(
        jnp.bfloat16
    )
    result = jnp.dot(
        normed_tri.reshape(row_count * col_count, channels),
        triangle_output_weight,
        preferred_element_type=jnp.float32,
    )
    result = result.reshape(row_count, col_count, channels) + outer_pair_bias
    return (updated.astype(jnp.float32) + gating * result).astype(jnp.bfloat16)


def solution(mesh):
    placed = (
        P(("groups", "resj", "seq"), "resi", None),
        P(("groups", "resj", "seq"), "resi"),
        P(("groups", "resi"), ("resj", "seq"), None),
        P("groups"),
        P("groups"),
        P(),
        P(),
        P(),
        P(),
        P(),
        P(),
        P(),
        P(),
        P(),
        P(),
        P(),
        P(),
        P(),
        P(),
    )
    return jax.shard_map(
        body,
        mesh=mesh,
        in_specs=placed,
        out_specs=P(("groups", "resi"), ("resj", "seq"), None),
        check_vma=False,
    )
```

profile of v0, /device:TPU:1, one launch (start us, length us, event | category | flops | bytes accessed | tf_op | source)
XLA Modules:
  0.0 209.1 jit_solution(10508211096695731784)
XLA Ops:
  6.5 0.7 convert_element_type.54
  7.2 1.2 convert_reduce_fusion
  8.5 1.4 fusion.10
  10.0 0.8 convert_bitcast_fusion.1
  10.8 1.6 fusion.7
  12.6 0.3 reshape.168
  12.9 10.8 %all_gather.15 = bf16[32,4096]{1,0:T(8,128)(2,1)S(1)} all-gather(bf16[32,1024]{1,0:T(8,128)(2,1)S(1)} %reshape.168), channel_id=1, replica_groups=mesh['groups'=2,'resi'=4,'resj'=2,'seq'=2] {'resj','seq'}, dimensions={1}, use_global_device_ids=true | all-gather | bytes 327680 | tf_op jit(solution)/shard_map/all_gather | solution.py:76
  23.8 0.8 reshape.169
  24.6 1.0 copy.60
  26.1 9.9 %all_gather.17 = bf16[32,128]{0,1:T(8,128)(2,1)S(1)} all-gather(bf16[32,32]{0,1:T(8,128)(2,1)S(1)} %get-tuple-element.5), channel_id=1, replica_groups=mesh['groups'=2,'resi'=4,'resj'=2,'seq'=2] {'resj','seq'}, dimensions={1}, use_global_device_ids=true | all-gather | bytes 10240 | tf_op jit(solution)/shard_map/all_gather | solution.py:77
  36.1 10.7 %all_gather.16 = bf16[32,4096]{1,0:T(8,128)(2,1)S(1)} all-gather(bf16[32,1024]{1,0:T(8,128)(2,1)S(1)} %reshape.170), channel_id=1, replica_groups=mesh['groups'=2,'resi'=4,'resj'=2,'seq'=2] {'resj','seq'}, dimensions={1}, use_global_device_ids=true | all-gather | bytes 327680 | tf_op jit(solution)/shard_map/all_gather | solution.py:75
  46.8 0.8 reshape.171
  47.6 16.2 %psum.22 = bf16[32,128]{0,1:T(8,128)(2,1)S(1)} all-reduce(bf16[32,128]{0,1:T(8,128)(2,1)S(1)} %broadcast_select_fusion.2), channel_id=1, replica_groups=mesh['groups'=2,'resi'=4,'resj'=2,'seq'=2] {'resi'}, use_global_device_ids=true, to_apply=%region_3.4 | all-reduce | flops 4096 | bytes 16384 | tf_op jit(solution)/shard_map/psum | solution.py:11
  64.0 6.5 %convert_bitcast_fusion = bf16[32,32,32,32]{2,3,0,1:T(8,128)(2,1)} fusion(bf16[32,128,32]{2,1,0:T(8,128)(2,1)S(1)} %reshape.171, bf16[32,128,32]{1,2,0:T(8,128)(2,1)} %all-reduce.3.cloned.1.call-done), kind=kOutput, calls=%fused_computation | convolution fusion | flops 269484032 | bytes 2621440 | tf_op jit(solution)/shard_map/isc,jsd->ijcd/dot_general | solution.py:84
  70.5 12.0 %copy.63 = bf16[32,32,32,32]{3,2,1,0:T(8,128)(2,1)} copy(bf16[32,32,32,32]{2,3,0,1:T(8,128)(2,1)} %convert_bitcast_fusion) | data formatting | bytes 4194304 | tf_op jit(solution)/shard_map/convert_element_type | solution.py:91
  82.5 11.3 %dot_general.29 = bf16[32,32,1024]{2,1,0:T(8,128)(2,1)S(1)} reshape(bf16[32,32,32,32]{3,2,1,0:T(8,128)(2,1)} %copy.63) | data formatting | bytes 4194304 | tf_op jit(solution)/shard_map/dot_general | solution.py:92
  93.9 0.7 convolution_divide_fusion
  94.8 0.7 fusion.50
  95.6 0.4 multiply_reduce_fusion.1
  96.0 0.6 convolution_add_fusion
  96.6 1.1 fusion.17
  97.8 0.7 all-gather.5.cloned.1.call-update
  98.7 17.8 %all-gather.3.cloned.1.call-done = bf16[32,128,128]{2,1,0:T(8,128)(2,1)} async-done(((bf16[32,32,128]{2,1,0:T(8,128)(2,1)}), bf16[32,128,128]{2,1,0:T(8,128)(2,1)}) %all-gather.3.cloned.1.call-update) | async-done | bytes 1048592 | tf_op jit(solution)/shard_map/all_gather | solution.py:133
  116.5 1.1 broadcast_select_fusion
  117.6 17.3 %all-gather.5.cloned.1.call-done = bf16[32,128,128]{2,1,0:T(8,128)(2,1)} async-done(((bf16[32,32,128]{2,1,0:T(8,128)(2,1)}), bf16[32,128,128]{2,1,0:T(8,128)(2,1)}) %all-gather.5.cloned.1.call-update) | async-done | bytes 1048592 | tf_op jit(solution)/shard_map/all_gather | solution.py:132
  134.9 2.7 %copy.65 = bf16[32,128,128]{1,0,2:T(8,128)(2,1)} copy(bf16[32,128,128]{2,1,0:T(8,128)(2,1)} %all-gather.5.cloned.1.call-done) | data formatting | bytes 2097152 | tf_op jit(solution)/shard_map/all_gather | solution.py:132
  137.6 51.3 %all-reduce.5.cloned.1.call-done = bf16[32,128,128]{2,1,0:T(8,128)(2,1)} async-done(((bf16[32,128,128]{2,1,0:T(8,128)(2,1)}), bf16[32,128,128]{2,1,0:T(8,128)(2,1)}) %all-reduce.5.cloned.1.call-update) | async-done | bytes 1048592 | tf_op jit(solution)/shard_map/psum | solution.py:11
  188.9 2.7 %copy.64 = bf16[32,128,128]{1,0,2:T(8,128)(2,1)} copy(bf16[32,128,128]{2,1,0:T(8,128)(2,1)} %all-reduce.5.cloned.1.call-done) | data formatting | bytes 2097152 | tf_op jit(solution)/shard_map/psum | solution.py:11
  191.6 3.5 %bitcast_reduce_fusion = (f32[32,32]{0,1:T(8,128)S(1)}, f32[128,32,32]{2,1,0:T(8,128)}) fusion(bf16[32,128,128]{1,0,2:T(8,128)(2,1)} %copy.64, bf16[32,128,128]{1,0,2:T(8,128)(2,1)} %copy.65), kind=kOutput, calls=%fused_computation.1 | convolution fusion | flops 33684480 | bytes 2625536 | tf_op jit(solution)/shard_map/ikc,jkc->ijc/dot_general | solution.py:136
  195.2 3.6 %copy.66 = f32[128,32,32]{0,1,2:T(8,128)} copy(f32[128,32,32]{2,1,0:T(8,128)} %get-tuple-element.19) | data formatting | bytes 1048576 | tf_op jit(solution)/shard_map/ikc,jkc->ijc/dot_general | solution.py:136
  198.9 1.4 multiply_reduce_fusion
  200.3 2.2 %fusion.6 = bf16[32,32,128]{2,1,0:T(8,128)(2,1)} fusion(f32[32,32,128]{2,1,0:T(8,128)S(1)} %get-tuple-element.17, f32[32,32,640]{2,1,0:T(8,128)S(1)} %convolution_add_fusion, f32[128,32,32]{0,1,2:T(8,128)} %copy.66, f32[128]{0:T(128)S(1)} %copy-done.9, f32[128]{0:T(128)S(1)} %copy-done.10, f32[128]{0:T(128)S(1)} %copy-done.11, ...), kind=kOutput, calls=%fused_computation.15 | convolution fusion | flops 35127296 | bytes 1877504 | tf_op jit(solution)/shard_map/dot_general | solution.py:142
  (49 shorter events, 1.8 us)
Async XLA Ops:
  6.5 87.3 %copy-start = (bf16[1024,128]{1,0:T(8,128)(2,1)S(1)}, bf16[1024,128]{1,0:T(8,128)(2,1)}, u32[]{:S(2)}) copy-start(bf16[1024,128]{1,0:T(8,128)(2,1)} %param.28) | copy-start | bytes 786436
  6.5 57.5 %all-reduce.3.cloned.1.call-start = ((), (), s32[]{:S(2)}) async-start(), calls=%async_computation | async-start | bytes 524288 | tf_op jit(solution)/shard_map/psum | solution.py:11
  12.6 23.3 %copy-start.5 = (s32[128]{0:T(128)S(1)}, s32[128]{0:T(128)}, u32[]{:S(2)}) copy-start(s32[128]{0:T(128)} %param.23) | copy-start | bytes 1540
  25.6 90.9 %all-gather.3.cloned.1.call-start = ((), (), s32[]{:S(2)}) async-start(), calls=%async_computation.1 | async-start | bytes 1310720 | tf_op jit(solution)/shard_map/all_gather | solution.py:133
  93.9 1.0 copy-start.1
  93.9 0.9 copy-start.3
  93.9 2.1 copy-start.2
  93.9 2.1 copy-start.4
  93.9 2.1 copy-start.6
  93.9 2.1 copy-start.7
  97.7 37.2 %all-gather.5.cloned.1.call-start = ((), (), s32[]{:S(2)}) async-start(), calls=%async_computation.3 | async-start | bytes 1310720 | tf_op jit(solution)/shard_map/all_gather | solution.py:132
  98.5 90.5 %all-reduce.5.cloned.1.call-start = ((), (), s32[]{:S(2)}) async-start(), calls=%async_computation.2 | async-start | bytes 2097152 | tf_op jit(solution)/shard_map/psum | solution.py:11
  195.1 5.2 %copy-start.8 = (bf16[128,128]{1,0:T(8,128)(2,1)S(1)}, bf16[128,128]{1,0:T(8,128)(2,1)}, u32[]{:S(2)}) copy-start(bf16[128,128]{1,0:T(8,128)(2,1)} %param.36) | copy-start | bytes 98308
  195.1 5.2 %copy-start.9 = (f32[128]{0:T(128)S(1)}, f32[128]{0:T(128)}, u32[]{:S(2)}) copy-start(f32[128]{0:T(128)} %param.37) | copy-start | bytes 1540
  195.1 5.2 %copy-start.10 = (f32[128]{0:T(128)S(1)}, f32[128]{0:T(128)}, u32[]{:S(2)}) copy-start(f32[128]{0:T(128)} %param.35) | copy-start | bytes 1540
  195.1 5.2 %copy-start.11 = (f32[128]{0:T(128)S(1)}, f32[128]{0:T(128)}, u32[]{:S(2)}) copy-start(f32[128]{0:T(128)} %param.34) | copy-start | bytes 1540
Sparse Core Ops, SparseCore 0:
  25.7 35.8 all-reduce.2
  97.8 18.6 all-gather.2
  118.2 16.7 all-gather.4
  137.3 51.6 all-reduce.4
where the time goes:
time: 211 us; the launch traced here: 209 us
  waiting for transfers between devices  87.2 us (41%)
  blocking collectives  47.6 us (23%)
  local copies, waits for them, and re-layouts  36.3 us (17%)
  matrix products  16 us (8%)
  between operations  13.4 us (6%)
  other arithmetic  8.24 us (4%)
    psum x2, waiting for transfers between devices, broadcast(): return lax.psum(block, axis)  51.3 us
    all_gather x1, waiting for transfers between devices, body(): lax.all_gather(right_edge, ('resj', 'seq'), axis=1, tiled=True)  17.8 us
    all_gather x1, waiting for transfers between devices, body(): lax.all_gather(left_edge, ('resj', 'seq'), axis=1, tiled=True)  17.3 us
    psum x1, blocking collectives, broadcast(): return lax.psum(block, axis)  16.2 us
    convert_element_type x1, local copies, waits for them, and re-layouts, body(): products.astype(jnp.bfloat16)  12 us
    dot_general x1, local copies, waits for them, and re-layouts, body(): jnp.dot(flattened, outer_pair_projection, preferred_element_type=jnp.floa...  11.3 us
    all_gather x1, blocking collectives, body(): lax.all_gather(right_rows, ('resj', 'seq'), axis=1, tiled=True)  10.8 us
    all_gather x1, blocking collectives, body(): lax.all_gather(left_rows, ('resj', 'seq'), axis=1, tiled=True)  10.7 us
  transfers between devices with their start and end apart: 4, of which 3 were waited for; matrix products, arithmetic and copies ran while one was open for 3% of the time, Pallas kernels for 0%

commit v1 on v0

--- a/solution.py
+++ b/solution.py
@@ -6,9 +6,29 @@
 RELMAX = 32
 
 
-def broadcast(block, axis, holder):
-    block = jnp.where(lax.axis_index(axis) == holder, block, jnp.zeros_like(block))
-    return lax.psum(block, axis)
+PLANE = ("resj", "seq")
+GROUP = ("resi", "resj", "seq")
+
+
+def gather_plane(block, count):
+    me = lax.axis_index(PLANE)
+    parts = [block]
+    for step in range(1, count):
+        parts.append(lax.ppermute(block, PLANE, [(p, p ^ step) for p in range(count)]))
+    stacked = jnp.stack(parts)
+    return jnp.stack([lax.dynamic_index_in_dim(stacked, b ^ me, 0, False) for b in range(count)])
+
+
+def gather_turned(block, count):
+    me = lax.axis_index("resi")
+    parts = []
+    for step in range(count):
+        pairs = [
+            (z * count + p, (p ^ step) * count + z) for z in range(count) for p in range(count)
+        ]
+        parts.append(lax.ppermute(block, GROUP, pairs))
+    stacked = jnp.stack(parts)
+    return jnp.stack([lax.dynamic_index_in_dim(stacked, b ^ me, 0, False) for b in range(count)])
 
 
 def apply_layer_norm(values, gain_vec, shift_vec):
@@ -64,30 +84,25 @@
     ) * seq_live[:, :, None]
     mapped_factors = mapped_factors.astype(jnp.bfloat16)
     live_bf = seq_live.astype(jnp.bfloat16)
-    left_rows = (
-        mapped_factors[:, :, :narrow].transpose(1, 0, 2).reshape(row_count, seq_local * narrow)
+    count = lax.axis_size(PLANE)
+    left_pack = jnp.concatenate(
+        [mapped_factors[:, :, :narrow].reshape(seq_local, row_count * narrow), live_bf], axis=1
     )
-    live_rows = live_bf.T
-    right_rows = (
-        mapped_factors[:, :, narrow:].transpose(1, 0, 2).reshape(row_count, seq_local * narrow)
+    right_pack = jnp.concatenate(
+        [mapped_factors[:, :, narrow:].reshape(seq_local, row_count * narrow), live_bf], axis=1
     )
-    left_all, right_all, live_all = (
-        lax.all_gather(left_rows, ("resj", "seq"), axis=1, tiled=True),
-        lax.all_gather(right_rows, ("resj", "seq"), axis=1, tiled=True),
-        lax.all_gather(live_rows, ("resj", "seq"), axis=1, tiled=True),
-    )
-    right_cols, live_cols = (
-        broadcast(right_all, "resi", col_index),
-        broadcast(live_all, "resi", col_index),
-    )
-    total_seqs = live_all.shape[1]
+    left_all = gather_plane(left_pack, count).reshape(count * seq_local, -1)
+    right_all = gather_turned(right_pack, count).reshape(count * seq_local, -1)
+    wide = row_count * narrow
+    live_all, live_cols = left_all[:, wide:], right_all[:, wide:]
+    total_seqs = count * seq_local
     products = jnp.einsum(
-        "isc,jsd->ijcd",
-        left_all.reshape(row_count, total_seqs, narrow),
-        right_cols.reshape(col_count, total_seqs, narrow),
+        "sic,sjd->ijcd",
+        left_all[:, :wide].reshape(total_seqs, row_count, narrow),
+        right_all[:, :wide].reshape(total_seqs, col_count, narrow),
         preferred_element_type=jnp.float32,
     )
-    counts = jnp.dot(live_all, live_cols.T, preferred_element_type=jnp.float32)
+    counts = jnp.dot(live_all.T, live_cols, preferred_element_type=jnp.float32)
     flattened = products.astype(jnp.bfloat16).reshape(row_count * col_count, narrow * narrow)
     outer_sum = jnp.dot(
         flattened, outer_pair_projection, preferred_element_type=jnp.float32
@@ -128,13 +143,10 @@
         * pair_live
     ).astype(jnp.bfloat16)
     gating = jax.nn.sigmoid(mixture[:, :, 4 * channels :])
-    left_panel, right_panel = (
-        lax.all_gather(left_edge, ("resj", "seq"), axis=1, tiled=True),
-        lax.all_gather(right_edge, ("resj", "seq"), axis=1, tiled=True),
-    )
-    right_match = broadcast(right_panel, "resi", col_index)
+    left_panel = gather_plane(left_edge, count)
+    right_match = gather_turned(right_edge, count)
     triangle = jnp.einsum(
-        "ikc,jkc->ijc", left_panel, right_match, preferred_element_type=jnp.float32
+        "bikc,bjkc->ijc", left_panel, right_match, preferred_element_type=jnp.float32
     )
     normed_tri = apply_layer_norm(triangle, triangle_sum_norm_gain, triangle_sum_norm_bias).astype(
         jnp.bfloat16

time: 211 us -> 116 us (0.55)
  waiting for transfers between devices: 87.2 us -> 17 us
  blocking collectives: 47.6 us -> 0 us
  starting transfers between devices: 0.3 us -> 25.7 us
  between operations: 13.4 us -> 0.4 us
  local copies, waits for them, and re-layouts: 36.3 us -> 44 us
  other arithmetic: 8.24 us -> 10.4 us
    psum x2 -> x0, waiting for transfers between devices: 51.3 us -> none  [broadcast(): return lax.psum(block, axis)]
    all_gather x2 -> x0, waiting for transfers between devices: 35.2 us -> none  [the longest x1 17.8 us: body(): lax.all_gather(right_edge, ('resj', 'seq'), axis=1, tiled=True)]
    all_gather x3 -> x0, blocking collectives: 31.4 us -> none  [the longest x1 10.8 us: body(): lax.all_gather(right_rows, ('resj', 'seq'), axis=1, tiled=True)]
    ppermute x0 -> x14, starting transfers between devices: none -> 25.7 us  [the longest x8 19.4 us: gather_turned(): parts.append(lax.ppermute(block, GROUP, pairs))]
    ppermute x0 -> x14, waiting for transfers between devices: none -> 17 us  [the longest x8 11.5 us: gather_turned(): parts.append(lax.ppermute(block, GROUP, pairs))]
    psum x1 -> x0, blocking collectives: 16.2 us -> none  [broadcast(): return lax.psum(block, axis)]
    another operation x0 -> x2, local copies, waits for them, and re-layouts: none -> 14.5 us  [the longest x1 7.24 us: gather_turned(): jnp.stack([lax.dynamic_index_in_dim(stacked, b ^ me, 0, False) for b in r...]
    another operation x0 -> x9, other arithmetic: none -> 4 us  [the longest x2 2.44 us: gather_plane(): jnp.stack([lax.dynamic_index_in_dim(stacked, b ^ me, 0, False) for b in r...]
  transfers between devices with their start and end apart: 4 -> 14, of which waited for: 3 -> 6; matrix products, arithmetic and copies ran while one was open for 3% -> 1% of each run, Pallas kernels for 0% -> 0%
where the time goes in v1:
time: 116 us; the launch traced here: 115 us
  local copies, waits for them, and re-layouts  44 us (38%)
  starting transfers between devices  25.7 us (22%)
  matrix products  17.7 us (15%)
  waiting for transfers between devices  17 us (15%)
  other arithmetic  10.4 us (9%)
    ppermute x8, starting transfers between devices, gather_turned(): parts.append(lax.ppermute(block, GROUP, pairs))  19.4 us
    convert_element_type x1, local copies, waits for them, and re-layouts, body(): products.astype(jnp.bfloat16)  11.9 us
    ppermute x8, waiting for transfers between devices, gather_turned(): parts.append(lax.ppermute(block, GROUP, pairs))  11.5 us
    dot_general x1, local copies, waits for them, and re-layouts, body(): jnp.dot(flattened, outer_pair_projection, preferred_element_type=jnp.floa...  11.3 us
    another operation x1, local copies, waits for them, and re-layouts, gather_turned(): jnp.stack([lax.dynamic_index_in_dim(stacked, b ^ me, 0, False) for b in r...  7.24 us
    another operation x1, local copies, waits for them, and re-layouts, gather_plane(): jnp.stack([lax.dynamic_index_in_dim(stacked, b ^ me, 0, False) for b in r...  7.23 us
    ppermute x6, starting transfers between devices, gather_plane(): lax.ppermute(block, PLANE, [(p, p ^ step) for p in range(count)])  6.3 us
    dot_general x1, matrix products, body(): jnp.einsum('bikc,bjkc->ijc', left_panel, right_match, preferred_element_t...  6.13 us
  transfers between devices with their start and end apart: 14, of which 6 were waited for; matrix products, arithmetic and copies ran while one was open for 1% of the time, Pallas kernels for 0%

profile of v1, /device:TPU:1, one launch (start us, length us, event | category | flops | bytes accessed | tf_op | source)
XLA Modules:
  0.0 115.1 jit_solution(8287065500303910356)
XLA Ops:
  0.7 1.2 %convert_reduce_fusion = f32[32,32]{1,0:T(8,128)S(1)} fusion(bf16[32,32,256]{2,1,0:T(8,128)(2,1)} %param.19), kind=kLoop, calls=%fused_computation.4 | loop fusion | flops 523264 | bytes 528384 | tf_op jit(solution)/shard_map/reduce_sum | solution.py:35
  2.0 1.4 %fusion.10 = f32[32,32]{1,0:T(8,128)S(1)} fusion(bf16[32,32,256]{2,1,0:T(8,128)(2,1)} %param.19, f32[32,32]{1,0:T(8,128)S(1)} %broadcast_multiply_fusion.3), kind=kLoop, calls=%fused_computation.20 | loop fusion | flops 1047552 | bytes 532480 | tf_op jit(solution)/shard_map/reduce_sum | solution.py:37
  3.5 0.8 fusion.49
  4.3 1.6 %fusion.7 = bf16[32,32,64]{2,1,0:T(8,128)(2,1)S(1)} fusion(bf16[32,32,256]{2,1,0:T(8,128)(2,1)} %param.19, f32[256]{0:T(256)} %param.25, f32[256]{0:T(256)} %param.24, f32[32,32]{1,0:T(8,128)S(1)} %get-tuple-element.39, f32[32,32]{1,0:T(8,128)S(1)} %broadcast_multiply_fusion.3, f32[32,32]{1,0:T(8,128)S(1)} %get-tuple-element.6, f32[64]{0:T(128)} %param.27, ...), kind=kOutput, calls=%fused_computation.16 | convolution fusion | flops 35323904 | bytes 702720 | tf_op jit(solution)/shard_map/dot_general | solution.py:77
  6.7 2.7 %collective-permute-start.4 = (bf16[32,1056]{1,0:T(8,128)(2,1)S(1)}, bf16[32,1056]{1,0:T(8,128)(2,1)S(1)}, u32[]{:S(2)}, u32[]{:S(2)}) collective-permute-start(bf16[32,1056]{1,0:T(8,128)(2,1)S(1)} %get-tuple-element.28), channel_id=1, source_target_pairs={{0,1},{1,0},{2,3},{3,2},{4,5},{5,4},{6,7},{7,6},{8,9},{9,8},{10,11... | collective-permute-start | bytes 202760 | tf_op jit(solution)/shard_map/ppermute | solution.py:17
  9.4 1.8 %collective-permute-start.3 = (bf16[32,1056]{1,0:T(8,128)(2,1)S(1)}, bf16[32,1056]{1,0:T(8,128)(2,1)S(1)}, u32[]{:S(2)}, u32[]{:S(2)}) collective-permute-start(bf16[32,1056]{1,0:T(8,128)(2,1)S(1)} %get-tuple-element.29), channel_id=1, source_target_pairs={{0,12},{1,8},{2,4},{3,0},{4,13},{5,9},{6,5},{7,1},{8,14},{9,10},{1... | collective-permute-start | bytes 202760 | tf_op jit(solution)/shard_map/ppermute | solution.py:29
  11.2 2.4 %collective-permute-start.2 = (bf16[32,1056]{1,0:T(8,128)(2,1)S(1)}, bf16[32,1056]{1,0:T(8,128)(2,1)S(1)}, u32[]{:S(2)}, u32[]{:S(2)}) collective-permute-start(bf16[32,1056]{1,0:T(8,128)(2,1)S(1)} %get-tuple-element.29), channel_id=1, source_target_pairs={{0,8},{1,12},{2,0},{3,4},{4,9},{5,13},{6,1},{7,5},{8,10},{9,14},{1... | collective-permute-start | bytes 202760 | tf_op jit(solution)/shard_map/ppermute | solution.py:29
  13.8 1.1 collective-permute-start.1
  14.9 3.5 %collective-permute-start = (bf16[32,1056]{1,0:T(8,128)(2,1)S(1)}, bf16[32,1056]{1,0:T(8,128)(2,1)S(1)}, u32[]{:S(2)}, u32[]{:S(2)}) collective-permute-start(bf16[32,1056]{1,0:T(8,128)(2,1)S(1)} %get-tuple-element.29), channel_id=1, source_target_pairs={{0,0},{1,4},{2,8},{3,12},{4,1},{5,5},{6,9},{7,13},{8,2},{9,6},{10,... | collective-permute-start | bytes 202760 | tf_op jit(solution)/shard_map/ppermute | solution.py:29
  18.7 0.8 collective-permute-done.1
  19.5 2.1 %collective-permute-done = bf16[32,1056]{1,0:T(8,128)(2,1)S(1)} collective-permute-done((bf16[32,1056]{1,0:T(8,128)(2,1)S(1)}, bf16[32,1056]{1,0:T(8,128)(2,1)S(1)}, u32[]{:S(2)}, u32[]{:S(2)}) %collective-permute-start) | collective-permute-done | bytes 67616 | tf_op jit(solution)/shard_map/ppermute | solution.py:29
  22.2 5.6 %convert_bitcast_fusion = bf16[32,32,32,32]{2,3,0,1:T(8,128)(2,1)} fusion(bf16[128,32,32,1]{0,2,3,1:T(8,128)(2,1)S(1)} %bitcast.70, bf16[128,32,32,1]{0,2,1,3:T(8,128)(2,1)S(1)} %bitcast.71), kind=kOutput, calls=%fused_computation | convolution fusion | flops 269484032 | bytes 2621440 | tf_op jit(solution)/shard_map/sic,sjd->ijcd/dot_general | solution.py:99
  27.8 11.9 %copy.57 = bf16[32,32,32,32]{3,2,1,0:T(8,128)(2,1)} copy(bf16[32,32,32,32]{2,3,0,1:T(8,128)(2,1)} %convert_bitcast_fusion) | data formatting | bytes 4194304 | tf_op jit(solution)/shard_map/convert_element_type | solution.py:106
  39.8 11.3 %dot_general.29 = bf16[32,32,1024]{2,1,0:T(8,128)(2,1)S(1)} reshape(bf16[32,32,32,32]{3,2,1,0:T(8,128)(2,1)} %copy.57) | data formatting | bytes 4194304 | tf_op jit(solution)/shard_map/dot_general | solution.py:107
  54.2 2.6 %collective-permute-start.13 = (bf16[32,32,128]{2,1,0:T(8,128)(2,1)S(1)}, bf16[32,32,128]{2,1,0:T(8,128)(2,1)S(1)}, u32[]{:S(2)}, u32[]{:S(2)}) collective-permute-start(bf16[32,32,128]{2,1,0:T(8,128)(2,1)S(1)} %get-tuple-element.7), channel_id=1, source_target_pairs={{0,3},{1,2},{2,1},{3,0},{4,7},{5,6},{6,5},{7,4},{8,11},{9,10},{10,... | collective-permute-start | bytes 786440 | tf_op jit(solution)/shard_map/ppermute | solution.py:17
  56.7 0.9 collective-permute-start.12
  57.6 1.0 collective-permute-start.10
  58.6 2.1 %collective-permute-start.9 = (bf16[32,32,128]{2,1,0:T(8,128)(2,1)S(1)}, bf16[32,32,128]{2,1,0:T(8,128)(2,1)S(1)}, u32[]{:S(2)}, u32[]{:S(2)}) collective-permute-start(bf16[32,32,128]{2,1,0:T(8,128)(2,1)S(1)} %get-tuple-element.8), channel_id=1, source_target_pairs={{0,8},{1,12},{2,0},{3,4},{4,9},{5,13},{6,1},{7,5},{8,10},{9,14},{1... | collective-permute-start | bytes 786440 | tf_op jit(solution)/shard_map/ppermute | solution.py:29
  60.7 5.5 %collective-permute-done.13 = bf16[32,32,128]{2,1,0:T(8,128)(2,1)S(1)} collective-permute-done((bf16[32,32,128]{2,1,0:T(8,128)(2,1)S(1)}, bf16[32,32,128]{2,1,0:T(8,128)(2,1)S(1)}, u32[]{:S(2)}, u32[]{:S(2)}) %collective-permute-start.13) | collective-permute-done | bytes 262176 | tf_op jit(solution)/shard_map/ppermute | solution.py:17
  66.2 5.4 %collective-permute-start.8 = (bf16[32,32,128]{2,1,0:T(8,128)(2,1)S(1)}, bf16[32,32,128]{2,1,0:T(8,128)(2,1)S(1)}, u32[]{:S(2)}, u32[]{:S(2)}) collective-permute-start(bf16[32,32,128]{2,1,0:T(8,128)(2,1)S(1)} %get-tuple-element.8), channel_id=1, source_target_pairs={{0,4},{1,0},{2,12},{3,8},{4,5},{5,1},{6,13},{7,9},{8,6},{9,2},{10,... | collective-permute-start | bytes 786440 | tf_op jit(solution)/shard_map/ppermute | solution.py:29
  71.6 2.1 %collective-permute-start.7 = (bf16[32,32,128]{2,1,0:T(8,128)(2,1)S(1)}, bf16[32,32,128]{2,1,0:T(8,128)(2,1)S(1)}, u32[]{:S(2)}, u32[]{:S(2)}) collective-permute-start(bf16[32,32,128]{2,1,0:T(8,128)(2,1)S(1)} %get-tuple-element.8), channel_id=1, source_target_pairs={{0,0},{1,4},{2,8},{3,12},{4,1},{5,5},{6,9},{7,13},{8,2},{9,6},{10,... | collective-permute-start | bytes 786440 | tf_op jit(solution)/shard_map/ppermute | solution.py:29
  73.8 1.0 constant_dynamic-slice_fusion.3
  74.8 1.0 collective-permute-done.9
  76.2 7.3 %collective-permute-done.7 = bf16[32,32,128]{2,1,0:T(8,128)(2,1)S(1)} collective-permute-done((bf16[32,32,128]{2,1,0:T(8,128)(2,1)S(1)}, bf16[32,32,128]{2,1,0:T(8,128)(2,1)S(1)}, u32[]{:S(2)}, u32[]{:S(2)}) %collective-permute-start.7) | collective-permute-done | bytes 262176 | tf_op jit(solution)/shard_map/ppermute | solution.py:29
  83.7 1.1 pad_maximum_fusion.1
  84.8 7.2 %copy.58 = bf16[4,32,32,128]{2,1,0,3:T(8,128)(2,1)} copy(bf16[4,32,32,128]{3,2,1,0:T(8,128)(2,1)} %pad_maximum_fusion.1) | data formatting | bytes 2097152 | tf_op jit(solution)/shard_map/stack | solution.py:31
  92.0 2.4 %pad_maximum_fusion.3 = bf16[4,32,32,128]{3,2,1,0:T(8,128)(2,1)} fusion(bf16[1,32,32,128]{3,2,1,0:T(8,128)(2,1)} %get-tuple-element.10, bf16[1,32,32,128]{3,2,1,0:T(8,128)(2,1)} %get-tuple-element.11, bf16[1,32,32,128]{3,2,1,0:T(8,128)(2,1)} %get-tuple-element.12, bf16[1,32,32,128]{3,2,1,0:T(8,128)(2,1)} %get-tuple-element.9), kind=kLoop, calls=%fused_computation.27 | loop fusion | flops 1572864 | bytes 2097152 | tf_op jit(solution)/shard_map/stack | solution.py:19
  94.4 7.2 %copy.59 = bf16[4,32,32,128]{2,1,0,3:T(8,128)(2,1)} copy(bf16[4,32,32,128]{3,2,1,0:T(8,128)(2,1)} %pad_maximum_fusion.3) | data formatting | bytes 2097152 | tf_op jit(solution)/shard_map/stack | solution.py:19
  101.6 6.1 %bitcast_reduce_fusion = (f32[32,32]{0,1:T(8,128)S(1)}, f32[128,32,32,1]{2,1,3,0:T(8,128)}) fusion(bf16[4,32,32,128]{2,1,0,3:T(8,128)(2,1)} %copy.58, bf16[4,32,32,128]{2,1,0,3:T(8,128)(2,1)} %copy.59), kind=kOutput, calls=%fused_computation.1 | convolution fusion | flops 33684480 | bytes 2625536 | tf_op jit(solution)/shard_map/bikc,bjkc->ijc/dot_general | solution.py:148
  107.9 3.6 %copy.60 = f32[128,32,32]{0,1,2:T(8,128)} copy(f32[128,32,32]{2,1,0:T(8,128)} %bitcast.65) | data formatting | bytes 1048576 | tf_op jit(solution)/shard_map/bikc,bjkc->ijc/dot_general | solution.py:148
  111.5 1.4 %multiply_reduce_fusion = f32[32,32]{1,0:T(8,128)S(1)} fusion(f32[128,32,32]{0,1,2:T(8,128)} %copy.60, f32[32,32]{1,0:T(8,128)S(1)} %broadcast_multiply_fusion.1), kind=kLoop, calls=%fused_computation.48 | loop fusion | flops 392192 | bytes 532480 | tf_op jit(solution)/shard_map/reduce_sum | solution.py:37
  112.9 2.2 %fusion.6 = bf16[32,32,128]{2,1,0:T(8,128)(2,1)} fusion(f32[32,32,128]{2,1,0:T(8,128)S(1)} %get-tuple-element.36, f32[32,32,640]{2,1,0:T(8,128)S(1)} %convolution_add_fusion, f32[128,32,32]{0,1,2:T(8,128)} %copy.60, f32[128]{0:T(128)S(1)} %copy-done.9, f32[128]{0:T(128)S(1)} %copy-done.10, f32[128]{0:T(128)S(1)} %copy-done.11, ...), kind=kOutput, calls=%fused_computation.15 | convolution fusion | flops 35127296 | bytes 1877504 | tf_op jit(solution)/shard_map/dot_general | solution.py:154
  (70 shorter events, 6.5 us)
Async XLA Ops:
  0.0 51.1 %copy-start = (bf16[1024,128]{1,0:T(8,128)(2,1)S(1)}, bf16[1024,128]{1,0:T(8,128)(2,1)}, u32[]{:S(2)}) copy-start(bf16[1024,128]{1,0:T(8,128)(2,1)} %param.28) | copy-start | bytes 786436
  0.0 13.6 %copy-start.5 = (s32[128]{0:T(128)S(1)}, s32[128]{0:T(128)}, u32[]{:S(2)}) copy-start(s32[128]{0:T(128)} %param.23) | copy-start | bytes 1540
  6.6 7.2 %collective-permute-start.5 = (bf16[32,1056]{1,0:T(8,128)(2,1)S(1)}, bf16[32,1056]{1,0:T(8,128)(2,1)S(1)}, u32[]{:S(2)}, u32[]{:S(2)}) collective-permute-start(bf16[32,1056]{1,0:T(8,128)(2,1)S(1)} %get-tuple-element.28), channel_id=1, source_target_pairs={{0,2},{1,3},{2,0},{3,1},{4,6},{5,7},{6,4},{7,5},{8,10},{9,11},{10,... | collective-permute-start | bytes 202760 | tf_op jit(solution)/shard_map/ppermute | solution.py:17
  6.7 8.2 %collective-permute-start.4 = (bf16[32,1056]{1,0:T(8,128)(2,1)S(1)}, bf16[32,1056]{1,0:T(8,128)(2,1)S(1)}, u32[]{:S(2)}, u32[]{:S(2)}) collective-permute-start(bf16[32,1056]{1,0:T(8,128)(2,1)S(1)} %get-tuple-element.28), channel_id=1, source_target_pairs={{0,1},{1,0},{2,3},{3,2},{4,5},{5,4},{6,7},{7,6},{8,9},{9,8},{10,11... | collective-permute-start | bytes 202760 | tf_op jit(solution)/shard_map/ppermute | solution.py:17
  9.4 9.1 %collective-permute-start.6 = (bf16[32,1056]{1,0:T(8,128)(2,1)S(1)}, bf16[32,1056]{1,0:T(8,128)(2,1)S(1)}, u32[]{:S(2)}, u32[]{:S(2)}) collective-permute-start(bf16[32,1056]{1,0:T(8,128)(2,1)S(1)} %get-tuple-element.28), channel_id=1, source_target_pairs={{0,3},{1,2},{2,1},{3,0},{4,7},{5,6},{6,5},{7,4},{8,11},{9,10},{10,... | collective-permute-start | bytes 202760 | tf_op jit(solution)/shard_map/ppermute | solution.py:17
  9.4 9.2 %collective-permute-start.3 = (bf16[32,1056]{1,0:T(8,128)(2,1)S(1)}, bf16[32,1056]{1,0:T(8,128)(2,1)S(1)}, u32[]{:S(2)}, u32[]{:S(2)}) collective-permute-start(bf16[32,1056]{1,0:T(8,128)(2,1)S(1)} %get-tuple-element.29), channel_id=1, source_target_pairs={{0,12},{1,8},{2,4},{3,0},{4,13},{5,9},{6,5},{7,1},{8,14},{9,10},{1... | collective-permute-start | bytes 202760 | tf_op jit(solution)/shard_map/ppermute | solution.py:29
  11.2 7.5 %collective-permute-start.2 = (bf16[32,1056]{1,0:T(8,128)(2,1)S(1)}, bf16[32,1056]{1,0:T(8,128)(2,1)S(1)}, u32[]{:S(2)}, u32[]{:S(2)}) collective-permute-start(bf16[32,1056]{1,0:T(8,128)(2,1)S(1)} %get-tuple-element.29), channel_id=1, source_target_pairs={{0,8},{1,12},{2,0},{3,4},{4,9},{5,13},{6,1},{7,5},{8,10},{9,14},{1... | collective-permute-start | bytes 202760 | tf_op jit(solution)/shard_map/ppermute | solution.py:29
  13.8 5.7 %collective-permute-start.1 = (bf16[32,1056]{1,0:T(8,128)(2,1)S(1)}, bf16[32,1056]{1,0:T(8,128)(2,1)S(1)}, u32[]{:S(2)}, u32[]{:S(2)}) collective-permute-start(bf16[32,1056]{1,0:T(8,128)(2,1)S(1)} %get-tuple-element.29), channel_id=1, source_target_pairs={{0,4},{1,0},{2,12},{3,8},{4,5},{5,1},{6,13},{7,9},{8,6},{9,2},{10,... | collective-permute-start | bytes 202760 | tf_op jit(solution)/shard_map/ppermute | solution.py:29
  14.9 6.6 %collective-permute-start = (bf16[32,1056]{1,0:T(8,128)(2,1)S(1)}, bf16[32,1056]{1,0:T(8,128)(2,1)S(1)}, u32[]{:S(2)}, u32[]{:S(2)}) collective-permute-start(bf16[32,1056]{1,0:T(8,128)(2,1)S(1)} %get-tuple-element.29), channel_id=1, source_target_pairs={{0,0},{1,4},{2,8},{3,12},{4,1},{5,5},{6,9},{7,13},{8,2},{9,6},{10,... | collective-permute-start | bytes 202760 | tf_op jit(solution)/shard_map/ppermute | solution.py:29
  51.1 1.0 copy-start.1
  51.1 0.9 copy-start.3
  51.1 2.1 %copy-start.2 = (bf16[128,640]{1,0:T(8,128)(2,1)S(1)}, bf16[128,640]{1,0:T(8,128)(2,1)}, u32[]{:S(2)}) copy-start(bf16[128,640]{1,0:T(8,128)(2,1)} %param.32) | copy-start | bytes 491524
  51.1 2.1 %copy-start.4 = (f32[640]{0:T(1024)S(1)}, f32[640]{0:T(1024)}, u32[]{:S(2)}) copy-start(f32[640]{0:T(1024)} %param.33) | copy-start | bytes 7684
  51.2 2.1 %copy-start.6 = (f32[128]{0:T(128)S(1)}, f32[128]{0:T(128)}, u32[]{:S(2)}) copy-start(f32[128]{0:T(128)} %param.31) | copy-start | bytes 1540
  51.2 2.1 %copy-start.7 = (f32[128]{0:T(128)S(1)}, f32[128]{0:T(128)}, u32[]{:S(2)}) copy-start(f32[128]{0:T(128)} %param.30) | copy-start | bytes 1540
  54.2 12.0 %collective-permute-start.13 = (bf16[32,32,128]{2,1,0:T(8,128)(2,1)S(1)}, bf16[32,32,128]{2,1,0:T(8,128)(2,1)S(1)}, u32[]{:S(2)}, u32[]{:S(2)}) collective-permute-start(bf16[32,32,128]{2,1,0:T(8,128)(2,1)S(1)} %get-tuple-element.7), channel_id=1, source_target_pairs={{0,3},{1,2},{2,1},{3,0},{4,7},{5,6},{6,5},{7,4},{8,11},{9,10},{10,... | collective-permute-start | bytes 786440 | tf_op jit(solution)/shard_map/ppermute | solution.py:17
  56.7 14.8 %collective-permute-start.12 = (bf16[32,32,128]{2,1,0:T(8,128)(2,1)S(1)}, bf16[32,32,128]{2,1,0:T(8,128)(2,1)S(1)}, u32[]{:S(2)}, u32[]{:S(2)}) collective-permute-start(bf16[32,32,128]{2,1,0:T(8,128)(2,1)S(1)} %get-tuple-element.7), channel_id=1, source_target_pairs={{0,2},{1,3},{2,0},{3,1},{4,6},{5,7},{6,4},{7,5},{8,10},{9,11},{10,... | collective-permute-start | bytes 786440 | tf_op jit(solution)/shard_map/ppermute | solution.py:17
  57.6 16.0 %collective-permute-start.11 = (bf16[32,32,128]{2,1,0:T(8,128)(2,1)S(1)}, bf16[32,32,128]{2,1,0:T(8,128)(2,1)S(1)}, u32[]{:S(2)}, u32[]{:S(2)}) collective-permute-start(bf16[32,32,128]{2,1,0:T(8,128)(2,1)S(1)} %get-tuple-element.7), channel_id=1, source_target_pairs={{0,1},{1,0},{2,3},{3,2},{4,5},{5,4},{6,7},{7,6},{8,9},{9,8},{10,11... | collective-permute-start | bytes 786440 | tf_op jit(solution)/shard_map/ppermute | solution.py:17
  57.6 17.2 %collective-permute-start.10 = (bf16[32,32,128]{2,1,0:T(8,128)(2,1)S(1)}, bf16[32,32,128]{2,1,0:T(8,128)(2,1)S(1)}, u32[]{:S(2)}, u32[]{:S(2)}) collective-permute-start(bf16[32,32,128]{2,1,0:T(8,128)(2,1)S(1)} %get-tuple-element.8), channel_id=1, source_target_pairs={{0,12},{1,8},{2,4},{3,0},{4,13},{5,9},{6,5},{7,1},{8,14},{9,10},{1... | collective-permute-start | bytes 786440 | tf_op jit(solution)/shard_map/ppermute | solution.py:29
  58.6 17.1 %collective-permute-start.9 = (bf16[32,32,128]{2,1,0:T(8,128)(2,1)S(1)}, bf16[32,32,128]{2,1,0:T(8,128)(2,1)S(1)}, u32[]{:S(2)}, u32[]{:S(2)}) collective-permute-start(bf16[32,32,128]{2,1,0:T(8,128)(2,1)S(1)} %get-tuple-element.8), channel_id=1, source_target_pairs={{0,8},{1,12},{2,0},{3,4},{4,9},{5,13},{6,1},{7,5},{8,10},{9,14},{1... | collective-permute-start | bytes 786440 | tf_op jit(solution)/shard_map/ppermute | solution.py:29
  66.2 10.0 %collective-permute-start.8 = (bf16[32,32,128]{2,1,0:T(8,128)(2,1)S(1)}, bf16[32,32,128]{2,1,0:T(8,128)(2,1)S(1)}, u32[]{:S(2)}, u32[]{:S(2)}) collective-permute-start(bf16[32,32,128]{2,1,0:T(8,128)(2,1)S(1)} %get-tuple-element.8), channel_id=1, source_target_pairs={{0,4},{1,0},{2,12},{3,8},{4,5},{5,1},{6,13},{7,9},{8,6},{9,2},{10,... | collective-permute-start | bytes 786440 | tf_op jit(solution)/shard_map/ppermute | solution.py:29
  71.6 11.9 %collective-permute-start.7 = (bf16[32,32,128]{2,1,0:T(8,128)(2,1)S(1)}, bf16[32,32,128]{2,1,0:T(8,128)(2,1)S(1)}, u32[]{:S(2)}, u32[]{:S(2)}) collective-permute-start(bf16[32,32,128]{2,1,0:T(8,128)(2,1)S(1)} %get-tuple-element.8), channel_id=1, source_target_pairs={{0,0},{1,4},{2,8},{3,12},{4,1},{5,5},{6,9},{7,13},{8,2},{9,6},{10,... | collective-permute-start | bytes 786440 | tf_op jit(solution)/shard_map/ppermute | solution.py:29
  101.6 11.3 %copy-start.8 = (bf16[128,128]{1,0:T(8,128)(2,1)S(1)}, bf16[128,128]{1,0:T(8,128)(2,1)}, u32[]{:S(2)}) copy-start(bf16[128,128]{1,0:T(8,128)(2,1)} %param.36) | copy-start | bytes 98308
  101.6 11.3 %copy-start.9 = (f32[128]{0:T(128)S(1)}, f32[128]{0:T(128)}, u32[]{:S(2)}) copy-start(f32[128]{0:T(128)} %param.37) | copy-start | bytes 1540
  101.6 11.3 %copy-start.10 = (f32[128]{0:T(128)S(1)}, f32[128]{0:T(128)}, u32[]{:S(2)}) copy-start(f32[128]{0:T(128)} %param.35) | copy-start | bytes 1540
  101.6 11.3 %copy-start.11 = (f32[128]{0:T(128)S(1)}, f32[128]{0:T(128)}, u32[]{:S(2)}) copy-start(f32[128]{0:T(128)} %param.34) | copy-start | bytes 1540

commit v2 on v1

--- a/solution.py
+++ b/solution.py
@@ -143,11 +143,28 @@
         * pair_live
     ).astype(jnp.bfloat16)
     gating = jax.nn.sigmoid(mixture[:, :, 4 * channels :])
-    left_panel = gather_plane(left_edge, count)
-    right_match = gather_turned(right_edge, count)
-    triangle = jnp.einsum(
-        "bikc,bjkc->ijc", left_panel, right_match, preferred_element_type=jnp.float32
-    )
+    devices = lax.axis_size(GROUP)
+    if channels % (8 * devices) == 0:
+        share = channels // devices
+        edges = jnp.stack([left_edge, right_edge]).reshape(
+            2, row_count * col_count, devices, share
+        ).transpose(2, 0, 3, 1)
+        edges = lax.all_to_all(edges, GROUP, 0, 0, tiled=True)
+        edges = edges.reshape(count, count, 2, share, row_count, col_count)
+        edges = edges.transpose(2, 3, 0, 4, 1, 5).reshape(
+            2, share, count * row_count, count * col_count
+        )
+        sums = jnp.einsum("cik,cjk->cij", edges[0], edges[1], preferred_element_type=jnp.float32)
+        sums = sums.astype(jnp.bfloat16).reshape(share, count, row_count, count, col_count)
+        sums = sums.transpose(1, 3, 0, 2, 4).reshape(devices, share, row_count * col_count)
+        sums = lax.all_to_all(sums, GROUP, 0, 0, tiled=True)
+        triangle = sums.reshape(channels, row_count, col_count).transpose(1, 2, 0).astype(jnp.float32)
+    else:
+        left_panel = gather_plane(left_edge, count)
+        right_match = gather_turned(right_edge, count)
+        triangle = jnp.einsum(
+            "bikc,bjkc->ijc", left_panel, right_match, preferred_element_type=jnp.float32
+        )
     normed_tri = apply_layer_norm(triangle, triangle_sum_norm_gain, triangle_sum_norm_bias).astype(
         jnp.bfloat16
     )

time: 116 us -> 129 us (1.11)
  blocking collectives: 0 us -> 34.2 us
  local copies, waits for them, and re-layouts: 44 us -> 59.6 us
  waiting for transfers between devices: 17 us -> 2.85 us
  starting transfers between devices: 25.7 us -> 11.7 us
  matrix products: 17.7 us -> 12.6 us
  other arithmetic: 10.4 us -> 5.83 us
    all_to_all x0 -> x2, blocking collectives: none -> 34.2 us  [the longest x1 20.7 us: body(): edges = lax.all_to_all(edges, GROUP, 0, 0, tiled=True)]
    reshape x0 -> x5, local copies, waits for them, and re-layouts: none -> 14.3 us  [the longest x2 6.85 us: body(): edges = edges.reshape(count, count, 2, share, row_count, col_count)]
    ppermute x8 -> x4, starting transfers between devices: 19.4 us -> 8.86 us  [gather_turned(): parts.append(lax.ppermute(block, GROUP, pairs))]
    another operation x2, local copies, waits for them, and re-layouts: 14.5 us -> 4.63 us  [body(): jnp.stack([left_edge, right_edge])]
    convert_element_type x0 -> x4, local copies, waits for them, and re-layouts: none -> 9.28 us  [the longest x2 4.68 us: body(): sums.reshape(channels, row_count, col_count).transpose(1, 2, 0)]
    ppermute x8 -> x4, waiting for transfers between devices: 11.5 us -> 2.84 us  [gather_turned(): parts.append(lax.ppermute(block, GROUP, pairs))]
    ppermute x6 -> x3, waiting for transfers between devices: 5.49 us -> 0.01 us  [gather_plane(): lax.ppermute(block, PLANE, [(p, p ^ step) for p in range(count)])]
    dot_general x1, matrix products: 6.13 us -> 1.01 us  [body(): jnp.einsum('cik,cjk->cij', edges[0], edges[1], preferred_element_type=jnp...]
  transfers between devices with their start and end apart: 14 -> 7, of which waited for: 6 -> 2; matrix products, arithmetic and copies ran while one was open for 1% -> 0% of each run, Pallas kernels for 0% -> 0%
where the time goes in v2:
time: 129 us; the launch traced here: 127 us
  local copies, waits for them, and re-layouts  59.6 us (46%)
  blocking collectives  34.2 us (27%)
  matrix products  12.6 us (10%)
  starting transfers between devices  11.7 us (9%)
  other arithmetic  5.83 us (5%)
  waiting for transfers between devices  2.85 us (2%)
    all_to_all x1, blocking collectives, body(): edges = lax.all_to_all(edges, GROUP, 0, 0, tiled=True)  20.7 us
    all_to_all x1, blocking collectives, body(): sums = lax.all_to_all(sums, GROUP, 0, 0, tiled=True)  13.4 us
    convert_element_type x1, local copies, waits for them, and re-layouts, body(): products.astype(jnp.bfloat16)  11.9 us
    dot_general x1, local copies, waits for them, and re-layouts, body(): jnp.dot(flattened, outer_pair_projection, preferred_element_type=jnp.floa...  11.3 us
    ppermute x4, starting transfers between devices, gather_turned(): parts.append(lax.ppermute(block, GROUP, pairs))  8.86 us
    reshape x2, local copies, waits for them, and re-layouts, body(): edges = edges.reshape(count, count, 2, share, row_count, col_count)  6.85 us
    dot_general x1, matrix products, body(): jnp.einsum('sic,sjd->ijcd', left_all[:, :wide].reshape(total_seqs, row_co...  5.59 us
    reshape x2, local copies, waits for them, and re-layouts, body(): sums.astype(jnp.bfloat16).reshape(share, count, row_count, count, col_count)  5.17 us
  transfers between devices with their start and end apart: 7, of which 2 were waited for; matrix products, arithmetic and copies ran while one was open for 0% of the time, Pallas kernels for 0%

profile of v2, /device:TPU:1, one launch (start us, length us, event | category | flops | bytes accessed | tf_op | source)
XLA Modules:
  0.0 127.1 jit_solution(16885025830871673622)
XLA Ops:
  0.7 1.3 convert_reduce_fusion
  2.0 1.4 %fusion.10 = f32[32,32]{1,0:T(8,128)S(1)} fusion(bf16[32,32,256]{2,1,0:T(8,128)(2,1)} %param.19, f32[32,32]{1,0:T(8,128)S(1)} %broadcast_multiply_fusion.3), kind=kLoop, calls=%fused_computation.21 | loop fusion | flops 1047552 | bytes 532480 | tf_op jit(solution)/shard_map/reduce_sum | solution.py:37
  3.5 0.8 fusion.49
  4.3 1.6 %fusion.7 = bf16[32,32,64]{2,1,0:T(8,128)(2,1)S(1)} fusion(bf16[32,32,256]{2,1,0:T(8,128)(2,1)} %param.19, f32[256]{0:T(256)} %param.25, f32[256]{0:T(256)} %param.24, f32[32,32]{1,0:T(8,128)S(1)} %get-tuple-element.31, f32[32,32]{1,0:T(8,128)S(1)} %broadcast_multiply_fusion.3, f32[32,32]{1,0:T(8,128)S(1)} %get-tuple-element.6, f32[64]{0:T(128)} %param.27, ...), kind=kOutput, calls=%fused_computation.16 | convolution fusion | flops 35323904 | bytes 702720 | tf_op jit(solution)/shard_map/dot_general | solution.py:77
  6.7 2.7 %collective-permute-start.4 = (bf16[32,1056]{1,0:T(8,128)(2,1)S(1)}, bf16[32,1056]{1,0:T(8,128)(2,1)S(1)}, u32[]{:S(2)}, u32[]{:S(2)}) collective-permute-start(bf16[32,1056]{1,0:T(8,128)(2,1)S(1)} %get-tuple-element.22), channel_id=1, source_target_pairs={{0,1},{1,0},{2,3},{3,2},{4,5},{5,4},{6,7},{7,6},{8,9},{9,8},{10,11... | collective-permute-start | bytes 202760 | tf_op jit(solution)/shard_map/ppermute | solution.py:17
  9.4 1.8 %collective-permute-start.3 = (bf16[32,1056]{1,0:T(8,128)(2,1)S(1)}, bf16[32,1056]{1,0:T(8,128)(2,1)S(1)}, u32[]{:S(2)}, u32[]{:S(2)}) collective-permute-start(bf16[32,1056]{1,0:T(8,128)(2,1)S(1)} %get-tuple-element.23), channel_id=1, source_target_pairs={{0,12},{1,8},{2,4},{3,0},{4,13},{5,9},{6,5},{7,1},{8,14},{9,10},{1... | collective-permute-start | bytes 202760 | tf_op jit(solution)/shard_map/ppermute | solution.py:29
  11.2 2.4 %collective-permute-start.2 = (bf16[32,1056]{1,0:T(8,128)(2,1)S(1)}, bf16[32,1056]{1,0:T(8,128)(2,1)S(1)}, u32[]{:S(2)}, u32[]{:S(2)}) collective-permute-start(bf16[32,1056]{1,0:T(8,128)(2,1)S(1)} %get-tuple-element.23), channel_id=1, source_target_pairs={{0,8},{1,12},{2,0},{3,4},{4,9},{5,13},{6,1},{7,5},{8,10},{9,14},{1... | collective-permute-start | bytes 202760 | tf_op jit(solution)/shard_map/ppermute | solution.py:29
  13.8 1.1 collective-permute-start.1
  14.9 3.5 %collective-permute-start = (bf16[32,1056]{1,0:T(8,128)(2,1)S(1)}, bf16[32,1056]{1,0:T(8,128)(2,1)S(1)}, u32[]{:S(2)}, u32[]{:S(2)}) collective-permute-start(bf16[32,1056]{1,0:T(8,128)(2,1)S(1)} %get-tuple-element.23), channel_id=1, source_target_pairs={{0,0},{1,4},{2,8},{3,12},{4,1},{5,5},{6,9},{7,13},{8,2},{9,6},{10,... | collective-permute-start | bytes 202760 | tf_op jit(solution)/shard_map/ppermute | solution.py:29
  18.7 0.8 collective-permute-done.1
  19.5 2.1 %collective-permute-done = bf16[32,1056]{1,0:T(8,128)(2,1)S(1)} collective-permute-done((bf16[32,1056]{1,0:T(8,128)(2,1)S(1)}, bf16[32,1056]{1,0:T(8,128)(2,1)S(1)}, u32[]{:S(2)}, u32[]{:S(2)}) %collective-permute-start) | collective-permute-done | bytes 67616 | tf_op jit(solution)/shard_map/ppermute | solution.py:29
  22.2 5.6 %convert_bitcast_fusion = bf16[32,32,32,32]{2,3,0,1:T(8,128)(2,1)} fusion(bf16[128,32,32,1]{0,2,3,1:T(8,128)(2,1)S(1)} %bitcast.75, bf16[128,32,32,1]{0,2,1,3:T(8,128)(2,1)S(1)} %bitcast.76), kind=kOutput, calls=%fused_computation | convolution fusion | flops 269484032 | bytes 2621440 | tf_op jit(solution)/shard_map/sic,sjd->ijcd/dot_general | solution.py:99
  27.8 11.9 %copy.42 = bf16[32,32,32,32]{3,2,1,0:T(8,128)(2,1)} copy(bf16[32,32,32,32]{2,3,0,1:T(8,128)(2,1)} %convert_bitcast_fusion) | data formatting | bytes 4194304 | tf_op jit(solution)/shard_map/convert_element_type | solution.py:106
  39.8 11.3 %dot_general.29 = bf16[32,32,1024]{2,1,0:T(8,128)(2,1)S(1)} reshape(bf16[32,32,32,32]{3,2,1,0:T(8,128)(2,1)} %copy.42) | data formatting | bytes 4194304 | tf_op jit(solution)/shard_map/dot_general | solution.py:107
  54.5 2.3 %copy.43 = bf16[32,32,128]{1,0,2:T(8,128)(2,1)} copy(bf16[32,32,128]{2,1,0:T(8,128)(2,1)S(1)} %get-tuple-element.7) | data formatting | bytes 524288 | tf_op jit(solution)/shard_map/convert_element_type | solution.py:139
  56.8 2.3 %stack.65 = bf16[1,1024,16,8]{1,3,2,0:T(8,128)(2,1)S(1)} reshape(bf16[32,32,128]{1,0,2:T(8,128)(2,1)} %copy.43) | data formatting | bytes 524288 | tf_op jit(solution)/shard_map/stack | solution.py:149
  59.1 2.3 %copy.44 = bf16[32,32,128]{1,0,2:T(8,128)(2,1)} copy(bf16[32,32,128]{2,1,0:T(8,128)(2,1)S(1)} %get-tuple-element.8) | data formatting | bytes 524288 | tf_op jit(solution)/shard_map/convert_element_type | solution.py:144
  61.4 2.3 %stack.66 = bf16[1,1024,16,8]{1,3,2,0:T(8,128)(2,1)S(1)} reshape(bf16[32,32,128]{1,0,2:T(8,128)(2,1)} %copy.44) | data formatting | bytes 524288 | tf_op jit(solution)/shard_map/stack | solution.py:149
  63.9 20.7 %all_to_all.10 = bf16[16,2,8,1024]{3,2,1,0:T(8,128)(2,1)S(1)} all-to-all(bf16[16,2,8,1024]{3,2,1,0:T(8,128)(2,1)S(1)} %copy.45), channel_id=1, replica_groups=mesh['groups'=2,'resi'=4,'resj'=2,'seq'=2] {'resi','resj','seq'}, dimensions={0} | all-to-all | bytes 1048576 | tf_op jit(solution)/shard_map/all_to_all | solution.py:152
  84.6 2.6 %reshape.202 = bf16[4,4,2,8,32,32]{5,4,3,2,1,0:T(8,128)(2,1)} reshape(bf16[16,2,8,1024]{3,2,1,0:T(8,128)(2,1)S(1)} %all_to_all.10) | data formatting | bytes 1048576 | tf_op jit(solution)/shard_map/reshape | solution.py:153
  87.2 4.3 %copy.54 = bf16[4,4,2,8,32,32]{5,1,4,0,3,2:T(4,128)(2,1)S(1)} copy(bf16[4,4,2,8,32,32]{5,4,3,2,1,0:T(8,128)(2,1)} %reshape.202) | data formatting | bytes 1048576 | tf_op jit(solution)/shard_map/reshape | solution.py:153
  91.5 2.2 %fusion.50 = (bf16[1,8,4,32,4,32]{5,4,3,2,1,0:T(4,128)(2,1)}, bf16[1,8,4,32,4,32]{5,4,3,2,1,0:T(4,128)(2,1)}) fusion(bf16[2,8,4,32,4,32]{5,4,3,2,1,0:T(4,128)(2,1)S(1)} %bitcast.69), kind=kLoop, calls=%fused_computation.99 | loop fusion | bytes 1048576 | tf_op jit(solution)/shard_map/slice | solution.py:157
  93.7 2.0 %squeeze.16 = bf16[8,128,128]{2,1,0:T(8,128)(2,1)S(1)} reshape(bf16[1,8,4,32,4,32]{5,4,3,2,1,0:T(4,128)(2,1)} %get-tuple-element.9) | data formatting | bytes 524288 | tf_op jit(solution)/shard_map/squeeze | solution.py:157
  95.7 2.0 %squeeze.15 = bf16[8,128,128]{2,1,0:T(8,128)(2,1)S(1)} reshape(bf16[1,8,4,32,4,32]{5,4,3,2,1,0:T(4,128)(2,1)} %get-tuple-element.10) | data formatting | bytes 524288 | tf_op jit(solution)/shard_map/squeeze | solution.py:157
  97.6 1.0 convolution_convert_fusion
  98.6 2.7 %reshape.203 = bf16[8,4,32,4,32]{4,3,2,1,0:T(4,128)(2,1)} reshape(bf16[8,128,128]{2,1,0:T(8,128)(2,1)} %convolution_convert_fusion) | data formatting | bytes 524288 | tf_op jit(solution)/shard_map/reshape | solution.py:158
  101.4 2.4 %copy.55 = bf16[8,4,32,4,32]{4,2,0,3,1:T(8,128)(2,1)} copy(bf16[8,4,32,4,32]{4,3,2,1,0:T(4,128)(2,1)} %reshape.203) | data formatting | bytes 524288 | tf_op jit(solution)/shard_map/reshape | solution.py:158
  103.8 2.3 %reshape.204 = bf16[16,8,1024]{2,1,0:T(8,128)(2,1)S(1)} reshape(bf16[4,4,8,32,32]{4,3,2,1,0:T(8,128)(2,1)} %bitcast.70) | data formatting | bytes 524288 | tf_op jit(solution)/shard_map/reshape | solution.py:159
  106.1 13.4 %all_to_all.11 = bf16[16,8,1024]{2,1,0:T(8,128)(2,1)S(1)} all-to-all(bf16[16,8,1024]{2,1,0:T(8,128)(2,1)S(1)} %reshape.204), channel_id=1, replica_groups=mesh['groups'=2,'resi'=4,'resj'=2,'seq'=2] {'resi','resj','seq'}, dimensions={0} | all-to-all | bytes 524288 | tf_op jit(solution)/shard_map/all_to_all | solution.py:160
  119.6 2.0 %reshape.205 = f32[128,32,32]{2,1,0:T(8,128)} reshape(bf16[16,8,1024]{2,1,0:T(8,128)(2,1)S(1)} %all_to_all.11) | data formatting | bytes 786432 | tf_op jit(solution)/shard_map/convert_element_type | solution.py:161
  121.6 2.7 %copy.48 = f32[128,32,32]{0,2,1:T(8,128)S(1)} copy(f32[128,32,32]{2,1,0:T(8,128)} %reshape.205) | data formatting | bytes 1048576 | tf_op jit(solution)/shard_map/convert_element_type | solution.py:161
  124.9 2.2 %fusion.6 = bf16[32,32,128]{2,1,0:T(8,128)(2,1)} fusion(f32[32,32,128]{2,1,0:T(8,128)} %copy-done.1, f32[32,32,640]{2,1,0:T(8,128)S(1)} %convolution_add_fusion, f32[128,32,32]{0,2,1:T(8,128)S(1)} %copy.48, f32[128]{0:T(128)S(1)} %copy-done.10, f32[128]{0:T(128)S(1)} %copy-done.11, f32[128]{0:T(128)S(1)} %copy-done.12, f32[32,32]{1,0:T(8,128)S(1)} %add_rsqrt_fusion, ...), kind=kOutput, calls=%fused_computation.15 | convolution fusion | flops 35127296 | bytes 1877504 | tf_op jit(solution)/shard_map/dot_general | solution.py:171
  (67 shorter events, 6.7 us)
Async XLA Ops:
  0.0 51.1 %copy-start = (bf16[1024,128]{1,0:T(8,128)(2,1)S(1)}, bf16[1024,128]{1,0:T(8,128)(2,1)}, u32[]{:S(2)}) copy-start(bf16[1024,128]{1,0:T(8,128)(2,1)} %param.28) | copy-start | bytes 786436
  0.7 12.9 %copy-start.6 = (s32[128]{0:T(128)S(1)}, s32[128]{0:T(128)}, u32[]{:S(2)}) copy-start(s32[128]{0:T(128)} %param.23) | copy-start | bytes 1540
  6.6 7.2 %collective-permute-start.5 = (bf16[32,1056]{1,0:T(8,128)(2,1)S(1)}, bf16[32,1056]{1,0:T(8,128)(2,1)S(1)}, u32[]{:S(2)}, u32[]{:S(2)}) collective-permute-start(bf16[32,1056]{1,0:T(8,128)(2,1)S(1)} %get-tuple-element.22), channel_id=1, source_target_pairs={{0,2},{1,3},{2,0},{3,1},{4,6},{5,7},{6,4},{7,5},{8,10},{9,11},{10,... | collective-permute-start | bytes 202760 | tf_op jit(solution)/shard_map/ppermute | solution.py:17
  6.7 8.2 %collective-permute-start.4 = (bf16[32,1056]{1,0:T(8,128)(2,1)S(1)}, bf16[32,1056]{1,0:T(8,128)(2,1)S(1)}, u32[]{:S(2)}, u32[]{:S(2)}) collective-permute-start(bf16[32,1056]{1,0:T(8,128)(2,1)S(1)} %get-tuple-element.22), channel_id=1, source_target_pairs={{0,1},{1,0},{2,3},{3,2},{4,5},{5,4},{6,7},{7,6},{8,9},{9,8},{10,11... | collective-permute-start | bytes 202760 | tf_op jit(solution)/shard_map/ppermute | solution.py:17
  9.4 9.1 %collective-permute-start.6 = (bf16[32,1056]{1,0:T(8,128)(2,1)S(1)}, bf16[32,1056]{1,0:T(8,128)(2,1)S(1)}, u32[]{:S(2)}, u32[]{:S(2)}) collective-permute-start(bf16[32,1056]{1,0:T(8,128)(2,1)S(1)} %get-tuple-element.22), channel_id=1, source_target_pairs={{0,3},{1,2},{2,1},{3,0},{4,7},{5,6},{6,5},{7,4},{8,11},{9,10},{10,... | collective-permute-start | bytes 202760 | tf_op jit(solution)/shard_map/ppermute | solution.py:17
  9.4 9.2 %collective-permute-start.3 = (bf16[32,1056]{1,0:T(8,128)(2,1)S(1)}, bf16[32,1056]{1,0:T(8,128)(2,1)S(1)}, u32[]{:S(2)}, u32[]{:S(2)}) collective-permute-start(bf16[32,1056]{1,0:T(8,128)(2,1)S(1)} %get-tuple-element.23), channel_id=1, source_target_pairs={{0,12},{1,8},{2,4},{3,0},{4,13},{5,9},{6,5},{7,1},{8,14},{9,10},{1... | collective-permute-start | bytes 202760 | tf_op jit(solution)/shard_map/ppermute | solution.py:29
  11.2 7.5 %collective-permute-start.2 = (bf16[32,1056]{1,0:T(8,128)(2,1)S(1)}, bf16[32,1056]{1,0:T(8,128)(2,1)S(1)}, u32[]{:S(2)}, u32[]{:S(2)}) collective-permute-start(bf16[32,1056]{1,0:T(8,128)(2,1)S(1)} %get-tuple-element.23), channel_id=1, source_target_pairs={{0,8},{1,12},{2,0},{3,4},{4,9},{5,13},{6,1},{7,5},{8,10},{9,14},{1... | collective-permute-start | bytes 202760 | tf_op jit(solution)/shard_map/ppermute | solution.py:29
  13.8 5.7 %collective-permute-start.1 = (bf16[32,1056]{1,0:T(8,128)(2,1)S(1)}, bf16[32,1056]{1,0:T(8,128)(2,1)S(1)}, u32[]{:S(2)}, u32[]{:S(2)}) collective-permute-start(bf16[32,1056]{1,0:T(8,128)(2,1)S(1)} %get-tuple-element.23), channel_id=1, source_target_pairs={{0,4},{1,0},{2,12},{3,8},{4,5},{5,1},{6,13},{7,9},{8,6},{9,2},{10,... | collective-permute-start | bytes 202760 | tf_op jit(solution)/shard_map/ppermute | solution.py:29
  14.9 6.6 %collective-permute-start = (bf16[32,1056]{1,0:T(8,128)(2,1)S(1)}, bf16[32,1056]{1,0:T(8,128)(2,1)S(1)}, u32[]{:S(2)}, u32[]{:S(2)}) collective-permute-start(bf16[32,1056]{1,0:T(8,128)(2,1)S(1)} %get-tuple-element.23), channel_id=1, source_target_pairs={{0,0},{1,4},{2,8},{3,12},{4,1},{5,5},{6,9},{7,13},{8,2},{9,6},{10,... | collective-permute-start | bytes 202760 | tf_op jit(solution)/shard_map/ppermute | solution.py:29
  51.1 1.0 copy-start.2
  51.1 0.9 copy-start.4
  51.1 2.5 %copy-start.3 = (bf16[128,640]{1,0:T(8,128)(2,1)S(1)}, bf16[128,640]{1,0:T(8,128)(2,1)}, u32[]{:S(2)}) copy-start(bf16[128,640]{1,0:T(8,128)(2,1)} %param.32) | copy-start | bytes 491524
  51.1 2.4 %copy-start.5 = (f32[640]{0:T(1024)S(1)}, f32[640]{0:T(1024)}, u32[]{:S(2)}) copy-start(f32[640]{0:T(1024)} %param.33) | copy-start | bytes 7684
  51.1 2.4 %copy-start.7 = (f32[128]{0:T(128)S(1)}, f32[128]{0:T(128)}, u32[]{:S(2)}) copy-start(f32[128]{0:T(128)} %param.31) | copy-start | bytes 1540
  51.2 2.4 %copy-start.8 = (f32[128]{0:T(128)S(1)}, f32[128]{0:T(128)}, u32[]{:S(2)}) copy-start(f32[128]{0:T(128)} %param.30) | copy-start | bytes 1540
  52.8 0.8 copy-start.1
  119.6 5.3 %copy-start.9 = (bf16[128,128]{1,0:T(8,128)(2,1)S(1)}, bf16[128,128]{1,0:T(8,128)(2,1)}, u32[]{:S(2)}) copy-start(bf16[128,128]{1,0:T(8,128)(2,1)} %param.36) | copy-start | bytes 98308
  119.6 5.3 %copy-start.10 = (f32[128]{0:T(128)S(1)}, f32[128]{0:T(128)}, u32[]{:S(2)}) copy-start(f32[128]{0:T(128)} %param.37) | copy-start | bytes 1540
  119.6 5.3 %copy-start.11 = (f32[128]{0:T(128)S(1)}, f32[128]{0:T(128)}, u32[]{:S(2)}) copy-start(f32[128]{0:T(128)} %param.35) | copy-start | bytes 1540
  119.6 5.3 %copy-start.12 = (f32[128]{0:T(128)S(1)}, f32[128]{0:T(128)}, u32[]{:S(2)}) copy-start(f32[128]{0:T(128)} %param.34) | copy-start | bytes 1540

commit v3 on v0

v3 whole, which is shorter than its diff:
```python
import functools

import jax
import jax.numpy as jnp
from jax import lax
from jax.experimental import pallas as pl
from jax.experimental.pallas import tpu as pltpu
from jax.sharding import PartitionSpec as P

RELMAX = 32
LANES = 128
PLANE = ("resj", "seq")
GROUP = ("resi", "resj", "seq")
F32 = jnp.float32
BF16 = jnp.bfloat16
MIB = 1 << 20


def iota(shape, axis):
    return lax.broadcasted_iota(jnp.int32, shape, axis)


def dot(a, b):
    return jnp.dot(a, b, preferred_element_type=F32)


def sigmoid(v):
    return 0.5 * jnp.tanh(0.5 * v) + 0.5


def layer_norm(values, gain, shift):
    average = jnp.mean(values, axis=-1, keepdims=True)
    centred = values - average
    variance = jnp.mean(centred * centred, axis=-1, keepdims=True)
    return centred * lax.rsqrt(variance + 1e-05) * gain + shift


def pack_kernel(x_ref, mask_ref, res_ref, gain_ref, shift_ref, w_ref, bias_ref,
                left_ref, right_ref, lscr, rscr):
    seqs, rows, depth = x_ref.shape
    half = w_ref.shape[1] // 2
    per = LANES // half
    row_start = lax.axis_index("resi") * rows
    x = x_ref[...].reshape(seqs * rows, depth).astype(F32)
    normed = layer_norm(x, gain_ref[...], shift_ref[...]).astype(BF16)
    lane = iota((2 * half, 2 * LANES), 1)
    spread = lane % half + jnp.where(lane >= LANES, half, 0) == iota((2 * half, 2 * LANES), 0)
    spread = spread.astype(F32)
    wide = dot(w_ref[...], spread.astype(BF16)).astype(BF16)
    bias = jnp.dot(jnp.broadcast_to(bias_ref[...], (8, 2 * half)), spread,
                   precision=lax.Precision.HIGHEST, preferred_element_type=F32)[0:1]
    mapped = dot(normed, wide)
    lscr[...] = mapped[:, :LANES]
    rscr[...] = mapped[:, LANES:]
    total = res_ref.shape[1]
    pick = (iota((total, rows), 0) == iota((total, rows), 1) + row_start).astype(BF16)
    row_live = dot(jnp.broadcast_to(res_ref[...].astype(F32), (8, total)).astype(BF16), pick)[0:1]
    live = (mask_ref[...].astype(F32) * row_live).astype(BF16)
    width = rows * half
    spread_live = (iota((rows, width), 1) // half == iota((rows, width), 0)).astype(BF16)
    live_wide = dot(live, spread_live)
    sub = iota((seqs, LANES), 1) // half
    for tile in range(width // LANES):
        at = slice(tile * LANES, (tile + 1) * LANES)
        for scr, ref, first in ((lscr, left_ref, 0), (rscr, right_ref, LANES)):
            value = scr[pl.ds(tile * per, seqs, stride=rows), :]
            for k in range(1, per):
                value = jnp.where(sub == k, scr[pl.ds(tile * per + k, seqs, stride=rows), :], value)
            value = (value + bias[:, first:first + LANES]) * live_wide[:, at]
            ref[:, at] = value.astype(BF16)
    live_tile = dot(live, (iota((rows, LANES), 0) == iota((rows, LANES), 1)).astype(BF16))
    left_ref[:, width:] = live_tile.astype(BF16)
    right_ref[:, width:] = live_tile.astype(BF16)


def base_kernel(pair_ref, table_ref, chain_ref, chain_smem, w_ref, base_ref, block_ref, tscr, wscr):
    rows, cols, channels = pair_ref.shape
    total = chain_ref.shape[1]
    row_start = lax.axis_index("resi") * rows
    col_start = lax.axis_index(PLANE) * cols
    tscr[...] = jnp.zeros_like(tscr)
    tscr[0:table_ref.shape[0], :] = table_ref[...].astype(F32)
    table = tscr[...].astype(BF16)
    own = iota((cols, total), 1) == iota((cols, total), 0) + col_start
    chain_cols = jnp.sum(
        jnp.where(own, jnp.broadcast_to(chain_ref[...], (cols, total)).astype(F32), 0.0),
        axis=1, keepdims=True)
    col_pos = iota((cols, 1), 0) + col_start
    for i in range(rows):
        offset = jnp.clip(col_pos - (row_start + i) + RELMAX, 0, 2 * RELMAX)
        same = chain_cols == chain_smem[row_start + i].astype(F32)
        bins = jnp.where(same, offset, 2 * RELMAX + 1)
        one_hot = (iota((cols, LANES), 1) == bins).astype(F32).astype(BF16)
        base_ref[i] = pair_ref[i].astype(F32) + dot(one_hot, table)
    wscr[...] = w_ref[...].astype(F32)
    half = int(round(w_ref.shape[0] ** 0.5))
    per = LANES // half
    block_ref[...] = jnp.zeros_like(block_ref)
    for d in range(half):
        value = wscr[pl.ds(d, half, stride=half), :].astype(BF16)
        for k in range(per):
            block_ref[pl.ds(d * LANES + k * half, half), k * channels:(k + 1) * channels] = value


def edges_kernel(count, *refs):
    lefts, rights = refs[:count], refs[count:2 * count]
    (base_ref, block_ref, res_ref, res_smem, gain_ref, shift_ref, w_ref, bias_ref,
     updated_ref, left_ref, right_ref, gate_ref,
     lall, rall, tscr, rscr, oscr, nscr, escr) = refs[2 * count:]
    rows, cols, channels = base_ref.shape
    seqs = lefts[0].shape[0]
    half = block_ref.shape[0] // LANES
    per = LANES // half
    width = rows * half
    total_seqs = count * seqs
    z = lax.axis_index("resi")
    q = lax.axis_index(PLANE)
    row_start, col_start = z * rows, q * cols
    for step in range(count):
        lall[q ^ step] = lefts[step][...]
        rall[z ^ step] = rights[step][...]
    right = rall[...].reshape(total_seqs, -1)
    left = lall[...].reshape(total_seqs, -1)
    for at in range(0, width, LANES):
        for s in range(0, total_seqs, LANES):
            tscr[s // LANES, at:at + LANES, :] = right[s:s + LANES, at:at + LANES].astype(F32).T
    for d in range(half):
        for s in range(0, total_seqs, LANES):
            turned = tscr[s // LANES, pl.ds(d, cols, stride=half), :]
            rscr[d * cols:(d + 1) * cols, s:s + LANES] = turned.astype(BF16)
    live_cols = right[:, width:].astype(F32).T[0:cols].astype(BF16)
    counts = dot(live_cols, left[:, width:])
    inverse = 1.0 / jnp.maximum(counts, 1.0)
    wide = 2 * LANES
    tall = 8
    for first in range(0, width, wide):
        for d0 in range(0, half, tall):
            product = dot(rscr[d0 * cols:(d0 + tall) * cols, :], left[:, first:first + wide])
            product = product.astype(BF16)
            for dd in range(tall):
                for t in range(wide // LANES):
                    g = first // LANES + t
                    oscr[g * cols:(g + 1) * cols, (d0 + dd) * LANES:(d0 + dd + 1) * LANES] = (
                        product[dd * cols:(dd + 1) * cols, t * LANES:(t + 1) * LANES])
    outer = dot(oscr[...], block_ref[...])
    for i in range(rows):
        g, k = i // per, i % per
        part = outer[g * cols:(g + 1) * cols, k * channels:(k + 1) * channels]
        updated = (base_ref[i] + part * inverse[:, i:i + 1]).astype(BF16)
        updated_ref[i] = updated
        normed = layer_norm(updated.astype(F32), gain_ref[...], shift_ref[...])
        nscr[i * cols:(i + 1) * cols, :] = normed.astype(BF16)
    total = res_ref.shape[1]
    own = iota((cols, total), 1) == iota((cols, total), 0) + col_start
    col_live = jnp.sum(
        jnp.where(own, jnp.broadcast_to(res_ref[...], (cols, total)).astype(F32), 0.0),
        axis=1, keepdims=True)
    col_live = jnp.broadcast_to(col_live, (cols, channels))
    chunk = 8
    for i0 in range(0, rows, chunk):
        mixture = dot(nscr[i0 * cols:(i0 + chunk) * cols, :], w_ref[...]) + bias_ref[...]
        part = [mixture[:, n * channels:(n + 1) * channels] for n in range(5)]
        left_edge = sigmoid(part[0]) * part[1]
        right_edge = sigmoid(part[2]) * part[3]
        gate_ref[i0 * cols:(i0 + chunk) * cols, :] = sigmoid(part[4])
        for ii in range(chunk):
            live = col_live * res_smem[row_start + i0 + ii].astype(F32)
            at = slice(ii * cols, (ii + 1) * cols)
            left_ref[i0 + ii] = (left_edge[at] * live).astype(BF16)
            escr[(i0 + ii) * cols:(i0 + ii + 1) * cols, :] = right_edge[at] * live
    for k in range(cols):
        right_ref[k] = escr[pl.ds(k, rows, stride=cols), :].astype(BF16)


def triangle_kernel(count, *refs):
    lefts, rights = refs[:count], refs[count:2 * count]
    (updated_ref, gate_ref, gain_ref, shift_ref, w_ref, bias_ref,
     out_ref, lscr, rscr, acc) = refs[2 * count:]
    rows, depth, channels = lefts[0].shape
    cols = rights[0].shape[1]
    turn = lax.axis_index("resi") ^ lax.axis_index(PLANE)
    for step in range(count):
        lscr[step] = lefts[step][...].astype(F32).reshape(rows * depth, channels)
        rscr[step] = rights[step][...].astype(F32).reshape(depth * cols, channels)
    block = 4
    tiles = cols // 8

    def rows_body(at, carry):
        sums = [[jnp.zeros((8, channels), F32) for _ in range(tiles)] for _ in range(block)]

        def step_body(step, sums):
            own = step ^ turn
            for k in range(depth):
                column = [rscr[step, k * cols + t * 8:k * cols + t * 8 + 8, :] for t in range(tiles)]
                for b in range(block):
                    row = lscr[own, pl.ds((at * block + b) * depth + k, 1), :]
                    for t in range(tiles):
                        sums[b][t] = sums[b][t] + row * column[t]
            return sums

        sums = lax.fori_loop(0, count, step_body, sums)
        for b in range(block):
            for t in range(tiles):
                acc[pl.ds(pl.multiple_of((at * block + b) * cols + t * 8, 8), 8), :] = sums[b][t]
        return carry

    lax.fori_loop(0, rows // block, rows_body, 0)
    chunk = 8
    for i0 in range(0, rows, chunk):
        at = slice(i0 * cols, (i0 + chunk) * cols)
        normed = layer_norm(acc[at, :], gain_ref[...], shift_ref[...]).astype(BF16)
        result = dot(normed, w_ref[...]) + bias_ref[...]
        updated = updated_ref[i0:i0 + chunk].reshape(chunk * cols, channels).astype(F32)
        value = updated + gate_ref[at, :] * result
        out_ref[i0:i0 + chunk] = value.astype(BF16).reshape(chunk, cols, channels)


def send_plane(block, count):
    return [block] + [
        lax.ppermute(block, PLANE, [(p, p ^ m) for p in range(count)]) for m in range(1, count)
    ]


def send_turned(block, count):
    return [
        lax.ppermute(
            block, GROUP,
            [(z * count + p, (p ^ m) * count + z) for z in range(count) for p in range(count)])
        for m in range(count)
    ]


def call(kernel, outs, scratch, args, smem=(), flops=0, name=None):
    vmem = pl.BlockSpec(memory_space=pltpu.VMEM)
    specs = [pl.BlockSpec(memory_space=pltpu.SMEM) if n in smem else vmem for n in range(len(args))]
    size = sum(a.size * a.dtype.itemsize for a in args)
    return pl.pallas_call(
        kernel,
        out_shape=outs,
        in_specs=specs,
        out_specs=[vmem] * len(outs) if isinstance(outs, list) else vmem,
        scratch_shapes=scratch,
        compiler_params=pltpu.CompilerParams(vmem_limit_bytes=40 * MIB),
        cost_estimate=pl.CostEstimate(flops=flops, bytes_accessed=size, transcendentals=0),
        name=name,
    )(*args)


def body(
    homolog_matrix,
    sequence_pad_mask,
    pair_features,
    residue_pad_mask,
    residue_chain_index,
    homolog_standard_factor,
    homolog_standard_offset,
    factor_mapping_matrices,
    outer_side_biases,
    outer_pair_projection,
    relative_position_table,
    pair_norm_gain,
    pair_norm_bias,
    triangle_projection_weights,
    triangle_projection_biases,
    triangle_sum_norm_gain,
    triangle_sum_norm_bias,
    triangle_output_weight,
    outer_pair_bias,
):
    rows, cols, channels = pair_features.shape
    seqs, _, depth = homolog_matrix.shape
    half = factor_mapping_matrices.shape[1] // 2
    per = LANES // half
    count = lax.axis_size(PLANE)
    width = rows * half
    flat = lambda v: v.reshape(1, -1)
    shape = jax.ShapeDtypeStruct
    residue = flat(residue_pad_mask)
    chain = flat(residue_chain_index)
    pack = shape((seqs, width + LANES), BF16)
    left, right = call(
        pack_kernel, [pack, pack],
        [pltpu.VMEM((seqs * rows, LANES), F32)] * 2,
        [homolog_matrix, sequence_pad_mask, residue, flat(homolog_standard_factor),
         flat(homolog_standard_offset), factor_mapping_matrices, flat(outer_side_biases)],
        name="pack")
    rights = send_turned(right, count)
    lefts = send_plane(left, count)
    base, block = call(
        base_kernel,
        [shape((rows, cols, channels), F32), shape((half * LANES, per * channels), BF16)],
        [pltpu.VMEM((LANES, channels), F32), pltpu.VMEM((half * half, channels), F32)],
        [pair_features, relative_position_table, chain, residue_chain_index, outer_pair_projection],
        smem=(3,), flops=1 << 30, name="base")
    updated, left_edge, right_edge, gate = call(
        functools.partial(edges_kernel, count),
        [shape((rows, cols, channels), BF16), shape((rows, cols, channels), BF16),
         shape((cols, rows, channels), BF16), shape((rows * cols, channels), F32)],
        [pltpu.VMEM((count, seqs, width + LANES), BF16), pltpu.VMEM((count, seqs, width + LANES), BF16),
         pltpu.VMEM((count * seqs // LANES, width, LANES), F32),
         pltpu.VMEM((width, count * seqs), BF16),
         pltpu.VMEM((rows // per * cols, half * LANES), BF16),
         pltpu.VMEM((rows * cols, channels), BF16), pltpu.VMEM((rows * cols, channels), F32)],
        lefts + rights + [base, block, residue, residue_pad_mask, flat(pair_norm_gain),
                          flat(pair_norm_bias), triangle_projection_weights,
                          flat(triangle_projection_biases)],
        smem=(2 * count + 3,), name="edges")
    right_edges = send_turned(right_edge, count)
    left_edges = send_plane(left_edge, count)
    return call(
        functools.partial(triangle_kernel, count),
        shape((rows, cols, channels), BF16),
        [pltpu.VMEM((count, rows * cols, channels), F32), pltpu.VMEM((count, rows * cols, channels), F32),
         pltpu.VMEM((rows * cols, channels), F32)],
        left_edges + right_edges + [updated, gate, flat(triangle_sum_norm_gain),
                                    flat(triangle_sum_norm_bias), triangle_output_weight,
                                    flat(outer_pair_bias)],
        name="triangle")


def solution(mesh):
    pair = P(("groups", "resi"), ("resj", "seq"), None)
    placed = (
        P(("groups", "resj", "seq"), "resi", None),
        P(("groups", "resj", "seq"), "resi"),
        pair,
        P("groups"),
        P("groups"),
    ) + (P(),) * 14
    return jax.shard_map(body, mesh=mesh, in_specs=placed, out_specs=pair, check_vma=False)
```

time: 211 us -> 63.1 us (0.30)
  waiting for transfers between devices: 87.2 us -> 20.2 us
  blocking collectives: 47.6 us -> 0 us
  local copies, waits for them, and re-layouts: 36.3 us -> 9.32 us
  starting transfers between devices: 0.3 us -> 20.2 us
  matrix products: 16 us -> 0 us
  between operations: 13.4 us -> 0.17 us
  Pallas kernels: 0 us -> 12.8 us
  other arithmetic: 8.24 us -> 0 us
    psum x2 -> x0, waiting for transfers between devices: 51.3 us -> none  [broadcast(): return lax.psum(block, axis)]
    all_gather x2 -> x0, waiting for transfers between devices: 35.2 us -> none  [the longest x1 17.8 us: body(): lax.all_gather(right_edge, ('resj', 'seq'), axis=1, tiled=True)]
    all_gather x3 -> x0, blocking collectives: 31.4 us -> none  [the longest x1 10.8 us: body(): lax.all_gather(right_rows, ('resj', 'seq'), axis=1, tiled=True)]
    ppermute x0 -> x14, starting transfers between devices: none -> 20.2 us  [the longest x8 15.4 us: send_turned(): lax.ppermute(block, GROUP, [(z * count + p, (p ^ m) * count + z) for z in...]
    ppermute x0 -> x14, waiting for transfers between devices: none -> 20.2 us  [the longest x8 11.8 us: send_turned(): lax.ppermute(block, GROUP, [(z * count + p, (p ^ m) * count + z) for z in...]
    psum x1 -> x0, blocking collectives: 16.2 us -> none  [broadcast(): return lax.psum(block, axis)]
    dot_general x8 -> x0, matrix products: 16 us -> none  [the longest x1 6.52 us: body(): jnp.einsum('isc,jsd->ijcd', left_all.reshape(row_count, total_seqs, narro...]
    dot_general x2 -> x0, local copies, waits for them, and re-layouts: 15 us -> none  [the longest x1 11.3 us: body(): jnp.dot(flattened, outer_pair_projection, preferred_element_type=jnp.floa...]
  transfers between devices with their start and end apart: 4 -> 14, of which waited for: 3 -> 5; matrix products, arithmetic and copies ran while one was open for 3% -> 1% of each run, Pallas kernels for 0% -> 3%
where the time goes in v3:
time: 63.1 us; the launch traced here: 62.6 us
  starting transfers between devices  20.2 us (32%)
  waiting for transfers between devices  20.2 us (32%)
  Pallas kernels  12.8 us (20%)
  local copies, waits for them, and re-layouts  9.32 us (15%)
    ppermute x8, starting transfers between devices, send_turned(): lax.ppermute(block, GROUP, [(z * count + p, (p ^ m) * count + z) for z in...  15.4 us
    pallas_call x4, Pallas kernels, call(): pl.pallas_call(kernel, out_shape=outs, in_specs=specs, out_specs=[vmem] *...  12.8 us
    ppermute x8, waiting for transfers between devices, send_turned(): lax.ppermute(block, GROUP, [(z * count + p, (p ^ m) * count + z) for z in...  11.8 us
    unnamed x37, local copies, waits for them, and re-layouts  8.63 us
    ppermute x6, waiting for transfers between devices, send_plane(): lax.ppermute(block, PLANE, [(p, p ^ m) for p in range(count)])  8.33 us
    ppermute x6, starting transfers between devices, send_plane(): lax.ppermute(block, PLANE, [(p, p ^ m) for p in range(count)])  4.8 us
  transfers between devices with their start and end apart: 14, of which 5 were waited for; matrix products, arithmetic and copies ran while one was open for 1% of the time, Pallas kernels for 3%

profile of v3, /device:TPU:1, one launch (start us, length us, event | category | flops | bytes accessed | tf_op | source)
XLA Modules:
  0.0 62.6 jit_solution(11898815856985415452)
XLA Ops:
  0.0 0.9 %copy.20.w_ref = bf16[256,64]{1,0:T(8,128)(2,1)S(1)} copy(bf16[256,64]{0,1:T(8,128)(2,1)} %param.26) | data formatting | bytes 65536 | tf_op args[7]
  0.9 1.0 %copy-done = bf16[32,32,256]{2,1,0:T(8,128)(2,1)S(1)} copy-done((bf16[32,32,256]{2,1,0:T(8,128)(2,1)S(1)}, bf16[32,32,256]{2,1,0:T(8,128)(2,1)}, u32[]{:S(2)}) %copy-start) | copy-done | bytes 524312
  2.0 0.7 %copy-done.3 = s32[32,32]{1,0:T(8,128)S(1)} copy-done((s32[32,32]{1,0:T(8,128)S(1)}, s32[32,32]{1,0:T(8,128)}, u32[]{:S(2)}) %copy-start.3) | copy-done | bytes 4120
  2.7 0.7 %copy-done.4 = s32[128]{0:T(128)S(1)} copy-done((s32[128]{0:T(128)S(1)}, s32[128]{0:T(128)}, u32[]{:S(2)}) %copy-start.4) | copy-done | bytes 536
  3.3 0.7 %copy-done.6 = f32[256]{0:T(256)S(1)} copy-done((f32[256]{0:T(256)S(1)}, f32[256]{0:T(256)}, u32[]{:S(2)}) %copy-start.6) | copy-done | bytes 1048
  4.0 0.7 %copy-done.7 = f32[256]{0:T(256)S(1)} copy-done((f32[256]{0:T(256)S(1)}, f32[256]{0:T(256)}, u32[]{:S(2)}) %copy-start.7) | copy-done | bytes 1048
  4.7 0.7 %copy-done.8 = f32[64]{0:T(128)S(1)} copy-done((f32[64]{0:T(128)S(1)}, f32[64]{0:T(128)}, u32[]{:S(2)}) %copy-start.8) | copy-done | bytes 280
  5.4 1.2 %pack.1 = (bf16[32,1152]{1,0:T(8,128)(2,1)S(1)}, bf16[32,1152]{1,0:T(8,128)(2,1)S(1)}) custom-call(bf16[32,32,256]{2,1,0:T(8,128)(2,1)S(1)} %copy-done, s32[32,32]{1,0:T(8,128)S(1)} %copy-done.3, s32[1,128]{1,0:T(1,128)S(1)} %bitcast.10, f32[1,256]{1,0:T(1,128)S(1)} %bitcast.12, f32[1,256]{1,0:T(1,128)S(1)} %bitcast.13, bf16[256,64]{1,0:T(8,128)(2,1)S(1)} %copy.20.w_ref, ...), custom_call_target="tpu_custom_call" | custom-call | bytes 563968 | tf_op jit(solution)/shard_map/pack/pallas_call | solution.py:237
  6.6 2.7 %collective-permute-start.2 = (bf16[32,1152]{1,0:T(8,128)(2,1)S(1)}, bf16[32,1152]{1,0:T(8,128)(2,1)S(1)}, u32[]{:S(2)}, u32[]{:S(2)}) collective-permute-start(bf16[32,1152]{1,0:T(8,128)(2,1)S(1)} %get-tuple-element.13.refs_0_), channel_id=1, source_target_pairs={{0,3},{1,2},{2,1},{3,0},{4,7},{5,6},{6,5},{7,4},{8,11},{9,10},{10,... | collective-permute-start | bytes 221192 | tf_op jit(solution)/shard_map/ppermute | solution.py:220
  9.4 2.0 %collective-permute-start.6 = (bf16[32,1152]{1,0:T(8,128)(2,1)S(1)}, bf16[32,1152]{1,0:T(8,128)(2,1)S(1)}, u32[]{:S(2)}, u32[]{:S(2)}) collective-permute-start(bf16[32,1152]{1,0:T(8,128)(2,1)S(1)} %get-tuple-element.14), channel_id=1, source_target_pairs={{0,12},{1,8},{2,4},{3,0},{4,13},{5,9},{6,5},{7,1},{8,14},{9,10},{1... | collective-permute-start | bytes 221192 | tf_op jit(solution)/shard_map/ppermute | solution.py:226
  11.5 2.4 %collective-permute-start.5 = (bf16[32,1152]{1,0:T(8,128)(2,1)S(1)}, bf16[32,1152]{1,0:T(8,128)(2,1)S(1)}, u32[]{:S(2)}, u32[]{:S(2)}) collective-permute-start(bf16[32,1152]{1,0:T(8,128)(2,1)S(1)} %get-tuple-element.14), channel_id=1, source_target_pairs={{0,8},{1,12},{2,0},{3,4},{4,9},{5,13},{6,1},{7,5},{8,10},{9,14},{1... | collective-permute-start | bytes 221192 | tf_op jit(solution)/shard_map/ppermute | solution.py:226
  13.9 0.7 %reshape.40.refs_15_ = f32[1,640]{1,0:T(1,128)S(1)} reshape(f32[640]{0:T(1024)} %param.33) | data formatting | bytes 5120 | tf_op jit(solution)/shard_map/reshape | solution.py:276
  14.6 1.3 %collective-permute-start.4 = (bf16[32,1152]{1,0:T(8,128)(2,1)S(1)}, bf16[32,1152]{1,0:T(8,128)(2,1)S(1)}, u32[]{:S(2)}, u32[]{:S(2)}) collective-permute-start(bf16[32,1152]{1,0:T(8,128)(2,1)S(1)} %get-tuple-element.14), channel_id=1, source_target_pairs={{0,4},{1,0},{2,12},{3,8},{4,5},{5,1},{6,13},{7,9},{8,6},{9,2},{10,... | collective-permute-start | bytes 221192 | tf_op jit(solution)/shard_map/ppermute | solution.py:226
  15.9 3.3 %collective-permute-start.3 = (bf16[32,1152]{1,0:T(8,128)(2,1)S(1)}, bf16[32,1152]{1,0:T(8,128)(2,1)S(1)}, u32[]{:S(2)}, u32[]{:S(2)}) collective-permute-start(bf16[32,1152]{1,0:T(8,128)(2,1)S(1)} %get-tuple-element.14), channel_id=1, source_target_pairs={{0,0},{1,4},{2,8},{3,12},{4,1},{5,5},{6,9},{7,13},{8,2},{9,6},{10,... | collective-permute-start | bytes 221192 | tf_op jit(solution)/shard_map/ppermute | solution.py:226
  19.2 0.9 %copy-done.14 = bf16[32,32,128]{2,1,0:T(8,128)(2,1)S(1)} copy-done((bf16[32,32,128]{2,1,0:T(8,128)(2,1)S(1)}, bf16[32,32,128]{2,1,0:T(8,128)(2,1)}, u32[]{:S(2)}) %copy-start.14) | copy-done | bytes 262168
  20.1 0.9 %copy-done.15 = bf16[1024,128]{1,0:T(8,128)(2,1)S(1)} copy-done((bf16[1024,128]{1,0:T(8,128)(2,1)S(1)}, bf16[1024,128]{1,0:T(8,128)(2,1)}, u32[]{:S(2)}) %copy-start.15) | copy-done | bytes 262168
  21.1 0.7 %copy-done.16 = bf16[66,128]{1,0:T(8,128)(2,1)S(1)} copy-done((bf16[66,128]{1,0:T(8,128)(2,1)S(1)}, bf16[66,128]{1,0:T(8,128)(2,1)}, u32[]{:S(2)}) %copy-start.16) | copy-done | bytes 16920
  21.8 0.7 %copy-done.17 = s32[128]{0:T(128)S(1)} copy-done((s32[128]{0:T(128)S(1)}, s32[128]{0:T(128)}, u32[]{:S(2)}) %copy-start.17) | copy-done | bytes 536
  22.5 1.6 %base.1 = (f32[32,32,128]{2,1,0:T(8,128)S(1)}, bf16[4096,512]{1,0:T(8,128)(2,1)S(1)}) custom-call(bf16[32,32,128]{2,1,0:T(8,128)(2,1)S(1)} %copy-done.14, bf16[66,128]{1,0:T(8,128)(2,1)S(1)} %copy-done.16, s32[1,128]{1,0:T(1,128)S(1)} %bitcast.20, s32[128]{0:T(128)S(1)} %copy-done.17, bf16[1024,128]{1,0:T(8,128)(2,1)S(1)} %copy-done.15), custom_call_target="tpu_custom_call" | custom-call | flops 1073741824 | bytes 542208 | tf_op jit(solution)/shard_map/base/pallas_call | solution.py:237
  24.2 3.9 %edges.1 = (bf16[32,32,128]{2,1,0:T(8,128)(2,1)S(1)}, bf16[32,32,128]{2,1,0:T(8,128)(2,1)S(1)}, bf16[32,32,128]{2,1,0:T(8,128)(2,1)S(1)}, f32[1024,128]{1,0:T(8,128)S(1)}) custom-call(bf16[32,1152]{1,0:T(8,128)(2,1)S(1)} %get-tuple-element.13.refs_0_, bf16[32,1152]{1,0:T(8,128)(2,1)S(1)} %collective-permute-done.refs_1_, ...), custom_call_target="tpu_custom_call" | custom-call | bytes 5476864 | tf_op jit(solution)/shard_map/edges/pallas_call | solution.py:237
  28.2 0.5 collective-permute-start.9
  28.6 1.0 %collective-permute-start.8 = (bf16[32,32,128]{2,1,0:T(8,128)(2,1)S(1)}, bf16[32,32,128]{2,1,0:T(8,128)(2,1)S(1)}, u32[]{:S(2)}, u32[]{:S(2)}) collective-permute-start(bf16[32,32,128]{2,1,0:T(8,128)(2,1)S(1)} %get-tuple-element.17.refs_0_), channel_id=1, source_target_pairs={{0,2},{1,3},{2,0},{3,1},{4,6},{5,7},{6,4},{7,5},{8,10},{9,11},{10,... | collective-permute-start | bytes 786440 | tf_op jit(solution)/shard_map/ppermute | solution.py:220
  29.7 0.4 collective-permute-start.7
  30.1 2.3 %collective-permute-start.13 = (bf16[32,32,128]{2,1,0:T(8,128)(2,1)S(1)}, bf16[32,32,128]{2,1,0:T(8,128)(2,1)S(1)}, u32[]{:S(2)}, u32[]{:S(2)}) collective-permute-start(bf16[32,32,128]{2,1,0:T(8,128)(2,1)S(1)} %get-tuple-element.18), channel_id=1, source_target_pairs={{0,12},{1,8},{2,4},{3,0},{4,13},{5,9},{6,5},{7,1},{8,14},{9,10},{1... | collective-permute-start | bytes 786440 | tf_op jit(solution)/shard_map/ppermute | solution.py:226
  32.4 1.2 %collective-permute-start.12 = (bf16[32,32,128]{2,1,0:T(8,128)(2,1)S(1)}, bf16[32,32,128]{2,1,0:T(8,128)(2,1)S(1)}, u32[]{:S(2)}, u32[]{:S(2)}) collective-permute-start(bf16[32,32,128]{2,1,0:T(8,128)(2,1)S(1)} %get-tuple-element.18), channel_id=1, source_target_pairs={{0,8},{1,12},{2,0},{3,4},{4,9},{5,13},{6,1},{7,5},{8,10},{9,14},{1... | collective-permute-start | bytes 786440 | tf_op jit(solution)/shard_map/ppermute | solution.py:226
  33.6 6.0 %collective-permute-done.9.refs_3_ = bf16[32,32,128]{2,1,0:T(8,128)(2,1)S(1)} collective-permute-done((bf16[32,32,128]{2,1,0:T(8,128)(2,1)S(1)}, bf16[32,32,128]{2,1,0:T(8,128)(2,1)S(1)}, u32[]{:S(2)}, u32[]{:S(2)}) %collective-permute-start.9) | collective-permute-done | bytes 262176 | tf_op jit(solution)/shard_map/ppermute | solution.py:220
  39.7 2.8 %collective-permute-start.10 = (bf16[32,32,128]{2,1,0:T(8,128)(2,1)S(1)}, bf16[32,32,128]{2,1,0:T(8,128)(2,1)S(1)}, u32[]{:S(2)}, u32[]{:S(2)}) collective-permute-start(bf16[32,32,128]{2,1,0:T(8,128)(2,1)S(1)} %get-tuple-element.18), channel_id=1, source_target_pairs={{0,0},{1,4},{2,8},{3,12},{4,1},{5,5},{6,9},{7,13},{8,2},{9,6},{10,... | collective-permute-start | bytes 786440 | tf_op jit(solution)/shard_map/ppermute | solution.py:226
  42.5 2.3 %collective-permute-done.7.refs_1_ = bf16[32,32,128]{2,1,0:T(8,128)(2,1)S(1)} collective-permute-done((bf16[32,32,128]{2,1,0:T(8,128)(2,1)S(1)}, bf16[32,32,128]{2,1,0:T(8,128)(2,1)S(1)}, u32[]{:S(2)}, u32[]{:S(2)}) %collective-permute-start.7) | collective-permute-done | bytes 262176 | tf_op jit(solution)/shard_map/ppermute | solution.py:220
  44.8 1.3 %collective-permute-done.12.refs_6_ = bf16[32,32,128]{2,1,0:T(8,128)(2,1)S(1)} collective-permute-done((bf16[32,32,128]{2,1,0:T(8,128)(2,1)S(1)}, bf16[32,32,128]{2,1,0:T(8,128)(2,1)S(1)}, u32[]{:S(2)}, u32[]{:S(2)}) %collective-permute-start.12) | collective-permute-done | bytes 262176 | tf_op jit(solution)/shard_map/ppermute | solution.py:226
  46.1 7.9 %collective-permute-done.11.refs_5_ = bf16[32,32,128]{2,1,0:T(8,128)(2,1)S(1)} collective-permute-done((bf16[32,32,128]{2,1,0:T(8,128)(2,1)S(1)}, bf16[32,32,128]{2,1,0:T(8,128)(2,1)S(1)}, u32[]{:S(2)}, u32[]{:S(2)}) %collective-permute-start.11) | collective-permute-done | bytes 262176 | tf_op jit(solution)/shard_map/ppermute | solution.py:226
  54.1 2.6 %collective-permute-done.10.refs_4_ = bf16[32,32,128]{2,1,0:T(8,128)(2,1)S(1)} collective-permute-done((bf16[32,32,128]{2,1,0:T(8,128)(2,1)S(1)}, bf16[32,32,128]{2,1,0:T(8,128)(2,1)S(1)}, u32[]{:S(2)}, u32[]{:S(2)}) %collective-permute-start.10) | collective-permute-done | bytes 262176 | tf_op jit(solution)/shard_map/ppermute | solution.py:226
  56.6 6.0 %triangle.1 = bf16[32,32,128]{2,1,0:T(8,128)(2,1)} custom-call(bf16[32,32,128]{2,1,0:T(8,128)(2,1)S(1)} %get-tuple-element.17.refs_0_, bf16[32,32,128]{2,1,0:T(8,128)(2,1)S(1)} %collective-permute-done.7.refs_1_, bf16[32,32,128]{2,1,0:T(8,128)(2,1)S(1)} %collective-permute-done.8.refs_2_, bf16[32,32,128]{2,1,0:T(8,128)(2,1)S(1)} %collective-permute-done.9.refs_3_, ...), custom_call_target="tpu_custom_call" | custom-call | bytes 2917888 | tf_op jit(solution)/shard_map/triangle/pallas_call | solution.py:237
  (38 shorter events, 0.3 us)
Async XLA Ops:
  0.0 24.2 %copy-start.5 = (s32[128]{0:T(128)S(1)}, s32[128]{0:T(128)}, u32[]{:S(2)}) copy-start(s32[128]{0:T(128)} %refs_11_.1) | copy-start | bytes 1540
  0.0 24.2 %copy-start.10 = (f32[128]{0:T(128)S(1)}, f32[128]{0:T(128)}, u32[]{:S(2)}) copy-start(f32[128]{0:T(128)} %param.31) | copy-start | bytes 1540
  0.0 24.2 %copy-start.9 = (f32[128]{0:T(128)S(1)}, f32[128]{0:T(128)}, u32[]{:S(2)}) copy-start(f32[128]{0:T(128)} %param.30) | copy-start | bytes 1540
  0.9 1.0 %copy-start = (bf16[32,32,256]{2,1,0:T(8,128)(2,1)S(1)}, bf16[32,32,256]{2,1,0:T(8,128)(2,1)}, u32[]{:S(2)}) copy-start(bf16[32,32,256]{2,1,0:T(8,128)(2,1)} %x_ref.1) | copy-start | bytes 1572868
  2.0 0.7 %copy-start.3 = (s32[32,32]{1,0:T(8,128)S(1)}, s32[32,32]{1,0:T(8,128)}, u32[]{:S(2)}) copy-start(s32[32,32]{1,0:T(8,128)} %mask_ref.1) | copy-start | bytes 12292
  2.7 0.7 %copy-start.4 = (s32[128]{0:T(128)S(1)}, s32[128]{0:T(128)}, u32[]{:S(2)}) copy-start(s32[128]{0:T(128)} %refs_11_.1) | copy-start | bytes 1540
  3.3 0.7 %copy-start.6 = (f32[256]{0:T(256)S(1)}, f32[256]{0:T(256)}, u32[]{:S(2)}) copy-start(f32[256]{0:T(256)} %param.24) | copy-start | bytes 3076
  4.0 0.7 %copy-start.7 = (f32[256]{0:T(256)S(1)}, f32[256]{0:T(256)}, u32[]{:S(2)}) copy-start(f32[256]{0:T(256)} %param.25) | copy-start | bytes 3076
  4.7 0.7 %copy-start.8 = (f32[64]{0:T(128)S(1)}, f32[64]{0:T(128)}, u32[]{:S(2)}) copy-start(f32[64]{0:T(128)} %param.27) | copy-start | bytes 772
  5.4 18.9 %copy-start.1 = (bf16[128,640]{1,0:T(8,128)(2,1)S(1)}, bf16[128,640]{1,0:T(8,128)(2,1)}, u32[]{:S(2)}) copy-start(bf16[128,640]{1,0:T(8,128)(2,1)} %refs_14_.1) | copy-start | bytes 491524
  6.6 8.0 %collective-permute-start.2 = (bf16[32,1152]{1,0:T(8,128)(2,1)S(1)}, bf16[32,1152]{1,0:T(8,128)(2,1)S(1)}, u32[]{:S(2)}, u32[]{:S(2)}) collective-permute-start(bf16[32,1152]{1,0:T(8,128)(2,1)S(1)} %get-tuple-element.13.refs_0_), channel_id=1, source_target_pairs={{0,3},{1,2},{2,1},{3,0},{4,7},{5,6},{6,5},{7,4},{8,11},{9,10},{10,... | collective-permute-start | bytes 221192 | tf_op jit(solution)/shard_map/ppermute | solution.py:220
  9.2 6.6 %collective-permute-start.1 = (bf16[32,1152]{1,0:T(8,128)(2,1)S(1)}, bf16[32,1152]{1,0:T(8,128)(2,1)S(1)}, u32[]{:S(2)}, u32[]{:S(2)}) collective-permute-start(bf16[32,1152]{1,0:T(8,128)(2,1)S(1)} %get-tuple-element.13.refs_0_), channel_id=1, source_target_pairs={{0,2},{1,3},{2,0},{3,1},{4,6},{5,7},{6,4},{7,5},{8,10},{9,11},{10,... | collective-permute-start | bytes 221192 | tf_op jit(solution)/shard_map/ppermute | solution.py:220
  9.2 14.9 %collective-permute-start = (bf16[32,1152]{1,0:T(8,128)(2,1)S(1)}, bf16[32,1152]{1,0:T(8,128)(2,1)S(1)}, u32[]{:S(2)}, u32[]{:S(2)}) collective-permute-start(bf16[32,1152]{1,0:T(8,128)(2,1)S(1)} %get-tuple-element.13.refs_0_), channel_id=1, source_target_pairs={{0,1},{1,0},{2,3},{3,2},{4,5},{5,4},{6,7},{7,6},{8,9},{9,8},{10,11... | collective-permute-start | bytes 221192 | tf_op jit(solution)/shard_map/ppermute | solution.py:220
  9.4 14.7 %collective-permute-start.6 = (bf16[32,1152]{1,0:T(8,128)(2,1)S(1)}, bf16[32,1152]{1,0:T(8,128)(2,1)S(1)}, u32[]{:S(2)}, u32[]{:S(2)}) collective-permute-start(bf16[32,1152]{1,0:T(8,128)(2,1)S(1)} %get-tuple-element.14), channel_id=1, source_target_pairs={{0,12},{1,8},{2,4},{3,0},{4,13},{5,9},{6,5},{7,1},{8,14},{9,10},{1... | collective-permute-start | bytes 221192 | tf_op jit(solution)/shard_map/ppermute | solution.py:226
  11.5 12.7 %collective-permute-start.5 = (bf16[32,1152]{1,0:T(8,128)(2,1)S(1)}, bf16[32,1152]{1,0:T(8,128)(2,1)S(1)}, u32[]{:S(2)}, u32[]{:S(2)}) collective-permute-start(bf16[32,1152]{1,0:T(8,128)(2,1)S(1)} %get-tuple-element.14), channel_id=1, source_target_pairs={{0,8},{1,12},{2,0},{3,4},{4,9},{5,13},{6,1},{7,5},{8,10},{9,14},{1... | collective-permute-start | bytes 221192 | tf_op jit(solution)/shard_map/ppermute | solution.py:226
  14.6 9.6 %collective-permute-start.4 = (bf16[32,1152]{1,0:T(8,128)(2,1)S(1)}, bf16[32,1152]{1,0:T(8,128)(2,1)S(1)}, u32[]{:S(2)}, u32[]{:S(2)}) collective-permute-start(bf16[32,1152]{1,0:T(8,128)(2,1)S(1)} %get-tuple-element.14), channel_id=1, source_target_pairs={{0,4},{1,0},{2,12},{3,8},{4,5},{5,1},{6,13},{7,9},{8,6},{9,2},{10,... | collective-permute-start | bytes 221192 | tf_op jit(solution)/shard_map/ppermute | solution.py:226
  15.9 8.3 %collective-permute-start.3 = (bf16[32,1152]{1,0:T(8,128)(2,1)S(1)}, bf16[32,1152]{1,0:T(8,128)(2,1)S(1)}, u32[]{:S(2)}, u32[]{:S(2)}) collective-permute-start(bf16[32,1152]{1,0:T(8,128)(2,1)S(1)} %get-tuple-element.14), channel_id=1, source_target_pairs={{0,0},{1,4},{2,8},{3,12},{4,1},{5,5},{6,9},{7,13},{8,2},{9,6},{10,... | collective-permute-start | bytes 221192 | tf_op jit(solution)/shard_map/ppermute | solution.py:226
  19.2 1.0 %copy-start.14 = (bf16[32,32,128]{2,1,0:T(8,128)(2,1)S(1)}, bf16[32,32,128]{2,1,0:T(8,128)(2,1)}, u32[]{:S(2)}) copy-start(bf16[32,32,128]{2,1,0:T(8,128)(2,1)} %pair_ref.1) | copy-start | bytes 786436
  20.1 0.9 %copy-start.15 = (bf16[1024,128]{1,0:T(8,128)(2,1)S(1)}, bf16[1024,128]{1,0:T(8,128)(2,1)}, u32[]{:S(2)}) copy-start(bf16[1024,128]{1,0:T(8,128)(2,1)} %w_ref.2) | copy-start | bytes 786436
  21.1 0.7 %copy-start.16 = (bf16[66,128]{1,0:T(8,128)(2,1)S(1)}, bf16[66,128]{1,0:T(8,128)(2,1)}, u32[]{:S(2)}) copy-start(bf16[66,128]{1,0:T(8,128)(2,1)} %table_ref.1) | copy-start | bytes 50692
  21.8 0.7 %copy-start.17 = (s32[128]{0:T(128)S(1)}, s32[128]{0:T(128)}, u32[]{:S(2)}) copy-start(s32[128]{0:T(128)} %chain_smem.1) | copy-start | bytes 1540
  22.5 34.2 %copy-start.2 = (bf16[128,128]{1,0:T(8,128)(2,1)S(1)}, bf16[128,128]{1,0:T(8,128)(2,1)}, u32[]{:S(2)}) copy-start(bf16[128,128]{1,0:T(8,128)(2,1)} %refs_12_.1) | copy-start | bytes 98308
  22.5 34.2 %copy-start.11 = (f32[128]{0:T(128)S(1)}, f32[128]{0:T(128)}, u32[]{:S(2)}) copy-start(f32[128]{0:T(128)} %param.34) | copy-start | bytes 1540
  22.5 34.2 %copy-start.12 = (f32[128]{0:T(128)S(1)}, f32[128]{0:T(128)}, u32[]{:S(2)}) copy-start(f32[128]{0:T(128)} %param.35) | copy-start | bytes 1540
  22.5 34.2 %copy-start.13 = (f32[128]{0:T(128)S(1)}, f32[128]{0:T(128)}, u32[]{:S(2)}) copy-start(f32[128]{0:T(128)} %param.37) | copy-start | bytes 1540
  28.2 11.5 %collective-permute-start.9 = (bf16[32,32,128]{2,1,0:T(8,128)(2,1)S(1)}, bf16[32,32,128]{2,1,0:T(8,128)(2,1)S(1)}, u32[]{:S(2)}, u32[]{:S(2)}) collective-permute-start(bf16[32,32,128]{2,1,0:T(8,128)(2,1)S(1)} %get-tuple-element.17.refs_0_), channel_id=1, source_target_pairs={{0,3},{1,2},{2,1},{3,0},{4,7},{5,6},{6,5},{7,4},{8,11},{9,10},{10,... | collective-permute-start | bytes 786440 | tf_op jit(solution)/shard_map/ppermute | solution.py:220
  28.6 11.0 %collective-permute-start.8 = (bf16[32,32,128]{2,1,0:T(8,128)(2,1)S(1)}, bf16[32,32,128]{2,1,0:T(8,128)(2,1)S(1)}, u32[]{:S(2)}, u32[]{:S(2)}) collective-permute-start(bf16[32,32,128]{2,1,0:T(8,128)(2,1)S(1)} %get-tuple-element.17.refs_0_), channel_id=1, source_target_pairs={{0,2},{1,3},{2,0},{3,1},{4,6},{5,7},{6,4},{7,5},{8,10},{9,11},{10,... | collective-permute-start | bytes 786440 | tf_op jit(solution)/shard_map/ppermute | solution.py:220
  29.7 15.1 %collective-permute-start.7 = (bf16[32,32,128]{2,1,0:T(8,128)(2,1)S(1)}, bf16[32,32,128]{2,1,0:T(8,128)(2,1)S(1)}, u32[]{:S(2)}, u32[]{:S(2)}) collective-permute-start(bf16[32,32,128]{2,1,0:T(8,128)(2,1)S(1)} %get-tuple-element.17.refs_0_), channel_id=1, source_target_pairs={{0,1},{1,0},{2,3},{3,2},{4,5},{5,4},{6,7},{7,6},{8,9},{9,8},{10,11... | collective-permute-start | bytes 786440 | tf_op jit(solution)/shard_map/ppermute | solution.py:220
  30.1 14.7 %collective-permute-start.13 = (bf16[32,32,128]{2,1,0:T(8,128)(2,1)S(1)}, bf16[32,32,128]{2,1,0:T(8,128)(2,1)S(1)}, u32[]{:S(2)}, u32[]{:S(2)}) collective-permute-start(bf16[32,32,128]{2,1,0:T(8,128)(2,1)S(1)} %get-tuple-element.18), channel_id=1, source_target_pairs={{0,12},{1,8},{2,4},{3,0},{4,13},{5,9},{6,5},{7,1},{8,14},{9,10},{1... | collective-permute-start | bytes 786440 | tf_op jit(solution)/shard_map/ppermute | solution.py:226
  32.4 13.8 %collective-permute-start.12 = (bf16[32,32,128]{2,1,0:T(8,128)(2,1)S(1)}, bf16[32,32,128]{2,1,0:T(8,128)(2,1)S(1)}, u32[]{:S(2)}, u32[]{:S(2)}) collective-permute-start(bf16[32,32,128]{2,1,0:T(8,128)(2,1)S(1)} %get-tuple-element.18), channel_id=1, source_target_pairs={{0,8},{1,12},{2,0},{3,4},{4,9},{5,13},{6,1},{7,5},{8,10},{9,14},{1... | collective-permute-start | bytes 786440 | tf_op jit(solution)/shard_map/ppermute | solution.py:226
  39.6 14.4 %collective-permute-start.11 = (bf16[32,32,128]{2,1,0:T(8,128)(2,1)S(1)}, bf16[32,32,128]{2,1,0:T(8,128)(2,1)S(1)}, u32[]{:S(2)}, u32[]{:S(2)}) collective-permute-start(bf16[32,32,128]{2,1,0:T(8,128)(2,1)S(1)} %get-tuple-element.18), channel_id=1, source_target_pairs={{0,4},{1,0},{2,12},{3,8},{4,5},{5,1},{6,13},{7,9},{8,6},{9,2},{10,... | collective-permute-start | bytes 786440 | tf_op jit(solution)/shard_map/ppermute | solution.py:226
  39.7 17.0 %collective-permute-start.10 = (bf16[32,32,128]{2,1,0:T(8,128)(2,1)S(1)}, bf16[32,32,128]{2,1,0:T(8,128)(2,1)S(1)}, u32[]{:S(2)}, u32[]{:S(2)}) collective-permute-start(bf16[32,32,128]{2,1,0:T(8,128)(2,1)S(1)} %get-tuple-element.18), channel_id=1, source_target_pairs={{0,0},{1,4},{2,8},{3,12},{4,1},{5,5},{6,9},{7,13},{8,2},{9,6},{10,... | collective-permute-start | bytes 786440 | tf_op jit(solution)/shard_map/ppermute | solution.py:226

commit v4 on v3

--- a/solution.py
+++ b/solution.py
@@ -35,26 +35,30 @@
     return centred * lax.rsqrt(variance + 1e-05) * gain + shift
 
 
+def norm_kernel(x_ref, out_ref):
+    x = x_ref[...].reshape(out_ref.shape).astype(F32)
+    out_ref[...] = layer_norm(x, 1.0, 0.0)
+
+
 def pack_kernel(x_ref, mask_ref, res_ref, gain_ref, shift_ref, w_ref, bias_ref,
                 left_ref, right_ref, lscr, rscr):
-    seqs, rows, depth = x_ref.shape
-    half = w_ref.shape[1] // 2
+    seqs, rows = mask_ref.shape
+    half = w_ref.shape[0] // 2
     per = LANES // half
     row_start = lax.axis_index("resi") * rows
-    x = x_ref[...].reshape(seqs * rows, depth).astype(F32)
-    normed = layer_norm(x, gain_ref[...], shift_ref[...]).astype(BF16)
+    normed = (x_ref[...] * gain_ref[...] + shift_ref[...]).astype(BF16)
     lane = iota((2 * half, 2 * LANES), 1)
     spread = lane % half + jnp.where(lane >= LANES, half, 0) == iota((2 * half, 2 * LANES), 0)
     spread = spread.astype(F32)
-    wide = dot(w_ref[...], spread.astype(BF16)).astype(BF16)
+    wide = lax.dot_general(
+        w_ref[...], spread.astype(BF16), (((0,), (0,)), ((), ())), preferred_element_type=F32)
+    wide = wide.astype(BF16)
     bias = jnp.dot(jnp.broadcast_to(bias_ref[...], (8, 2 * half)), spread,
                    precision=lax.Precision.HIGHEST, preferred_element_type=F32)[0:1]
     mapped = dot(normed, wide)
     lscr[...] = mapped[:, :LANES]
     rscr[...] = mapped[:, LANES:]
-    total = res_ref.shape[1]
-    pick = (iota((total, rows), 0) == iota((total, rows), 1) + row_start).astype(BF16)
-    row_live = dot(jnp.broadcast_to(res_ref[...].astype(F32), (8, total)).astype(BF16), pick)[0:1]
+    row_live = pick_rows(res_ref[...], row_start, rows)
     live = (mask_ref[...].astype(F32) * row_live).astype(BF16)
     width = rows * half
     spread_live = (iota((rows, width), 1) // half == iota((rows, width), 0)).astype(BF16)
@@ -73,24 +77,33 @@
     right_ref[:, width:] = live_tile.astype(BF16)
 
 
-def base_kernel(pair_ref, table_ref, chain_ref, chain_smem, w_ref, base_ref, block_ref, tscr, wscr):
+def pick_columns(values, start, size):
+    total = values.shape[1]
+    own = iota((size, total), 1) == iota((size, total), 0) + start
+    spread = jnp.broadcast_to(values, (size, total)).astype(F32)
+    return jnp.sum(jnp.where(own, spread, 0.0), axis=1, keepdims=True)
+
+
+def pick_rows(values, start, size):
+    total = values.shape[1]
+    pick = (iota((total, size), 0) == iota((total, size), 1) + start).astype(BF16)
+    return dot(jnp.broadcast_to(values.astype(F32), (8, total)).astype(BF16), pick)[0:1]
+
+
+def base_kernel(pair_ref, table_ref, chain_ref, w_ref, base_ref, block_ref, tscr, wscr):
     rows, cols, channels = pair_ref.shape
-    total = chain_ref.shape[1]
     row_start = lax.axis_index("resi") * rows
     col_start = lax.axis_index(PLANE) * cols
     tscr[...] = jnp.zeros_like(tscr)
     tscr[0:table_ref.shape[0], :] = table_ref[...].astype(F32)
     table = tscr[...].astype(BF16)
-    own = iota((cols, total), 1) == iota((cols, total), 0) + col_start
-    chain_cols = jnp.sum(
-        jnp.where(own, jnp.broadcast_to(chain_ref[...], (cols, total)).astype(F32), 0.0),
-        axis=1, keepdims=True)
-    col_pos = iota((cols, 1), 0) + col_start
+    chain = chain_ref[...]
+    same = pick_columns(chain, col_start, cols) == pick_rows(chain, row_start, rows)
+    offset = iota((cols, rows), 0) + col_start - iota((cols, rows), 1) - row_start + RELMAX
+    bins = jnp.where(same, jnp.clip(offset, 0, 2 * RELMAX), 2 * RELMAX + 1)
+    lane = iota((cols, LANES), 1)
     for i in range(rows):
-        offset = jnp.clip(col_pos - (row_start + i) + RELMAX, 0, 2 * RELMAX)
-        same = chain_cols == chain_smem[row_start + i].astype(F32)
-        bins = jnp.where(same, offset, 2 * RELMAX + 1)
-        one_hot = (iota((cols, LANES), 1) == bins).astype(F32).astype(BF16)
+        one_hot = (lane == bins[:, i:i + 1]).astype(F32).astype(BF16)
         base_ref[i] = pair_ref[i].astype(F32) + dot(one_hot, table)
     wscr[...] = w_ref[...].astype(F32)
     half = int(round(w_ref.shape[0] ** 0.5))
@@ -104,7 +117,7 @@
 
 def edges_kernel(count, *refs):
     lefts, rights = refs[:count], refs[count:2 * count]
-    (base_ref, block_ref, res_ref, res_smem, gain_ref, shift_ref, w_ref, bias_ref,
+    (base_ref, block_ref, res_ref, gain_ref, shift_ref, w_ref, bias_ref,
      updated_ref, left_ref, right_ref, gate_ref,
      lall, rall, tscr, rscr, oscr, nscr, escr) = refs[2 * count:]
     rows, cols, channels = base_ref.shape
@@ -150,12 +163,7 @@
         updated_ref[i] = updated
         normed = layer_norm(updated.astype(F32), gain_ref[...], shift_ref[...])
         nscr[i * cols:(i + 1) * cols, :] = normed.astype(BF16)
-    total = res_ref.shape[1]
-    own = iota((cols, total), 1) == iota((cols, total), 0) + col_start
-    col_live = jnp.sum(
-        jnp.where(own, jnp.broadcast_to(res_ref[...], (cols, total)).astype(F32), 0.0),
-        axis=1, keepdims=True)
-    col_live = jnp.broadcast_to(col_live, (cols, channels))
+    live = pick_columns(res_ref[...], col_start, cols) * pick_rows(res_ref[...], row_start, rows)
     chunk = 8
     for i0 in range(0, rows, chunk):
         mixture = dot(nscr[i0 * cols:(i0 + chunk) * cols, :], w_ref[...]) + bias_ref[...]
@@ -164,47 +172,59 @@
         right_edge = sigmoid(part[2]) * part[3]
         gate_ref[i0 * cols:(i0 + chunk) * cols, :] = sigmoid(part[4])
         for ii in range(chunk):
-            live = col_live * res_smem[row_start + i0 + ii].astype(F32)
+            here = live[:, i0 + ii:i0 + ii + 1]
             at = slice(ii * cols, (ii + 1) * cols)
-            left_ref[i0 + ii] = (left_edge[at] * live).astype(BF16)
-            escr[(i0 + ii) * cols:(i0 + ii + 1) * cols, :] = right_edge[at] * live
+            left_ref[i0 + ii] = (left_edge[at] * here).astype(BF16)
+            escr[(i0 + ii) * cols:(i0 + ii + 1) * cols, :] = right_edge[at] * here
     for k in range(cols):
         right_ref[k] = escr[pl.ds(k, rows, stride=cols), :].astype(BF16)
 
 
-def triangle_kernel(count, *refs):
-    lefts, rights = refs[:count], refs[count:2 * count]
-    (updated_ref, gate_ref, gain_ref, shift_ref, w_ref, bias_ref,
-     out_ref, lscr, rscr, acc) = refs[2 * count:]
-    rows, depth, channels = lefts[0].shape
-    cols = rights[0].shape[1]
-    turn = lax.axis_index("resi") ^ lax.axis_index(PLANE)
+def panel_kernel(count, *refs):
+    lefts, panel_ref = refs[:count], refs[count]
+    q = lax.axis_index(PLANE)
     for step in range(count):
-        lscr[step] = lefts[step][...].astype(F32).reshape(rows * depth, channels)
-        rscr[step] = rights[step][...].astype(F32).reshape(depth * cols, channels)
+        panel_ref[q ^ step] = lefts[step][...].astype(F32).reshape(panel_ref.shape[1:])
+
+
+def add_block(step, panel_ref, right_ref, rscr, before, store):
+    depth, cols, channels = right_ref.shape
+    rows = panel_ref.shape[1] // depth
+    own = lax.axis_index("resi") ^ step
+    rscr[...] = right_ref[...].astype(F32).reshape(rscr.shape)
     block = 4
     tiles = cols // 8
 
     def rows_body(at, carry):
-        sums = [[jnp.zeros((8, channels), F32) for _ in range(tiles)] for _ in range(block)]
-
-        def step_body(step, sums):
-            own = step ^ turn
-            for k in range(depth):
-                column = [rscr[step, k * cols + t * 8:k * cols + t * 8 + 8, :] for t in range(tiles)]
-                for b in range(block):
-                    row = lscr[own, pl.ds((at * block + b) * depth + k, 1), :]
-                    for t in range(tiles):
-                        sums[b][t] = sums[b][t] + row * column[t]
-            return sums
-
-        sums = lax.fori_loop(0, count, step_body, sums)
+        place = [[pl.ds(pl.multiple_of((at * block + b) * cols + t * 8, 8), 8) for t in range(tiles)]
+                 for b in range(block)]
+        if before is None:
+            sums = [[jnp.zeros((8, channels), F32) for _ in range(tiles)] for _ in range(block)]
+        else:
+            sums = [[before[place[b][t], :] for t in range(tiles)] for b in range(block)]
+        for k in range(depth):
+            column = [rscr[k * cols + t * 8:k * cols + t * 8 + 8, :] for t in range(tiles)]
+            for b in range(block):
+                row = panel_ref[own, pl.ds((at * block + b) * depth + k, 1), :]
+                for t in range(tiles):
+                    sums[b][t] = sums[b][t] + row * column[t]
         for b in range(block):
             for t in range(tiles):
-                acc[pl.ds(pl.multiple_of((at * block + b) * cols + t * 8, 8), 8), :] = sums[b][t]
+                store[place[b][t], :] = sums[b][t]
         return carry
 
     lax.fori_loop(0, rows // block, rows_body, 0)
+
+
+def step_kernel(step, panel_ref, right_ref, *refs):
+    before = refs[0] if len(refs) == 3 else None
+    add_block(step, panel_ref, right_ref, refs[-1], before, refs[-2])
+
+
+def final_kernel(step, panel_ref, right_ref, before, updated_ref, gate_ref, gain_ref, shift_ref,
+                 w_ref, bias_ref, out_ref, acc, rscr):
+    add_block(step, panel_ref, right_ref, rscr, before, acc)
+    rows, cols, channels = out_ref.shape
     chunk = 8
     for i0 in range(0, rows, chunk):
         at = slice(i0 * cols, (i0 + chunk) * cols)
@@ -216,9 +236,12 @@
 
 
 def send_plane(block, count):
-    return [block] + [
-        lax.ppermute(block, PLANE, [(p, p ^ m) for p in range(count)]) for m in range(1, count)
-    ]
+    parts, bit = [block], 1
+    while bit < count:
+        pairs = [(p, p ^ bit) for p in range(count)]
+        parts += [lax.ppermute(part, PLANE, pairs) for part in parts]
+        bit *= 2
+    return parts
 
 
 def send_turned(block, count):
@@ -230,14 +253,13 @@
     ]
 
 
-def call(kernel, outs, scratch, args, smem=(), flops=0, name=None):
+def call(kernel, outs, scratch, args, flops=0, name=None):
     vmem = pl.BlockSpec(memory_space=pltpu.VMEM)
-    specs = [pl.BlockSpec(memory_space=pltpu.SMEM) if n in smem else vmem for n in range(len(args))]
     size = sum(a.size * a.dtype.itemsize for a in args)
     return pl.pallas_call(
         kernel,
         out_shape=outs,
-        in_specs=specs,
+        in_specs=[vmem] * len(args),
         out_specs=[vmem] * len(outs) if isinstance(outs, list) else vmem,
         scratch_shapes=scratch,
         compiler_params=pltpu.CompilerParams(vmem_limit_bytes=40 * MIB),
@@ -278,20 +300,22 @@
     residue = flat(residue_pad_mask)
     chain = flat(residue_chain_index)
     pack = shape((seqs, width + LANES), BF16)
+    normed = call(norm_kernel, shape((seqs * rows, depth), F32), [], [homolog_matrix],
+                  flops=1 << 36, name="norm")
     left, right = call(
         pack_kernel, [pack, pack],
         [pltpu.VMEM((seqs * rows, LANES), F32)] * 2,
-        [homolog_matrix, sequence_pad_mask, residue, flat(homolog_standard_factor),
-         flat(homolog_standard_offset), factor_mapping_matrices, flat(outer_side_biases)],
-        name="pack")
+        [normed, sequence_pad_mask, residue, flat(homolog_standard_factor),
+         flat(homolog_standard_offset), factor_mapping_matrices.T, flat(outer_side_biases)],
+        flops=1 << 30, name="pack")
     rights = send_turned(right, count)
     lefts = send_plane(left, count)
     base, block = call(
         base_kernel,
         [shape((rows, cols, channels), F32), shape((half * LANES, per * channels), BF16)],
         [pltpu.VMEM((LANES, channels), F32), pltpu.VMEM((half * half, channels), F32)],
-        [pair_features, relative_position_table, chain, residue_chain_index, outer_pair_projection],
-        smem=(3,), flops=1 << 30, name="base")
+        [pair_features, relative_position_table, chain, outer_pair_projection],
+        flops=1 << 30, name="base")
     updated, left_edge, right_edge, gate = call(
         functools.partial(edges_kernel, count),
         [shape((rows, cols, channels), BF16), shape((rows, cols, channels), BF16),
@@ -301,21 +325,27 @@
          pltpu.VMEM((width, count * seqs), BF16),
          pltpu.VMEM((rows // per * cols, half * LANES), BF16),
          pltpu.VMEM((rows * cols, channels), BF16), pltpu.VMEM((rows * cols, channels), F32)],
-        lefts + rights + [base, block, residue, residue_pad_mask, flat(pair_norm_gain),
-                          flat(pair_norm_bias), triangle_projection_weights,
-                          flat(triangle_projection_biases)],
-        smem=(2 * count + 3,), name="edges")
+        lefts + rights + [base, block, residue, flat(pair_norm_gain), flat(pair_norm_bias),
+                          triangle_projection_weights, flat(triangle_projection_biases)],
+        name="edges")
     right_edges = send_turned(right_edge, count)
     left_edges = send_plane(left_edge, count)
+    sums = shape((rows * cols, channels), F32)
+    turned = pltpu.VMEM((rows * cols, channels), F32)
+    panel = call(
+        functools.partial(panel_kernel, count), shape((count, rows * cols, channels), F32), [],
+        left_edges, name="panel")
+    args = []
+    for step in range(count - 1):
+        args = [call(functools.partial(step_kernel, step), sums, [turned],
+                     [panel, right_edges[step]] + args, name="triangle")]
     return call(
-        functools.partial(triangle_kernel, count),
-        shape((rows, cols, channels), BF16),
-        [pltpu.VMEM((count, rows * cols, channels), F32), pltpu.VMEM((count, rows * cols, channels), F32),
-         pltpu.VMEM((rows * cols, channels), F32)],
-        left_edges + right_edges + [updated, gate, flat(triangle_sum_norm_gain),
-                                    flat(triangle_sum_norm_bias), triangle_output_weight,
-                                    flat(outer_pair_bias)],
-        name="triangle")
+        functools.partial(final_kernel, count - 1), shape((rows, cols, channels), BF16),
+        [turned, turned],
+        [panel, right_edges[-1]] + args + [
+            updated, gate, flat(triangle_sum_norm_gain), flat(triangle_sum_norm_bias),
+            triangle_output_weight, flat(outer_pair_bias)],
+        name="final")
 
 
 def solution(mesh):

time: 63.1 us -> 62.9 us (level)
  local copies, waits for them, and re-layouts: 9.32 us -> 1.39 us
  starting transfers between devices: 20.2 us -> 23.5 us
  waiting for transfers between devices: 20.2 us -> 23.5 us
  Pallas kernels: 12.8 us -> 14 us
    ppermute x8, waiting for transfers between devices: 11.8 us -> 19.3 us  [send_turned(): lax.ppermute(block, GROUP, [(z * count + p, (p ^ m) * count + z) for z in...]
    unnamed x37 -> x38, local copies, waits for them, and re-layouts: 8.63 us -> 1.39 us
    ppermute x6, waiting for transfers between devices: 8.33 us -> 4.19 us  [send_plane(): parts += [lax.ppermute(part, PLANE, pairs) for part in parts]]
    ppermute x6, starting transfers between devices: 4.8 us -> 8.27 us  [send_plane(): parts += [lax.ppermute(part, PLANE, pairs) for part in parts]]
    pallas_call x4 -> x9, Pallas kernels: 12.8 us -> 14 us  [call(): pl.pallas_call(kernel, out_shape=outs, in_specs=[vmem] * len(args), out_s...]
    reshape x1, local copies, waits for them, and re-layouts: 0.69 us -> 0.01 us  [body(): flat = lambda v: v.reshape(1, -1)]
  transfers between devices with their start and end apart: 14 -> 14, of which waited for: 5 -> 4; matrix products, arithmetic and copies ran while one was open for 1% -> 0% of each run, Pallas kernels for 3% -> 10%
where the time goes in v4:
time: 62.9 us; the launch traced here: 62.7 us
  starting transfers between devices  23.5 us (37%)
  waiting for transfers between devices  23.5 us (37%)
  Pallas kernels  14 us (22%)
  local copies, waits for them, and re-layouts  1.39 us (2%)
    ppermute x8, waiting for transfers between devices, send_turned(): lax.ppermute(block, GROUP, [(z * count + p, (p ^ m) * count + z) for z in...  19.3 us
    ppermute x8, starting transfers between devices, send_turned(): lax.ppermute(block, GROUP, [(z * count + p, (p ^ m) * count + z) for z in...  15.2 us
    pallas_call x9, Pallas kernels, call(): pl.pallas_call(kernel, out_shape=outs, in_specs=[vmem] * len(args), out_s...  14 us
    ppermute x6, starting transfers between devices, send_plane(): parts += [lax.ppermute(part, PLANE, pairs) for part in parts]  8.27 us
    ppermute x6, waiting for transfers between devices, send_plane(): parts += [lax.ppermute(part, PLANE, pairs) for part in parts]  4.19 us
    unnamed x38, local copies, waits for them, and re-layouts  1.39 us
  transfers between devices with their start and end apart: 14, of which 4 were waited for; matrix products, arithmetic and copies ran while one was open for 0% of the time, Pallas kernels for 10%

profile of v4, /device:TPU:1, one launch (start us, length us, event | category | flops | bytes accessed | tf_op | source)
XLA Modules:
  0.0 62.7 jit_solution(9770625023165226803)
XLA Ops:
  0.0 1.1 %copy-done.8 = bf16[32,32,256]{2,1,0:T(8,128)(2,1)S(1)} copy-done((bf16[32,32,256]{2,1,0:T(8,128)(2,1)S(1)}, bf16[32,32,256]{2,1,0:T(8,128)(2,1)}, u32[]{:S(2)}) %copy-start.8) | copy-done | bytes 524312
  1.1 0.4 norm.1.x_ref
  1.5 0.0 copy-start
  1.5 0.0 copy-start.3
  1.5 0.0 copy-start.4
  1.6 0.3 copy-done.11
  1.8 1.1 %pack.1 = (bf16[32,1152]{1,0:T(8,128)(2,1)S(1)}, bf16[32,1152]{1,0:T(8,128)(2,1)S(1)}) custom-call(f32[1024,256]{1,0:T(8,128)S(1)} %norm.1.x_ref, s32[32,32]{1,0:T(8,128)S(1)} %copy-done.13, s32[1,128]{1,0:T(1,128)S(1)} %bitcast.11, f32[1,256]{1,0:T(1,128)S(1)} %bitcast.19, f32[1,256]{1,0:T(1,128)S(1)} %bitcast.20, bf16[64,256]{1,0:T(8,128)(2,1)S(1)} %bitcast.18, ...), custom_call_target="tpu_custom_call" | custom-call | flops 1073741824 | bytes 1088256 | tf_op jit(solution)/shard_map/pack/pallas_call | solution.py:259
  2.9 0.1 collective-permute-start.1
  3.0 2.7 %collective-permute-start = (bf16[32,1152]{1,0:T(8,128)(2,1)S(1)}, bf16[32,1152]{1,0:T(8,128)(2,1)S(1)}, u32[]{:S(2)}, u32[]{:S(2)}) collective-permute-start(bf16[32,1152]{1,0:T(8,128)(2,1)S(1)} %get-tuple-element.13.refs_0_), channel_id=1, source_target_pairs={{0,1},{1,0},{2,3},{3,2},{4,5},{5,4},{6,7},{7,6},{8,9},{9,8},{10,11... | collective-permute-start | bytes 221192 | tf_op jit(solution)/shard_map/ppermute | solution.py:242
  5.7 1.5 %collective-permute-start.6 = (bf16[32,1152]{1,0:T(8,128)(2,1)S(1)}, bf16[32,1152]{1,0:T(8,128)(2,1)S(1)}, u32[]{:S(2)}, u32[]{:S(2)}) collective-permute-start(bf16[32,1152]{1,0:T(8,128)(2,1)S(1)} %get-tuple-element.14), channel_id=1, source_target_pairs={{0,12},{1,8},{2,4},{3,0},{4,13},{5,9},{6,5},{7,1},{8,14},{9,10},{1... | collective-permute-start | bytes 221192 | tf_op jit(solution)/shard_map/ppermute | solution.py:249
  7.2 2.4 %collective-permute-start.5 = (bf16[32,1152]{1,0:T(8,128)(2,1)S(1)}, bf16[32,1152]{1,0:T(8,128)(2,1)S(1)}, u32[]{:S(2)}, u32[]{:S(2)}) collective-permute-start(bf16[32,1152]{1,0:T(8,128)(2,1)S(1)} %get-tuple-element.14), channel_id=1, source_target_pairs={{0,8},{1,12},{2,0},{3,4},{4,9},{5,13},{6,1},{7,5},{8,10},{9,14},{1... | collective-permute-start | bytes 221192 | tf_op jit(solution)/shard_map/ppermute | solution.py:249
  9.7 0.8 %collective-permute-start.4 = (bf16[32,1152]{1,0:T(8,128)(2,1)S(1)}, bf16[32,1152]{1,0:T(8,128)(2,1)S(1)}, u32[]{:S(2)}, u32[]{:S(2)}) collective-permute-start(bf16[32,1152]{1,0:T(8,128)(2,1)S(1)} %get-tuple-element.14), channel_id=1, source_target_pairs={{0,4},{1,0},{2,12},{3,8},{4,5},{5,1},{6,13},{7,9},{8,6},{9,2},{10,... | collective-permute-start | bytes 221192 | tf_op jit(solution)/shard_map/ppermute | solution.py:249
  10.5 3.8 %collective-permute-start.3 = (bf16[32,1152]{1,0:T(8,128)(2,1)S(1)}, bf16[32,1152]{1,0:T(8,128)(2,1)S(1)}, u32[]{:S(2)}, u32[]{:S(2)}) collective-permute-start(bf16[32,1152]{1,0:T(8,128)(2,1)S(1)} %get-tuple-element.14), channel_id=1, source_target_pairs={{0,0},{1,4},{2,8},{3,12},{4,1},{5,5},{6,9},{7,13},{8,2},{9,6},{10,... | collective-permute-start | bytes 221192 | tf_op jit(solution)/shard_map/ppermute | solution.py:249
  14.3 0.1 collective-permute-start.2
  14.4 1.2 %base.1 = (f32[32,32,128]{2,1,0:T(8,128)S(1)}, bf16[4096,512]{1,0:T(8,128)(2,1)S(1)}) custom-call(bf16[32,32,128]{2,1,0:T(8,128)(2,1)S(1)} %copy-done.9, bf16[66,128]{1,0:T(8,128)(2,1)S(1)} %copy-done.12, s32[1,128]{1,0:T(1,128)S(1)} %bitcast.22, bf16[1024,128]{1,0:T(8,128)(2,1)S(1)} %copy-done.10), custom_call_target="tpu_custom_call" | custom-call | flops 1073741824 | bytes 541696 | tf_op jit(solution)/shard_map/base/pallas_call | solution.py:259
  15.6 1.5 %collective-permute-done.3.refs_4_ = bf16[32,1152]{1,0:T(8,128)(2,1)S(1)} collective-permute-done((bf16[32,1152]{1,0:T(8,128)(2,1)S(1)}, bf16[32,1152]{1,0:T(8,128)(2,1)S(1)}, u32[]{:S(2)}, u32[]{:S(2)}) %collective-permute-start.3) | collective-permute-done | bytes 73760 | tf_op jit(solution)/shard_map/ppermute | solution.py:249
  17.2 3.8 %edges.1 = (bf16[32,32,128]{2,1,0:T(8,128)(2,1)S(1)}, bf16[32,32,128]{2,1,0:T(8,128)(2,1)S(1)}, bf16[32,32,128]{2,1,0:T(8,128)(2,1)S(1)}, f32[1024,128]{1,0:T(8,128)S(1)}) custom-call(bf16[32,1152]{1,0:T(8,128)(2,1)S(1)} %get-tuple-element.13.refs_0_, bf16[32,1152]{1,0:T(8,128)(2,1)S(1)} %collective-permute-done.refs_1_, ...), custom_call_target="tpu_custom_call" | custom-call | bytes 5476352 | tf_op jit(solution)/shard_map/edges/pallas_call | solution.py:259
  20.9 2.3 %collective-permute-start.7 = (bf16[32,32,128]{2,1,0:T(8,128)(2,1)S(1)}, bf16[32,32,128]{2,1,0:T(8,128)(2,1)S(1)}, u32[]{:S(2)}, u32[]{:S(2)}) collective-permute-start(bf16[32,32,128]{2,1,0:T(8,128)(2,1)S(1)} %get-tuple-element.17.refs_0_), channel_id=1, source_target_pairs={{0,1},{1,0},{2,3},{3,2},{4,5},{5,4},{6,7},{7,6},{8,9},{9,8},{10,11... | collective-permute-start | bytes 786440 | tf_op jit(solution)/shard_map/ppermute | solution.py:242
  23.2 1.4 %collective-permute-start.8 = (bf16[32,32,128]{2,1,0:T(8,128)(2,1)S(1)}, bf16[32,32,128]{2,1,0:T(8,128)(2,1)S(1)}, u32[]{:S(2)}, u32[]{:S(2)}) collective-permute-start(bf16[32,32,128]{2,1,0:T(8,128)(2,1)S(1)} %get-tuple-element.17.refs_0_), channel_id=1, source_target_pairs={{0,2},{1,3},{2,0},{3,1},{4,6},{5,7},{6,4},{7,5},{8,10},{9,11},{10,... | collective-permute-start | bytes 786440 | tf_op jit(solution)/shard_map/ppermute | solution.py:242
  24.6 4.2 %collective-permute-done.7.refs_1_ = bf16[32,32,128]{2,1,0:T(8,128)(2,1)S(1)} collective-permute-done((bf16[32,32,128]{2,1,0:T(8,128)(2,1)S(1)}, bf16[32,32,128]{2,1,0:T(8,128)(2,1)S(1)}, u32[]{:S(2)}, u32[]{:S(2)}) %collective-permute-start.7) | collective-permute-done | bytes 262176 | tf_op jit(solution)/shard_map/ppermute | solution.py:242
  28.8 1.7 %collective-permute-start.9 = (bf16[32,32,128]{2,1,0:T(8,128)(2,1)S(1)}, bf16[32,32,128]{2,1,0:T(8,128)(2,1)S(1)}, u32[]{:S(2)}, u32[]{:S(2)}) collective-permute-start(bf16[32,32,128]{2,1,0:T(8,128)(2,1)S(1)} %collective-permute-done.7.refs_1_), channel_id=1, source_target_pairs={{0,2},{1,3},{2,0},{3,1},{4,6},{5,7},{6,4},{7,5},{8,10},{9,11},{10,... | collective-permute-start | bytes 786440 | tf_op jit(solution)/shard_map/ppermute | solution.py:242
  30.5 1.9 %collective-permute-start.13 = (bf16[32,32,128]{2,1,0:T(8,128)(2,1)S(1)}, bf16[32,32,128]{2,1,0:T(8,128)(2,1)S(1)}, u32[]{:S(2)}, u32[]{:S(2)}) collective-permute-start(bf16[32,32,128]{2,1,0:T(8,128)(2,1)S(1)} %get-tuple-element.18), channel_id=1, source_target_pairs={{0,0},{1,4},{2,8},{3,12},{4,1},{5,5},{6,9},{7,13},{8,2},{9,6},{10,... | collective-permute-start | bytes 786440 | tf_op jit(solution)/shard_map/ppermute | solution.py:249
  32.4 4.8 %collective-permute-start.12 = (bf16[32,32,128]{2,1,0:T(8,128)(2,1)S(1)}, bf16[32,32,128]{2,1,0:T(8,128)(2,1)S(1)}, u32[]{:S(2)}, u32[]{:S(2)}) collective-permute-start(bf16[32,32,128]{2,1,0:T(8,128)(2,1)S(1)} %get-tuple-element.18), channel_id=1, source_target_pairs={{0,4},{1,0},{2,12},{3,8},{4,5},{5,1},{6,13},{7,9},{8,6},{9,2},{10,... | collective-permute-start | bytes 786440 | tf_op jit(solution)/shard_map/ppermute | solution.py:249
  37.2 0.1 panel.1.panel_ref
  37.4 0.0 copy-start.5
  37.4 0.0 copy-start.6
  37.4 13.0 %collective-permute-done.13.right_ref = bf16[32,32,128]{2,1,0:T(8,128)(2,1)S(1)} collective-permute-done((bf16[32,32,128]{2,1,0:T(8,128)(2,1)S(1)}, bf16[32,32,128]{2,1,0:T(8,128)(2,1)S(1)}, u32[]{:S(2)}, u32[]{:S(2)}) %collective-permute-start.13) | collective-permute-done | bytes 262176 | tf_op jit(solution)/shard_map/ppermute | solution.py:249
  50.4 1.6 %triangle.3.refs_0_ = f32[1024,128]{1,0:T(8,128)S(1)} custom-call(f32[4,1024,128]{2,1,0:T(8,128)S(1)} %panel.1.panel_ref, bf16[32,32,128]{2,1,0:T(8,128)(2,1)S(1)} %collective-permute-done.13.right_ref), custom_call_target="tpu_custom_call" | custom-call | bytes 2359296 | tf_op jit(solution)/shard_map/triangle/pallas_call | solution.py:259
  52.0 4.8 %collective-permute-done.12.right_ref = bf16[32,32,128]{2,1,0:T(8,128)(2,1)S(1)} collective-permute-done((bf16[32,32,128]{2,1,0:T(8,128)(2,1)S(1)}, bf16[32,32,128]{2,1,0:T(8,128)(2,1)S(1)}, u32[]{:S(2)}, u32[]{:S(2)}) %collective-permute-start.12) | collective-permute-done | bytes 262176 | tf_op jit(solution)/shard_map/ppermute | solution.py:249
  56.7 1.6 %triangle.4.refs_0_ = f32[1024,128]{1,0:T(8,128)S(1)} custom-call(f32[4,1024,128]{2,1,0:T(8,128)S(1)} %panel.1.panel_ref, bf16[32,32,128]{2,1,0:T(8,128)(2,1)S(1)} %collective-permute-done.12.right_ref, f32[1024,128]{1,0:T(8,128)S(1)} %triangle.3.refs_0_), custom_call_target="tpu_custom_call" | custom-call | bytes 2883584 | tf_op jit(solution)/shard_map/triangle/pallas_call | solution.py:259
  58.3 1.6 %triangle.5.before = f32[1024,128]{1,0:T(8,128)S(1)} custom-call(f32[4,1024,128]{2,1,0:T(8,128)S(1)} %panel.1.panel_ref, bf16[32,32,128]{2,1,0:T(8,128)(2,1)S(1)} %collective-permute-done.11.right_ref, f32[1024,128]{1,0:T(8,128)S(1)} %triangle.4.refs_0_), custom_call_target="tpu_custom_call" | custom-call | bytes 2883584 | tf_op jit(solution)/shard_map/triangle/pallas_call | solution.py:259
  60.0 2.8 %final.1 = bf16[32,32,128]{2,1,0:T(8,128)(2,1)} custom-call(f32[4,1024,128]{2,1,0:T(8,128)S(1)} %panel.1.panel_ref, bf16[32,32,128]{2,1,0:T(8,128)(2,1)S(1)} %collective-permute-done.10.right_ref, f32[1024,128]{1,0:T(8,128)S(1)} %triangle.5.before, bf16[32,32,128]{2,1,0:T(8,128)(2,1)S(1)} %get-tuple-element.19.updated_ref, ...), custom_call_target="tpu_custom_call" | custom-call | bytes 3704320 | tf_op jit(solution)/shard_map/final/pallas_call | solution.py:259
  (44 shorter events, 0.1 us)
Async XLA Ops:
  0.0 1.6 %copy-start.2 = (s32[128]{0:T(128)S(1)}, s32[128]{0:T(128)}, u32[]{:S(2)}) copy-start(s32[128]{0:T(128)} %param.22) | copy-start | bytes 1540
  0.0 1.1 %copy-start.8 = (bf16[32,32,256]{2,1,0:T(8,128)(2,1)S(1)}, bf16[32,32,256]{2,1,0:T(8,128)(2,1)}, u32[]{:S(2)}) copy-start(bf16[32,32,256]{2,1,0:T(8,128)(2,1)} %x_ref.1) | copy-start | bytes 1572868
  1.1 0.8 %copy-start.11 = (bf16[256,64]{0,1:T(8,128)(2,1)S(1)}, bf16[256,64]{0,1:T(8,128)(2,1)}, u32[]{:S(2)}) copy-start(bf16[256,64]{0,1:T(8,128)(2,1)} %param.26) | copy-start | bytes 98308
  1.1 0.8 %copy-start.13 = (s32[32,32]{1,0:T(8,128)S(1)}, s32[32,32]{1,0:T(8,128)}, u32[]{:S(2)}) copy-start(s32[32,32]{1,0:T(8,128)} %mask_ref.1) | copy-start | bytes 12292
  1.1 0.8 %copy-start.14 = (f32[256]{0:T(256)S(1)}, f32[256]{0:T(256)}, u32[]{:S(2)}) copy-start(f32[256]{0:T(256)} %param.24) | copy-start | bytes 3076
  1.1 0.8 %copy-start.15 = (f32[256]{0:T(256)S(1)}, f32[256]{0:T(256)}, u32[]{:S(2)}) copy-start(f32[256]{0:T(256)} %param.25) | copy-start | bytes 3076
  1.1 9.4 %copy-start.18 = (f32[640]{0:T(1024)S(1)}, f32[640]{0:T(1024)}, u32[]{:S(2)}) copy-start(f32[640]{0:T(1024)} %param.33) | copy-start | bytes 7684
  1.1 13.3 %copy-start.9 = (bf16[32,32,128]{2,1,0:T(8,128)(2,1)S(1)}, bf16[32,32,128]{2,1,0:T(8,128)(2,1)}, u32[]{:S(2)}) copy-start(bf16[32,32,128]{2,1,0:T(8,128)(2,1)} %pair_ref.1) | copy-start | bytes 786436
  1.1 13.3 %copy-start.10 = (bf16[1024,128]{1,0:T(8,128)(2,1)S(1)}, bf16[1024,128]{1,0:T(8,128)(2,1)}, u32[]{:S(2)}) copy-start(bf16[1024,128]{1,0:T(8,128)(2,1)} %w_ref.2) | copy-start | bytes 786436
  1.1 13.3 %copy-start.12 = (bf16[66,128]{1,0:T(8,128)(2,1)S(1)}, bf16[66,128]{1,0:T(8,128)(2,1)}, u32[]{:S(2)}) copy-start(bf16[66,128]{1,0:T(8,128)(2,1)} %table_ref.1) | copy-start | bytes 50692
  1.1 13.3 %copy-start.17 = (s32[128]{0:T(128)S(1)}, s32[128]{0:T(128)}, u32[]{:S(2)}) copy-start(s32[128]{0:T(128)} %param.23) | copy-start | bytes 1540
  1.5 15.6 %copy-start = (bf16[128,640]{1,0:T(8,128)(2,1)S(1)}, bf16[128,640]{1,0:T(8,128)(2,1)}, u32[]{:S(2)}) copy-start(bf16[128,640]{1,0:T(8,128)(2,1)} %refs_13_.1) | copy-start | bytes 491524
  1.5 15.6 %copy-start.3 = (f32[128]{0:T(128)S(1)}, f32[128]{0:T(128)}, u32[]{:S(2)}) copy-start(f32[128]{0:T(128)} %param.30) | copy-start | bytes 1540
  1.5 15.6 %copy-start.4 = (f32[128]{0:T(128)S(1)}, f32[128]{0:T(128)}, u32[]{:S(2)}) copy-start(f32[128]{0:T(128)} %param.31) | copy-start | bytes 1540
  2.9 7.5 %collective-permute-start.1 = (bf16[32,1152]{1,0:T(8,128)(2,1)S(1)}, bf16[32,1152]{1,0:T(8,128)(2,1)S(1)}, u32[]{:S(2)}, u32[]{:S(2)}) collective-permute-start(bf16[32,1152]{1,0:T(8,128)(2,1)S(1)} %get-tuple-element.13.refs_0_), channel_id=1, source_target_pairs={{0,2},{1,3},{2,0},{3,1},{4,6},{5,7},{6,4},{7,5},{8,10},{9,11},{10,... | collective-permute-start | bytes 221192 | tf_op jit(solution)/shard_map/ppermute | solution.py:242
  3.0 11.3 %collective-permute-start = (bf16[32,1152]{1,0:T(8,128)(2,1)S(1)}, bf16[32,1152]{1,0:T(8,128)(2,1)S(1)}, u32[]{:S(2)}, u32[]{:S(2)}) collective-permute-start(bf16[32,1152]{1,0:T(8,128)(2,1)S(1)} %get-tuple-element.13.refs_0_), channel_id=1, source_target_pairs={{0,1},{1,0},{2,3},{3,2},{4,5},{5,4},{6,7},{7,6},{8,9},{9,8},{10,11... | collective-permute-start | bytes 221192 | tf_op jit(solution)/shard_map/ppermute | solution.py:242
  5.7 9.9 %collective-permute-start.6 = (bf16[32,1152]{1,0:T(8,128)(2,1)S(1)}, bf16[32,1152]{1,0:T(8,128)(2,1)S(1)}, u32[]{:S(2)}, u32[]{:S(2)}) collective-permute-start(bf16[32,1152]{1,0:T(8,128)(2,1)S(1)} %get-tuple-element.14), channel_id=1, source_target_pairs={{0,12},{1,8},{2,4},{3,0},{4,13},{5,9},{6,5},{7,1},{8,14},{9,10},{1... | collective-permute-start | bytes 221192 | tf_op jit(solution)/shard_map/ppermute | solution.py:249
  7.2 8.4 %collective-permute-start.5 = (bf16[32,1152]{1,0:T(8,128)(2,1)S(1)}, bf16[32,1152]{1,0:T(8,128)(2,1)S(1)}, u32[]{:S(2)}, u32[]{:S(2)}) collective-permute-start(bf16[32,1152]{1,0:T(8,128)(2,1)S(1)} %get-tuple-element.14), channel_id=1, source_target_pairs={{0,8},{1,12},{2,0},{3,4},{4,9},{5,13},{6,1},{7,5},{8,10},{9,14},{1... | collective-permute-start | bytes 221192 | tf_op jit(solution)/shard_map/ppermute | solution.py:249
  9.7 5.9 %collective-permute-start.4 = (bf16[32,1152]{1,0:T(8,128)(2,1)S(1)}, bf16[32,1152]{1,0:T(8,128)(2,1)S(1)}, u32[]{:S(2)}, u32[]{:S(2)}) collective-permute-start(bf16[32,1152]{1,0:T(8,128)(2,1)S(1)} %get-tuple-element.14), channel_id=1, source_target_pairs={{0,4},{1,0},{2,12},{3,8},{4,5},{5,1},{6,13},{7,9},{8,6},{9,2},{10,... | collective-permute-start | bytes 221192 | tf_op jit(solution)/shard_map/ppermute | solution.py:249
  10.5 6.7 %collective-permute-start.3 = (bf16[32,1152]{1,0:T(8,128)(2,1)S(1)}, bf16[32,1152]{1,0:T(8,128)(2,1)S(1)}, u32[]{:S(2)}, u32[]{:S(2)}) collective-permute-start(bf16[32,1152]{1,0:T(8,128)(2,1)S(1)} %get-tuple-element.14), channel_id=1, source_target_pairs={{0,0},{1,4},{2,8},{3,12},{4,1},{5,5},{6,9},{7,13},{8,2},{9,6},{10,... | collective-permute-start | bytes 221192 | tf_op jit(solution)/shard_map/ppermute | solution.py:249
  14.3 2.8 %collective-permute-start.2 = (bf16[32,1152]{1,0:T(8,128)(2,1)S(1)}, bf16[32,1152]{1,0:T(8,128)(2,1)S(1)}, u32[]{:S(2)}, u32[]{:S(2)}) collective-permute-start(bf16[32,1152]{1,0:T(8,128)(2,1)S(1)} %collective-permute-done.refs_1_), channel_id=1, source_target_pairs={{0,2},{1,3},{2,0},{3,1},{4,6},{5,7},{6,4},{7,5},{8,10},{9,11},{10,... | collective-permute-start | bytes 221192 | tf_op jit(solution)/shard_map/ppermute | solution.py:242
  20.9 7.9 %collective-permute-start.7 = (bf16[32,32,128]{2,1,0:T(8,128)(2,1)S(1)}, bf16[32,32,128]{2,1,0:T(8,128)(2,1)S(1)}, u32[]{:S(2)}, u32[]{:S(2)}) collective-permute-start(bf16[32,32,128]{2,1,0:T(8,128)(2,1)S(1)} %get-tuple-element.17.refs_0_), channel_id=1, source_target_pairs={{0,1},{1,0},{2,3},{3,2},{4,5},{5,4},{6,7},{7,6},{8,9},{9,8},{10,11... | collective-permute-start | bytes 786440 | tf_op jit(solution)/shard_map/ppermute | solution.py:242
  23.2 13.9 %collective-permute-start.8 = (bf16[32,32,128]{2,1,0:T(8,128)(2,1)S(1)}, bf16[32,32,128]{2,1,0:T(8,128)(2,1)S(1)}, u32[]{:S(2)}, u32[]{:S(2)}) collective-permute-start(bf16[32,32,128]{2,1,0:T(8,128)(2,1)S(1)} %get-tuple-element.17.refs_0_), channel_id=1, source_target_pairs={{0,2},{1,3},{2,0},{3,1},{4,6},{5,7},{6,4},{7,5},{8,10},{9,11},{10,... | collective-permute-start | bytes 786440 | tf_op jit(solution)/shard_map/ppermute | solution.py:242
  28.8 8.4 %collective-permute-start.9 = (bf16[32,32,128]{2,1,0:T(8,128)(2,1)S(1)}, bf16[32,32,128]{2,1,0:T(8,128)(2,1)S(1)}, u32[]{:S(2)}, u32[]{:S(2)}) collective-permute-start(bf16[32,32,128]{2,1,0:T(8,128)(2,1)S(1)} %collective-permute-done.7.refs_1_), channel_id=1, source_target_pairs={{0,2},{1,3},{2,0},{3,1},{4,6},{5,7},{6,4},{7,5},{8,10},{9,11},{10,... | collective-permute-start | bytes 786440 | tf_op jit(solution)/shard_map/ppermute | solution.py:242
  30.5 19.9 %collective-permute-start.13 = (bf16[32,32,128]{2,1,0:T(8,128)(2,1)S(1)}, bf16[32,32,128]{2,1,0:T(8,128)(2,1)S(1)}, u32[]{:S(2)}, u32[]{:S(2)}) collective-permute-start(bf16[32,32,128]{2,1,0:T(8,128)(2,1)S(1)} %get-tuple-element.18), channel_id=1, source_target_pairs={{0,0},{1,4},{2,8},{3,12},{4,1},{5,5},{6,9},{7,13},{8,2},{9,6},{10,... | collective-permute-start | bytes 786440 | tf_op jit(solution)/shard_map/ppermute | solution.py:249
  32.4 24.3 %collective-permute-start.12 = (bf16[32,32,128]{2,1,0:T(8,128)(2,1)S(1)}, bf16[32,32,128]{2,1,0:T(8,128)(2,1)S(1)}, u32[]{:S(2)}, u32[]{:S(2)}) collective-permute-start(bf16[32,32,128]{2,1,0:T(8,128)(2,1)S(1)} %get-tuple-element.18), channel_id=1, source_target_pairs={{0,4},{1,0},{2,12},{3,8},{4,5},{5,1},{6,13},{7,9},{8,6},{9,2},{10,... | collective-permute-start | bytes 786440 | tf_op jit(solution)/shard_map/ppermute | solution.py:249
  37.2 21.1 %collective-permute-start.11 = (bf16[32,32,128]{2,1,0:T(8,128)(2,1)S(1)}, bf16[32,32,128]{2,1,0:T(8,128)(2,1)S(1)}, u32[]{:S(2)}, u32[]{:S(2)}) collective-permute-start(bf16[32,32,128]{2,1,0:T(8,128)(2,1)S(1)} %get-tuple-element.18), channel_id=1, source_target_pairs={{0,8},{1,12},{2,0},{3,4},{4,9},{5,13},{6,1},{7,5},{8,10},{9,14},{1... | collective-permute-start | bytes 786440 | tf_op jit(solution)/shard_map/ppermute | solution.py:249
  37.2 22.7 %collective-permute-start.10 = (bf16[32,32,128]{2,1,0:T(8,128)(2,1)S(1)}, bf16[32,32,128]{2,1,0:T(8,128)(2,1)S(1)}, u32[]{:S(2)}, u32[]{:S(2)}) collective-permute-start(bf16[32,32,128]{2,1,0:T(8,128)(2,1)S(1)} %get-tuple-element.18), channel_id=1, source_target_pairs={{0,12},{1,8},{2,4},{3,0},{4,13},{5,9},{6,5},{7,1},{8,14},{9,10},{1... | collective-permute-start | bytes 786440 | tf_op jit(solution)/shard_map/ppermute | solution.py:249
  37.4 22.6 %copy-start.1 = (bf16[128,128]{1,0:T(8,128)(2,1)S(1)}, bf16[128,128]{1,0:T(8,128)(2,1)}, u32[]{:S(2)}) copy-start(bf16[128,128]{1,0:T(8,128)(2,1)} %w_ref.3) | copy-start | bytes 98308
  37.4 22.6 %copy-start.5 = (f32[128]{0:T(128)S(1)}, f32[128]{0:T(128)}, u32[]{:S(2)}) copy-start(f32[128]{0:T(128)} %param.34) | copy-start | bytes 1540
  37.4 22.6 %copy-start.6 = (f32[128]{0:T(128)S(1)}, f32[128]{0:T(128)}, u32[]{:S(2)}) copy-start(f32[128]{0:T(128)} %param.35) | copy-start | bytes 1540
  37.4 22.6 %copy-start.7 = (f32[128]{0:T(128)S(1)}, f32[128]{0:T(128)}, u32[]{:S(2)}) copy-start(f32[128]{0:T(128)} %param.37) | copy-start | bytes 1540
  (1 other events, 0.8 us)

commit v5 on v4

--- a/solution.py
+++ b/solution.py
@@ -116,7 +116,7 @@
 
 
 def edges_kernel(count, *refs):
-    lefts, rights = refs[:count], refs[count:2 * count]
+    rights, lefts = refs[:count], refs[count:2 * count]
     (base_ref, block_ref, res_ref, gain_ref, shift_ref, w_ref, bias_ref,
      updated_ref, left_ref, right_ref, gate_ref,
      lall, rall, tscr, rscr, oscr, nscr, escr) = refs[2 * count:]
@@ -180,11 +180,9 @@
         right_ref[k] = escr[pl.ds(k, rows, stride=cols), :].astype(BF16)
 
 
-def panel_kernel(count, *refs):
-    lefts, panel_ref = refs[:count], refs[count]
-    q = lax.axis_index(PLANE)
-    for step in range(count):
-        panel_ref[q ^ step] = lefts[step][...].astype(F32).reshape(panel_ref.shape[1:])
+def panel_kernel(left_ref, panel_ref):
+    for step in range(left_ref.shape[0]):
+        panel_ref[step] = left_ref[step].astype(F32).reshape(panel_ref.shape[1:])
 
 
 def add_block(step, panel_ref, right_ref, rscr, before, store):
@@ -216,12 +214,12 @@
     lax.fori_loop(0, rows // block, rows_body, 0)
 
 
-def step_kernel(step, panel_ref, right_ref, *refs):
+def step_kernel(step, right_ref, panel_ref, *refs):
     before = refs[0] if len(refs) == 3 else None
     add_block(step, panel_ref, right_ref, refs[-1], before, refs[-2])
 
 
-def final_kernel(step, panel_ref, right_ref, before, updated_ref, gate_ref, gain_ref, shift_ref,
+def final_kernel(step, right_ref, panel_ref, before, updated_ref, gate_ref, gain_ref, shift_ref,
                  w_ref, bias_ref, out_ref, acc, rscr):
     add_block(step, panel_ref, right_ref, rscr, before, acc)
     rows, cols, channels = out_ref.shape
@@ -236,12 +234,9 @@
 
 
 def send_plane(block, count):
-    parts, bit = [block], 1
-    while bit < count:
-        pairs = [(p, p ^ bit) for p in range(count)]
-        parts += [lax.ppermute(part, PLANE, pairs) for part in parts]
-        bit *= 2
-    return parts
+    return [block] + [
+        lax.ppermute(block, PLANE, [(p, p ^ m) for p in range(count)]) for m in range(1, count)
+    ]
 
 
 def send_turned(block, count):
@@ -325,24 +320,23 @@
          pltpu.VMEM((width, count * seqs), BF16),
          pltpu.VMEM((rows // per * cols, half * LANES), BF16),
          pltpu.VMEM((rows * cols, channels), BF16), pltpu.VMEM((rows * cols, channels), F32)],
-        lefts + rights + [base, block, residue, flat(pair_norm_gain), flat(pair_norm_bias),
+        rights + lefts + [base, block, residue, flat(pair_norm_gain), flat(pair_norm_bias),
                           triangle_projection_weights, flat(triangle_projection_biases)],
         name="edges")
     right_edges = send_turned(right_edge, count)
-    left_edges = send_plane(left_edge, count)
+    left_edges = lax.all_gather(left_edge, PLANE)
     sums = shape((rows * cols, channels), F32)
     turned = pltpu.VMEM((rows * cols, channels), F32)
     panel = call(
-        functools.partial(panel_kernel, count), shape((count, rows * cols, channels), F32), [],
-        left_edges, name="panel")
+        panel_kernel, shape((count, rows * cols, channels), F32), [], [left_edges], name="panel")
     args = []
     for step in range(count - 1):
         args = [call(functools.partial(step_kernel, step), sums, [turned],
-                     [panel, right_edges[step]] + args, name="triangle")]
+                     [right_edges[step], panel] + args, name="triangle")]
     return call(
         functools.partial(final_kernel, count - 1), shape((rows, cols, channels), BF16),
         [turned, turned],
-        [panel, right_edges[-1]] + args + [
+        [right_edges[-1], panel] + args + [
             updated, gate, flat(triangle_sum_norm_gain), flat(triangle_sum_norm_bias),
             triangle_output_weight, flat(outer_pair_bias)],
         name="final")

time: 62.9 us -> 71.9 us (1.14)
  between operations: 0.33 us -> 13.6 us
  waiting for transfers between devices: 23.5 us -> 18.9 us
  starting transfers between devices: 23.5 us -> 21.4 us
  local copies, waits for them, and re-layouts: 1.39 us -> 2.62 us
    ppermute x8, waiting for transfers between devices: 19.3 us -> 1.17 us  [send_turned(): lax.ppermute(block, GROUP, [(z * count + p, (p ^ m) * count + z) for z in...]
    all_gather x0 -> x1, waiting for transfers between devices: none -> 15.5 us  [body(): left_edges = lax.all_gather(left_edge, PLANE)]
    ppermute x6 -> x3, starting transfers between devices: 8.27 us -> 2.01 us  [send_plane(): lax.ppermute(block, PLANE, [(p, p ^ m) for p in range(count)])]
    ppermute x8, starting transfers between devices: 15.2 us -> 19.4 us  [send_turned(): lax.ppermute(block, GROUP, [(z * count + p, (p ^ m) * count + z) for z in...]
    ppermute x6 -> x3, waiting for transfers between devices: 4.19 us -> 2.2 us  [send_plane(): lax.ppermute(block, PLANE, [(p, p ^ m) for p in range(count)])]
    unnamed x38 -> x40, local copies, waits for them, and re-layouts: 1.39 us -> 2.61 us
  transfers between devices with their start and end apart: 14 -> 12, of which waited for: 4 -> 4; matrix products, arithmetic and copies ran while one was open for 0% -> 0% of each run, Pallas kernels for 10% -> 8%
where the time goes in v5:
time: 71.9 us; the launch traced here: 71.2 us
  starting transfers between devices  21.4 us (30%)
  waiting for transfers between devices  18.9 us (26%)
  Pallas kernels  14.7 us (20%)
  between operations  13.6 us (19%)
  local copies, waits for them, and re-layouts  2.62 us (4%)
    ppermute x8, starting transfers between devices, send_turned(): lax.ppermute(block, GROUP, [(z * count + p, (p ^ m) * count + z) for z in...  19.4 us
    all_gather x1, waiting for transfers between devices, body(): left_edges = lax.all_gather(left_edge, PLANE)  15.5 us
    pallas_call x9, Pallas kernels, call(): pl.pallas_call(kernel, out_shape=outs, in_specs=[vmem] * len(args), out_s...  14.7 us
    unnamed x40, local copies, waits for them, and re-layouts  2.61 us
    ppermute x3, waiting for transfers between devices, send_plane(): lax.ppermute(block, PLANE, [(p, p ^ m) for p in range(count)])  2.2 us
    ppermute x3, starting transfers between devices, send_plane(): lax.ppermute(block, PLANE, [(p, p ^ m) for p in range(count)])  2.01 us
  transfers between devices with their start and end apart: 12, of which 4 were waited for; matrix products, arithmetic and copies ran while one was open for 0% of the time, Pallas kernels for 8%

profile of v5, /device:TPU:1, one launch (start us, length us, event | category | flops | bytes accessed | tf_op | source)
XLA Modules:
  0.0 71.2 jit_solution(15301425797667517760)
XLA Ops:
  6.5 1.1 %copy-done.9 = bf16[32,32,256]{2,1,0:T(8,128)(2,1)S(1)} copy-done((bf16[32,32,256]{2,1,0:T(8,128)(2,1)S(1)}, bf16[32,32,256]{2,1,0:T(8,128)(2,1)}, u32[]{:S(2)}) %copy-start.9) | copy-done | bytes 524312
  7.7 0.4 norm.1.x_ref
  8.1 0.0 copy-start.1
  8.1 0.0 copy-start.4
  8.1 0.0 copy-start.5
  8.1 0.3 copy-done.12
  8.4 1.1 %pack.1 = (bf16[32,1152]{1,0:T(8,128)(2,1)S(1)}, bf16[32,1152]{1,0:T(8,128)(2,1)S(1)}) custom-call(f32[1024,256]{1,0:T(8,128)S(1)} %norm.1.x_ref, s32[32,32]{1,0:T(8,128)S(1)} %copy-done.14, s32[1,128]{1,0:T(1,128)S(1)} %bitcast.13, f32[1,256]{1,0:T(1,128)S(1)} %bitcast.21, f32[1,256]{1,0:T(1,128)S(1)} %bitcast.22, bf16[64,256]{1,0:T(8,128)(2,1)S(1)} %bitcast.20, ...), custom_call_target="tpu_custom_call" | custom-call | flops 1073741824 | bytes 1088256 | tf_op jit(solution)/shard_map/pack/pallas_call | solution.py:254
  9.5 2.7 %collective-permute-start.3 = (bf16[32,1152]{1,0:T(8,128)(2,1)S(1)}, bf16[32,1152]{1,0:T(8,128)(2,1)S(1)}, u32[]{:S(2)}, u32[]{:S(2)}) collective-permute-start(bf16[32,1152]{1,0:T(8,128)(2,1)S(1)} %get-tuple-element.13), channel_id=1, source_target_pairs={{0,12},{1,8},{2,4},{3,0},{4,13},{5,9},{6,5},{7,1},{8,14},{9,10},{1... | collective-permute-start | bytes 221192 | tf_op jit(solution)/shard_map/ppermute | solution.py:244
  12.2 2.4 %collective-permute-start.2 = (bf16[32,1152]{1,0:T(8,128)(2,1)S(1)}, bf16[32,1152]{1,0:T(8,128)(2,1)S(1)}, u32[]{:S(2)}, u32[]{:S(2)}) collective-permute-start(bf16[32,1152]{1,0:T(8,128)(2,1)S(1)} %get-tuple-element.13), channel_id=1, source_target_pairs={{0,8},{1,12},{2,0},{3,4},{4,9},{5,13},{6,1},{7,5},{8,10},{9,14},{1... | collective-permute-start | bytes 221192 | tf_op jit(solution)/shard_map/ppermute | solution.py:244
  14.6 0.5 collective-permute-start.1
  15.2 4.1 %collective-permute-start = (bf16[32,1152]{1,0:T(8,128)(2,1)S(1)}, bf16[32,1152]{1,0:T(8,128)(2,1)S(1)}, u32[]{:S(2)}, u32[]{:S(2)}) collective-permute-start(bf16[32,1152]{1,0:T(8,128)(2,1)S(1)} %get-tuple-element.13), channel_id=1, source_target_pairs={{0,0},{1,4},{2,8},{3,12},{4,1},{5,5},{6,9},{7,13},{8,2},{9,6},{10,... | collective-permute-start | bytes 221192 | tf_op jit(solution)/shard_map/ppermute | solution.py:244
  19.2 0.6 collective-permute-start.6
  19.8 1.0 %collective-permute-start.5 = (bf16[32,1152]{1,0:T(8,128)(2,1)S(1)}, bf16[32,1152]{1,0:T(8,128)(2,1)S(1)}, u32[]{:S(2)}, u32[]{:S(2)}) collective-permute-start(bf16[32,1152]{1,0:T(8,128)(2,1)S(1)} %get-tuple-element.14.refs_4_), channel_id=1, source_target_pairs={{0,2},{1,3},{2,0},{3,1},{4,6},{5,7},{6,4},{7,5},{8,10},{9,11},{10,... | collective-permute-start | bytes 221192 | tf_op jit(solution)/shard_map/ppermute | solution.py:238
  20.8 0.4 collective-permute-start.4
  21.3 1.2 %base.1 = (f32[32,32,128]{2,1,0:T(8,128)S(1)}, bf16[4096,512]{1,0:T(8,128)(2,1)S(1)}) custom-call(bf16[32,32,128]{2,1,0:T(8,128)(2,1)S(1)} %copy-done.10, bf16[66,128]{1,0:T(8,128)(2,1)S(1)} %copy-done.13, s32[1,128]{1,0:T(1,128)S(1)} %bitcast.24, bf16[1024,128]{1,0:T(8,128)(2,1)S(1)} %copy-done.11), custom_call_target="tpu_custom_call" | custom-call | flops 1073741824 | bytes 541696 | tf_op jit(solution)/shard_map/base/pallas_call | solution.py:254
  22.4 0.6 collective-permute-done.6.refs_7_
  23.1 1.6 %collective-permute-done.4.refs_5_ = bf16[32,1152]{1,0:T(8,128)(2,1)S(1)} collective-permute-done((bf16[32,1152]{1,0:T(8,128)(2,1)S(1)}, bf16[32,1152]{1,0:T(8,128)(2,1)S(1)}, u32[]{:S(2)}, u32[]{:S(2)}) %collective-permute-start.4) | collective-permute-done | bytes 73760 | tf_op jit(solution)/shard_map/ppermute | solution.py:238
  24.7 4.4 %edges.1 = (bf16[32,32,128]{2,1,0:T(8,128)(2,1)S(1)}, bf16[32,32,128]{2,1,0:T(8,128)(2,1)}, bf16[32,32,128]{2,1,0:T(8,128)(2,1)S(1)}, f32[1024,128]{1,0:T(8,128)S(1)}) custom-call(bf16[32,1152]{1,0:T(8,128)(2,1)S(1)} %collective-permute-done.refs_0_, bf16[32,1152]{1,0:T(8,128)(2,1)S(1)} %collective-permute-done.1.refs_1_, ...), custom_call_target="tpu_custom_call" | custom-call | bytes 5476352 | tf_op jit(solution)/shard_map/edges/pallas_call | solution.py:254
  29.1 0.0 all-gather.3.cloned.1.call-update
  29.1 5.5 %collective-permute-start.10 = (bf16[32,32,128]{2,1,0:T(8,128)(2,1)S(1)}, bf16[32,32,128]{2,1,0:T(8,128)(2,1)S(1)}, u32[]{:S(2)}, u32[]{:S(2)}) collective-permute-start(bf16[32,32,128]{2,1,0:T(8,128)(2,1)S(1)} %get-tuple-element.17), channel_id=1, source_target_pairs={{0,0},{1,4},{2,8},{3,12},{4,1},{5,5},{6,9},{7,13},{8,2},{9,6},{10,... | collective-permute-start | bytes 786440 | tf_op jit(solution)/shard_map/ppermute | solution.py:244
  34.6 1.6 %collective-permute-start.9 = (bf16[32,32,128]{2,1,0:T(8,128)(2,1)S(1)}, bf16[32,32,128]{2,1,0:T(8,128)(2,1)S(1)}, u32[]{:S(2)}, u32[]{:S(2)}) collective-permute-start(bf16[32,32,128]{2,1,0:T(8,128)(2,1)S(1)} %get-tuple-element.17), channel_id=1, source_target_pairs={{0,4},{1,0},{2,12},{3,8},{4,5},{5,1},{6,13},{7,9},{8,6},{9,2},{10,... | collective-permute-start | bytes 786440 | tf_op jit(solution)/shard_map/ppermute | solution.py:244
  36.2 2.6 %collective-permute-start.7 = (bf16[32,32,128]{2,1,0:T(8,128)(2,1)S(1)}, bf16[32,32,128]{2,1,0:T(8,128)(2,1)S(1)}, u32[]{:S(2)}, u32[]{:S(2)}) collective-permute-start(bf16[32,32,128]{2,1,0:T(8,128)(2,1)S(1)} %get-tuple-element.17), channel_id=1, source_target_pairs={{0,12},{1,8},{2,4},{3,0},{4,13},{5,9},{6,5},{7,1},{8,14},{9,10},{1... | collective-permute-start | bytes 786440 | tf_op jit(solution)/shard_map/ppermute | solution.py:244
  38.8 15.5 %all-gather.3.cloned.1.call-done = bf16[128,32,128]{2,1,0:T(8,128)(2,1)} async-done(((bf16[32,32,128]{2,1,0:T(8,128)(2,1)}), bf16[128,32,128]{2,1,0:T(8,128)(2,1)}) %all-gather.3.cloned.1.call-update) | async-done | bytes 1048592 | tf_op jit(solution)/shard_map/all_gather | solution.py:327
  54.2 1.2 %copy-done = bf16[128,32,128]{2,1,0:T(8,128)(2,1)S(1)} copy-done((bf16[128,32,128]{2,1,0:T(8,128)(2,1)S(1)}, bf16[128,32,128]{2,1,0:T(8,128)(2,1)}, u32[]{:S(2)}) %copy-start) | copy-done | bytes 1048600
  55.4 0.1 panel.1.panel_ref
  55.6 0.0 copy-start.2
  55.6 0.0 copy-start.8
  55.6 1.6 %triangle.3.refs_0_ = f32[1024,128]{1,0:T(8,128)S(1)} custom-call(bf16[32,32,128]{2,1,0:T(8,128)(2,1)S(1)} %collective-permute-done.10.right_ref, f32[4,1024,128]{2,1,0:T(8,128)S(1)} %panel.1.panel_ref), custom_call_target="tpu_custom_call" | custom-call | bytes 2359296 | tf_op jit(solution)/shard_map/triangle/pallas_call | solution.py:254
  57.2 1.2 %collective-permute-done.9.right_ref = bf16[32,32,128]{2,1,0:T(8,128)(2,1)S(1)} collective-permute-done((bf16[32,32,128]{2,1,0:T(8,128)(2,1)S(1)}, bf16[32,32,128]{2,1,0:T(8,128)(2,1)S(1)}, u32[]{:S(2)}, u32[]{:S(2)}) %collective-permute-start.9) | collective-permute-done | bytes 262176 | tf_op jit(solution)/shard_map/ppermute | solution.py:244
  58.4 1.6 %triangle.4.refs_0_ = f32[1024,128]{1,0:T(8,128)S(1)} custom-call(bf16[32,32,128]{2,1,0:T(8,128)(2,1)S(1)} %collective-permute-done.9.right_ref, f32[4,1024,128]{2,1,0:T(8,128)S(1)} %panel.1.panel_ref, f32[1024,128]{1,0:T(8,128)S(1)} %triangle.3.refs_0_), custom_call_target="tpu_custom_call" | custom-call | bytes 2883584 | tf_op jit(solution)/shard_map/triangle/pallas_call | solution.py:254
  60.0 1.6 %triangle.5.before = f32[1024,128]{1,0:T(8,128)S(1)} custom-call(bf16[32,32,128]{2,1,0:T(8,128)(2,1)S(1)} %collective-permute-done.8.right_ref, f32[4,1024,128]{2,1,0:T(8,128)S(1)} %panel.1.panel_ref, f32[1024,128]{1,0:T(8,128)S(1)} %triangle.4.refs_0_), custom_call_target="tpu_custom_call" | custom-call | bytes 2883584 | tf_op jit(solution)/shard_map/triangle/pallas_call | solution.py:254
  61.6 2.8 %final.1 = bf16[32,32,128]{2,1,0:T(8,128)(2,1)} custom-call(bf16[32,32,128]{2,1,0:T(8,128)(2,1)S(1)} %collective-permute-done.7.right_ref, f32[4,1024,128]{2,1,0:T(8,128)S(1)} %panel.1.panel_ref, f32[1024,128]{1,0:T(8,128)S(1)} %triangle.5.before, bf16[32,32,128]{2,1,0:T(8,128)(2,1)S(1)} %get-tuple-element.19.updated_ref, ...), custom_call_target="tpu_custom_call" | custom-call | bytes 3704320 | tf_op jit(solution)/shard_map/final/pallas_call | solution.py:254
  (43 shorter events, 0.1 us)
Async XLA Ops:
  6.5 1.6 %copy-start.3 = (s32[128]{0:T(128)S(1)}, s32[128]{0:T(128)}, u32[]{:S(2)}) copy-start(s32[128]{0:T(128)} %param.22) | copy-start | bytes 1540
  6.5 47.7 %all-gather.3.cloned.1.call-start = ((), (), s32[]{:S(2)}) async-start(), calls=%async_computation | async-start | bytes 1310720 | tf_op jit(solution)/shard_map/all_gather | solution.py:327
  6.5 1.1 %copy-start.9 = (bf16[32,32,256]{2,1,0:T(8,128)(2,1)S(1)}, bf16[32,32,256]{2,1,0:T(8,128)(2,1)}, u32[]{:S(2)}) copy-start(bf16[32,32,256]{2,1,0:T(8,128)(2,1)} %x_ref.1) | copy-start | bytes 1572868
  7.6 0.8 %copy-start.12 = (bf16[256,64]{0,1:T(8,128)(2,1)S(1)}, bf16[256,64]{0,1:T(8,128)(2,1)}, u32[]{:S(2)}) copy-start(bf16[256,64]{0,1:T(8,128)(2,1)} %param.26) | copy-start | bytes 98308
  7.6 0.8 %copy-start.14 = (s32[32,32]{1,0:T(8,128)S(1)}, s32[32,32]{1,0:T(8,128)}, u32[]{:S(2)}) copy-start(s32[32,32]{1,0:T(8,128)} %mask_ref.1) | copy-start | bytes 12292
  7.6 0.8 %copy-start.15 = (f32[256]{0:T(256)S(1)}, f32[256]{0:T(256)}, u32[]{:S(2)}) copy-start(f32[256]{0:T(256)} %param.24) | copy-start | bytes 3076
  7.6 0.8 %copy-start.16 = (f32[256]{0:T(256)S(1)}, f32[256]{0:T(256)}, u32[]{:S(2)}) copy-start(f32[256]{0:T(256)} %param.25) | copy-start | bytes 3076
  7.6 0.8 %copy-start.17 = (f32[64]{0:T(128)S(1)}, f32[64]{0:T(128)}, u32[]{:S(2)}) copy-start(f32[64]{0:T(128)} %param.27) | copy-start | bytes 772
  7.6 12.2 %copy-start.19 = (f32[640]{0:T(1024)S(1)}, f32[640]{0:T(1024)}, u32[]{:S(2)}) copy-start(f32[640]{0:T(1024)} %param.33) | copy-start | bytes 7684
  7.6 13.6 %copy-start.10 = (bf16[32,32,128]{2,1,0:T(8,128)(2,1)S(1)}, bf16[32,32,128]{2,1,0:T(8,128)(2,1)}, u32[]{:S(2)}) copy-start(bf16[32,32,128]{2,1,0:T(8,128)(2,1)} %pair_ref.1) | copy-start | bytes 786436
  7.6 13.6 %copy-start.11 = (bf16[1024,128]{1,0:T(8,128)(2,1)S(1)}, bf16[1024,128]{1,0:T(8,128)(2,1)}, u32[]{:S(2)}) copy-start(bf16[1024,128]{1,0:T(8,128)(2,1)} %w_ref.2) | copy-start | bytes 786436
  7.6 13.6 %copy-start.13 = (bf16[66,128]{1,0:T(8,128)(2,1)S(1)}, bf16[66,128]{1,0:T(8,128)(2,1)}, u32[]{:S(2)}) copy-start(bf16[66,128]{1,0:T(8,128)(2,1)} %table_ref.1) | copy-start | bytes 50692
  7.7 13.6 %copy-start.18 = (s32[128]{0:T(128)S(1)}, s32[128]{0:T(128)}, u32[]{:S(2)}) copy-start(s32[128]{0:T(128)} %param.23) | copy-start | bytes 1540
  8.1 16.6 %copy-start.1 = (bf16[128,640]{1,0:T(8,128)(2,1)S(1)}, bf16[128,640]{1,0:T(8,128)(2,1)}, u32[]{:S(2)}) copy-start(bf16[128,640]{1,0:T(8,128)(2,1)} %refs_13_.1) | copy-start | bytes 491524
  8.1 16.6 %copy-start.4 = (f32[128]{0:T(128)S(1)}, f32[128]{0:T(128)}, u32[]{:S(2)}) copy-start(f32[128]{0:T(128)} %param.30) | copy-start | bytes 1540
  8.1 16.6 %copy-start.5 = (f32[128]{0:T(128)S(1)}, f32[128]{0:T(128)}, u32[]{:S(2)}) copy-start(f32[128]{0:T(128)} %param.31) | copy-start | bytes 1540
  9.5 10.3 %collective-permute-start.3 = (bf16[32,1152]{1,0:T(8,128)(2,1)S(1)}, bf16[32,1152]{1,0:T(8,128)(2,1)S(1)}, u32[]{:S(2)}, u32[]{:S(2)}) collective-permute-start(bf16[32,1152]{1,0:T(8,128)(2,1)S(1)} %get-tuple-element.13), channel_id=1, source_target_pairs={{0,12},{1,8},{2,4},{3,0},{4,13},{5,9},{6,5},{7,1},{8,14},{9,10},{1... | collective-permute-start | bytes 221192 | tf_op jit(solution)/shard_map/ppermute | solution.py:244
  12.2 8.6 %collective-permute-start.2 = (bf16[32,1152]{1,0:T(8,128)(2,1)S(1)}, bf16[32,1152]{1,0:T(8,128)(2,1)S(1)}, u32[]{:S(2)}, u32[]{:S(2)}) collective-permute-start(bf16[32,1152]{1,0:T(8,128)(2,1)S(1)} %get-tuple-element.13), channel_id=1, source_target_pairs={{0,8},{1,12},{2,0},{3,4},{4,9},{5,13},{6,1},{7,5},{8,10},{9,14},{1... | collective-permute-start | bytes 221192 | tf_op jit(solution)/shard_map/ppermute | solution.py:244
  14.6 7.8 %collective-permute-start.1 = (bf16[32,1152]{1,0:T(8,128)(2,1)S(1)}, bf16[32,1152]{1,0:T(8,128)(2,1)S(1)}, u32[]{:S(2)}, u32[]{:S(2)}) collective-permute-start(bf16[32,1152]{1,0:T(8,128)(2,1)S(1)} %get-tuple-element.13), channel_id=1, source_target_pairs={{0,4},{1,0},{2,12},{3,8},{4,5},{5,1},{6,13},{7,9},{8,6},{9,2},{10,... | collective-permute-start | bytes 221192 | tf_op jit(solution)/shard_map/ppermute | solution.py:244
  15.2 7.3 %collective-permute-start = (bf16[32,1152]{1,0:T(8,128)(2,1)S(1)}, bf16[32,1152]{1,0:T(8,128)(2,1)S(1)}, u32[]{:S(2)}, u32[]{:S(2)}) collective-permute-start(bf16[32,1152]{1,0:T(8,128)(2,1)S(1)} %get-tuple-element.13), channel_id=1, source_target_pairs={{0,0},{1,4},{2,8},{3,12},{4,1},{5,5},{6,9},{7,13},{8,2},{9,6},{10,... | collective-permute-start | bytes 221192 | tf_op jit(solution)/shard_map/ppermute | solution.py:244
  19.2 3.8 %collective-permute-start.6 = (bf16[32,1152]{1,0:T(8,128)(2,1)S(1)}, bf16[32,1152]{1,0:T(8,128)(2,1)S(1)}, u32[]{:S(2)}, u32[]{:S(2)}) collective-permute-start(bf16[32,1152]{1,0:T(8,128)(2,1)S(1)} %get-tuple-element.14.refs_4_), channel_id=1, source_target_pairs={{0,3},{1,2},{2,1},{3,0},{4,7},{5,6},{6,5},{7,4},{8,11},{9,10},{10,... | collective-permute-start | bytes 221192 | tf_op jit(solution)/shard_map/ppermute | solution.py:238
  19.8 3.3 %collective-permute-start.5 = (bf16[32,1152]{1,0:T(8,128)(2,1)S(1)}, bf16[32,1152]{1,0:T(8,128)(2,1)S(1)}, u32[]{:S(2)}, u32[]{:S(2)}) collective-permute-start(bf16[32,1152]{1,0:T(8,128)(2,1)S(1)} %get-tuple-element.14.refs_4_), channel_id=1, source_target_pairs={{0,2},{1,3},{2,0},{3,1},{4,6},{5,7},{6,4},{7,5},{8,10},{9,11},{10,... | collective-permute-start | bytes 221192 | tf_op jit(solution)/shard_map/ppermute | solution.py:238
  20.8 3.8 %collective-permute-start.4 = (bf16[32,1152]{1,0:T(8,128)(2,1)S(1)}, bf16[32,1152]{1,0:T(8,128)(2,1)S(1)}, u32[]{:S(2)}, u32[]{:S(2)}) collective-permute-start(bf16[32,1152]{1,0:T(8,128)(2,1)S(1)} %get-tuple-element.14.refs_4_), channel_id=1, source_target_pairs={{0,1},{1,0},{2,3},{3,2},{4,5},{5,4},{6,7},{7,6},{8,9},{9,8},{10,11... | collective-permute-start | bytes 221192 | tf_op jit(solution)/shard_map/ppermute | solution.py:238
  29.1 26.5 %collective-permute-start.10 = (bf16[32,32,128]{2,1,0:T(8,128)(2,1)S(1)}, bf16[32,32,128]{2,1,0:T(8,128)(2,1)S(1)}, u32[]{:S(2)}, u32[]{:S(2)}) collective-permute-start(bf16[32,32,128]{2,1,0:T(8,128)(2,1)S(1)} %get-tuple-element.17), channel_id=1, source_target_pairs={{0,0},{1,4},{2,8},{3,12},{4,1},{5,5},{6,9},{7,13},{8,2},{9,6},{10,... | collective-permute-start | bytes 786440 | tf_op jit(solution)/shard_map/ppermute | solution.py:244
  34.6 23.8 %collective-permute-start.9 = (bf16[32,32,128]{2,1,0:T(8,128)(2,1)S(1)}, bf16[32,32,128]{2,1,0:T(8,128)(2,1)S(1)}, u32[]{:S(2)}, u32[]{:S(2)}) collective-permute-start(bf16[32,32,128]{2,1,0:T(8,128)(2,1)S(1)} %get-tuple-element.17), channel_id=1, source_target_pairs={{0,4},{1,0},{2,12},{3,8},{4,5},{5,1},{6,13},{7,9},{8,6},{9,2},{10,... | collective-permute-start | bytes 786440 | tf_op jit(solution)/shard_map/ppermute | solution.py:244
  36.2 23.8 %collective-permute-start.8 = (bf16[32,32,128]{2,1,0:T(8,128)(2,1)S(1)}, bf16[32,32,128]{2,1,0:T(8,128)(2,1)S(1)}, u32[]{:S(2)}, u32[]{:S(2)}) collective-permute-start(bf16[32,32,128]{2,1,0:T(8,128)(2,1)S(1)} %get-tuple-element.17), channel_id=1, source_target_pairs={{0,8},{1,12},{2,0},{3,4},{4,9},{5,13},{6,1},{7,5},{8,10},{9,14},{1... | collective-permute-start | bytes 786440 | tf_op jit(solution)/shard_map/ppermute | solution.py:244
  36.2 25.4 %collective-permute-start.7 = (bf16[32,32,128]{2,1,0:T(8,128)(2,1)S(1)}, bf16[32,32,128]{2,1,0:T(8,128)(2,1)S(1)}, u32[]{:S(2)}, u32[]{:S(2)}) collective-permute-start(bf16[32,32,128]{2,1,0:T(8,128)(2,1)S(1)} %get-tuple-element.17), channel_id=1, source_target_pairs={{0,12},{1,8},{2,4},{3,0},{4,13},{5,9},{6,5},{7,1},{8,14},{9,10},{1... | collective-permute-start | bytes 786440 | tf_op jit(solution)/shard_map/ppermute | solution.py:244
  54.2 1.2 %copy-start = (bf16[128,32,128]{2,1,0:T(8,128)(2,1)S(1)}, bf16[128,32,128]{2,1,0:T(8,128)(2,1)}, u32[]{:S(2)}) copy-start(bf16[128,32,128]{2,1,0:T(8,128)(2,1)} %all-gather.3.cloned.1.call-done) | copy-start | bytes 3145732
  55.6 6.0 %copy-start.2 = (bf16[128,128]{1,0:T(8,128)(2,1)S(1)}, bf16[128,128]{1,0:T(8,128)(2,1)}, u32[]{:S(2)}) copy-start(bf16[128,128]{1,0:T(8,128)(2,1)} %w_ref.3) | copy-start | bytes 98308
  55.6 6.0 %copy-start.6 = (f32[128]{0:T(128)S(1)}, f32[128]{0:T(128)}, u32[]{:S(2)}) copy-start(f32[128]{0:T(128)} %param.34) | copy-start | bytes 1540
  55.6 6.0 %copy-start.7 = (f32[128]{0:T(128)S(1)}, f32[128]{0:T(128)}, u32[]{:S(2)}) copy-start(f32[128]{0:T(128)} %param.35) | copy-start | bytes 1540
  55.6 6.0 %copy-start.8 = (f32[128]{0:T(128)S(1)}, f32[128]{0:T(128)}, u32[]{:S(2)}) copy-start(f32[128]{0:T(128)} %param.37) | copy-start | bytes 1540
Sparse Core Ops, SparseCore 0:
  29.2 24.9 all-gather.2

commit v6 on v5

--- a/solution.py
+++ b/solution.py
@@ -41,7 +41,7 @@
 
 
 def pack_kernel(x_ref, mask_ref, res_ref, gain_ref, shift_ref, w_ref, bias_ref,
-                left_ref, right_ref, lscr, rscr):
+                out_ref, lscr, rscr):
     seqs, rows = mask_ref.shape
     half = w_ref.shape[0] // 2
     per = LANES // half
@@ -66,15 +66,26 @@
     sub = iota((seqs, LANES), 1) // half
     for tile in range(width // LANES):
         at = slice(tile * LANES, (tile + 1) * LANES)
-        for scr, ref, first in ((lscr, left_ref, 0), (rscr, right_ref, LANES)):
+        for side, scr, first in ((0, lscr, 0), (1, rscr, LANES)):
             value = scr[pl.ds(tile * per, seqs, stride=rows), :]
             for k in range(1, per):
                 value = jnp.where(sub == k, scr[pl.ds(tile * per + k, seqs, stride=rows), :], value)
             value = (value + bias[:, first:first + LANES]) * live_wide[:, at]
-            ref[:, at] = value.astype(BF16)
+            out_ref[side, :, at] = value.astype(BF16)
     live_tile = dot(live, (iota((rows, LANES), 0) == iota((rows, LANES), 1)).astype(BF16))
-    left_ref[:, width:] = live_tile.astype(BF16)
-    right_ref[:, width:] = live_tile.astype(BF16)
+    for side in range(2):
+        out_ref[side, :, width:] = live_tile.astype(BF16)
+
+
+def join_kernel(own_ref, other_ref, base_ref, left_ref, right_ref):
+    for n, ref in enumerate((own_ref, other_ref)):
+        left_ref[n] = ref[0]
+        right_ref[n] = ref[1]
+
+
+def pair_kernel(own_ref, other_ref, pair_ref):
+    pair_ref[0] = own_ref[...]
+    pair_ref[1] = other_ref[...]
 
 
 def pick_columns(values, start, size):
@@ -116,12 +127,13 @@
 
 
 def edges_kernel(count, *refs):
-    rights, lefts = refs[:count], refs[count:2 * count]
+    pairs = count // 2
+    rights, lefts = refs[:pairs], refs[pairs:2 * pairs]
     (base_ref, block_ref, res_ref, gain_ref, shift_ref, w_ref, bias_ref,
      updated_ref, left_ref, right_ref, gate_ref,
-     lall, rall, tscr, rscr, oscr, nscr, escr) = refs[2 * count:]
+     lall, rall, tscr, rscr, oscr, nscr, escr) = refs[2 * pairs:]
     rows, cols, channels = base_ref.shape
-    seqs = lefts[0].shape[0]
+    seqs = lefts[0].shape[1]
     half = block_ref.shape[0] // LANES
     per = LANES // half
     width = rows * half
@@ -129,9 +141,10 @@
     z = lax.axis_index("resi")
     q = lax.axis_index(PLANE)
     row_start, col_start = z * rows, q * cols
-    for step in range(count):
-        lall[q ^ step] = lefts[step][...]
-        rall[z ^ step] = rights[step][...]
+    for step in range(pairs):
+        for n in range(2):
+            lall[q ^ (step + n * pairs)] = lefts[step][n]
+            rall[z ^ (step + n * pairs)] = rights[step][n]
     right = rall[...].reshape(total_seqs, -1)
     left = lall[...].reshape(total_seqs, -1)
     for at in range(0, width, LANES):
@@ -180,9 +193,14 @@
         right_ref[k] = escr[pl.ds(k, rows, stride=cols), :].astype(BF16)
 
 
-def panel_kernel(left_ref, panel_ref):
-    for step in range(left_ref.shape[0]):
-        panel_ref[step] = left_ref[step].astype(F32).reshape(panel_ref.shape[1:])
+def panel_kernel(count, *refs):
+    pairs = count // 2
+    lefts, panel_ref = refs[:pairs], refs[pairs]
+    q = lax.axis_index(PLANE)
+    for step in range(pairs):
+        for n in range(2):
+            panel_ref[q ^ (step + n * pairs)] = (
+                lefts[step][n].astype(F32).reshape(panel_ref.shape[1:]))
 
 
 def add_block(step, panel_ref, right_ref, rscr, before, store):
@@ -233,18 +251,22 @@
         out_ref[i0:i0 + chunk] = value.astype(BF16).reshape(chunk, cols, channels)
 
 
-def send_plane(block, count):
-    return [block] + [
-        lax.ppermute(block, PLANE, [(p, p ^ m) for p in range(count)]) for m in range(1, count)
+def swap_cores(block, count):
+    return lax.ppermute(block, PLANE, [(p, p ^ (count // 2)) for p in range(count)])
+
+
+def send_plane(pair, count):
+    return [pair] + [
+        lax.ppermute(pair, PLANE, [(p, p ^ m) for p in range(count)]) for m in range(1, count // 2)
     ]
 
 
-def send_turned(block, count):
+def send_turned(block, count, steps):
     return [
         lax.ppermute(
             block, GROUP,
             [(z * count + p, (p ^ m) * count + z) for z in range(count) for p in range(count)])
-        for m in range(count)
+        for m in range(steps)
     ]
 
 
@@ -294,23 +316,25 @@
     shape = jax.ShapeDtypeStruct
     residue = flat(residue_pad_mask)
     chain = flat(residue_chain_index)
-    pack = shape((seqs, width + LANES), BF16)
+    pack = shape((2, seqs, width + LANES), BF16)
     normed = call(norm_kernel, shape((seqs * rows, depth), F32), [], [homolog_matrix],
                   flops=1 << 36, name="norm")
-    left, right = call(
-        pack_kernel, [pack, pack],
+    factors = call(
+        pack_kernel, pack,
         [pltpu.VMEM((seqs * rows, LANES), F32)] * 2,
         [normed, sequence_pad_mask, residue, flat(homolog_standard_factor),
          flat(homolog_standard_offset), factor_mapping_matrices.T, flat(outer_side_biases)],
         flops=1 << 30, name="pack")
-    rights = send_turned(right, count)
-    lefts = send_plane(left, count)
+    other = swap_cores(factors, count)
     base, block = call(
         base_kernel,
         [shape((rows, cols, channels), F32), shape((half * LANES, per * channels), BF16)],
         [pltpu.VMEM((LANES, channels), F32), pltpu.VMEM((half * half, channels), F32)],
         [pair_features, relative_position_table, chain, outer_pair_projection],
         flops=1 << 30, name="base")
+    left, right = call(join_kernel, [pack, pack], [], [factors, other, base], name="join")
+    rights = send_turned(right, count, count // 2)
+    lefts = send_plane(left, count)
     updated, left_edge, right_edge, gate = call(
         functools.partial(edges_kernel, count),
         [shape((rows, cols, channels), BF16), shape((rows, cols, channels), BF16),
@@ -323,12 +347,15 @@
         rights + lefts + [base, block, residue, flat(pair_norm_gain), flat(pair_norm_bias),
                           triangle_projection_weights, flat(triangle_projection_biases)],
         name="edges")
-    right_edges = send_turned(right_edge, count)
-    left_edges = lax.all_gather(left_edge, PLANE)
+    right_edges = send_turned(right_edge, count, count)
+    left_pair = call(pair_kernel, shape((2,) + left_edge.shape, BF16), [],
+                     [left_edge, swap_cores(left_edge, count)], name="pair")
+    left_edges = send_plane(left_pair, count)
     sums = shape((rows * cols, channels), F32)
     turned = pltpu.VMEM((rows * cols, channels), F32)
     panel = call(
-        panel_kernel, shape((count, rows * cols, channels), F32), [], [left_edges], name="panel")
+        functools.partial(panel_kernel, count), shape((count, rows * cols, channels), F32), [],
+        left_edges, name="panel")
     args = []
     for step in range(count - 1):
         args = [call(functools.partial(step_kernel, step), sums, [turned],

time: 71.9 us -> 57.7 us (0.80)
  between operations: 13.6 us -> 0.27 us
  waiting for transfers between devices: 18.9 us -> 22.4 us
  starting transfers between devices: 21.4 us -> 19.3 us
  local copies, waits for them, and re-layouts: 2.62 us -> 1.44 us
    all_gather x1 -> x0, waiting for transfers between devices: 15.5 us -> none  [body(): left_edges = lax.all_gather(left_edge, PLANE)]
    ppermute x3 -> x4, waiting for transfers between devices: 2.2 us -> 15.8 us  [the longest x2 14.1 us: send_plane(): lax.ppermute(pair, PLANE, [(p, p ^ m) for p in range(count)])]
    ppermute x8 -> x6, waiting for transfers between devices: 1.17 us -> 6.6 us  [send_turned(): lax.ppermute(block, GROUP, [(z * count + p, (p ^ m) * count + z) for z in...]
    ppermute x8 -> x6, starting transfers between devices: 19.4 us -> 14.9 us  [send_turned(): lax.ppermute(block, GROUP, [(z * count + p, (p ^ m) * count + z) for z in...]
    ppermute x3 -> x4, starting transfers between devices: 2.01 us -> 4.38 us  [the longest x2 4.18 us: send_plane(): lax.ppermute(pair, PLANE, [(p, p ^ m) for p in range(count)])]
    unnamed x40 -> x38, local copies, waits for them, and re-layouts: 2.61 us -> 1.44 us
    pallas_call x9 -> x11, Pallas kernels: 14.7 us -> 14.1 us  [call(): pl.pallas_call(kernel, out_shape=outs, in_specs=[vmem] * len(args), out_s...]
  transfers between devices with their start and end apart: 12 -> 10, of which waited for: 4 -> 5; matrix products, arithmetic and copies ran while one was open for 0% -> 0% of each run, Pallas kernels for 8% -> 10%
where the time goes in v6:
time: 57.7 us; the launch traced here: 57.5 us
  waiting for transfers between devices  22.4 us (39%)
  starting transfers between devices  19.3 us (33%)
  Pallas kernels  14.1 us (24%)
  local copies, waits for them, and re-layouts  1.44 us (2%)
    ppermute x6, starting transfers between devices, send_turned(): lax.ppermute(block, GROUP, [(z * count + p, (p ^ m) * count + z) for z in...  14.9 us
    ppermute x2, waiting for transfers between devices, send_plane(): lax.ppermute(pair, PLANE, [(p, p ^ m) for p in range(count)])  14.1 us
    pallas_call x11, Pallas kernels, call(): pl.pallas_call(kernel, out_shape=outs, in_specs=[vmem] * len(args), out_s...  14.1 us
    ppermute x6, waiting for transfers between devices, send_turned(): lax.ppermute(block, GROUP, [(z * count + p, (p ^ m) * count + z) for z in...  6.6 us
    ppermute x2, starting transfers between devices, send_plane(): lax.ppermute(pair, PLANE, [(p, p ^ m) for p in range(count)])  4.18 us
    ppermute x2, waiting for transfers between devices, swap_cores(): lax.ppermute(block, PLANE, [(p, p ^ count // 2) for p in range(count)])  1.66 us
    unnamed x38, local copies, waits for them, and re-layouts  1.44 us
  transfers between devices with their start and end apart: 10, of which 5 were waited for; matrix products, arithmetic and copies ran while one was open for 0% of the time, Pallas kernels for 10%

profile of v6, /device:TPU:1, one launch (start us, length us, event | category | flops | bytes accessed | tf_op | source)
XLA Modules:
  0.0 57.5 jit_solution(15972401119583704282)
XLA Ops:
  0.0 1.1 %copy-done.8 = bf16[32,32,256]{2,1,0:T(8,128)(2,1)S(1)} copy-done((bf16[32,32,256]{2,1,0:T(8,128)(2,1)S(1)}, bf16[32,32,256]{2,1,0:T(8,128)(2,1)}, u32[]{:S(2)}) %copy-start.8) | copy-done | bytes 524312
  1.1 0.4 norm.1.x_ref
  1.5 0.3 copy-done.11
  1.8 0.0 copy-start.18
  1.8 0.0 copy-start
  1.9 0.0 copy-start.3
  1.9 0.0 copy-start.4
  1.9 1.1 %pack.1.own_ref = bf16[2,32,1152]{2,1,0:T(8,128)(2,1)S(1)} custom-call(f32[1024,256]{1,0:T(8,128)S(1)} %norm.1.x_ref, s32[32,32]{1,0:T(8,128)S(1)} %copy-done.13, s32[1,128]{1,0:T(1,128)S(1)} %bitcast.11, f32[1,256]{1,0:T(1,128)S(1)} %bitcast.19, f32[1,256]{1,0:T(1,128)S(1)} %bitcast.20, bf16[64,256]{1,0:T(8,128)(2,1)S(1)} %bitcast.18, f32[1,64]{1,0:T(1,128)S(1)} %bitcast.21), custom_call_target="tpu_custom_call" | custom-call | flops 1073741824 | bytes 1088256 | tf_op jit(solution)/shard_map/pack/pallas_call | solution.py:276
  3.0 0.1 collective-permute-start
  3.1 1.2 %base.1 = (f32[32,32,128]{2,1,0:T(8,128)S(1)}, bf16[4096,512]{1,0:T(8,128)(2,1)S(1)}) custom-call(bf16[32,32,128]{2,1,0:T(8,128)(2,1)S(1)} %copy-done.9, bf16[66,128]{1,0:T(8,128)(2,1)S(1)} %copy-done.12, s32[1,128]{1,0:T(1,128)S(1)} %bitcast.22, bf16[1024,128]{1,0:T(8,128)(2,1)S(1)} %copy-done.10), custom_call_target="tpu_custom_call" | custom-call | flops 1073741824 | bytes 541696 | tf_op jit(solution)/shard_map/base/pallas_call | solution.py:276
  4.3 0.1 collective-permute-done.other_ref
  4.4 4.8 %collective-permute-start.2 = (bf16[2,32,1152]{2,1,0:T(8,128)(2,1)S(1)}, bf16[2,32,1152]{2,1,0:T(8,128)(2,1)S(1)}, u32[]{:S(2)}, u32[]{:S(2)}) collective-permute-start(bf16[2,32,1152]{2,1,0:T(8,128)(2,1)S(1)} %get-tuple-element.14), channel_id=1, source_target_pairs={{0,4},{1,0},{2,12},{3,8},{4,5},{5,1},{6,13},{7,9},{8,6},{9,2},{10,... | collective-permute-start | bytes 442376 | tf_op jit(solution)/shard_map/ppermute | solution.py:266
  9.2 1.9 %collective-permute-start.1 = (bf16[2,32,1152]{2,1,0:T(8,128)(2,1)S(1)}, bf16[2,32,1152]{2,1,0:T(8,128)(2,1)S(1)}, u32[]{:S(2)}, u32[]{:S(2)}) collective-permute-start(bf16[2,32,1152]{2,1,0:T(8,128)(2,1)S(1)} %get-tuple-element.14), channel_id=1, source_target_pairs={{0,0},{1,4},{2,8},{3,12},{4,1},{5,5},{6,9},{7,13},{8,2},{9,6},{10,... | collective-permute-start | bytes 442376 | tf_op jit(solution)/shard_map/ppermute | solution.py:266
  11.1 2.4 %collective-permute-start.3 = (bf16[2,32,1152]{2,1,0:T(8,128)(2,1)S(1)}, bf16[2,32,1152]{2,1,0:T(8,128)(2,1)S(1)}, u32[]{:S(2)}, u32[]{:S(2)}) collective-permute-start(bf16[2,32,1152]{2,1,0:T(8,128)(2,1)S(1)} %get-tuple-element.15.refs_2_), channel_id=1, source_target_pairs={{0,1},{1,0},{2,3},{3,2},{4,5},{5,4},{6,7},{7,6},{8,9},{9,8},{10,11... | collective-permute-start | bytes 442376 | tf_op jit(solution)/shard_map/ppermute | solution.py:260
  13.6 4.6 %collective-permute-done.1.refs_0_ = bf16[2,32,1152]{2,1,0:T(8,128)(2,1)S(1)} collective-permute-done((bf16[2,32,1152]{2,1,0:T(8,128)(2,1)S(1)}, bf16[2,32,1152]{2,1,0:T(8,128)(2,1)S(1)}, u32[]{:S(2)}, u32[]{:S(2)}) %collective-permute-start.1) | collective-permute-done | bytes 147488 | tf_op jit(solution)/shard_map/ppermute | solution.py:266
  18.1 3.8 %edges.1 = (bf16[32,32,128]{2,1,0:T(8,128)(2,1)S(1)}, bf16[32,32,128]{2,1,0:T(8,128)(2,1)S(1)}, bf16[32,32,128]{2,1,0:T(8,128)(2,1)S(1)}, f32[1024,128]{1,0:T(8,128)S(1)}) custom-call(bf16[2,32,1152]{2,1,0:T(8,128)(2,1)S(1)} %collective-permute-done.1.refs_0_, bf16[2,32,1152]{2,1,0:T(8,128)(2,1)S(1)} %collective-permute-done.2.refs_1_, ...), custom_call_target="tpu_custom_call" | custom-call | bytes 5476352 | tf_op jit(solution)/shard_map/edges/pallas_call | solution.py:276
  21.9 0.1 collective-permute-start.5
  22.0 1.5 %collective-permute-done.5.other_ref = bf16[32,32,128]{2,1,0:T(8,128)(2,1)S(1)} collective-permute-done((bf16[32,32,128]{2,1,0:T(8,128)(2,1)S(1)}, bf16[32,32,128]{2,1,0:T(8,128)(2,1)S(1)}, u32[]{:S(2)}, u32[]{:S(2)}) %collective-permute-start.5) | collective-permute-done | bytes 262176 | tf_op jit(solution)/shard_map/ppermute | solution.py:255
  23.6 1.8 %collective-permute-start.6 = (bf16[2,32,32,128]{3,2,1,0:T(8,128)(2,1)S(1)}, bf16[2,32,32,128]{3,2,1,0:T(8,128)(2,1)S(1)}, u32[]{:S(2)}, u32[]{:S(2)}) collective-permute-start(bf16[2,32,32,128]{3,2,1,0:T(8,128)(2,1)S(1)} %pair.1.refs_0_), channel_id=1, source_target_pairs={{0,1},{1,0},{2,3},{3,2},{4,5},{5,4},{6,7},{7,6},{8,9},{9,8},{10,11... | collective-permute-start | bytes 1572872 | tf_op jit(solution)/shard_map/ppermute | solution.py:260
  25.3 4.1 %collective-permute-start.9 = (bf16[32,32,128]{2,1,0:T(8,128)(2,1)S(1)}, bf16[32,32,128]{2,1,0:T(8,128)(2,1)S(1)}, u32[]{:S(2)}, u32[]{:S(2)}) collective-permute-start(bf16[32,32,128]{2,1,0:T(8,128)(2,1)S(1)} %get-tuple-element.17), channel_id=1, source_target_pairs={{0,0},{1,4},{2,8},{3,12},{4,1},{5,5},{6,9},{7,13},{8,2},{9,6},{10,... | collective-permute-start | bytes 786440 | tf_op jit(solution)/shard_map/ppermute | solution.py:266
  29.4 1.1 %collective-permute-start.8 = (bf16[32,32,128]{2,1,0:T(8,128)(2,1)S(1)}, bf16[32,32,128]{2,1,0:T(8,128)(2,1)S(1)}, u32[]{:S(2)}, u32[]{:S(2)}) collective-permute-start(bf16[32,32,128]{2,1,0:T(8,128)(2,1)S(1)} %get-tuple-element.17), channel_id=1, source_target_pairs={{0,4},{1,0},{2,12},{3,8},{4,5},{5,1},{6,13},{7,9},{8,6},{9,2},{10,... | collective-permute-start | bytes 786440 | tf_op jit(solution)/shard_map/ppermute | solution.py:266
  30.5 3.0 %collective-permute-start.4 = (bf16[32,32,128]{2,1,0:T(8,128)(2,1)S(1)}, bf16[32,32,128]{2,1,0:T(8,128)(2,1)S(1)}, u32[]{:S(2)}, u32[]{:S(2)}) collective-permute-start(bf16[32,32,128]{2,1,0:T(8,128)(2,1)S(1)} %get-tuple-element.17), channel_id=1, source_target_pairs={{0,12},{1,8},{2,4},{3,0},{4,13},{5,9},{6,5},{7,1},{8,14},{9,10},{1... | collective-permute-start | bytes 786440 | tf_op jit(solution)/shard_map/ppermute | solution.py:266
  33.6 14.1 %collective-permute-done.6.refs_1_ = bf16[2,32,32,128]{3,2,1,0:T(8,128)(2,1)S(1)} collective-permute-done((bf16[2,32,32,128]{3,2,1,0:T(8,128)(2,1)S(1)}, bf16[2,32,32,128]{3,2,1,0:T(8,128)(2,1)S(1)}, u32[]{:S(2)}, u32[]{:S(2)}) %collective-permute-start.6) | collective-permute-done | bytes 524320 | tf_op jit(solution)/shard_map/ppermute | solution.py:260
  47.7 0.1 panel.1.panel_ref
  47.9 0.0 copy-start.1
  47.9 0.0 copy-start.6
  47.9 0.0 copy-start.7
  47.9 1.6 %triangle.3.refs_0_ = f32[1024,128]{1,0:T(8,128)S(1)} custom-call(bf16[32,32,128]{2,1,0:T(8,128)(2,1)S(1)} %collective-permute-done.9.right_ref, f32[4,1024,128]{2,1,0:T(8,128)S(1)} %panel.1.panel_ref), custom_call_target="tpu_custom_call" | custom-call | bytes 2359296 | tf_op jit(solution)/shard_map/triangle/pallas_call | solution.py:276
  49.5 2.0 %collective-permute-done.8.right_ref = bf16[32,32,128]{2,1,0:T(8,128)(2,1)S(1)} collective-permute-done((bf16[32,32,128]{2,1,0:T(8,128)(2,1)S(1)}, bf16[32,32,128]{2,1,0:T(8,128)(2,1)S(1)}, u32[]{:S(2)}, u32[]{:S(2)}) %collective-permute-start.8) | collective-permute-done | bytes 262176 | tf_op jit(solution)/shard_map/ppermute | solution.py:266
  51.5 1.6 %triangle.4.refs_0_ = f32[1024,128]{1,0:T(8,128)S(1)} custom-call(bf16[32,32,128]{2,1,0:T(8,128)(2,1)S(1)} %collective-permute-done.8.right_ref, f32[4,1024,128]{2,1,0:T(8,128)S(1)} %panel.1.panel_ref, f32[1024,128]{1,0:T(8,128)S(1)} %triangle.3.refs_0_), custom_call_target="tpu_custom_call" | custom-call | bytes 2883584 | tf_op jit(solution)/shard_map/triangle/pallas_call | solution.py:276
  53.1 1.6 %triangle.5.before = f32[1024,128]{1,0:T(8,128)S(1)} custom-call(bf16[32,32,128]{2,1,0:T(8,128)(2,1)S(1)} %collective-permute-done.7.right_ref, f32[4,1024,128]{2,1,0:T(8,128)S(1)} %panel.1.panel_ref, f32[1024,128]{1,0:T(8,128)S(1)} %triangle.4.refs_0_), custom_call_target="tpu_custom_call" | custom-call | bytes 2883584 | tf_op jit(solution)/shard_map/triangle/pallas_call | solution.py:276
  54.7 2.8 %final.1 = bf16[32,32,128]{2,1,0:T(8,128)(2,1)} custom-call(bf16[32,32,128]{2,1,0:T(8,128)(2,1)S(1)} %collective-permute-done.4.right_ref, f32[4,1024,128]{2,1,0:T(8,128)S(1)} %panel.1.panel_ref, f32[1024,128]{1,0:T(8,128)S(1)} %triangle.5.before, bf16[32,32,128]{2,1,0:T(8,128)(2,1)S(1)} %get-tuple-element.19.updated_ref, ...), custom_call_target="tpu_custom_call" | custom-call | bytes 3704320 | tf_op jit(solution)/shard_map/final/pallas_call | solution.py:276
  (38 shorter events, 0.1 us)
Async XLA Ops:
  0.0 1.5 %copy-start.2 = (s32[128]{0:T(128)S(1)}, s32[128]{0:T(128)}, u32[]{:S(2)}) copy-start(s32[128]{0:T(128)} %param.22) | copy-start | bytes 1540
  0.0 1.1 %copy-start.8 = (bf16[32,32,256]{2,1,0:T(8,128)(2,1)S(1)}, bf16[32,32,256]{2,1,0:T(8,128)(2,1)}, u32[]{:S(2)}) copy-start(bf16[32,32,256]{2,1,0:T(8,128)(2,1)} %x_ref.1) | copy-start | bytes 1572868
  1.1 0.8 %copy-start.11 = (bf16[256,64]{0,1:T(8,128)(2,1)S(1)}, bf16[256,64]{0,1:T(8,128)(2,1)}, u32[]{:S(2)}) copy-start(bf16[256,64]{0,1:T(8,128)(2,1)} %param.26) | copy-start | bytes 98308
  1.1 0.8 %copy-start.13 = (s32[32,32]{1,0:T(8,128)S(1)}, s32[32,32]{1,0:T(8,128)}, u32[]{:S(2)}) copy-start(s32[32,32]{1,0:T(8,128)} %mask_ref.1) | copy-start | bytes 12292
  1.1 0.8 %copy-start.14 = (f32[256]{0:T(256)S(1)}, f32[256]{0:T(256)}, u32[]{:S(2)}) copy-start(f32[256]{0:T(256)} %param.24) | copy-start | bytes 3076
  1.1 0.8 %copy-start.15 = (f32[256]{0:T(256)S(1)}, f32[256]{0:T(256)}, u32[]{:S(2)}) copy-start(f32[256]{0:T(256)} %param.25) | copy-start | bytes 3076
  1.1 0.8 %copy-start.16 = (f32[64]{0:T(128)S(1)}, f32[64]{0:T(128)}, u32[]{:S(2)}) copy-start(f32[64]{0:T(128)} %param.27) | copy-start | bytes 772
  1.1 2.0 %copy-start.9 = (bf16[32,32,128]{2,1,0:T(8,128)(2,1)S(1)}, bf16[32,32,128]{2,1,0:T(8,128)(2,1)}, u32[]{:S(2)}) copy-start(bf16[32,32,128]{2,1,0:T(8,128)(2,1)} %pair_ref.1) | copy-start | bytes 786436
  1.1 2.0 %copy-start.10 = (bf16[1024,128]{1,0:T(8,128)(2,1)S(1)}, bf16[1024,128]{1,0:T(8,128)(2,1)}, u32[]{:S(2)}) copy-start(bf16[1024,128]{1,0:T(8,128)(2,1)} %w_ref.2) | copy-start | bytes 786436
  1.1 2.0 %copy-start.12 = (bf16[66,128]{1,0:T(8,128)(2,1)S(1)}, bf16[66,128]{1,0:T(8,128)(2,1)}, u32[]{:S(2)}) copy-start(bf16[66,128]{1,0:T(8,128)(2,1)} %table_ref.1) | copy-start | bytes 50692
  1.1 2.0 %copy-start.17 = (s32[128]{0:T(128)S(1)}, s32[128]{0:T(128)}, u32[]{:S(2)}) copy-start(s32[128]{0:T(128)} %param.23) | copy-start | bytes 1540
  1.8 11.7 %copy-start.18 = (f32[640]{0:T(1024)S(1)}, f32[640]{0:T(1024)}, u32[]{:S(2)}) copy-start(f32[640]{0:T(1024)} %param.33) | copy-start | bytes 7684
  1.8 16.3 %copy-start = (bf16[128,640]{1,0:T(8,128)(2,1)S(1)}, bf16[128,640]{1,0:T(8,128)(2,1)}, u32[]{:S(2)}) copy-start(bf16[128,640]{1,0:T(8,128)(2,1)} %refs_9_.1) | copy-start | bytes 491524
  1.9 16.3 %copy-start.3 = (f32[128]{0:T(128)S(1)}, f32[128]{0:T(128)}, u32[]{:S(2)}) copy-start(f32[128]{0:T(128)} %param.30) | copy-start | bytes 1540
  1.9 16.3 %copy-start.4 = (f32[128]{0:T(128)S(1)}, f32[128]{0:T(128)}, u32[]{:S(2)}) copy-start(f32[128]{0:T(128)} %param.31) | copy-start | bytes 1540
  3.0 1.4 %collective-permute-start = (bf16[2,32,1152]{2,1,0:T(8,128)(2,1)S(1)}, bf16[2,32,1152]{2,1,0:T(8,128)(2,1)S(1)}, u32[]{:S(2)}, u32[]{:S(2)}) collective-permute-start(bf16[2,32,1152]{2,1,0:T(8,128)(2,1)S(1)} %pack.1.own_ref), channel_id=1, source_target_pairs={{0,2},{1,3},{2,0},{3,1},{4,6},{5,7},{6,4},{7,5},{8,10},{9,11},{10,... | collective-permute-start | bytes 442376 | tf_op jit(solution)/shard_map/ppermute | solution.py:255
  4.4 9.1 %collective-permute-start.2 = (bf16[2,32,1152]{2,1,0:T(8,128)(2,1)S(1)}, bf16[2,32,1152]{2,1,0:T(8,128)(2,1)S(1)}, u32[]{:S(2)}, u32[]{:S(2)}) collective-permute-start(bf16[2,32,1152]{2,1,0:T(8,128)(2,1)S(1)} %get-tuple-element.14), channel_id=1, source_target_pairs={{0,4},{1,0},{2,12},{3,8},{4,5},{5,1},{6,13},{7,9},{8,6},{9,2},{10,... | collective-permute-start | bytes 442376 | tf_op jit(solution)/shard_map/ppermute | solution.py:266
  9.2 8.9 %collective-permute-start.1 = (bf16[2,32,1152]{2,1,0:T(8,128)(2,1)S(1)}, bf16[2,32,1152]{2,1,0:T(8,128)(2,1)S(1)}, u32[]{:S(2)}, u32[]{:S(2)}) collective-permute-start(bf16[2,32,1152]{2,1,0:T(8,128)(2,1)S(1)} %get-tuple-element.14), channel_id=1, source_target_pairs={{0,0},{1,4},{2,8},{3,12},{4,1},{5,5},{6,9},{7,13},{8,2},{9,6},{10,... | collective-permute-start | bytes 442376 | tf_op jit(solution)/shard_map/ppermute | solution.py:266
  11.1 7.0 %collective-permute-start.3 = (bf16[2,32,1152]{2,1,0:T(8,128)(2,1)S(1)}, bf16[2,32,1152]{2,1,0:T(8,128)(2,1)S(1)}, u32[]{:S(2)}, u32[]{:S(2)}) collective-permute-start(bf16[2,32,1152]{2,1,0:T(8,128)(2,1)S(1)} %get-tuple-element.15.refs_2_), channel_id=1, source_target_pairs={{0,1},{1,0},{2,3},{3,2},{4,5},{5,4},{6,7},{7,6},{8,9},{9,8},{10,11... | collective-permute-start | bytes 442376 | tf_op jit(solution)/shard_map/ppermute | solution.py:260
  21.9 1.6 %collective-permute-start.5 = (bf16[32,32,128]{2,1,0:T(8,128)(2,1)S(1)}, bf16[32,32,128]{2,1,0:T(8,128)(2,1)S(1)}, u32[]{:S(2)}, u32[]{:S(2)}) collective-permute-start(bf16[32,32,128]{2,1,0:T(8,128)(2,1)S(1)} %get-tuple-element.18.own_ref), channel_id=1, source_target_pairs={{0,2},{1,3},{2,0},{3,1},{4,6},{5,7},{6,4},{7,5},{8,10},{9,11},{10,... | collective-permute-start | bytes 786440 | tf_op jit(solution)/shard_map/ppermute | solution.py:255
  23.6 24.2 %collective-permute-start.6 = (bf16[2,32,32,128]{3,2,1,0:T(8,128)(2,1)S(1)}, bf16[2,32,32,128]{3,2,1,0:T(8,128)(2,1)S(1)}, u32[]{:S(2)}, u32[]{:S(2)}) collective-permute-start(bf16[2,32,32,128]{3,2,1,0:T(8,128)(2,1)S(1)} %pair.1.refs_0_), channel_id=1, source_target_pairs={{0,1},{1,0},{2,3},{3,2},{4,5},{5,4},{6,7},{7,6},{8,9},{9,8},{10,11... | collective-permute-start | bytes 1572872 | tf_op jit(solution)/shard_map/ppermute | solution.py:260
  25.3 22.6 %collective-permute-start.9 = (bf16[32,32,128]{2,1,0:T(8,128)(2,1)S(1)}, bf16[32,32,128]{2,1,0:T(8,128)(2,1)S(1)}, u32[]{:S(2)}, u32[]{:S(2)}) collective-permute-start(bf16[32,32,128]{2,1,0:T(8,128)(2,1)S(1)} %get-tuple-element.17), channel_id=1, source_target_pairs={{0,0},{1,4},{2,8},{3,12},{4,1},{5,5},{6,9},{7,13},{8,2},{9,6},{10,... | collective-permute-start | bytes 786440 | tf_op jit(solution)/shard_map/ppermute | solution.py:266
  29.4 22.1 %collective-permute-start.8 = (bf16[32,32,128]{2,1,0:T(8,128)(2,1)S(1)}, bf16[32,32,128]{2,1,0:T(8,128)(2,1)S(1)}, u32[]{:S(2)}, u32[]{:S(2)}) collective-permute-start(bf16[32,32,128]{2,1,0:T(8,128)(2,1)S(1)} %get-tuple-element.17), channel_id=1, source_target_pairs={{0,4},{1,0},{2,12},{3,8},{4,5},{5,1},{6,13},{7,9},{8,6},{9,2},{10,... | collective-permute-start | bytes 786440 | tf_op jit(solution)/shard_map/ppermute | solution.py:266
  30.5 22.6 %collective-permute-start.7 = (bf16[32,32,128]{2,1,0:T(8,128)(2,1)S(1)}, bf16[32,32,128]{2,1,0:T(8,128)(2,1)S(1)}, u32[]{:S(2)}, u32[]{:S(2)}) collective-permute-start(bf16[32,32,128]{2,1,0:T(8,128)(2,1)S(1)} %get-tuple-element.17), channel_id=1, source_target_pairs={{0,8},{1,12},{2,0},{3,4},{4,9},{5,13},{6,1},{7,5},{8,10},{9,14},{1... | collective-permute-start | bytes 786440 | tf_op jit(solution)/shard_map/ppermute | solution.py:266
  30.5 24.2 %collective-permute-start.4 = (bf16[32,32,128]{2,1,0:T(8,128)(2,1)S(1)}, bf16[32,32,128]{2,1,0:T(8,128)(2,1)S(1)}, u32[]{:S(2)}, u32[]{:S(2)}) collective-permute-start(bf16[32,32,128]{2,1,0:T(8,128)(2,1)S(1)} %get-tuple-element.17), channel_id=1, source_target_pairs={{0,12},{1,8},{2,4},{3,0},{4,13},{5,9},{6,5},{7,1},{8,14},{9,10},{1... | collective-permute-start | bytes 786440 | tf_op jit(solution)/shard_map/ppermute | solution.py:266
  47.9 6.8 %copy-start.1 = (bf16[128,128]{1,0:T(8,128)(2,1)S(1)}, bf16[128,128]{1,0:T(8,128)(2,1)}, u32[]{:S(2)}) copy-start(bf16[128,128]{1,0:T(8,128)(2,1)} %w_ref.3) | copy-start | bytes 98308
  47.9 6.8 %copy-start.5 = (f32[128]{0:T(128)S(1)}, f32[128]{0:T(128)}, u32[]{:S(2)}) copy-start(f32[128]{0:T(128)} %param.34) | copy-start | bytes 1540
  47.9 6.8 %copy-start.6 = (f32[128]{0:T(128)S(1)}, f32[128]{0:T(128)}, u32[]{:S(2)}) copy-start(f32[128]{0:T(128)} %param.35) | copy-start | bytes 1540
  47.9 6.8 %copy-start.7 = (f32[128]{0:T(128)S(1)}, f32[128]{0:T(128)}, u32[]{:S(2)}) copy-start(f32[128]{0:T(128)} %param.37) | copy-start | bytes 1540

commit v7 on v6

--- a/solution.py
+++ b/solution.py
@@ -81,11 +81,6 @@
     for n, ref in enumerate((own_ref, other_ref)):
         left_ref[n] = ref[0]
         right_ref[n] = ref[1]
-
-
-def pair_kernel(own_ref, other_ref, pair_ref):
-    pair_ref[0] = own_ref[...]
-    pair_ref[1] = other_ref[...]
 
 
 def pick_columns(values, start, size):
@@ -193,21 +188,21 @@
         right_ref[k] = escr[pl.ds(k, rows, stride=cols), :].astype(BF16)
 
 
-def panel_kernel(count, *refs):
-    pairs = count // 2
-    lefts, panel_ref = refs[:pairs], refs[pairs]
-    q = lax.axis_index(PLANE)
-    for step in range(pairs):
-        for n in range(2):
-            panel_ref[q ^ (step + n * pairs)] = (
-                lefts[step][n].astype(F32).reshape(panel_ref.shape[1:]))
-
-
-def add_block(step, panel_ref, right_ref, rscr, before, store):
-    depth, cols, channels = right_ref.shape
-    rows = panel_ref.shape[1] // depth
-    own = lax.axis_index("resi") ^ step
-    rscr[...] = right_ref[...].astype(F32).reshape(rscr.shape)
+def panel_kernel(*refs):
+    *lefts, panel_ref = refs
+    x = lax.axis_index("seq")
+    for step, left in enumerate(lefts):
+        panel_ref[x ^ step] = left[...].astype(F32).reshape(panel_ref.shape[1:])
+
+
+def origin(step, chips):
+    source = lax.axis_index("resi") ^ step
+    return (source // chips) ^ lax.axis_index("resj"), source % chips
+
+
+def add_block(panel_ref, chip, rscr, rows, before, store):
+    cols = store.shape[0] // rows
+    depth, channels = rscr.shape[0] // cols, rscr.shape[1]
     block = 4
     tiles = cols // 8
 
@@ -221,30 +216,49 @@
         for k in range(depth):
             column = [rscr[k * cols + t * 8:k * cols + t * 8 + 8, :] for t in range(tiles)]
             for b in range(block):
-                row = panel_ref[own, pl.ds((at * block + b) * depth + k, 1), :]
+                row = panel_ref[chip, pl.ds((at * block + b) * depth + k, 1), :]
                 for t in range(tiles):
                     sums[b][t] = sums[b][t] + row * column[t]
         for b in range(block):
             for t in range(tiles):
-                store[place[b][t], :] = sums[b][t]
+                store[place[b][t], :] = sums[b][t].astype(store.dtype)
         return carry
 
     lax.fori_loop(0, rows // block, rows_body, 0)
 
 
-def step_kernel(step, right_ref, panel_ref, *refs):
-    before = refs[0] if len(refs) == 3 else None
-    add_block(step, panel_ref, right_ref, refs[-1], before, refs[-2])
-
-
-def final_kernel(step, right_ref, panel_ref, before, updated_ref, gate_ref, gain_ref, shift_ref,
-                 w_ref, bias_ref, out_ref, acc, rscr):
-    add_block(step, panel_ref, right_ref, rscr, before, acc)
+def step_kernel(step, chips, fresh, right_ref, panel_ref, *refs):
+    out_ref, rscr = refs[-2:]
+    side, chip = origin(step, chips)
+    rscr[...] = right_ref[...].astype(F32).reshape(rscr.shape)
+    before = None if fresh else refs[0].at[side]
+    add_block(panel_ref, chip, rscr, right_ref.shape[1], before, out_ref.at[side])
+
+
+def last_kernel(side, steps, chips, first_ref, second_ref, panel_ref, sums_ref, out_ref, rscr):
+    first_side, first_chip = origin(steps[0], chips)
+    second_chip = origin(steps[1], chips)[1]
+    mine = first_side == side
+
+    @pl.when(mine)
+    def _():
+        rscr[...] = first_ref[...].astype(F32).reshape(rscr.shape)
+
+    @pl.when(jnp.logical_not(mine))
+    def _():
+        rscr[...] = second_ref[...].astype(F32).reshape(rscr.shape)
+
+    chip = jnp.where(mine, first_chip, second_chip)
+    add_block(panel_ref, chip, rscr, first_ref.shape[1], sums_ref.at[side], out_ref)
+
+
+def final_kernel(own_ref, other_ref, updated_ref, gate_ref, gain_ref, shift_ref, w_ref, bias_ref, out_ref):
     rows, cols, channels = out_ref.shape
     chunk = 8
     for i0 in range(0, rows, chunk):
         at = slice(i0 * cols, (i0 + chunk) * cols)
-        normed = layer_norm(acc[at, :], gain_ref[...], shift_ref[...]).astype(BF16)
+        sums = own_ref[at, :] + other_ref[at, :].astype(F32)
+        normed = layer_norm(sums, gain_ref[...], shift_ref[...]).astype(BF16)
         result = dot(normed, w_ref[...]) + bias_ref[...]
         updated = updated_ref[i0:i0 + chunk].reshape(chunk * cols, channels).astype(F32)
         value = updated + gate_ref[at, :] * result
@@ -270,7 +284,20 @@
     ]
 
 
-def call(kernel, outs, scratch, args, flops=0, name=None):
+def send_same_core(block, count, chips, steps):
+    def target(z, p, m):
+        core, x = p // chips, p % chips
+        return ((z // chips * chips + x) ^ m) * count + core * chips + z % chips
+
+    return [
+        lax.ppermute(
+            block, GROUP,
+            [(z * count + p, target(z, p, m)) for z in range(count) for p in range(count)])
+        for m in steps
+    ]
+
+
+def call(kernel, outs, scratch, args, flops=0, aliases=None, name=None):
     vmem = pl.BlockSpec(memory_space=pltpu.VMEM)
     size = sum(a.size * a.dtype.itemsize for a in args)
     return pl.pallas_call(
@@ -279,6 +306,7 @@
         in_specs=[vmem] * len(args),
         out_specs=[vmem] * len(outs) if isinstance(outs, list) else vmem,
         scratch_shapes=scratch,
+        input_output_aliases=aliases or {},
         compiler_params=pltpu.CompilerParams(vmem_limit_bytes=40 * MIB),
         cost_estimate=pl.CostEstimate(flops=flops, bytes_accessed=size, transcendentals=0),
         name=name,
@@ -347,25 +375,32 @@
         rights + lefts + [base, block, residue, flat(pair_norm_gain), flat(pair_norm_bias),
                           triangle_projection_weights, flat(triangle_projection_biases)],
         name="edges")
-    right_edges = send_turned(right_edge, count, count)
-    left_pair = call(pair_kernel, shape((2,) + left_edge.shape, BF16), [],
-                     [left_edge, swap_cores(left_edge, count)], name="pair")
-    left_edges = send_plane(left_pair, count)
-    sums = shape((rows * cols, channels), F32)
+    chips = lax.axis_size("seq")
+    steps = [m + n * chips for m in range(chips) for n in range(2)]
+    right_edges = send_same_core(right_edge, count, chips, steps)
+    left_edges = [left_edge] + [
+        lax.ppermute(left_edge, "seq", [(x, x ^ m) for x in range(chips)]) for m in range(1, chips)
+    ]
+    block_sums = shape((rows * cols, channels), F32)
     turned = pltpu.VMEM((rows * cols, channels), F32)
-    panel = call(
-        functools.partial(panel_kernel, count), shape((count, rows * cols, channels), F32), [],
-        left_edges, name="panel")
-    args = []
-    for step in range(count - 1):
-        args = [call(functools.partial(step_kernel, step), sums, [turned],
-                     [right_edges[step], panel] + args, name="triangle")]
+    panel = call(panel_kernel, shape((chips, rows * cols, channels), F32), [], left_edges, name="panel")
+    sums = []
+    for n, step in enumerate(steps[:-2]):
+        sums = [call(
+            functools.partial(step_kernel, step, chips, n < 2), shape((2, rows * cols, channels), F32),
+            [turned], [right_edges[n], panel] + sums, aliases={2: 0} if n else None, name="triangle")]
+    last = right_edges[-2:] + [panel] + sums
+    half_sums = call(
+        functools.partial(last_kernel, 1, steps[-2:], chips), shape((rows * cols, channels), BF16),
+        [turned], last, name="others")
+    other_sums = swap_cores(half_sums, count)
+    own_sums = call(
+        functools.partial(last_kernel, 0, steps[-2:], chips), block_sums, [turned], last,
+        flops=1 << 32, name="own")
     return call(
-        functools.partial(final_kernel, count - 1), shape((rows, cols, channels), BF16),
-        [turned, turned],
-        [right_edges[-1], panel] + args + [
-            updated, gate, flat(triangle_sum_norm_gain), flat(triangle_sum_norm_bias),
-            triangle_output_weight, flat(outer_pair_bias)],
+        final_kernel, shape((rows, cols, channels), BF16), [],
+        [own_sums, other_sums, updated, gate, flat(triangle_sum_norm_gain),
+         flat(triangle_sum_norm_bias), triangle_output_weight, flat(outer_pair_bias)],
         name="final")
 
 

time: 57.7 us -> 56.2 us (0.974)
  starting transfers between devices: 19.3 us -> 17.8 us
  waiting for transfers between devices: 22.4 us -> 23.3 us
  Pallas kernels: 14.1 us -> 13.2 us
    ppermute x0 -> x5, waiting for transfers between devices: none -> 18.6 us  [the longest x4 18 us: send_same_core(): lax.ppermute(block, GROUP, [(z * count + p, target(z, p, m)) for z in ran...]
    ppermute x2 -> x1, waiting for transfers between devices: 14.1 us -> 0.01 us  [send_plane(): lax.ppermute(pair, PLANE, [(p, p ^ m) for p in range(count)])]
    ppermute x6 -> x2, starting transfers between devices: 14.9 us -> 6.67 us  [send_turned(): lax.ppermute(block, GROUP, [(z * count + p, (p ^ m) * count + z) for z in...]
    ppermute x0 -> x5, starting transfers between devices: none -> 8.02 us  [the longest x4 6.27 us: send_same_core(): lax.ppermute(block, GROUP, [(z * count + p, target(z, p, m)) for z in ran...]
    ppermute x6 -> x2, waiting for transfers between devices: 6.6 us -> 4.57 us  [send_turned(): lax.ppermute(block, GROUP, [(z * count + p, (p ^ m) * count + z) for z in...]
    ppermute x2 -> x1, starting transfers between devices: 4.18 us -> 2.43 us  [send_plane(): lax.ppermute(pair, PLANE, [(p, p ^ m) for p in range(count)])]
    ppermute x2, waiting for transfers between devices: 1.66 us -> 0.14 us  [swap_cores(): lax.ppermute(block, PLANE, [(p, p ^ count // 2) for p in range(count)])]
    pallas_call x11, Pallas kernels: 14.1 us -> 13.2 us  [call(): pl.pallas_call(kernel, out_shape=outs, in_specs=[vmem] * len(args), out_s...]
where the time goes in v7:
time: 56.2 us; the launch traced here: 56 us
  waiting for transfers between devices  23.3 us (41%)
  starting transfers between devices  17.8 us (32%)
  Pallas kernels  13.2 us (23%)
  local copies, waits for them, and re-layouts  1.44 us (3%)
    ppermute x4, waiting for transfers between devices, send_same_core(): lax.ppermute(block, GROUP, [(z * count + p, target(z, p, m)) for z in ran...  18 us
    pallas_call x11, Pallas kernels, call(): pl.pallas_call(kernel, out_shape=outs, in_specs=[vmem] * len(args), out_s...  13.2 us
    ppermute x2, starting transfers between devices, send_turned(): lax.ppermute(block, GROUP, [(z * count + p, (p ^ m) * count + z) for z in...  6.67 us
    ppermute x4, starting transfers between devices, send_same_core(): lax.ppermute(block, GROUP, [(z * count + p, target(z, p, m)) for z in ran...  6.27 us
    ppermute x2, waiting for transfers between devices, send_turned(): lax.ppermute(block, GROUP, [(z * count + p, (p ^ m) * count + z) for z in...  4.57 us
    ppermute x1, starting transfers between devices, send_plane(): lax.ppermute(pair, PLANE, [(p, p ^ m) for p in range(count)])  2.43 us
    ppermute x1, starting transfers between devices, body(): lax.ppermute(left_edge, 'seq', [(x, x ^ m) for x in range(chips)])  1.75 us
    unnamed x38, local copies, waits for them, and re-layouts  1.44 us
  transfers between devices with their start and end apart: 10, of which 5 were waited for; matrix products, arithmetic and copies ran while one was open for 0% of the time, Pallas kernels for 10%

profile of v7, /device:TPU:1, one launch (start us, length us, event | category | flops | bytes accessed | tf_op | source)
XLA Modules:
  0.0 56.0 jit_solution(6021306628018527944)
XLA Ops:
  0.0 1.1 %copy-done.8 = bf16[32,32,256]{2,1,0:T(8,128)(2,1)S(1)} copy-done((bf16[32,32,256]{2,1,0:T(8,128)(2,1)S(1)}, bf16[32,32,256]{2,1,0:T(8,128)(2,1)}, u32[]{:S(2)}) %copy-start.8) | copy-done | bytes 524312
  1.1 0.4 norm.1.x_ref
  1.5 0.3 copy-done.11
  1.8 0.0 copy-start.18
  1.8 0.0 copy-start
  1.9 0.0 copy-start.3
  1.9 0.0 copy-start.4
  1.9 1.1 %pack.1.own_ref = bf16[2,32,1152]{2,1,0:T(8,128)(2,1)S(1)} custom-call(f32[1024,256]{1,0:T(8,128)S(1)} %norm.1.x_ref, s32[32,32]{1,0:T(8,128)S(1)} %copy-done.13, s32[1,128]{1,0:T(1,128)S(1)} %bitcast.11, f32[1,256]{1,0:T(1,128)S(1)} %bitcast.19, f32[1,256]{1,0:T(1,128)S(1)} %bitcast.20, bf16[64,256]{1,0:T(8,128)(2,1)S(1)} %bitcast.18, f32[1,64]{1,0:T(1,128)S(1)} %bitcast.21), custom_call_target="tpu_custom_call" | custom-call | flops 1073741824 | bytes 1088256 | tf_op jit(solution)/shard_map/pack/pallas_call | solution.py:303
  3.0 0.1 collective-permute-start
  3.1 1.2 %base.1 = (f32[32,32,128]{2,1,0:T(8,128)S(1)}, bf16[4096,512]{1,0:T(8,128)(2,1)S(1)}) custom-call(bf16[32,32,128]{2,1,0:T(8,128)(2,1)S(1)} %copy-done.9, bf16[66,128]{1,0:T(8,128)(2,1)S(1)} %copy-done.12, s32[1,128]{1,0:T(1,128)S(1)} %bitcast.22, bf16[1024,128]{1,0:T(8,128)(2,1)S(1)} %copy-done.10), custom_call_target="tpu_custom_call" | custom-call | flops 1073741824 | bytes 541696 | tf_op jit(solution)/shard_map/base/pallas_call | solution.py:303
  4.3 0.1 collective-permute-done.other_ref
  4.4 4.8 %collective-permute-start.2 = (bf16[2,32,1152]{2,1,0:T(8,128)(2,1)S(1)}, bf16[2,32,1152]{2,1,0:T(8,128)(2,1)S(1)}, u32[]{:S(2)}, u32[]{:S(2)}) collective-permute-start(bf16[2,32,1152]{2,1,0:T(8,128)(2,1)S(1)} %get-tuple-element.14), channel_id=1, source_target_pairs={{0,4},{1,0},{2,12},{3,8},{4,5},{5,1},{6,13},{7,9},{8,6},{9,2},{10,... | collective-permute-start | bytes 442376 | tf_op jit(solution)/shard_map/ppermute | solution.py:280
  9.2 1.9 %collective-permute-start.1 = (bf16[2,32,1152]{2,1,0:T(8,128)(2,1)S(1)}, bf16[2,32,1152]{2,1,0:T(8,128)(2,1)S(1)}, u32[]{:S(2)}, u32[]{:S(2)}) collective-permute-start(bf16[2,32,1152]{2,1,0:T(8,128)(2,1)S(1)} %get-tuple-element.14), channel_id=1, source_target_pairs={{0,0},{1,4},{2,8},{3,12},{4,1},{5,5},{6,9},{7,13},{8,2},{9,6},{10,... | collective-permute-start | bytes 442376 | tf_op jit(solution)/shard_map/ppermute | solution.py:280
  11.1 2.4 %collective-permute-start.3 = (bf16[2,32,1152]{2,1,0:T(8,128)(2,1)S(1)}, bf16[2,32,1152]{2,1,0:T(8,128)(2,1)S(1)}, u32[]{:S(2)}, u32[]{:S(2)}) collective-permute-start(bf16[2,32,1152]{2,1,0:T(8,128)(2,1)S(1)} %get-tuple-element.15.refs_2_), channel_id=1, source_target_pairs={{0,1},{1,0},{2,3},{3,2},{4,5},{5,4},{6,7},{7,6},{8,9},{9,8},{10,11... | collective-permute-start | bytes 442376 | tf_op jit(solution)/shard_map/ppermute | solution.py:274
  13.6 4.6 %collective-permute-done.1.refs_0_ = bf16[2,32,1152]{2,1,0:T(8,128)(2,1)S(1)} collective-permute-done((bf16[2,32,1152]{2,1,0:T(8,128)(2,1)S(1)}, bf16[2,32,1152]{2,1,0:T(8,128)(2,1)S(1)}, u32[]{:S(2)}, u32[]{:S(2)}) %collective-permute-start.1) | collective-permute-done | bytes 147488 | tf_op jit(solution)/shard_map/ppermute | solution.py:280
  18.1 3.8 %edges.1 = (bf16[32,32,128]{2,1,0:T(8,128)(2,1)S(1)}, bf16[32,32,128]{2,1,0:T(8,128)(2,1)S(1)}, bf16[32,32,128]{2,1,0:T(8,128)(2,1)S(1)}, f32[1024,128]{1,0:T(8,128)S(1)}) custom-call(bf16[2,32,1152]{2,1,0:T(8,128)(2,1)S(1)} %collective-permute-done.1.refs_0_, bf16[2,32,1152]{2,1,0:T(8,128)(2,1)S(1)} %collective-permute-done.2.refs_1_, ...), custom_call_target="tpu_custom_call" | custom-call | bytes 5476352 | tf_op jit(solution)/shard_map/edges/pallas_call | solution.py:303
  21.9 1.8 %collective-permute-start.6 = (bf16[32,32,128]{2,1,0:T(8,128)(2,1)S(1)}, bf16[32,32,128]{2,1,0:T(8,128)(2,1)S(1)}, u32[]{:S(2)}, u32[]{:S(2)}) collective-permute-start(bf16[32,32,128]{2,1,0:T(8,128)(2,1)S(1)} %get-tuple-element.18.refs_0_), channel_id=1, source_target_pairs={{0,1},{1,0},{2,3},{3,2},{4,5},{5,4},{6,7},{7,6},{8,9},{9,8},{10,11... | collective-permute-start | bytes 786440 | tf_op jit(solution)/shard_map/ppermute | solution.py:382
  23.7 0.7 %collective-permute-start.8 = (bf16[32,32,128]{2,1,0:T(8,128)(2,1)S(1)}, bf16[32,32,128]{2,1,0:T(8,128)(2,1)S(1)}, u32[]{:S(2)}, u32[]{:S(2)}) collective-permute-start(bf16[32,32,128]{2,1,0:T(8,128)(2,1)S(1)} %get-tuple-element.17), channel_id=1, source_target_pairs={{0,0},{1,4},{2,2},{3,6},{4,1},{5,5},{6,3},{7,7},{8,8},{9,12},{10,1... | collective-permute-start | bytes 786440 | tf_op jit(solution)/shard_map/ppermute | solution.py:293
  24.3 0.1 collective-permute-start.7
  24.4 5.5 %collective-permute-start.5 = (bf16[32,32,128]{2,1,0:T(8,128)(2,1)S(1)}, bf16[32,32,128]{2,1,0:T(8,128)(2,1)S(1)}, u32[]{:S(2)}, u32[]{:S(2)}) collective-permute-start(bf16[32,32,128]{2,1,0:T(8,128)(2,1)S(1)} %get-tuple-element.17), channel_id=1, source_target_pairs={{0,12},{1,8},{2,14},{3,10},{4,13},{5,9},{6,15},{7,11},{8,4},{9,0},... | collective-permute-start | bytes 786440 | tf_op jit(solution)/shard_map/ppermute | solution.py:293
  30.0 0.6 %collective-permute-done.6.refs_1_ = bf16[32,32,128]{2,1,0:T(8,128)(2,1)S(1)} collective-permute-done((bf16[32,32,128]{2,1,0:T(8,128)(2,1)S(1)}, bf16[32,32,128]{2,1,0:T(8,128)(2,1)S(1)}, u32[]{:S(2)}, u32[]{:S(2)}) %collective-permute-start.6) | collective-permute-done | bytes 262176 | tf_op jit(solution)/shard_map/ppermute | solution.py:382
  30.5 0.1 panel.1.panel_ref
  30.6 1.4 %triangle.2.refs_0_ = f32[2,1024,128]{2,1,0:T(8,128)S(1)} custom-call(bf16[32,32,128]{2,1,0:T(8,128)(2,1)S(1)} %collective-permute-done.8.right_ref, f32[2,1024,128]{2,1,0:T(8,128)S(1)} %panel.1.panel_ref), custom_call_target="tpu_custom_call" | custom-call | bytes 1310720 | tf_op jit(solution)/shard_map/triangle/pallas_call | solution.py:303
  32.0 12.5 %collective-permute-done.7.right_ref = bf16[32,32,128]{2,1,0:T(8,128)(2,1)S(1)} collective-permute-done((bf16[32,32,128]{2,1,0:T(8,128)(2,1)S(1)}, bf16[32,32,128]{2,1,0:T(8,128)(2,1)S(1)}, u32[]{:S(2)}, u32[]{:S(2)}) %collective-permute-start.7) | collective-permute-done | bytes 262176 | tf_op jit(solution)/shard_map/ppermute | solution.py:293
  44.5 1.4 %triangle.3.sums_ref = f32[2,1024,128]{2,1,0:T(8,128)S(1)} custom-call(bf16[32,32,128]{2,1,0:T(8,128)(2,1)S(1)} %collective-permute-done.7.right_ref, f32[2,1024,128]{2,1,0:T(8,128)S(1)} %panel.1.panel_ref, f32[2,1024,128]{2,1,0:T(8,128)S(1)} %triangle.2.refs_0_), custom_call_target="tpu_custom_call", output_to_operand_aliasing={{}: (2, {})} | custom-call | bytes 2359296 | tf_op jit(solution)/shard_map/triangle/pallas_call | solution.py:303
  45.8 5.6 %collective-permute-done.5.second_ref = bf16[32,32,128]{2,1,0:T(8,128)(2,1)S(1)} collective-permute-done((bf16[32,32,128]{2,1,0:T(8,128)(2,1)S(1)}, bf16[32,32,128]{2,1,0:T(8,128)(2,1)S(1)}, u32[]{:S(2)}, u32[]{:S(2)}) %collective-permute-start.5) | collective-permute-done | bytes 262176 | tf_op jit(solution)/shard_map/ppermute | solution.py:293
  51.4 1.3 %others.1 = bf16[1024,128]{1,0:T(8,128)(2,1)S(1)} custom-call(bf16[32,32,128]{2,1,0:T(8,128)(2,1)S(1)} %collective-permute-done.4.first_ref, bf16[32,32,128]{2,1,0:T(8,128)(2,1)S(1)} %collective-permute-done.5.second_ref, f32[2,1024,128]{2,1,0:T(8,128)S(1)} %panel.1.panel_ref, f32[2,1024,128]{2,1,0:T(8,128)S(1)} %triangle.3.sums_ref), custom_call_target="tpu_custom_call" | custom-call | bytes 2621440 | tf_op jit(solution)/shard_map/others/pallas_call | solution.py:303
  52.7 0.0 copy-start.5
  52.8 0.0 copy-start.6
  52.8 0.6 collective-permute-start.9
  53.3 1.4 %own.1.own_ref = f32[1024,128]{1,0:T(8,128)S(1)} custom-call(bf16[32,32,128]{2,1,0:T(8,128)(2,1)S(1)} %collective-permute-done.4.first_ref, bf16[32,32,128]{2,1,0:T(8,128)(2,1)S(1)} %collective-permute-done.5.second_ref, f32[2,1024,128]{2,1,0:T(8,128)S(1)} %panel.1.panel_ref, f32[2,1024,128]{2,1,0:T(8,128)S(1)} %triangle.3.sums_ref), custom_call_target="tpu_custom_call" | custom-call | flops 4294967296 | bytes 2621440 | tf_op jit(solution)/shard_map/own/pallas_call | solution.py:303
  54.8 1.2 %final.1 = bf16[32,32,128]{2,1,0:T(8,128)(2,1)} custom-call(f32[1024,128]{1,0:T(8,128)S(1)} %own.1.own_ref, bf16[1024,128]{1,0:T(8,128)(2,1)S(1)} %collective-permute-done.9.other_ref, bf16[32,32,128]{2,1,0:T(8,128)(2,1)S(1)} %get-tuple-element.19.updated_ref, f32[1024,128]{1,0:T(8,128)S(1)} %get-tuple-element.20.gate_ref, f32[1,128]{1,0:T(1,128)S(1)} %bitcast.15, ...), custom_call_target="tpu_custom_call" | custom-call | bytes 1607168 | tf_op jit(solution)/shard_map/final/pallas_call | solution.py:303
  (38 shorter events, 0.1 us)
Async XLA Ops:
  0.0 1.5 %copy-start.2 = (s32[128]{0:T(128)S(1)}, s32[128]{0:T(128)}, u32[]{:S(2)}) copy-start(s32[128]{0:T(128)} %param.22) | copy-start | bytes 1540
  0.0 1.1 %copy-start.8 = (bf16[32,32,256]{2,1,0:T(8,128)(2,1)S(1)}, bf16[32,32,256]{2,1,0:T(8,128)(2,1)}, u32[]{:S(2)}) copy-start(bf16[32,32,256]{2,1,0:T(8,128)(2,1)} %x_ref.1) | copy-start | bytes 1572868
  1.1 0.8 %copy-start.11 = (bf16[256,64]{0,1:T(8,128)(2,1)S(1)}, bf16[256,64]{0,1:T(8,128)(2,1)}, u32[]{:S(2)}) copy-start(bf16[256,64]{0,1:T(8,128)(2,1)} %param.26) | copy-start | bytes 98308
  1.1 0.8 %copy-start.13 = (s32[32,32]{1,0:T(8,128)S(1)}, s32[32,32]{1,0:T(8,128)}, u32[]{:S(2)}) copy-start(s32[32,32]{1,0:T(8,128)} %mask_ref.1) | copy-start | bytes 12292
  1.1 0.8 %copy-start.14 = (f32[256]{0:T(256)S(1)}, f32[256]{0:T(256)}, u32[]{:S(2)}) copy-start(f32[256]{0:T(256)} %param.24) | copy-start | bytes 3076
  1.1 0.8 %copy-start.15 = (f32[256]{0:T(256)S(1)}, f32[256]{0:T(256)}, u32[]{:S(2)}) copy-start(f32[256]{0:T(256)} %param.25) | copy-start | bytes 3076
  1.1 0.8 %copy-start.16 = (f32[64]{0:T(128)S(1)}, f32[64]{0:T(128)}, u32[]{:S(2)}) copy-start(f32[64]{0:T(128)} %param.27) | copy-start | bytes 772
  1.1 2.0 %copy-start.9 = (bf16[32,32,128]{2,1,0:T(8,128)(2,1)S(1)}, bf16[32,32,128]{2,1,0:T(8,128)(2,1)}, u32[]{:S(2)}) copy-start(bf16[32,32,128]{2,1,0:T(8,128)(2,1)} %pair_ref.1) | copy-start | bytes 786436
  1.1 2.0 %copy-start.10 = (bf16[1024,128]{1,0:T(8,128)(2,1)S(1)}, bf16[1024,128]{1,0:T(8,128)(2,1)}, u32[]{:S(2)}) copy-start(bf16[1024,128]{1,0:T(8,128)(2,1)} %w_ref.2) | copy-start | bytes 786436
  1.1 2.0 %copy-start.12 = (bf16[66,128]{1,0:T(8,128)(2,1)S(1)}, bf16[66,128]{1,0:T(8,128)(2,1)}, u32[]{:S(2)}) copy-start(bf16[66,128]{1,0:T(8,128)(2,1)} %table_ref.1) | copy-start | bytes 50692
  1.1 2.0 %copy-start.17 = (s32[128]{0:T(128)S(1)}, s32[128]{0:T(128)}, u32[]{:S(2)}) copy-start(s32[128]{0:T(128)} %param.23) | copy-start | bytes 1540
  1.8 11.7 %copy-start.18 = (f32[640]{0:T(1024)S(1)}, f32[640]{0:T(1024)}, u32[]{:S(2)}) copy-start(f32[640]{0:T(1024)} %param.33) | copy-start | bytes 7684
  1.8 16.3 %copy-start = (bf16[128,640]{1,0:T(8,128)(2,1)S(1)}, bf16[128,640]{1,0:T(8,128)(2,1)}, u32[]{:S(2)}) copy-start(bf16[128,640]{1,0:T(8,128)(2,1)} %refs_9_.1) | copy-start | bytes 491524
  1.9 16.3 %copy-start.3 = (f32[128]{0:T(128)S(1)}, f32[128]{0:T(128)}, u32[]{:S(2)}) copy-start(f32[128]{0:T(128)} %param.30) | copy-start | bytes 1540
  1.9 16.3 %copy-start.4 = (f32[128]{0:T(128)S(1)}, f32[128]{0:T(128)}, u32[]{:S(2)}) copy-start(f32[128]{0:T(128)} %param.31) | copy-start | bytes 1540
  3.0 1.4 %collective-permute-start = (bf16[2,32,1152]{2,1,0:T(8,128)(2,1)S(1)}, bf16[2,32,1152]{2,1,0:T(8,128)(2,1)S(1)}, u32[]{:S(2)}, u32[]{:S(2)}) collective-permute-start(bf16[2,32,1152]{2,1,0:T(8,128)(2,1)S(1)} %pack.1.own_ref), channel_id=1, source_target_pairs={{0,2},{1,3},{2,0},{3,1},{4,6},{5,7},{6,4},{7,5},{8,10},{9,11},{10,... | collective-permute-start | bytes 442376 | tf_op jit(solution)/shard_map/ppermute | solution.py:269
  4.4 9.1 %collective-permute-start.2 = (bf16[2,32,1152]{2,1,0:T(8,128)(2,1)S(1)}, bf16[2,32,1152]{2,1,0:T(8,128)(2,1)S(1)}, u32[]{:S(2)}, u32[]{:S(2)}) collective-permute-start(bf16[2,32,1152]{2,1,0:T(8,128)(2,1)S(1)} %get-tuple-element.14), channel_id=1, source_target_pairs={{0,4},{1,0},{2,12},{3,8},{4,5},{5,1},{6,13},{7,9},{8,6},{9,2},{10,... | collective-permute-start | bytes 442376 | tf_op jit(solution)/shard_map/ppermute | solution.py:280
  9.2 8.9 %collective-permute-start.1 = (bf16[2,32,1152]{2,1,0:T(8,128)(2,1)S(1)}, bf16[2,32,1152]{2,1,0:T(8,128)(2,1)S(1)}, u32[]{:S(2)}, u32[]{:S(2)}) collective-permute-start(bf16[2,32,1152]{2,1,0:T(8,128)(2,1)S(1)} %get-tuple-element.14), channel_id=1, source_target_pairs={{0,0},{1,4},{2,8},{3,12},{4,1},{5,5},{6,9},{7,13},{8,2},{9,6},{10,... | collective-permute-start | bytes 442376 | tf_op jit(solution)/shard_map/ppermute | solution.py:280
  11.1 7.0 %collective-permute-start.3 = (bf16[2,32,1152]{2,1,0:T(8,128)(2,1)S(1)}, bf16[2,32,1152]{2,1,0:T(8,128)(2,1)S(1)}, u32[]{:S(2)}, u32[]{:S(2)}) collective-permute-start(bf16[2,32,1152]{2,1,0:T(8,128)(2,1)S(1)} %get-tuple-element.15.refs_2_), channel_id=1, source_target_pairs={{0,1},{1,0},{2,3},{3,2},{4,5},{5,4},{6,7},{7,6},{8,9},{9,8},{10,11... | collective-permute-start | bytes 442376 | tf_op jit(solution)/shard_map/ppermute | solution.py:274
  21.9 8.6 %collective-permute-start.6 = (bf16[32,32,128]{2,1,0:T(8,128)(2,1)S(1)}, bf16[32,32,128]{2,1,0:T(8,128)(2,1)S(1)}, u32[]{:S(2)}, u32[]{:S(2)}) collective-permute-start(bf16[32,32,128]{2,1,0:T(8,128)(2,1)S(1)} %get-tuple-element.18.refs_0_), channel_id=1, source_target_pairs={{0,1},{1,0},{2,3},{3,2},{4,5},{5,4},{6,7},{7,6},{8,9},{9,8},{10,11... | collective-permute-start | bytes 786440 | tf_op jit(solution)/shard_map/ppermute | solution.py:382
  23.7 6.9 %collective-permute-start.8 = (bf16[32,32,128]{2,1,0:T(8,128)(2,1)S(1)}, bf16[32,32,128]{2,1,0:T(8,128)(2,1)S(1)}, u32[]{:S(2)}, u32[]{:S(2)}) collective-permute-start(bf16[32,32,128]{2,1,0:T(8,128)(2,1)S(1)} %get-tuple-element.17), channel_id=1, source_target_pairs={{0,0},{1,4},{2,2},{3,6},{4,1},{5,5},{6,3},{7,7},{8,8},{9,12},{10,1... | collective-permute-start | bytes 786440 | tf_op jit(solution)/shard_map/ppermute | solution.py:293
  24.3 20.1 %collective-permute-start.7 = (bf16[32,32,128]{2,1,0:T(8,128)(2,1)S(1)}, bf16[32,32,128]{2,1,0:T(8,128)(2,1)S(1)}, u32[]{:S(2)}, u32[]{:S(2)}) collective-permute-start(bf16[32,32,128]{2,1,0:T(8,128)(2,1)S(1)} %get-tuple-element.17), channel_id=1, source_target_pairs={{0,8},{1,12},{2,10},{3,14},{4,9},{5,13},{6,11},{7,15},{8,0},{9,4},... | collective-permute-start | bytes 786440 | tf_op jit(solution)/shard_map/ppermute | solution.py:293
  24.4 27.0 %collective-permute-start.5 = (bf16[32,32,128]{2,1,0:T(8,128)(2,1)S(1)}, bf16[32,32,128]{2,1,0:T(8,128)(2,1)S(1)}, u32[]{:S(2)}, u32[]{:S(2)}) collective-permute-start(bf16[32,32,128]{2,1,0:T(8,128)(2,1)S(1)} %get-tuple-element.17), channel_id=1, source_target_pairs={{0,12},{1,8},{2,14},{3,10},{4,13},{5,9},{6,15},{7,11},{8,4},{9,0},... | collective-permute-start | bytes 786440 | tf_op jit(solution)/shard_map/ppermute | solution.py:293
  29.9 21.5 %collective-permute-start.4 = (bf16[32,32,128]{2,1,0:T(8,128)(2,1)S(1)}, bf16[32,32,128]{2,1,0:T(8,128)(2,1)S(1)}, u32[]{:S(2)}, u32[]{:S(2)}) collective-permute-start(bf16[32,32,128]{2,1,0:T(8,128)(2,1)S(1)} %get-tuple-element.17), channel_id=1, source_target_pairs={{0,4},{1,0},{2,6},{3,2},{4,5},{5,1},{6,7},{7,3},{8,12},{9,8},{10,1... | collective-permute-start | bytes 786440 | tf_op jit(solution)/shard_map/ppermute | solution.py:293
  52.7 2.0 %copy-start.1 = (bf16[128,128]{1,0:T(8,128)(2,1)S(1)}, bf16[128,128]{1,0:T(8,128)(2,1)}, u32[]{:S(2)}) copy-start(bf16[128,128]{1,0:T(8,128)(2,1)} %w_ref.3) | copy-start | bytes 98308
  52.7 2.0 %copy-start.5 = (f32[128]{0:T(128)S(1)}, f32[128]{0:T(128)}, u32[]{:S(2)}) copy-start(f32[128]{0:T(128)} %param.34) | copy-start | bytes 1540
  52.8 2.0 %copy-start.6 = (f32[128]{0:T(128)S(1)}, f32[128]{0:T(128)}, u32[]{:S(2)}) copy-start(f32[128]{0:T(128)} %param.35) | copy-start | bytes 1540
  52.8 2.0 %copy-start.7 = (f32[128]{0:T(128)S(1)}, f32[128]{0:T(128)}, u32[]{:S(2)}) copy-start(f32[128]{0:T(128)} %param.37) | copy-start | bytes 1540
  52.8 2.0 %collective-permute-start.9 = (bf16[1024,128]{1,0:T(8,128)(2,1)S(1)}, bf16[1024,128]{1,0:T(8,128)(2,1)S(1)}, u32[]{:S(2)}, u32[]{:S(2)}) collective-permute-start(bf16[1024,128]{1,0:T(8,128)(2,1)S(1)} %others.1), channel_id=1, source_target_pairs={{0,2},{1,3},{2,0},{3,1},{4,6},{5,7},{6,4},{7,5},{8,10},{9,11},{10,... | collective-permute-start | bytes 786440 | tf_op jit(solution)/shard_map/ppermute | solution.py:269

commit v8 on v7

--- a/solution.py
+++ b/solution.py
@@ -41,7 +41,7 @@
 
 
 def pack_kernel(x_ref, mask_ref, res_ref, gain_ref, shift_ref, w_ref, bias_ref,
-                out_ref, lscr, rscr):
+                left_ref, right_ref, lscr, rscr):
     seqs, rows = mask_ref.shape
     half = w_ref.shape[0] // 2
     per = LANES // half
@@ -66,21 +66,20 @@
     sub = iota((seqs, LANES), 1) // half
     for tile in range(width // LANES):
         at = slice(tile * LANES, (tile + 1) * LANES)
-        for side, scr, first in ((0, lscr, 0), (1, rscr, LANES)):
+        for ref, scr, first in ((left_ref, lscr, 0), (right_ref, rscr, LANES)):
             value = scr[pl.ds(tile * per, seqs, stride=rows), :]
             for k in range(1, per):
                 value = jnp.where(sub == k, scr[pl.ds(tile * per + k, seqs, stride=rows), :], value)
             value = (value + bias[:, first:first + LANES]) * live_wide[:, at]
-            out_ref[side, :, at] = value.astype(BF16)
+            ref[:, at] = value.astype(BF16)
     live_tile = dot(live, (iota((rows, LANES), 0) == iota((rows, LANES), 1)).astype(BF16))
-    for side in range(2):
-        out_ref[side, :, width:] = live_tile.astype(BF16)
-
-
-def join_kernel(own_ref, other_ref, base_ref, left_ref, right_ref):
-    for n, ref in enumerate((own_ref, other_ref)):
-        left_ref[n] = ref[0]
-        right_ref[n] = ref[1]
+    for ref in (left_ref, right_ref):
+        ref[:, width:] = live_tile.astype(BF16)
+
+
+def join_kernel(count, *refs):
+    for n in range(count):
+        refs[-1][n] = refs[n][...]
 
 
 def pick_columns(values, start, size):
@@ -123,10 +122,10 @@
 
 def edges_kernel(count, *refs):
     pairs = count // 2
-    rights, lefts = refs[:pairs], refs[pairs:2 * pairs]
+    rights, lefts = refs[:pairs], refs[pairs:pairs + 2]
     (base_ref, block_ref, res_ref, gain_ref, shift_ref, w_ref, bias_ref,
-     updated_ref, left_ref, right_ref, gate_ref,
-     lall, rall, tscr, rscr, oscr, nscr, escr) = refs[2 * pairs:]
+     updated_ref, left_ref, right_ref, nscr,
+     lall, rall, tscr, rscr, oscr, escr) = refs[pairs + 2:]
     rows, cols, channels = base_ref.shape
     seqs = lefts[0].shape[1]
     half = block_ref.shape[0] // LANES
@@ -138,7 +137,7 @@
     row_start, col_start = z * rows, q * cols
     for step in range(pairs):
         for n in range(2):
-            lall[q ^ (step + n * pairs)] = lefts[step][n]
+            lall[q ^ (step + n * pairs)] = lefts[n][step]
             rall[z ^ (step + n * pairs)] = rights[step][n]
     right = rall[...].reshape(total_seqs, -1)
     left = lall[...].reshape(total_seqs, -1)
@@ -174,11 +173,11 @@
     live = pick_columns(res_ref[...], col_start, cols) * pick_rows(res_ref[...], row_start, rows)
     chunk = 8
     for i0 in range(0, rows, chunk):
-        mixture = dot(nscr[i0 * cols:(i0 + chunk) * cols, :], w_ref[...]) + bias_ref[...]
-        part = [mixture[:, n * channels:(n + 1) * channels] for n in range(5)]
+        mixture = dot(nscr[i0 * cols:(i0 + chunk) * cols, :], w_ref[:, :4 * channels])
+        mixture = mixture + bias_ref[:, :4 * channels]
+        part = [mixture[:, n * channels:(n + 1) * channels] for n in range(4)]
         left_edge = sigmoid(part[0]) * part[1]
         right_edge = sigmoid(part[2]) * part[3]
-        gate_ref[i0 * cols:(i0 + chunk) * cols, :] = sigmoid(part[4])
         for ii in range(chunk):
             here = live[:, i0 + ii:i0 + ii + 1]
             at = slice(ii * cols, (ii + 1) * cols)
@@ -188,8 +187,13 @@
         right_ref[k] = escr[pl.ds(k, rows, stride=cols), :].astype(BF16)
 
 
+def gate_kernel(normed_ref, w_ref, bias_ref, gate_ref):
+    first = w_ref.shape[1] - gate_ref.shape[1]
+    gate_ref[...] = sigmoid(dot(normed_ref[...], w_ref[:, first:]) + bias_ref[:, first:])
+
+
 def panel_kernel(*refs):
-    *lefts, panel_ref = refs
+    *lefts, _, panel_ref = refs
     x = lax.axis_index("seq")
     for step, left in enumerate(lefts):
         panel_ref[x ^ step] = left[...].astype(F32).reshape(panel_ref.shape[1:])
@@ -203,7 +207,7 @@
 def add_block(panel_ref, chip, rscr, rows, before, store):
     cols = store.shape[0] // rows
     depth, channels = rscr.shape[0] // cols, rscr.shape[1]
-    block = 4
+    block = 8
     tiles = cols // 8
 
     def rows_body(at, carry):
@@ -269,9 +273,9 @@
     return lax.ppermute(block, PLANE, [(p, p ^ (count // 2)) for p in range(count)])
 
 
-def send_plane(pair, count):
-    return [pair] + [
-        lax.ppermute(pair, PLANE, [(p, p ^ m) for p in range(count)]) for m in range(1, count // 2)
+def send_chips(block, chips):
+    return [
+        lax.ppermute(block, "seq", [(x, x ^ m) for x in range(chips)]) for m in range(1, chips)
     ]
 
 
@@ -344,46 +348,52 @@
     shape = jax.ShapeDtypeStruct
     residue = flat(residue_pad_mask)
     chain = flat(residue_chain_index)
-    pack = shape((2, seqs, width + LANES), BF16)
+    pack = shape((seqs, width + LANES), BF16)
+    chips = lax.axis_size("seq")
     normed = call(norm_kernel, shape((seqs * rows, depth), F32), [], [homolog_matrix],
                   flops=1 << 36, name="norm")
-    factors = call(
-        pack_kernel, pack,
+    left, right = call(
+        pack_kernel, [pack, pack],
         [pltpu.VMEM((seqs * rows, LANES), F32)] * 2,
         [normed, sequence_pad_mask, residue, flat(homolog_standard_factor),
          flat(homolog_standard_offset), factor_mapping_matrices.T, flat(outer_side_biases)],
         flops=1 << 30, name="pack")
-    other = swap_cores(factors, count)
+    right_swap = swap_cores(right, count)
+    left_blocks = [left] + send_chips(left, chips)
     base, block = call(
         base_kernel,
         [shape((rows, cols, channels), F32), shape((half * LANES, per * channels), BF16)],
         [pltpu.VMEM((LANES, channels), F32), pltpu.VMEM((half * half, channels), F32)],
         [pair_features, relative_position_table, chain, outer_pair_projection],
         flops=1 << 30, name="base")
-    left, right = call(join_kernel, [pack, pack], [], [factors, other, base], name="join")
-    rights = send_turned(right, count, count // 2)
-    lefts = send_plane(left, count)
-    updated, left_edge, right_edge, gate = call(
+    pair = call(functools.partial(join_kernel, 2), shape((2,) + pack.shape, BF16), [],
+                [right, right_swap, base], name="join")
+    rights = send_turned(pair, count, count // 2)
+    own_lefts = call(functools.partial(join_kernel, chips), shape((chips,) + pack.shape, BF16), [],
+                     left_blocks, name="join")
+    lefts = [own_lefts, swap_cores(own_lefts, count)]
+    updated, left_edge, right_edge, normed_pair = call(
         functools.partial(edges_kernel, count),
         [shape((rows, cols, channels), BF16), shape((rows, cols, channels), BF16),
-         shape((cols, rows, channels), BF16), shape((rows * cols, channels), F32)],
+         shape((cols, rows, channels), BF16), shape((rows * cols, channels), BF16)],
         [pltpu.VMEM((count, seqs, width + LANES), BF16), pltpu.VMEM((count, seqs, width + LANES), BF16),
          pltpu.VMEM((count * seqs // LANES, width, LANES), F32),
          pltpu.VMEM((width, count * seqs), BF16),
          pltpu.VMEM((rows // per * cols, half * LANES), BF16),
-         pltpu.VMEM((rows * cols, channels), BF16), pltpu.VMEM((rows * cols, channels), F32)],
+         pltpu.VMEM((rows * cols, channels), F32)],
         rights + lefts + [base, block, residue, flat(pair_norm_gain), flat(pair_norm_bias),
                           triangle_projection_weights, flat(triangle_projection_biases)],
         name="edges")
-    chips = lax.axis_size("seq")
     steps = [m + n * chips for m in range(chips) for n in range(2)]
     right_edges = send_same_core(right_edge, count, chips, steps)
-    left_edges = [left_edge] + [
-        lax.ppermute(left_edge, "seq", [(x, x ^ m) for x in range(chips)]) for m in range(1, chips)
-    ]
+    left_edges = [left_edge] + send_chips(left_edge, chips)
+    gate = call(gate_kernel, shape((rows * cols, channels), F32), [],
+                [normed_pair, triangle_projection_weights, flat(triangle_projection_biases)],
+                flops=1 << 30, name="gate")
     block_sums = shape((rows * cols, channels), F32)
     turned = pltpu.VMEM((rows * cols, channels), F32)
-    panel = call(panel_kernel, shape((chips, rows * cols, channels), F32), [], left_edges, name="panel")
+    panel = call(panel_kernel, shape((chips, rows * cols, channels), F32), [],
+                 left_edges + [gate], name="panel")
     sums = []
     for n, step in enumerate(steps[:-2]):
         sums = [call(

time: 56.2 us -> 57.6 us (1.025)
  waiting for transfers between devices: 23.3 us -> 26.9 us
  starting transfers between devices: 17.8 us -> 15.9 us
    ppermute x2, waiting for transfers between devices: 4.57 us -> 6.98 us  [send_turned(): lax.ppermute(block, GROUP, [(z * count + p, (p ^ m) * count + z) for z in...]
    ppermute x2, starting transfers between devices: 6.67 us -> 5.46 us  [send_turned(): lax.ppermute(block, GROUP, [(z * count + p, (p ^ m) * count + z) for z in...]
    ppermute x2, starting transfers between devices: 4.18 us -> 3.23 us  [send_chips(): lax.ppermute(block, 'seq', [(x, x ^ m) for x in range(chips)])]
    ppermute x2, waiting for transfers between devices: 0.57 us -> 1.38 us  [send_chips(): lax.ppermute(block, 'seq', [(x, x ^ m) for x in range(chips)])]
    ppermute x2 -> x3, starting transfers between devices: 0.68 us -> 1.3 us  [swap_cores(): lax.ppermute(block, PLANE, [(p, p ^ count // 2) for p in range(count)])]
    pallas_call x11 -> x13, Pallas kernels: 13.2 us -> 12.7 us  [call(): pl.pallas_call(kernel, out_shape=outs, in_specs=[vmem] * len(args), out_s...]
  transfers between devices with their start and end apart: 10 -> 11, of which waited for: 5 -> 5; matrix products, arithmetic and copies ran while one was open for 0% -> 0% of each run, Pallas kernels for 10% -> 9%
where the time goes in v8:
time: 57.6 us; the launch traced here: 57.3 us
  waiting for transfers between devices  26.9 us (47%)
  starting transfers between devices  15.9 us (28%)
  Pallas kernels  12.7 us (22%)
  local copies, waits for them, and re-layouts  1.44 us (2%)
    ppermute x4, waiting for transfers between devices, send_same_core(): lax.ppermute(block, GROUP, [(z * count + p, target(z, p, m)) for z in ran...  18.5 us
    pallas_call x13, Pallas kernels, call(): pl.pallas_call(kernel, out_shape=outs, in_specs=[vmem] * len(args), out_s...  12.7 us
    ppermute x2, waiting for transfers between devices, send_turned(): lax.ppermute(block, GROUP, [(z * count + p, (p ^ m) * count + z) for z in...  6.98 us
    ppermute x4, starting transfers between devices, send_same_core(): lax.ppermute(block, GROUP, [(z * count + p, target(z, p, m)) for z in ran...  5.93 us
    ppermute x2, starting transfers between devices, send_turned(): lax.ppermute(block, GROUP, [(z * count + p, (p ^ m) * count + z) for z in...  5.46 us
    ppermute x2, starting transfers between devices, send_chips(): lax.ppermute(block, 'seq', [(x, x ^ m) for x in range(chips)])  3.23 us
    unnamed x38, local copies, waits for them, and re-layouts  1.44 us
    ppermute x2, waiting for transfers between devices, send_chips(): lax.ppermute(block, 'seq', [(x, x ^ m) for x in range(chips)])  1.38 us
  transfers between devices with their start and end apart: 11, of which 5 were waited for; matrix products, arithmetic and copies ran while one was open for 0% of the time, Pallas kernels for 9%

profile of v8, /device:TPU:1, one launch (start us, length us, event | category | flops | bytes accessed | tf_op | source)
XLA Modules:
  0.0 57.3 jit_solution(12426166424438690192)
XLA Ops:
  0.0 1.1 %copy-done.8 = bf16[32,32,256]{2,1,0:T(8,128)(2,1)S(1)} copy-done((bf16[32,32,256]{2,1,0:T(8,128)(2,1)S(1)}, bf16[32,32,256]{2,1,0:T(8,128)(2,1)}, u32[]{:S(2)}) %copy-start.8) | copy-done | bytes 524312
  1.1 0.4 norm.1.x_ref
  1.5 0.3 copy-done.11
  1.8 0.0 copy-start.18
  1.8 0.0 copy-start
  1.9 1.1 %pack.1 = (bf16[32,1152]{1,0:T(8,128)(2,1)S(1)}, bf16[32,1152]{1,0:T(8,128)(2,1)S(1)}) custom-call(f32[1024,256]{1,0:T(8,128)S(1)} %norm.1.x_ref, s32[32,32]{1,0:T(8,128)S(1)} %copy-done.13, s32[1,128]{1,0:T(1,128)S(1)} %bitcast.11, f32[1,256]{1,0:T(1,128)S(1)} %bitcast.19, f32[1,256]{1,0:T(1,128)S(1)} %bitcast.20, bf16[64,256]{1,0:T(8,128)(2,1)S(1)} %bitcast.18, ...), custom_call_target="tpu_custom_call" | custom-call | flops 1073741824 | bytes 1088256 | tf_op jit(solution)/shard_map/pack/pallas_call | solution.py:307
  3.0 0.1 collective-permute-start
  3.1 2.7 %collective-permute-start.3 = (bf16[32,1152]{1,0:T(8,128)(2,1)S(1)}, bf16[32,1152]{1,0:T(8,128)(2,1)S(1)}, u32[]{:S(2)}, u32[]{:S(2)}) collective-permute-start(bf16[32,1152]{1,0:T(8,128)(2,1)S(1)} %get-tuple-element.15.refs_0_), channel_id=1, source_target_pairs={{0,1},{1,0},{2,3},{3,2},{4,5},{5,4},{6,7},{7,6},{8,9},{9,8},{10,11... | collective-permute-start | bytes 221192 | tf_op jit(solution)/shard_map/ppermute | solution.py:278
  5.8 1.2 %base.1 = (f32[32,32,128]{2,1,0:T(8,128)S(1)}, bf16[4096,512]{1,0:T(8,128)(2,1)S(1)}) custom-call(bf16[32,32,128]{2,1,0:T(8,128)(2,1)S(1)} %copy-done.9, bf16[66,128]{1,0:T(8,128)(2,1)S(1)} %copy-done.12, s32[1,128]{1,0:T(1,128)S(1)} %bitcast.22, bf16[1024,128]{1,0:T(8,128)(2,1)S(1)} %copy-done.10), custom_call_target="tpu_custom_call" | custom-call | flops 1073741824 | bytes 541696 | tf_op jit(solution)/shard_map/base/pallas_call | solution.py:307
  6.9 1.4 %collective-permute-done.3.refs_1_ = bf16[32,1152]{1,0:T(8,128)(2,1)S(1)} collective-permute-done((bf16[32,1152]{1,0:T(8,128)(2,1)S(1)}, bf16[32,1152]{1,0:T(8,128)(2,1)S(1)}, u32[]{:S(2)}, u32[]{:S(2)}) %collective-permute-start.3) | collective-permute-done | bytes 73760 | tf_op jit(solution)/shard_map/ppermute | solution.py:278
  8.3 0.7 %collective-permute-start.4 = (bf16[2,32,1152]{2,1,0:T(8,128)(2,1)S(1)}, bf16[2,32,1152]{2,1,0:T(8,128)(2,1)S(1)}, u32[]{:S(2)}, u32[]{:S(2)}) collective-permute-start(bf16[2,32,1152]{2,1,0:T(8,128)(2,1)S(1)} %join.3.refs_2_), channel_id=1, source_target_pairs={{0,2},{1,3},{2,0},{3,1},{4,6},{5,7},{6,4},{7,5},{8,10},{9,11},{10,... | collective-permute-start | bytes 442376 | tf_op jit(solution)/shard_map/ppermute | solution.py:273
  9.1 3.6 %collective-permute-start.2 = (bf16[2,32,1152]{2,1,0:T(8,128)(2,1)S(1)}, bf16[2,32,1152]{2,1,0:T(8,128)(2,1)S(1)}, u32[]{:S(2)}, u32[]{:S(2)}) collective-permute-start(bf16[2,32,1152]{2,1,0:T(8,128)(2,1)S(1)} %join.2), channel_id=1, source_target_pairs={{0,4},{1,0},{2,12},{3,8},{4,5},{5,1},{6,13},{7,9},{8,6},{9,2},{10,... | collective-permute-start | bytes 442376 | tf_op jit(solution)/shard_map/ppermute | solution.py:284
  12.6 1.9 %collective-permute-start.1 = (bf16[2,32,1152]{2,1,0:T(8,128)(2,1)S(1)}, bf16[2,32,1152]{2,1,0:T(8,128)(2,1)S(1)}, u32[]{:S(2)}, u32[]{:S(2)}) collective-permute-start(bf16[2,32,1152]{2,1,0:T(8,128)(2,1)S(1)} %join.2), channel_id=1, source_target_pairs={{0,0},{1,4},{2,8},{3,12},{4,1},{5,5},{6,9},{7,13},{8,2},{9,6},{10,... | collective-permute-start | bytes 442376 | tf_op jit(solution)/shard_map/ppermute | solution.py:284
  14.6 1.5 %collective-permute-done.2.refs_1_ = bf16[2,32,1152]{2,1,0:T(8,128)(2,1)S(1)} collective-permute-done((bf16[2,32,1152]{2,1,0:T(8,128)(2,1)S(1)}, bf16[2,32,1152]{2,1,0:T(8,128)(2,1)S(1)}, u32[]{:S(2)}, u32[]{:S(2)}) %collective-permute-start.2) | collective-permute-done | bytes 147488 | tf_op jit(solution)/shard_map/ppermute | solution.py:284
  16.1 5.4 %collective-permute-done.1.refs_0_ = bf16[2,32,1152]{2,1,0:T(8,128)(2,1)S(1)} collective-permute-done((bf16[2,32,1152]{2,1,0:T(8,128)(2,1)S(1)}, bf16[2,32,1152]{2,1,0:T(8,128)(2,1)S(1)}, u32[]{:S(2)}, u32[]{:S(2)}) %collective-permute-start.1) | collective-permute-done | bytes 147488 | tf_op jit(solution)/shard_map/ppermute | solution.py:284
  21.6 3.5 %edges.1 = (bf16[32,32,128]{2,1,0:T(8,128)(2,1)S(1)}, bf16[32,32,128]{2,1,0:T(8,128)(2,1)S(1)}, bf16[32,32,128]{2,1,0:T(8,128)(2,1)S(1)}, bf16[1024,128]{1,0:T(8,128)(2,1)S(1)}) custom-call(bf16[2,32,1152]{2,1,0:T(8,128)(2,1)S(1)} %collective-permute-done.1.refs_0_, bf16[2,32,1152]{2,1,0:T(8,128)(2,1)S(1)} %collective-permute-done.2.refs_1_, ...), custom_call_target="tpu_custom_call" | custom-call | bytes 5476352 | tf_op jit(solution)/shard_map/edges/pallas_call | solution.py:307
  25.0 0.6 collective-permute-start.7
  25.6 0.7 %collective-permute-start.9 = (bf16[32,32,128]{2,1,0:T(8,128)(2,1)S(1)}, bf16[32,32,128]{2,1,0:T(8,128)(2,1)S(1)}, u32[]{:S(2)}, u32[]{:S(2)}) collective-permute-start(bf16[32,32,128]{2,1,0:T(8,128)(2,1)S(1)} %get-tuple-element.17), channel_id=1, source_target_pairs={{0,0},{1,4},{2,2},{3,6},{4,1},{5,5},{6,3},{7,7},{8,8},{9,12},{10,1... | collective-permute-start | bytes 786440 | tf_op jit(solution)/shard_map/ppermute | solution.py:297
  26.3 0.5 collective-permute-start.8
  26.7 4.8 %collective-permute-start.6 = (bf16[32,32,128]{2,1,0:T(8,128)(2,1)S(1)}, bf16[32,32,128]{2,1,0:T(8,128)(2,1)S(1)}, u32[]{:S(2)}, u32[]{:S(2)}) collective-permute-start(bf16[32,32,128]{2,1,0:T(8,128)(2,1)S(1)} %get-tuple-element.17), channel_id=1, source_target_pairs={{0,12},{1,8},{2,14},{3,10},{4,13},{5,9},{6,15},{7,11},{8,4},{9,0},... | collective-permute-start | bytes 786440 | tf_op jit(solution)/shard_map/ppermute | solution.py:297
  31.5 0.2 gate.1.refs_2_.gate_ref
  31.8 0.0 collective-permute-done.7.refs_1_
  31.8 0.1 panel.1.panel_ref
  31.9 1.3 %triangle.2.refs_0_ = f32[2,1024,128]{2,1,0:T(8,128)S(1)} custom-call(bf16[32,32,128]{2,1,0:T(8,128)(2,1)S(1)} %collective-permute-done.9.right_ref, f32[2,1024,128]{2,1,0:T(8,128)S(1)} %panel.1.panel_ref), custom_call_target="tpu_custom_call" | custom-call | bytes 1310720 | tf_op jit(solution)/shard_map/triangle/pallas_call | solution.py:307
  33.1 3.1 %collective-permute-done.8.right_ref = bf16[32,32,128]{2,1,0:T(8,128)(2,1)S(1)} collective-permute-done((bf16[32,32,128]{2,1,0:T(8,128)(2,1)S(1)}, bf16[32,32,128]{2,1,0:T(8,128)(2,1)S(1)}, u32[]{:S(2)}, u32[]{:S(2)}) %collective-permute-start.8) | collective-permute-done | bytes 262176 | tf_op jit(solution)/shard_map/ppermute | solution.py:297
  36.3 1.3 %triangle.3.sums_ref = f32[2,1024,128]{2,1,0:T(8,128)S(1)} custom-call(bf16[32,32,128]{2,1,0:T(8,128)(2,1)S(1)} %collective-permute-done.8.right_ref, f32[2,1024,128]{2,1,0:T(8,128)S(1)} %panel.1.panel_ref, f32[2,1024,128]{2,1,0:T(8,128)S(1)} %triangle.2.refs_0_), custom_call_target="tpu_custom_call", output_to_operand_aliasing={{}: (2, {})} | custom-call | bytes 2359296 | tf_op jit(solution)/shard_map/triangle/pallas_call | solution.py:307
  37.5 15.4 %collective-permute-done.6.second_ref = bf16[32,32,128]{2,1,0:T(8,128)(2,1)S(1)} collective-permute-done((bf16[32,32,128]{2,1,0:T(8,128)(2,1)S(1)}, bf16[32,32,128]{2,1,0:T(8,128)(2,1)S(1)}, u32[]{:S(2)}, u32[]{:S(2)}) %collective-permute-start.6) | collective-permute-done | bytes 262176 | tf_op jit(solution)/shard_map/ppermute | solution.py:297
  52.9 1.3 %others.1 = bf16[1024,128]{1,0:T(8,128)(2,1)S(1)} custom-call(bf16[32,32,128]{2,1,0:T(8,128)(2,1)S(1)} %collective-permute-done.5.first_ref, bf16[32,32,128]{2,1,0:T(8,128)(2,1)S(1)} %collective-permute-done.6.second_ref, f32[2,1024,128]{2,1,0:T(8,128)S(1)} %panel.1.panel_ref, f32[2,1024,128]{2,1,0:T(8,128)S(1)} %triangle.3.sums_ref), custom_call_target="tpu_custom_call" | custom-call | bytes 2621440 | tf_op jit(solution)/shard_map/others/pallas_call | solution.py:307
  54.3 0.0 copy-start.5
  54.3 0.5 collective-permute-start.10
  54.7 1.3 %own.1.own_ref = f32[1024,128]{1,0:T(8,128)S(1)} custom-call(bf16[32,32,128]{2,1,0:T(8,128)(2,1)S(1)} %collective-permute-done.5.first_ref, bf16[32,32,128]{2,1,0:T(8,128)(2,1)S(1)} %collective-permute-done.6.second_ref, f32[2,1024,128]{2,1,0:T(8,128)S(1)} %panel.1.panel_ref, f32[2,1024,128]{2,1,0:T(8,128)S(1)} %triangle.3.sums_ref), custom_call_target="tpu_custom_call" | custom-call | flops 4294967296 | bytes 2621440 | tf_op jit(solution)/shard_map/own/pallas_call | solution.py:307
  56.1 1.2 %final.1 = bf16[32,32,128]{2,1,0:T(8,128)(2,1)} custom-call(f32[1024,128]{1,0:T(8,128)S(1)} %own.1.own_ref, bf16[1024,128]{1,0:T(8,128)(2,1)S(1)} %collective-permute-done.10.other_ref, bf16[32,32,128]{2,1,0:T(8,128)(2,1)S(1)} %get-tuple-element.20.updated_ref, f32[1024,128]{1,0:T(8,128)S(1)} %gate.1.refs_2_.gate_ref, f32[1,128]{1,0:T(1,128)S(1)} %bitcast.15, ...), custom_call_target="tpu_custom_call" | custom-call | bytes 1607168 | tf_op jit(solution)/shard_map/final/pallas_call | solution.py:307
  (42 shorter events, 0.1 us)
Async XLA Ops:
  0.0 1.5 %copy-start.2 = (s32[128]{0:T(128)S(1)}, s32[128]{0:T(128)}, u32[]{:S(2)}) copy-start(s32[128]{0:T(128)} %param.22) | copy-start | bytes 1540
  0.0 1.1 %copy-start.8 = (bf16[32,32,256]{2,1,0:T(8,128)(2,1)S(1)}, bf16[32,32,256]{2,1,0:T(8,128)(2,1)}, u32[]{:S(2)}) copy-start(bf16[32,32,256]{2,1,0:T(8,128)(2,1)} %x_ref.1) | copy-start | bytes 1572868
  1.1 0.8 %copy-start.11 = (bf16[256,64]{0,1:T(8,128)(2,1)S(1)}, bf16[256,64]{0,1:T(8,128)(2,1)}, u32[]{:S(2)}) copy-start(bf16[256,64]{0,1:T(8,128)(2,1)} %param.26) | copy-start | bytes 98308
  1.1 0.8 %copy-start.13 = (s32[32,32]{1,0:T(8,128)S(1)}, s32[32,32]{1,0:T(8,128)}, u32[]{:S(2)}) copy-start(s32[32,32]{1,0:T(8,128)} %mask_ref.1) | copy-start | bytes 12292
  1.1 0.8 %copy-start.14 = (f32[256]{0:T(256)S(1)}, f32[256]{0:T(256)}, u32[]{:S(2)}) copy-start(f32[256]{0:T(256)} %param.24) | copy-start | bytes 3076
  1.1 0.8 %copy-start.15 = (f32[256]{0:T(256)S(1)}, f32[256]{0:T(256)}, u32[]{:S(2)}) copy-start(f32[256]{0:T(256)} %param.25) | copy-start | bytes 3076
  1.1 0.8 %copy-start.16 = (f32[64]{0:T(128)S(1)}, f32[64]{0:T(128)}, u32[]{:S(2)}) copy-start(f32[64]{0:T(128)} %param.27) | copy-start | bytes 772
  1.1 4.7 %copy-start.9 = (bf16[32,32,128]{2,1,0:T(8,128)(2,1)S(1)}, bf16[32,32,128]{2,1,0:T(8,128)(2,1)}, u32[]{:S(2)}) copy-start(bf16[32,32,128]{2,1,0:T(8,128)(2,1)} %pair_ref.1) | copy-start | bytes 786436
  1.1 4.7 %copy-start.10 = (bf16[1024,128]{1,0:T(8,128)(2,1)S(1)}, bf16[1024,128]{1,0:T(8,128)(2,1)}, u32[]{:S(2)}) copy-start(bf16[1024,128]{1,0:T(8,128)(2,1)} %w_ref.3) | copy-start | bytes 786436
  1.1 4.7 %copy-start.12 = (bf16[66,128]{1,0:T(8,128)(2,1)S(1)}, bf16[66,128]{1,0:T(8,128)(2,1)}, u32[]{:S(2)}) copy-start(bf16[66,128]{1,0:T(8,128)(2,1)} %table_ref.1) | copy-start | bytes 50692
  1.1 4.7 %copy-start.17 = (s32[128]{0:T(128)S(1)}, s32[128]{0:T(128)}, u32[]{:S(2)}) copy-start(s32[128]{0:T(128)} %param.23) | copy-start | bytes 1540
  1.8 12.7 %copy-start.18 = (f32[640]{0:T(1024)S(1)}, f32[640]{0:T(1024)}, u32[]{:S(2)}) copy-start(f32[640]{0:T(1024)} %param.33) | copy-start | bytes 7684
  1.8 19.7 %copy-start = (bf16[128,640]{1,0:T(8,128)(2,1)S(1)}, bf16[128,640]{1,0:T(8,128)(2,1)}, u32[]{:S(2)}) copy-start(bf16[128,640]{1,0:T(8,128)(2,1)} %w_ref.4) | copy-start | bytes 491524
  1.9 19.7 %copy-start.3 = (f32[128]{0:T(128)S(1)}, f32[128]{0:T(128)}, u32[]{:S(2)}) copy-start(f32[128]{0:T(128)} %param.30) | copy-start | bytes 1540
  1.9 19.7 %copy-start.4 = (f32[128]{0:T(128)S(1)}, f32[128]{0:T(128)}, u32[]{:S(2)}) copy-start(f32[128]{0:T(128)} %param.31) | copy-start | bytes 1540
  3.0 6.1 %collective-permute-start = (bf16[32,1152]{1,0:T(8,128)(2,1)S(1)}, bf16[32,1152]{1,0:T(8,128)(2,1)S(1)}, u32[]{:S(2)}, u32[]{:S(2)}) collective-permute-start(bf16[32,1152]{1,0:T(8,128)(2,1)S(1)} %get-tuple-element.13.refs_0_), channel_id=1, source_target_pairs={{0,2},{1,3},{2,0},{3,1},{4,6},{5,7},{6,4},{7,5},{8,10},{9,11},{10,... | collective-permute-start | bytes 221192 | tf_op jit(solution)/shard_map/ppermute | solution.py:273
  3.1 5.2 %collective-permute-start.3 = (bf16[32,1152]{1,0:T(8,128)(2,1)S(1)}, bf16[32,1152]{1,0:T(8,128)(2,1)S(1)}, u32[]{:S(2)}, u32[]{:S(2)}) collective-permute-start(bf16[32,1152]{1,0:T(8,128)(2,1)S(1)} %get-tuple-element.15.refs_0_), channel_id=1, source_target_pairs={{0,1},{1,0},{2,3},{3,2},{4,5},{5,4},{6,7},{7,6},{8,9},{9,8},{10,11... | collective-permute-start | bytes 221192 | tf_op jit(solution)/shard_map/ppermute | solution.py:278
  8.3 6.2 %collective-permute-start.4 = (bf16[2,32,1152]{2,1,0:T(8,128)(2,1)S(1)}, bf16[2,32,1152]{2,1,0:T(8,128)(2,1)S(1)}, u32[]{:S(2)}, u32[]{:S(2)}) collective-permute-start(bf16[2,32,1152]{2,1,0:T(8,128)(2,1)S(1)} %join.3.refs_2_), channel_id=1, source_target_pairs={{0,2},{1,3},{2,0},{3,1},{4,6},{5,7},{6,4},{7,5},{8,10},{9,11},{10,... | collective-permute-start | bytes 442376 | tf_op jit(solution)/shard_map/ppermute | solution.py:273
  9.1 7.0 %collective-permute-start.2 = (bf16[2,32,1152]{2,1,0:T(8,128)(2,1)S(1)}, bf16[2,32,1152]{2,1,0:T(8,128)(2,1)S(1)}, u32[]{:S(2)}, u32[]{:S(2)}) collective-permute-start(bf16[2,32,1152]{2,1,0:T(8,128)(2,1)S(1)} %join.2), channel_id=1, source_target_pairs={{0,4},{1,0},{2,12},{3,8},{4,5},{5,1},{6,13},{7,9},{8,6},{9,2},{10,... | collective-permute-start | bytes 442376 | tf_op jit(solution)/shard_map/ppermute | solution.py:284
  12.6 8.9 %collective-permute-start.1 = (bf16[2,32,1152]{2,1,0:T(8,128)(2,1)S(1)}, bf16[2,32,1152]{2,1,0:T(8,128)(2,1)S(1)}, u32[]{:S(2)}, u32[]{:S(2)}) collective-permute-start(bf16[2,32,1152]{2,1,0:T(8,128)(2,1)S(1)} %join.2), channel_id=1, source_target_pairs={{0,0},{1,4},{2,8},{3,12},{4,1},{5,5},{6,9},{7,13},{8,2},{9,6},{10,... | collective-permute-start | bytes 442376 | tf_op jit(solution)/shard_map/ppermute | solution.py:284
  25.0 6.7 %collective-permute-start.7 = (bf16[32,32,128]{2,1,0:T(8,128)(2,1)S(1)}, bf16[32,32,128]{2,1,0:T(8,128)(2,1)S(1)}, u32[]{:S(2)}, u32[]{:S(2)}) collective-permute-start(bf16[32,32,128]{2,1,0:T(8,128)(2,1)S(1)} %get-tuple-element.18.refs_0_), channel_id=1, source_target_pairs={{0,1},{1,0},{2,3},{3,2},{4,5},{5,4},{6,7},{7,6},{8,9},{9,8},{10,11... | collective-permute-start | bytes 786440 | tf_op jit(solution)/shard_map/ppermute | solution.py:278
  25.6 6.3 %collective-permute-start.9 = (bf16[32,32,128]{2,1,0:T(8,128)(2,1)S(1)}, bf16[32,32,128]{2,1,0:T(8,128)(2,1)S(1)}, u32[]{:S(2)}, u32[]{:S(2)}) collective-permute-start(bf16[32,32,128]{2,1,0:T(8,128)(2,1)S(1)} %get-tuple-element.17), channel_id=1, source_target_pairs={{0,0},{1,4},{2,2},{3,6},{4,1},{5,5},{6,3},{7,7},{8,8},{9,12},{10,1... | collective-permute-start | bytes 786440 | tf_op jit(solution)/shard_map/ppermute | solution.py:297
  26.3 10.0 %collective-permute-start.8 = (bf16[32,32,128]{2,1,0:T(8,128)(2,1)S(1)}, bf16[32,32,128]{2,1,0:T(8,128)(2,1)S(1)}, u32[]{:S(2)}, u32[]{:S(2)}) collective-permute-start(bf16[32,32,128]{2,1,0:T(8,128)(2,1)S(1)} %get-tuple-element.17), channel_id=1, source_target_pairs={{0,8},{1,12},{2,10},{3,14},{4,9},{5,13},{6,11},{7,15},{8,0},{9,4},... | collective-permute-start | bytes 786440 | tf_op jit(solution)/shard_map/ppermute | solution.py:297
  26.7 26.2 %collective-permute-start.6 = (bf16[32,32,128]{2,1,0:T(8,128)(2,1)S(1)}, bf16[32,32,128]{2,1,0:T(8,128)(2,1)S(1)}, u32[]{:S(2)}, u32[]{:S(2)}) collective-permute-start(bf16[32,32,128]{2,1,0:T(8,128)(2,1)S(1)} %get-tuple-element.17), channel_id=1, source_target_pairs={{0,12},{1,8},{2,14},{3,10},{4,13},{5,9},{6,15},{7,11},{8,4},{9,0},... | collective-permute-start | bytes 786440 | tf_op jit(solution)/shard_map/ppermute | solution.py:297
  31.5 21.4 %collective-permute-start.5 = (bf16[32,32,128]{2,1,0:T(8,128)(2,1)S(1)}, bf16[32,32,128]{2,1,0:T(8,128)(2,1)S(1)}, u32[]{:S(2)}, u32[]{:S(2)}) collective-permute-start(bf16[32,32,128]{2,1,0:T(8,128)(2,1)S(1)} %get-tuple-element.17), channel_id=1, source_target_pairs={{0,4},{1,0},{2,6},{3,2},{4,5},{5,1},{6,7},{7,3},{8,12},{9,8},{10,1... | collective-permute-start | bytes 786440 | tf_op jit(solution)/shard_map/ppermute | solution.py:297
  54.2 1.8 %copy-start.1 = (bf16[128,128]{1,0:T(8,128)(2,1)S(1)}, bf16[128,128]{1,0:T(8,128)(2,1)}, u32[]{:S(2)}) copy-start(bf16[128,128]{1,0:T(8,128)(2,1)} %w_ref.5) | copy-start | bytes 98308
  54.3 1.8 %copy-start.5 = (f32[128]{0:T(128)S(1)}, f32[128]{0:T(128)}, u32[]{:S(2)}) copy-start(f32[128]{0:T(128)} %param.34) | copy-start | bytes 1540
  54.3 1.8 %copy-start.6 = (f32[128]{0:T(128)S(1)}, f32[128]{0:T(128)}, u32[]{:S(2)}) copy-start(f32[128]{0:T(128)} %param.35) | copy-start | bytes 1540
  54.3 1.8 %copy-start.7 = (f32[128]{0:T(128)S(1)}, f32[128]{0:T(128)}, u32[]{:S(2)}) copy-start(f32[128]{0:T(128)} %param.37) | copy-start | bytes 1540
  54.3 1.8 %collective-permute-start.10 = (bf16[1024,128]{1,0:T(8,128)(2,1)S(1)}, bf16[1024,128]{1,0:T(8,128)(2,1)S(1)}, u32[]{:S(2)}, u32[]{:S(2)}) collective-permute-start(bf16[1024,128]{1,0:T(8,128)(2,1)S(1)} %others.1), channel_id=1, source_target_pairs={{0,2},{1,3},{2,0},{3,1},{4,6},{5,7},{6,4},{7,5},{8,10},{9,11},{10,... | collective-permute-start | bytes 786440 | tf_op jit(solution)/shard_map/ppermute | solution.py:273

commit v9 on v8

--- a/solution.py
+++ b/solution.py
@@ -120,42 +120,48 @@
             block_ref[pl.ds(d * LANES + k * half, half), k * channels:(k + 1) * channels] = value
 
 
-def edges_kernel(count, *refs):
+def turn_kernel(count, *refs):
     pairs = count // 2
-    rights, lefts = refs[:pairs], refs[pairs:pairs + 2]
-    (base_ref, block_ref, res_ref, gain_ref, shift_ref, w_ref, bias_ref,
-     updated_ref, left_ref, right_ref, nscr,
-     lall, rall, tscr, rscr, oscr, escr) = refs[pairs + 2:]
-    rows, cols, channels = base_ref.shape
-    seqs = lefts[0].shape[1]
-    half = block_ref.shape[0] // LANES
-    per = LANES // half
-    width = rows * half
-    total_seqs = count * seqs
+    rights, (turned_ref, live_ref, rall, tscr) = refs[:pairs], refs[pairs:]
     z = lax.axis_index("resi")
-    q = lax.axis_index(PLANE)
-    row_start, col_start = z * rows, q * cols
+    width, total_seqs = turned_ref.shape
+    cols = live_ref.shape[0]
+    half = width // cols
     for step in range(pairs):
         for n in range(2):
-            lall[q ^ (step + n * pairs)] = lefts[n][step]
             rall[z ^ (step + n * pairs)] = rights[step][n]
     right = rall[...].reshape(total_seqs, -1)
-    left = lall[...].reshape(total_seqs, -1)
     for at in range(0, width, LANES):
         for s in range(0, total_seqs, LANES):
             tscr[s // LANES, at:at + LANES, :] = right[s:s + LANES, at:at + LANES].astype(F32).T
     for d in range(half):
         for s in range(0, total_seqs, LANES):
             turned = tscr[s // LANES, pl.ds(d, cols, stride=half), :]
-            rscr[d * cols:(d + 1) * cols, s:s + LANES] = turned.astype(BF16)
-    live_cols = right[:, width:].astype(F32).T[0:cols].astype(BF16)
-    counts = dot(live_cols, left[:, width:])
+            turned_ref[d * cols:(d + 1) * cols, s:s + LANES] = turned.astype(BF16)
+    live_ref[...] = right[:, width:].astype(F32).T[0:cols].astype(BF16)
+
+
+def edges_kernel(turned_ref, live_ref, own_ref, swapped_ref, base_ref, block_ref, res_ref,
+                 gain_ref, shift_ref, w_ref, bias_ref,
+                 updated_ref, left_ref, right_ref, nscr, lall, oscr, escr):
+    rows, cols, channels = base_ref.shape
+    chips, seqs = own_ref.shape[:2]
+    half = block_ref.shape[0] // LANES
+    per = LANES // half
+    width = rows * half
+    q = lax.axis_index(PLANE)
+    row_start, col_start = lax.axis_index("resi") * rows, q * cols
+    for step in range(chips):
+        lall[q ^ step] = own_ref[step]
+        lall[q ^ (chips + step)] = swapped_ref[step]
+    left = lall[...].reshape(2 * chips * seqs, -1)
+    counts = dot(live_ref[...], left[:, width:])
     inverse = 1.0 / jnp.maximum(counts, 1.0)
     wide = 2 * LANES
     tall = 8
     for first in range(0, width, wide):
         for d0 in range(0, half, tall):
-            product = dot(rscr[d0 * cols:(d0 + tall) * cols, :], left[:, first:first + wide])
+            product = dot(turned_ref[d0 * cols:(d0 + tall) * cols, :], left[:, first:first + wide])
             product = product.astype(BF16)
             for dd in range(tall):
                 for t in range(wide // LANES):
@@ -199,9 +205,9 @@
         panel_ref[x ^ step] = left[...].astype(F32).reshape(panel_ref.shape[1:])
 
 
-def origin(step, chips):
-    source = lax.axis_index("resi") ^ step
-    return (source // chips) ^ lax.axis_index("resj"), source % chips
+def source_of(z, x, step, chips):
+    block = z ^ step ^ (x % 2 if step >= chips else 0)
+    return block // chips, block % chips
 
 
 def add_block(panel_ref, chip, rscr, rows, before, store):
@@ -233,27 +239,24 @@
 
 def step_kernel(step, chips, fresh, right_ref, panel_ref, *refs):
     out_ref, rscr = refs[-2:]
-    side, chip = origin(step, chips)
+    chip = source_of(lax.axis_index("resi"), lax.axis_index("seq"), step, chips)[1]
     rscr[...] = right_ref[...].astype(F32).reshape(rscr.shape)
-    before = None if fresh else refs[0].at[side]
-    add_block(panel_ref, chip, rscr, right_ref.shape[1], before, out_ref.at[side])
-
-
-def last_kernel(side, steps, chips, first_ref, second_ref, panel_ref, sums_ref, out_ref, rscr):
-    first_side, first_chip = origin(steps[0], chips)
-    second_chip = origin(steps[1], chips)[1]
-    mine = first_side == side
+    add_block(panel_ref, chip, rscr, right_ref.shape[1], None if fresh else refs[0], out_ref)
+
+
+def last_kernel(step, chips, right_ref, panel_ref, far_ref, near_ref, own_ref, other_ref, rscr, acc):
+    step_kernel(step, chips, False, right_ref, panel_ref, far_ref, acc, rscr)
+    mine = lax.axis_index("resi") // chips == lax.axis_index("resj")
 
     @pl.when(mine)
     def _():
-        rscr[...] = first_ref[...].astype(F32).reshape(rscr.shape)
+        own_ref[...] = near_ref[...]
+        other_ref[...] = acc[...].astype(BF16)
 
     @pl.when(jnp.logical_not(mine))
     def _():
-        rscr[...] = second_ref[...].astype(F32).reshape(rscr.shape)
-
-    chip = jnp.where(mine, first_chip, second_chip)
-    add_block(panel_ref, chip, rscr, first_ref.shape[1], sums_ref.at[side], out_ref)
+        own_ref[...] = acc[...]
+        other_ref[...] = near_ref[...].astype(BF16)
 
 
 def final_kernel(own_ref, other_ref, updated_ref, gate_ref, gain_ref, shift_ref, w_ref, bias_ref, out_ref):
@@ -288,17 +291,18 @@
     ]
 
 
-def send_same_core(block, count, chips, steps):
-    def target(z, p, m):
-        core, x = p // chips, p % chips
-        return ((z // chips * chips + x) ^ m) * count + core * chips + z % chips
-
-    return [
-        lax.ppermute(
-            block, GROUP,
-            [(z * count + p, target(z, p, m)) for z in range(count) for p in range(count)])
-        for m in steps
-    ]
+def send_same_core(block, count, chips, step):
+    pairs = []
+    for z in range(count):
+        for p in range(count):
+            core, x = p // chips, p % chips
+            far, chip = source_of(z, x, step, chips)
+            pairs.append(((far * chips + x) * count + core * chips + chip, z * count + p))
+    return lax.ppermute(block, GROUP, pairs)
+
+
+def pass_on(block, count):
+    return lax.ppermute(block, "resi", [(z, z ^ 1) for z in range(count)])
 
 
 def call(kernel, outs, scratch, args, flops=0, aliases=None, name=None):
@@ -372,41 +376,46 @@
     own_lefts = call(functools.partial(join_kernel, chips), shape((chips,) + pack.shape, BF16), [],
                      left_blocks, name="join")
     lefts = [own_lefts, swap_cores(own_lefts, count)]
+    turned, live = call(
+        functools.partial(turn_kernel, count),
+        [shape((width, count * seqs), BF16), shape((cols, count * seqs), BF16)],
+        [pltpu.VMEM((count,) + pack.shape, BF16),
+         pltpu.VMEM((count * seqs // LANES, width, LANES), F32)],
+        rights, flops=1 << 36, name="turn")
     updated, left_edge, right_edge, normed_pair = call(
-        functools.partial(edges_kernel, count),
+        edges_kernel,
         [shape((rows, cols, channels), BF16), shape((rows, cols, channels), BF16),
          shape((cols, rows, channels), BF16), shape((rows * cols, channels), BF16)],
-        [pltpu.VMEM((count, seqs, width + LANES), BF16), pltpu.VMEM((count, seqs, width + LANES), BF16),
-         pltpu.VMEM((count * seqs // LANES, width, LANES), F32),
-         pltpu.VMEM((width, count * seqs), BF16),
+        [pltpu.VMEM((count,) + pack.shape, BF16),
          pltpu.VMEM((rows // per * cols, half * LANES), BF16),
          pltpu.VMEM((rows * cols, channels), F32)],
-        rights + lefts + [base, block, residue, flat(pair_norm_gain), flat(pair_norm_bias),
-                          triangle_projection_weights, flat(triangle_projection_biases)],
+        [turned, live] + lefts + [
+            base, block, residue, flat(pair_norm_gain), flat(pair_norm_bias),
+            triangle_projection_weights, flat(triangle_projection_biases)],
         name="edges")
-    steps = [m + n * chips for m in range(chips) for n in range(2)]
-    right_edges = send_same_core(right_edge, count, chips, steps)
+    right_edges = [send_same_core(right_edge, count, chips, step) for step in range(chips)]
+    for step in range(chips, count, 2):
+        block_far = send_same_core(right_edge, count, chips, step)
+        right_edges += [block_far, pass_on(block_far, count)]
     left_edges = [left_edge] + send_chips(left_edge, chips)
     gate = call(gate_kernel, shape((rows * cols, channels), F32), [],
                 [normed_pair, triangle_projection_weights, flat(triangle_projection_biases)],
                 flops=1 << 30, name="gate")
     block_sums = shape((rows * cols, channels), F32)
-    turned = pltpu.VMEM((rows * cols, channels), F32)
+    scratch = pltpu.VMEM((rows * cols, channels), F32)
     panel = call(panel_kernel, shape((chips, rows * cols, channels), F32), [],
                  left_edges + [gate], name="panel")
-    sums = []
-    for n, step in enumerate(steps[:-2]):
-        sums = [call(
-            functools.partial(step_kernel, step, chips, n < 2), shape((2, rows * cols, channels), F32),
-            [turned], [right_edges[n], panel] + sums, aliases={2: 0} if n else None, name="triangle")]
-    last = right_edges[-2:] + [panel] + sums
-    half_sums = call(
-        functools.partial(last_kernel, 1, steps[-2:], chips), shape((rows * cols, channels), BF16),
-        [turned], last, name="others")
+    near, far = [], []
+    for step in range(count - 1):
+        sums = near if step < chips else far
+        sums[:] = [call(
+            functools.partial(step_kernel, step, chips, not sums), block_sums, [scratch],
+            [right_edges[step], panel] + sums, name="triangle")]
+    own_sums, half_sums = call(
+        functools.partial(last_kernel, count - 1, chips),
+        [block_sums, shape((rows * cols, channels), BF16)], [scratch, scratch],
+        [right_edges[-1], panel] + far + near, name="last")
     other_sums = swap_cores(half_sums, count)
-    own_sums = call(
-        functools.partial(last_kernel, 0, steps[-2:], chips), block_sums, [turned], last,
-        flops=1 << 32, name="own")
     return call(
         final_kernel, shape((rows, cols, channels), BF16), [],
         [own_sums, other_sums, updated, gate, flat(triangle_sum_norm_gain),

time: 57.6 us -> 51.3 us (0.89)
  waiting for transfers between devices: 26.9 us -> 12.4 us
  starting transfers between devices: 15.9 us -> 23.9 us
    ppermute x4, waiting for transfers between devices: 18.5 us -> 6.85 us  [the longest x3 5.61 us: send_same_core(): return lax.ppermute(block, GROUP, pairs)]
    ppermute x2, waiting for transfers between devices: 6.98 us -> 2.59 us  [send_turned(): lax.ppermute(block, GROUP, [(z * count + p, (p ^ m) * count + z) for z in...]
    ppermute x2, starting transfers between devices: 3.23 us -> 6.62 us  [send_chips(): lax.ppermute(block, 'seq', [(x, x ^ m) for x in range(chips)])]
    ppermute x4, starting transfers between devices: 5.93 us -> 8.52 us  [the longest x3 4.58 us: send_same_core(): return lax.ppermute(block, GROUP, pairs)]
    ppermute x2, starting transfers between devices: 5.46 us -> 6.67 us  [send_turned(): lax.ppermute(block, GROUP, [(z * count + p, (p ^ m) * count + z) for z in...]
    ppermute x3, waiting for transfers between devices: 0.01 us -> 1.19 us  [swap_cores(): lax.ppermute(block, PLANE, [(p, p ^ count // 2) for p in range(count)])]
    ppermute x3, starting transfers between devices: 1.3 us -> 2.04 us  [swap_cores(): lax.ppermute(block, PLANE, [(p, p ^ count // 2) for p in range(count)])]
    pallas_call x13 -> x14, Pallas kernels: 12.7 us -> 12.8 us  [call(): pl.pallas_call(kernel, out_shape=outs, in_specs=[vmem] * len(args), out_s...]
  transfers between devices with their start and end apart: 11 -> 11, of which waited for: 5 -> 5; matrix products, arithmetic and copies ran while one was open for 0% -> 0% of each run, Pallas kernels for 9% -> 11%
where the time goes in v9:
time: 51.3 us; the launch traced here: 50.8 us
  starting transfers between devices  23.9 us (47%)
  Pallas kernels  12.8 us (25%)
  waiting for transfers between devices  12.4 us (24%)
  local copies, waits for them, and re-layouts  1.44 us (3%)
    pallas_call x14, Pallas kernels, call(): pl.pallas_call(kernel, out_shape=outs, in_specs=[vmem] * len(args), out_s...  12.8 us
    ppermute x2, starting transfers between devices, send_turned(): lax.ppermute(block, GROUP, [(z * count + p, (p ^ m) * count + z) for z in...  6.67 us
    ppermute x2, starting transfers between devices, send_chips(): lax.ppermute(block, 'seq', [(x, x ^ m) for x in range(chips)])  6.62 us
    ppermute x3, waiting for transfers between devices, send_same_core(): return lax.ppermute(block, GROUP, pairs)  5.61 us
    ppermute x3, starting transfers between devices, send_same_core(): return lax.ppermute(block, GROUP, pairs)  4.58 us
    ppermute x1, starting transfers between devices, pass_on(): return lax.ppermute(block, 'resi', [(z, z ^ 1) for z in range(count)])  3.94 us
    ppermute x2, waiting for transfers between devices, send_turned(): lax.ppermute(block, GROUP, [(z * count + p, (p ^ m) * count + z) for z in...  2.59 us
    ppermute x3, starting transfers between devices, swap_cores(): lax.ppermute(block, PLANE, [(p, p ^ count // 2) for p in range(count)])  2.04 us
  transfers between devices with their start and end apart: 11, of which 5 were waited for; matrix products, arithmetic and copies ran while one was open for 0% of the time, Pallas kernels for 11%

profile of v9, /device:TPU:1, one launch (start us, length us, event | category | flops | bytes accessed | tf_op | source)
XLA Modules:
  0.0 50.8 jit_solution(16851952251939151429)
XLA Ops:
  0.0 1.1 %copy-done.8 = bf16[32,32,256]{2,1,0:T(8,128)(2,1)S(1)} copy-done((bf16[32,32,256]{2,1,0:T(8,128)(2,1)S(1)}, bf16[32,32,256]{2,1,0:T(8,128)(2,1)}, u32[]{:S(2)}) %copy-start.8) | copy-done | bytes 524312
  1.1 0.4 norm.1.x_ref
  1.5 0.3 copy-done.11
  1.8 0.0 copy-start.18
  1.8 1.1 %pack.1 = (bf16[32,1152]{1,0:T(8,128)(2,1)S(1)}, bf16[32,1152]{1,0:T(8,128)(2,1)S(1)}) custom-call(f32[1024,256]{1,0:T(8,128)S(1)} %norm.1.x_ref, s32[32,32]{1,0:T(8,128)S(1)} %copy-done.13, s32[1,128]{1,0:T(1,128)S(1)} %bitcast.11, f32[1,256]{1,0:T(1,128)S(1)} %bitcast.19, f32[1,256]{1,0:T(1,128)S(1)} %bitcast.20, bf16[64,256]{1,0:T(8,128)(2,1)S(1)} %bitcast.18, ...), custom_call_target="tpu_custom_call" | custom-call | flops 1073741824 | bytes 1088256 | tf_op jit(solution)/shard_map/pack/pallas_call | solution.py:311
  2.9 0.1 collective-permute-start
  3.1 1.2 %base.1 = (f32[32,32,128]{2,1,0:T(8,128)S(1)}, bf16[4096,512]{1,0:T(8,128)(2,1)S(1)}) custom-call(bf16[32,32,128]{2,1,0:T(8,128)(2,1)S(1)} %copy-done.9, bf16[66,128]{1,0:T(8,128)(2,1)S(1)} %copy-done.12, s32[1,128]{1,0:T(1,128)S(1)} %bitcast.22, bf16[1024,128]{1,0:T(8,128)(2,1)S(1)} %copy-done.10), custom_call_target="tpu_custom_call" | custom-call | flops 1073741824 | bytes 541696 | tf_op jit(solution)/shard_map/base/pallas_call | solution.py:311
  4.2 0.0 collective-permute-done.refs_1_
  4.3 4.8 %collective-permute-start.2 = (bf16[2,32,1152]{2,1,0:T(8,128)(2,1)S(1)}, bf16[2,32,1152]{2,1,0:T(8,128)(2,1)S(1)}, u32[]{:S(2)}, u32[]{:S(2)}) collective-permute-start(bf16[2,32,1152]{2,1,0:T(8,128)(2,1)S(1)} %join.2), channel_id=1, source_target_pairs={{0,4},{1,0},{2,12},{3,8},{4,5},{5,1},{6,13},{7,9},{8,6},{9,2},{10,... | collective-permute-start | bytes 442376 | tf_op jit(solution)/shard_map/ppermute | solution.py:287
  9.0 1.9 %collective-permute-start.1 = (bf16[2,32,1152]{2,1,0:T(8,128)(2,1)S(1)}, bf16[2,32,1152]{2,1,0:T(8,128)(2,1)S(1)}, u32[]{:S(2)}, u32[]{:S(2)}) collective-permute-start(bf16[2,32,1152]{2,1,0:T(8,128)(2,1)S(1)} %join.2), channel_id=1, source_target_pairs={{0,0},{1,4},{2,8},{3,12},{4,1},{5,5},{6,9},{7,13},{8,2},{9,6},{10,... | collective-permute-start | bytes 442376 | tf_op jit(solution)/shard_map/ppermute | solution.py:287
  11.0 2.5 %collective-permute-start.3 = (bf16[32,1152]{1,0:T(8,128)(2,1)S(1)}, bf16[32,1152]{1,0:T(8,128)(2,1)S(1)}, u32[]{:S(2)}, u32[]{:S(2)}) collective-permute-start(bf16[32,1152]{1,0:T(8,128)(2,1)S(1)} %get-tuple-element.21.refs_0_), channel_id=1, source_target_pairs={{0,1},{1,0},{2,3},{3,2},{4,5},{5,4},{6,7},{7,6},{8,9},{9,8},{10,11... | collective-permute-start | bytes 221192 | tf_op jit(solution)/shard_map/ppermute | solution.py:281
  13.5 1.7 %collective-permute-done.3.refs_1_ = bf16[32,1152]{1,0:T(8,128)(2,1)S(1)} collective-permute-done((bf16[32,1152]{1,0:T(8,128)(2,1)S(1)}, bf16[32,1152]{1,0:T(8,128)(2,1)S(1)}, u32[]{:S(2)}, u32[]{:S(2)}) %collective-permute-start.3) | collective-permute-done | bytes 73760 | tf_op jit(solution)/shard_map/ppermute | solution.py:281
  15.3 0.1 collective-permute-start.4
  15.4 2.6 %collective-permute-done.1.refs_0_ = bf16[2,32,1152]{2,1,0:T(8,128)(2,1)S(1)} collective-permute-done((bf16[2,32,1152]{2,1,0:T(8,128)(2,1)S(1)}, bf16[2,32,1152]{2,1,0:T(8,128)(2,1)S(1)}, u32[]{:S(2)}, u32[]{:S(2)}) %collective-permute-start.1) | collective-permute-done | bytes 147488 | tf_op jit(solution)/shard_map/ppermute | solution.py:287
  18.0 0.5 turn.1
  18.5 3.1 %edges.1 = (bf16[32,32,128]{2,1,0:T(8,128)(2,1)S(1)}, bf16[32,32,128]{2,1,0:T(8,128)(2,1)S(1)}, bf16[32,32,128]{2,1,0:T(8,128)(2,1)S(1)}, bf16[1024,128]{1,0:T(8,128)(2,1)S(1)}) custom-call(bf16[1024,128]{1,0:T(8,128)(2,1)S(1)} %get-tuple-element.19.turned_ref, bf16[32,128]{1,0:T(8,128)(2,1)S(1)} %get-tuple-element.20.live_ref, ...), custom_call_target="tpu_custom_call" | custom-call | bytes 5451776 | tf_op jit(solution)/shard_map/edges/pallas_call | solution.py:311
  21.6 1.4 %collective-permute-start.5 = (bf16[32,32,128]{2,1,0:T(8,128)(2,1)S(1)}, bf16[32,32,128]{2,1,0:T(8,128)(2,1)S(1)}, u32[]{:S(2)}, u32[]{:S(2)}) collective-permute-start(bf16[32,32,128]{2,1,0:T(8,128)(2,1)S(1)} %get-tuple-element.23), channel_id=1, source_target_pairs={{8,0},{13,1},{10,2},{15,3},{9,4},{12,5},{11,6},{14,7},{0,8},{5,9},... | collective-permute-start | bytes 786440 | tf_op jit(solution)/shard_map/ppermute | solution.py:301
  23.0 4.1 %collective-permute-start.7 = (bf16[32,32,128]{2,1,0:T(8,128)(2,1)S(1)}, bf16[32,32,128]{2,1,0:T(8,128)(2,1)S(1)}, u32[]{:S(2)}, u32[]{:S(2)}) collective-permute-start(bf16[32,32,128]{2,1,0:T(8,128)(2,1)S(1)} %get-tuple-element.24.refs_0_), channel_id=1, source_target_pairs={{0,1},{1,0},{2,3},{3,2},{4,5},{5,4},{6,7},{7,6},{8,9},{9,8},{10,11... | collective-permute-start | bytes 786440 | tf_op jit(solution)/shard_map/ppermute | solution.py:281
  27.1 0.7 %collective-permute-start.9 = (bf16[32,32,128]{2,1,0:T(8,128)(2,1)S(1)}, bf16[32,32,128]{2,1,0:T(8,128)(2,1)S(1)}, u32[]{:S(2)}, u32[]{:S(2)}) collective-permute-start(bf16[32,32,128]{2,1,0:T(8,128)(2,1)S(1)} %get-tuple-element.23), channel_id=1, source_target_pairs={{0,0},{4,1},{2,2},{6,3},{1,4},{5,5},{3,6},{7,7},{8,8},{12,9},{10,1... | collective-permute-start | bytes 786440 | tf_op jit(solution)/shard_map/ppermute | solution.py:301
  27.8 2.5 %collective-permute-start.8 = (bf16[32,32,128]{2,1,0:T(8,128)(2,1)S(1)}, bf16[32,32,128]{2,1,0:T(8,128)(2,1)S(1)}, u32[]{:S(2)}, u32[]{:S(2)}) collective-permute-start(bf16[32,32,128]{2,1,0:T(8,128)(2,1)S(1)} %get-tuple-element.23), channel_id=1, source_target_pairs={{1,0},{5,1},{3,2},{7,3},{0,4},{4,5},{2,6},{6,7},{9,8},{13,9},{11,1... | collective-permute-start | bytes 786440 | tf_op jit(solution)/shard_map/ppermute | solution.py:301
  30.2 5.6 %collective-permute-done.5.right_ref = bf16[32,32,128]{2,1,0:T(8,128)(2,1)S(1)} collective-permute-done((bf16[32,32,128]{2,1,0:T(8,128)(2,1)S(1)}, bf16[32,32,128]{2,1,0:T(8,128)(2,1)S(1)}, u32[]{:S(2)}, u32[]{:S(2)}) %collective-permute-start.5) | collective-permute-done | bytes 262176 | tf_op jit(solution)/shard_map/ppermute | solution.py:301
  35.8 3.9 %collective-permute-start.6 = (bf16[32,32,128]{2,1,0:T(8,128)(2,1)S(1)}, bf16[32,32,128]{2,1,0:T(8,128)(2,1)S(1)}, u32[]{:S(2)}, u32[]{:S(2)}) collective-permute-start(bf16[32,32,128]{2,1,0:T(8,128)(2,1)S(1)} %collective-permute-done.5.right_ref), channel_id=1, source_target_pairs={{0,4},{4,0},{8,12},{12,8},{1,5},{5,1},{9,13},{13,9},{2,6},{6,2},{1... | collective-permute-start | bytes 786440 | tf_op jit(solution)/shard_map/ppermute | solution.py:305
  39.8 0.2 gate.1.refs_2_.gate_ref
  40.0 0.1 panel.1.panel_ref
  40.2 1.3 %triangle.3.far_ref = f32[1024,128]{1,0:T(8,128)S(1)} custom-call(bf16[32,32,128]{2,1,0:T(8,128)(2,1)S(1)} %collective-permute-done.5.right_ref, f32[2,1024,128]{2,1,0:T(8,128)S(1)} %panel.1.panel_ref), custom_call_target="tpu_custom_call" | custom-call | bytes 1310720 | tf_op jit(solution)/shard_map/triangle/pallas_call | solution.py:311
  41.4 1.3 %triangle.4.refs_0_ = f32[1024,128]{1,0:T(8,128)S(1)} custom-call(bf16[32,32,128]{2,1,0:T(8,128)(2,1)S(1)} %collective-permute-done.9.right_ref, f32[2,1024,128]{2,1,0:T(8,128)S(1)} %panel.1.panel_ref), custom_call_target="tpu_custom_call" | custom-call | bytes 1310720 | tf_op jit(solution)/shard_map/triangle/pallas_call | solution.py:311
  42.7 1.3 %triangle.5.near_ref = f32[1024,128]{1,0:T(8,128)S(1)} custom-call(bf16[32,32,128]{2,1,0:T(8,128)(2,1)S(1)} %collective-permute-done.8.right_ref, f32[2,1024,128]{2,1,0:T(8,128)S(1)} %panel.1.panel_ref, f32[1024,128]{1,0:T(8,128)S(1)} %triangle.4.refs_0_), custom_call_target="tpu_custom_call" | custom-call | bytes 1835008 | tf_op jit(solution)/shard_map/triangle/pallas_call | solution.py:311
  44.0 1.2 %collective-permute-done.6.right_ref = bf16[32,32,128]{2,1,0:T(8,128)(2,1)S(1)} collective-permute-done((bf16[32,32,128]{2,1,0:T(8,128)(2,1)S(1)}, bf16[32,32,128]{2,1,0:T(8,128)(2,1)S(1)}, u32[]{:S(2)}, u32[]{:S(2)}) %collective-permute-start.6) | collective-permute-done | bytes 262176 | tf_op jit(solution)/shard_map/ppermute | solution.py:305
  45.3 1.3 %last.1 = (f32[1024,128]{1,0:T(8,128)S(1)}, bf16[1024,128]{1,0:T(8,128)(2,1)S(1)}) custom-call(bf16[32,32,128]{2,1,0:T(8,128)(2,1)S(1)} %collective-permute-done.6.right_ref, f32[2,1024,128]{2,1,0:T(8,128)S(1)} %panel.1.panel_ref, f32[1024,128]{1,0:T(8,128)S(1)} %triangle.3.far_ref, f32[1024,128]{1,0:T(8,128)S(1)} %triangle.5.near_ref), custom_call_target="tpu_custom_call" | custom-call | bytes 2359296 | tf_op jit(solution)/shard_map/last/pallas_call | solution.py:311
  46.6 1.8 %collective-permute-start.10 = (bf16[1024,128]{1,0:T(8,128)(2,1)S(1)}, bf16[1024,128]{1,0:T(8,128)(2,1)S(1)}, u32[]{:S(2)}, u32[]{:S(2)}) collective-permute-start(bf16[1024,128]{1,0:T(8,128)(2,1)S(1)} %get-tuple-element.27), channel_id=1, source_target_pairs={{0,2},{1,3},{2,0},{3,1},{4,6},{5,7},{6,4},{7,5},{8,10},{9,11},{10,... | collective-permute-start | bytes 786440 | tf_op jit(solution)/shard_map/ppermute | solution.py:276
  48.4 1.2 %collective-permute-done.10.other_ref = bf16[1024,128]{1,0:T(8,128)(2,1)S(1)} collective-permute-done((bf16[1024,128]{1,0:T(8,128)(2,1)S(1)}, bf16[1024,128]{1,0:T(8,128)(2,1)S(1)}, u32[]{:S(2)}, u32[]{:S(2)}) %collective-permute-start.10) | collective-permute-done | bytes 262176 | tf_op jit(solution)/shard_map/ppermute | solution.py:276
  49.6 1.2 %final.1 = bf16[32,32,128]{2,1,0:T(8,128)(2,1)} custom-call(f32[1024,128]{1,0:T(8,128)S(1)} %get-tuple-element.26.own_ref, bf16[1024,128]{1,0:T(8,128)(2,1)S(1)} %collective-permute-done.10.other_ref, bf16[32,32,128]{2,1,0:T(8,128)(2,1)S(1)} %get-tuple-element.28.updated_ref, f32[1024,128]{1,0:T(8,128)S(1)} %gate.1.refs_2_.gate_ref, f32[1,128]{1,0:T(1,128)S(1)} %bitcast.15, ...), custom_call_target="tpu_custom_call" | custom-call | bytes 1607168 | tf_op jit(solution)/shard_map/final/pallas_call | solution.py:311
  (43 shorter events, 0.1 us)
Async XLA Ops:
  0.0 1.5 %copy-start.2 = (s32[128]{0:T(128)S(1)}, s32[128]{0:T(128)}, u32[]{:S(2)}) copy-start(s32[128]{0:T(128)} %param.22) | copy-start | bytes 1540
  0.0 1.1 %copy-start.8 = (bf16[32,32,256]{2,1,0:T(8,128)(2,1)S(1)}, bf16[32,32,256]{2,1,0:T(8,128)(2,1)}, u32[]{:S(2)}) copy-start(bf16[32,32,256]{2,1,0:T(8,128)(2,1)} %x_ref.1) | copy-start | bytes 1572868
  1.1 0.8 %copy-start.11 = (bf16[256,64]{0,1:T(8,128)(2,1)S(1)}, bf16[256,64]{0,1:T(8,128)(2,1)}, u32[]{:S(2)}) copy-start(bf16[256,64]{0,1:T(8,128)(2,1)} %param.26) | copy-start | bytes 98308
  1.1 0.8 %copy-start.13 = (s32[32,32]{1,0:T(8,128)S(1)}, s32[32,32]{1,0:T(8,128)}, u32[]{:S(2)}) copy-start(s32[32,32]{1,0:T(8,128)} %mask_ref.1) | copy-start | bytes 12292
  1.1 0.8 %copy-start.14 = (f32[256]{0:T(256)S(1)}, f32[256]{0:T(256)}, u32[]{:S(2)}) copy-start(f32[256]{0:T(256)} %param.24) | copy-start | bytes 3076
  1.1 0.8 %copy-start.15 = (f32[256]{0:T(256)S(1)}, f32[256]{0:T(256)}, u32[]{:S(2)}) copy-start(f32[256]{0:T(256)} %param.25) | copy-start | bytes 3076
  1.1 0.8 %copy-start.16 = (f32[64]{0:T(128)S(1)}, f32[64]{0:T(128)}, u32[]{:S(2)}) copy-start(f32[64]{0:T(128)} %param.27) | copy-start | bytes 772
  1.1 2.0 %copy-start.9 = (bf16[32,32,128]{2,1,0:T(8,128)(2,1)S(1)}, bf16[32,32,128]{2,1,0:T(8,128)(2,1)}, u32[]{:S(2)}) copy-start(bf16[32,32,128]{2,1,0:T(8,128)(2,1)} %pair_ref.1) | copy-start | bytes 786436
  1.1 2.0 %copy-start.10 = (bf16[1024,128]{1,0:T(8,128)(2,1)S(1)}, bf16[1024,128]{1,0:T(8,128)(2,1)}, u32[]{:S(2)}) copy-start(bf16[1024,128]{1,0:T(8,128)(2,1)} %w_ref.4) | copy-start | bytes 786436
  1.1 2.0 %copy-start.12 = (bf16[66,128]{1,0:T(8,128)(2,1)S(1)}, bf16[66,128]{1,0:T(8,128)(2,1)}, u32[]{:S(2)}) copy-start(bf16[66,128]{1,0:T(8,128)(2,1)} %table_ref.1) | copy-start | bytes 50692
  1.1 2.0 %copy-start.17 = (s32[128]{0:T(128)S(1)}, s32[128]{0:T(128)}, u32[]{:S(2)}) copy-start(s32[128]{0:T(128)} %param.23) | copy-start | bytes 1540
  1.8 11.7 %copy-start.18 = (f32[640]{0:T(1024)S(1)}, f32[640]{0:T(1024)}, u32[]{:S(2)}) copy-start(f32[640]{0:T(1024)} %param.33) | copy-start | bytes 7684
  2.9 1.3 %collective-permute-start = (bf16[32,1152]{1,0:T(8,128)(2,1)S(1)}, bf16[32,1152]{1,0:T(8,128)(2,1)S(1)}, u32[]{:S(2)}, u32[]{:S(2)}) collective-permute-start(bf16[32,1152]{1,0:T(8,128)(2,1)S(1)} %get-tuple-element.17.refs_0_), channel_id=1, source_target_pairs={{0,2},{1,3},{2,0},{3,1},{4,6},{5,7},{6,4},{7,5},{8,10},{9,11},{10,... | collective-permute-start | bytes 221192 | tf_op jit(solution)/shard_map/ppermute | solution.py:276
  4.3 11.1 %collective-permute-start.2 = (bf16[2,32,1152]{2,1,0:T(8,128)(2,1)S(1)}, bf16[2,32,1152]{2,1,0:T(8,128)(2,1)S(1)}, u32[]{:S(2)}, u32[]{:S(2)}) collective-permute-start(bf16[2,32,1152]{2,1,0:T(8,128)(2,1)S(1)} %join.2), channel_id=1, source_target_pairs={{0,4},{1,0},{2,12},{3,8},{4,5},{5,1},{6,13},{7,9},{8,6},{9,2},{10,... | collective-permute-start | bytes 442376 | tf_op jit(solution)/shard_map/ppermute | solution.py:287
  9.0 8.9 %collective-permute-start.1 = (bf16[2,32,1152]{2,1,0:T(8,128)(2,1)S(1)}, bf16[2,32,1152]{2,1,0:T(8,128)(2,1)S(1)}, u32[]{:S(2)}, u32[]{:S(2)}) collective-permute-start(bf16[2,32,1152]{2,1,0:T(8,128)(2,1)S(1)} %join.2), channel_id=1, source_target_pairs={{0,0},{1,4},{2,8},{3,12},{4,1},{5,5},{6,9},{7,13},{8,2},{9,6},{10,... | collective-permute-start | bytes 442376 | tf_op jit(solution)/shard_map/ppermute | solution.py:287
  11.0 4.3 %collective-permute-start.3 = (bf16[32,1152]{1,0:T(8,128)(2,1)S(1)}, bf16[32,1152]{1,0:T(8,128)(2,1)S(1)}, u32[]{:S(2)}, u32[]{:S(2)}) collective-permute-start(bf16[32,1152]{1,0:T(8,128)(2,1)S(1)} %get-tuple-element.21.refs_0_), channel_id=1, source_target_pairs={{0,1},{1,0},{2,3},{3,2},{4,5},{5,4},{6,7},{7,6},{8,9},{9,8},{10,11... | collective-permute-start | bytes 221192 | tf_op jit(solution)/shard_map/ppermute | solution.py:281
  15.3 3.2 %copy-start = (bf16[128,640]{1,0:T(8,128)(2,1)S(1)}, bf16[128,640]{1,0:T(8,128)(2,1)}, u32[]{:S(2)}) copy-start(bf16[128,640]{1,0:T(8,128)(2,1)} %w_ref.6) | copy-start | bytes 491524
  15.3 3.2 %copy-start.3 = (f32[128]{0:T(128)S(1)}, f32[128]{0:T(128)}, u32[]{:S(2)}) copy-start(f32[128]{0:T(128)} %param.30) | copy-start | bytes 1540
  15.3 3.2 %copy-start.4 = (f32[128]{0:T(128)S(1)}, f32[128]{0:T(128)}, u32[]{:S(2)}) copy-start(f32[128]{0:T(128)} %param.31) | copy-start | bytes 1540
  15.3 3.2 %collective-permute-start.4 = (bf16[2,32,1152]{2,1,0:T(8,128)(2,1)S(1)}, bf16[2,32,1152]{2,1,0:T(8,128)(2,1)S(1)}, u32[]{:S(2)}, u32[]{:S(2)}) collective-permute-start(bf16[2,32,1152]{2,1,0:T(8,128)(2,1)S(1)} %join.3.own_ref), channel_id=1, source_target_pairs={{0,2},{1,3},{2,0},{3,1},{4,6},{5,7},{6,4},{7,5},{8,10},{9,11},{10,... | collective-permute-start | bytes 442376 | tf_op jit(solution)/shard_map/ppermute | solution.py:276
  21.6 14.3 %collective-permute-start.5 = (bf16[32,32,128]{2,1,0:T(8,128)(2,1)S(1)}, bf16[32,32,128]{2,1,0:T(8,128)(2,1)S(1)}, u32[]{:S(2)}, u32[]{:S(2)}) collective-permute-start(bf16[32,32,128]{2,1,0:T(8,128)(2,1)S(1)} %get-tuple-element.23), channel_id=1, source_target_pairs={{8,0},{13,1},{10,2},{15,3},{9,4},{12,5},{11,6},{14,7},{0,8},{5,9},... | collective-permute-start | bytes 786440 | tf_op jit(solution)/shard_map/ppermute | solution.py:301
  23.0 17.0 %collective-permute-start.7 = (bf16[32,32,128]{2,1,0:T(8,128)(2,1)S(1)}, bf16[32,32,128]{2,1,0:T(8,128)(2,1)S(1)}, u32[]{:S(2)}, u32[]{:S(2)}) collective-permute-start(bf16[32,32,128]{2,1,0:T(8,128)(2,1)S(1)} %get-tuple-element.24.refs_0_), channel_id=1, source_target_pairs={{0,1},{1,0},{2,3},{3,2},{4,5},{5,4},{6,7},{7,6},{8,9},{9,8},{10,11... | collective-permute-start | bytes 786440 | tf_op jit(solution)/shard_map/ppermute | solution.py:281
  27.1 14.3 %collective-permute-start.9 = (bf16[32,32,128]{2,1,0:T(8,128)(2,1)S(1)}, bf16[32,32,128]{2,1,0:T(8,128)(2,1)S(1)}, u32[]{:S(2)}, u32[]{:S(2)}) collective-permute-start(bf16[32,32,128]{2,1,0:T(8,128)(2,1)S(1)} %get-tuple-element.23), channel_id=1, source_target_pairs={{0,0},{4,1},{2,2},{6,3},{1,4},{5,5},{3,6},{7,7},{8,8},{12,9},{10,1... | collective-permute-start | bytes 786440 | tf_op jit(solution)/shard_map/ppermute | solution.py:301
  27.8 14.9 %collective-permute-start.8 = (bf16[32,32,128]{2,1,0:T(8,128)(2,1)S(1)}, bf16[32,32,128]{2,1,0:T(8,128)(2,1)S(1)}, u32[]{:S(2)}, u32[]{:S(2)}) collective-permute-start(bf16[32,32,128]{2,1,0:T(8,128)(2,1)S(1)} %get-tuple-element.23), channel_id=1, source_target_pairs={{1,0},{5,1},{3,2},{7,3},{0,4},{4,5},{2,6},{6,7},{9,8},{13,9},{11,1... | collective-permute-start | bytes 786440 | tf_op jit(solution)/shard_map/ppermute | solution.py:301
  35.8 9.4 %collective-permute-start.6 = (bf16[32,32,128]{2,1,0:T(8,128)(2,1)S(1)}, bf16[32,32,128]{2,1,0:T(8,128)(2,1)S(1)}, u32[]{:S(2)}, u32[]{:S(2)}) collective-permute-start(bf16[32,32,128]{2,1,0:T(8,128)(2,1)S(1)} %collective-permute-done.5.right_ref), channel_id=1, source_target_pairs={{0,4},{4,0},{8,12},{12,8},{1,5},{5,1},{9,13},{13,9},{2,6},{6,2},{1... | collective-permute-start | bytes 786440 | tf_op jit(solution)/shard_map/ppermute | solution.py:305
  40.1 9.5 %copy-start.1 = (bf16[128,128]{1,0:T(8,128)(2,1)S(1)}, bf16[128,128]{1,0:T(8,128)(2,1)}, u32[]{:S(2)}) copy-start(bf16[128,128]{1,0:T(8,128)(2,1)} %w_ref.7) | copy-start | bytes 98308
  40.1 9.5 %copy-start.5 = (f32[128]{0:T(128)S(1)}, f32[128]{0:T(128)}, u32[]{:S(2)}) copy-start(f32[128]{0:T(128)} %param.34) | copy-start | bytes 1540
  40.1 9.4 %copy-start.6 = (f32[128]{0:T(128)S(1)}, f32[128]{0:T(128)}, u32[]{:S(2)}) copy-start(f32[128]{0:T(128)} %param.35) | copy-start | bytes 1540
  40.2 9.4 %copy-start.7 = (f32[128]{0:T(128)S(1)}, f32[128]{0:T(128)}, u32[]{:S(2)}) copy-start(f32[128]{0:T(128)} %param.37) | copy-start | bytes 1540
  46.6 3.0 %collective-permute-start.10 = (bf16[1024,128]{1,0:T(8,128)(2,1)S(1)}, bf16[1024,128]{1,0:T(8,128)(2,1)S(1)}, u32[]{:S(2)}, u32[]{:S(2)}) collective-permute-start(bf16[1024,128]{1,0:T(8,128)(2,1)S(1)} %get-tuple-element.27), channel_id=1, source_target_pairs={{0,2},{1,3},{2,0},{3,1},{4,6},{5,7},{6,4},{7,5},{8,10},{9,11},{10,... | collective-permute-start | bytes 786440 | tf_op jit(solution)/shard_map/ppermute | solution.py:276

commit v10 on v9

--- a/solution.py
+++ b/solution.py
@@ -205,8 +205,8 @@
         panel_ref[x ^ step] = left[...].astype(F32).reshape(panel_ref.shape[1:])
 
 
-def source_of(z, x, step, chips):
-    block = z ^ step ^ (x % 2 if step >= chips else 0)
+def source_of(z, core, x, step, chips):
+    block = z ^ step ^ ((x + core) % 2 if step >= chips else 0)
     return block // chips, block % chips
 
 
@@ -239,7 +239,8 @@
 
 def step_kernel(step, chips, fresh, right_ref, panel_ref, *refs):
     out_ref, rscr = refs[-2:]
-    chip = source_of(lax.axis_index("resi"), lax.axis_index("seq"), step, chips)[1]
+    z, core, x = [lax.axis_index(axis) for axis in GROUP]
+    chip = source_of(z, core, x, step, chips)[1]
     rscr[...] = right_ref[...].astype(F32).reshape(rscr.shape)
     add_block(panel_ref, chip, rscr, right_ref.shape[1], None if fresh else refs[0], out_ref)
 
@@ -296,7 +297,7 @@
     for z in range(count):
         for p in range(count):
             core, x = p // chips, p % chips
-            far, chip = source_of(z, x, step, chips)
+            far, chip = source_of(z, core, x, step, chips)
             pairs.append(((far * chips + x) * count + core * chips + chip, z * count + p))
     return lax.ppermute(block, GROUP, pairs)
 
@@ -374,7 +375,7 @@
                 [right, right_swap, base], name="join")
     rights = send_turned(pair, count, count // 2)
     own_lefts = call(functools.partial(join_kernel, chips), shape((chips,) + pack.shape, BF16), [],
-                     left_blocks, name="join")
+                     left_blocks, flops=1 << 36, name="join")
     lefts = [own_lefts, swap_cores(own_lefts, count)]
     turned, live = call(
         functools.partial(turn_kernel, count),

time: 51.3 us -> 49.3 us (0.961)
  starting transfers between devices: 23.9 us -> 15.4 us
  waiting for transfers between devices: 12.4 us -> 18.8 us
    ppermute x2, waiting for transfers between devices: 2.59 us -> 6.87 us  [send_turned(): lax.ppermute(block, GROUP, [(z * count + p, (p ^ m) * count + z) for z in...]
    ppermute x2, starting transfers between devices: 6.62 us -> 2.68 us  [send_chips(): lax.ppermute(block, 'seq', [(x, x ^ m) for x in range(chips)])]
    ppermute x1, starting transfers between devices: 3.94 us -> 0.8 us  [pass_on(): return lax.ppermute(block, 'resi', [(z, z ^ 1) for z in range(count)])]
    ppermute x3, waiting for transfers between devices: 5.61 us -> 8.27 us  [send_same_core(): return lax.ppermute(block, GROUP, pairs)]
    ppermute x2, waiting for transfers between devices: 1.74 us -> 0.01 us  [send_chips(): lax.ppermute(block, 'seq', [(x, x ^ m) for x in range(chips)])]
    ppermute x3, starting transfers between devices: 2.04 us -> 0.76 us  [swap_cores(): lax.ppermute(block, PLANE, [(p, p ^ count // 2) for p in range(count)])]
    ppermute x1, waiting for transfers between devices: 1.24 us -> 2.52 us  [pass_on(): return lax.ppermute(block, 'resi', [(z, z ^ 1) for z in range(count)])]
    ppermute x2, starting transfers between devices: 6.67 us -> 5.51 us  [send_turned(): lax.ppermute(block, GROUP, [(z * count + p, (p ^ m) * count + z) for z in...]
  transfers between devices with their start and end apart: 11 -> 11, of which waited for: 5 -> 6; matrix products, arithmetic and copies ran while one was open for 0% -> 0% of each run, Pallas kernels for 11% -> 12%
where the time goes in v10:
time: 49.3 us; the launch traced here: 48.8 us
  waiting for transfers between devices  18.8 us (38%)
  starting transfers between devices  15.4 us (31%)
  Pallas kernels  12.8 us (26%)
  local copies, waits for them, and re-layouts  1.43 us (3%)
    pallas_call x14, Pallas kernels, call(): pl.pallas_call(kernel, out_shape=outs, in_specs=[vmem] * len(args), out_s...  12.8 us
    ppermute x3, waiting for transfers between devices, send_same_core(): return lax.ppermute(block, GROUP, pairs)  8.27 us
    ppermute x2, waiting for transfers between devices, send_turned(): lax.ppermute(block, GROUP, [(z * count + p, (p ^ m) * count + z) for z in...  6.87 us
    ppermute x3, starting transfers between devices, send_same_core(): return lax.ppermute(block, GROUP, pairs)  5.69 us
    ppermute x2, starting transfers between devices, send_turned(): lax.ppermute(block, GROUP, [(z * count + p, (p ^ m) * count + z) for z in...  5.51 us
    ppermute x2, starting transfers between devices, send_chips(): lax.ppermute(block, 'seq', [(x, x ^ m) for x in range(chips)])  2.68 us
    ppermute x1, waiting for transfers between devices, pass_on(): return lax.ppermute(block, 'resi', [(z, z ^ 1) for z in range(count)])  2.52 us
    unnamed x38, local copies, waits for them, and re-layouts  1.43 us
  transfers between devices with their start and end apart: 11, of which 6 were waited for; matrix products, arithmetic and copies ran while one was open for 0% of the time, Pallas kernels for 12%

profile of v10, /device:TPU:1, one launch (start us, length us, event | category | flops | bytes accessed | tf_op | source)
XLA Modules:
  0.0 48.8 jit_solution(14453577762843474351)
XLA Ops:
  0.0 1.1 %copy-done.8 = bf16[32,32,256]{2,1,0:T(8,128)(2,1)S(1)} copy-done((bf16[32,32,256]{2,1,0:T(8,128)(2,1)S(1)}, bf16[32,32,256]{2,1,0:T(8,128)(2,1)}, u32[]{:S(2)}) %copy-start.8) | copy-done | bytes 524312
  1.1 0.4 norm.1.x_ref
  1.5 0.3 copy-done.11
  1.8 1.1 %pack.1 = (bf16[32,1152]{1,0:T(8,128)(2,1)S(1)}, bf16[32,1152]{1,0:T(8,128)(2,1)S(1)}) custom-call(f32[1024,256]{1,0:T(8,128)S(1)} %norm.1.x_ref, s32[32,32]{1,0:T(8,128)S(1)} %copy-done.13, s32[1,128]{1,0:T(1,128)S(1)} %bitcast.11, f32[1,256]{1,0:T(1,128)S(1)} %bitcast.19, f32[1,256]{1,0:T(1,128)S(1)} %bitcast.20, bf16[64,256]{1,0:T(8,128)(2,1)S(1)} %bitcast.18, ...), custom_call_target="tpu_custom_call" | custom-call | flops 1073741824 | bytes 1088256 | tf_op jit(solution)/shard_map/pack/pallas_call | solution.py:312
  2.9 0.1 collective-permute-start
  3.0 2.7 %collective-permute-start.3 = (bf16[32,1152]{1,0:T(8,128)(2,1)S(1)}, bf16[32,1152]{1,0:T(8,128)(2,1)S(1)}, u32[]{:S(2)}, u32[]{:S(2)}) collective-permute-start(bf16[32,1152]{1,0:T(8,128)(2,1)S(1)} %get-tuple-element.21.refs_0_), channel_id=1, source_target_pairs={{0,1},{1,0},{2,3},{3,2},{4,5},{5,4},{6,7},{7,6},{8,9},{9,8},{10,11... | collective-permute-start | bytes 221192 | tf_op jit(solution)/shard_map/ppermute | solution.py:282
  5.8 1.2 %base.1 = (f32[32,32,128]{2,1,0:T(8,128)S(1)}, bf16[4096,512]{1,0:T(8,128)(2,1)S(1)}) custom-call(bf16[32,32,128]{2,1,0:T(8,128)(2,1)S(1)} %copy-done.9, bf16[66,128]{1,0:T(8,128)(2,1)S(1)} %copy-done.12, s32[1,128]{1,0:T(1,128)S(1)} %bitcast.22, bf16[1024,128]{1,0:T(8,128)(2,1)S(1)} %copy-done.10), custom_call_target="tpu_custom_call" | custom-call | flops 1073741824 | bytes 541696 | tf_op jit(solution)/shard_map/base/pallas_call | solution.py:312
  7.0 3.6 %collective-permute-start.2 = (bf16[2,32,1152]{2,1,0:T(8,128)(2,1)S(1)}, bf16[2,32,1152]{2,1,0:T(8,128)(2,1)S(1)}, u32[]{:S(2)}, u32[]{:S(2)}) collective-permute-start(bf16[2,32,1152]{2,1,0:T(8,128)(2,1)S(1)} %join.2), channel_id=1, source_target_pairs={{0,4},{1,0},{2,12},{3,8},{4,5},{5,1},{6,13},{7,9},{8,6},{9,2},{10,... | collective-permute-start | bytes 442376 | tf_op jit(solution)/shard_map/ppermute | solution.py:288
  10.6 1.9 %collective-permute-start.1 = (bf16[2,32,1152]{2,1,0:T(8,128)(2,1)S(1)}, bf16[2,32,1152]{2,1,0:T(8,128)(2,1)S(1)}, u32[]{:S(2)}, u32[]{:S(2)}) collective-permute-start(bf16[2,32,1152]{2,1,0:T(8,128)(2,1)S(1)} %join.2), channel_id=1, source_target_pairs={{0,0},{1,4},{2,8},{3,12},{4,1},{5,5},{6,9},{7,13},{8,2},{9,6},{10,... | collective-permute-start | bytes 442376 | tf_op jit(solution)/shard_map/ppermute | solution.py:288
  12.5 0.0 copy-start
  12.5 0.0 copy-start.3
  12.5 0.1 collective-permute-start.4
  12.6 2.3 %collective-permute-done.2.refs_1_ = bf16[2,32,1152]{2,1,0:T(8,128)(2,1)S(1)} collective-permute-done((bf16[2,32,1152]{2,1,0:T(8,128)(2,1)S(1)}, bf16[2,32,1152]{2,1,0:T(8,128)(2,1)S(1)}, u32[]{:S(2)}, u32[]{:S(2)}) %collective-permute-start.2) | collective-permute-done | bytes 147488 | tf_op jit(solution)/shard_map/ppermute | solution.py:288
  14.9 4.5 %collective-permute-done.1.refs_0_ = bf16[2,32,1152]{2,1,0:T(8,128)(2,1)S(1)} collective-permute-done((bf16[2,32,1152]{2,1,0:T(8,128)(2,1)S(1)}, bf16[2,32,1152]{2,1,0:T(8,128)(2,1)S(1)}, u32[]{:S(2)}, u32[]{:S(2)}) %collective-permute-start.1) | collective-permute-done | bytes 147488 | tf_op jit(solution)/shard_map/ppermute | solution.py:288
  19.5 0.5 turn.1
  20.0 3.1 %edges.1 = (bf16[32,32,128]{2,1,0:T(8,128)(2,1)S(1)}, bf16[32,32,128]{2,1,0:T(8,128)(2,1)S(1)}, bf16[32,32,128]{2,1,0:T(8,128)(2,1)S(1)}, bf16[1024,128]{1,0:T(8,128)(2,1)S(1)}) custom-call(bf16[1024,128]{1,0:T(8,128)(2,1)S(1)} %get-tuple-element.19.turned_ref, bf16[32,128]{1,0:T(8,128)(2,1)S(1)} %get-tuple-element.20.live_ref, ...), custom_call_target="tpu_custom_call" | custom-call | bytes 5451776 | tf_op jit(solution)/shard_map/edges/pallas_call | solution.py:312
  23.1 1.1 %collective-permute-start.5 = (bf16[32,32,128]{2,1,0:T(8,128)(2,1)S(1)}, bf16[32,32,128]{2,1,0:T(8,128)(2,1)S(1)}, u32[]{:S(2)}, u32[]{:S(2)}) collective-permute-start(bf16[32,32,128]{2,1,0:T(8,128)(2,1)S(1)} %get-tuple-element.23), channel_id=1, source_target_pairs={{8,0},{13,1},{11,2},{14,3},{9,4},{12,5},{10,6},{15,7},{0,8},{5,9},... | collective-permute-start | bytes 786440 | tf_op jit(solution)/shard_map/ppermute | solution.py:302
  24.2 0.7 %collective-permute-start.9 = (bf16[32,32,128]{2,1,0:T(8,128)(2,1)S(1)}, bf16[32,32,128]{2,1,0:T(8,128)(2,1)S(1)}, u32[]{:S(2)}, u32[]{:S(2)}) collective-permute-start(bf16[32,32,128]{2,1,0:T(8,128)(2,1)S(1)} %get-tuple-element.23), channel_id=1, source_target_pairs={{0,0},{4,1},{2,2},{6,3},{1,4},{5,5},{3,6},{7,7},{8,8},{12,9},{10,1... | collective-permute-start | bytes 786440 | tf_op jit(solution)/shard_map/ppermute | solution.py:302
  24.8 3.9 %collective-permute-start.8 = (bf16[32,32,128]{2,1,0:T(8,128)(2,1)S(1)}, bf16[32,32,128]{2,1,0:T(8,128)(2,1)S(1)}, u32[]{:S(2)}, u32[]{:S(2)}) collective-permute-start(bf16[32,32,128]{2,1,0:T(8,128)(2,1)S(1)} %get-tuple-element.23), channel_id=1, source_target_pairs={{1,0},{5,1},{3,2},{7,3},{0,4},{4,5},{2,6},{6,7},{9,8},{13,9},{11,1... | collective-permute-start | bytes 786440 | tf_op jit(solution)/shard_map/ppermute | solution.py:302
  28.8 6.5 %collective-permute-done.5.right_ref = bf16[32,32,128]{2,1,0:T(8,128)(2,1)S(1)} collective-permute-done((bf16[32,32,128]{2,1,0:T(8,128)(2,1)S(1)}, bf16[32,32,128]{2,1,0:T(8,128)(2,1)S(1)}, u32[]{:S(2)}, u32[]{:S(2)}) %collective-permute-start.5) | collective-permute-done | bytes 262176 | tf_op jit(solution)/shard_map/ppermute | solution.py:302
  35.2 0.8 %collective-permute-start.6 = (bf16[32,32,128]{2,1,0:T(8,128)(2,1)S(1)}, bf16[32,32,128]{2,1,0:T(8,128)(2,1)S(1)}, u32[]{:S(2)}, u32[]{:S(2)}) collective-permute-start(bf16[32,32,128]{2,1,0:T(8,128)(2,1)S(1)} %collective-permute-done.5.right_ref), channel_id=1, source_target_pairs={{0,4},{4,0},{8,12},{12,8},{1,5},{5,1},{9,13},{13,9},{2,6},{6,2},{1... | collective-permute-start | bytes 786440 | tf_op jit(solution)/shard_map/ppermute | solution.py:306
  36.0 0.2 gate.1.refs_2_.gate_ref
  36.3 0.1 panel.1.panel_ref
  36.4 1.3 %triangle.3.far_ref = f32[1024,128]{1,0:T(8,128)S(1)} custom-call(bf16[32,32,128]{2,1,0:T(8,128)(2,1)S(1)} %collective-permute-done.5.right_ref, f32[2,1024,128]{2,1,0:T(8,128)S(1)} %panel.1.panel_ref), custom_call_target="tpu_custom_call" | custom-call | bytes 1310720 | tf_op jit(solution)/shard_map/triangle/pallas_call | solution.py:312
  37.7 1.3 %triangle.4.refs_0_ = f32[1024,128]{1,0:T(8,128)S(1)} custom-call(bf16[32,32,128]{2,1,0:T(8,128)(2,1)S(1)} %collective-permute-done.9.right_ref, f32[2,1024,128]{2,1,0:T(8,128)S(1)} %panel.1.panel_ref), custom_call_target="tpu_custom_call" | custom-call | bytes 1310720 | tf_op jit(solution)/shard_map/triangle/pallas_call | solution.py:312
  39.0 1.8 %collective-permute-done.8.right_ref = bf16[32,32,128]{2,1,0:T(8,128)(2,1)S(1)} collective-permute-done((bf16[32,32,128]{2,1,0:T(8,128)(2,1)S(1)}, bf16[32,32,128]{2,1,0:T(8,128)(2,1)S(1)}, u32[]{:S(2)}, u32[]{:S(2)}) %collective-permute-start.8) | collective-permute-done | bytes 262176 | tf_op jit(solution)/shard_map/ppermute | solution.py:302
  40.8 1.3 %triangle.5.near_ref = f32[1024,128]{1,0:T(8,128)S(1)} custom-call(bf16[32,32,128]{2,1,0:T(8,128)(2,1)S(1)} %collective-permute-done.8.right_ref, f32[2,1024,128]{2,1,0:T(8,128)S(1)} %panel.1.panel_ref, f32[1024,128]{1,0:T(8,128)S(1)} %triangle.4.refs_0_), custom_call_target="tpu_custom_call" | custom-call | bytes 1835008 | tf_op jit(solution)/shard_map/triangle/pallas_call | solution.py:312
  42.1 2.5 %collective-permute-done.6.right_ref = bf16[32,32,128]{2,1,0:T(8,128)(2,1)S(1)} collective-permute-done((bf16[32,32,128]{2,1,0:T(8,128)(2,1)S(1)}, bf16[32,32,128]{2,1,0:T(8,128)(2,1)S(1)}, u32[]{:S(2)}, u32[]{:S(2)}) %collective-permute-start.6) | collective-permute-done | bytes 262176 | tf_op jit(solution)/shard_map/ppermute | solution.py:306
  44.6 1.3 %last.1 = (f32[1024,128]{1,0:T(8,128)S(1)}, bf16[1024,128]{1,0:T(8,128)(2,1)S(1)}) custom-call(bf16[32,32,128]{2,1,0:T(8,128)(2,1)S(1)} %collective-permute-done.6.right_ref, f32[2,1024,128]{2,1,0:T(8,128)S(1)} %panel.1.panel_ref, f32[1024,128]{1,0:T(8,128)S(1)} %triangle.3.far_ref, f32[1024,128]{1,0:T(8,128)S(1)} %triangle.5.near_ref), custom_call_target="tpu_custom_call" | custom-call | bytes 2359296 | tf_op jit(solution)/shard_map/last/pallas_call | solution.py:312
  45.9 0.6 %collective-permute-start.10 = (bf16[1024,128]{1,0:T(8,128)(2,1)S(1)}, bf16[1024,128]{1,0:T(8,128)(2,1)S(1)}, u32[]{:S(2)}, u32[]{:S(2)}) collective-permute-start(bf16[1024,128]{1,0:T(8,128)(2,1)S(1)} %get-tuple-element.27), channel_id=1, source_target_pairs={{0,2},{1,3},{2,0},{3,1},{4,6},{5,7},{6,4},{7,5},{8,10},{9,11},{10,... | collective-permute-start | bytes 786440 | tf_op jit(solution)/shard_map/ppermute | solution.py:277
  46.5 1.2 %collective-permute-done.10.other_ref = bf16[1024,128]{1,0:T(8,128)(2,1)S(1)} collective-permute-done((bf16[1024,128]{1,0:T(8,128)(2,1)S(1)}, bf16[1024,128]{1,0:T(8,128)(2,1)S(1)}, u32[]{:S(2)}, u32[]{:S(2)}) %collective-permute-start.10) | collective-permute-done | bytes 262176 | tf_op jit(solution)/shard_map/ppermute | solution.py:277
  47.6 1.2 %final.1 = bf16[32,32,128]{2,1,0:T(8,128)(2,1)} custom-call(f32[1024,128]{1,0:T(8,128)S(1)} %get-tuple-element.26.own_ref, bf16[1024,128]{1,0:T(8,128)(2,1)S(1)} %collective-permute-done.10.other_ref, bf16[32,32,128]{2,1,0:T(8,128)(2,1)S(1)} %get-tuple-element.28.updated_ref, f32[1024,128]{1,0:T(8,128)S(1)} %gate.1.refs_2_.gate_ref, f32[1,128]{1,0:T(1,128)S(1)} %bitcast.15, ...), custom_call_target="tpu_custom_call" | custom-call | bytes 1607168 | tf_op jit(solution)/shard_map/final/pallas_call | solution.py:312
  (43 shorter events, 0.1 us)
Async XLA Ops:
  0.0 1.5 %copy-start.2 = (s32[128]{0:T(128)S(1)}, s32[128]{0:T(128)}, u32[]{:S(2)}) copy-start(s32[128]{0:T(128)} %param.22) | copy-start | bytes 1540
  0.0 1.1 %copy-start.8 = (bf16[32,32,256]{2,1,0:T(8,128)(2,1)S(1)}, bf16[32,32,256]{2,1,0:T(8,128)(2,1)}, u32[]{:S(2)}) copy-start(bf16[32,32,256]{2,1,0:T(8,128)(2,1)} %x_ref.1) | copy-start | bytes 1572868
  1.1 0.8 %copy-start.11 = (bf16[256,64]{0,1:T(8,128)(2,1)S(1)}, bf16[256,64]{0,1:T(8,128)(2,1)}, u32[]{:S(2)}) copy-start(bf16[256,64]{0,1:T(8,128)(2,1)} %param.26) | copy-start | bytes 98308
  1.1 0.8 %copy-start.13 = (s32[32,32]{1,0:T(8,128)S(1)}, s32[32,32]{1,0:T(8,128)}, u32[]{:S(2)}) copy-start(s32[32,32]{1,0:T(8,128)} %mask_ref.1) | copy-start | bytes 12292
  1.1 0.8 %copy-start.14 = (f32[256]{0:T(256)S(1)}, f32[256]{0:T(256)}, u32[]{:S(2)}) copy-start(f32[256]{0:T(256)} %param.24) | copy-start | bytes 3076
  1.1 0.8 %copy-start.15 = (f32[256]{0:T(256)S(1)}, f32[256]{0:T(256)}, u32[]{:S(2)}) copy-start(f32[256]{0:T(256)} %param.25) | copy-start | bytes 3076
  1.1 0.8 %copy-start.16 = (f32[64]{0:T(128)S(1)}, f32[64]{0:T(128)}, u32[]{:S(2)}) copy-start(f32[64]{0:T(128)} %param.27) | copy-start | bytes 772
  1.1 4.6 %copy-start.18 = (f32[640]{0:T(1024)S(1)}, f32[640]{0:T(1024)}, u32[]{:S(2)}) copy-start(f32[640]{0:T(1024)} %param.33) | copy-start | bytes 7684
  1.1 4.6 %copy-start.9 = (bf16[32,32,128]{2,1,0:T(8,128)(2,1)S(1)}, bf16[32,32,128]{2,1,0:T(8,128)(2,1)}, u32[]{:S(2)}) copy-start(bf16[32,32,128]{2,1,0:T(8,128)(2,1)} %pair_ref.1) | copy-start | bytes 786436
  1.1 4.6 %copy-start.10 = (bf16[1024,128]{1,0:T(8,128)(2,1)S(1)}, bf16[1024,128]{1,0:T(8,128)(2,1)}, u32[]{:S(2)}) copy-start(bf16[1024,128]{1,0:T(8,128)(2,1)} %w_ref.4) | copy-start | bytes 786436
  1.1 4.6 %copy-start.12 = (bf16[66,128]{1,0:T(8,128)(2,1)S(1)}, bf16[66,128]{1,0:T(8,128)(2,1)}, u32[]{:S(2)}) copy-start(bf16[66,128]{1,0:T(8,128)(2,1)} %table_ref.1) | copy-start | bytes 50692
  1.1 4.6 %copy-start.17 = (s32[128]{0:T(128)S(1)}, s32[128]{0:T(128)}, u32[]{:S(2)}) copy-start(s32[128]{0:T(128)} %param.23) | copy-start | bytes 1540
  2.9 4.0 %collective-permute-start = (bf16[32,1152]{1,0:T(8,128)(2,1)S(1)}, bf16[32,1152]{1,0:T(8,128)(2,1)S(1)}, u32[]{:S(2)}, u32[]{:S(2)}) collective-permute-start(bf16[32,1152]{1,0:T(8,128)(2,1)S(1)} %get-tuple-element.17.refs_0_), channel_id=1, source_target_pairs={{0,2},{1,3},{2,0},{3,1},{4,6},{5,7},{6,4},{7,5},{8,10},{9,11},{10,... | collective-permute-start | bytes 221192 | tf_op jit(solution)/shard_map/ppermute | solution.py:277
  3.0 9.4 %collective-permute-start.3 = (bf16[32,1152]{1,0:T(8,128)(2,1)S(1)}, bf16[32,1152]{1,0:T(8,128)(2,1)S(1)}, u32[]{:S(2)}, u32[]{:S(2)}) collective-permute-start(bf16[32,1152]{1,0:T(8,128)(2,1)S(1)} %get-tuple-element.21.refs_0_), channel_id=1, source_target_pairs={{0,1},{1,0},{2,3},{3,2},{4,5},{5,4},{6,7},{7,6},{8,9},{9,8},{10,11... | collective-permute-start | bytes 221192 | tf_op jit(solution)/shard_map/ppermute | solution.py:282
  7.0 8.0 %collective-permute-start.2 = (bf16[2,32,1152]{2,1,0:T(8,128)(2,1)S(1)}, bf16[2,32,1152]{2,1,0:T(8,128)(2,1)S(1)}, u32[]{:S(2)}, u32[]{:S(2)}) collective-permute-start(bf16[2,32,1152]{2,1,0:T(8,128)(2,1)S(1)} %join.2), channel_id=1, source_target_pairs={{0,4},{1,0},{2,12},{3,8},{4,5},{5,1},{6,13},{7,9},{8,6},{9,2},{10,... | collective-permute-start | bytes 442376 | tf_op jit(solution)/shard_map/ppermute | solution.py:288
  10.6 8.9 %collective-permute-start.1 = (bf16[2,32,1152]{2,1,0:T(8,128)(2,1)S(1)}, bf16[2,32,1152]{2,1,0:T(8,128)(2,1)S(1)}, u32[]{:S(2)}, u32[]{:S(2)}) collective-permute-start(bf16[2,32,1152]{2,1,0:T(8,128)(2,1)S(1)} %join.2), channel_id=1, source_target_pairs={{0,0},{1,4},{2,8},{3,12},{4,1},{5,5},{6,9},{7,13},{8,2},{9,6},{10,... | collective-permute-start | bytes 442376 | tf_op jit(solution)/shard_map/ppermute | solution.py:288
  12.5 7.5 %copy-start = (bf16[128,640]{1,0:T(8,128)(2,1)S(1)}, bf16[128,640]{1,0:T(8,128)(2,1)}, u32[]{:S(2)}) copy-start(bf16[128,640]{1,0:T(8,128)(2,1)} %w_ref.6) | copy-start | bytes 491524
  12.5 7.5 %copy-start.3 = (f32[128]{0:T(128)S(1)}, f32[128]{0:T(128)}, u32[]{:S(2)}) copy-start(f32[128]{0:T(128)} %param.30) | copy-start | bytes 1540
  12.5 7.5 %copy-start.4 = (f32[128]{0:T(128)S(1)}, f32[128]{0:T(128)}, u32[]{:S(2)}) copy-start(f32[128]{0:T(128)} %param.31) | copy-start | bytes 1540
  12.5 7.4 %collective-permute-start.4 = (bf16[2,32,1152]{2,1,0:T(8,128)(2,1)S(1)}, bf16[2,32,1152]{2,1,0:T(8,128)(2,1)S(1)}, u32[]{:S(2)}, u32[]{:S(2)}) collective-permute-start(bf16[2,32,1152]{2,1,0:T(8,128)(2,1)S(1)} %join.3.own_ref), channel_id=1, source_target_pairs={{0,2},{1,3},{2,0},{3,1},{4,6},{5,7},{6,4},{7,5},{8,10},{9,11},{10,... | collective-permute-start | bytes 442376 | tf_op jit(solution)/shard_map/ppermute | solution.py:277
  23.1 12.2 %collective-permute-start.5 = (bf16[32,32,128]{2,1,0:T(8,128)(2,1)S(1)}, bf16[32,32,128]{2,1,0:T(8,128)(2,1)S(1)}, u32[]{:S(2)}, u32[]{:S(2)}) collective-permute-start(bf16[32,32,128]{2,1,0:T(8,128)(2,1)S(1)} %get-tuple-element.23), channel_id=1, source_target_pairs={{8,0},{13,1},{11,2},{14,3},{9,4},{12,5},{10,6},{15,7},{0,8},{5,9},... | collective-permute-start | bytes 786440 | tf_op jit(solution)/shard_map/ppermute | solution.py:302
  24.2 12.1 %collective-permute-start.7 = (bf16[32,32,128]{2,1,0:T(8,128)(2,1)S(1)}, bf16[32,32,128]{2,1,0:T(8,128)(2,1)S(1)}, u32[]{:S(2)}, u32[]{:S(2)}) collective-permute-start(bf16[32,32,128]{2,1,0:T(8,128)(2,1)S(1)} %get-tuple-element.24.refs_0_), channel_id=1, source_target_pairs={{0,1},{1,0},{2,3},{3,2},{4,5},{5,4},{6,7},{7,6},{8,9},{9,8},{10,11... | collective-permute-start | bytes 786440 | tf_op jit(solution)/shard_map/ppermute | solution.py:282
  24.2 13.5 %collective-permute-start.9 = (bf16[32,32,128]{2,1,0:T(8,128)(2,1)S(1)}, bf16[32,32,128]{2,1,0:T(8,128)(2,1)S(1)}, u32[]{:S(2)}, u32[]{:S(2)}) collective-permute-start(bf16[32,32,128]{2,1,0:T(8,128)(2,1)S(1)} %get-tuple-element.23), channel_id=1, source_target_pairs={{0,0},{4,1},{2,2},{6,3},{1,4},{5,5},{3,6},{7,7},{8,8},{12,9},{10,1... | collective-permute-start | bytes 786440 | tf_op jit(solution)/shard_map/ppermute | solution.py:302
  24.8 15.9 %collective-permute-start.8 = (bf16[32,32,128]{2,1,0:T(8,128)(2,1)S(1)}, bf16[32,32,128]{2,1,0:T(8,128)(2,1)S(1)}, u32[]{:S(2)}, u32[]{:S(2)}) collective-permute-start(bf16[32,32,128]{2,1,0:T(8,128)(2,1)S(1)} %get-tuple-element.23), channel_id=1, source_target_pairs={{1,0},{5,1},{3,2},{7,3},{0,4},{4,5},{2,6},{6,7},{9,8},{13,9},{11,1... | collective-permute-start | bytes 786440 | tf_op jit(solution)/shard_map/ppermute | solution.py:302
  35.2 9.3 %collective-permute-start.6 = (bf16[32,32,128]{2,1,0:T(8,128)(2,1)S(1)}, bf16[32,32,128]{2,1,0:T(8,128)(2,1)S(1)}, u32[]{:S(2)}, u32[]{:S(2)}) collective-permute-start(bf16[32,32,128]{2,1,0:T(8,128)(2,1)S(1)} %collective-permute-done.5.right_ref), channel_id=1, source_target_pairs={{0,4},{4,0},{8,12},{12,8},{1,5},{5,1},{9,13},{13,9},{2,6},{6,2},{1... | collective-permute-start | bytes 786440 | tf_op jit(solution)/shard_map/ppermute | solution.py:306
  36.4 11.3 %copy-start.1 = (bf16[128,128]{1,0:T(8,128)(2,1)S(1)}, bf16[128,128]{1,0:T(8,128)(2,1)}, u32[]{:S(2)}) copy-start(bf16[128,128]{1,0:T(8,128)(2,1)} %w_ref.7) | copy-start | bytes 98308
  36.4 11.3 %copy-start.5 = (f32[128]{0:T(128)S(1)}, f32[128]{0:T(128)}, u32[]{:S(2)}) copy-start(f32[128]{0:T(128)} %param.34) | copy-start | bytes 1540
  36.4 11.2 %copy-start.6 = (f32[128]{0:T(128)S(1)}, f32[128]{0:T(128)}, u32[]{:S(2)}) copy-start(f32[128]{0:T(128)} %param.35) | copy-start | bytes 1540
  36.4 11.2 %copy-start.7 = (f32[128]{0:T(128)S(1)}, f32[128]{0:T(128)}, u32[]{:S(2)}) copy-start(f32[128]{0:T(128)} %param.37) | copy-start | bytes 1540
  45.9 1.7 %collective-permute-start.10 = (bf16[1024,128]{1,0:T(8,128)(2,1)S(1)}, bf16[1024,128]{1,0:T(8,128)(2,1)S(1)}, u32[]{:S(2)}, u32[]{:S(2)}) collective-permute-start(bf16[1024,128]{1,0:T(8,128)(2,1)S(1)} %get-tuple-element.27), channel_id=1, source_target_pairs={{0,2},{1,3},{2,0},{3,1},{4,6},{5,7},{6,4},{7,5},{8,10},{9,11},{10,... | collective-permute-start | bytes 786440 | tf_op jit(solution)/shard_map/ppermute | solution.py:277

commit v11 on v10

--- a/solution.py
+++ b/solution.py
@@ -95,7 +95,7 @@
     return dot(jnp.broadcast_to(values.astype(F32), (8, total)).astype(BF16), pick)[0:1]
 
 
-def base_kernel(pair_ref, table_ref, chain_ref, w_ref, base_ref, block_ref, tscr, wscr):
+def base_kernel(pair_ref, table_ref, chain_ref, w_ref, _, base_ref, block_ref, tscr, wscr):
     rows, cols, channels = pair_ref.shape
     row_start = lax.axis_index("resi") * rows
     col_start = lax.axis_index(PLANE) * cols
@@ -123,13 +123,13 @@
 def turn_kernel(count, *refs):
     pairs = count // 2
     rights, (turned_ref, live_ref, rall, tscr) = refs[:pairs], refs[pairs:]
-    z = lax.axis_index("resi")
+    z, shift = lax.axis_index("resi"), lax.axis_index("resj")
     width, total_seqs = turned_ref.shape
     cols = live_ref.shape[0]
     half = width // cols
     for step in range(pairs):
         for n in range(2):
-            rall[z ^ (step + n * pairs)] = rights[step][n]
+            rall[z ^ shift ^ (step + n * pairs)] = rights[step][n]
     right = rall[...].reshape(total_seqs, -1)
     for at in range(0, width, LANES):
         for s in range(0, total_seqs, LANES):
@@ -206,7 +206,7 @@
 
 
 def source_of(z, core, x, step, chips):
-    block = z ^ step ^ ((x + core) % 2 if step >= chips else 0)
+    block = z ^ step ^ ((x + core) % 2 if step >= chips else core % 2)
     return block // chips, block % chips
 
 
@@ -283,11 +283,12 @@
     ]
 
 
-def send_turned(block, count, steps):
+def send_turned(block, count, chips, steps):
     return [
         lax.ppermute(
             block, GROUP,
-            [(z * count + p, (p ^ m) * count + z) for z in range(count) for p in range(count)])
+            [(z * count + p, (p ^ m ^ (z // chips)) * count + z)
+             for z in range(count) for p in range(count)])
         for m in range(steps)
     ]
 
@@ -365,15 +366,15 @@
         flops=1 << 30, name="pack")
     right_swap = swap_cores(right, count)
     left_blocks = [left] + send_chips(left, chips)
+    pair = call(functools.partial(join_kernel, 2), shape((2,) + pack.shape, BF16), [],
+                [right, right_swap], name="join")
     base, block = call(
         base_kernel,
         [shape((rows, cols, channels), F32), shape((half * LANES, per * channels), BF16)],
         [pltpu.VMEM((LANES, channels), F32), pltpu.VMEM((half * half, channels), F32)],
-        [pair_features, relative_position_table, chain, outer_pair_projection],
+        [pair_features, relative_position_table, chain, outer_pair_projection, pair],
         flops=1 << 30, name="base")
-    pair = call(functools.partial(join_kernel, 2), shape((2,) + pack.shape, BF16), [],
-                [right, right_swap, base], name="join")
-    rights = send_turned(pair, count, count // 2)
+    rights = send_turned(pair, count, chips, count // 2)
     own_lefts = call(functools.partial(join_kernel, chips), shape((chips,) + pack.shape, BF16), [],
                      left_blocks, flops=1 << 36, name="join")
     lefts = [own_lefts, swap_cores(own_lefts, count)]

time: 49.3 us -> 50.7 us (1.028)
  waiting for transfers between devices: 18.8 us -> 21.4 us
  starting transfers between devices: 15.4 us -> 14 us
    ppermute x3, waiting for transfers between devices: 8.27 us -> 11.5 us  [send_same_core(): return lax.ppermute(block, GROUP, pairs)]
    ppermute x3, starting transfers between devices: 5.69 us -> 2.66 us  [send_same_core(): return lax.ppermute(block, GROUP, pairs)]
    ppermute x2, starting transfers between devices: 5.51 us -> 7.51 us  [send_turned(): lax.ppermute(block, GROUP, [(z * count + p, (p ^ m ^ z // chips) * count...]
    ppermute x1, starting transfers between devices: 0.8 us -> 0.01 us  [pass_on(): return lax.ppermute(block, 'resi', [(z, z ^ 1) for z in range(count)])]
  transfers between devices with their start and end apart: 11 -> 11, of which waited for: 6 -> 5; matrix products, arithmetic and copies ran while one was open for 0% -> 0% of each run, Pallas kernels for 12% -> 12%
where the time goes in v11:
time: 50.7 us; the launch traced here: 50 us
  waiting for transfers between devices  21.4 us (42%)
  starting transfers between devices  14 us (28%)
  Pallas kernels  12.8 us (25%)
  local copies, waits for them, and re-layouts  1.48 us (3%)
    pallas_call x14, Pallas kernels, call(): pl.pallas_call(kernel, out_shape=outs, in_specs=[vmem] * len(args), out_s...  12.8 us
    ppermute x3, waiting for transfers between devices, send_same_core(): return lax.ppermute(block, GROUP, pairs)  11.5 us
    ppermute x2, starting transfers between devices, send_turned(): lax.ppermute(block, GROUP, [(z * count + p, (p ^ m ^ z // chips) * count...  7.51 us
    ppermute x2, waiting for transfers between devices, send_turned(): lax.ppermute(block, GROUP, [(z * count + p, (p ^ m ^ z // chips) * count...  6.44 us
    ppermute x2, starting transfers between devices, send_chips(): lax.ppermute(block, 'seq', [(x, x ^ m) for x in range(chips)])  2.74 us
    ppermute x3, starting transfers between devices, send_same_core(): return lax.ppermute(block, GROUP, pairs)  2.66 us
    ppermute x1, waiting for transfers between devices, pass_on(): return lax.ppermute(block, 'resi', [(z, z ^ 1) for z in range(count)])  2.21 us
    unnamed x38, local copies, waits for them, and re-layouts  1.48 us
  transfers between devices with their start and end apart: 11, of which 5 were waited for; matrix products, arithmetic and copies ran while one was open for 0% of the time, Pallas kernels for 12%

profile of v11, /device:TPU:1, one launch (start us, length us, event | category | flops | bytes accessed | tf_op | source)
XLA Modules:
  0.0 50.0 jit_solution(2816236135653314025)
XLA Ops:
  0.0 1.1 %copy-done.8 = bf16[32,32,256]{2,1,0:T(8,128)(2,1)S(1)} copy-done((bf16[32,32,256]{2,1,0:T(8,128)(2,1)S(1)}, bf16[32,32,256]{2,1,0:T(8,128)(2,1)}, u32[]{:S(2)}) %copy-start.8) | copy-done | bytes 524312
  1.1 0.4 norm.1.x_ref
  1.5 0.3 copy-done.11
  1.8 1.1 %pack.1 = (bf16[32,1152]{1,0:T(8,128)(2,1)S(1)}, bf16[32,1152]{1,0:T(8,128)(2,1)S(1)}) custom-call(f32[1024,256]{1,0:T(8,128)S(1)} %norm.1.x_ref, s32[32,32]{1,0:T(8,128)S(1)} %copy-done.13, s32[1,128]{1,0:T(1,128)S(1)} %bitcast.11, f32[1,256]{1,0:T(1,128)S(1)} %bitcast.19, f32[1,256]{1,0:T(1,128)S(1)} %bitcast.20, bf16[64,256]{1,0:T(8,128)(2,1)S(1)} %bitcast.18, ...), custom_call_target="tpu_custom_call" | custom-call | flops 1073741824 | bytes 1088256 | tf_op jit(solution)/shard_map/pack/pallas_call | solution.py:313
  2.9 0.1 collective-permute-start
  3.0 2.7 %collective-permute-start.3 = (bf16[32,1152]{1,0:T(8,128)(2,1)S(1)}, bf16[32,1152]{1,0:T(8,128)(2,1)S(1)}, u32[]{:S(2)}, u32[]{:S(2)}) collective-permute-start(bf16[32,1152]{1,0:T(8,128)(2,1)S(1)} %get-tuple-element.20.refs_0_), channel_id=1, source_target_pairs={{0,1},{1,0},{2,3},{3,2},{4,5},{5,4},{6,7},{7,6},{8,9},{9,8},{10,11... | collective-permute-start | bytes 221192 | tf_op jit(solution)/shard_map/ppermute | solution.py:282
  5.8 0.0 copy-start.9
  5.8 0.0 copy-start.10
  5.8 5.6 %collective-permute-start.2 = (bf16[2,32,1152]{2,1,0:T(8,128)(2,1)S(1)}, bf16[2,32,1152]{2,1,0:T(8,128)(2,1)S(1)}, u32[]{:S(2)}, u32[]{:S(2)}) collective-permute-start(bf16[2,32,1152]{2,1,0:T(8,128)(2,1)S(1)} %join.2._), channel_id=1, source_target_pairs={{0,4},{1,0},{2,12},{3,8},{4,5},{5,1},{6,13},{7,9},{8,2},{9,6},{10,... | collective-permute-start | bytes 442376 | tf_op jit(solution)/shard_map/ppermute | solution.py:288
  11.4 1.9 %collective-permute-start.1 = (bf16[2,32,1152]{2,1,0:T(8,128)(2,1)S(1)}, bf16[2,32,1152]{2,1,0:T(8,128)(2,1)S(1)}, u32[]{:S(2)}, u32[]{:S(2)}) collective-permute-start(bf16[2,32,1152]{2,1,0:T(8,128)(2,1)S(1)} %join.2._), channel_id=1, source_target_pairs={{0,0},{1,4},{2,8},{3,12},{4,1},{5,5},{6,9},{7,13},{8,6},{9,2},{10,... | collective-permute-start | bytes 442376 | tf_op jit(solution)/shard_map/ppermute | solution.py:288
  13.4 0.1 collective-permute-start.4
  13.5 1.2 %base.1 = (f32[32,32,128]{2,1,0:T(8,128)S(1)}, bf16[4096,512]{1,0:T(8,128)(2,1)S(1)}) custom-call(bf16[32,32,128]{2,1,0:T(8,128)(2,1)S(1)} %copy-done.9, bf16[66,128]{1,0:T(8,128)(2,1)S(1)} %copy-done.12, s32[1,128]{1,0:T(1,128)S(1)} %bitcast.22, bf16[1024,128]{1,0:T(8,128)(2,1)S(1)} %copy-done.10, bf16[2,32,1152]{2,1,0:T(8,128)(2,1)S(1)} %join.2._), custom_call_target="tpu_custom_call" | custom-call | flops 1073741824 | bytes 689152 | tf_op jit(solution)/shard_map/base/pallas_call | solution.py:313
  14.7 0.0 copy-start.4
  14.7 6.4 %collective-permute-done.1.refs_0_ = bf16[2,32,1152]{2,1,0:T(8,128)(2,1)S(1)} collective-permute-done((bf16[2,32,1152]{2,1,0:T(8,128)(2,1)S(1)}, bf16[2,32,1152]{2,1,0:T(8,128)(2,1)S(1)}, u32[]{:S(2)}, u32[]{:S(2)}) %collective-permute-start.1) | collective-permute-done | bytes 147488 | tf_op jit(solution)/shard_map/ppermute | solution.py:288
  21.1 0.5 turn.1
  21.6 3.1 %edges.1 = (bf16[32,32,128]{2,1,0:T(8,128)(2,1)S(1)}, bf16[32,32,128]{2,1,0:T(8,128)(2,1)S(1)}, bf16[32,32,128]{2,1,0:T(8,128)(2,1)S(1)}, bf16[1024,128]{1,0:T(8,128)(2,1)S(1)}) custom-call(bf16[1024,128]{1,0:T(8,128)(2,1)S(1)} %get-tuple-element.18.turned_ref, bf16[32,128]{1,0:T(8,128)(2,1)S(1)} %get-tuple-element.19.live_ref, ...), custom_call_target="tpu_custom_call" | custom-call | bytes 5451776 | tf_op jit(solution)/shard_map/edges/pallas_call | solution.py:313
  24.7 0.1 collective-permute-start.5
  24.8 0.1 collective-permute-start.7
  24.9 1.9 %collective-permute-start.9 = (bf16[32,32,128]{2,1,0:T(8,128)(2,1)S(1)}, bf16[32,32,128]{2,1,0:T(8,128)(2,1)S(1)}, u32[]{:S(2)}, u32[]{:S(2)}) collective-permute-start(bf16[32,32,128]{2,1,0:T(8,128)(2,1)S(1)} %get-tuple-element.23), channel_id=1, source_target_pairs={{0,0},{4,1},{3,2},{7,3},{1,4},{5,5},{2,6},{6,7},{8,8},{12,9},{11,1... | collective-permute-start | bytes 786440 | tf_op jit(solution)/shard_map/ppermute | solution.py:303
  26.8 0.7 %collective-permute-start.8 = (bf16[32,32,128]{2,1,0:T(8,128)(2,1)S(1)}, bf16[32,32,128]{2,1,0:T(8,128)(2,1)S(1)}, u32[]{:S(2)}, u32[]{:S(2)}) collective-permute-start(bf16[32,32,128]{2,1,0:T(8,128)(2,1)S(1)} %get-tuple-element.23), channel_id=1, source_target_pairs={{1,0},{5,1},{2,2},{6,3},{0,4},{4,5},{3,6},{7,7},{9,8},{13,9},{10,1... | collective-permute-start | bytes 786440 | tf_op jit(solution)/shard_map/ppermute | solution.py:303
  27.5 10.1 %collective-permute-done.5.right_ref = bf16[32,32,128]{2,1,0:T(8,128)(2,1)S(1)} collective-permute-done((bf16[32,32,128]{2,1,0:T(8,128)(2,1)S(1)}, bf16[32,32,128]{2,1,0:T(8,128)(2,1)S(1)}, u32[]{:S(2)}, u32[]{:S(2)}) %collective-permute-start.5) | collective-permute-done | bytes 262176 | tf_op jit(solution)/shard_map/ppermute | solution.py:303
  37.6 0.2 gate.1.refs_2_.gate_ref
  37.8 0.1 panel.1.panel_ref
  38.0 1.3 %triangle.3.far_ref = f32[1024,128]{1,0:T(8,128)S(1)} custom-call(bf16[32,32,128]{2,1,0:T(8,128)(2,1)S(1)} %collective-permute-done.5.right_ref, f32[2,1024,128]{2,1,0:T(8,128)S(1)} %panel.1.panel_ref), custom_call_target="tpu_custom_call" | custom-call | bytes 1310720 | tf_op jit(solution)/shard_map/triangle/pallas_call | solution.py:313
  39.2 1.4 %collective-permute-done.9.right_ref = bf16[32,32,128]{2,1,0:T(8,128)(2,1)S(1)} collective-permute-done((bf16[32,32,128]{2,1,0:T(8,128)(2,1)S(1)}, bf16[32,32,128]{2,1,0:T(8,128)(2,1)S(1)}, u32[]{:S(2)}, u32[]{:S(2)}) %collective-permute-start.9) | collective-permute-done | bytes 262176 | tf_op jit(solution)/shard_map/ppermute | solution.py:303
  40.7 1.3 %triangle.4.refs_0_ = f32[1024,128]{1,0:T(8,128)S(1)} custom-call(bf16[32,32,128]{2,1,0:T(8,128)(2,1)S(1)} %collective-permute-done.9.right_ref, f32[2,1024,128]{2,1,0:T(8,128)S(1)} %panel.1.panel_ref), custom_call_target="tpu_custom_call" | custom-call | bytes 1310720 | tf_op jit(solution)/shard_map/triangle/pallas_call | solution.py:313
  41.9 1.3 %triangle.5.near_ref = f32[1024,128]{1,0:T(8,128)S(1)} custom-call(bf16[32,32,128]{2,1,0:T(8,128)(2,1)S(1)} %collective-permute-done.8.right_ref, f32[2,1024,128]{2,1,0:T(8,128)S(1)} %panel.1.panel_ref, f32[1024,128]{1,0:T(8,128)S(1)} %triangle.4.refs_0_), custom_call_target="tpu_custom_call" | custom-call | bytes 1835008 | tf_op jit(solution)/shard_map/triangle/pallas_call | solution.py:313
  43.2 2.2 %collective-permute-done.6.right_ref = bf16[32,32,128]{2,1,0:T(8,128)(2,1)S(1)} collective-permute-done((bf16[32,32,128]{2,1,0:T(8,128)(2,1)S(1)}, bf16[32,32,128]{2,1,0:T(8,128)(2,1)S(1)}, u32[]{:S(2)}, u32[]{:S(2)}) %collective-permute-start.6) | collective-permute-done | bytes 262176 | tf_op jit(solution)/shard_map/ppermute | solution.py:307
  45.5 1.3 %last.1 = (f32[1024,128]{1,0:T(8,128)S(1)}, bf16[1024,128]{1,0:T(8,128)(2,1)S(1)}) custom-call(bf16[32,32,128]{2,1,0:T(8,128)(2,1)S(1)} %collective-permute-done.6.right_ref, f32[2,1024,128]{2,1,0:T(8,128)S(1)} %panel.1.panel_ref, f32[1024,128]{1,0:T(8,128)S(1)} %triangle.3.far_ref, f32[1024,128]{1,0:T(8,128)S(1)} %triangle.5.near_ref), custom_call_target="tpu_custom_call" | custom-call | bytes 2359296 | tf_op jit(solution)/shard_map/last/pallas_call | solution.py:313
  46.8 0.9 %collective-permute-start.10 = (bf16[1024,128]{1,0:T(8,128)(2,1)S(1)}, bf16[1024,128]{1,0:T(8,128)(2,1)S(1)}, u32[]{:S(2)}, u32[]{:S(2)}) collective-permute-start(bf16[1024,128]{1,0:T(8,128)(2,1)S(1)} %get-tuple-element.27), channel_id=1, source_target_pairs={{0,2},{1,3},{2,0},{3,1},{4,6},{5,7},{6,4},{7,5},{8,10},{9,11},{10,... | collective-permute-start | bytes 786440 | tf_op jit(solution)/shard_map/ppermute | solution.py:277
  47.7 1.2 %collective-permute-done.10.other_ref = bf16[1024,128]{1,0:T(8,128)(2,1)S(1)} collective-permute-done((bf16[1024,128]{1,0:T(8,128)(2,1)S(1)}, bf16[1024,128]{1,0:T(8,128)(2,1)S(1)}, u32[]{:S(2)}, u32[]{:S(2)}) %collective-permute-start.10) | collective-permute-done | bytes 262176 | tf_op jit(solution)/shard_map/ppermute | solution.py:277
  48.8 1.2 %final.1 = bf16[32,32,128]{2,1,0:T(8,128)(2,1)} custom-call(f32[1024,128]{1,0:T(8,128)S(1)} %get-tuple-element.26.own_ref, bf16[1024,128]{1,0:T(8,128)(2,1)S(1)} %collective-permute-done.10.other_ref, bf16[32,32,128]{2,1,0:T(8,128)(2,1)S(1)} %get-tuple-element.28.updated_ref, f32[1024,128]{1,0:T(8,128)S(1)} %gate.1.refs_2_.gate_ref, f32[1,128]{1,0:T(1,128)S(1)} %bitcast.15, ...), custom_call_target="tpu_custom_call" | custom-call | bytes 1607168 | tf_op jit(solution)/shard_map/final/pallas_call | solution.py:313
  (43 shorter events, 0.1 us)
Async XLA Ops:
  0.0 1.5 %copy-start.2 = (s32[128]{0:T(128)S(1)}, s32[128]{0:T(128)}, u32[]{:S(2)}) copy-start(s32[128]{0:T(128)} %param.22) | copy-start | bytes 1540
  0.0 1.1 %copy-start.8 = (bf16[32,32,256]{2,1,0:T(8,128)(2,1)S(1)}, bf16[32,32,256]{2,1,0:T(8,128)(2,1)}, u32[]{:S(2)}) copy-start(bf16[32,32,256]{2,1,0:T(8,128)(2,1)} %x_ref.1) | copy-start | bytes 1572868
  1.1 0.8 %copy-start.11 = (bf16[256,64]{0,1:T(8,128)(2,1)S(1)}, bf16[256,64]{0,1:T(8,128)(2,1)}, u32[]{:S(2)}) copy-start(bf16[256,64]{0,1:T(8,128)(2,1)} %param.26) | copy-start | bytes 98308
  1.1 0.8 %copy-start.13 = (s32[32,32]{1,0:T(8,128)S(1)}, s32[32,32]{1,0:T(8,128)}, u32[]{:S(2)}) copy-start(s32[32,32]{1,0:T(8,128)} %mask_ref.1) | copy-start | bytes 12292
  1.1 0.8 %copy-start.14 = (f32[256]{0:T(256)S(1)}, f32[256]{0:T(256)}, u32[]{:S(2)}) copy-start(f32[256]{0:T(256)} %param.24) | copy-start | bytes 3076
  1.1 0.8 %copy-start.15 = (f32[256]{0:T(256)S(1)}, f32[256]{0:T(256)}, u32[]{:S(2)}) copy-start(f32[256]{0:T(256)} %param.25) | copy-start | bytes 3076
  1.1 0.8 %copy-start.16 = (f32[64]{0:T(128)S(1)}, f32[64]{0:T(128)}, u32[]{:S(2)}) copy-start(f32[64]{0:T(128)} %param.27) | copy-start | bytes 772
  1.1 4.6 %copy-start.18 = (f32[640]{0:T(1024)S(1)}, f32[640]{0:T(1024)}, u32[]{:S(2)}) copy-start(f32[640]{0:T(1024)} %param.33) | copy-start | bytes 7684
  2.9 2.8 %collective-permute-start = (bf16[32,1152]{1,0:T(8,128)(2,1)S(1)}, bf16[32,1152]{1,0:T(8,128)(2,1)S(1)}, u32[]{:S(2)}, u32[]{:S(2)}) collective-permute-start(bf16[32,1152]{1,0:T(8,128)(2,1)S(1)} %get-tuple-element.17.refs_0_), channel_id=1, source_target_pairs={{0,2},{1,3},{2,0},{3,1},{4,6},{5,7},{6,4},{7,5},{8,10},{9,11},{10,... | collective-permute-start | bytes 221192 | tf_op jit(solution)/shard_map/ppermute | solution.py:277
  3.0 10.3 %collective-permute-start.3 = (bf16[32,1152]{1,0:T(8,128)(2,1)S(1)}, bf16[32,1152]{1,0:T(8,128)(2,1)S(1)}, u32[]{:S(2)}, u32[]{:S(2)}) collective-permute-start(bf16[32,1152]{1,0:T(8,128)(2,1)S(1)} %get-tuple-element.20.refs_0_), channel_id=1, source_target_pairs={{0,1},{1,0},{2,3},{3,2},{4,5},{5,4},{6,7},{7,6},{8,9},{9,8},{10,11... | collective-permute-start | bytes 221192 | tf_op jit(solution)/shard_map/ppermute | solution.py:282
  5.8 7.7 %copy-start.9 = (bf16[32,32,128]{2,1,0:T(8,128)(2,1)S(1)}, bf16[32,32,128]{2,1,0:T(8,128)(2,1)}, u32[]{:S(2)}) copy-start(bf16[32,32,128]{2,1,0:T(8,128)(2,1)} %pair_ref.1) | copy-start | bytes 786436
  5.8 7.7 %copy-start.10 = (bf16[1024,128]{1,0:T(8,128)(2,1)S(1)}, bf16[1024,128]{1,0:T(8,128)(2,1)}, u32[]{:S(2)}) copy-start(bf16[1024,128]{1,0:T(8,128)(2,1)} %w_ref.4) | copy-start | bytes 786436
  5.8 7.7 %copy-start.12 = (bf16[66,128]{1,0:T(8,128)(2,1)S(1)}, bf16[66,128]{1,0:T(8,128)(2,1)}, u32[]{:S(2)}) copy-start(bf16[66,128]{1,0:T(8,128)(2,1)} %table_ref.1) | copy-start | bytes 50692
  5.8 7.7 %copy-start.17 = (s32[128]{0:T(128)S(1)}, s32[128]{0:T(128)}, u32[]{:S(2)}) copy-start(s32[128]{0:T(128)} %param.23) | copy-start | bytes 1540
  5.8 8.9 %collective-permute-start.2 = (bf16[2,32,1152]{2,1,0:T(8,128)(2,1)S(1)}, bf16[2,32,1152]{2,1,0:T(8,128)(2,1)S(1)}, u32[]{:S(2)}, u32[]{:S(2)}) collective-permute-start(bf16[2,32,1152]{2,1,0:T(8,128)(2,1)S(1)} %join.2._), channel_id=1, source_target_pairs={{0,4},{1,0},{2,12},{3,8},{4,5},{5,1},{6,13},{7,9},{8,2},{9,6},{10,... | collective-permute-start | bytes 442376 | tf_op jit(solution)/shard_map/ppermute | solution.py:288
  11.4 9.7 %collective-permute-start.1 = (bf16[2,32,1152]{2,1,0:T(8,128)(2,1)S(1)}, bf16[2,32,1152]{2,1,0:T(8,128)(2,1)S(1)}, u32[]{:S(2)}, u32[]{:S(2)}) collective-permute-start(bf16[2,32,1152]{2,1,0:T(8,128)(2,1)S(1)} %join.2._), channel_id=1, source_target_pairs={{0,0},{1,4},{2,8},{3,12},{4,1},{5,5},{6,9},{7,13},{8,6},{9,2},{10,... | collective-permute-start | bytes 442376 | tf_op jit(solution)/shard_map/ppermute | solution.py:288
  13.4 8.3 %collective-permute-start.4 = (bf16[2,32,1152]{2,1,0:T(8,128)(2,1)S(1)}, bf16[2,32,1152]{2,1,0:T(8,128)(2,1)S(1)}, u32[]{:S(2)}, u32[]{:S(2)}) collective-permute-start(bf16[2,32,1152]{2,1,0:T(8,128)(2,1)S(1)} %join.3.own_ref), channel_id=1, source_target_pairs={{0,2},{1,3},{2,0},{3,1},{4,6},{5,7},{6,4},{7,5},{8,10},{9,11},{10,... | collective-permute-start | bytes 442376 | tf_op jit(solution)/shard_map/ppermute | solution.py:277
  14.6 7.0 %copy-start = (bf16[128,640]{1,0:T(8,128)(2,1)S(1)}, bf16[128,640]{1,0:T(8,128)(2,1)}, u32[]{:S(2)}) copy-start(bf16[128,640]{1,0:T(8,128)(2,1)} %w_ref.6) | copy-start | bytes 491524
  14.6 7.0 %copy-start.3 = (f32[128]{0:T(128)S(1)}, f32[128]{0:T(128)}, u32[]{:S(2)}) copy-start(f32[128]{0:T(128)} %param.30) | copy-start | bytes 1540
  14.7 7.0 %copy-start.4 = (f32[128]{0:T(128)S(1)}, f32[128]{0:T(128)}, u32[]{:S(2)}) copy-start(f32[128]{0:T(128)} %param.31) | copy-start | bytes 1540
  24.7 12.8 %collective-permute-start.5 = (bf16[32,32,128]{2,1,0:T(8,128)(2,1)S(1)}, bf16[32,32,128]{2,1,0:T(8,128)(2,1)S(1)}, u32[]{:S(2)}, u32[]{:S(2)}) collective-permute-start(bf16[32,32,128]{2,1,0:T(8,128)(2,1)S(1)} %get-tuple-element.23), channel_id=1, source_target_pairs={{8,0},{13,1},{11,2},{14,3},{9,4},{12,5},{10,6},{15,7},{0,8},{5,9},... | collective-permute-start | bytes 786440 | tf_op jit(solution)/shard_map/ppermute | solution.py:303
  24.8 13.0 %collective-permute-start.7 = (bf16[32,32,128]{2,1,0:T(8,128)(2,1)S(1)}, bf16[32,32,128]{2,1,0:T(8,128)(2,1)S(1)}, u32[]{:S(2)}, u32[]{:S(2)}) collective-permute-start(bf16[32,32,128]{2,1,0:T(8,128)(2,1)S(1)} %get-tuple-element.24.refs_0_), channel_id=1, source_target_pairs={{0,1},{1,0},{2,3},{3,2},{4,5},{5,4},{6,7},{7,6},{8,9},{9,8},{10,11... | collective-permute-start | bytes 786440 | tf_op jit(solution)/shard_map/ppermute | solution.py:282
  24.9 15.8 %collective-permute-start.9 = (bf16[32,32,128]{2,1,0:T(8,128)(2,1)S(1)}, bf16[32,32,128]{2,1,0:T(8,128)(2,1)S(1)}, u32[]{:S(2)}, u32[]{:S(2)}) collective-permute-start(bf16[32,32,128]{2,1,0:T(8,128)(2,1)S(1)} %get-tuple-element.23), channel_id=1, source_target_pairs={{0,0},{4,1},{3,2},{7,3},{1,4},{5,5},{2,6},{6,7},{8,8},{12,9},{11,1... | collective-permute-start | bytes 786440 | tf_op jit(solution)/shard_map/ppermute | solution.py:303
  26.8 15.1 %collective-permute-start.8 = (bf16[32,32,128]{2,1,0:T(8,128)(2,1)S(1)}, bf16[32,32,128]{2,1,0:T(8,128)(2,1)S(1)}, u32[]{:S(2)}, u32[]{:S(2)}) collective-permute-start(bf16[32,32,128]{2,1,0:T(8,128)(2,1)S(1)} %get-tuple-element.23), channel_id=1, source_target_pairs={{1,0},{5,1},{2,2},{6,3},{0,4},{4,5},{3,6},{7,7},{9,8},{13,9},{10,1... | collective-permute-start | bytes 786440 | tf_op jit(solution)/shard_map/ppermute | solution.py:303
  37.6 7.9 %collective-permute-start.6 = (bf16[32,32,128]{2,1,0:T(8,128)(2,1)S(1)}, bf16[32,32,128]{2,1,0:T(8,128)(2,1)S(1)}, u32[]{:S(2)}, u32[]{:S(2)}) collective-permute-start(bf16[32,32,128]{2,1,0:T(8,128)(2,1)S(1)} %collective-permute-done.5.right_ref), channel_id=1, source_target_pairs={{0,4},{4,0},{8,12},{12,8},{1,5},{5,1},{9,13},{13,9},{2,6},{6,2},{1... | collective-permute-start | bytes 786440 | tf_op jit(solution)/shard_map/ppermute | solution.py:307
  37.9 10.9 %copy-start.1 = (bf16[128,128]{1,0:T(8,128)(2,1)S(1)}, bf16[128,128]{1,0:T(8,128)(2,1)}, u32[]{:S(2)}) copy-start(bf16[128,128]{1,0:T(8,128)(2,1)} %w_ref.7) | copy-start | bytes 98308
  37.9 10.9 %copy-start.5 = (f32[128]{0:T(128)S(1)}, f32[128]{0:T(128)}, u32[]{:S(2)}) copy-start(f32[128]{0:T(128)} %param.34) | copy-start | bytes 1540
  37.9 10.9 %copy-start.6 = (f32[128]{0:T(128)S(1)}, f32[128]{0:T(128)}, u32[]{:S(2)}) copy-start(f32[128]{0:T(128)} %param.35) | copy-start | bytes 1540
  37.9 10.9 %copy-start.7 = (f32[128]{0:T(128)S(1)}, f32[128]{0:T(128)}, u32[]{:S(2)}) copy-start(f32[128]{0:T(128)} %param.37) | copy-start | bytes 1540
  46.8 2.1 %collective-permute-start.10 = (bf16[1024,128]{1,0:T(8,128)(2,1)S(1)}, bf16[1024,128]{1,0:T(8,128)(2,1)S(1)}, u32[]{:S(2)}, u32[]{:S(2)}) collective-permute-start(bf16[1024,128]{1,0:T(8,128)(2,1)S(1)} %get-tuple-element.27), channel_id=1, source_target_pairs={{0,2},{1,3},{2,0},{3,1},{4,6},{5,7},{6,4},{7,5},{8,10},{9,11},{10,... | collective-permute-start | bytes 786440 | tf_op jit(solution)/shard_map/ppermute | solution.py:277

commit v12 on v11

--- a/solution.py
+++ b/solution.py
@@ -95,7 +95,7 @@
     return dot(jnp.broadcast_to(values.astype(F32), (8, total)).astype(BF16), pick)[0:1]
 
 
-def base_kernel(pair_ref, table_ref, chain_ref, w_ref, _, base_ref, block_ref, tscr, wscr):
+def base_kernel(pair_ref, table_ref, chain_ref, w_ref, base_ref, block_ref, tscr, wscr):
     rows, cols, channels = pair_ref.shape
     row_start = lax.axis_index("resi") * rows
     col_start = lax.axis_index(PLANE) * cols
@@ -210,67 +210,77 @@
     return block // chips, block % chips
 
 
-def add_block(panel_ref, chip, rscr, rows, before, store):
-    cols = store.shape[0] // rows
-    depth, channels = rscr.shape[0] // cols, rscr.shape[1]
+def add_block(panel_ref, chip, rscr, cols, first, before, store):
+    rows, depth, channels = store.shape[0] // cols, rscr.shape[0] // cols, rscr.shape[1]
     block = 8
     tiles = cols // 8
 
     def rows_body(at, carry):
-        place = [[pl.ds(pl.multiple_of((at * block + b) * cols + t * 8, 8), 8) for t in range(tiles)]
-                 for b in range(block)]
+        def place(b, t, start=0):
+            return pl.ds(pl.multiple_of((start + at * block + b) * cols + t * 8, 8), 8)
+
         if before is None:
             sums = [[jnp.zeros((8, channels), F32) for _ in range(tiles)] for _ in range(block)]
         else:
-            sums = [[before[place[b][t], :] for t in range(tiles)] for b in range(block)]
+            sums = [[before[place(b, t, first), :] for t in range(tiles)] for b in range(block)]
         for k in range(depth):
             column = [rscr[k * cols + t * 8:k * cols + t * 8 + 8, :] for t in range(tiles)]
             for b in range(block):
-                row = panel_ref[chip, pl.ds((at * block + b) * depth + k, 1), :]
+                row = panel_ref[chip, pl.ds((first + at * block + b) * depth + k, 1), :]
                 for t in range(tiles):
                     sums[b][t] = sums[b][t] + row * column[t]
         for b in range(block):
             for t in range(tiles):
-                store[place[b][t], :] = sums[b][t].astype(store.dtype)
+                store[place(b, t), :] = sums[b][t].astype(store.dtype)
         return carry
 
     lax.fori_loop(0, rows // block, rows_body, 0)
 
 
-def step_kernel(step, chips, fresh, right_ref, panel_ref, *refs):
+def step_kernel(step, chips, first, fresh, right_ref, panel_ref, *refs):
     out_ref, rscr = refs[-2:]
     z, core, x = [lax.axis_index(axis) for axis in GROUP]
     chip = source_of(z, core, x, step, chips)[1]
     rscr[...] = right_ref[...].astype(F32).reshape(rscr.shape)
-    add_block(panel_ref, chip, rscr, right_ref.shape[1], None if fresh else refs[0], out_ref)
-
-
-def last_kernel(step, chips, right_ref, panel_ref, far_ref, near_ref, own_ref, other_ref, rscr, acc):
-    step_kernel(step, chips, False, right_ref, panel_ref, far_ref, acc, rscr)
+    add_block(panel_ref, chip, rscr, right_ref.shape[1], first, None if fresh else refs[0], out_ref)
+
+
+def last_kernel(step, chips, first, right_ref, panel_ref, far_ref, near_ref, own_ref, other_ref,
+                rscr, acc):
+    step_kernel(step, chips, first, False, right_ref, panel_ref, far_ref, acc, rscr)
     mine = lax.axis_index("resi") // chips == lax.axis_index("resj")
+    at = pl.ds(first * right_ref.shape[1], acc.shape[0])
 
     @pl.when(mine)
     def _():
-        own_ref[...] = near_ref[...]
+        own_ref[...] = near_ref[at, :]
         other_ref[...] = acc[...].astype(BF16)
 
     @pl.when(jnp.logical_not(mine))
     def _():
         own_ref[...] = acc[...]
-        other_ref[...] = near_ref[...].astype(BF16)
-
-
-def final_kernel(own_ref, other_ref, updated_ref, gate_ref, gain_ref, shift_ref, w_ref, bias_ref, out_ref):
-    rows, cols, channels = out_ref.shape
+        other_ref[...] = near_ref[at, :].astype(BF16)
+
+
+def final_kernel(first, own_ref, other_ref, updated_ref, gate_ref, gain_ref, shift_ref, w_ref, bias_ref,
+                 *refs):
+    out_ref = refs[-1]
+    cols, channels = out_ref.shape[1:]
+    rows = own_ref.shape[0] // cols
+    start = 0
+    if first:
+        out_ref[:first] = refs[0][...]
+        start = first
     chunk = 8
     for i0 in range(0, rows, chunk):
         at = slice(i0 * cols, (i0 + chunk) * cols)
+        here = slice((first + i0) * cols, (first + i0 + chunk) * cols)
         sums = own_ref[at, :] + other_ref[at, :].astype(F32)
         normed = layer_norm(sums, gain_ref[...], shift_ref[...]).astype(BF16)
         result = dot(normed, w_ref[...]) + bias_ref[...]
-        updated = updated_ref[i0:i0 + chunk].reshape(chunk * cols, channels).astype(F32)
-        value = updated + gate_ref[at, :] * result
-        out_ref[i0:i0 + chunk] = value.astype(BF16).reshape(chunk, cols, channels)
+        updated = updated_ref[first + i0:first + i0 + chunk].reshape(chunk * cols, channels).astype(F32)
+        value = updated + gate_ref[here, :] * result
+        out_ref[start + i0:start + i0 + chunk] = value.astype(BF16).reshape(chunk, cols, channels)
 
 
 def swap_cores(block, count):
@@ -366,14 +376,14 @@
         flops=1 << 30, name="pack")
     right_swap = swap_cores(right, count)
     left_blocks = [left] + send_chips(left, chips)
-    pair = call(functools.partial(join_kernel, 2), shape((2,) + pack.shape, BF16), [],
-                [right, right_swap], name="join")
     base, block = call(
         base_kernel,
         [shape((rows, cols, channels), F32), shape((half * LANES, per * channels), BF16)],
         [pltpu.VMEM((LANES, channels), F32), pltpu.VMEM((half * half, channels), F32)],
-        [pair_features, relative_position_table, chain, outer_pair_projection, pair],
+        [pair_features, relative_position_table, chain, outer_pair_projection],
         flops=1 << 30, name="base")
+    pair = call(functools.partial(join_kernel, 2), shape((2,) + pack.shape, BF16), [],
+                [right, right_swap, base], name="join")
     rights = send_turned(pair, count, chips, count // 2)
     own_lefts = call(functools.partial(join_kernel, chips), shape((chips,) + pack.shape, BF16), [],
                      left_blocks, flops=1 << 36, name="join")
@@ -411,18 +421,25 @@
     for step in range(count - 1):
         sums = near if step < chips else far
         sums[:] = [call(
-            functools.partial(step_kernel, step, chips, not sums), block_sums, [scratch],
+            functools.partial(step_kernel, step, chips, 0, not sums), block_sums, [scratch],
             [right_edges[step], panel] + sums, name="triangle")]
-    own_sums, half_sums = call(
-        functools.partial(last_kernel, count - 1, chips),
-        [block_sums, shape((rows * cols, channels), BF16)], [scratch, scratch],
-        [right_edges[-1], panel] + far + near, name="last")
-    other_sums = swap_cores(half_sums, count)
-    return call(
-        final_kernel, shape((rows, cols, channels), BF16), [],
-        [own_sums, other_sums, updated, gate, flat(triangle_sum_norm_gain),
-         flat(triangle_sum_norm_bias), triangle_output_weight, flat(outer_pair_bias)],
-        name="final")
+    part = rows // 2
+    own_sums, other_sums, result = [], [], []
+    for first in (0, part):
+        own, half_sums = call(
+            functools.partial(last_kernel, count - 1, chips, first),
+            [shape((part * cols, channels), F32), shape((part * cols, channels), BF16)],
+            [scratch, pltpu.VMEM((part * cols, channels), F32)],
+            [right_edges[-1], panel] + far + near, flops=1 << 28, name="last")
+        own_sums.append(own)
+        other_sums.append(swap_cores(half_sums, count))
+    for n, first in enumerate((0, part)):
+        result = [call(
+            functools.partial(final_kernel, first), shape((first + part, cols, channels), BF16), [],
+            [own_sums[n], other_sums[n], updated, gate, flat(triangle_sum_norm_gain),
+             flat(triangle_sum_norm_bias), triangle_output_weight, flat(outer_pair_bias)] + result,
+            flops=1 << 28, name="final")]
+    return result[0]
 
 
 def solution(mesh):

time: 50.7 us -> 50.9 us (level)
    ppermute x1, waiting for transfers between devices: 2.21 us -> 0.97 us  [pass_on(): return lax.ppermute(block, 'resi', [(z, z ^ 1) for z in range(count)])]
    ppermute x2, waiting for transfers between devices: 6.44 us -> 7.65 us  [send_turned(): lax.ppermute(block, GROUP, [(z * count + p, (p ^ m ^ z // chips) * count...]
    ppermute x3, waiting for transfers between devices: 11.5 us -> 12.2 us  [send_same_core(): return lax.ppermute(block, GROUP, pairs)]
    pallas_call x14 -> x16, Pallas kernels: 12.8 us -> 13.1 us  [call(): pl.pallas_call(kernel, out_shape=outs, in_specs=[vmem] * len(args), out_s...]
    ppermute x3 -> x4, waiting for transfers between devices: 1.17 us -> 0.95 us  [swap_cores(): lax.ppermute(block, PLANE, [(p, p ^ count // 2) for p in range(count)])]
    ppermute x3 -> x4, starting transfers between devices: 1.1 us -> 1.17 us  [swap_cores(): lax.ppermute(block, PLANE, [(p, p ^ count // 2) for p in range(count)])]
  transfers between devices with their start and end apart: 11 -> 12, of which waited for: 5 -> 7; matrix products, arithmetic and copies ran while one was open for 0% -> 0% of each run, Pallas kernels for 12% -> 13%
where the time goes in v12:
time: 50.9 us; the launch traced here: 50.6 us
  waiting for transfers between devices  21.7 us (43%)
  starting transfers between devices  13.9 us (27%)
  Pallas kernels  13.1 us (26%)
  local copies, waits for them, and re-layouts  1.43 us (3%)
    pallas_call x16, Pallas kernels, call(): pl.pallas_call(kernel, out_shape=outs, in_specs=[vmem] * len(args), out_s...  13.1 us
    ppermute x3, waiting for transfers between devices, send_same_core(): return lax.ppermute(block, GROUP, pairs)  12.2 us
    ppermute x2, waiting for transfers between devices, send_turned(): lax.ppermute(block, GROUP, [(z * count + p, (p ^ m ^ z // chips) * count...  7.65 us
    ppermute x2, starting transfers between devices, send_turned(): lax.ppermute(block, GROUP, [(z * count + p, (p ^ m ^ z // chips) * count...  7.38 us
    ppermute x2, starting transfers between devices, send_chips(): lax.ppermute(block, 'seq', [(x, x ^ m) for x in range(chips)])  2.74 us
    ppermute x3, starting transfers between devices, send_same_core(): return lax.ppermute(block, GROUP, pairs)  2.66 us
    unnamed x38, local copies, waits for them, and re-layouts  1.43 us
    ppermute x4, starting transfers between devices, swap_cores(): lax.ppermute(block, PLANE, [(p, p ^ count // 2) for p in range(count)])  1.17 us
  transfers between devices with their start and end apart: 12, of which 7 were waited for; matrix products, arithmetic and copies ran while one was open for 0% of the time, Pallas kernels for 13%

profile of v12, /device:TPU:1, one launch (start us, length us, event | category | flops | bytes accessed | tf_op | source)
XLA Modules:
  0.0 50.6 jit_solution(4108331009501136771)
XLA Ops:
  0.0 1.1 %copy-done.8 = bf16[32,32,256]{2,1,0:T(8,128)(2,1)S(1)} copy-done((bf16[32,32,256]{2,1,0:T(8,128)(2,1)S(1)}, bf16[32,32,256]{2,1,0:T(8,128)(2,1)}, u32[]{:S(2)}) %copy-start.8) | copy-done | bytes 524312
  1.1 0.4 norm.1.x_ref
  1.5 0.3 copy-done.11
  1.8 1.1 %pack.1 = (bf16[32,1152]{1,0:T(8,128)(2,1)S(1)}, bf16[32,1152]{1,0:T(8,128)(2,1)S(1)}) custom-call(f32[1024,256]{1,0:T(8,128)S(1)} %norm.1.x_ref, s32[32,32]{1,0:T(8,128)S(1)} %copy-done.13, s32[1,128]{1,0:T(1,128)S(1)} %bitcast.17, f32[1,256]{1,0:T(1,128)S(1)} %bitcast.22, f32[1,256]{1,0:T(1,128)S(1)} %bitcast.23, bf16[64,256]{1,0:T(8,128)(2,1)S(1)} %bitcast.21, ...), custom_call_target="tpu_custom_call" | custom-call | flops 1073741824 | bytes 1088256 | tf_op jit(solution)/shard_map/pack/pallas_call | solution.py:323
  2.9 0.1 collective-permute-start
  3.0 2.7 %collective-permute-start.3 = (bf16[32,1152]{1,0:T(8,128)(2,1)S(1)}, bf16[32,1152]{1,0:T(8,128)(2,1)S(1)}, u32[]{:S(2)}, u32[]{:S(2)}) collective-permute-start(bf16[32,1152]{1,0:T(8,128)(2,1)S(1)} %get-tuple-element.23.refs_0_), channel_id=1, source_target_pairs={{0,1},{1,0},{2,3},{3,2},{4,5},{5,4},{6,7},{7,6},{8,9},{9,8},{10,11... | collective-permute-start | bytes 221192 | tf_op jit(solution)/shard_map/ppermute | solution.py:292
  5.8 1.2 %base.1 = (f32[32,32,128]{2,1,0:T(8,128)S(1)}, bf16[4096,512]{1,0:T(8,128)(2,1)S(1)}) custom-call(bf16[32,32,128]{2,1,0:T(8,128)(2,1)S(1)} %copy-done.9, bf16[66,128]{1,0:T(8,128)(2,1)S(1)} %copy-done.12, s32[1,128]{1,0:T(1,128)S(1)} %bitcast.25, bf16[1024,128]{1,0:T(8,128)(2,1)S(1)} %copy-done.10), custom_call_target="tpu_custom_call" | custom-call | flops 1073741824 | bytes 541696 | tf_op jit(solution)/shard_map/base/pallas_call | solution.py:323
  7.0 5.5 %collective-permute-start.2 = (bf16[2,32,1152]{2,1,0:T(8,128)(2,1)S(1)}, bf16[2,32,1152]{2,1,0:T(8,128)(2,1)S(1)}, u32[]{:S(2)}, u32[]{:S(2)}) collective-permute-start(bf16[2,32,1152]{2,1,0:T(8,128)(2,1)S(1)} %join.2), channel_id=1, source_target_pairs={{0,4},{1,0},{2,12},{3,8},{4,5},{5,1},{6,13},{7,9},{8,2},{9,6},{10,... | collective-permute-start | bytes 442376 | tf_op jit(solution)/shard_map/ppermute | solution.py:298
  12.4 1.9 %collective-permute-start.1 = (bf16[2,32,1152]{2,1,0:T(8,128)(2,1)S(1)}, bf16[2,32,1152]{2,1,0:T(8,128)(2,1)S(1)}, u32[]{:S(2)}, u32[]{:S(2)}) collective-permute-start(bf16[2,32,1152]{2,1,0:T(8,128)(2,1)S(1)} %join.2), channel_id=1, source_target_pairs={{0,0},{1,4},{2,8},{3,12},{4,1},{5,5},{6,9},{7,13},{8,6},{9,2},{10,... | collective-permute-start | bytes 442376 | tf_op jit(solution)/shard_map/ppermute | solution.py:298
  14.4 0.1 collective-permute-start.4
  14.5 0.6 %collective-permute-done.2.refs_1_ = bf16[2,32,1152]{2,1,0:T(8,128)(2,1)S(1)} collective-permute-done((bf16[2,32,1152]{2,1,0:T(8,128)(2,1)S(1)}, bf16[2,32,1152]{2,1,0:T(8,128)(2,1)S(1)}, u32[]{:S(2)}, u32[]{:S(2)}) %collective-permute-start.2) | collective-permute-done | bytes 147488 | tf_op jit(solution)/shard_map/ppermute | solution.py:298
  15.1 7.1 %collective-permute-done.1.refs_0_ = bf16[2,32,1152]{2,1,0:T(8,128)(2,1)S(1)} collective-permute-done((bf16[2,32,1152]{2,1,0:T(8,128)(2,1)S(1)}, bf16[2,32,1152]{2,1,0:T(8,128)(2,1)S(1)}, u32[]{:S(2)}, u32[]{:S(2)}) %collective-permute-start.1) | collective-permute-done | bytes 147488 | tf_op jit(solution)/shard_map/ppermute | solution.py:298
  22.1 0.5 turn.1
  22.7 3.1 %edges.1 = (bf16[32,32,128]{2,1,0:T(8,128)(2,1)S(1)}, bf16[32,32,128]{2,1,0:T(8,128)(2,1)S(1)}, bf16[32,32,128]{2,1,0:T(8,128)(2,1)S(1)}, bf16[1024,128]{1,0:T(8,128)(2,1)S(1)}) custom-call(bf16[1024,128]{1,0:T(8,128)(2,1)S(1)} %get-tuple-element.21.turned_ref, bf16[32,128]{1,0:T(8,128)(2,1)S(1)} %get-tuple-element.22.live_ref, ...), custom_call_target="tpu_custom_call" | custom-call | bytes 5451776 | tf_op jit(solution)/shard_map/edges/pallas_call | solution.py:323
  25.9 1.9 %collective-permute-start.9 = (bf16[32,32,128]{2,1,0:T(8,128)(2,1)S(1)}, bf16[32,32,128]{2,1,0:T(8,128)(2,1)S(1)}, u32[]{:S(2)}, u32[]{:S(2)}) collective-permute-start(bf16[32,32,128]{2,1,0:T(8,128)(2,1)S(1)} %get-tuple-element.25), channel_id=1, source_target_pairs={{0,0},{4,1},{3,2},{7,3},{1,4},{5,5},{2,6},{6,7},{8,8},{12,9},{11,1... | collective-permute-start | bytes 786440 | tf_op jit(solution)/shard_map/ppermute | solution.py:313
  27.8 0.7 %collective-permute-start.8 = (bf16[32,32,128]{2,1,0:T(8,128)(2,1)S(1)}, bf16[32,32,128]{2,1,0:T(8,128)(2,1)S(1)}, u32[]{:S(2)}, u32[]{:S(2)}) collective-permute-start(bf16[32,32,128]{2,1,0:T(8,128)(2,1)S(1)} %get-tuple-element.25), channel_id=1, source_target_pairs={{1,0},{5,1},{2,2},{6,3},{0,4},{4,5},{3,6},{7,7},{9,8},{13,9},{10,1... | collective-permute-start | bytes 786440 | tf_op jit(solution)/shard_map/ppermute | solution.py:313
  28.5 9.5 %collective-permute-done.5.right_ref = bf16[32,32,128]{2,1,0:T(8,128)(2,1)S(1)} collective-permute-done((bf16[32,32,128]{2,1,0:T(8,128)(2,1)S(1)}, bf16[32,32,128]{2,1,0:T(8,128)(2,1)S(1)}, u32[]{:S(2)}, u32[]{:S(2)}) %collective-permute-start.5) | collective-permute-done | bytes 262176 | tf_op jit(solution)/shard_map/ppermute | solution.py:313
  38.0 0.2 gate.1.refs_2_.gate_ref
  38.2 0.1 panel.1.panel_ref
  38.3 1.3 %triangle.3.far_ref = f32[1024,128]{1,0:T(8,128)S(1)} custom-call(bf16[32,32,128]{2,1,0:T(8,128)(2,1)S(1)} %collective-permute-done.5.right_ref, f32[2,1024,128]{2,1,0:T(8,128)S(1)} %panel.1.panel_ref), custom_call_target="tpu_custom_call" | custom-call | bytes 1310720 | tf_op jit(solution)/shard_map/triangle/pallas_call | solution.py:323
  39.6 2.7 %collective-permute-done.9.right_ref = bf16[32,32,128]{2,1,0:T(8,128)(2,1)S(1)} collective-permute-done((bf16[32,32,128]{2,1,0:T(8,128)(2,1)S(1)}, bf16[32,32,128]{2,1,0:T(8,128)(2,1)S(1)}, u32[]{:S(2)}, u32[]{:S(2)}) %collective-permute-start.9) | collective-permute-done | bytes 262176 | tf_op jit(solution)/shard_map/ppermute | solution.py:313
  42.3 1.3 %triangle.4.refs_0_ = f32[1024,128]{1,0:T(8,128)S(1)} custom-call(bf16[32,32,128]{2,1,0:T(8,128)(2,1)S(1)} %collective-permute-done.9.right_ref, f32[2,1024,128]{2,1,0:T(8,128)S(1)} %panel.1.panel_ref), custom_call_target="tpu_custom_call" | custom-call | bytes 1310720 | tf_op jit(solution)/shard_map/triangle/pallas_call | solution.py:323
  43.6 1.3 %triangle.5.near_ref = f32[1024,128]{1,0:T(8,128)S(1)} custom-call(bf16[32,32,128]{2,1,0:T(8,128)(2,1)S(1)} %collective-permute-done.8.right_ref, f32[2,1024,128]{2,1,0:T(8,128)S(1)} %panel.1.panel_ref, f32[1024,128]{1,0:T(8,128)S(1)} %triangle.4.refs_0_), custom_call_target="tpu_custom_call" | custom-call | bytes 1835008 | tf_op jit(solution)/shard_map/triangle/pallas_call | solution.py:323
  44.9 1.0 %collective-permute-done.6.right_ref = bf16[32,32,128]{2,1,0:T(8,128)(2,1)S(1)} collective-permute-done((bf16[32,32,128]{2,1,0:T(8,128)(2,1)S(1)}, bf16[32,32,128]{2,1,0:T(8,128)(2,1)S(1)}, u32[]{:S(2)}, u32[]{:S(2)}) %collective-permute-start.6) | collective-permute-done | bytes 262176 | tf_op jit(solution)/shard_map/ppermute | solution.py:317
  45.9 0.7 %last.3 = (f32[512,128]{1,0:T(8,128)S(1)}, bf16[512,128]{1,0:T(8,128)(2,1)S(1)}) custom-call(bf16[32,32,128]{2,1,0:T(8,128)(2,1)S(1)} %collective-permute-done.6.right_ref, f32[2,1024,128]{2,1,0:T(8,128)S(1)} %panel.1.panel_ref, f32[1024,128]{1,0:T(8,128)S(1)} %triangle.3.far_ref, f32[1024,128]{1,0:T(8,128)S(1)} %triangle.5.near_ref), custom_call_target="tpu_custom_call" | custom-call | flops 268435456 | bytes 2359296 | tf_op jit(solution)/shard_map/last/pallas_call | solution.py:323
  46.5 0.9 %collective-permute-start.11 = (bf16[512,128]{1,0:T(8,128)(2,1)S(1)}, bf16[512,128]{1,0:T(8,128)(2,1)S(1)}, u32[]{:S(2)}, u32[]{:S(2)}) collective-permute-start(bf16[512,128]{1,0:T(8,128)(2,1)S(1)} %get-tuple-element.32), channel_id=1, source_target_pairs={{0,2},{1,3},{2,0},{3,1},{4,6},{5,7},{6,4},{7,5},{8,10},{9,11},{10,... | collective-permute-start | bytes 393224 | tf_op jit(solution)/shard_map/ppermute | solution.py:287
  47.4 0.7 %last.2 = (f32[512,128]{1,0:T(8,128)S(1)}, bf16[512,128]{1,0:T(8,128)(2,1)S(1)}) custom-call(bf16[32,32,128]{2,1,0:T(8,128)(2,1)S(1)} %collective-permute-done.6.right_ref, f32[2,1024,128]{2,1,0:T(8,128)S(1)} %panel.1.panel_ref, f32[1024,128]{1,0:T(8,128)S(1)} %triangle.3.far_ref, f32[1024,128]{1,0:T(8,128)S(1)} %triangle.5.near_ref), custom_call_target="tpu_custom_call" | custom-call | flops 268435456 | bytes 2359296 | tf_op jit(solution)/shard_map/last/pallas_call | solution.py:323
  48.1 0.1 collective-permute-start.10
  48.2 0.2 collective-permute-done.11.other_ref
  48.4 0.4 final.2.refs_0_
  48.8 0.7 %collective-permute-done.10.other_ref = bf16[512,128]{1,0:T(8,128)(2,1)S(1)} collective-permute-done((bf16[512,128]{1,0:T(8,128)(2,1)S(1)}, bf16[512,128]{1,0:T(8,128)(2,1)S(1)}, u32[]{:S(2)}, u32[]{:S(2)}) %collective-permute-start.10) | collective-permute-done | bytes 131104 | tf_op jit(solution)/shard_map/ppermute | solution.py:287
  49.5 1.1 %final.3 = bf16[32,32,128]{2,1,0:T(8,128)(2,1)} custom-call(f32[512,128]{1,0:T(8,128)S(1)} %get-tuple-element.28.own_ref, bf16[512,128]{1,0:T(8,128)(2,1)S(1)} %collective-permute-done.10.other_ref, bf16[32,32,128]{2,1,0:T(8,128)(2,1)S(1)} %get-tuple-element.30.updated_ref, f32[1024,128]{1,0:T(8,128)S(1)} %gate.1.refs_2_.gate_ref, f32[1,128]{1,0:T(1,128)S(1)} %bitcast.12, ...), custom_call_target="tpu_custom_call" | custom-call | flops 268435456 | bytes 1345024 | tf_op jit(solution)/shard_map/final/pallas_call | solution.py:323
  (47 shorter events, 0.3 us)
Async XLA Ops:
  0.0 1.5 %copy-start.5 = (s32[128]{0:T(128)S(1)}, s32[128]{0:T(128)}, u32[]{:S(2)}) copy-start(s32[128]{0:T(128)} %param.22) | copy-start | bytes 1540
  0.0 1.1 %copy-start.8 = (bf16[32,32,256]{2,1,0:T(8,128)(2,1)S(1)}, bf16[32,32,256]{2,1,0:T(8,128)(2,1)}, u32[]{:S(2)}) copy-start(bf16[32,32,256]{2,1,0:T(8,128)(2,1)} %x_ref.1) | copy-start | bytes 1572868
  1.1 0.8 %copy-start.11 = (bf16[256,64]{0,1:T(8,128)(2,1)S(1)}, bf16[256,64]{0,1:T(8,128)(2,1)}, u32[]{:S(2)}) copy-start(bf16[256,64]{0,1:T(8,128)(2,1)} %param.26) | copy-start | bytes 98308
  1.1 0.8 %copy-start.13 = (s32[32,32]{1,0:T(8,128)S(1)}, s32[32,32]{1,0:T(8,128)}, u32[]{:S(2)}) copy-start(s32[32,32]{1,0:T(8,128)} %mask_ref.1) | copy-start | bytes 12292
  1.1 0.8 %copy-start.14 = (f32[256]{0:T(256)S(1)}, f32[256]{0:T(256)}, u32[]{:S(2)}) copy-start(f32[256]{0:T(256)} %param.24) | copy-start | bytes 3076
  1.1 0.8 %copy-start.15 = (f32[256]{0:T(256)S(1)}, f32[256]{0:T(256)}, u32[]{:S(2)}) copy-start(f32[256]{0:T(256)} %param.25) | copy-start | bytes 3076
  1.1 0.8 %copy-start.16 = (f32[64]{0:T(128)S(1)}, f32[64]{0:T(128)}, u32[]{:S(2)}) copy-start(f32[64]{0:T(128)} %param.27) | copy-start | bytes 772
  1.1 4.6 %copy-start.18 = (f32[640]{0:T(1024)S(1)}, f32[640]{0:T(1024)}, u32[]{:S(2)}) copy-start(f32[640]{0:T(1024)} %param.33) | copy-start | bytes 7684
  1.1 4.6 %copy-start.9 = (bf16[32,32,128]{2,1,0:T(8,128)(2,1)S(1)}, bf16[32,32,128]{2,1,0:T(8,128)(2,1)}, u32[]{:S(2)}) copy-start(bf16[32,32,128]{2,1,0:T(8,128)(2,1)} %pair_ref.1) | copy-start | bytes 786436
  1.1 4.6 %copy-start.10 = (bf16[1024,128]{1,0:T(8,128)(2,1)S(1)}, bf16[1024,128]{1,0:T(8,128)(2,1)}, u32[]{:S(2)}) copy-start(bf16[1024,128]{1,0:T(8,128)(2,1)} %w_ref.5) | copy-start | bytes 786436
  1.1 4.6 %copy-start.12 = (bf16[66,128]{1,0:T(8,128)(2,1)S(1)}, bf16[66,128]{1,0:T(8,128)(2,1)}, u32[]{:S(2)}) copy-start(bf16[66,128]{1,0:T(8,128)(2,1)} %table_ref.1) | copy-start | bytes 50692
  1.1 4.6 %copy-start.17 = (s32[128]{0:T(128)S(1)}, s32[128]{0:T(128)}, u32[]{:S(2)}) copy-start(s32[128]{0:T(128)} %param.23) | copy-start | bytes 1540
  2.9 4.0 %collective-permute-start = (bf16[32,1152]{1,0:T(8,128)(2,1)S(1)}, bf16[32,1152]{1,0:T(8,128)(2,1)S(1)}, u32[]{:S(2)}, u32[]{:S(2)}) collective-permute-start(bf16[32,1152]{1,0:T(8,128)(2,1)S(1)} %get-tuple-element.19.refs_0_), channel_id=1, source_target_pairs={{0,2},{1,3},{2,0},{3,1},{4,6},{5,7},{6,4},{7,5},{8,10},{9,11},{10,... | collective-permute-start | bytes 221192 | tf_op jit(solution)/shard_map/ppermute | solution.py:287
  3.0 11.3 %collective-permute-start.3 = (bf16[32,1152]{1,0:T(8,128)(2,1)S(1)}, bf16[32,1152]{1,0:T(8,128)(2,1)S(1)}, u32[]{:S(2)}, u32[]{:S(2)}) collective-permute-start(bf16[32,1152]{1,0:T(8,128)(2,1)S(1)} %get-tuple-element.23.refs_0_), channel_id=1, source_target_pairs={{0,1},{1,0},{2,3},{3,2},{4,5},{5,4},{6,7},{7,6},{8,9},{9,8},{10,11... | collective-permute-start | bytes 221192 | tf_op jit(solution)/shard_map/ppermute | solution.py:292
  7.0 8.1 %collective-permute-start.2 = (bf16[2,32,1152]{2,1,0:T(8,128)(2,1)S(1)}, bf16[2,32,1152]{2,1,0:T(8,128)(2,1)S(1)}, u32[]{:S(2)}, u32[]{:S(2)}) collective-permute-start(bf16[2,32,1152]{2,1,0:T(8,128)(2,1)S(1)} %join.2), channel_id=1, source_target_pairs={{0,4},{1,0},{2,12},{3,8},{4,5},{5,1},{6,13},{7,9},{8,2},{9,6},{10,... | collective-permute-start | bytes 442376 | tf_op jit(solution)/shard_map/ppermute | solution.py:298
  12.4 9.7 %collective-permute-start.1 = (bf16[2,32,1152]{2,1,0:T(8,128)(2,1)S(1)}, bf16[2,32,1152]{2,1,0:T(8,128)(2,1)S(1)}, u32[]{:S(2)}, u32[]{:S(2)}) collective-permute-start(bf16[2,32,1152]{2,1,0:T(8,128)(2,1)S(1)} %join.2), channel_id=1, source_target_pairs={{0,0},{1,4},{2,8},{3,12},{4,1},{5,5},{6,9},{7,13},{8,6},{9,2},{10,... | collective-permute-start | bytes 442376 | tf_op jit(solution)/shard_map/ppermute | solution.py:298
  14.4 8.3 %copy-start = (bf16[128,640]{1,0:T(8,128)(2,1)S(1)}, bf16[128,640]{1,0:T(8,128)(2,1)}, u32[]{:S(2)}) copy-start(bf16[128,640]{1,0:T(8,128)(2,1)} %w_ref.7) | copy-start | bytes 491524
  14.4 8.3 %copy-start.6 = (f32[128]{0:T(128)S(1)}, f32[128]{0:T(128)}, u32[]{:S(2)}) copy-start(f32[128]{0:T(128)} %param.30) | copy-start | bytes 1540
  14.4 8.3 %copy-start.7 = (f32[128]{0:T(128)S(1)}, f32[128]{0:T(128)}, u32[]{:S(2)}) copy-start(f32[128]{0:T(128)} %param.31) | copy-start | bytes 1540
  14.4 8.2 %collective-permute-start.4 = (bf16[2,32,1152]{2,1,0:T(8,128)(2,1)S(1)}, bf16[2,32,1152]{2,1,0:T(8,128)(2,1)S(1)}, u32[]{:S(2)}, u32[]{:S(2)}) collective-permute-start(bf16[2,32,1152]{2,1,0:T(8,128)(2,1)S(1)} %join.3.own_ref), channel_id=1, source_target_pairs={{0,2},{1,3},{2,0},{3,1},{4,6},{5,7},{6,4},{7,5},{8,10},{9,11},{10,... | collective-permute-start | bytes 442376 | tf_op jit(solution)/shard_map/ppermute | solution.py:287
  25.7 12.2 %collective-permute-start.5 = (bf16[32,32,128]{2,1,0:T(8,128)(2,1)S(1)}, bf16[32,32,128]{2,1,0:T(8,128)(2,1)S(1)}, u32[]{:S(2)}, u32[]{:S(2)}) collective-permute-start(bf16[32,32,128]{2,1,0:T(8,128)(2,1)S(1)} %get-tuple-element.25), channel_id=1, source_target_pairs={{8,0},{13,1},{11,2},{14,3},{9,4},{12,5},{10,6},{15,7},{0,8},{5,9},... | collective-permute-start | bytes 786440 | tf_op jit(solution)/shard_map/ppermute | solution.py:313
  25.8 12.4 %collective-permute-start.7 = (bf16[32,32,128]{2,1,0:T(8,128)(2,1)S(1)}, bf16[32,32,128]{2,1,0:T(8,128)(2,1)S(1)}, u32[]{:S(2)}, u32[]{:S(2)}) collective-permute-start(bf16[32,32,128]{2,1,0:T(8,128)(2,1)S(1)} %get-tuple-element.26.refs_0_), channel_id=1, source_target_pairs={{0,1},{1,0},{2,3},{3,2},{4,5},{5,4},{6,7},{7,6},{8,9},{9,8},{10,11... | collective-permute-start | bytes 786440 | tf_op jit(solution)/shard_map/ppermute | solution.py:292
  25.9 16.4 %collective-permute-start.9 = (bf16[32,32,128]{2,1,0:T(8,128)(2,1)S(1)}, bf16[32,32,128]{2,1,0:T(8,128)(2,1)S(1)}, u32[]{:S(2)}, u32[]{:S(2)}) collective-permute-start(bf16[32,32,128]{2,1,0:T(8,128)(2,1)S(1)} %get-tuple-element.25), channel_id=1, source_target_pairs={{0,0},{4,1},{3,2},{7,3},{1,4},{5,5},{2,6},{6,7},{8,8},{12,9},{11,1... | collective-permute-start | bytes 786440 | tf_op jit(solution)/shard_map/ppermute | solution.py:313
  27.8 15.8 %collective-permute-start.8 = (bf16[32,32,128]{2,1,0:T(8,128)(2,1)S(1)}, bf16[32,32,128]{2,1,0:T(8,128)(2,1)S(1)}, u32[]{:S(2)}, u32[]{:S(2)}) collective-permute-start(bf16[32,32,128]{2,1,0:T(8,128)(2,1)S(1)} %get-tuple-element.25), channel_id=1, source_target_pairs={{1,0},{5,1},{2,2},{6,3},{0,4},{4,5},{3,6},{7,7},{9,8},{13,9},{10,1... | collective-permute-start | bytes 786440 | tf_op jit(solution)/shard_map/ppermute | solution.py:313
  38.0 7.9 %collective-permute-start.6 = (bf16[32,32,128]{2,1,0:T(8,128)(2,1)S(1)}, bf16[32,32,128]{2,1,0:T(8,128)(2,1)S(1)}, u32[]{:S(2)}, u32[]{:S(2)}) collective-permute-start(bf16[32,32,128]{2,1,0:T(8,128)(2,1)S(1)} %collective-permute-done.5.right_ref), channel_id=1, source_target_pairs={{0,4},{4,0},{8,12},{12,8},{1,5},{5,1},{9,13},{13,9},{2,6},{6,2},{1... | collective-permute-start | bytes 786440 | tf_op jit(solution)/shard_map/ppermute | solution.py:317
  39.6 8.9 %copy-start.1 = (bf16[128,128]{1,0:T(8,128)(2,1)S(1)}, bf16[128,128]{1,0:T(8,128)(2,1)}, u32[]{:S(2)}) copy-start(bf16[128,128]{1,0:T(8,128)(2,1)} %w_ref.9) | copy-start | bytes 98308
  39.6 8.8 %copy-start.2 = (f32[128]{0:T(128)S(1)}, f32[128]{0:T(128)}, u32[]{:S(2)}) copy-start(f32[128]{0:T(128)} %param.34) | copy-start | bytes 1540
  39.6 8.8 %copy-start.3 = (f32[128]{0:T(128)S(1)}, f32[128]{0:T(128)}, u32[]{:S(2)}) copy-start(f32[128]{0:T(128)} %param.35) | copy-start | bytes 1540
  39.6 8.8 %copy-start.4 = (f32[128]{0:T(128)S(1)}, f32[128]{0:T(128)}, u32[]{:S(2)}) copy-start(f32[128]{0:T(128)} %param.37) | copy-start | bytes 1540
  46.5 1.9 %collective-permute-start.11 = (bf16[512,128]{1,0:T(8,128)(2,1)S(1)}, bf16[512,128]{1,0:T(8,128)(2,1)S(1)}, u32[]{:S(2)}, u32[]{:S(2)}) collective-permute-start(bf16[512,128]{1,0:T(8,128)(2,1)S(1)} %get-tuple-element.32), channel_id=1, source_target_pairs={{0,2},{1,3},{2,0},{3,1},{4,6},{5,7},{6,4},{7,5},{8,10},{9,11},{10,... | collective-permute-start | bytes 393224 | tf_op jit(solution)/shard_map/ppermute | solution.py:287
  48.1 1.4 %collective-permute-start.10 = (bf16[512,128]{1,0:T(8,128)(2,1)S(1)}, bf16[512,128]{1,0:T(8,128)(2,1)S(1)}, u32[]{:S(2)}, u32[]{:S(2)}) collective-permute-start(bf16[512,128]{1,0:T(8,128)(2,1)S(1)} %get-tuple-element.29), channel_id=1, source_target_pairs={{0,2},{1,3},{2,0},{3,1},{4,6},{5,7},{6,4},{7,5},{8,10},{9,11},{10,... | collective-permute-start | bytes 393224 | tf_op jit(solution)/shard_map/ppermute | solution.py:287

commit v13 on v12

--- a/solution.py
+++ b/solution.py
@@ -95,7 +95,7 @@
     return dot(jnp.broadcast_to(values.astype(F32), (8, total)).astype(BF16), pick)[0:1]
 
 
-def base_kernel(pair_ref, table_ref, chain_ref, w_ref, base_ref, block_ref, tscr, wscr):
+def base_kernel(pair_ref, table_ref, chain_ref, w_ref, _, base_ref, block_ref, tscr, wscr):
     rows, cols, channels = pair_ref.shape
     row_start = lax.axis_index("resi") * rows
     col_start = lax.axis_index(PLANE) * cols
@@ -123,13 +123,13 @@
 def turn_kernel(count, *refs):
     pairs = count // 2
     rights, (turned_ref, live_ref, rall, tscr) = refs[:pairs], refs[pairs:]
-    z, shift = lax.axis_index("resi"), lax.axis_index("resj")
+    z = lax.axis_index("resi")
     width, total_seqs = turned_ref.shape
     cols = live_ref.shape[0]
     half = width // cols
     for step in range(pairs):
         for n in range(2):
-            rall[z ^ shift ^ (step + n * pairs)] = rights[step][n]
+            rall[z ^ (step + n * pairs)] = rights[step][n]
     right = rall[...].reshape(total_seqs, -1)
     for at in range(0, width, LANES):
         for s in range(0, total_seqs, LANES):
@@ -264,14 +264,10 @@
 
 def final_kernel(first, own_ref, other_ref, updated_ref, gate_ref, gain_ref, shift_ref, w_ref, bias_ref,
                  *refs):
-    out_ref = refs[-1]
-    cols, channels = out_ref.shape[1:]
-    rows = own_ref.shape[0] // cols
-    start = 0
-    if first:
-        out_ref[:first] = refs[0][...]
-        start = first
+    out_hbm, vscr, sems = refs[-3:]
+    rows, cols, channels = vscr.shape
     chunk = 8
+    moves = []
     for i0 in range(0, rows, chunk):
         at = slice(i0 * cols, (i0 + chunk) * cols)
         here = slice((first + i0) * cols, (first + i0 + chunk) * cols)
@@ -280,7 +276,12 @@
         result = dot(normed, w_ref[...]) + bias_ref[...]
         updated = updated_ref[first + i0:first + i0 + chunk].reshape(chunk * cols, channels).astype(F32)
         value = updated + gate_ref[here, :] * result
-        out_ref[start + i0:start + i0 + chunk] = value.astype(BF16).reshape(chunk, cols, channels)
+        vscr[i0:i0 + chunk] = value.astype(BF16).reshape(chunk, cols, channels)
+        moves.append(pltpu.make_async_copy(
+            vscr.at[i0:i0 + chunk], out_hbm.at[first + i0:first + i0 + chunk], sems.at[i0 // chunk]))
+        moves[-1].start()
+    for move in moves:
+        move.wait()
 
 
 def swap_cores(block, count):
@@ -293,12 +294,11 @@
     ]
 
 
-def send_turned(block, count, chips, steps):
+def send_turned(block, count, steps):
     return [
         lax.ppermute(
             block, GROUP,
-            [(z * count + p, (p ^ m ^ (z // chips)) * count + z)
-             for z in range(count) for p in range(count)])
+            [(z * count + p, (p ^ m) * count + z) for z in range(count) for p in range(count)])
         for m in range(steps)
     ]
 
@@ -317,14 +317,15 @@
     return lax.ppermute(block, "resi", [(z, z ^ 1) for z in range(count)])
 
 
-def call(kernel, outs, scratch, args, flops=0, aliases=None, name=None):
+def call(kernel, outs, scratch, args, flops=0, aliases=None, hbm=False, name=None):
     vmem = pl.BlockSpec(memory_space=pltpu.VMEM)
+    result = pl.BlockSpec(memory_space=pl.ANY) if hbm else vmem
     size = sum(a.size * a.dtype.itemsize for a in args)
     return pl.pallas_call(
         kernel,
         out_shape=outs,
-        in_specs=[vmem] * len(args),
-        out_specs=[vmem] * len(outs) if isinstance(outs, list) else vmem,
+        in_specs=[result if n in (aliases or {}) else vmem for n in range(len(args))],
+        out_specs=[vmem] * len(outs) if isinstance(outs, list) else result,
         scratch_shapes=scratch,
         input_output_aliases=aliases or {},
         compiler_params=pltpu.CompilerParams(vmem_limit_bytes=40 * MIB),
@@ -376,15 +377,15 @@
         flops=1 << 30, name="pack")
     right_swap = swap_cores(right, count)
     left_blocks = [left] + send_chips(left, chips)
+    pair = call(functools.partial(join_kernel, 2), shape((2,) + pack.shape, BF16), [],
+                [right, right_swap], name="join")
     base, block = call(
         base_kernel,
         [shape((rows, cols, channels), F32), shape((half * LANES, per * channels), BF16)],
         [pltpu.VMEM((LANES, channels), F32), pltpu.VMEM((half * half, channels), F32)],
-        [pair_features, relative_position_table, chain, outer_pair_projection],
+        [pair_features, relative_position_table, chain, outer_pair_projection, pair],
         flops=1 << 30, name="base")
-    pair = call(functools.partial(join_kernel, 2), shape((2,) + pack.shape, BF16), [],
-                [right, right_swap, base], name="join")
-    rights = send_turned(pair, count, chips, count // 2)
+    rights = send_turned(pair, count, count // 2)
     own_lefts = call(functools.partial(join_kernel, chips), shape((chips,) + pack.shape, BF16), [],
                      left_blocks, flops=1 << 36, name="join")
     lefts = [own_lefts, swap_cores(own_lefts, count)]
@@ -434,11 +435,13 @@
         own_sums.append(own)
         other_sums.append(swap_cores(half_sums, count))
     for n, first in enumerate((0, part)):
+        args = [own_sums[n], other_sums[n], updated, gate, flat(triangle_sum_norm_gain),
+                flat(triangle_sum_norm_bias), triangle_output_weight, flat(outer_pair_bias)]
         result = [call(
-            functools.partial(final_kernel, first), shape((first + part, cols, channels), BF16), [],
-            [own_sums[n], other_sums[n], updated, gate, flat(triangle_sum_norm_gain),
-             flat(triangle_sum_norm_bias), triangle_output_weight, flat(outer_pair_bias)] + result,
-            flops=1 << 28, name="final")]
+            functools.partial(final_kernel, first), shape((rows, cols, channels), BF16),
+            [pltpu.VMEM((part, cols, channels), BF16), pltpu.SemaphoreType.DMA((part // 8,))],
+            args + result, flops=1 << 28, aliases={len(args): 0} if n else None, hbm=True,
+            name="final")]
     return result[0]
 
 

time: 50.9 us -> 48.3 us (0.949)
  waiting for transfers between devices: 21.7 us -> 18.7 us
  Pallas kernels: 13.1 us -> 13.7 us
    ppermute x2, waiting for transfers between devices: 7.65 us -> 5.66 us  [send_turned(): lax.ppermute(block, GROUP, [(z * count + p, (p ^ m) * count + z) for z in...]
    ppermute x2, starting transfers between devices: 7.38 us -> 5.51 us  [send_turned(): lax.ppermute(block, GROUP, [(z * count + p, (p ^ m) * count + z) for z in...]
    ppermute x3, starting transfers between devices: 2.66 us -> 4.31 us  [send_same_core(): return lax.ppermute(block, GROUP, pairs)]
    ppermute x4, waiting for transfers between devices: 0.95 us -> 0.19 us  [swap_cores(): lax.ppermute(block, PLANE, [(p, p ^ count // 2) for p in range(count)])]
    pallas_call x16, Pallas kernels: 13.1 us -> 13.7 us  [call(): pl.pallas_call(kernel, out_shape=outs, in_specs=[result if n in (aliases...]
  transfers between devices with their start and end apart: 12 -> 12, of which waited for: 7 -> 7; matrix products, arithmetic and copies ran while one was open for 0% -> 0% of each run, Pallas kernels for 13% -> 16%
where the time goes in v13:
time: 48.3 us; the launch traced here: 47.7 us
  waiting for transfers between devices  18.7 us (39%)
  Pallas kernels  13.7 us (28%)
  starting transfers between devices  13.5 us (28%)
  local copies, waits for them, and re-layouts  1.48 us (3%)
    pallas_call x16, Pallas kernels, call(): pl.pallas_call(kernel, out_shape=outs, in_specs=[result if n in (aliases...  13.7 us
    ppermute x3, waiting for transfers between devices, send_same_core(): return lax.ppermute(block, GROUP, pairs)  12.2 us
    ppermute x2, waiting for transfers between devices, send_turned(): lax.ppermute(block, GROUP, [(z * count + p, (p ^ m) * count + z) for z in...  5.66 us
    ppermute x2, starting transfers between devices, send_turned(): lax.ppermute(block, GROUP, [(z * count + p, (p ^ m) * count + z) for z in...  5.51 us
    ppermute x3, starting transfers between devices, send_same_core(): return lax.ppermute(block, GROUP, pairs)  4.31 us
    ppermute x2, starting transfers between devices, send_chips(): lax.ppermute(block, 'seq', [(x, x ^ m) for x in range(chips)])  2.68 us
    unnamed x38, local copies, waits for them, and re-layouts  1.48 us
  transfers between devices with their start and end apart: 12, of which 7 were waited for; matrix products, arithmetic and copies ran while one was open for 0% of the time, Pallas kernels for 16%

profile of v13, /device:TPU:1, one launch (start us, length us, event | category | flops | bytes accessed | tf_op | source)
XLA Modules:
  0.0 47.7 jit_solution(1129217498858073746)
XLA Ops:
  0.0 1.1 %copy-done.8 = bf16[32,32,256]{2,1,0:T(8,128)(2,1)S(1)} copy-done((bf16[32,32,256]{2,1,0:T(8,128)(2,1)S(1)}, bf16[32,32,256]{2,1,0:T(8,128)(2,1)}, u32[]{:S(2)}) %copy-start.8) | copy-done | bytes 524312
  1.1 0.4 norm.1.x_ref
  1.5 0.3 copy-done.11
  1.8 1.1 %pack.1 = (bf16[32,1152]{1,0:T(8,128)(2,1)S(1)}, bf16[32,1152]{1,0:T(8,128)(2,1)S(1)}) custom-call(f32[1024,256]{1,0:T(8,128)S(1)} %norm.1.x_ref, s32[32,32]{1,0:T(8,128)S(1)} %copy-done.13, s32[1,128]{1,0:T(1,128)S(1)} %bitcast.17, f32[1,256]{1,0:T(1,128)S(1)} %bitcast.22, f32[1,256]{1,0:T(1,128)S(1)} %bitcast.23, bf16[64,256]{1,0:T(8,128)(2,1)S(1)} %bitcast.21, ...), custom_call_target="tpu_custom_call" | custom-call | flops 1073741824 | bytes 1088256 | tf_op jit(solution)/shard_map/pack/pallas_call | solution.py:324
  2.9 0.1 collective-permute-start
  3.0 2.7 %collective-permute-start.3 = (bf16[32,1152]{1,0:T(8,128)(2,1)S(1)}, bf16[32,1152]{1,0:T(8,128)(2,1)S(1)}, u32[]{:S(2)}, u32[]{:S(2)}) collective-permute-start(bf16[32,1152]{1,0:T(8,128)(2,1)S(1)} %get-tuple-element.22.refs_0_), channel_id=1, source_target_pairs={{0,1},{1,0},{2,3},{3,2},{4,5},{5,4},{6,7},{7,6},{8,9},{9,8},{10,11... | collective-permute-start | bytes 221192 | tf_op jit(solution)/shard_map/ppermute | solution.py:293
  5.8 3.6 %collective-permute-start.2 = (bf16[2,32,1152]{2,1,0:T(8,128)(2,1)S(1)}, bf16[2,32,1152]{2,1,0:T(8,128)(2,1)S(1)}, u32[]{:S(2)}, u32[]{:S(2)}) collective-permute-start(bf16[2,32,1152]{2,1,0:T(8,128)(2,1)S(1)} %join.2._), channel_id=1, source_target_pairs={{0,4},{1,0},{2,12},{3,8},{4,5},{5,1},{6,13},{7,9},{8,6},{9,2},{10,... | collective-permute-start | bytes 442376 | tf_op jit(solution)/shard_map/ppermute | solution.py:299
  9.4 1.9 %collective-permute-start.1 = (bf16[2,32,1152]{2,1,0:T(8,128)(2,1)S(1)}, bf16[2,32,1152]{2,1,0:T(8,128)(2,1)S(1)}, u32[]{:S(2)}, u32[]{:S(2)}) collective-permute-start(bf16[2,32,1152]{2,1,0:T(8,128)(2,1)S(1)} %join.2._), channel_id=1, source_target_pairs={{0,0},{1,4},{2,8},{3,12},{4,1},{5,5},{6,9},{7,13},{8,2},{9,6},{10,... | collective-permute-start | bytes 442376 | tf_op jit(solution)/shard_map/ppermute | solution.py:299
  11.5 1.2 %base.1 = (f32[32,32,128]{2,1,0:T(8,128)S(1)}, bf16[4096,512]{1,0:T(8,128)(2,1)S(1)}) custom-call(bf16[32,32,128]{2,1,0:T(8,128)(2,1)S(1)} %copy-done.9, bf16[66,128]{1,0:T(8,128)(2,1)S(1)} %copy-done.12, s32[1,128]{1,0:T(1,128)S(1)} %bitcast.25, bf16[1024,128]{1,0:T(8,128)(2,1)S(1)} %copy-done.10, bf16[2,32,1152]{2,1,0:T(8,128)(2,1)S(1)} %join.2._), custom_call_target="tpu_custom_call" | custom-call | flops 1073741824 | bytes 689152 | tf_op jit(solution)/shard_map/base/pallas_call | solution.py:324
  12.7 0.8 %collective-permute-done.2.refs_1_ = bf16[2,32,1152]{2,1,0:T(8,128)(2,1)S(1)} collective-permute-done((bf16[2,32,1152]{2,1,0:T(8,128)(2,1)S(1)}, bf16[2,32,1152]{2,1,0:T(8,128)(2,1)S(1)}, u32[]{:S(2)}, u32[]{:S(2)}) %collective-permute-start.2) | collective-permute-done | bytes 147488 | tf_op jit(solution)/shard_map/ppermute | solution.py:299
  13.4 4.9 %collective-permute-done.1.refs_0_ = bf16[2,32,1152]{2,1,0:T(8,128)(2,1)S(1)} collective-permute-done((bf16[2,32,1152]{2,1,0:T(8,128)(2,1)S(1)}, bf16[2,32,1152]{2,1,0:T(8,128)(2,1)S(1)}, u32[]{:S(2)}, u32[]{:S(2)}) %collective-permute-start.1) | collective-permute-done | bytes 147488 | tf_op jit(solution)/shard_map/ppermute | solution.py:299
  18.3 0.5 turn.1
  18.8 3.1 %edges.1 = (bf16[32,32,128]{2,1,0:T(8,128)(2,1)S(1)}, bf16[32,32,128]{2,1,0:T(8,128)(2,1)S(1)}, bf16[32,32,128]{2,1,0:T(8,128)(2,1)S(1)}, bf16[1024,128]{1,0:T(8,128)(2,1)S(1)}) custom-call(bf16[1024,128]{1,0:T(8,128)(2,1)S(1)} %get-tuple-element.20.turned_ref, bf16[32,128]{1,0:T(8,128)(2,1)S(1)} %get-tuple-element.21.live_ref, ...), custom_call_target="tpu_custom_call" | custom-call | bytes 5451776 | tf_op jit(solution)/shard_map/edges/pallas_call | solution.py:324
  21.9 1.7 %collective-permute-start.5 = (bf16[32,32,128]{2,1,0:T(8,128)(2,1)S(1)}, bf16[32,32,128]{2,1,0:T(8,128)(2,1)S(1)}, u32[]{:S(2)}, u32[]{:S(2)}) collective-permute-start(bf16[32,32,128]{2,1,0:T(8,128)(2,1)S(1)} %get-tuple-element.25), channel_id=1, source_target_pairs={{8,0},{13,1},{11,2},{14,3},{9,4},{12,5},{10,6},{15,7},{0,8},{5,9},... | collective-permute-start | bytes 786440 | tf_op jit(solution)/shard_map/ppermute | solution.py:313
  23.7 1.9 %collective-permute-start.9 = (bf16[32,32,128]{2,1,0:T(8,128)(2,1)S(1)}, bf16[32,32,128]{2,1,0:T(8,128)(2,1)S(1)}, u32[]{:S(2)}, u32[]{:S(2)}) collective-permute-start(bf16[32,32,128]{2,1,0:T(8,128)(2,1)S(1)} %get-tuple-element.25), channel_id=1, source_target_pairs={{0,0},{4,1},{3,2},{7,3},{1,4},{5,5},{2,6},{6,7},{8,8},{12,9},{11,1... | collective-permute-start | bytes 786440 | tf_op jit(solution)/shard_map/ppermute | solution.py:313
  25.6 0.7 %collective-permute-start.8 = (bf16[32,32,128]{2,1,0:T(8,128)(2,1)S(1)}, bf16[32,32,128]{2,1,0:T(8,128)(2,1)S(1)}, u32[]{:S(2)}, u32[]{:S(2)}) collective-permute-start(bf16[32,32,128]{2,1,0:T(8,128)(2,1)S(1)} %get-tuple-element.25), channel_id=1, source_target_pairs={{1,0},{5,1},{2,2},{6,3},{0,4},{4,5},{3,6},{7,7},{9,8},{13,9},{10,1... | collective-permute-start | bytes 786440 | tf_op jit(solution)/shard_map/ppermute | solution.py:313
  26.3 8.5 %collective-permute-done.5.right_ref = bf16[32,32,128]{2,1,0:T(8,128)(2,1)S(1)} collective-permute-done((bf16[32,32,128]{2,1,0:T(8,128)(2,1)S(1)}, bf16[32,32,128]{2,1,0:T(8,128)(2,1)S(1)}, u32[]{:S(2)}, u32[]{:S(2)}) %collective-permute-start.5) | collective-permute-done | bytes 262176 | tf_op jit(solution)/shard_map/ppermute | solution.py:313
  34.7 0.2 collective-permute-start.6
  34.9 0.2 gate.1.refs_2_.gate_ref
  35.1 0.1 panel.1.panel_ref
  35.2 1.3 %triangle.3.far_ref = f32[1024,128]{1,0:T(8,128)S(1)} custom-call(bf16[32,32,128]{2,1,0:T(8,128)(2,1)S(1)} %collective-permute-done.5.right_ref, f32[2,1024,128]{2,1,0:T(8,128)S(1)} %panel.1.panel_ref), custom_call_target="tpu_custom_call" | custom-call | bytes 1310720 | tf_op jit(solution)/shard_map/triangle/pallas_call | solution.py:324
  36.5 3.7 %collective-permute-done.9.right_ref = bf16[32,32,128]{2,1,0:T(8,128)(2,1)S(1)} collective-permute-done((bf16[32,32,128]{2,1,0:T(8,128)(2,1)S(1)}, bf16[32,32,128]{2,1,0:T(8,128)(2,1)S(1)}, u32[]{:S(2)}, u32[]{:S(2)}) %collective-permute-start.9) | collective-permute-done | bytes 262176 | tf_op jit(solution)/shard_map/ppermute | solution.py:313
  40.3 1.3 %triangle.4.refs_0_ = f32[1024,128]{1,0:T(8,128)S(1)} custom-call(bf16[32,32,128]{2,1,0:T(8,128)(2,1)S(1)} %collective-permute-done.9.right_ref, f32[2,1024,128]{2,1,0:T(8,128)S(1)} %panel.1.panel_ref), custom_call_target="tpu_custom_call" | custom-call | bytes 1310720 | tf_op jit(solution)/shard_map/triangle/pallas_call | solution.py:324
  41.5 1.3 %triangle.5.near_ref = f32[1024,128]{1,0:T(8,128)S(1)} custom-call(bf16[32,32,128]{2,1,0:T(8,128)(2,1)S(1)} %collective-permute-done.8.right_ref, f32[2,1024,128]{2,1,0:T(8,128)S(1)} %panel.1.panel_ref, f32[1024,128]{1,0:T(8,128)S(1)} %triangle.4.refs_0_), custom_call_target="tpu_custom_call" | custom-call | bytes 1835008 | tf_op jit(solution)/shard_map/triangle/pallas_call | solution.py:324
  42.8 0.7 %collective-permute-done.6.right_ref = bf16[32,32,128]{2,1,0:T(8,128)(2,1)S(1)} collective-permute-done((bf16[32,32,128]{2,1,0:T(8,128)(2,1)S(1)}, bf16[32,32,128]{2,1,0:T(8,128)(2,1)S(1)}, u32[]{:S(2)}, u32[]{:S(2)}) %collective-permute-start.6) | collective-permute-done | bytes 262176 | tf_op jit(solution)/shard_map/ppermute | solution.py:317
  43.5 0.7 %last.3 = (f32[512,128]{1,0:T(8,128)S(1)}, bf16[512,128]{1,0:T(8,128)(2,1)S(1)}) custom-call(bf16[32,32,128]{2,1,0:T(8,128)(2,1)S(1)} %collective-permute-done.6.right_ref, f32[2,1024,128]{2,1,0:T(8,128)S(1)} %panel.1.panel_ref, f32[1024,128]{1,0:T(8,128)S(1)} %triangle.3.far_ref, f32[1024,128]{1,0:T(8,128)S(1)} %triangle.5.near_ref), custom_call_target="tpu_custom_call" | custom-call | flops 268435456 | bytes 2359296 | tf_op jit(solution)/shard_map/last/pallas_call | solution.py:324
  44.2 0.5 collective-permute-start.11
  44.6 0.7 %last.2 = (f32[512,128]{1,0:T(8,128)S(1)}, bf16[512,128]{1,0:T(8,128)(2,1)S(1)}) custom-call(bf16[32,32,128]{2,1,0:T(8,128)(2,1)S(1)} %collective-permute-done.6.right_ref, f32[2,1024,128]{2,1,0:T(8,128)S(1)} %panel.1.panel_ref, f32[1024,128]{1,0:T(8,128)S(1)} %triangle.3.far_ref, f32[1024,128]{1,0:T(8,128)S(1)} %triangle.5.near_ref), custom_call_target="tpu_custom_call" | custom-call | flops 268435456 | bytes 2359296 | tf_op jit(solution)/shard_map/last/pallas_call | solution.py:324
  45.3 0.2 collective-permute-start.10
  45.5 0.1 collective-permute-done.11.other_ref
  45.6 1.0 %final.2.refs_0_ = bf16[32,32,128]{2,1,0:T(8,128)(2,1)} custom-call(f32[512,128]{1,0:T(8,128)S(1)} %get-tuple-element.31.own_ref, bf16[512,128]{1,0:T(8,128)(2,1)S(1)} %collective-permute-done.11.other_ref, bf16[32,32,128]{2,1,0:T(8,128)(2,1)S(1)} %get-tuple-element.30.updated_ref, f32[1024,128]{1,0:T(8,128)S(1)} %gate.1.refs_2_.gate_ref, ...), custom_call_target="tpu_custom_call" | custom-call | flops 268435456 | bytes 1213952 | tf_op jit(solution)/shard_map/final/pallas_call | solution.py:324
  46.7 1.0 %final.3 = bf16[32,32,128]{2,1,0:T(8,128)(2,1)} custom-call(f32[512,128]{1,0:T(8,128)S(1)} %get-tuple-element.28.own_ref, bf16[512,128]{1,0:T(8,128)(2,1)S(1)} %collective-permute-done.10.other_ref, bf16[32,32,128]{2,1,0:T(8,128)(2,1)S(1)} %get-tuple-element.30.updated_ref, f32[1024,128]{1,0:T(8,128)S(1)} %gate.1.refs_2_.gate_ref, ...), custom_call_target="tpu_custom_call", output_to_operand_aliasing={{}: (8, {})} | custom-call | flops 268435456 | bytes 1476096 | tf_op jit(solution)/shard_map/final/pallas_call | solution.py:324
  (47 shorter events, 0.3 us)
Async XLA Ops:
  0.0 1.5 %copy-start.5 = (s32[128]{0:T(128)S(1)}, s32[128]{0:T(128)}, u32[]{:S(2)}) copy-start(s32[128]{0:T(128)} %param.22) | copy-start | bytes 1540
  0.0 1.1 %copy-start.8 = (bf16[32,32,256]{2,1,0:T(8,128)(2,1)S(1)}, bf16[32,32,256]{2,1,0:T(8,128)(2,1)}, u32[]{:S(2)}) copy-start(bf16[32,32,256]{2,1,0:T(8,128)(2,1)} %x_ref.1) | copy-start | bytes 1572868
  1.1 0.8 %copy-start.11 = (bf16[256,64]{0,1:T(8,128)(2,1)S(1)}, bf16[256,64]{0,1:T(8,128)(2,1)}, u32[]{:S(2)}) copy-start(bf16[256,64]{0,1:T(8,128)(2,1)} %param.26) | copy-start | bytes 98308
  1.1 0.8 %copy-start.13 = (s32[32,32]{1,0:T(8,128)S(1)}, s32[32,32]{1,0:T(8,128)}, u32[]{:S(2)}) copy-start(s32[32,32]{1,0:T(8,128)} %mask_ref.1) | copy-start | bytes 12292
  1.1 0.8 %copy-start.14 = (f32[256]{0:T(256)S(1)}, f32[256]{0:T(256)}, u32[]{:S(2)}) copy-start(f32[256]{0:T(256)} %param.24) | copy-start | bytes 3076
  1.1 0.8 %copy-start.15 = (f32[256]{0:T(256)S(1)}, f32[256]{0:T(256)}, u32[]{:S(2)}) copy-start(f32[256]{0:T(256)} %param.25) | copy-start | bytes 3076
  1.1 0.8 %copy-start.16 = (f32[64]{0:T(128)S(1)}, f32[64]{0:T(128)}, u32[]{:S(2)}) copy-start(f32[64]{0:T(128)} %param.27) | copy-start | bytes 772
  1.1 4.6 %copy-start.18 = (f32[640]{0:T(1024)S(1)}, f32[640]{0:T(1024)}, u32[]{:S(2)}) copy-start(f32[640]{0:T(1024)} %param.33) | copy-start | bytes 7684
  2.9 2.8 %collective-permute-start = (bf16[32,1152]{1,0:T(8,128)(2,1)S(1)}, bf16[32,1152]{1,0:T(8,128)(2,1)S(1)}, u32[]{:S(2)}, u32[]{:S(2)}) collective-permute-start(bf16[32,1152]{1,0:T(8,128)(2,1)S(1)} %get-tuple-element.19.refs_0_), channel_id=1, source_target_pairs={{0,2},{1,3},{2,0},{3,1},{4,6},{5,7},{6,4},{7,5},{8,10},{9,11},{10,... | collective-permute-start | bytes 221192 | tf_op jit(solution)/shard_map/ppermute | solution.py:288
  3.0 8.3 %collective-permute-start.3 = (bf16[32,1152]{1,0:T(8,128)(2,1)S(1)}, bf16[32,1152]{1,0:T(8,128)(2,1)S(1)}, u32[]{:S(2)}, u32[]{:S(2)}) collective-permute-start(bf16[32,1152]{1,0:T(8,128)(2,1)S(1)} %get-tuple-element.22.refs_0_), channel_id=1, source_target_pairs={{0,1},{1,0},{2,3},{3,2},{4,5},{5,4},{6,7},{7,6},{8,9},{9,8},{10,11... | collective-permute-start | bytes 221192 | tf_op jit(solution)/shard_map/ppermute | solution.py:293
  5.8 5.7 %copy-start.9 = (bf16[32,32,128]{2,1,0:T(8,128)(2,1)S(1)}, bf16[32,32,128]{2,1,0:T(8,128)(2,1)}, u32[]{:S(2)}) copy-start(bf16[32,32,128]{2,1,0:T(8,128)(2,1)} %pair_ref.1) | copy-start | bytes 786436
  5.8 5.7 %copy-start.10 = (bf16[1024,128]{1,0:T(8,128)(2,1)S(1)}, bf16[1024,128]{1,0:T(8,128)(2,1)}, u32[]{:S(2)}) copy-start(bf16[1024,128]{1,0:T(8,128)(2,1)} %w_ref.5) | copy-start | bytes 786436
  5.8 5.7 %copy-start.12 = (bf16[66,128]{1,0:T(8,128)(2,1)S(1)}, bf16[66,128]{1,0:T(8,128)(2,1)}, u32[]{:S(2)}) copy-start(bf16[66,128]{1,0:T(8,128)(2,1)} %table_ref.1) | copy-start | bytes 50692
  5.8 5.7 %copy-start.17 = (s32[128]{0:T(128)S(1)}, s32[128]{0:T(128)}, u32[]{:S(2)}) copy-start(s32[128]{0:T(128)} %param.23) | copy-start | bytes 1540
  5.8 7.6 %collective-permute-start.2 = (bf16[2,32,1152]{2,1,0:T(8,128)(2,1)S(1)}, bf16[2,32,1152]{2,1,0:T(8,128)(2,1)S(1)}, u32[]{:S(2)}, u32[]{:S(2)}) collective-permute-start(bf16[2,32,1152]{2,1,0:T(8,128)(2,1)S(1)} %join.2._), channel_id=1, source_target_pairs={{0,4},{1,0},{2,12},{3,8},{4,5},{5,1},{6,13},{7,9},{8,6},{9,2},{10,... | collective-permute-start | bytes 442376 | tf_op jit(solution)/shard_map/ppermute | solution.py:299
  9.4 8.9 %collective-permute-start.1 = (bf16[2,32,1152]{2,1,0:T(8,128)(2,1)S(1)}, bf16[2,32,1152]{2,1,0:T(8,128)(2,1)S(1)}, u32[]{:S(2)}, u32[]{:S(2)}) collective-permute-start(bf16[2,32,1152]{2,1,0:T(8,128)(2,1)S(1)} %join.2._), channel_id=1, source_target_pairs={{0,0},{1,4},{2,8},{3,12},{4,1},{5,5},{6,9},{7,13},{8,2},{9,6},{10,... | collective-permute-start | bytes 442376 | tf_op jit(solution)/shard_map/ppermute | solution.py:299
  11.3 7.5 %collective-permute-start.4 = (bf16[2,32,1152]{2,1,0:T(8,128)(2,1)S(1)}, bf16[2,32,1152]{2,1,0:T(8,128)(2,1)S(1)}, u32[]{:S(2)}, u32[]{:S(2)}) collective-permute-start(bf16[2,32,1152]{2,1,0:T(8,128)(2,1)S(1)} %join.3.own_ref), channel_id=1, source_target_pairs={{0,2},{1,3},{2,0},{3,1},{4,6},{5,7},{6,4},{7,5},{8,10},{9,11},{10,... | collective-permute-start | bytes 442376 | tf_op jit(solution)/shard_map/ppermute | solution.py:288
  12.6 6.2 %copy-start = (bf16[128,640]{1,0:T(8,128)(2,1)S(1)}, bf16[128,640]{1,0:T(8,128)(2,1)}, u32[]{:S(2)}) copy-start(bf16[128,640]{1,0:T(8,128)(2,1)} %w_ref.7) | copy-start | bytes 491524
  12.6 6.2 %copy-start.6 = (f32[128]{0:T(128)S(1)}, f32[128]{0:T(128)}, u32[]{:S(2)}) copy-start(f32[128]{0:T(128)} %param.30) | copy-start | bytes 1540
  12.7 6.2 %copy-start.7 = (f32[128]{0:T(128)S(1)}, f32[128]{0:T(128)}, u32[]{:S(2)}) copy-start(f32[128]{0:T(128)} %param.31) | copy-start | bytes 1540
  21.9 12.8 %collective-permute-start.5 = (bf16[32,32,128]{2,1,0:T(8,128)(2,1)S(1)}, bf16[32,32,128]{2,1,0:T(8,128)(2,1)S(1)}, u32[]{:S(2)}, u32[]{:S(2)}) collective-permute-start(bf16[32,32,128]{2,1,0:T(8,128)(2,1)S(1)} %get-tuple-element.25), channel_id=1, source_target_pairs={{8,0},{13,1},{11,2},{14,3},{9,4},{12,5},{10,6},{15,7},{0,8},{5,9},... | collective-permute-start | bytes 786440 | tf_op jit(solution)/shard_map/ppermute | solution.py:313
  23.7 11.5 %collective-permute-start.7 = (bf16[32,32,128]{2,1,0:T(8,128)(2,1)S(1)}, bf16[32,32,128]{2,1,0:T(8,128)(2,1)S(1)}, u32[]{:S(2)}, u32[]{:S(2)}) collective-permute-start(bf16[32,32,128]{2,1,0:T(8,128)(2,1)S(1)} %get-tuple-element.26.refs_0_), channel_id=1, source_target_pairs={{0,1},{1,0},{2,3},{3,2},{4,5},{5,4},{6,7},{7,6},{8,9},{9,8},{10,11... | collective-permute-start | bytes 786440 | tf_op jit(solution)/shard_map/ppermute | solution.py:293
  23.7 16.6 %collective-permute-start.9 = (bf16[32,32,128]{2,1,0:T(8,128)(2,1)S(1)}, bf16[32,32,128]{2,1,0:T(8,128)(2,1)S(1)}, u32[]{:S(2)}, u32[]{:S(2)}) collective-permute-start(bf16[32,32,128]{2,1,0:T(8,128)(2,1)S(1)} %get-tuple-element.25), channel_id=1, source_target_pairs={{0,0},{4,1},{3,2},{7,3},{1,4},{5,5},{2,6},{6,7},{8,8},{12,9},{11,1... | collective-permute-start | bytes 786440 | tf_op jit(solution)/shard_map/ppermute | solution.py:313
  25.6 16.0 %collective-permute-start.8 = (bf16[32,32,128]{2,1,0:T(8,128)(2,1)S(1)}, bf16[32,32,128]{2,1,0:T(8,128)(2,1)S(1)}, u32[]{:S(2)}, u32[]{:S(2)}) collective-permute-start(bf16[32,32,128]{2,1,0:T(8,128)(2,1)S(1)} %get-tuple-element.25), channel_id=1, source_target_pairs={{1,0},{5,1},{2,2},{6,3},{0,4},{4,5},{3,6},{7,7},{9,8},{13,9},{10,1... | collective-permute-start | bytes 786440 | tf_op jit(solution)/shard_map/ppermute | solution.py:313
  34.7 8.8 %collective-permute-start.6 = (bf16[32,32,128]{2,1,0:T(8,128)(2,1)S(1)}, bf16[32,32,128]{2,1,0:T(8,128)(2,1)S(1)}, u32[]{:S(2)}, u32[]{:S(2)}) collective-permute-start(bf16[32,32,128]{2,1,0:T(8,128)(2,1)S(1)} %collective-permute-done.5.right_ref), channel_id=1, source_target_pairs={{0,4},{4,0},{8,12},{12,8},{1,5},{5,1},{9,13},{13,9},{2,6},{6,2},{1... | collective-permute-start | bytes 786440 | tf_op jit(solution)/shard_map/ppermute | solution.py:317
  36.5 9.1 %copy-start.1 = (bf16[128,128]{1,0:T(8,128)(2,1)S(1)}, bf16[128,128]{1,0:T(8,128)(2,1)}, u32[]{:S(2)}) copy-start(bf16[128,128]{1,0:T(8,128)(2,1)} %w_ref.9) | copy-start | bytes 98308
  36.5 9.1 %copy-start.2 = (f32[128]{0:T(128)S(1)}, f32[128]{0:T(128)}, u32[]{:S(2)}) copy-start(f32[128]{0:T(128)} %param.34) | copy-start | bytes 1540
  36.5 9.1 %copy-start.3 = (f32[128]{0:T(128)S(1)}, f32[128]{0:T(128)}, u32[]{:S(2)}) copy-start(f32[128]{0:T(128)} %param.35) | copy-start | bytes 1540
  36.5 9.1 %copy-start.4 = (f32[128]{0:T(128)S(1)}, f32[128]{0:T(128)}, u32[]{:S(2)}) copy-start(f32[128]{0:T(128)} %param.37) | copy-start | bytes 1540
  44.2 1.4 %collective-permute-start.11 = (bf16[512,128]{1,0:T(8,128)(2,1)S(1)}, bf16[512,128]{1,0:T(8,128)(2,1)S(1)}, u32[]{:S(2)}, u32[]{:S(2)}) collective-permute-start(bf16[512,128]{1,0:T(8,128)(2,1)S(1)} %get-tuple-element.32), channel_id=1, source_target_pairs={{0,2},{1,3},{2,0},{3,1},{4,6},{5,7},{6,4},{7,5},{8,10},{9,11},{10,... | collective-permute-start | bytes 393224 | tf_op jit(solution)/shard_map/ppermute | solution.py:288
  45.3 1.4 %collective-permute-start.10 = (bf16[512,128]{1,0:T(8,128)(2,1)S(1)}, bf16[512,128]{1,0:T(8,128)(2,1)S(1)}, u32[]{:S(2)}, u32[]{:S(2)}) collective-permute-start(bf16[512,128]{1,0:T(8,128)(2,1)S(1)} %get-tuple-element.29), channel_id=1, source_target_pairs={{0,2},{1,3},{2,0},{3,1},{4,6},{5,7},{6,4},{7,5},{8,10},{9,11},{10,... | collective-permute-start | bytes 393224 | tf_op jit(solution)/shard_map/ppermute | solution.py:288

commit v14 on v13

--- a/solution.py
+++ b/solution.py
@@ -77,6 +77,10 @@
         ref[:, width:] = live_tile.astype(BF16)
 
 
+def carry_kernel(in_ref, out_ref):
+    out_ref[...] = in_ref[...]
+
+
 def join_kernel(count, *refs):
     for n in range(count):
         refs[-1][n] = refs[n][...]
@@ -143,7 +147,7 @@
 
 def edges_kernel(turned_ref, live_ref, own_ref, swapped_ref, base_ref, block_ref, res_ref,
                  gain_ref, shift_ref, w_ref, bias_ref,
-                 updated_ref, left_ref, right_ref, nscr, lall, oscr, escr):
+                 updated_ref, left_ref, right_ref, low_ref, high_ref, nscr, lall, oscr, escr):
     rows, cols, channels = base_ref.shape
     chips, seqs = own_ref.shape[:2]
     half = block_ref.shape[0] // LANES
@@ -189,8 +193,11 @@
             at = slice(ii * cols, (ii + 1) * cols)
             left_ref[i0 + ii] = (left_edge[at] * here).astype(BF16)
             escr[(i0 + ii) * cols:(i0 + ii + 1) * cols, :] = right_edge[at] * here
+    part = cols // 2
     for k in range(cols):
-        right_ref[k] = escr[pl.ds(k, rows, stride=cols), :].astype(BF16)
+        value = escr[pl.ds(k, rows, stride=cols), :].astype(BF16)
+        right_ref[k] = value
+        (low_ref if k < part else high_ref)[k % part] = value
 
 
 def gate_kernel(normed_ref, w_ref, bias_ref, gate_ref):
@@ -210,8 +217,9 @@
     return block // chips, block % chips
 
 
-def add_block(panel_ref, chip, rscr, cols, first, before, store):
+def add_block(panel_ref, chip, rscr, cols, skip, first, before, store):
     rows, depth, channels = store.shape[0] // cols, rscr.shape[0] // cols, rscr.shape[1]
+    whole = panel_ref.shape[1] // cols
     block = 8
     tiles = cols // 8
 
@@ -226,7 +234,7 @@
         for k in range(depth):
             column = [rscr[k * cols + t * 8:k * cols + t * 8 + 8, :] for t in range(tiles)]
             for b in range(block):
-                row = panel_ref[chip, pl.ds((first + at * block + b) * depth + k, 1), :]
+                row = panel_ref[chip, pl.ds((first + at * block + b) * whole + skip + k, 1), :]
                 for t in range(tiles):
                     sums[b][t] = sums[b][t] + row * column[t]
         for b in range(block):
@@ -237,17 +245,18 @@
     lax.fori_loop(0, rows // block, rows_body, 0)
 
 
-def step_kernel(step, chips, first, fresh, right_ref, panel_ref, *refs):
+def step_kernel(step, chips, skip, first, fresh, right_ref, panel_ref, *refs):
     out_ref, rscr = refs[-2:]
     z, core, x = [lax.axis_index(axis) for axis in GROUP]
     chip = source_of(z, core, x, step, chips)[1]
     rscr[...] = right_ref[...].astype(F32).reshape(rscr.shape)
-    add_block(panel_ref, chip, rscr, right_ref.shape[1], first, None if fresh else refs[0], out_ref)
-
-
-def last_kernel(step, chips, first, right_ref, panel_ref, far_ref, near_ref, own_ref, other_ref,
+    add_block(
+        panel_ref, chip, rscr, right_ref.shape[1], skip, first, None if fresh else refs[0], out_ref)
+
+
+def last_kernel(step, chips, skip, first, right_ref, panel_ref, far_ref, near_ref, own_ref, other_ref,
                 rscr, acc):
-    step_kernel(step, chips, first, False, right_ref, panel_ref, far_ref, acc, rscr)
+    step_kernel(step, chips, skip, first, False, right_ref, panel_ref, far_ref, acc, rscr)
     mine = lax.axis_index("resi") // chips == lax.axis_index("resj")
     at = pl.ds(first * right_ref.shape[1], acc.shape[0])
 
@@ -264,10 +273,14 @@
 
 def final_kernel(first, own_ref, other_ref, updated_ref, gate_ref, gain_ref, shift_ref, w_ref, bias_ref,
                  *refs):
-    out_hbm, vscr, sems = refs[-3:]
-    rows, cols, channels = vscr.shape
+    if first:
+        before_ref, out_hbm, value_ref, sems = refs
+        moves = [pltpu.make_async_copy(before_ref, out_hbm.at[:first], sems.at[0])]
+        moves[0].start()
+    else:
+        value_ref, = refs
+    rows, cols, channels = value_ref.shape
     chunk = 8
-    moves = []
     for i0 in range(0, rows, chunk):
         at = slice(i0 * cols, (i0 + chunk) * cols)
         here = slice((first + i0) * cols, (first + i0 + chunk) * cols)
@@ -276,12 +289,15 @@
         result = dot(normed, w_ref[...]) + bias_ref[...]
         updated = updated_ref[first + i0:first + i0 + chunk].reshape(chunk * cols, channels).astype(F32)
         value = updated + gate_ref[here, :] * result
-        vscr[i0:i0 + chunk] = value.astype(BF16).reshape(chunk, cols, channels)
-        moves.append(pltpu.make_async_copy(
-            vscr.at[i0:i0 + chunk], out_hbm.at[first + i0:first + i0 + chunk], sems.at[i0 // chunk]))
-        moves[-1].start()
-    for move in moves:
-        move.wait()
+        value_ref[i0:i0 + chunk] = value.astype(BF16).reshape(chunk, cols, channels)
+        if first:
+            moves.append(pltpu.make_async_copy(
+                value_ref.at[i0:i0 + chunk], out_hbm.at[first + i0:first + i0 + chunk],
+                sems.at[1 + i0 // chunk]))
+            moves[-1].start()
+    if first:
+        for move in moves:
+            move.wait()
 
 
 def swap_cores(block, count):
@@ -317,17 +333,16 @@
     return lax.ppermute(block, "resi", [(z, z ^ 1) for z in range(count)])
 
 
-def call(kernel, outs, scratch, args, flops=0, aliases=None, hbm=False, name=None):
+def call(kernel, outs, scratch, args, flops=0, hbm=False, name=None):
     vmem = pl.BlockSpec(memory_space=pltpu.VMEM)
-    result = pl.BlockSpec(memory_space=pl.ANY) if hbm else vmem
     size = sum(a.size * a.dtype.itemsize for a in args)
     return pl.pallas_call(
         kernel,
         out_shape=outs,
-        in_specs=[result if n in (aliases or {}) else vmem for n in range(len(args))],
-        out_specs=[vmem] * len(outs) if isinstance(outs, list) else result,
+        in_specs=[vmem] * len(args),
+        out_specs=[vmem] * len(outs) if isinstance(outs, list) else (
+            pl.BlockSpec(memory_space=pl.ANY) if hbm else vmem),
         scratch_shapes=scratch,
-        input_output_aliases=aliases or {},
         compiler_params=pltpu.CompilerParams(vmem_limit_bytes=40 * MIB),
         cost_estimate=pl.CostEstimate(flops=flops, bytes_accessed=size, transcendentals=0),
         name=name,
@@ -395,10 +410,11 @@
         [pltpu.VMEM((count,) + pack.shape, BF16),
          pltpu.VMEM((count * seqs // LANES, width, LANES), F32)],
         rights, flops=1 << 36, name="turn")
-    updated, left_edge, right_edge, normed_pair = call(
+    updated, left_edge, right_edge, low_edge, high_edge, normed_pair = call(
         edges_kernel,
         [shape((rows, cols, channels), BF16), shape((rows, cols, channels), BF16),
-         shape((cols, rows, channels), BF16), shape((rows * cols, channels), BF16)],
+         shape((cols, rows, channels), BF16), shape((cols // 2, rows, channels), BF16),
+         shape((cols // 2, rows, channels), BF16), shape((rows * cols, channels), BF16)],
         [pltpu.VMEM((count,) + pack.shape, BF16),
          pltpu.VMEM((rows // per * cols, half * LANES), BF16),
          pltpu.VMEM((rows * cols, channels), F32)],
@@ -406,42 +422,50 @@
             base, block, residue, flat(pair_norm_gain), flat(pair_norm_bias),
             triangle_projection_weights, flat(triangle_projection_biases)],
         name="edges")
-    right_edges = [send_same_core(right_edge, count, chips, step) for step in range(chips)]
-    for step in range(chips, count, 2):
-        block_far = send_same_core(right_edge, count, chips, step)
-        right_edges += [block_far, pass_on(block_far, count)]
+    near_parts = [
+        (step, 0, send_same_core(right_edge, count, chips, step)) for step in range(chips)]
+    far_parts = [
+        (step, skip, send_same_core(half_edge, count, chips, step))
+        for step in range(chips, count, 2) for skip, half_edge in ((0, low_edge), (cols // 2, high_edge))]
+    for step, skip, block_far in far_parts[:]:
+        carried = call(carry_kernel, shape(block_far.shape, BF16), [], [block_far], flops=1 << 29,
+                       name="carry")
+        far_parts.append((step + 1, skip, pass_on(carried, count)))
     left_edges = [left_edge] + send_chips(left_edge, chips)
     gate = call(gate_kernel, shape((rows * cols, channels), F32), [],
                 [normed_pair, triangle_projection_weights, flat(triangle_projection_biases)],
                 flops=1 << 30, name="gate")
     block_sums = shape((rows * cols, channels), F32)
-    scratch = pltpu.VMEM((rows * cols, channels), F32)
     panel = call(panel_kernel, shape((chips, rows * cols, channels), F32), [],
-                 left_edges + [gate], name="panel")
+                 left_edges + [gate], flops=1 << 28, name="panel")
     near, far = [], []
-    for step in range(count - 1):
-        sums = near if step < chips else far
-        sums[:] = [call(
-            functools.partial(step_kernel, step, chips, 0, not sums), block_sums, [scratch],
-            [right_edges[step], panel] + sums, name="triangle")]
+    for sums, parts in ((far, far_parts[:-1]), (near, near_parts)):
+        for step, skip, right_block in parts:
+            sums[:] = [call(
+                functools.partial(step_kernel, step, chips, skip, 0, not sums), block_sums,
+                [pltpu.VMEM((right_block.shape[0] * rows, channels), F32)],
+                [right_block, panel] + sums, name="triangle")]
+    step, skip, right_block = far_parts[-1]
     part = rows // 2
     own_sums, other_sums, result = [], [], []
     for first in (0, part):
         own, half_sums = call(
-            functools.partial(last_kernel, count - 1, chips, first),
+            functools.partial(last_kernel, step, chips, skip, first),
             [shape((part * cols, channels), F32), shape((part * cols, channels), BF16)],
-            [scratch, pltpu.VMEM((part * cols, channels), F32)],
-            [right_edges[-1], panel] + far + near, flops=1 << 28, name="last")
+            [pltpu.VMEM((right_block.shape[0] * rows, channels), F32),
+             pltpu.VMEM((part * cols, channels), F32)],
+            [right_block, panel] + far + near, flops=1 << 28, name="last")
         own_sums.append(own)
         other_sums.append(swap_cores(half_sums, count))
     for n, first in enumerate((0, part)):
         args = [own_sums[n], other_sums[n], updated, gate, flat(triangle_sum_norm_gain),
                 flat(triangle_sum_norm_bias), triangle_output_weight, flat(outer_pair_bias)]
+        half_shape = (part, cols, channels)
         result = [call(
-            functools.partial(final_kernel, first), shape((rows, cols, channels), BF16),
-            [pltpu.VMEM((part, cols, channels), BF16), pltpu.SemaphoreType.DMA((part // 8,))],
-            args + result, flops=1 << 28, aliases={len(args): 0} if n else None, hbm=True,
-            name="final")]
+            functools.partial(final_kernel, first),
+            shape((rows, cols, channels) if n else half_shape, BF16),
+            [pltpu.VMEM(half_shape, BF16), pltpu.SemaphoreType.DMA((1 + part // 8,))] if n else [],
+            args + result, flops=1 << 28, hbm=n == 1, name="final")]
     return result[0]
 
 

time: 48.3 us -> 48.5 us (level)
  starting transfers between devices: 13.5 us -> 16.6 us
  waiting for transfers between devices: 18.7 us -> 16.5 us
  Pallas kernels: 13.7 us -> 13.1 us
    ppermute x3 -> x4, waiting for transfers between devices: 12.2 us -> 5.63 us  [send_same_core(): return lax.ppermute(block, GROUP, pairs)]
    ppermute x2, waiting for transfers between devices: 0.01 us -> 4.51 us  [send_chips(): lax.ppermute(block, 'seq', [(x, x ^ m) for x in range(chips)])]
    ppermute x3 -> x4, starting transfers between devices: 4.31 us -> 6.17 us  [send_same_core(): return lax.ppermute(block, GROUP, pairs)]
    ppermute x1 -> x2, starting transfers between devices: 0.16 us -> 1.41 us  [pass_on(): return lax.ppermute(block, 'resi', [(z, z ^ 1) for z in range(count)])]
    pallas_call x16 -> x20, Pallas kernels: 13.7 us -> 13.1 us  [call(): pl.pallas_call(kernel, out_shape=outs, in_specs=[vmem] * len(args), out_s...]
    ppermute x1 -> x2, waiting for transfers between devices: 0.66 us -> 0.01 us  [pass_on(): return lax.ppermute(block, 'resi', [(z, z ^ 1) for z in range(count)])]
  transfers between devices with their start and end apart: 12 -> 14, of which waited for: 7 -> 8; matrix products, arithmetic and copies ran while one was open for 0% -> 0% of each run, Pallas kernels for 16% -> 15%
where the time goes in v14:
time: 48.5 us; the launch traced here: 48 us
  starting transfers between devices  16.6 us (34%)
  waiting for transfers between devices  16.5 us (34%)
  Pallas kernels  13.1 us (27%)
  local copies, waits for them, and re-layouts  1.48 us (3%)
    pallas_call x20, Pallas kernels, call(): pl.pallas_call(kernel, out_shape=outs, in_specs=[vmem] * len(args), out_s...  13.1 us
    ppermute x4, starting transfers between devices, send_same_core(): return lax.ppermute(block, GROUP, pairs)  6.17 us
    ppermute x2, waiting for transfers between devices, send_turned(): lax.ppermute(block, GROUP, [(z * count + p, (p ^ m) * count + z) for z in...  5.66 us
    ppermute x4, waiting for transfers between devices, send_same_core(): return lax.ppermute(block, GROUP, pairs)  5.63 us
    ppermute x2, starting transfers between devices, send_turned(): lax.ppermute(block, GROUP, [(z * count + p, (p ^ m) * count + z) for z in...  5.51 us
    ppermute x2, waiting for transfers between devices, send_chips(): lax.ppermute(block, 'seq', [(x, x ^ m) for x in range(chips)])  4.51 us
    ppermute x2, starting transfers between devices, send_chips(): lax.ppermute(block, 'seq', [(x, x ^ m) for x in range(chips)])  2.68 us
    unnamed x38, local copies, waits for them, and re-layouts  1.48 us
  transfers between devices with their start and end apart: 14, of which 8 were waited for; matrix products, arithmetic and copies ran while one was open for 0% of the time, Pallas kernels for 15%

profile of v14, /device:TPU:1, one launch (start us, length us, event | category | flops | bytes accessed | tf_op | source)
XLA Modules:
  0.0 48.0 jit_solution(15444771913195348162)
XLA Ops:
  0.0 1.1 %copy-done.8 = bf16[32,32,256]{2,1,0:T(8,128)(2,1)S(1)} copy-done((bf16[32,32,256]{2,1,0:T(8,128)(2,1)S(1)}, bf16[32,32,256]{2,1,0:T(8,128)(2,1)}, u32[]{:S(2)}) %copy-start.8) | copy-done | bytes 524312
  1.1 0.4 norm.1.x_ref
  1.5 0.3 copy-done.11
  1.8 1.1 %pack.1 = (bf16[32,1152]{1,0:T(8,128)(2,1)S(1)}, bf16[32,1152]{1,0:T(8,128)(2,1)S(1)}) custom-call(f32[1024,256]{1,0:T(8,128)S(1)} %norm.1.x_ref, s32[32,32]{1,0:T(8,128)S(1)} %copy-done.13, s32[1,128]{1,0:T(1,128)S(1)} %bitcast.17, f32[1,256]{1,0:T(1,128)S(1)} %bitcast.22, f32[1,256]{1,0:T(1,128)S(1)} %bitcast.23, bf16[64,256]{1,0:T(8,128)(2,1)S(1)} %bitcast.21, ...), custom_call_target="tpu_custom_call" | custom-call | flops 1073741824 | bytes 1088256 | tf_op jit(solution)/shard_map/pack/pallas_call | solution.py:339
  3.0 2.7 %collective-permute-start.3 = (bf16[32,1152]{1,0:T(8,128)(2,1)S(1)}, bf16[32,1152]{1,0:T(8,128)(2,1)S(1)}, u32[]{:S(2)}, u32[]{:S(2)}) collective-permute-start(bf16[32,1152]{1,0:T(8,128)(2,1)S(1)} %get-tuple-element.24.refs_0_), channel_id=1, source_target_pairs={{0,1},{1,0},{2,3},{3,2},{4,5},{5,4},{6,7},{7,6},{8,9},{9,8},{10,11... | collective-permute-start | bytes 221192 | tf_op jit(solution)/shard_map/ppermute | solution.py:309
  5.8 3.6 %collective-permute-start.2 = (bf16[2,32,1152]{2,1,0:T(8,128)(2,1)S(1)}, bf16[2,32,1152]{2,1,0:T(8,128)(2,1)S(1)}, u32[]{:S(2)}, u32[]{:S(2)}) collective-permute-start(bf16[2,32,1152]{2,1,0:T(8,128)(2,1)S(1)} %join.2._), channel_id=1, source_target_pairs={{0,4},{1,0},{2,12},{3,8},{4,5},{5,1},{6,13},{7,9},{8,6},{9,2},{10,... | collective-permute-start | bytes 442376 | tf_op jit(solution)/shard_map/ppermute | solution.py:315
  9.4 1.9 %collective-permute-start.1 = (bf16[2,32,1152]{2,1,0:T(8,128)(2,1)S(1)}, bf16[2,32,1152]{2,1,0:T(8,128)(2,1)S(1)}, u32[]{:S(2)}, u32[]{:S(2)}) collective-permute-start(bf16[2,32,1152]{2,1,0:T(8,128)(2,1)S(1)} %join.2._), channel_id=1, source_target_pairs={{0,0},{1,4},{2,8},{3,12},{4,1},{5,5},{6,9},{7,13},{8,2},{9,6},{10,... | collective-permute-start | bytes 442376 | tf_op jit(solution)/shard_map/ppermute | solution.py:315
  11.5 1.2 %base.1 = (f32[32,32,128]{2,1,0:T(8,128)S(1)}, bf16[4096,512]{1,0:T(8,128)(2,1)S(1)}) custom-call(bf16[32,32,128]{2,1,0:T(8,128)(2,1)S(1)} %copy-done.9, bf16[66,128]{1,0:T(8,128)(2,1)S(1)} %copy-done.12, s32[1,128]{1,0:T(1,128)S(1)} %bitcast.25, bf16[1024,128]{1,0:T(8,128)(2,1)S(1)} %copy-done.10, bf16[2,32,1152]{2,1,0:T(8,128)(2,1)S(1)} %join.2._), custom_call_target="tpu_custom_call" | custom-call | flops 1073741824 | bytes 689152 | tf_op jit(solution)/shard_map/base/pallas_call | solution.py:339
  12.7 0.8 %collective-permute-done.2.refs_1_ = bf16[2,32,1152]{2,1,0:T(8,128)(2,1)S(1)} collective-permute-done((bf16[2,32,1152]{2,1,0:T(8,128)(2,1)S(1)}, bf16[2,32,1152]{2,1,0:T(8,128)(2,1)S(1)}, u32[]{:S(2)}, u32[]{:S(2)}) %collective-permute-start.2) | collective-permute-done | bytes 147488 | tf_op jit(solution)/shard_map/ppermute | solution.py:315
  13.4 4.9 %collective-permute-done.1.refs_0_ = bf16[2,32,1152]{2,1,0:T(8,128)(2,1)S(1)} collective-permute-done((bf16[2,32,1152]{2,1,0:T(8,128)(2,1)S(1)}, bf16[2,32,1152]{2,1,0:T(8,128)(2,1)S(1)}, u32[]{:S(2)}, u32[]{:S(2)}) %collective-permute-start.1) | collective-permute-done | bytes 147488 | tf_op jit(solution)/shard_map/ppermute | solution.py:315
  18.3 0.5 turn.1
  18.8 3.1 %edges.1 = (bf16[32,32,128]{2,1,0:T(8,128)(2,1)S(1)}, bf16[32,32,128]{2,1,0:T(8,128)(2,1)S(1)}, bf16[32,32,128]{2,1,0:T(8,128)(2,1)S(1)}, bf16[16,32,128]{2,1,0:...) custom-call(bf16[1024,128]{1,0:T(8,128)(2,1)S(1)} %get-tuple-element.22.turned_ref, ...), custom_call_target="tpu_custom_call" | custom-call | bytes 5451776 | tf_op jit(solution)/shard_map/edges/pallas_call | solution.py:339
  21.9 1.7 %collective-permute-start.8 = (bf16[16,32,128]{2,1,0:T(8,128)(2,1)S(1)}, bf16[16,32,128]{2,1,0:T(8,128)(2,1)S(1)}, u32[]{:S(2)}, u32[]{:S(2)}) collective-permute-start(bf16[16,32,128]{2,1,0:T(8,128)(2,1)S(1)} %get-tuple-element.30), channel_id=1, source_target_pairs={{8,0},{13,1},{11,2},{14,3},{9,4},{12,5},{10,6},{15,7},{0,8},{5,9},... | collective-permute-start | bytes 393224 | tf_op jit(solution)/shard_map/ppermute | solution.py:329
  23.7 1.8 %collective-permute-start.5 = (bf16[16,32,128]{2,1,0:T(8,128)(2,1)S(1)}, bf16[16,32,128]{2,1,0:T(8,128)(2,1)S(1)}, u32[]{:S(2)}, u32[]{:S(2)}) collective-permute-start(bf16[16,32,128]{2,1,0:T(8,128)(2,1)S(1)} %get-tuple-element.27), channel_id=1, source_target_pairs={{8,0},{13,1},{11,2},{14,3},{9,4},{12,5},{10,6},{15,7},{0,8},{5,9},... | collective-permute-start | bytes 393224 | tf_op jit(solution)/shard_map/ppermute | solution.py:329
  25.5 2.0 %collective-permute-start.11 = (bf16[32,32,128]{2,1,0:T(8,128)(2,1)S(1)}, bf16[32,32,128]{2,1,0:T(8,128)(2,1)S(1)}, u32[]{:S(2)}, u32[]{:S(2)}) collective-permute-start(bf16[32,32,128]{2,1,0:T(8,128)(2,1)S(1)} %get-tuple-element.31), channel_id=1, source_target_pairs={{0,0},{4,1},{3,2},{7,3},{1,4},{5,5},{2,6},{6,7},{8,8},{12,9},{11,1... | collective-permute-start | bytes 786440 | tf_op jit(solution)/shard_map/ppermute | solution.py:329
  27.4 0.7 %collective-permute-start.10 = (bf16[32,32,128]{2,1,0:T(8,128)(2,1)S(1)}, bf16[32,32,128]{2,1,0:T(8,128)(2,1)S(1)}, u32[]{:S(2)}, u32[]{:S(2)}) collective-permute-start(bf16[32,32,128]{2,1,0:T(8,128)(2,1)S(1)} %get-tuple-element.31), channel_id=1, source_target_pairs={{1,0},{5,1},{2,2},{6,3},{0,4},{4,5},{3,6},{7,7},{9,8},{13,9},{10,1... | collective-permute-start | bytes 786440 | tf_op jit(solution)/shard_map/ppermute | solution.py:329
  28.1 3.8 %collective-permute-done.8.in_ref.right_ref = bf16[16,32,128]{2,1,0:T(8,128)(2,1)S(1)} collective-permute-done((bf16[16,32,128]{2,1,0:T(8,128)(2,1)S(1)}, bf16[16,32,128]{2,1,0:T(8,128)(2,1)S(1)}, u32[]{:S(2)}, u32[]{:S(2)}) %collective-permute-start.8) | collective-permute-done | bytes 131104 | tf_op jit(solution)/shard_map/ppermute | solution.py:329
  31.9 1.2 %collective-permute-start.9 = (bf16[16,32,128]{2,1,0:T(8,128)(2,1)S(1)}, bf16[16,32,128]{2,1,0:T(8,128)(2,1)S(1)}, u32[]{:S(2)}, u32[]{:S(2)}) collective-permute-start(bf16[16,32,128]{2,1,0:T(8,128)(2,1)S(1)} %carry.3), channel_id=1, source_target_pairs={{0,4},{4,0},{8,12},{12,8},{1,5},{5,1},{9,13},{13,9},{2,6},{6,2},{1... | collective-permute-start | bytes 393224 | tf_op jit(solution)/shard_map/ppermute | solution.py:333
  33.1 1.6 %collective-permute-done.5.in_ref.right_ref = bf16[16,32,128]{2,1,0:T(8,128)(2,1)S(1)} collective-permute-done((bf16[16,32,128]{2,1,0:T(8,128)(2,1)S(1)}, bf16[16,32,128]{2,1,0:T(8,128)(2,1)S(1)}, u32[]{:S(2)}, u32[]{:S(2)}) %collective-permute-start.5) | collective-permute-done | bytes 131104 | tf_op jit(solution)/shard_map/ppermute | solution.py:329
  35.2 4.5 %collective-permute-done.7.refs_1_ = bf16[32,32,128]{2,1,0:T(8,128)(2,1)S(1)} collective-permute-done((bf16[32,32,128]{2,1,0:T(8,128)(2,1)S(1)}, bf16[32,32,128]{2,1,0:T(8,128)(2,1)S(1)}, u32[]{:S(2)}, u32[]{:S(2)}) %collective-permute-start.7) | collective-permute-done | bytes 262176 | tf_op jit(solution)/shard_map/ppermute | solution.py:309
  39.8 0.6 %triangle.5.refs_0_ = f32[1024,128]{1,0:T(8,128)S(1)} custom-call(bf16[16,32,128]{2,1,0:T(8,128)(2,1)S(1)} %collective-permute-done.8.in_ref.right_ref, f32[2,1024,128]{2,1,0:T(8,128)S(1)} %panel.1.panel_ref), custom_call_target="tpu_custom_call" | custom-call | bytes 1179648 | tf_op jit(solution)/shard_map/triangle/pallas_call | solution.py:339
  40.6 1.3 %triangle.8.refs_0_ = f32[1024,128]{1,0:T(8,128)S(1)} custom-call(bf16[32,32,128]{2,1,0:T(8,128)(2,1)S(1)} %collective-permute-done.11.right_ref, f32[2,1024,128]{2,1,0:T(8,128)S(1)} %panel.1.panel_ref), custom_call_target="tpu_custom_call" | custom-call | bytes 1310720 | tf_op jit(solution)/shard_map/triangle/pallas_call | solution.py:339
  41.9 0.6 %triangle.6.refs_0_ = f32[1024,128]{1,0:T(8,128)S(1)} custom-call(bf16[16,32,128]{2,1,0:T(8,128)(2,1)S(1)} %collective-permute-done.5.in_ref.right_ref, f32[2,1024,128]{2,1,0:T(8,128)S(1)} %panel.1.panel_ref, f32[1024,128]{1,0:T(8,128)S(1)} %triangle.5.refs_0_), custom_call_target="tpu_custom_call" | custom-call | bytes 1703936 | tf_op jit(solution)/shard_map/triangle/pallas_call | solution.py:339
  42.6 1.3 %triangle.9.near_ref = f32[1024,128]{1,0:T(8,128)S(1)} custom-call(bf16[32,32,128]{2,1,0:T(8,128)(2,1)S(1)} %collective-permute-done.10.right_ref, f32[2,1024,128]{2,1,0:T(8,128)S(1)} %panel.1.panel_ref, f32[1024,128]{1,0:T(8,128)S(1)} %triangle.8.refs_0_), custom_call_target="tpu_custom_call" | custom-call | bytes 1835008 | tf_op jit(solution)/shard_map/triangle/pallas_call | solution.py:339
  43.9 0.6 %triangle.7.far_ref = f32[1024,128]{1,0:T(8,128)S(1)} custom-call(bf16[16,32,128]{2,1,0:T(8,128)(2,1)S(1)} %collective-permute-done.9.right_ref, f32[2,1024,128]{2,1,0:T(8,128)S(1)} %panel.1.panel_ref, f32[1024,128]{1,0:T(8,128)S(1)} %triangle.6.refs_0_), custom_call_target="tpu_custom_call" | custom-call | bytes 1703936 | tf_op jit(solution)/shard_map/triangle/pallas_call | solution.py:339
  44.5 0.4 last.3
  44.9 0.3 collective-permute-start.13
  45.2 0.4 last.2
  45.5 0.4 collective-permute-start.12
  45.9 0.4 collective-permute-done.13.other_ref
  46.3 0.4 final.2.refs_0_
  47.0 1.0 %final.3 = bf16[32,32,128]{2,1,0:T(8,128)(2,1)} custom-call(f32[512,128]{1,0:T(8,128)S(1)} %get-tuple-element.32.own_ref, bf16[512,128]{1,0:T(8,128)(2,1)S(1)} %collective-permute-done.12.other_ref, bf16[32,32,128]{2,1,0:T(8,128)(2,1)S(1)} %get-tuple-element.34.updated_ref, f32[1024,128]{1,0:T(8,128)S(1)} %gate.1.refs_2_.gate_ref, f32[1,128]{1,0:T(1,128)S(1)} %bitcast.12, ...), custom_call_target="tpu_custom_call" | custom-call | flops 268435456 | bytes 1345024 | tf_op jit(solution)/shard_map/final/pallas_call | solution.py:339
  (55 shorter events, 1.3 us)
Async XLA Ops:
  0.0 1.5 %copy-start.5 = (s32[128]{0:T(128)S(1)}, s32[128]{0:T(128)}, u32[]{:S(2)}) copy-start(s32[128]{0:T(128)} %param.22) | copy-start | bytes 1540
  0.0 1.1 %copy-start.8 = (bf16[32,32,256]{2,1,0:T(8,128)(2,1)S(1)}, bf16[32,32,256]{2,1,0:T(8,128)(2,1)}, u32[]{:S(2)}) copy-start(bf16[32,32,256]{2,1,0:T(8,128)(2,1)} %x_ref.1) | copy-start | bytes 1572868
  1.1 0.8 %copy-start.11 = (bf16[256,64]{0,1:T(8,128)(2,1)S(1)}, bf16[256,64]{0,1:T(8,128)(2,1)}, u32[]{:S(2)}) copy-start(bf16[256,64]{0,1:T(8,128)(2,1)} %param.26) | copy-start | bytes 98308
  1.1 0.8 %copy-start.13 = (s32[32,32]{1,0:T(8,128)S(1)}, s32[32,32]{1,0:T(8,128)}, u32[]{:S(2)}) copy-start(s32[32,32]{1,0:T(8,128)} %mask_ref.1) | copy-start | bytes 12292
  1.1 0.8 %copy-start.14 = (f32[256]{0:T(256)S(1)}, f32[256]{0:T(256)}, u32[]{:S(2)}) copy-start(f32[256]{0:T(256)} %param.24) | copy-start | bytes 3076
  1.1 0.8 %copy-start.15 = (f32[256]{0:T(256)S(1)}, f32[256]{0:T(256)}, u32[]{:S(2)}) copy-start(f32[256]{0:T(256)} %param.25) | copy-start | bytes 3076
  1.1 4.6 %copy-start.18 = (f32[640]{0:T(1024)S(1)}, f32[640]{0:T(1024)}, u32[]{:S(2)}) copy-start(f32[640]{0:T(1024)} %param.33) | copy-start | bytes 7684
  2.9 2.8 %collective-permute-start = (bf16[32,1152]{1,0:T(8,128)(2,1)S(1)}, bf16[32,1152]{1,0:T(8,128)(2,1)S(1)}, u32[]{:S(2)}, u32[]{:S(2)}) collective-permute-start(bf16[32,1152]{1,0:T(8,128)(2,1)S(1)} %get-tuple-element.21.refs_0_), channel_id=1, source_target_pairs={{0,2},{1,3},{2,0},{3,1},{4,6},{5,7},{6,4},{7,5},{8,10},{9,11},{10,... | collective-permute-start | bytes 221192 | tf_op jit(solution)/shard_map/ppermute | solution.py:304
  3.0 8.3 %collective-permute-start.3 = (bf16[32,1152]{1,0:T(8,128)(2,1)S(1)}, bf16[32,1152]{1,0:T(8,128)(2,1)S(1)}, u32[]{:S(2)}, u32[]{:S(2)}) collective-permute-start(bf16[32,1152]{1,0:T(8,128)(2,1)S(1)} %get-tuple-element.24.refs_0_), channel_id=1, source_target_pairs={{0,1},{1,0},{2,3},{3,2},{4,5},{5,4},{6,7},{7,6},{8,9},{9,8},{10,11... | collective-permute-start | bytes 221192 | tf_op jit(solution)/shard_map/ppermute | solution.py:309
  5.8 5.7 %copy-start.9 = (bf16[32,32,128]{2,1,0:T(8,128)(2,1)S(1)}, bf16[32,32,128]{2,1,0:T(8,128)(2,1)}, u32[]{:S(2)}) copy-start(bf16[32,32,128]{2,1,0:T(8,128)(2,1)} %pair_ref.1) | copy-start | bytes 786436
  5.8 5.7 %copy-start.10 = (bf16[1024,128]{1,0:T(8,128)(2,1)S(1)}, bf16[1024,128]{1,0:T(8,128)(2,1)}, u32[]{:S(2)}) copy-start(bf16[1024,128]{1,0:T(8,128)(2,1)} %w_ref.5) | copy-start | bytes 786436
  5.8 5.7 %copy-start.12 = (bf16[66,128]{1,0:T(8,128)(2,1)S(1)}, bf16[66,128]{1,0:T(8,128)(2,1)}, u32[]{:S(2)}) copy-start(bf16[66,128]{1,0:T(8,128)(2,1)} %table_ref.1) | copy-start | bytes 50692
  5.8 5.7 %copy-start.17 = (s32[128]{0:T(128)S(1)}, s32[128]{0:T(128)}, u32[]{:S(2)}) copy-start(s32[128]{0:T(128)} %param.23) | copy-start | bytes 1540
  5.8 7.6 %collective-permute-start.2 = (bf16[2,32,1152]{2,1,0:T(8,128)(2,1)S(1)}, bf16[2,32,1152]{2,1,0:T(8,128)(2,1)S(1)}, u32[]{:S(2)}, u32[]{:S(2)}) collective-permute-start(bf16[2,32,1152]{2,1,0:T(8,128)(2,1)S(1)} %join.2._), channel_id=1, source_target_pairs={{0,4},{1,0},{2,12},{3,8},{4,5},{5,1},{6,13},{7,9},{8,6},{9,2},{10,... | collective-permute-start | bytes 442376 | tf_op jit(solution)/shard_map/ppermute | solution.py:315
  9.4 8.9 %collective-permute-start.1 = (bf16[2,32,1152]{2,1,0:T(8,128)(2,1)S(1)}, bf16[2,32,1152]{2,1,0:T(8,128)(2,1)S(1)}, u32[]{:S(2)}, u32[]{:S(2)}) collective-permute-start(bf16[2,32,1152]{2,1,0:T(8,128)(2,1)S(1)} %join.2._), channel_id=1, source_target_pairs={{0,0},{1,4},{2,8},{3,12},{4,1},{5,5},{6,9},{7,13},{8,2},{9,6},{10,... | collective-permute-start | bytes 442376 | tf_op jit(solution)/shard_map/ppermute | solution.py:315
  11.3 7.5 %collective-permute-start.4 = (bf16[2,32,1152]{2,1,0:T(8,128)(2,1)S(1)}, bf16[2,32,1152]{2,1,0:T(8,128)(2,1)S(1)}, u32[]{:S(2)}, u32[]{:S(2)}) collective-permute-start(bf16[2,32,1152]{2,1,0:T(8,128)(2,1)S(1)} %join.3.own_ref), channel_id=1, source_target_pairs={{0,2},{1,3},{2,0},{3,1},{4,6},{5,7},{6,4},{7,5},{8,10},{9,11},{10,... | collective-permute-start | bytes 442376 | tf_op jit(solution)/shard_map/ppermute | solution.py:304
  12.6 6.2 %copy-start = (bf16[128,640]{1,0:T(8,128)(2,1)S(1)}, bf16[128,640]{1,0:T(8,128)(2,1)}, u32[]{:S(2)}) copy-start(bf16[128,640]{1,0:T(8,128)(2,1)} %w_ref.7) | copy-start | bytes 491524
  12.6 6.2 %copy-start.6 = (f32[128]{0:T(128)S(1)}, f32[128]{0:T(128)}, u32[]{:S(2)}) copy-start(f32[128]{0:T(128)} %param.30) | copy-start | bytes 1540
  12.7 6.2 %copy-start.7 = (f32[128]{0:T(128)S(1)}, f32[128]{0:T(128)}, u32[]{:S(2)}) copy-start(f32[128]{0:T(128)} %param.31) | copy-start | bytes 1540
  21.9 10.0 %collective-permute-start.8 = (bf16[16,32,128]{2,1,0:T(8,128)(2,1)S(1)}, bf16[16,32,128]{2,1,0:T(8,128)(2,1)S(1)}, u32[]{:S(2)}, u32[]{:S(2)}) collective-permute-start(bf16[16,32,128]{2,1,0:T(8,128)(2,1)S(1)} %get-tuple-element.30), channel_id=1, source_target_pairs={{8,0},{13,1},{11,2},{14,3},{9,4},{12,5},{10,6},{15,7},{0,8},{5,9},... | collective-permute-start | bytes 393224 | tf_op jit(solution)/shard_map/ppermute | solution.py:329
  23.7 11.1 %collective-permute-start.5 = (bf16[16,32,128]{2,1,0:T(8,128)(2,1)S(1)}, bf16[16,32,128]{2,1,0:T(8,128)(2,1)S(1)}, u32[]{:S(2)}, u32[]{:S(2)}) collective-permute-start(bf16[16,32,128]{2,1,0:T(8,128)(2,1)S(1)} %get-tuple-element.27), channel_id=1, source_target_pairs={{8,0},{13,1},{11,2},{14,3},{9,4},{12,5},{10,6},{15,7},{0,8},{5,9},... | collective-permute-start | bytes 393224 | tf_op jit(solution)/shard_map/ppermute | solution.py:329
  25.5 14.3 %collective-permute-start.7 = (bf16[32,32,128]{2,1,0:T(8,128)(2,1)S(1)}, bf16[32,32,128]{2,1,0:T(8,128)(2,1)S(1)}, u32[]{:S(2)}, u32[]{:S(2)}) collective-permute-start(bf16[32,32,128]{2,1,0:T(8,128)(2,1)S(1)} %get-tuple-element.28.refs_0_), channel_id=1, source_target_pairs={{0,1},{1,0},{2,3},{3,2},{4,5},{5,4},{6,7},{7,6},{8,9},{9,8},{10,11... | collective-permute-start | bytes 786440 | tf_op jit(solution)/shard_map/ppermute | solution.py:309
  25.5 15.2 %collective-permute-start.11 = (bf16[32,32,128]{2,1,0:T(8,128)(2,1)S(1)}, bf16[32,32,128]{2,1,0:T(8,128)(2,1)S(1)}, u32[]{:S(2)}, u32[]{:S(2)}) collective-permute-start(bf16[32,32,128]{2,1,0:T(8,128)(2,1)S(1)} %get-tuple-element.31), channel_id=1, source_target_pairs={{0,0},{4,1},{3,2},{7,3},{1,4},{5,5},{2,6},{6,7},{8,8},{12,9},{11,1... | collective-permute-start | bytes 786440 | tf_op jit(solution)/shard_map/ppermute | solution.py:329
  27.4 15.1 %collective-permute-start.10 = (bf16[32,32,128]{2,1,0:T(8,128)(2,1)S(1)}, bf16[32,32,128]{2,1,0:T(8,128)(2,1)S(1)}, u32[]{:S(2)}, u32[]{:S(2)}) collective-permute-start(bf16[32,32,128]{2,1,0:T(8,128)(2,1)S(1)} %get-tuple-element.31), channel_id=1, source_target_pairs={{1,0},{5,1},{2,2},{6,3},{0,4},{4,5},{3,6},{7,7},{9,8},{13,9},{10,1... | collective-permute-start | bytes 786440 | tf_op jit(solution)/shard_map/ppermute | solution.py:329
  31.9 12.0 %collective-permute-start.9 = (bf16[16,32,128]{2,1,0:T(8,128)(2,1)S(1)}, bf16[16,32,128]{2,1,0:T(8,128)(2,1)S(1)}, u32[]{:S(2)}, u32[]{:S(2)}) collective-permute-start(bf16[16,32,128]{2,1,0:T(8,128)(2,1)S(1)} %carry.3), channel_id=1, source_target_pairs={{0,4},{4,0},{8,12},{12,8},{1,5},{5,1},{9,13},{13,9},{2,6},{6,2},{1... | collective-permute-start | bytes 393224 | tf_op jit(solution)/shard_map/ppermute | solution.py:333
  34.7 9.8 %collective-permute-start.6 = (bf16[16,32,128]{2,1,0:T(8,128)(2,1)S(1)}, bf16[16,32,128]{2,1,0:T(8,128)(2,1)S(1)}, u32[]{:S(2)}, u32[]{:S(2)}) collective-permute-start(bf16[16,32,128]{2,1,0:T(8,128)(2,1)S(1)} %carry.2), channel_id=1, source_target_pairs={{0,4},{4,0},{8,12},{12,8},{1,5},{5,1},{9,13},{13,9},{2,6},{6,2},{1... | collective-permute-start | bytes 393224 | tf_op jit(solution)/shard_map/ppermute | solution.py:333
  42.5 3.8 %copy-start.1 = (bf16[128,128]{1,0:T(8,128)(2,1)S(1)}, bf16[128,128]{1,0:T(8,128)(2,1)}, u32[]{:S(2)}) copy-start(bf16[128,128]{1,0:T(8,128)(2,1)} %w_ref.9) | copy-start | bytes 98308
  42.5 3.8 %copy-start.2 = (f32[128]{0:T(128)S(1)}, f32[128]{0:T(128)}, u32[]{:S(2)}) copy-start(f32[128]{0:T(128)} %param.34) | copy-start | bytes 1540
  42.6 3.8 %copy-start.3 = (f32[128]{0:T(128)S(1)}, f32[128]{0:T(128)}, u32[]{:S(2)}) copy-start(f32[128]{0:T(128)} %param.35) | copy-start | bytes 1540
  42.6 3.8 %copy-start.4 = (f32[128]{0:T(128)S(1)}, f32[128]{0:T(128)}, u32[]{:S(2)}) copy-start(f32[128]{0:T(128)} %param.37) | copy-start | bytes 1540
  44.9 1.4 %collective-permute-start.13 = (bf16[512,128]{1,0:T(8,128)(2,1)S(1)}, bf16[512,128]{1,0:T(8,128)(2,1)S(1)}, u32[]{:S(2)}, u32[]{:S(2)}) collective-permute-start(bf16[512,128]{1,0:T(8,128)(2,1)S(1)} %get-tuple-element.36), channel_id=1, source_target_pairs={{0,2},{1,3},{2,0},{3,1},{4,6},{5,7},{6,4},{7,5},{8,10},{9,11},{10,... | collective-permute-start | bytes 393224 | tf_op jit(solution)/shard_map/ppermute | solution.py:304
  45.5 1.4 %collective-permute-start.12 = (bf16[512,128]{1,0:T(8,128)(2,1)S(1)}, bf16[512,128]{1,0:T(8,128)(2,1)S(1)}, u32[]{:S(2)}, u32[]{:S(2)}) collective-permute-start(bf16[512,128]{1,0:T(8,128)(2,1)S(1)} %get-tuple-element.33), channel_id=1, source_target_pairs={{0,2},{1,3},{2,0},{3,1},{4,6},{5,7},{6,4},{7,5},{8,10},{9,11},{10,... | collective-permute-start | bytes 393224 | tf_op jit(solution)/shard_map/ppermute | solution.py:304
  (1 other events, 0.8 us)

commit v15 on v14

--- a/solution.py
+++ b/solution.py
@@ -427,8 +427,8 @@
     far_parts = [
         (step, skip, send_same_core(half_edge, count, chips, step))
         for step in range(chips, count, 2) for skip, half_edge in ((0, low_edge), (cols // 2, high_edge))]
-    for step, skip, block_far in far_parts[:]:
-        carried = call(carry_kernel, shape(block_far.shape, BF16), [], [block_far], flops=1 << 29,
+    for step, skip, block_far in far_parts[::-1]:
+        carried = call(carry_kernel, shape(block_far.shape, BF16), [], [block_far], flops=1 << 27,
                        name="carry")
         far_parts.append((step + 1, skip, pass_on(carried, count)))
     left_edges = [left_edge] + send_chips(left_edge, chips)

time: 48.5 us -> 49.3 us (1.016)
  waiting for transfers between devices: 16.5 us -> 17.6 us
    ppermute x2, waiting for transfers between devices: 4.51 us -> 0.01 us  [send_chips(): lax.ppermute(block, 'seq', [(x, x ^ m) for x in range(chips)])]
    ppermute x2, waiting for transfers between devices: 0.01 us -> 3.26 us  [pass_on(): return lax.ppermute(block, 'resi', [(z, z ^ 1) for z in range(count)])]
    ppermute x4, waiting for transfers between devices: 5.63 us -> 8.07 us  [send_same_core(): return lax.ppermute(block, GROUP, pairs)]
    ppermute x2, starting transfers between devices: 1.41 us -> 0.14 us  [pass_on(): return lax.ppermute(block, 'resi', [(z, z ^ 1) for z in range(count)])]
    ppermute x2, starting transfers between devices: 2.68 us -> 3.23 us  [send_chips(): lax.ppermute(block, 'seq', [(x, x ^ m) for x in range(chips)])]
  transfers between devices with their start and end apart: 14 -> 14, of which waited for: 8 -> 9; matrix products, arithmetic and copies ran while one was open for 0% -> 0% of each run, Pallas kernels for 15% -> 15%
where the time goes in v15:
time: 49.3 us; the launch traced here: 48.8 us
  waiting for transfers between devices  17.6 us (36%)
  starting transfers between devices  16.2 us (33%)
  Pallas kernels  13.1 us (27%)
  local copies, waits for them, and re-layouts  1.48 us (3%)
    pallas_call x20, Pallas kernels, call(): pl.pallas_call(kernel, out_shape=outs, in_specs=[vmem] * len(args), out_s...  13.1 us
    ppermute x4, waiting for transfers between devices, send_same_core(): return lax.ppermute(block, GROUP, pairs)  8.07 us
    ppermute x4, starting transfers between devices, send_same_core(): return lax.ppermute(block, GROUP, pairs)  6.54 us
    ppermute x2, waiting for transfers between devices, send_turned(): lax.ppermute(block, GROUP, [(z * count + p, (p ^ m) * count + z) for z in...  5.66 us
    ppermute x2, starting transfers between devices, send_turned(): lax.ppermute(block, GROUP, [(z * count + p, (p ^ m) * count + z) for z in...  5.51 us
    ppermute x2, waiting for transfers between devices, pass_on(): return lax.ppermute(block, 'resi', [(z, z ^ 1) for z in range(count)])  3.26 us
    ppermute x2, starting transfers between devices, send_chips(): lax.ppermute(block, 'seq', [(x, x ^ m) for x in range(chips)])  3.23 us
    unnamed x38, local copies, waits for them, and re-layouts  1.48 us
  transfers between devices with their start and end apart: 14, of which 9 were waited for; matrix products, arithmetic and copies ran while one was open for 0% of the time, Pallas kernels for 15%

profile of v15, /device:TPU:1, one launch (start us, length us, event | category | flops | bytes accessed | tf_op | source)
XLA Modules:
  0.0 48.8 jit_solution(4370111753171283076)
XLA Ops:
  0.0 1.1 %copy-done.8 = bf16[32,32,256]{2,1,0:T(8,128)(2,1)S(1)} copy-done((bf16[32,32,256]{2,1,0:T(8,128)(2,1)S(1)}, bf16[32,32,256]{2,1,0:T(8,128)(2,1)}, u32[]{:S(2)}) %copy-start.8) | copy-done | bytes 524312
  1.1 0.4 norm.1.x_ref
  1.8 1.1 %pack.1 = (bf16[32,1152]{1,0:T(8,128)(2,1)S(1)}, bf16[32,1152]{1,0:T(8,128)(2,1)S(1)}) custom-call(f32[1024,256]{1,0:T(8,128)S(1)} %norm.1.x_ref, s32[32,32]{1,0:T(8,128)S(1)} %copy-done.13, s32[1,128]{1,0:T(1,128)S(1)} %bitcast.17, f32[1,256]{1,0:T(1,128)S(1)} %bitcast.22, f32[1,256]{1,0:T(1,128)S(1)} %bitcast.23, bf16[64,256]{1,0:T(8,128)(2,1)S(1)} %bitcast.21, ...), custom_call_target="tpu_custom_call" | custom-call | flops 1073741824 | bytes 1088256 | tf_op jit(solution)/shard_map/pack/pallas_call | solution.py:339
  3.0 2.7 %collective-permute-start.3 = (bf16[32,1152]{1,0:T(8,128)(2,1)S(1)}, bf16[32,1152]{1,0:T(8,128)(2,1)S(1)}, u32[]{:S(2)}, u32[]{:S(2)}) collective-permute-start(bf16[32,1152]{1,0:T(8,128)(2,1)S(1)} %get-tuple-element.24.refs_0_), channel_id=1, source_target_pairs={{0,1},{1,0},{2,3},{3,2},{4,5},{5,4},{6,7},{7,6},{8,9},{9,8},{10,11... | collective-permute-start | bytes 221192 | tf_op jit(solution)/shard_map/ppermute | solution.py:309
  5.8 3.6 %collective-permute-start.2 = (bf16[2,32,1152]{2,1,0:T(8,128)(2,1)S(1)}, bf16[2,32,1152]{2,1,0:T(8,128)(2,1)S(1)}, u32[]{:S(2)}, u32[]{:S(2)}) collective-permute-start(bf16[2,32,1152]{2,1,0:T(8,128)(2,1)S(1)} %join.2._), channel_id=1, source_target_pairs={{0,4},{1,0},{2,12},{3,8},{4,5},{5,1},{6,13},{7,9},{8,6},{9,2},{10,... | collective-permute-start | bytes 442376 | tf_op jit(solution)/shard_map/ppermute | solution.py:315
  9.4 1.9 %collective-permute-start.1 = (bf16[2,32,1152]{2,1,0:T(8,128)(2,1)S(1)}, bf16[2,32,1152]{2,1,0:T(8,128)(2,1)S(1)}, u32[]{:S(2)}, u32[]{:S(2)}) collective-permute-start(bf16[2,32,1152]{2,1,0:T(8,128)(2,1)S(1)} %join.2._), channel_id=1, source_target_pairs={{0,0},{1,4},{2,8},{3,12},{4,1},{5,5},{6,9},{7,13},{8,2},{9,6},{10,... | collective-permute-start | bytes 442376 | tf_op jit(solution)/shard_map/ppermute | solution.py:315
  11.5 1.2 %base.1 = (f32[32,32,128]{2,1,0:T(8,128)S(1)}, bf16[4096,512]{1,0:T(8,128)(2,1)S(1)}) custom-call(bf16[32,32,128]{2,1,0:T(8,128)(2,1)S(1)} %copy-done.9, bf16[66,128]{1,0:T(8,128)(2,1)S(1)} %copy-done.12, s32[1,128]{1,0:T(1,128)S(1)} %bitcast.25, bf16[1024,128]{1,0:T(8,128)(2,1)S(1)} %copy-done.10, bf16[2,32,1152]{2,1,0:T(8,128)(2,1)S(1)} %join.2._), custom_call_target="tpu_custom_call" | custom-call | flops 1073741824 | bytes 689152 | tf_op jit(solution)/shard_map/base/pallas_call | solution.py:339
  12.7 0.8 %collective-permute-done.2.refs_1_ = bf16[2,32,1152]{2,1,0:T(8,128)(2,1)S(1)} collective-permute-done((bf16[2,32,1152]{2,1,0:T(8,128)(2,1)S(1)}, bf16[2,32,1152]{2,1,0:T(8,128)(2,1)S(1)}, u32[]{:S(2)}, u32[]{:S(2)}) %collective-permute-start.2) | collective-permute-done | bytes 147488 | tf_op jit(solution)/shard_map/ppermute | solution.py:315
  13.4 4.9 %collective-permute-done.1.refs_0_ = bf16[2,32,1152]{2,1,0:T(8,128)(2,1)S(1)} collective-permute-done((bf16[2,32,1152]{2,1,0:T(8,128)(2,1)S(1)}, bf16[2,32,1152]{2,1,0:T(8,128)(2,1)S(1)}, u32[]{:S(2)}, u32[]{:S(2)}) %collective-permute-start.1) | collective-permute-done | bytes 147488 | tf_op jit(solution)/shard_map/ppermute | solution.py:315
  18.3 0.5 turn.1
  18.8 3.1 %edges.1 = (bf16[32,32,128]{2,1,0:T(8,128)(2,1)S(1)}, bf16[32,32,128]{2,1,0:T(8,128)(2,1)S(1)}, bf16[32,32,128]{2,1,0:T(8,128)(2,1)S(1)}, bf16[16,32,128]{2,1,0:...) custom-call(bf16[1024,128]{1,0:T(8,128)(2,1)S(1)} %get-tuple-element.22.turned_ref, ...), custom_call_target="tpu_custom_call" | custom-call | bytes 5451776 | tf_op jit(solution)/shard_map/edges/pallas_call | solution.py:339
  21.9 0.6 %collective-permute-start.7 = (bf16[32,32,128]{2,1,0:T(8,128)(2,1)S(1)}, bf16[32,32,128]{2,1,0:T(8,128)(2,1)S(1)}, u32[]{:S(2)}, u32[]{:S(2)}) collective-permute-start(bf16[32,32,128]{2,1,0:T(8,128)(2,1)S(1)} %get-tuple-element.28.refs_0_), channel_id=1, source_target_pairs={{0,1},{1,0},{2,3},{3,2},{4,5},{5,4},{6,7},{7,6},{8,9},{9,8},{10,11... | collective-permute-start | bytes 786440 | tf_op jit(solution)/shard_map/ppermute | solution.py:309
  22.5 1.2 %collective-permute-start.8 = (bf16[16,32,128]{2,1,0:T(8,128)(2,1)S(1)}, bf16[16,32,128]{2,1,0:T(8,128)(2,1)S(1)}, u32[]{:S(2)}, u32[]{:S(2)}) collective-permute-start(bf16[16,32,128]{2,1,0:T(8,128)(2,1)S(1)} %get-tuple-element.30), channel_id=1, source_target_pairs={{8,0},{13,1},{11,2},{14,3},{9,4},{12,5},{10,6},{15,7},{0,8},{5,9},... | collective-permute-start | bytes 393224 | tf_op jit(solution)/shard_map/ppermute | solution.py:329
  23.7 2.7 %collective-permute-start.5 = (bf16[16,32,128]{2,1,0:T(8,128)(2,1)S(1)}, bf16[16,32,128]{2,1,0:T(8,128)(2,1)S(1)}, u32[]{:S(2)}, u32[]{:S(2)}) collective-permute-start(bf16[16,32,128]{2,1,0:T(8,128)(2,1)S(1)} %get-tuple-element.27), channel_id=1, source_target_pairs={{8,0},{13,1},{11,2},{14,3},{9,4},{12,5},{10,6},{15,7},{0,8},{5,9},... | collective-permute-start | bytes 393224 | tf_op jit(solution)/shard_map/ppermute | solution.py:329
  26.4 1.9 %collective-permute-start.11 = (bf16[32,32,128]{2,1,0:T(8,128)(2,1)S(1)}, bf16[32,32,128]{2,1,0:T(8,128)(2,1)S(1)}, u32[]{:S(2)}, u32[]{:S(2)}) collective-permute-start(bf16[32,32,128]{2,1,0:T(8,128)(2,1)S(1)} %get-tuple-element.31), channel_id=1, source_target_pairs={{0,0},{4,1},{3,2},{7,3},{1,4},{5,5},{2,6},{6,7},{8,8},{12,9},{11,1... | collective-permute-start | bytes 786440 | tf_op jit(solution)/shard_map/ppermute | solution.py:329
  28.4 0.7 %collective-permute-start.10 = (bf16[32,32,128]{2,1,0:T(8,128)(2,1)S(1)}, bf16[32,32,128]{2,1,0:T(8,128)(2,1)S(1)}, u32[]{:S(2)}, u32[]{:S(2)}) collective-permute-start(bf16[32,32,128]{2,1,0:T(8,128)(2,1)S(1)} %get-tuple-element.31), channel_id=1, source_target_pairs={{1,0},{5,1},{2,2},{6,3},{0,4},{4,5},{3,6},{7,7},{9,8},{13,9},{10,1... | collective-permute-start | bytes 786440 | tf_op jit(solution)/shard_map/ppermute | solution.py:329
  29.0 5.6 %collective-permute-done.8.in_ref.right_ref = bf16[16,32,128]{2,1,0:T(8,128)(2,1)S(1)} collective-permute-done((bf16[16,32,128]{2,1,0:T(8,128)(2,1)S(1)}, bf16[16,32,128]{2,1,0:T(8,128)(2,1)S(1)}, u32[]{:S(2)}, u32[]{:S(2)}) %collective-permute-start.8) | collective-permute-done | bytes 131104 | tf_op jit(solution)/shard_map/ppermute | solution.py:329
  34.8 1.8 %collective-permute-done.5.in_ref.right_ref = bf16[16,32,128]{2,1,0:T(8,128)(2,1)S(1)} collective-permute-done((bf16[16,32,128]{2,1,0:T(8,128)(2,1)S(1)}, bf16[16,32,128]{2,1,0:T(8,128)(2,1)S(1)}, u32[]{:S(2)}, u32[]{:S(2)}) %collective-permute-start.5) | collective-permute-done | bytes 131104 | tf_op jit(solution)/shard_map/ppermute | solution.py:329
  37.0 0.6 %triangle.5.refs_0_ = f32[1024,128]{1,0:T(8,128)S(1)} custom-call(bf16[16,32,128]{2,1,0:T(8,128)(2,1)S(1)} %collective-permute-done.5.in_ref.right_ref, f32[2,1024,128]{2,1,0:T(8,128)S(1)} %panel.1.panel_ref), custom_call_target="tpu_custom_call" | custom-call | bytes 1179648 | tf_op jit(solution)/shard_map/triangle/pallas_call | solution.py:339
  37.6 0.7 %collective-permute-done.11.right_ref = bf16[32,32,128]{2,1,0:T(8,128)(2,1)S(1)} collective-permute-done((bf16[32,32,128]{2,1,0:T(8,128)(2,1)S(1)}, bf16[32,32,128]{2,1,0:T(8,128)(2,1)S(1)}, u32[]{:S(2)}, u32[]{:S(2)}) %collective-permute-start.11) | collective-permute-done | bytes 262176 | tf_op jit(solution)/shard_map/ppermute | solution.py:329
  38.3 1.3 %triangle.8.refs_0_ = f32[1024,128]{1,0:T(8,128)S(1)} custom-call(bf16[32,32,128]{2,1,0:T(8,128)(2,1)S(1)} %collective-permute-done.11.right_ref, f32[2,1024,128]{2,1,0:T(8,128)S(1)} %panel.1.panel_ref), custom_call_target="tpu_custom_call" | custom-call | bytes 1310720 | tf_op jit(solution)/shard_map/triangle/pallas_call | solution.py:339
  39.5 0.6 %triangle.6.refs_0_ = f32[1024,128]{1,0:T(8,128)S(1)} custom-call(bf16[16,32,128]{2,1,0:T(8,128)(2,1)S(1)} %collective-permute-done.8.in_ref.right_ref, f32[2,1024,128]{2,1,0:T(8,128)S(1)} %panel.1.panel_ref, f32[1024,128]{1,0:T(8,128)S(1)} %triangle.5.refs_0_), custom_call_target="tpu_custom_call" | custom-call | bytes 1703936 | tf_op jit(solution)/shard_map/triangle/pallas_call | solution.py:339
  40.2 1.3 %triangle.9.near_ref = f32[1024,128]{1,0:T(8,128)S(1)} custom-call(bf16[32,32,128]{2,1,0:T(8,128)(2,1)S(1)} %collective-permute-done.10.right_ref, f32[2,1024,128]{2,1,0:T(8,128)S(1)} %panel.1.panel_ref, f32[1024,128]{1,0:T(8,128)S(1)} %triangle.8.refs_0_), custom_call_target="tpu_custom_call" | custom-call | bytes 1835008 | tf_op jit(solution)/shard_map/triangle/pallas_call | solution.py:339
  41.5 2.6 %collective-permute-done.9.right_ref = bf16[16,32,128]{2,1,0:T(8,128)(2,1)S(1)} collective-permute-done((bf16[16,32,128]{2,1,0:T(8,128)(2,1)S(1)}, bf16[16,32,128]{2,1,0:T(8,128)(2,1)S(1)}, u32[]{:S(2)}, u32[]{:S(2)}) %collective-permute-start.9) | collective-permute-done | bytes 131104 | tf_op jit(solution)/shard_map/ppermute | solution.py:333
  44.1 0.6 %triangle.7.far_ref = f32[1024,128]{1,0:T(8,128)S(1)} custom-call(bf16[16,32,128]{2,1,0:T(8,128)(2,1)S(1)} %collective-permute-done.9.right_ref, f32[2,1024,128]{2,1,0:T(8,128)S(1)} %panel.1.panel_ref, f32[1024,128]{1,0:T(8,128)S(1)} %triangle.6.refs_0_), custom_call_target="tpu_custom_call" | custom-call | bytes 1703936 | tf_op jit(solution)/shard_map/triangle/pallas_call | solution.py:339
  44.7 0.7 %collective-permute-done.6.right_ref = bf16[16,32,128]{2,1,0:T(8,128)(2,1)S(1)} collective-permute-done((bf16[16,32,128]{2,1,0:T(8,128)(2,1)S(1)}, bf16[16,32,128]{2,1,0:T(8,128)(2,1)S(1)}, u32[]{:S(2)}, u32[]{:S(2)}) %collective-permute-start.6) | collective-permute-done | bytes 131104 | tf_op jit(solution)/shard_map/ppermute | solution.py:333
  45.4 0.4 last.3
  45.8 0.4 last.2
  46.2 0.6 %collective-permute-start.12 = (bf16[512,128]{1,0:T(8,128)(2,1)S(1)}, bf16[512,128]{1,0:T(8,128)(2,1)S(1)}, u32[]{:S(2)}, u32[]{:S(2)}) collective-permute-start(bf16[512,128]{1,0:T(8,128)(2,1)S(1)} %get-tuple-element.33), channel_id=1, source_target_pairs={{0,2},{1,3},{2,0},{3,1},{4,6},{5,7},{6,4},{7,5},{8,10},{9,11},{10,... | collective-permute-start | bytes 393224 | tf_op jit(solution)/shard_map/ppermute | solution.py:304
  46.8 0.4 collective-permute-done.13.other_ref
  47.2 0.4 final.2.refs_0_
  47.7 1.0 %final.3 = bf16[32,32,128]{2,1,0:T(8,128)(2,1)} custom-call(f32[512,128]{1,0:T(8,128)S(1)} %get-tuple-element.32.own_ref, bf16[512,128]{1,0:T(8,128)(2,1)S(1)} %collective-permute-done.12.other_ref, bf16[32,32,128]{2,1,0:T(8,128)(2,1)S(1)} %get-tuple-element.34.updated_ref, f32[1024,128]{1,0:T(8,128)S(1)} %gate.1.refs_2_.gate_ref, f32[1,128]{1,0:T(1,128)S(1)} %bitcast.12, ...), custom_call_target="tpu_custom_call" | custom-call | flops 268435456 | bytes 1345024 | tf_op jit(solution)/shard_map/final/pallas_call | solution.py:339
  (55 shorter events, 1.4 us)
Async XLA Ops:
  0.0 1.5 %copy-start.5 = (s32[128]{0:T(128)S(1)}, s32[128]{0:T(128)}, u32[]{:S(2)}) copy-start(s32[128]{0:T(128)} %param.22) | copy-start | bytes 1540
  0.0 1.1 %copy-start.8 = (bf16[32,32,256]{2,1,0:T(8,128)(2,1)S(1)}, bf16[32,32,256]{2,1,0:T(8,128)(2,1)}, u32[]{:S(2)}) copy-start(bf16[32,32,256]{2,1,0:T(8,128)(2,1)} %x_ref.1) | copy-start | bytes 1572868
  1.1 0.8 %copy-start.11 = (bf16[256,64]{0,1:T(8,128)(2,1)S(1)}, bf16[256,64]{0,1:T(8,128)(2,1)}, u32[]{:S(2)}) copy-start(bf16[256,64]{0,1:T(8,128)(2,1)} %param.26) | copy-start | bytes 98308
  1.1 0.8 %copy-start.13 = (s32[32,32]{1,0:T(8,128)S(1)}, s32[32,32]{1,0:T(8,128)}, u32[]{:S(2)}) copy-start(s32[32,32]{1,0:T(8,128)} %mask_ref.1) | copy-start | bytes 12292
  1.1 0.8 %copy-start.14 = (f32[256]{0:T(256)S(1)}, f32[256]{0:T(256)}, u32[]{:S(2)}) copy-start(f32[256]{0:T(256)} %param.24) | copy-start | bytes 3076
  1.1 0.8 %copy-start.15 = (f32[256]{0:T(256)S(1)}, f32[256]{0:T(256)}, u32[]{:S(2)}) copy-start(f32[256]{0:T(256)} %param.25) | copy-start | bytes 3076
  1.1 4.6 %copy-start.18 = (f32[640]{0:T(1024)S(1)}, f32[640]{0:T(1024)}, u32[]{:S(2)}) copy-start(f32[640]{0:T(1024)} %param.33) | copy-start | bytes 7684
  2.9 2.8 %collective-permute-start = (bf16[32,1152]{1,0:T(8,128)(2,1)S(1)}, bf16[32,1152]{1,0:T(8,128)(2,1)S(1)}, u32[]{:S(2)}, u32[]{:S(2)}) collective-permute-start(bf16[32,1152]{1,0:T(8,128)(2,1)S(1)} %get-tuple-element.21.refs_0_), channel_id=1, source_target_pairs={{0,2},{1,3},{2,0},{3,1},{4,6},{5,7},{6,4},{7,5},{8,10},{9,11},{10,... | collective-permute-start | bytes 221192 | tf_op jit(solution)/shard_map/ppermute | solution.py:304
  3.0 8.3 %collective-permute-start.3 = (bf16[32,1152]{1,0:T(8,128)(2,1)S(1)}, bf16[32,1152]{1,0:T(8,128)(2,1)S(1)}, u32[]{:S(2)}, u32[]{:S(2)}) collective-permute-start(bf16[32,1152]{1,0:T(8,128)(2,1)S(1)} %get-tuple-element.24.refs_0_), channel_id=1, source_target_pairs={{0,1},{1,0},{2,3},{3,2},{4,5},{5,4},{6,7},{7,6},{8,9},{9,8},{10,11... | collective-permute-start | bytes 221192 | tf_op jit(solution)/shard_map/ppermute | solution.py:309
  5.8 5.7 %copy-start.9 = (bf16[32,32,128]{2,1,0:T(8,128)(2,1)S(1)}, bf16[32,32,128]{2,1,0:T(8,128)(2,1)}, u32[]{:S(2)}) copy-start(bf16[32,32,128]{2,1,0:T(8,128)(2,1)} %pair_ref.1) | copy-start | bytes 786436
  5.8 5.7 %copy-start.10 = (bf16[1024,128]{1,0:T(8,128)(2,1)S(1)}, bf16[1024,128]{1,0:T(8,128)(2,1)}, u32[]{:S(2)}) copy-start(bf16[1024,128]{1,0:T(8,128)(2,1)} %w_ref.5) | copy-start | bytes 786436
  5.8 5.7 %copy-start.12 = (bf16[66,128]{1,0:T(8,128)(2,1)S(1)}, bf16[66,128]{1,0:T(8,128)(2,1)}, u32[]{:S(2)}) copy-start(bf16[66,128]{1,0:T(8,128)(2,1)} %table_ref.1) | copy-start | bytes 50692
  5.8 5.7 %copy-start.17 = (s32[128]{0:T(128)S(1)}, s32[128]{0:T(128)}, u32[]{:S(2)}) copy-start(s32[128]{0:T(128)} %param.23) | copy-start | bytes 1540
  5.8 7.6 %collective-permute-start.2 = (bf16[2,32,1152]{2,1,0:T(8,128)(2,1)S(1)}, bf16[2,32,1152]{2,1,0:T(8,128)(2,1)S(1)}, u32[]{:S(2)}, u32[]{:S(2)}) collective-permute-start(bf16[2,32,1152]{2,1,0:T(8,128)(2,1)S(1)} %join.2._), channel_id=1, source_target_pairs={{0,4},{1,0},{2,12},{3,8},{4,5},{5,1},{6,13},{7,9},{8,6},{9,2},{10,... | collective-permute-start | bytes 442376 | tf_op jit(solution)/shard_map/ppermute | solution.py:315
  9.4 8.9 %collective-permute-start.1 = (bf16[2,32,1152]{2,1,0:T(8,128)(2,1)S(1)}, bf16[2,32,1152]{2,1,0:T(8,128)(2,1)S(1)}, u32[]{:S(2)}, u32[]{:S(2)}) collective-permute-start(bf16[2,32,1152]{2,1,0:T(8,128)(2,1)S(1)} %join.2._), channel_id=1, source_target_pairs={{0,0},{1,4},{2,8},{3,12},{4,1},{5,5},{6,9},{7,13},{8,2},{9,6},{10,... | collective-permute-start | bytes 442376 | tf_op jit(solution)/shard_map/ppermute | solution.py:315
  11.3 7.5 %collective-permute-start.4 = (bf16[2,32,1152]{2,1,0:T(8,128)(2,1)S(1)}, bf16[2,32,1152]{2,1,0:T(8,128)(2,1)S(1)}, u32[]{:S(2)}, u32[]{:S(2)}) collective-permute-start(bf16[2,32,1152]{2,1,0:T(8,128)(2,1)S(1)} %join.3.own_ref), channel_id=1, source_target_pairs={{0,2},{1,3},{2,0},{3,1},{4,6},{5,7},{6,4},{7,5},{8,10},{9,11},{10,... | collective-permute-start | bytes 442376 | tf_op jit(solution)/shard_map/ppermute | solution.py:304
  12.6 6.2 %copy-start = (bf16[128,640]{1,0:T(8,128)(2,1)S(1)}, bf16[128,640]{1,0:T(8,128)(2,1)}, u32[]{:S(2)}) copy-start(bf16[128,640]{1,0:T(8,128)(2,1)} %w_ref.7) | copy-start | bytes 491524
  12.6 6.2 %copy-start.6 = (f32[128]{0:T(128)S(1)}, f32[128]{0:T(128)}, u32[]{:S(2)}) copy-start(f32[128]{0:T(128)} %param.30) | copy-start | bytes 1540
  12.7 6.2 %copy-start.7 = (f32[128]{0:T(128)S(1)}, f32[128]{0:T(128)}, u32[]{:S(2)}) copy-start(f32[128]{0:T(128)} %param.31) | copy-start | bytes 1540
  21.9 15.0 %collective-permute-start.7 = (bf16[32,32,128]{2,1,0:T(8,128)(2,1)S(1)}, bf16[32,32,128]{2,1,0:T(8,128)(2,1)S(1)}, u32[]{:S(2)}, u32[]{:S(2)}) collective-permute-start(bf16[32,32,128]{2,1,0:T(8,128)(2,1)S(1)} %get-tuple-element.28.refs_0_), channel_id=1, source_target_pairs={{0,1},{1,0},{2,3},{3,2},{4,5},{5,4},{6,7},{7,6},{8,9},{9,8},{10,11... | collective-permute-start | bytes 786440 | tf_op jit(solution)/shard_map/ppermute | solution.py:309
  22.5 12.2 %collective-permute-start.8 = (bf16[16,32,128]{2,1,0:T(8,128)(2,1)S(1)}, bf16[16,32,128]{2,1,0:T(8,128)(2,1)S(1)}, u32[]{:S(2)}, u32[]{:S(2)}) collective-permute-start(bf16[16,32,128]{2,1,0:T(8,128)(2,1)S(1)} %get-tuple-element.30), channel_id=1, source_target_pairs={{8,0},{13,1},{11,2},{14,3},{9,4},{12,5},{10,6},{15,7},{0,8},{5,9},... | collective-permute-start | bytes 393224 | tf_op jit(solution)/shard_map/ppermute | solution.py:329
  23.7 12.8 %collective-permute-start.5 = (bf16[16,32,128]{2,1,0:T(8,128)(2,1)S(1)}, bf16[16,32,128]{2,1,0:T(8,128)(2,1)S(1)}, u32[]{:S(2)}, u32[]{:S(2)}) collective-permute-start(bf16[16,32,128]{2,1,0:T(8,128)(2,1)S(1)} %get-tuple-element.27), channel_id=1, source_target_pairs={{8,0},{13,1},{11,2},{14,3},{9,4},{12,5},{10,6},{15,7},{0,8},{5,9},... | collective-permute-start | bytes 393224 | tf_op jit(solution)/shard_map/ppermute | solution.py:329
  26.4 11.8 %collective-permute-start.11 = (bf16[32,32,128]{2,1,0:T(8,128)(2,1)S(1)}, bf16[32,32,128]{2,1,0:T(8,128)(2,1)S(1)}, u32[]{:S(2)}, u32[]{:S(2)}) collective-permute-start(bf16[32,32,128]{2,1,0:T(8,128)(2,1)S(1)} %get-tuple-element.31), channel_id=1, source_target_pairs={{0,0},{4,1},{3,2},{7,3},{1,4},{5,5},{2,6},{6,7},{8,8},{12,9},{11,1... | collective-permute-start | bytes 786440 | tf_op jit(solution)/shard_map/ppermute | solution.py:329
  28.4 11.8 %collective-permute-start.10 = (bf16[32,32,128]{2,1,0:T(8,128)(2,1)S(1)}, bf16[32,32,128]{2,1,0:T(8,128)(2,1)S(1)}, u32[]{:S(2)}, u32[]{:S(2)}) collective-permute-start(bf16[32,32,128]{2,1,0:T(8,128)(2,1)S(1)} %get-tuple-element.31), channel_id=1, source_target_pairs={{1,0},{5,1},{2,2},{6,3},{0,4},{4,5},{3,6},{7,7},{9,8},{13,9},{10,1... | collective-permute-start | bytes 786440 | tf_op jit(solution)/shard_map/ppermute | solution.py:329
  34.7 9.4 %collective-permute-start.9 = (bf16[16,32,128]{2,1,0:T(8,128)(2,1)S(1)}, bf16[16,32,128]{2,1,0:T(8,128)(2,1)S(1)}, u32[]{:S(2)}, u32[]{:S(2)}) collective-permute-start(bf16[16,32,128]{2,1,0:T(8,128)(2,1)S(1)} %carry.3), channel_id=1, source_target_pairs={{0,4},{4,0},{8,12},{12,8},{1,5},{5,1},{9,13},{13,9},{2,6},{6,2},{1... | collective-permute-start | bytes 393224 | tf_op jit(solution)/shard_map/ppermute | solution.py:333
  36.6 8.8 %collective-permute-start.6 = (bf16[16,32,128]{2,1,0:T(8,128)(2,1)S(1)}, bf16[16,32,128]{2,1,0:T(8,128)(2,1)S(1)}, u32[]{:S(2)}, u32[]{:S(2)}) collective-permute-start(bf16[16,32,128]{2,1,0:T(8,128)(2,1)S(1)} %carry.2), channel_id=1, source_target_pairs={{0,4},{4,0},{8,12},{12,8},{1,5},{5,1},{9,13},{13,9},{2,6},{6,2},{1... | collective-permute-start | bytes 393224 | tf_op jit(solution)/shard_map/ppermute | solution.py:333
  40.2 7.0 %copy-start.1 = (bf16[128,128]{1,0:T(8,128)(2,1)S(1)}, bf16[128,128]{1,0:T(8,128)(2,1)}, u32[]{:S(2)}) copy-start(bf16[128,128]{1,0:T(8,128)(2,1)} %w_ref.9) | copy-start | bytes 98308
  40.2 7.0 %copy-start.2 = (f32[128]{0:T(128)S(1)}, f32[128]{0:T(128)}, u32[]{:S(2)}) copy-start(f32[128]{0:T(128)} %param.34) | copy-start | bytes 1540
  40.2 7.0 %copy-start.3 = (f32[128]{0:T(128)S(1)}, f32[128]{0:T(128)}, u32[]{:S(2)}) copy-start(f32[128]{0:T(128)} %param.35) | copy-start | bytes 1540
  40.2 7.0 %copy-start.4 = (f32[128]{0:T(128)S(1)}, f32[128]{0:T(128)}, u32[]{:S(2)}) copy-start(f32[128]{0:T(128)} %param.37) | copy-start | bytes 1540
  45.8 1.4 %collective-permute-start.13 = (bf16[512,128]{1,0:T(8,128)(2,1)S(1)}, bf16[512,128]{1,0:T(8,128)(2,1)S(1)}, u32[]{:S(2)}, u32[]{:S(2)}) collective-permute-start(bf16[512,128]{1,0:T(8,128)(2,1)S(1)} %get-tuple-element.36), channel_id=1, source_target_pairs={{0,2},{1,3},{2,0},{3,1},{4,6},{5,7},{6,4},{7,5},{8,10},{9,11},{10,... | collective-permute-start | bytes 393224 | tf_op jit(solution)/shard_map/ppermute | solution.py:304
  46.2 1.5 %collective-permute-start.12 = (bf16[512,128]{1,0:T(8,128)(2,1)S(1)}, bf16[512,128]{1,0:T(8,128)(2,1)S(1)}, u32[]{:S(2)}, u32[]{:S(2)}) collective-permute-start(bf16[512,128]{1,0:T(8,128)(2,1)S(1)} %get-tuple-element.33), channel_id=1, source_target_pairs={{0,2},{1,3},{2,0},{3,1},{4,6},{5,7},{6,4},{7,5},{8,10},{9,11},{10,... | collective-permute-start | bytes 393224 | tf_op jit(solution)/shard_map/ppermute | solution.py:304
  (1 other events, 0.8 us)

commit v16 on v13

--- a/solution.py
+++ b/solution.py
@@ -264,10 +264,14 @@
 
 def final_kernel(first, own_ref, other_ref, updated_ref, gate_ref, gain_ref, shift_ref, w_ref, bias_ref,
                  *refs):
-    out_hbm, vscr, sems = refs[-3:]
-    rows, cols, channels = vscr.shape
+    if first:
+        before_ref, out_hbm, value_ref, sems = refs
+        moves = [pltpu.make_async_copy(before_ref, out_hbm.at[:first], sems.at[0])]
+        moves[0].start()
+    else:
+        value_ref, = refs
+    rows, cols, channels = value_ref.shape
     chunk = 8
-    moves = []
     for i0 in range(0, rows, chunk):
         at = slice(i0 * cols, (i0 + chunk) * cols)
         here = slice((first + i0) * cols, (first + i0 + chunk) * cols)
@@ -276,12 +280,15 @@
         result = dot(normed, w_ref[...]) + bias_ref[...]
         updated = updated_ref[first + i0:first + i0 + chunk].reshape(chunk * cols, channels).astype(F32)
         value = updated + gate_ref[here, :] * result
-        vscr[i0:i0 + chunk] = value.astype(BF16).reshape(chunk, cols, channels)
-        moves.append(pltpu.make_async_copy(
-            vscr.at[i0:i0 + chunk], out_hbm.at[first + i0:first + i0 + chunk], sems.at[i0 // chunk]))
-        moves[-1].start()
-    for move in moves:
-        move.wait()
+        value_ref[i0:i0 + chunk] = value.astype(BF16).reshape(chunk, cols, channels)
+        if first:
+            moves.append(pltpu.make_async_copy(
+                value_ref.at[i0:i0 + chunk], out_hbm.at[first + i0:first + i0 + chunk],
+                sems.at[1 + i0 // chunk]))
+            moves[-1].start()
+    if first:
+        for move in moves:
+            move.wait()
 
 
 def swap_cores(block, count):
@@ -317,17 +324,16 @@
     return lax.ppermute(block, "resi", [(z, z ^ 1) for z in range(count)])
 
 
-def call(kernel, outs, scratch, args, flops=0, aliases=None, hbm=False, name=None):
+def call(kernel, outs, scratch, args, flops=0, hbm=False, name=None):
     vmem = pl.BlockSpec(memory_space=pltpu.VMEM)
-    result = pl.BlockSpec(memory_space=pl.ANY) if hbm else vmem
     size = sum(a.size * a.dtype.itemsize for a in args)
     return pl.pallas_call(
         kernel,
         out_shape=outs,
-        in_specs=[result if n in (aliases or {}) else vmem for n in range(len(args))],
-        out_specs=[vmem] * len(outs) if isinstance(outs, list) else result,
+        in_specs=[vmem] * len(args),
+        out_specs=[vmem] * len(outs) if isinstance(outs, list) else (
+            pl.BlockSpec(memory_space=pl.ANY) if hbm else vmem),
         scratch_shapes=scratch,
-        input_output_aliases=aliases or {},
         compiler_params=pltpu.CompilerParams(vmem_limit_bytes=40 * MIB),
         cost_estimate=pl.CostEstimate(flops=flops, bytes_accessed=size, transcendentals=0),
         name=name,
@@ -437,11 +443,12 @@
     for n, first in enumerate((0, part)):
         args = [own_sums[n], other_sums[n], updated, gate, flat(triangle_sum_norm_gain),
                 flat(triangle_sum_norm_bias), triangle_output_weight, flat(outer_pair_bias)]
+        half_shape = (part, cols, channels)
         result = [call(
-            functools.partial(final_kernel, first), shape((rows, cols, channels), BF16),
-            [pltpu.VMEM((part, cols, channels), BF16), pltpu.SemaphoreType.DMA((part // 8,))],
-            args + result, flops=1 << 28, aliases={len(args): 0} if n else None, hbm=True,
-            name="final")]
+            functools.partial(final_kernel, first),
+            shape((rows, cols, channels) if n else half_shape, BF16),
+            [pltpu.VMEM(half_shape, BF16), pltpu.SemaphoreType.DMA((1 + part // 8,))] if n else [],
+            args + result, flops=1 << 28, hbm=n == 1, name="final")]
     return result[0]
 
 

time: 48.3 us -> 48.1 us (level)
  waiting for transfers between devices: 18.7 us -> 19.4 us
  Pallas kernels: 13.7 us -> 13.1 us
    ppermute x4, waiting for transfers between devices: 0.19 us -> 0.85 us  [swap_cores(): lax.ppermute(block, PLANE, [(p, p ^ count // 2) for p in range(count)])]
    pallas_call x16, Pallas kernels: 13.7 us -> 13.1 us  [call(): pl.pallas_call(kernel, out_shape=outs, in_specs=[vmem] * len(args), out_s...]
  transfers between devices with their start and end apart: 12 -> 12, of which waited for: 7 -> 7; matrix products, arithmetic and copies ran while one was open for 0% -> 0% of each run, Pallas kernels for 16% -> 14%
where the time goes in v16:
time: 48.1 us; the launch traced here: 47.8 us
  waiting for transfers between devices  19.4 us (40%)
  starting transfers between devices  13.5 us (28%)
  Pallas kernels  13.1 us (27%)
  local copies, waits for them, and re-layouts  1.48 us (3%)
    pallas_call x16, Pallas kernels, call(): pl.pallas_call(kernel, out_shape=outs, in_specs=[vmem] * len(args), out_s...  13.1 us
    ppermute x3, waiting for transfers between devices, send_same_core(): return lax.ppermute(block, GROUP, pairs)  12.2 us
    ppermute x2, waiting for transfers between devices, send_turned(): lax.ppermute(block, GROUP, [(z * count + p, (p ^ m) * count + z) for z in...  5.66 us
    ppermute x2, starting transfers between devices, send_turned(): lax.ppermute(block, GROUP, [(z * count + p, (p ^ m) * count + z) for z in...  5.51 us
    ppermute x3, starting transfers between devices, send_same_core(): return lax.ppermute(block, GROUP, pairs)  4.31 us
    ppermute x2, starting transfers between devices, send_chips(): lax.ppermute(block, 'seq', [(x, x ^ m) for x in range(chips)])  2.68 us
    unnamed x38, local copies, waits for them, and re-layouts  1.48 us
  transfers between devices with their start and end apart: 12, of which 7 were waited for; matrix products, arithmetic and copies ran while one was open for 0% of the time, Pallas kernels for 14%

profile of v16, /device:TPU:1, one launch (start us, length us, event | category | flops | bytes accessed | tf_op | source)
XLA Modules:
  0.0 47.8 jit_solution(8241692544689212913)
XLA Ops:
  0.0 1.1 %copy-done.8 = bf16[32,32,256]{2,1,0:T(8,128)(2,1)S(1)} copy-done((bf16[32,32,256]{2,1,0:T(8,128)(2,1)S(1)}, bf16[32,32,256]{2,1,0:T(8,128)(2,1)}, u32[]{:S(2)}) %copy-start.8) | copy-done | bytes 524312
  1.1 0.4 norm.1.x_ref
  1.5 0.3 copy-done.11
  1.8 1.1 %pack.1 = (bf16[32,1152]{1,0:T(8,128)(2,1)S(1)}, bf16[32,1152]{1,0:T(8,128)(2,1)S(1)}) custom-call(f32[1024,256]{1,0:T(8,128)S(1)} %norm.1.x_ref, s32[32,32]{1,0:T(8,128)S(1)} %copy-done.13, s32[1,128]{1,0:T(1,128)S(1)} %bitcast.17, f32[1,256]{1,0:T(1,128)S(1)} %bitcast.22, f32[1,256]{1,0:T(1,128)S(1)} %bitcast.23, bf16[64,256]{1,0:T(8,128)(2,1)S(1)} %bitcast.21, ...), custom_call_target="tpu_custom_call" | custom-call | flops 1073741824 | bytes 1088256 | tf_op jit(solution)/shard_map/pack/pallas_call | solution.py:330
  2.9 0.1 collective-permute-start
  3.0 2.7 %collective-permute-start.3 = (bf16[32,1152]{1,0:T(8,128)(2,1)S(1)}, bf16[32,1152]{1,0:T(8,128)(2,1)S(1)}, u32[]{:S(2)}, u32[]{:S(2)}) collective-permute-start(bf16[32,1152]{1,0:T(8,128)(2,1)S(1)} %get-tuple-element.22.refs_0_), channel_id=1, source_target_pairs={{0,1},{1,0},{2,3},{3,2},{4,5},{5,4},{6,7},{7,6},{8,9},{9,8},{10,11... | collective-permute-start | bytes 221192 | tf_op jit(solution)/shard_map/ppermute | solution.py:300
  5.8 3.6 %collective-permute-start.2 = (bf16[2,32,1152]{2,1,0:T(8,128)(2,1)S(1)}, bf16[2,32,1152]{2,1,0:T(8,128)(2,1)S(1)}, u32[]{:S(2)}, u32[]{:S(2)}) collective-permute-start(bf16[2,32,1152]{2,1,0:T(8,128)(2,1)S(1)} %join.2._), channel_id=1, source_target_pairs={{0,4},{1,0},{2,12},{3,8},{4,5},{5,1},{6,13},{7,9},{8,6},{9,2},{10,... | collective-permute-start | bytes 442376 | tf_op jit(solution)/shard_map/ppermute | solution.py:306
  9.4 1.9 %collective-permute-start.1 = (bf16[2,32,1152]{2,1,0:T(8,128)(2,1)S(1)}, bf16[2,32,1152]{2,1,0:T(8,128)(2,1)S(1)}, u32[]{:S(2)}, u32[]{:S(2)}) collective-permute-start(bf16[2,32,1152]{2,1,0:T(8,128)(2,1)S(1)} %join.2._), channel_id=1, source_target_pairs={{0,0},{1,4},{2,8},{3,12},{4,1},{5,5},{6,9},{7,13},{8,2},{9,6},{10,... | collective-permute-start | bytes 442376 | tf_op jit(solution)/shard_map/ppermute | solution.py:306
  11.5 1.2 %base.1 = (f32[32,32,128]{2,1,0:T(8,128)S(1)}, bf16[4096,512]{1,0:T(8,128)(2,1)S(1)}) custom-call(bf16[32,32,128]{2,1,0:T(8,128)(2,1)S(1)} %copy-done.9, bf16[66,128]{1,0:T(8,128)(2,1)S(1)} %copy-done.12, s32[1,128]{1,0:T(1,128)S(1)} %bitcast.25, bf16[1024,128]{1,0:T(8,128)(2,1)S(1)} %copy-done.10, bf16[2,32,1152]{2,1,0:T(8,128)(2,1)S(1)} %join.2._), custom_call_target="tpu_custom_call" | custom-call | flops 1073741824 | bytes 689152 | tf_op jit(solution)/shard_map/base/pallas_call | solution.py:330
  12.7 0.8 %collective-permute-done.2.refs_1_ = bf16[2,32,1152]{2,1,0:T(8,128)(2,1)S(1)} collective-permute-done((bf16[2,32,1152]{2,1,0:T(8,128)(2,1)S(1)}, bf16[2,32,1152]{2,1,0:T(8,128)(2,1)S(1)}, u32[]{:S(2)}, u32[]{:S(2)}) %collective-permute-start.2) | collective-permute-done | bytes 147488 | tf_op jit(solution)/shard_map/ppermute | solution.py:306
  13.4 4.9 %collective-permute-done.1.refs_0_ = bf16[2,32,1152]{2,1,0:T(8,128)(2,1)S(1)} collective-permute-done((bf16[2,32,1152]{2,1,0:T(8,128)(2,1)S(1)}, bf16[2,32,1152]{2,1,0:T(8,128)(2,1)S(1)}, u32[]{:S(2)}, u32[]{:S(2)}) %collective-permute-start.1) | collective-permute-done | bytes 147488 | tf_op jit(solution)/shard_map/ppermute | solution.py:306
  18.3 0.5 turn.1
  18.8 3.1 %edges.1 = (bf16[32,32,128]{2,1,0:T(8,128)(2,1)S(1)}, bf16[32,32,128]{2,1,0:T(8,128)(2,1)S(1)}, bf16[32,32,128]{2,1,0:T(8,128)(2,1)S(1)}, bf16[1024,128]{1,0:T(8,128)(2,1)S(1)}) custom-call(bf16[1024,128]{1,0:T(8,128)(2,1)S(1)} %get-tuple-element.20.turned_ref, bf16[32,128]{1,0:T(8,128)(2,1)S(1)} %get-tuple-element.21.live_ref, ...), custom_call_target="tpu_custom_call" | custom-call | bytes 5451776 | tf_op jit(solution)/shard_map/edges/pallas_call | solution.py:330
  21.9 1.7 %collective-permute-start.5 = (bf16[32,32,128]{2,1,0:T(8,128)(2,1)S(1)}, bf16[32,32,128]{2,1,0:T(8,128)(2,1)S(1)}, u32[]{:S(2)}, u32[]{:S(2)}) collective-permute-start(bf16[32,32,128]{2,1,0:T(8,128)(2,1)S(1)} %get-tuple-element.25), channel_id=1, source_target_pairs={{8,0},{13,1},{11,2},{14,3},{9,4},{12,5},{10,6},{15,7},{0,8},{5,9},... | collective-permute-start | bytes 786440 | tf_op jit(solution)/shard_map/ppermute | solution.py:320
  23.7 1.9 %collective-permute-start.9 = (bf16[32,32,128]{2,1,0:T(8,128)(2,1)S(1)}, bf16[32,32,128]{2,1,0:T(8,128)(2,1)S(1)}, u32[]{:S(2)}, u32[]{:S(2)}) collective-permute-start(bf16[32,32,128]{2,1,0:T(8,128)(2,1)S(1)} %get-tuple-element.25), channel_id=1, source_target_pairs={{0,0},{4,1},{3,2},{7,3},{1,4},{5,5},{2,6},{6,7},{8,8},{12,9},{11,1... | collective-permute-start | bytes 786440 | tf_op jit(solution)/shard_map/ppermute | solution.py:320
  25.6 0.7 %collective-permute-start.8 = (bf16[32,32,128]{2,1,0:T(8,128)(2,1)S(1)}, bf16[32,32,128]{2,1,0:T(8,128)(2,1)S(1)}, u32[]{:S(2)}, u32[]{:S(2)}) collective-permute-start(bf16[32,32,128]{2,1,0:T(8,128)(2,1)S(1)} %get-tuple-element.25), channel_id=1, source_target_pairs={{1,0},{5,1},{2,2},{6,3},{0,4},{4,5},{3,6},{7,7},{9,8},{13,9},{10,1... | collective-permute-start | bytes 786440 | tf_op jit(solution)/shard_map/ppermute | solution.py:320
  26.3 8.5 %collective-permute-done.5.right_ref = bf16[32,32,128]{2,1,0:T(8,128)(2,1)S(1)} collective-permute-done((bf16[32,32,128]{2,1,0:T(8,128)(2,1)S(1)}, bf16[32,32,128]{2,1,0:T(8,128)(2,1)S(1)}, u32[]{:S(2)}, u32[]{:S(2)}) %collective-permute-start.5) | collective-permute-done | bytes 262176 | tf_op jit(solution)/shard_map/ppermute | solution.py:320
  34.7 0.2 collective-permute-start.6
  34.9 0.2 gate.1.refs_2_.gate_ref
  35.2 1.3 %triangle.3.far_ref = f32[1024,128]{1,0:T(8,128)S(1)} custom-call(bf16[32,32,128]{2,1,0:T(8,128)(2,1)S(1)} %collective-permute-done.5.right_ref, f32[2,1024,128]{2,1,0:T(8,128)S(1)} %panel.1.panel_ref), custom_call_target="tpu_custom_call" | custom-call | bytes 1310720 | tf_op jit(solution)/shard_map/triangle/pallas_call | solution.py:330
  36.5 3.7 %collective-permute-done.9.right_ref = bf16[32,32,128]{2,1,0:T(8,128)(2,1)S(1)} collective-permute-done((bf16[32,32,128]{2,1,0:T(8,128)(2,1)S(1)}, bf16[32,32,128]{2,1,0:T(8,128)(2,1)S(1)}, u32[]{:S(2)}, u32[]{:S(2)}) %collective-permute-start.9) | collective-permute-done | bytes 262176 | tf_op jit(solution)/shard_map/ppermute | solution.py:320
  40.3 1.3 %triangle.4.refs_0_ = f32[1024,128]{1,0:T(8,128)S(1)} custom-call(bf16[32,32,128]{2,1,0:T(8,128)(2,1)S(1)} %collective-permute-done.9.right_ref, f32[2,1024,128]{2,1,0:T(8,128)S(1)} %panel.1.panel_ref), custom_call_target="tpu_custom_call" | custom-call | bytes 1310720 | tf_op jit(solution)/shard_map/triangle/pallas_call | solution.py:330
  41.5 1.3 %triangle.5.near_ref = f32[1024,128]{1,0:T(8,128)S(1)} custom-call(bf16[32,32,128]{2,1,0:T(8,128)(2,1)S(1)} %collective-permute-done.8.right_ref, f32[2,1024,128]{2,1,0:T(8,128)S(1)} %panel.1.panel_ref, f32[1024,128]{1,0:T(8,128)S(1)} %triangle.4.refs_0_), custom_call_target="tpu_custom_call" | custom-call | bytes 1835008 | tf_op jit(solution)/shard_map/triangle/pallas_call | solution.py:330
  42.8 0.7 %collective-permute-done.6.right_ref = bf16[32,32,128]{2,1,0:T(8,128)(2,1)S(1)} collective-permute-done((bf16[32,32,128]{2,1,0:T(8,128)(2,1)S(1)}, bf16[32,32,128]{2,1,0:T(8,128)(2,1)S(1)}, u32[]{:S(2)}, u32[]{:S(2)}) %collective-permute-start.6) | collective-permute-done | bytes 262176 | tf_op jit(solution)/shard_map/ppermute | solution.py:324
  43.5 0.7 %last.3 = (f32[512,128]{1,0:T(8,128)S(1)}, bf16[512,128]{1,0:T(8,128)(2,1)S(1)}) custom-call(bf16[32,32,128]{2,1,0:T(8,128)(2,1)S(1)} %collective-permute-done.6.right_ref, f32[2,1024,128]{2,1,0:T(8,128)S(1)} %panel.1.panel_ref, f32[1024,128]{1,0:T(8,128)S(1)} %triangle.3.far_ref, f32[1024,128]{1,0:T(8,128)S(1)} %triangle.5.near_ref), custom_call_target="tpu_custom_call" | custom-call | flops 268435456 | bytes 2359296 | tf_op jit(solution)/shard_map/last/pallas_call | solution.py:330
  44.2 0.5 collective-permute-start.11
  44.6 0.7 %last.2 = (f32[512,128]{1,0:T(8,128)S(1)}, bf16[512,128]{1,0:T(8,128)(2,1)S(1)}) custom-call(bf16[32,32,128]{2,1,0:T(8,128)(2,1)S(1)} %collective-permute-done.6.right_ref, f32[2,1024,128]{2,1,0:T(8,128)S(1)} %panel.1.panel_ref, f32[1024,128]{1,0:T(8,128)S(1)} %triangle.3.far_ref, f32[1024,128]{1,0:T(8,128)S(1)} %triangle.5.near_ref), custom_call_target="tpu_custom_call" | custom-call | flops 268435456 | bytes 2359296 | tf_op jit(solution)/shard_map/last/pallas_call | solution.py:330
  45.3 0.2 collective-permute-start.10
  45.5 0.1 collective-permute-done.11.other_ref
  45.6 0.4 final.2.refs_0_
  46.0 0.7 %collective-permute-done.10.other_ref = bf16[512,128]{1,0:T(8,128)(2,1)S(1)} collective-permute-done((bf16[512,128]{1,0:T(8,128)(2,1)S(1)}, bf16[512,128]{1,0:T(8,128)(2,1)S(1)}, u32[]{:S(2)}, u32[]{:S(2)}) %collective-permute-start.10) | collective-permute-done | bytes 131104 | tf_op jit(solution)/shard_map/ppermute | solution.py:295
  46.7 1.0 %final.3 = bf16[32,32,128]{2,1,0:T(8,128)(2,1)} custom-call(f32[512,128]{1,0:T(8,128)S(1)} %get-tuple-element.28.own_ref, bf16[512,128]{1,0:T(8,128)(2,1)S(1)} %collective-permute-done.10.other_ref, bf16[32,32,128]{2,1,0:T(8,128)(2,1)S(1)} %get-tuple-element.30.updated_ref, f32[1024,128]{1,0:T(8,128)S(1)} %gate.1.refs_2_.gate_ref, f32[1,128]{1,0:T(1,128)S(1)} %bitcast.12, ...), custom_call_target="tpu_custom_call" | custom-call | flops 268435456 | bytes 1345024 | tf_op jit(solution)/shard_map/final/pallas_call | solution.py:330
  (47 shorter events, 0.3 us)
Async XLA Ops:
  0.0 1.5 %copy-start.5 = (s32[128]{0:T(128)S(1)}, s32[128]{0:T(128)}, u32[]{:S(2)}) copy-start(s32[128]{0:T(128)} %param.22) | copy-start | bytes 1540
  0.0 1.1 %copy-start.8 = (bf16[32,32,256]{2,1,0:T(8,128)(2,1)S(1)}, bf16[32,32,256]{2,1,0:T(8,128)(2,1)}, u32[]{:S(2)}) copy-start(bf16[32,32,256]{2,1,0:T(8,128)(2,1)} %x_ref.1) | copy-start | bytes 1572868
  1.1 0.8 %copy-start.11 = (bf16[256,64]{0,1:T(8,128)(2,1)S(1)}, bf16[256,64]{0,1:T(8,128)(2,1)}, u32[]{:S(2)}) copy-start(bf16[256,64]{0,1:T(8,128)(2,1)} %param.26) | copy-start | bytes 98308
  1.1 0.8 %copy-start.13 = (s32[32,32]{1,0:T(8,128)S(1)}, s32[32,32]{1,0:T(8,128)}, u32[]{:S(2)}) copy-start(s32[32,32]{1,0:T(8,128)} %mask_ref.1) | copy-start | bytes 12292
  1.1 0.8 %copy-start.14 = (f32[256]{0:T(256)S(1)}, f32[256]{0:T(256)}, u32[]{:S(2)}) copy-start(f32[256]{0:T(256)} %param.24) | copy-start | bytes 3076
  1.1 0.8 %copy-start.15 = (f32[256]{0:T(256)S(1)}, f32[256]{0:T(256)}, u32[]{:S(2)}) copy-start(f32[256]{0:T(256)} %param.25) | copy-start | bytes 3076
  1.1 0.8 %copy-start.16 = (f32[64]{0:T(128)S(1)}, f32[64]{0:T(128)}, u32[]{:S(2)}) copy-start(f32[64]{0:T(128)} %param.27) | copy-start | bytes 772
  1.1 4.6 %copy-start.18 = (f32[640]{0:T(1024)S(1)}, f32[640]{0:T(1024)}, u32[]{:S(2)}) copy-start(f32[640]{0:T(1024)} %param.33) | copy-start | bytes 7684
  2.9 2.8 %collective-permute-start = (bf16[32,1152]{1,0:T(8,128)(2,1)S(1)}, bf16[32,1152]{1,0:T(8,128)(2,1)S(1)}, u32[]{:S(2)}, u32[]{:S(2)}) collective-permute-start(bf16[32,1152]{1,0:T(8,128)(2,1)S(1)} %get-tuple-element.19.refs_0_), channel_id=1, source_target_pairs={{0,2},{1,3},{2,0},{3,1},{4,6},{5,7},{6,4},{7,5},{8,10},{9,11},{10,... | collective-permute-start | bytes 221192 | tf_op jit(solution)/shard_map/ppermute | solution.py:295
  3.0 8.3 %collective-permute-start.3 = (bf16[32,1152]{1,0:T(8,128)(2,1)S(1)}, bf16[32,1152]{1,0:T(8,128)(2,1)S(1)}, u32[]{:S(2)}, u32[]{:S(2)}) collective-permute-start(bf16[32,1152]{1,0:T(8,128)(2,1)S(1)} %get-tuple-element.22.refs_0_), channel_id=1, source_target_pairs={{0,1},{1,0},{2,3},{3,2},{4,5},{5,4},{6,7},{7,6},{8,9},{9,8},{10,11... | collective-permute-start | bytes 221192 | tf_op jit(solution)/shard_map/ppermute | solution.py:300
  5.8 5.7 %copy-start.9 = (bf16[32,32,128]{2,1,0:T(8,128)(2,1)S(1)}, bf16[32,32,128]{2,1,0:T(8,128)(2,1)}, u32[]{:S(2)}) copy-start(bf16[32,32,128]{2,1,0:T(8,128)(2,1)} %pair_ref.1) | copy-start | bytes 786436
  5.8 5.7 %copy-start.10 = (bf16[1024,128]{1,0:T(8,128)(2,1)S(1)}, bf16[1024,128]{1,0:T(8,128)(2,1)}, u32[]{:S(2)}) copy-start(bf16[1024,128]{1,0:T(8,128)(2,1)} %w_ref.5) | copy-start | bytes 786436
  5.8 5.7 %copy-start.12 = (bf16[66,128]{1,0:T(8,128)(2,1)S(1)}, bf16[66,128]{1,0:T(8,128)(2,1)}, u32[]{:S(2)}) copy-start(bf16[66,128]{1,0:T(8,128)(2,1)} %table_ref.1) | copy-start | bytes 50692
  5.8 5.7 %copy-start.17 = (s32[128]{0:T(128)S(1)}, s32[128]{0:T(128)}, u32[]{:S(2)}) copy-start(s32[128]{0:T(128)} %param.23) | copy-start | bytes 1540
  5.8 7.6 %collective-permute-start.2 = (bf16[2,32,1152]{2,1,0:T(8,128)(2,1)S(1)}, bf16[2,32,1152]{2,1,0:T(8,128)(2,1)S(1)}, u32[]{:S(2)}, u32[]{:S(2)}) collective-permute-start(bf16[2,32,1152]{2,1,0:T(8,128)(2,1)S(1)} %join.2._), channel_id=1, source_target_pairs={{0,4},{1,0},{2,12},{3,8},{4,5},{5,1},{6,13},{7,9},{8,6},{9,2},{10,... | collective-permute-start | bytes 442376 | tf_op jit(solution)/shard_map/ppermute | solution.py:306
  9.4 8.9 %collective-permute-start.1 = (bf16[2,32,1152]{2,1,0:T(8,128)(2,1)S(1)}, bf16[2,32,1152]{2,1,0:T(8,128)(2,1)S(1)}, u32[]{:S(2)}, u32[]{:S(2)}) collective-permute-start(bf16[2,32,1152]{2,1,0:T(8,128)(2,1)S(1)} %join.2._), channel_id=1, source_target_pairs={{0,0},{1,4},{2,8},{3,12},{4,1},{5,5},{6,9},{7,13},{8,2},{9,6},{10,... | collective-permute-start | bytes 442376 | tf_op jit(solution)/shard_map/ppermute | solution.py:306
  11.3 7.5 %collective-permute-start.4 = (bf16[2,32,1152]{2,1,0:T(8,128)(2,1)S(1)}, bf16[2,32,1152]{2,1,0:T(8,128)(2,1)S(1)}, u32[]{:S(2)}, u32[]{:S(2)}) collective-permute-start(bf16[2,32,1152]{2,1,0:T(8,128)(2,1)S(1)} %join.3.own_ref), channel_id=1, source_target_pairs={{0,2},{1,3},{2,0},{3,1},{4,6},{5,7},{6,4},{7,5},{8,10},{9,11},{10,... | collective-permute-start | bytes 442376 | tf_op jit(solution)/shard_map/ppermute | solution.py:295
  12.6 6.2 %copy-start = (bf16[128,640]{1,0:T(8,128)(2,1)S(1)}, bf16[128,640]{1,0:T(8,128)(2,1)}, u32[]{:S(2)}) copy-start(bf16[128,640]{1,0:T(8,128)(2,1)} %w_ref.7) | copy-start | bytes 491524
  12.6 6.2 %copy-start.6 = (f32[128]{0:T(128)S(1)}, f32[128]{0:T(128)}, u32[]{:S(2)}) copy-start(f32[128]{0:T(128)} %param.30) | copy-start | bytes 1540
  12.7 6.2 %copy-start.7 = (f32[128]{0:T(128)S(1)}, f32[128]{0:T(128)}, u32[]{:S(2)}) copy-start(f32[128]{0:T(128)} %param.31) | copy-start | bytes 1540
  21.9 12.8 %collective-permute-start.5 = (bf16[32,32,128]{2,1,0:T(8,128)(2,1)S(1)}, bf16[32,32,128]{2,1,0:T(8,128)(2,1)S(1)}, u32[]{:S(2)}, u32[]{:S(2)}) collective-permute-start(bf16[32,32,128]{2,1,0:T(8,128)(2,1)S(1)} %get-tuple-element.25), channel_id=1, source_target_pairs={{8,0},{13,1},{11,2},{14,3},{9,4},{12,5},{10,6},{15,7},{0,8},{5,9},... | collective-permute-start | bytes 786440 | tf_op jit(solution)/shard_map/ppermute | solution.py:320
  23.7 11.5 %collective-permute-start.7 = (bf16[32,32,128]{2,1,0:T(8,128)(2,1)S(1)}, bf16[32,32,128]{2,1,0:T(8,128)(2,1)S(1)}, u32[]{:S(2)}, u32[]{:S(2)}) collective-permute-start(bf16[32,32,128]{2,1,0:T(8,128)(2,1)S(1)} %get-tuple-element.26.refs_0_), channel_id=1, source_target_pairs={{0,1},{1,0},{2,3},{3,2},{4,5},{5,4},{6,7},{7,6},{8,9},{9,8},{10,11... | collective-permute-start | bytes 786440 | tf_op jit(solution)/shard_map/ppermute | solution.py:300
  23.7 16.6 %collective-permute-start.9 = (bf16[32,32,128]{2,1,0:T(8,128)(2,1)S(1)}, bf16[32,32,128]{2,1,0:T(8,128)(2,1)S(1)}, u32[]{:S(2)}, u32[]{:S(2)}) collective-permute-start(bf16[32,32,128]{2,1,0:T(8,128)(2,1)S(1)} %get-tuple-element.25), channel_id=1, source_target_pairs={{0,0},{4,1},{3,2},{7,3},{1,4},{5,5},{2,6},{6,7},{8,8},{12,9},{11,1... | collective-permute-start | bytes 786440 | tf_op jit(solution)/shard_map/ppermute | solution.py:320
  25.6 16.0 %collective-permute-start.8 = (bf16[32,32,128]{2,1,0:T(8,128)(2,1)S(1)}, bf16[32,32,128]{2,1,0:T(8,128)(2,1)S(1)}, u32[]{:S(2)}, u32[]{:S(2)}) collective-permute-start(bf16[32,32,128]{2,1,0:T(8,128)(2,1)S(1)} %get-tuple-element.25), channel_id=1, source_target_pairs={{1,0},{5,1},{2,2},{6,3},{0,4},{4,5},{3,6},{7,7},{9,8},{13,9},{10,1... | collective-permute-start | bytes 786440 | tf_op jit(solution)/shard_map/ppermute | solution.py:320
  34.7 8.8 %collective-permute-start.6 = (bf16[32,32,128]{2,1,0:T(8,128)(2,1)S(1)}, bf16[32,32,128]{2,1,0:T(8,128)(2,1)S(1)}, u32[]{:S(2)}, u32[]{:S(2)}) collective-permute-start(bf16[32,32,128]{2,1,0:T(8,128)(2,1)S(1)} %collective-permute-done.5.right_ref), channel_id=1, source_target_pairs={{0,4},{4,0},{8,12},{12,8},{1,5},{5,1},{9,13},{13,9},{2,6},{6,2},{1... | collective-permute-start | bytes 786440 | tf_op jit(solution)/shard_map/ppermute | solution.py:324
  36.5 9.1 %copy-start.1 = (bf16[128,128]{1,0:T(8,128)(2,1)S(1)}, bf16[128,128]{1,0:T(8,128)(2,1)}, u32[]{:S(2)}) copy-start(bf16[128,128]{1,0:T(8,128)(2,1)} %w_ref.9) | copy-start | bytes 98308
  36.5 9.1 %copy-start.2 = (f32[128]{0:T(128)S(1)}, f32[128]{0:T(128)}, u32[]{:S(2)}) copy-start(f32[128]{0:T(128)} %param.34) | copy-start | bytes 1540
  36.5 9.1 %copy-start.3 = (f32[128]{0:T(128)S(1)}, f32[128]{0:T(128)}, u32[]{:S(2)}) copy-start(f32[128]{0:T(128)} %param.35) | copy-start | bytes 1540
  36.5 9.1 %copy-start.4 = (f32[128]{0:T(128)S(1)}, f32[128]{0:T(128)}, u32[]{:S(2)}) copy-start(f32[128]{0:T(128)} %param.37) | copy-start | bytes 1540
  44.2 1.4 %collective-permute-start.11 = (bf16[512,128]{1,0:T(8,128)(2,1)S(1)}, bf16[512,128]{1,0:T(8,128)(2,1)S(1)}, u32[]{:S(2)}, u32[]{:S(2)}) collective-permute-start(bf16[512,128]{1,0:T(8,128)(2,1)S(1)} %get-tuple-element.32), channel_id=1, source_target_pairs={{0,2},{1,3},{2,0},{3,1},{4,6},{5,7},{6,4},{7,5},{8,10},{9,11},{10,... | collective-permute-start | bytes 393224 | tf_op jit(solution)/shard_map/ppermute | solution.py:295
  45.3 1.4 %collective-permute-start.10 = (bf16[512,128]{1,0:T(8,128)(2,1)S(1)}, bf16[512,128]{1,0:T(8,128)(2,1)S(1)}, u32[]{:S(2)}, u32[]{:S(2)}) collective-permute-start(bf16[512,128]{1,0:T(8,128)(2,1)S(1)} %get-tuple-element.29), channel_id=1, source_target_pairs={{0,2},{1,3},{2,0},{3,1},{4,6},{5,7},{6,4},{7,5},{8,10},{9,11},{10,... | collective-permute-start | bytes 393224 | tf_op jit(solution)/shard_map/ppermute | solution.py:295

commit v17 on v16

--- a/solution.py
+++ b/solution.py
@@ -206,7 +206,7 @@
 
 
 def source_of(z, core, x, step, chips):
-    block = z ^ step ^ ((x + core) % 2 if step >= chips else core % 2)
+    block = z ^ step ^ ((x + core) % 2 if step >= chips else 0)
     return block // chips, block % chips
 
 
@@ -430,9 +430,9 @@
         sums[:] = [call(
             functools.partial(step_kernel, step, chips, 0, not sums), block_sums, [scratch],
             [right_edges[step], panel] + sums, name="triangle")]
-    part = rows // 2
+    parts = ((0, rows * 3 // 4), (rows * 3 // 4, rows // 4))
     own_sums, other_sums, result = [], [], []
-    for first in (0, part):
+    for first, part in parts:
         own, half_sums = call(
             functools.partial(last_kernel, count - 1, chips, first),
             [shape((part * cols, channels), F32), shape((part * cols, channels), BF16)],
@@ -440,14 +440,14 @@
             [right_edges[-1], panel] + far + near, flops=1 << 28, name="last")
         own_sums.append(own)
         other_sums.append(swap_cores(half_sums, count))
-    for n, first in enumerate((0, part)):
+    for n, (first, part) in enumerate(parts):
         args = [own_sums[n], other_sums[n], updated, gate, flat(triangle_sum_norm_gain),
                 flat(triangle_sum_norm_bias), triangle_output_weight, flat(outer_pair_bias)]
-        half_shape = (part, cols, channels)
+        part_shape = (part, cols, channels)
         result = [call(
             functools.partial(final_kernel, first),
-            shape((rows, cols, channels) if n else half_shape, BF16),
-            [pltpu.VMEM(half_shape, BF16), pltpu.SemaphoreType.DMA((1 + part // 8,))] if n else [],
+            shape((rows, cols, channels) if n else part_shape, BF16),
+            [pltpu.VMEM(part_shape, BF16), pltpu.SemaphoreType.DMA((1 + part // 8,))] if n else [],
             args + result, flops=1 << 28, hbm=n == 1, name="final")]
     return result[0]
 

time: 48.1 us -> 48 us (level)
  waiting for transfers between devices: 19.4 us -> 17.3 us
  starting transfers between devices: 13.5 us -> 15.5 us
    ppermute x3, waiting for transfers between devices: 12.2 us -> 8.91 us  [send_same_core(): return lax.ppermute(block, GROUP, pairs)]
    ppermute x3, starting transfers between devices: 4.31 us -> 6.32 us  [send_same_core(): return lax.ppermute(block, GROUP, pairs)]
    ppermute x1, waiting for transfers between devices: 0.66 us -> 1.88 us  [pass_on(): return lax.ppermute(block, 'resi', [(z, z ^ 1) for z in range(count)])]
where the time goes in v17:
time: 48 us; the launch traced here: 47.6 us
  waiting for transfers between devices  17.3 us (36%)
  starting transfers between devices  15.5 us (32%)
  Pallas kernels  13 us (27%)
  local copies, waits for them, and re-layouts  1.48 us (3%)
    pallas_call x16, Pallas kernels, call(): pl.pallas_call(kernel, out_shape=outs, in_specs=[vmem] * len(args), out_s...  13 us
    ppermute x3, waiting for transfers between devices, send_same_core(): return lax.ppermute(block, GROUP, pairs)  8.91 us
    ppermute x3, starting transfers between devices, send_same_core(): return lax.ppermute(block, GROUP, pairs)  6.32 us
    ppermute x2, waiting for transfers between devices, send_turned(): lax.ppermute(block, GROUP, [(z * count + p, (p ^ m) * count + z) for z in...  5.66 us
    ppermute x2, starting transfers between devices, send_turned(): lax.ppermute(block, GROUP, [(z * count + p, (p ^ m) * count + z) for z in...  5.51 us
    ppermute x2, starting transfers between devices, send_chips(): lax.ppermute(block, 'seq', [(x, x ^ m) for x in range(chips)])  2.68 us
    ppermute x1, waiting for transfers between devices, pass_on(): return lax.ppermute(block, 'resi', [(z, z ^ 1) for z in range(count)])  1.88 us
    unnamed x38, local copies, waits for them, and re-layouts  1.48 us
  transfers between devices with their start and end apart: 12, of which 7 were waited for; matrix products, arithmetic and copies ran while one was open for 0% of the time, Pallas kernels for 14%

profile of v17, /device:TPU:1, one launch (start us, length us, event | category | flops | bytes accessed | tf_op | source)
XLA Modules:
  0.0 47.6 jit_solution(5348598675782869476)
XLA Ops:
  0.0 1.1 %copy-done.8 = bf16[32,32,256]{2,1,0:T(8,128)(2,1)S(1)} copy-done((bf16[32,32,256]{2,1,0:T(8,128)(2,1)S(1)}, bf16[32,32,256]{2,1,0:T(8,128)(2,1)}, u32[]{:S(2)}) %copy-start.8) | copy-done | bytes 524312
  1.1 0.4 norm.1.x_ref
  1.5 0.3 copy-done.11
  1.8 1.1 %pack.1 = (bf16[32,1152]{1,0:T(8,128)(2,1)S(1)}, bf16[32,1152]{1,0:T(8,128)(2,1)S(1)}) custom-call(f32[1024,256]{1,0:T(8,128)S(1)} %norm.1.x_ref, s32[32,32]{1,0:T(8,128)S(1)} %copy-done.13, s32[1,128]{1,0:T(1,128)S(1)} %bitcast.17, f32[1,256]{1,0:T(1,128)S(1)} %bitcast.22, f32[1,256]{1,0:T(1,128)S(1)} %bitcast.23, bf16[64,256]{1,0:T(8,128)(2,1)S(1)} %bitcast.21, ...), custom_call_target="tpu_custom_call" | custom-call | flops 1073741824 | bytes 1088256 | tf_op jit(solution)/shard_map/pack/pallas_call | solution.py:330
  2.9 0.1 collective-permute-start
  3.0 2.7 %collective-permute-start.3 = (bf16[32,1152]{1,0:T(8,128)(2,1)S(1)}, bf16[32,1152]{1,0:T(8,128)(2,1)S(1)}, u32[]{:S(2)}, u32[]{:S(2)}) collective-permute-start(bf16[32,1152]{1,0:T(8,128)(2,1)S(1)} %get-tuple-element.22.refs_0_), channel_id=1, source_target_pairs={{0,1},{1,0},{2,3},{3,2},{4,5},{5,4},{6,7},{7,6},{8,9},{9,8},{10,11... | collective-permute-start | bytes 221192 | tf_op jit(solution)/shard_map/ppermute | solution.py:300
  5.8 3.6 %collective-permute-start.2 = (bf16[2,32,1152]{2,1,0:T(8,128)(2,1)S(1)}, bf16[2,32,1152]{2,1,0:T(8,128)(2,1)S(1)}, u32[]{:S(2)}, u32[]{:S(2)}) collective-permute-start(bf16[2,32,1152]{2,1,0:T(8,128)(2,1)S(1)} %join.2._), channel_id=1, source_target_pairs={{0,4},{1,0},{2,12},{3,8},{4,5},{5,1},{6,13},{7,9},{8,6},{9,2},{10,... | collective-permute-start | bytes 442376 | tf_op jit(solution)/shard_map/ppermute | solution.py:306
  9.4 1.9 %collective-permute-start.1 = (bf16[2,32,1152]{2,1,0:T(8,128)(2,1)S(1)}, bf16[2,32,1152]{2,1,0:T(8,128)(2,1)S(1)}, u32[]{:S(2)}, u32[]{:S(2)}) collective-permute-start(bf16[2,32,1152]{2,1,0:T(8,128)(2,1)S(1)} %join.2._), channel_id=1, source_target_pairs={{0,0},{1,4},{2,8},{3,12},{4,1},{5,5},{6,9},{7,13},{8,2},{9,6},{10,... | collective-permute-start | bytes 442376 | tf_op jit(solution)/shard_map/ppermute | solution.py:306
  11.5 1.2 %base.1 = (f32[32,32,128]{2,1,0:T(8,128)S(1)}, bf16[4096,512]{1,0:T(8,128)(2,1)S(1)}) custom-call(bf16[32,32,128]{2,1,0:T(8,128)(2,1)S(1)} %copy-done.9, bf16[66,128]{1,0:T(8,128)(2,1)S(1)} %copy-done.12, s32[1,128]{1,0:T(1,128)S(1)} %bitcast.25, bf16[1024,128]{1,0:T(8,128)(2,1)S(1)} %copy-done.10, bf16[2,32,1152]{2,1,0:T(8,128)(2,1)S(1)} %join.2._), custom_call_target="tpu_custom_call" | custom-call | flops 1073741824 | bytes 689152 | tf_op jit(solution)/shard_map/base/pallas_call | solution.py:330
  12.7 0.8 %collective-permute-done.2.refs_1_ = bf16[2,32,1152]{2,1,0:T(8,128)(2,1)S(1)} collective-permute-done((bf16[2,32,1152]{2,1,0:T(8,128)(2,1)S(1)}, bf16[2,32,1152]{2,1,0:T(8,128)(2,1)S(1)}, u32[]{:S(2)}, u32[]{:S(2)}) %collective-permute-start.2) | collective-permute-done | bytes 147488 | tf_op jit(solution)/shard_map/ppermute | solution.py:306
  13.4 4.9 %collective-permute-done.1.refs_0_ = bf16[2,32,1152]{2,1,0:T(8,128)(2,1)S(1)} collective-permute-done((bf16[2,32,1152]{2,1,0:T(8,128)(2,1)S(1)}, bf16[2,32,1152]{2,1,0:T(8,128)(2,1)S(1)}, u32[]{:S(2)}, u32[]{:S(2)}) %collective-permute-start.1) | collective-permute-done | bytes 147488 | tf_op jit(solution)/shard_map/ppermute | solution.py:306
  18.3 0.5 turn.1
  18.8 3.1 %edges.1 = (bf16[32,32,128]{2,1,0:T(8,128)(2,1)S(1)}, bf16[32,32,128]{2,1,0:T(8,128)(2,1)S(1)}, bf16[32,32,128]{2,1,0:T(8,128)(2,1)S(1)}, bf16[1024,128]{1,0:T(8,128)(2,1)S(1)}) custom-call(bf16[1024,128]{1,0:T(8,128)(2,1)S(1)} %get-tuple-element.20.turned_ref, bf16[32,128]{1,0:T(8,128)(2,1)S(1)} %get-tuple-element.21.live_ref, ...), custom_call_target="tpu_custom_call" | custom-call | bytes 5451776 | tf_op jit(solution)/shard_map/edges/pallas_call | solution.py:330
  21.9 1.7 %collective-permute-start.5 = (bf16[32,32,128]{2,1,0:T(8,128)(2,1)S(1)}, bf16[32,32,128]{2,1,0:T(8,128)(2,1)S(1)}, u32[]{:S(2)}, u32[]{:S(2)}) collective-permute-start(bf16[32,32,128]{2,1,0:T(8,128)(2,1)S(1)} %get-tuple-element.25), channel_id=1, source_target_pairs={{8,0},{13,1},{11,2},{14,3},{9,4},{12,5},{10,6},{15,7},{0,8},{5,9},... | collective-permute-start | bytes 786440 | tf_op jit(solution)/shard_map/ppermute | solution.py:320
  23.7 0.7 %collective-permute-start.9 = (bf16[32,32,128]{2,1,0:T(8,128)(2,1)S(1)}, bf16[32,32,128]{2,1,0:T(8,128)(2,1)S(1)}, u32[]{:S(2)}, u32[]{:S(2)}) collective-permute-start(bf16[32,32,128]{2,1,0:T(8,128)(2,1)S(1)} %get-tuple-element.25), channel_id=1, source_target_pairs={{0,0},{4,1},{2,2},{6,3},{1,4},{5,5},{3,6},{7,7},{8,8},{12,9},{10,1... | collective-permute-start | bytes 786440 | tf_op jit(solution)/shard_map/ppermute | solution.py:320
  24.3 3.9 %collective-permute-start.8 = (bf16[32,32,128]{2,1,0:T(8,128)(2,1)S(1)}, bf16[32,32,128]{2,1,0:T(8,128)(2,1)S(1)}, u32[]{:S(2)}, u32[]{:S(2)}) collective-permute-start(bf16[32,32,128]{2,1,0:T(8,128)(2,1)S(1)} %get-tuple-element.25), channel_id=1, source_target_pairs={{1,0},{5,1},{3,2},{7,3},{0,4},{4,5},{2,6},{6,7},{9,8},{13,9},{11,1... | collective-permute-start | bytes 786440 | tf_op jit(solution)/shard_map/ppermute | solution.py:320
  28.3 6.5 %collective-permute-done.5.right_ref = bf16[32,32,128]{2,1,0:T(8,128)(2,1)S(1)} collective-permute-done((bf16[32,32,128]{2,1,0:T(8,128)(2,1)S(1)}, bf16[32,32,128]{2,1,0:T(8,128)(2,1)S(1)}, u32[]{:S(2)}, u32[]{:S(2)}) %collective-permute-start.5) | collective-permute-done | bytes 262176 | tf_op jit(solution)/shard_map/ppermute | solution.py:320
  34.7 0.2 collective-permute-start.6
  34.9 0.2 gate.1.refs_2_.gate_ref
  35.1 0.1 panel.1.panel_ref
  35.2 1.3 %triangle.3.far_ref = f32[1024,128]{1,0:T(8,128)S(1)} custom-call(bf16[32,32,128]{2,1,0:T(8,128)(2,1)S(1)} %collective-permute-done.5.right_ref, f32[2,1024,128]{2,1,0:T(8,128)S(1)} %panel.1.panel_ref), custom_call_target="tpu_custom_call" | custom-call | bytes 1310720 | tf_op jit(solution)/shard_map/triangle/pallas_call | solution.py:330
  36.5 1.3 %triangle.4.refs_0_ = f32[1024,128]{1,0:T(8,128)S(1)} custom-call(bf16[32,32,128]{2,1,0:T(8,128)(2,1)S(1)} %collective-permute-done.9.right_ref, f32[2,1024,128]{2,1,0:T(8,128)S(1)} %panel.1.panel_ref), custom_call_target="tpu_custom_call" | custom-call | bytes 1310720 | tf_op jit(solution)/shard_map/triangle/pallas_call | solution.py:330
  37.8 2.4 %collective-permute-done.8.right_ref = bf16[32,32,128]{2,1,0:T(8,128)(2,1)S(1)} collective-permute-done((bf16[32,32,128]{2,1,0:T(8,128)(2,1)S(1)}, bf16[32,32,128]{2,1,0:T(8,128)(2,1)S(1)}, u32[]{:S(2)}, u32[]{:S(2)}) %collective-permute-start.8) | collective-permute-done | bytes 262176 | tf_op jit(solution)/shard_map/ppermute | solution.py:320
  40.3 1.3 %triangle.5.near_ref = f32[1024,128]{1,0:T(8,128)S(1)} custom-call(bf16[32,32,128]{2,1,0:T(8,128)(2,1)S(1)} %collective-permute-done.8.right_ref, f32[2,1024,128]{2,1,0:T(8,128)S(1)} %panel.1.panel_ref, f32[1024,128]{1,0:T(8,128)S(1)} %triangle.4.refs_0_), custom_call_target="tpu_custom_call" | custom-call | bytes 1835008 | tf_op jit(solution)/shard_map/triangle/pallas_call | solution.py:330
  41.5 1.9 %collective-permute-done.6.right_ref = bf16[32,32,128]{2,1,0:T(8,128)(2,1)S(1)} collective-permute-done((bf16[32,32,128]{2,1,0:T(8,128)(2,1)S(1)}, bf16[32,32,128]{2,1,0:T(8,128)(2,1)S(1)}, u32[]{:S(2)}, u32[]{:S(2)}) %collective-permute-start.6) | collective-permute-done | bytes 262176 | tf_op jit(solution)/shard_map/ppermute | solution.py:324
  43.4 1.0 %last.3 = (f32[768,128]{1,0:T(8,128)S(1)}, bf16[768,128]{1,0:T(8,128)(2,1)S(1)}) custom-call(bf16[32,32,128]{2,1,0:T(8,128)(2,1)S(1)} %collective-permute-done.6.right_ref, f32[2,1024,128]{2,1,0:T(8,128)S(1)} %panel.1.panel_ref, f32[1024,128]{1,0:T(8,128)S(1)} %triangle.3.far_ref, f32[1024,128]{1,0:T(8,128)S(1)} %triangle.5.near_ref), custom_call_target="tpu_custom_call" | custom-call | flops 268435456 | bytes 2359296 | tf_op jit(solution)/shard_map/last/pallas_call | solution.py:330
  44.4 0.6 %collective-permute-start.11 = (bf16[768,128]{1,0:T(8,128)(2,1)S(1)}, bf16[768,128]{1,0:T(8,128)(2,1)S(1)}, u32[]{:S(2)}, u32[]{:S(2)}) collective-permute-start(bf16[768,128]{1,0:T(8,128)(2,1)S(1)} %get-tuple-element.32), channel_id=1, source_target_pairs={{0,2},{1,3},{2,0},{3,1},{4,6},{5,7},{6,4},{7,5},{8,10},{9,11},{10,... | collective-permute-start | bytes 589832 | tf_op jit(solution)/shard_map/ppermute | solution.py:295
  45.0 0.3 last.2
  45.4 0.7 %collective-permute-done.11.other_ref = bf16[768,128]{1,0:T(8,128)(2,1)S(1)} collective-permute-done((bf16[768,128]{1,0:T(8,128)(2,1)S(1)}, bf16[768,128]{1,0:T(8,128)(2,1)S(1)}, u32[]{:S(2)}, u32[]{:S(2)}) %collective-permute-start.11) | collective-permute-done | bytes 196640 | tf_op jit(solution)/shard_map/ppermute | solution.py:295
  46.1 0.4 final.2.refs_0_
  46.5 0.2 collective-permute-done.10.other_ref
  46.6 1.0 %final.3 = bf16[32,32,128]{2,1,0:T(8,128)(2,1)} custom-call(f32[256,128]{1,0:T(8,128)S(1)} %get-tuple-element.28.own_ref, bf16[256,128]{1,0:T(8,128)(2,1)S(1)} %collective-permute-done.10.other_ref, bf16[32,32,128]{2,1,0:T(8,128)(2,1)S(1)} %get-tuple-element.30.updated_ref, f32[1024,128]{1,0:T(8,128)S(1)} %gate.1.refs_2_.gate_ref, f32[1,128]{1,0:T(1,128)S(1)} %bitcast.12, ...), custom_call_target="tpu_custom_call" | custom-call | flops 268435456 | bytes 1213952 | tf_op jit(solution)/shard_map/final/pallas_call | solution.py:330
  (47 shorter events, 0.3 us)
Async XLA Ops:
  0.0 1.5 %copy-start.5 = (s32[128]{0:T(128)S(1)}, s32[128]{0:T(128)}, u32[]{:S(2)}) copy-start(s32[128]{0:T(128)} %param.22) | copy-start | bytes 1540
  0.0 1.1 %copy-start.8 = (bf16[32,32,256]{2,1,0:T(8,128)(2,1)S(1)}, bf16[32,32,256]{2,1,0:T(8,128)(2,1)}, u32[]{:S(2)}) copy-start(bf16[32,32,256]{2,1,0:T(8,128)(2,1)} %x_ref.1) | copy-start | bytes 1572868
  1.1 0.8 %copy-start.11 = (bf16[256,64]{0,1:T(8,128)(2,1)S(1)}, bf16[256,64]{0,1:T(8,128)(2,1)}, u32[]{:S(2)}) copy-start(bf16[256,64]{0,1:T(8,128)(2,1)} %param.26) | copy-start | bytes 98308
  1.1 0.8 %copy-start.13 = (s32[32,32]{1,0:T(8,128)S(1)}, s32[32,32]{1,0:T(8,128)}, u32[]{:S(2)}) copy-start(s32[32,32]{1,0:T(8,128)} %mask_ref.1) | copy-start | bytes 12292
  1.1 0.8 %copy-start.14 = (f32[256]{0:T(256)S(1)}, f32[256]{0:T(256)}, u32[]{:S(2)}) copy-start(f32[256]{0:T(256)} %param.24) | copy-start | bytes 3076
  1.1 0.8 %copy-start.15 = (f32[256]{0:T(256)S(1)}, f32[256]{0:T(256)}, u32[]{:S(2)}) copy-start(f32[256]{0:T(256)} %param.25) | copy-start | bytes 3076
  1.1 0.8 %copy-start.16 = (f32[64]{0:T(128)S(1)}, f32[64]{0:T(128)}, u32[]{:S(2)}) copy-start(f32[64]{0:T(128)} %param.27) | copy-start | bytes 772
  1.1 4.6 %copy-start.18 = (f32[640]{0:T(1024)S(1)}, f32[640]{0:T(1024)}, u32[]{:S(2)}) copy-start(f32[640]{0:T(1024)} %param.33) | copy-start | bytes 7684
  2.9 2.8 %collective-permute-start = (bf16[32,1152]{1,0:T(8,128)(2,1)S(1)}, bf16[32,1152]{1,0:T(8,128)(2,1)S(1)}, u32[]{:S(2)}, u32[]{:S(2)}) collective-permute-start(bf16[32,1152]{1,0:T(8,128)(2,1)S(1)} %get-tuple-element.19.refs_0_), channel_id=1, source_target_pairs={{0,2},{1,3},{2,0},{3,1},{4,6},{5,7},{6,4},{7,5},{8,10},{9,11},{10,... | collective-permute-start | bytes 221192 | tf_op jit(solution)/shard_map/ppermute | solution.py:295
  3.0 8.3 %collective-permute-start.3 = (bf16[32,1152]{1,0:T(8,128)(2,1)S(1)}, bf16[32,1152]{1,0:T(8,128)(2,1)S(1)}, u32[]{:S(2)}, u32[]{:S(2)}) collective-permute-start(bf16[32,1152]{1,0:T(8,128)(2,1)S(1)} %get-tuple-element.22.refs_0_), channel_id=1, source_target_pairs={{0,1},{1,0},{2,3},{3,2},{4,5},{5,4},{6,7},{7,6},{8,9},{9,8},{10,11... | collective-permute-start | bytes 221192 | tf_op jit(solution)/shard_map/ppermute | solution.py:300
  5.8 5.7 %copy-start.9 = (bf16[32,32,128]{2,1,0:T(8,128)(2,1)S(1)}, bf16[32,32,128]{2,1,0:T(8,128)(2,1)}, u32[]{:S(2)}) copy-start(bf16[32,32,128]{2,1,0:T(8,128)(2,1)} %pair_ref.1) | copy-start | bytes 786436
  5.8 5.7 %copy-start.10 = (bf16[1024,128]{1,0:T(8,128)(2,1)S(1)}, bf16[1024,128]{1,0:T(8,128)(2,1)}, u32[]{:S(2)}) copy-start(bf16[1024,128]{1,0:T(8,128)(2,1)} %w_ref.5) | copy-start | bytes 786436
  5.8 5.7 %copy-start.12 = (bf16[66,128]{1,0:T(8,128)(2,1)S(1)}, bf16[66,128]{1,0:T(8,128)(2,1)}, u32[]{:S(2)}) copy-start(bf16[66,128]{1,0:T(8,128)(2,1)} %table_ref.1) | copy-start | bytes 50692
  5.8 5.7 %copy-start.17 = (s32[128]{0:T(128)S(1)}, s32[128]{0:T(128)}, u32[]{:S(2)}) copy-start(s32[128]{0:T(128)} %param.23) | copy-start | bytes 1540
  5.8 7.6 %collective-permute-start.2 = (bf16[2,32,1152]{2,1,0:T(8,128)(2,1)S(1)}, bf16[2,32,1152]{2,1,0:T(8,128)(2,1)S(1)}, u32[]{:S(2)}, u32[]{:S(2)}) collective-permute-start(bf16[2,32,1152]{2,1,0:T(8,128)(2,1)S(1)} %join.2._), channel_id=1, source_target_pairs={{0,4},{1,0},{2,12},{3,8},{4,5},{5,1},{6,13},{7,9},{8,6},{9,2},{10,... | collective-permute-start | bytes 442376 | tf_op jit(solution)/shard_map/ppermute | solution.py:306
  9.4 8.9 %collective-permute-start.1 = (bf16[2,32,1152]{2,1,0:T(8,128)(2,1)S(1)}, bf16[2,32,1152]{2,1,0:T(8,128)(2,1)S(1)}, u32[]{:S(2)}, u32[]{:S(2)}) collective-permute-start(bf16[2,32,1152]{2,1,0:T(8,128)(2,1)S(1)} %join.2._), channel_id=1, source_target_pairs={{0,0},{1,4},{2,8},{3,12},{4,1},{5,5},{6,9},{7,13},{8,2},{9,6},{10,... | collective-permute-start | bytes 442376 | tf_op jit(solution)/shard_map/ppermute | solution.py:306
  11.3 7.5 %collective-permute-start.4 = (bf16[2,32,1152]{2,1,0:T(8,128)(2,1)S(1)}, bf16[2,32,1152]{2,1,0:T(8,128)(2,1)S(1)}, u32[]{:S(2)}, u32[]{:S(2)}) collective-permute-start(bf16[2,32,1152]{2,1,0:T(8,128)(2,1)S(1)} %join.3.own_ref), channel_id=1, source_target_pairs={{0,2},{1,3},{2,0},{3,1},{4,6},{5,7},{6,4},{7,5},{8,10},{9,11},{10,... | collective-permute-start | bytes 442376 | tf_op jit(solution)/shard_map/ppermute | solution.py:295
  12.6 6.2 %copy-start = (bf16[128,640]{1,0:T(8,128)(2,1)S(1)}, bf16[128,640]{1,0:T(8,128)(2,1)}, u32[]{:S(2)}) copy-start(bf16[128,640]{1,0:T(8,128)(2,1)} %w_ref.7) | copy-start | bytes 491524
  12.6 6.2 %copy-start.6 = (f32[128]{0:T(128)S(1)}, f32[128]{0:T(128)}, u32[]{:S(2)}) copy-start(f32[128]{0:T(128)} %param.30) | copy-start | bytes 1540
  12.7 6.2 %copy-start.7 = (f32[128]{0:T(128)S(1)}, f32[128]{0:T(128)}, u32[]{:S(2)}) copy-start(f32[128]{0:T(128)} %param.31) | copy-start | bytes 1540
  21.9 12.8 %collective-permute-start.5 = (bf16[32,32,128]{2,1,0:T(8,128)(2,1)S(1)}, bf16[32,32,128]{2,1,0:T(8,128)(2,1)S(1)}, u32[]{:S(2)}, u32[]{:S(2)}) collective-permute-start(bf16[32,32,128]{2,1,0:T(8,128)(2,1)S(1)} %get-tuple-element.25), channel_id=1, source_target_pairs={{8,0},{13,1},{11,2},{14,3},{9,4},{12,5},{10,6},{15,7},{0,8},{5,9},... | collective-permute-start | bytes 786440 | tf_op jit(solution)/shard_map/ppermute | solution.py:320
  23.7 11.5 %collective-permute-start.7 = (bf16[32,32,128]{2,1,0:T(8,128)(2,1)S(1)}, bf16[32,32,128]{2,1,0:T(8,128)(2,1)S(1)}, u32[]{:S(2)}, u32[]{:S(2)}) collective-permute-start(bf16[32,32,128]{2,1,0:T(8,128)(2,1)S(1)} %get-tuple-element.26.refs_0_), channel_id=1, source_target_pairs={{0,1},{1,0},{2,3},{3,2},{4,5},{5,4},{6,7},{7,6},{8,9},{9,8},{10,11... | collective-permute-start | bytes 786440 | tf_op jit(solution)/shard_map/ppermute | solution.py:300
  23.7 12.9 %collective-permute-start.9 = (bf16[32,32,128]{2,1,0:T(8,128)(2,1)S(1)}, bf16[32,32,128]{2,1,0:T(8,128)(2,1)S(1)}, u32[]{:S(2)}, u32[]{:S(2)}) collective-permute-start(bf16[32,32,128]{2,1,0:T(8,128)(2,1)S(1)} %get-tuple-element.25), channel_id=1, source_target_pairs={{0,0},{4,1},{2,2},{6,3},{1,4},{5,5},{3,6},{7,7},{8,8},{12,9},{10,1... | collective-permute-start | bytes 786440 | tf_op jit(solution)/shard_map/ppermute | solution.py:320
  24.3 15.9 %collective-permute-start.8 = (bf16[32,32,128]{2,1,0:T(8,128)(2,1)S(1)}, bf16[32,32,128]{2,1,0:T(8,128)(2,1)S(1)}, u32[]{:S(2)}, u32[]{:S(2)}) collective-permute-start(bf16[32,32,128]{2,1,0:T(8,128)(2,1)S(1)} %get-tuple-element.25), channel_id=1, source_target_pairs={{1,0},{5,1},{3,2},{7,3},{0,4},{4,5},{2,6},{6,7},{9,8},{13,9},{11,1... | collective-permute-start | bytes 786440 | tf_op jit(solution)/shard_map/ppermute | solution.py:320
  34.7 8.7 %collective-permute-start.6 = (bf16[32,32,128]{2,1,0:T(8,128)(2,1)S(1)}, bf16[32,32,128]{2,1,0:T(8,128)(2,1)S(1)}, u32[]{:S(2)}, u32[]{:S(2)}) collective-permute-start(bf16[32,32,128]{2,1,0:T(8,128)(2,1)S(1)} %collective-permute-done.5.right_ref), channel_id=1, source_target_pairs={{0,4},{4,0},{8,12},{12,8},{1,5},{5,1},{9,13},{13,9},{2,6},{6,2},{1... | collective-permute-start | bytes 786440 | tf_op jit(solution)/shard_map/ppermute | solution.py:324
  36.5 9.6 %copy-start.1 = (bf16[128,128]{1,0:T(8,128)(2,1)S(1)}, bf16[128,128]{1,0:T(8,128)(2,1)}, u32[]{:S(2)}) copy-start(bf16[128,128]{1,0:T(8,128)(2,1)} %w_ref.9) | copy-start | bytes 98308
  36.5 9.6 %copy-start.2 = (f32[128]{0:T(128)S(1)}, f32[128]{0:T(128)}, u32[]{:S(2)}) copy-start(f32[128]{0:T(128)} %param.34) | copy-start | bytes 1540
  36.5 9.6 %copy-start.3 = (f32[128]{0:T(128)S(1)}, f32[128]{0:T(128)}, u32[]{:S(2)}) copy-start(f32[128]{0:T(128)} %param.35) | copy-start | bytes 1540
  36.5 9.5 %copy-start.4 = (f32[128]{0:T(128)S(1)}, f32[128]{0:T(128)}, u32[]{:S(2)}) copy-start(f32[128]{0:T(128)} %param.37) | copy-start | bytes 1540
  44.4 1.6 %collective-permute-start.11 = (bf16[768,128]{1,0:T(8,128)(2,1)S(1)}, bf16[768,128]{1,0:T(8,128)(2,1)S(1)}, u32[]{:S(2)}, u32[]{:S(2)}) collective-permute-start(bf16[768,128]{1,0:T(8,128)(2,1)S(1)} %get-tuple-element.32), channel_id=1, source_target_pairs={{0,2},{1,3},{2,0},{3,1},{4,6},{5,7},{6,4},{7,5},{8,10},{9,11},{10,... | collective-permute-start | bytes 589832 | tf_op jit(solution)/shard_map/ppermute | solution.py:295
  45.3 1.3 %collective-permute-start.10 = (bf16[256,128]{1,0:T(8,128)(2,1)S(1)}, bf16[256,128]{1,0:T(8,128)(2,1)S(1)}, u32[]{:S(2)}, u32[]{:S(2)}) collective-permute-start(bf16[256,128]{1,0:T(8,128)(2,1)S(1)} %get-tuple-element.29), channel_id=1, source_target_pairs={{0,2},{1,3},{2,0},{3,1},{4,6},{5,7},{6,4},{7,5},{8,10},{9,11},{10,... | collective-permute-start | bytes 196616 | tf_op jit(solution)/shard_map/ppermute | solution.py:295

commit v18 on v17

--- a/solution.py
+++ b/solution.py
@@ -205,8 +205,8 @@
         panel_ref[x ^ step] = left[...].astype(F32).reshape(panel_ref.shape[1:])
 
 
-def source_of(z, core, x, step, chips):
-    block = z ^ step ^ ((x + core) % 2 if step >= chips else 0)
+def source_of(z, x, step, chips):
+    block = z ^ step ^ ((x + z // chips) % 2 if step >= chips else 0)
     return block // chips, block % chips
 
 
@@ -239,8 +239,7 @@
 
 def step_kernel(step, chips, first, fresh, right_ref, panel_ref, *refs):
     out_ref, rscr = refs[-2:]
-    z, core, x = [lax.axis_index(axis) for axis in GROUP]
-    chip = source_of(z, core, x, step, chips)[1]
+    chip = source_of(lax.axis_index("resi"), lax.axis_index("seq"), step, chips)[1]
     rscr[...] = right_ref[...].astype(F32).reshape(rscr.shape)
     add_block(panel_ref, chip, rscr, right_ref.shape[1], first, None if fresh else refs[0], out_ref)
 
@@ -315,7 +314,7 @@
     for z in range(count):
         for p in range(count):
             core, x = p // chips, p % chips
-            far, chip = source_of(z, core, x, step, chips)
+            far, chip = source_of(z, x, step, chips)
             pairs.append(((far * chips + x) * count + core * chips + chip, z * count + p))
     return lax.ppermute(block, GROUP, pairs)
 

time: 48 us -> 52.4 us (1.092)
  starting transfers between devices: 15.5 us -> 22.7 us
  waiting for transfers between devices: 17.3 us -> 14.4 us
    ppermute x1, starting transfers between devices: 0.16 us -> 6.6 us  [pass_on(): return lax.ppermute(block, 'resi', [(z, z ^ 1) for z in range(count)])]
    ppermute x3, waiting for transfers between devices: 8.91 us -> 6.16 us  [send_same_core(): return lax.ppermute(block, GROUP, pairs)]
    ppermute x4, starting transfers between devices: 0.83 us -> 1.61 us  [swap_cores(): lax.ppermute(block, PLANE, [(p, p ^ count // 2) for p in range(count)])]
  transfers between devices with their start and end apart: 12 -> 12, of which waited for: 7 -> 6; matrix products, arithmetic and copies ran while one was open for 0% -> 0% of each run, Pallas kernels for 14% -> 13%
where the time goes in v18:
time: 52.4 us; the launch traced here: 52 us
  starting transfers between devices  22.7 us (43%)
  waiting for transfers between devices  14.4 us (27%)
  Pallas kernels  13.1 us (25%)
  local copies, waits for them, and re-layouts  1.48 us (3%)
    pallas_call x16, Pallas kernels, call(): pl.pallas_call(kernel, out_shape=outs, in_specs=[vmem] * len(args), out_s...  13.1 us
    ppermute x1, starting transfers between devices, pass_on(): return lax.ppermute(block, 'resi', [(z, z ^ 1) for z in range(count)])  6.6 us
    ppermute x3, starting transfers between devices, send_same_core(): return lax.ppermute(block, GROUP, pairs)  6.32 us
    ppermute x3, waiting for transfers between devices, send_same_core(): return lax.ppermute(block, GROUP, pairs)  6.16 us
    ppermute x2, waiting for transfers between devices, send_turned(): lax.ppermute(block, GROUP, [(z * count + p, (p ^ m) * count + z) for z in...  5.66 us
    ppermute x2, starting transfers between devices, send_turned(): lax.ppermute(block, GROUP, [(z * count + p, (p ^ m) * count + z) for z in...  5.51 us
    ppermute x2, starting transfers between devices, send_chips(): lax.ppermute(block, 'seq', [(x, x ^ m) for x in range(chips)])  2.68 us
    ppermute x1, waiting for transfers between devices, pass_on(): return lax.ppermute(block, 'resi', [(z, z ^ 1) for z in range(count)])  1.74 us
  transfers between devices with their start and end apart: 12, of which 6 were waited for; matrix products, arithmetic and copies ran while one was open for 0% of the time, Pallas kernels for 13%

profile of v18, /device:TPU:1, one launch (start us, length us, event | category | flops | bytes accessed | tf_op | source)
XLA Modules:
  0.0 52.0 jit_solution(1970359056440051476)
XLA Ops:
  0.0 1.1 %copy-done.8 = bf16[32,32,256]{2,1,0:T(8,128)(2,1)S(1)} copy-done((bf16[32,32,256]{2,1,0:T(8,128)(2,1)S(1)}, bf16[32,32,256]{2,1,0:T(8,128)(2,1)}, u32[]{:S(2)}) %copy-start.8) | copy-done | bytes 524312
  1.1 0.4 norm.1.x_ref
  1.5 0.3 copy-done.11
  1.8 1.1 %pack.1 = (bf16[32,1152]{1,0:T(8,128)(2,1)S(1)}, bf16[32,1152]{1,0:T(8,128)(2,1)S(1)}) custom-call(f32[1024,256]{1,0:T(8,128)S(1)} %norm.1.x_ref, s32[32,32]{1,0:T(8,128)S(1)} %copy-done.13, s32[1,128]{1,0:T(1,128)S(1)} %bitcast.17, f32[1,256]{1,0:T(1,128)S(1)} %bitcast.22, f32[1,256]{1,0:T(1,128)S(1)} %bitcast.23, bf16[64,256]{1,0:T(8,128)(2,1)S(1)} %bitcast.21, ...), custom_call_target="tpu_custom_call" | custom-call | flops 1073741824 | bytes 1088256 | tf_op jit(solution)/shard_map/pack/pallas_call | solution.py:329
  2.9 0.1 collective-permute-start
  3.0 2.7 %collective-permute-start.3 = (bf16[32,1152]{1,0:T(8,128)(2,1)S(1)}, bf16[32,1152]{1,0:T(8,128)(2,1)S(1)}, u32[]{:S(2)}, u32[]{:S(2)}) collective-permute-start(bf16[32,1152]{1,0:T(8,128)(2,1)S(1)} %get-tuple-element.22.refs_0_), channel_id=1, source_target_pairs={{0,1},{1,0},{2,3},{3,2},{4,5},{5,4},{6,7},{7,6},{8,9},{9,8},{10,11... | collective-permute-start | bytes 221192 | tf_op jit(solution)/shard_map/ppermute | solution.py:299
  5.8 3.6 %collective-permute-start.2 = (bf16[2,32,1152]{2,1,0:T(8,128)(2,1)S(1)}, bf16[2,32,1152]{2,1,0:T(8,128)(2,1)S(1)}, u32[]{:S(2)}, u32[]{:S(2)}) collective-permute-start(bf16[2,32,1152]{2,1,0:T(8,128)(2,1)S(1)} %join.2._), channel_id=1, source_target_pairs={{0,4},{1,0},{2,12},{3,8},{4,5},{5,1},{6,13},{7,9},{8,6},{9,2},{10,... | collective-permute-start | bytes 442376 | tf_op jit(solution)/shard_map/ppermute | solution.py:305
  9.4 1.9 %collective-permute-start.1 = (bf16[2,32,1152]{2,1,0:T(8,128)(2,1)S(1)}, bf16[2,32,1152]{2,1,0:T(8,128)(2,1)S(1)}, u32[]{:S(2)}, u32[]{:S(2)}) collective-permute-start(bf16[2,32,1152]{2,1,0:T(8,128)(2,1)S(1)} %join.2._), channel_id=1, source_target_pairs={{0,0},{1,4},{2,8},{3,12},{4,1},{5,5},{6,9},{7,13},{8,2},{9,6},{10,... | collective-permute-start | bytes 442376 | tf_op jit(solution)/shard_map/ppermute | solution.py:305
  11.5 1.2 %base.1 = (f32[32,32,128]{2,1,0:T(8,128)S(1)}, bf16[4096,512]{1,0:T(8,128)(2,1)S(1)}) custom-call(bf16[32,32,128]{2,1,0:T(8,128)(2,1)S(1)} %copy-done.9, bf16[66,128]{1,0:T(8,128)(2,1)S(1)} %copy-done.12, s32[1,128]{1,0:T(1,128)S(1)} %bitcast.25, bf16[1024,128]{1,0:T(8,128)(2,1)S(1)} %copy-done.10, bf16[2,32,1152]{2,1,0:T(8,128)(2,1)S(1)} %join.2._), custom_call_target="tpu_custom_call" | custom-call | flops 1073741824 | bytes 689152 | tf_op jit(solution)/shard_map/base/pallas_call | solution.py:329
  12.7 0.8 %collective-permute-done.2.refs_1_ = bf16[2,32,1152]{2,1,0:T(8,128)(2,1)S(1)} collective-permute-done((bf16[2,32,1152]{2,1,0:T(8,128)(2,1)S(1)}, bf16[2,32,1152]{2,1,0:T(8,128)(2,1)S(1)}, u32[]{:S(2)}, u32[]{:S(2)}) %collective-permute-start.2) | collective-permute-done | bytes 147488 | tf_op jit(solution)/shard_map/ppermute | solution.py:305
  13.4 4.9 %collective-permute-done.1.refs_0_ = bf16[2,32,1152]{2,1,0:T(8,128)(2,1)S(1)} collective-permute-done((bf16[2,32,1152]{2,1,0:T(8,128)(2,1)S(1)}, bf16[2,32,1152]{2,1,0:T(8,128)(2,1)S(1)}, u32[]{:S(2)}, u32[]{:S(2)}) %collective-permute-start.1) | collective-permute-done | bytes 147488 | tf_op jit(solution)/shard_map/ppermute | solution.py:305
  18.3 0.5 turn.1
  18.8 3.1 %edges.1 = (bf16[32,32,128]{2,1,0:T(8,128)(2,1)S(1)}, bf16[32,32,128]{2,1,0:T(8,128)(2,1)S(1)}, bf16[32,32,128]{2,1,0:T(8,128)(2,1)S(1)}, bf16[1024,128]{1,0:T(8,128)(2,1)S(1)}) custom-call(bf16[1024,128]{1,0:T(8,128)(2,1)S(1)} %get-tuple-element.20.turned_ref, bf16[32,128]{1,0:T(8,128)(2,1)S(1)} %get-tuple-element.21.live_ref, ...), custom_call_target="tpu_custom_call" | custom-call | bytes 5451776 | tf_op jit(solution)/shard_map/edges/pallas_call | solution.py:329
  21.9 1.7 %collective-permute-start.5 = (bf16[32,32,128]{2,1,0:T(8,128)(2,1)S(1)}, bf16[32,32,128]{2,1,0:T(8,128)(2,1)S(1)}, u32[]{:S(2)}, u32[]{:S(2)}) collective-permute-start(bf16[32,32,128]{2,1,0:T(8,128)(2,1)S(1)} %get-tuple-element.25), channel_id=1, source_target_pairs={{8,0},{13,1},{10,2},{15,3},{9,4},{12,5},{11,6},{14,7},{1,8},{4,9},... | collective-permute-start | bytes 786440 | tf_op jit(solution)/shard_map/ppermute | solution.py:319
  23.7 0.7 %collective-permute-start.9 = (bf16[32,32,128]{2,1,0:T(8,128)(2,1)S(1)}, bf16[32,32,128]{2,1,0:T(8,128)(2,1)S(1)}, u32[]{:S(2)}, u32[]{:S(2)}) collective-permute-start(bf16[32,32,128]{2,1,0:T(8,128)(2,1)S(1)} %get-tuple-element.25), channel_id=1, source_target_pairs={{0,0},{4,1},{2,2},{6,3},{1,4},{5,5},{3,6},{7,7},{8,8},{12,9},{10,1... | collective-permute-start | bytes 786440 | tf_op jit(solution)/shard_map/ppermute | solution.py:319
  24.3 3.9 %collective-permute-start.8 = (bf16[32,32,128]{2,1,0:T(8,128)(2,1)S(1)}, bf16[32,32,128]{2,1,0:T(8,128)(2,1)S(1)}, u32[]{:S(2)}, u32[]{:S(2)}) collective-permute-start(bf16[32,32,128]{2,1,0:T(8,128)(2,1)S(1)} %get-tuple-element.25), channel_id=1, source_target_pairs={{1,0},{5,1},{3,2},{7,3},{0,4},{4,5},{2,6},{6,7},{9,8},{13,9},{11,1... | collective-permute-start | bytes 786440 | tf_op jit(solution)/shard_map/ppermute | solution.py:319
  28.3 6.2 %collective-permute-done.5.right_ref = bf16[32,32,128]{2,1,0:T(8,128)(2,1)S(1)} collective-permute-done((bf16[32,32,128]{2,1,0:T(8,128)(2,1)S(1)}, bf16[32,32,128]{2,1,0:T(8,128)(2,1)S(1)}, u32[]{:S(2)}, u32[]{:S(2)}) %collective-permute-start.5) | collective-permute-done | bytes 262176 | tf_op jit(solution)/shard_map/ppermute | solution.py:319
  34.4 6.6 %collective-permute-start.6 = (bf16[32,32,128]{2,1,0:T(8,128)(2,1)S(1)}, bf16[32,32,128]{2,1,0:T(8,128)(2,1)S(1)}, u32[]{:S(2)}, u32[]{:S(2)}) collective-permute-start(bf16[32,32,128]{2,1,0:T(8,128)(2,1)S(1)} %collective-permute-done.5.right_ref), channel_id=1, source_target_pairs={{0,4},{4,0},{8,12},{12,8},{1,5},{5,1},{9,13},{13,9},{2,6},{6,2},{1... | collective-permute-start | bytes 786440 | tf_op jit(solution)/shard_map/ppermute | solution.py:323
  41.0 0.2 gate.1.refs_2_.gate_ref
  41.3 0.1 panel.1.panel_ref
  41.4 1.3 %triangle.3.far_ref = f32[1024,128]{1,0:T(8,128)S(1)} custom-call(bf16[32,32,128]{2,1,0:T(8,128)(2,1)S(1)} %collective-permute-done.5.right_ref, f32[2,1024,128]{2,1,0:T(8,128)S(1)} %panel.1.panel_ref), custom_call_target="tpu_custom_call" | custom-call | bytes 1310720 | tf_op jit(solution)/shard_map/triangle/pallas_call | solution.py:329
  42.7 1.3 %triangle.4.refs_0_ = f32[1024,128]{1,0:T(8,128)S(1)} custom-call(bf16[32,32,128]{2,1,0:T(8,128)(2,1)S(1)} %collective-permute-done.9.right_ref, f32[2,1024,128]{2,1,0:T(8,128)S(1)} %panel.1.panel_ref), custom_call_target="tpu_custom_call" | custom-call | bytes 1310720 | tf_op jit(solution)/shard_map/triangle/pallas_call | solution.py:329
  44.0 1.3 %triangle.5.near_ref = f32[1024,128]{1,0:T(8,128)S(1)} custom-call(bf16[32,32,128]{2,1,0:T(8,128)(2,1)S(1)} %collective-permute-done.8.right_ref, f32[2,1024,128]{2,1,0:T(8,128)S(1)} %panel.1.panel_ref, f32[1024,128]{1,0:T(8,128)S(1)} %triangle.4.refs_0_), custom_call_target="tpu_custom_call" | custom-call | bytes 1835008 | tf_op jit(solution)/shard_map/triangle/pallas_call | solution.py:329
  45.3 1.7 %collective-permute-done.6.right_ref = bf16[32,32,128]{2,1,0:T(8,128)(2,1)S(1)} collective-permute-done((bf16[32,32,128]{2,1,0:T(8,128)(2,1)S(1)}, bf16[32,32,128]{2,1,0:T(8,128)(2,1)S(1)}, u32[]{:S(2)}, u32[]{:S(2)}) %collective-permute-start.6) | collective-permute-done | bytes 262176 | tf_op jit(solution)/shard_map/ppermute | solution.py:323
  47.0 1.0 %last.3 = (f32[768,128]{1,0:T(8,128)S(1)}, bf16[768,128]{1,0:T(8,128)(2,1)S(1)}) custom-call(bf16[32,32,128]{2,1,0:T(8,128)(2,1)S(1)} %collective-permute-done.6.right_ref, f32[2,1024,128]{2,1,0:T(8,128)S(1)} %panel.1.panel_ref, f32[1024,128]{1,0:T(8,128)S(1)} %triangle.3.far_ref, f32[1024,128]{1,0:T(8,128)S(1)} %triangle.5.near_ref), custom_call_target="tpu_custom_call" | custom-call | flops 268435456 | bytes 2359296 | tf_op jit(solution)/shard_map/last/pallas_call | solution.py:329
  48.0 1.3 %collective-permute-start.11 = (bf16[768,128]{1,0:T(8,128)(2,1)S(1)}, bf16[768,128]{1,0:T(8,128)(2,1)S(1)}, u32[]{:S(2)}, u32[]{:S(2)}) collective-permute-start(bf16[768,128]{1,0:T(8,128)(2,1)S(1)} %get-tuple-element.32), channel_id=1, source_target_pairs={{0,2},{1,3},{2,0},{3,1},{4,6},{5,7},{6,4},{7,5},{8,10},{9,11},{10,... | collective-permute-start | bytes 589832 | tf_op jit(solution)/shard_map/ppermute | solution.py:294
  49.3 0.3 last.2
  49.7 0.1 collective-permute-start.10
  49.8 0.6 %collective-permute-done.11.other_ref = bf16[768,128]{1,0:T(8,128)(2,1)S(1)} collective-permute-done((bf16[768,128]{1,0:T(8,128)(2,1)S(1)}, bf16[768,128]{1,0:T(8,128)(2,1)S(1)}, u32[]{:S(2)}, u32[]{:S(2)}) %collective-permute-start.11) | collective-permute-done | bytes 196640 | tf_op jit(solution)/shard_map/ppermute | solution.py:294
  50.4 0.4 final.2.refs_0_
  50.8 0.2 collective-permute-done.10.other_ref
  51.0 1.0 %final.3 = bf16[32,32,128]{2,1,0:T(8,128)(2,1)} custom-call(f32[256,128]{1,0:T(8,128)S(1)} %get-tuple-element.28.own_ref, bf16[256,128]{1,0:T(8,128)(2,1)S(1)} %collective-permute-done.10.other_ref, bf16[32,32,128]{2,1,0:T(8,128)(2,1)S(1)} %get-tuple-element.30.updated_ref, f32[1024,128]{1,0:T(8,128)S(1)} %gate.1.refs_2_.gate_ref, f32[1,128]{1,0:T(1,128)S(1)} %bitcast.12, ...), custom_call_target="tpu_custom_call" | custom-call | flops 268435456 | bytes 1213952 | tf_op jit(solution)/shard_map/final/pallas_call | solution.py:329
  (47 shorter events, 0.2 us)
Async XLA Ops:
  0.0 1.5 %copy-start.5 = (s32[128]{0:T(128)S(1)}, s32[128]{0:T(128)}, u32[]{:S(2)}) copy-start(s32[128]{0:T(128)} %param.22) | copy-start | bytes 1540
  0.0 1.1 %copy-start.8 = (bf16[32,32,256]{2,1,0:T(8,128)(2,1)S(1)}, bf16[32,32,256]{2,1,0:T(8,128)(2,1)}, u32[]{:S(2)}) copy-start(bf16[32,32,256]{2,1,0:T(8,128)(2,1)} %x_ref.1) | copy-start | bytes 1572868
  1.1 0.8 %copy-start.11 = (bf16[256,64]{0,1:T(8,128)(2,1)S(1)}, bf16[256,64]{0,1:T(8,128)(2,1)}, u32[]{:S(2)}) copy-start(bf16[256,64]{0,1:T(8,128)(2,1)} %param.26) | copy-start | bytes 98308
  1.1 0.8 %copy-start.13 = (s32[32,32]{1,0:T(8,128)S(1)}, s32[32,32]{1,0:T(8,128)}, u32[]{:S(2)}) copy-start(s32[32,32]{1,0:T(8,128)} %mask_ref.1) | copy-start | bytes 12292
  1.1 0.8 %copy-start.14 = (f32[256]{0:T(256)S(1)}, f32[256]{0:T(256)}, u32[]{:S(2)}) copy-start(f32[256]{0:T(256)} %param.24) | copy-start | bytes 3076
  1.1 0.8 %copy-start.15 = (f32[256]{0:T(256)S(1)}, f32[256]{0:T(256)}, u32[]{:S(2)}) copy-start(f32[256]{0:T(256)} %param.25) | copy-start | bytes 3076
  1.1 0.8 %copy-start.16 = (f32[64]{0:T(128)S(1)}, f32[64]{0:T(128)}, u32[]{:S(2)}) copy-start(f32[64]{0:T(128)} %param.27) | copy-start | bytes 772
  1.1 4.6 %copy-start.18 = (f32[640]{0:T(1024)S(1)}, f32[640]{0:T(1024)}, u32[]{:S(2)}) copy-start(f32[640]{0:T(1024)} %param.33) | copy-start | bytes 7684
  2.9 2.8 %collective-permute-start = (bf16[32,1152]{1,0:T(8,128)(2,1)S(1)}, bf16[32,1152]{1,0:T(8,128)(2,1)S(1)}, u32[]{:S(2)}, u32[]{:S(2)}) collective-permute-start(bf16[32,1152]{1,0:T(8,128)(2,1)S(1)} %get-tuple-element.19.refs_0_), channel_id=1, source_target_pairs={{0,2},{1,3},{2,0},{3,1},{4,6},{5,7},{6,4},{7,5},{8,10},{9,11},{10,... | collective-permute-start | bytes 221192 | tf_op jit(solution)/shard_map/ppermute | solution.py:294
  3.0 8.3 %collective-permute-start.3 = (bf16[32,1152]{1,0:T(8,128)(2,1)S(1)}, bf16[32,1152]{1,0:T(8,128)(2,1)S(1)}, u32[]{:S(2)}, u32[]{:S(2)}) collective-permute-start(bf16[32,1152]{1,0:T(8,128)(2,1)S(1)} %get-tuple-element.22.refs_0_), channel_id=1, source_target_pairs={{0,1},{1,0},{2,3},{3,2},{4,5},{5,4},{6,7},{7,6},{8,9},{9,8},{10,11... | collective-permute-start | bytes 221192 | tf_op jit(solution)/shard_map/ppermute | solution.py:299
  5.8 5.7 %copy-start.9 = (bf16[32,32,128]{2,1,0:T(8,128)(2,1)S(1)}, bf16[32,32,128]{2,1,0:T(8,128)(2,1)}, u32[]{:S(2)}) copy-start(bf16[32,32,128]{2,1,0:T(8,128)(2,1)} %pair_ref.1) | copy-start | bytes 786436
  5.8 5.7 %copy-start.10 = (bf16[1024,128]{1,0:T(8,128)(2,1)S(1)}, bf16[1024,128]{1,0:T(8,128)(2,1)}, u32[]{:S(2)}) copy-start(bf16[1024,128]{1,0:T(8,128)(2,1)} %w_ref.5) | copy-start | bytes 786436
  5.8 5.7 %copy-start.12 = (bf16[66,128]{1,0:T(8,128)(2,1)S(1)}, bf16[66,128]{1,0:T(8,128)(2,1)}, u32[]{:S(2)}) copy-start(bf16[66,128]{1,0:T(8,128)(2,1)} %table_ref.1) | copy-start | bytes 50692
  5.8 5.7 %copy-start.17 = (s32[128]{0:T(128)S(1)}, s32[128]{0:T(128)}, u32[]{:S(2)}) copy-start(s32[128]{0:T(128)} %param.23) | copy-start | bytes 1540
  5.8 7.6 %collective-permute-start.2 = (bf16[2,32,1152]{2,1,0:T(8,128)(2,1)S(1)}, bf16[2,32,1152]{2,1,0:T(8,128)(2,1)S(1)}, u32[]{:S(2)}, u32[]{:S(2)}) collective-permute-start(bf16[2,32,1152]{2,1,0:T(8,128)(2,1)S(1)} %join.2._), channel_id=1, source_target_pairs={{0,4},{1,0},{2,12},{3,8},{4,5},{5,1},{6,13},{7,9},{8,6},{9,2},{10,... | collective-permute-start | bytes 442376 | tf_op jit(solution)/shard_map/ppermute | solution.py:305
  9.4 8.9 %collective-permute-start.1 = (bf16[2,32,1152]{2,1,0:T(8,128)(2,1)S(1)}, bf16[2,32,1152]{2,1,0:T(8,128)(2,1)S(1)}, u32[]{:S(2)}, u32[]{:S(2)}) collective-permute-start(bf16[2,32,1152]{2,1,0:T(8,128)(2,1)S(1)} %join.2._), channel_id=1, source_target_pairs={{0,0},{1,4},{2,8},{3,12},{4,1},{5,5},{6,9},{7,13},{8,2},{9,6},{10,... | collective-permute-start | bytes 442376 | tf_op jit(solution)/shard_map/ppermute | solution.py:305
  11.3 7.5 %collective-permute-start.4 = (bf16[2,32,1152]{2,1,0:T(8,128)(2,1)S(1)}, bf16[2,32,1152]{2,1,0:T(8,128)(2,1)S(1)}, u32[]{:S(2)}, u32[]{:S(2)}) collective-permute-start(bf16[2,32,1152]{2,1,0:T(8,128)(2,1)S(1)} %join.3.own_ref), channel_id=1, source_target_pairs={{0,2},{1,3},{2,0},{3,1},{4,6},{5,7},{6,4},{7,5},{8,10},{9,11},{10,... | collective-permute-start | bytes 442376 | tf_op jit(solution)/shard_map/ppermute | solution.py:294
  12.6 6.2 %copy-start = (bf16[128,640]{1,0:T(8,128)(2,1)S(1)}, bf16[128,640]{1,0:T(8,128)(2,1)}, u32[]{:S(2)}) copy-start(bf16[128,640]{1,0:T(8,128)(2,1)} %w_ref.7) | copy-start | bytes 491524
  12.6 6.2 %copy-start.6 = (f32[128]{0:T(128)S(1)}, f32[128]{0:T(128)}, u32[]{:S(2)}) copy-start(f32[128]{0:T(128)} %param.30) | copy-start | bytes 1540
  12.7 6.2 %copy-start.7 = (f32[128]{0:T(128)S(1)}, f32[128]{0:T(128)}, u32[]{:S(2)}) copy-start(f32[128]{0:T(128)} %param.31) | copy-start | bytes 1540
  21.9 12.5 %collective-permute-start.5 = (bf16[32,32,128]{2,1,0:T(8,128)(2,1)S(1)}, bf16[32,32,128]{2,1,0:T(8,128)(2,1)S(1)}, u32[]{:S(2)}, u32[]{:S(2)}) collective-permute-start(bf16[32,32,128]{2,1,0:T(8,128)(2,1)S(1)} %get-tuple-element.25), channel_id=1, source_target_pairs={{8,0},{13,1},{10,2},{15,3},{9,4},{12,5},{11,6},{14,7},{1,8},{4,9},... | collective-permute-start | bytes 786440 | tf_op jit(solution)/shard_map/ppermute | solution.py:319
  23.7 17.6 %collective-permute-start.7 = (bf16[32,32,128]{2,1,0:T(8,128)(2,1)S(1)}, bf16[32,32,128]{2,1,0:T(8,128)(2,1)S(1)}, u32[]{:S(2)}, u32[]{:S(2)}) collective-permute-start(bf16[32,32,128]{2,1,0:T(8,128)(2,1)S(1)} %get-tuple-element.26.refs_0_), channel_id=1, source_target_pairs={{0,1},{1,0},{2,3},{3,2},{4,5},{5,4},{6,7},{7,6},{8,9},{9,8},{10,11... | collective-permute-start | bytes 786440 | tf_op jit(solution)/shard_map/ppermute | solution.py:299
  23.7 19.0 %collective-permute-start.9 = (bf16[32,32,128]{2,1,0:T(8,128)(2,1)S(1)}, bf16[32,32,128]{2,1,0:T(8,128)(2,1)S(1)}, u32[]{:S(2)}, u32[]{:S(2)}) collective-permute-start(bf16[32,32,128]{2,1,0:T(8,128)(2,1)S(1)} %get-tuple-element.25), channel_id=1, source_target_pairs={{0,0},{4,1},{2,2},{6,3},{1,4},{5,5},{3,6},{7,7},{8,8},{12,9},{10,1... | collective-permute-start | bytes 786440 | tf_op jit(solution)/shard_map/ppermute | solution.py:319
  24.3 19.6 %collective-permute-start.8 = (bf16[32,32,128]{2,1,0:T(8,128)(2,1)S(1)}, bf16[32,32,128]{2,1,0:T(8,128)(2,1)S(1)}, u32[]{:S(2)}, u32[]{:S(2)}) collective-permute-start(bf16[32,32,128]{2,1,0:T(8,128)(2,1)S(1)} %get-tuple-element.25), channel_id=1, source_target_pairs={{1,0},{5,1},{3,2},{7,3},{0,4},{4,5},{2,6},{6,7},{9,8},{13,9},{11,1... | collective-permute-start | bytes 786440 | tf_op jit(solution)/shard_map/ppermute | solution.py:319
  34.4 12.6 %collective-permute-start.6 = (bf16[32,32,128]{2,1,0:T(8,128)(2,1)S(1)}, bf16[32,32,128]{2,1,0:T(8,128)(2,1)S(1)}, u32[]{:S(2)}, u32[]{:S(2)}) collective-permute-start(bf16[32,32,128]{2,1,0:T(8,128)(2,1)S(1)} %collective-permute-done.5.right_ref), channel_id=1, source_target_pairs={{0,4},{4,0},{8,12},{12,8},{1,5},{5,1},{9,13},{13,9},{2,6},{6,2},{1... | collective-permute-start | bytes 786440 | tf_op jit(solution)/shard_map/ppermute | solution.py:323
  42.6 7.8 %copy-start.1 = (bf16[128,128]{1,0:T(8,128)(2,1)S(1)}, bf16[128,128]{1,0:T(8,128)(2,1)}, u32[]{:S(2)}) copy-start(bf16[128,128]{1,0:T(8,128)(2,1)} %w_ref.9) | copy-start | bytes 98308
  42.6 7.8 %copy-start.2 = (f32[128]{0:T(128)S(1)}, f32[128]{0:T(128)}, u32[]{:S(2)}) copy-start(f32[128]{0:T(128)} %param.34) | copy-start | bytes 1540
  42.6 7.8 %copy-start.3 = (f32[128]{0:T(128)S(1)}, f32[128]{0:T(128)}, u32[]{:S(2)}) copy-start(f32[128]{0:T(128)} %param.35) | copy-start | bytes 1540
  42.7 7.8 %copy-start.4 = (f32[128]{0:T(128)S(1)}, f32[128]{0:T(128)}, u32[]{:S(2)}) copy-start(f32[128]{0:T(128)} %param.37) | copy-start | bytes 1540
  48.0 2.4 %collective-permute-start.11 = (bf16[768,128]{1,0:T(8,128)(2,1)S(1)}, bf16[768,128]{1,0:T(8,128)(2,1)S(1)}, u32[]{:S(2)}, u32[]{:S(2)}) collective-permute-start(bf16[768,128]{1,0:T(8,128)(2,1)S(1)} %get-tuple-element.32), channel_id=1, source_target_pairs={{0,2},{1,3},{2,0},{3,1},{4,6},{5,7},{6,4},{7,5},{8,10},{9,11},{10,... | collective-permute-start | bytes 589832 | tf_op jit(solution)/shard_map/ppermute | solution.py:294
  49.7 1.3 %collective-permute-start.10 = (bf16[256,128]{1,0:T(8,128)(2,1)S(1)}, bf16[256,128]{1,0:T(8,128)(2,1)S(1)}, u32[]{:S(2)}, u32[]{:S(2)}) collective-permute-start(bf16[256,128]{1,0:T(8,128)(2,1)S(1)} %get-tuple-element.29), channel_id=1, source_target_pairs={{0,2},{1,3},{2,0},{3,1},{4,6},{5,7},{6,4},{7,5},{8,10},{9,11},{10,... | collective-permute-start | bytes 196616 | tf_op jit(solution)/shard_map/ppermute | solution.py:294

commit v19 on v17

--- a/solution.py
+++ b/solution.py
@@ -143,7 +143,7 @@
 
 def edges_kernel(turned_ref, live_ref, own_ref, swapped_ref, base_ref, block_ref, res_ref,
                  gain_ref, shift_ref, w_ref, bias_ref,
-                 updated_ref, left_ref, right_ref, nscr, lall, oscr, escr):
+                 updated_ref, right_ref, nscr, lall, oscr, escr):
     rows, cols, channels = base_ref.shape
     chips, seqs = own_ref.shape[:2]
     half = block_ref.shape[0] // LANES
@@ -179,18 +179,28 @@
     live = pick_columns(res_ref[...], col_start, cols) * pick_rows(res_ref[...], row_start, rows)
     chunk = 8
     for i0 in range(0, rows, chunk):
-        mixture = dot(nscr[i0 * cols:(i0 + chunk) * cols, :], w_ref[:, :4 * channels])
-        mixture = mixture + bias_ref[:, :4 * channels]
-        part = [mixture[:, n * channels:(n + 1) * channels] for n in range(4)]
-        left_edge = sigmoid(part[0]) * part[1]
-        right_edge = sigmoid(part[2]) * part[3]
+        mixture = dot(nscr[i0 * cols:(i0 + chunk) * cols, :], w_ref[:, 2 * channels:4 * channels])
+        mixture = mixture + bias_ref[:, 2 * channels:4 * channels]
+        right_edge = sigmoid(mixture[:, :channels]) * mixture[:, channels:]
         for ii in range(chunk):
-            here = live[:, i0 + ii:i0 + ii + 1]
             at = slice(ii * cols, (ii + 1) * cols)
-            left_ref[i0 + ii] = (left_edge[at] * here).astype(BF16)
-            escr[(i0 + ii) * cols:(i0 + ii + 1) * cols, :] = right_edge[at] * here
+            escr[(i0 + ii) * cols:(i0 + ii + 1) * cols, :] = right_edge[at] * live[:, i0 + ii:i0 + ii + 1]
     for k in range(cols):
         right_ref[k] = escr[pl.ds(k, rows, stride=cols), :].astype(BF16)
+
+
+def left_kernel(normed_ref, res_ref, w_ref, bias_ref, left_ref):
+    rows, cols, channels = left_ref.shape
+    row_start, col_start = lax.axis_index("resi") * rows, lax.axis_index(PLANE) * cols
+    live = pick_columns(res_ref[...], col_start, cols) * pick_rows(res_ref[...], row_start, rows)
+    chunk = 8
+    for i0 in range(0, rows, chunk):
+        mixture = dot(normed_ref[i0 * cols:(i0 + chunk) * cols, :], w_ref[:, :2 * channels])
+        mixture = mixture + bias_ref[:, :2 * channels]
+        left_edge = sigmoid(mixture[:, :channels]) * mixture[:, channels:]
+        for ii in range(chunk):
+            here = left_edge[ii * cols:(ii + 1) * cols] * live[:, i0 + ii:i0 + ii + 1]
+            left_ref[i0 + ii] = here.astype(BF16)
 
 
 def gate_kernel(normed_ref, w_ref, bias_ref, gate_ref):
@@ -401,10 +411,10 @@
         [pltpu.VMEM((count,) + pack.shape, BF16),
          pltpu.VMEM((count * seqs // LANES, width, LANES), F32)],
         rights, flops=1 << 36, name="turn")
-    updated, left_edge, right_edge, normed_pair = call(
+    updated, right_edge, normed_pair = call(
         edges_kernel,
-        [shape((rows, cols, channels), BF16), shape((rows, cols, channels), BF16),
-         shape((cols, rows, channels), BF16), shape((rows * cols, channels), BF16)],
+        [shape((rows, cols, channels), BF16), shape((cols, rows, channels), BF16),
+         shape((rows * cols, channels), BF16)],
         [pltpu.VMEM((count,) + pack.shape, BF16),
          pltpu.VMEM((rows // per * cols, half * LANES), BF16),
          pltpu.VMEM((rows * cols, channels), F32)],
@@ -416,6 +426,9 @@
     for step in range(chips, count, 2):
         block_far = send_same_core(right_edge, count, chips, step)
         right_edges += [block_far, pass_on(block_far, count)]
+    left_edge = call(left_kernel, shape((rows, cols, channels), BF16), [],
+                     [normed_pair, residue, triangle_projection_weights,
+                      flat(triangle_projection_biases)], name="left")
     left_edges = [left_edge] + send_chips(left_edge, chips)
     gate = call(gate_kernel, shape((rows * cols, channels), F32), [],
                 [normed_pair, triangle_projection_weights, flat(triangle_projection_biases)],

time: 48 us -> 47.8 us (level)
  waiting for transfers between devices: 17.3 us -> 16.8 us
    pallas_call x16 -> x17, Pallas kernels: 13 us -> 13.2 us  [call(): pl.pallas_call(kernel, out_shape=outs, in_specs=[vmem] * len(args), out_s...]
  transfers between devices with their start and end apart: 12 -> 12, of which waited for: 7 -> 7; matrix products, arithmetic and copies ran while one was open for 0% -> 0% of each run, Pallas kernels for 14% -> 15%
where the time goes in v19:
time: 47.8 us; the launch traced here: 47.4 us
  waiting for transfers between devices  16.8 us (35%)
  starting transfers between devices  15.6 us (33%)
  Pallas kernels  13.2 us (28%)
  local copies, waits for them, and re-layouts  1.48 us (3%)
    pallas_call x17, Pallas kernels, call(): pl.pallas_call(kernel, out_shape=outs, in_specs=[vmem] * len(args), out_s...  13.2 us
    ppermute x3, waiting for transfers between devices, send_same_core(): return lax.ppermute(block, GROUP, pairs)  8.89 us
    ppermute x3, starting transfers between devices, send_same_core(): return lax.ppermute(block, GROUP, pairs)  6.3 us
    ppermute x2, waiting for transfers between devices, send_turned(): lax.ppermute(block, GROUP, [(z * count + p, (p ^ m) * count + z) for z in...  5.66 us
    ppermute x2, starting transfers between devices, send_turned(): lax.ppermute(block, GROUP, [(z * count + p, (p ^ m) * count + z) for z in...  5.51 us
    ppermute x2, starting transfers between devices, send_chips(): lax.ppermute(block, 'seq', [(x, x ^ m) for x in range(chips)])  2.74 us
    unnamed x38, local copies, waits for them, and re-layouts  1.48 us
    ppermute x1, waiting for transfers between devices, pass_on(): return lax.ppermute(block, 'resi', [(z, z ^ 1) for z in range(count)])  1.44 us
  transfers between devices with their start and end apart: 12, of which 7 were waited for; matrix products, arithmetic and copies ran while one was open for 0% of the time, Pallas kernels for 15%

profile of v19, /device:TPU:1, one launch (start us, length us, event | category | flops | bytes accessed | tf_op | source)
XLA Modules:
  0.0 47.4 jit_solution(13565398439490892689)
XLA Ops:
  0.0 1.1 %copy-done.8 = bf16[32,32,256]{2,1,0:T(8,128)(2,1)S(1)} copy-done((bf16[32,32,256]{2,1,0:T(8,128)(2,1)S(1)}, bf16[32,32,256]{2,1,0:T(8,128)(2,1)}, u32[]{:S(2)}) %copy-start.8) | copy-done | bytes 524312
  1.1 0.4 norm.1.x_ref
  1.5 0.3 copy-done.11
  1.8 1.1 %pack.1 = (bf16[32,1152]{1,0:T(8,128)(2,1)S(1)}, bf16[32,1152]{1,0:T(8,128)(2,1)S(1)}) custom-call(f32[1024,256]{1,0:T(8,128)S(1)} %norm.1.x_ref, s32[32,32]{1,0:T(8,128)S(1)} %copy-done.13, s32[1,128]{1,0:T(1,128)S(1)} %bitcast.17, f32[1,256]{1,0:T(1,128)S(1)} %bitcast.23, f32[1,256]{1,0:T(1,128)S(1)} %bitcast.24, bf16[64,256]{1,0:T(8,128)(2,1)S(1)} %bitcast.22, ...), custom_call_target="tpu_custom_call" | custom-call | flops 1073741824 | bytes 1088256 | tf_op jit(solution)/shard_map/pack/pallas_call | solution.py:340
  2.9 0.1 collective-permute-start
  3.0 2.7 %collective-permute-start.3 = (bf16[32,1152]{1,0:T(8,128)(2,1)S(1)}, bf16[32,1152]{1,0:T(8,128)(2,1)S(1)}, u32[]{:S(2)}, u32[]{:S(2)}) collective-permute-start(bf16[32,1152]{1,0:T(8,128)(2,1)S(1)} %get-tuple-element.21.refs_0_), channel_id=1, source_target_pairs={{0,1},{1,0},{2,3},{3,2},{4,5},{5,4},{6,7},{7,6},{8,9},{9,8},{10,11... | collective-permute-start | bytes 221192 | tf_op jit(solution)/shard_map/ppermute | solution.py:310
  5.8 3.6 %collective-permute-start.2 = (bf16[2,32,1152]{2,1,0:T(8,128)(2,1)S(1)}, bf16[2,32,1152]{2,1,0:T(8,128)(2,1)S(1)}, u32[]{:S(2)}, u32[]{:S(2)}) collective-permute-start(bf16[2,32,1152]{2,1,0:T(8,128)(2,1)S(1)} %join.2._), channel_id=1, source_target_pairs={{0,4},{1,0},{2,12},{3,8},{4,5},{5,1},{6,13},{7,9},{8,6},{9,2},{10,... | collective-permute-start | bytes 442376 | tf_op jit(solution)/shard_map/ppermute | solution.py:316
  9.4 1.9 %collective-permute-start.1 = (bf16[2,32,1152]{2,1,0:T(8,128)(2,1)S(1)}, bf16[2,32,1152]{2,1,0:T(8,128)(2,1)S(1)}, u32[]{:S(2)}, u32[]{:S(2)}) collective-permute-start(bf16[2,32,1152]{2,1,0:T(8,128)(2,1)S(1)} %join.2._), channel_id=1, source_target_pairs={{0,0},{1,4},{2,8},{3,12},{4,1},{5,5},{6,9},{7,13},{8,2},{9,6},{10,... | collective-permute-start | bytes 442376 | tf_op jit(solution)/shard_map/ppermute | solution.py:316
  11.5 1.2 %base.1 = (f32[32,32,128]{2,1,0:T(8,128)S(1)}, bf16[4096,512]{1,0:T(8,128)(2,1)S(1)}) custom-call(bf16[32,32,128]{2,1,0:T(8,128)(2,1)S(1)} %copy-done.9, bf16[66,128]{1,0:T(8,128)(2,1)S(1)} %copy-done.12, s32[1,128]{1,0:T(1,128)S(1)} %bitcast.26, bf16[1024,128]{1,0:T(8,128)(2,1)S(1)} %copy-done.10, bf16[2,32,1152]{2,1,0:T(8,128)(2,1)S(1)} %join.2._), custom_call_target="tpu_custom_call" | custom-call | flops 1073741824 | bytes 689152 | tf_op jit(solution)/shard_map/base/pallas_call | solution.py:340
  12.7 0.8 %collective-permute-done.2.refs_1_ = bf16[2,32,1152]{2,1,0:T(8,128)(2,1)S(1)} collective-permute-done((bf16[2,32,1152]{2,1,0:T(8,128)(2,1)S(1)}, bf16[2,32,1152]{2,1,0:T(8,128)(2,1)S(1)}, u32[]{:S(2)}, u32[]{:S(2)}) %collective-permute-start.2) | collective-permute-done | bytes 147488 | tf_op jit(solution)/shard_map/ppermute | solution.py:316
  13.4 4.9 %collective-permute-done.1.refs_0_ = bf16[2,32,1152]{2,1,0:T(8,128)(2,1)S(1)} collective-permute-done((bf16[2,32,1152]{2,1,0:T(8,128)(2,1)S(1)}, bf16[2,32,1152]{2,1,0:T(8,128)(2,1)S(1)}, u32[]{:S(2)}, u32[]{:S(2)}) %collective-permute-start.1) | collective-permute-done | bytes 147488 | tf_op jit(solution)/shard_map/ppermute | solution.py:316
  18.3 0.5 turn.1
  18.8 2.8 %edges.1 = (bf16[32,32,128]{2,1,0:T(8,128)(2,1)S(1)}, bf16[32,32,128]{2,1,0:T(8,128)(2,1)S(1)}, bf16[1024,128]{1,0:T(8,128)(2,1)S(1)}) custom-call(bf16[1024,128]{1,0:T(8,128)(2,1)S(1)} %get-tuple-element.19.turned_ref, bf16[32,128]{1,0:T(8,128)(2,1)S(1)} %get-tuple-element.20.live_ref, bf16[2,32,1152]{2,1,0:T(8,128)(2,1)S(1)} %join.3.own_ref, ...), custom_call_target="tpu_custom_call" | custom-call | bytes 5451776 | tf_op jit(solution)/shard_map/edges/pallas_call | solution.py:340
  21.6 1.7 %collective-permute-start.5 = (bf16[32,32,128]{2,1,0:T(8,128)(2,1)S(1)}, bf16[32,32,128]{2,1,0:T(8,128)(2,1)S(1)}, u32[]{:S(2)}, u32[]{:S(2)}) collective-permute-start(bf16[32,32,128]{2,1,0:T(8,128)(2,1)S(1)} %get-tuple-element.24), channel_id=1, source_target_pairs={{8,0},{13,1},{11,2},{14,3},{9,4},{12,5},{10,6},{15,7},{0,8},{5,9},... | collective-permute-start | bytes 786440 | tf_op jit(solution)/shard_map/ppermute | solution.py:330
  23.4 0.4 left.1.refs_0_
  23.9 0.7 %collective-permute-start.9 = (bf16[32,32,128]{2,1,0:T(8,128)(2,1)S(1)}, bf16[32,32,128]{2,1,0:T(8,128)(2,1)S(1)}, u32[]{:S(2)}, u32[]{:S(2)}) collective-permute-start(bf16[32,32,128]{2,1,0:T(8,128)(2,1)S(1)} %get-tuple-element.24), channel_id=1, source_target_pairs={{0,0},{4,1},{2,2},{6,3},{1,4},{5,5},{3,6},{7,7},{8,8},{12,9},{10,1... | collective-permute-start | bytes 786440 | tf_op jit(solution)/shard_map/ppermute | solution.py:330
  24.6 3.9 %collective-permute-start.8 = (bf16[32,32,128]{2,1,0:T(8,128)(2,1)S(1)}, bf16[32,32,128]{2,1,0:T(8,128)(2,1)S(1)}, u32[]{:S(2)}, u32[]{:S(2)}) collective-permute-start(bf16[32,32,128]{2,1,0:T(8,128)(2,1)S(1)} %get-tuple-element.24), channel_id=1, source_target_pairs={{1,0},{5,1},{3,2},{7,3},{0,4},{4,5},{2,6},{6,7},{9,8},{13,9},{11,1... | collective-permute-start | bytes 786440 | tf_op jit(solution)/shard_map/ppermute | solution.py:330
  28.5 6.0 %collective-permute-done.5.right_ref = bf16[32,32,128]{2,1,0:T(8,128)(2,1)S(1)} collective-permute-done((bf16[32,32,128]{2,1,0:T(8,128)(2,1)S(1)}, bf16[32,32,128]{2,1,0:T(8,128)(2,1)S(1)}, u32[]{:S(2)}, u32[]{:S(2)}) %collective-permute-start.5) | collective-permute-done | bytes 262176 | tf_op jit(solution)/shard_map/ppermute | solution.py:330
  34.4 0.2 collective-permute-start.6
  34.6 0.2 gate.1.refs_2_.gate_ref
  34.9 1.3 %triangle.3.far_ref = f32[1024,128]{1,0:T(8,128)S(1)} custom-call(bf16[32,32,128]{2,1,0:T(8,128)(2,1)S(1)} %collective-permute-done.5.right_ref, f32[2,1024,128]{2,1,0:T(8,128)S(1)} %panel.1.panel_ref), custom_call_target="tpu_custom_call" | custom-call | bytes 1310720 | tf_op jit(solution)/shard_map/triangle/pallas_call | solution.py:340
  36.3 1.3 %triangle.4.refs_0_ = f32[1024,128]{1,0:T(8,128)S(1)} custom-call(bf16[32,32,128]{2,1,0:T(8,128)(2,1)S(1)} %collective-permute-done.9.right_ref, f32[2,1024,128]{2,1,0:T(8,128)S(1)} %panel.1.panel_ref), custom_call_target="tpu_custom_call" | custom-call | bytes 1310720 | tf_op jit(solution)/shard_map/triangle/pallas_call | solution.py:340
  37.5 2.9 %collective-permute-done.8.right_ref = bf16[32,32,128]{2,1,0:T(8,128)(2,1)S(1)} collective-permute-done((bf16[32,32,128]{2,1,0:T(8,128)(2,1)S(1)}, bf16[32,32,128]{2,1,0:T(8,128)(2,1)S(1)}, u32[]{:S(2)}, u32[]{:S(2)}) %collective-permute-start.8) | collective-permute-done | bytes 262176 | tf_op jit(solution)/shard_map/ppermute | solution.py:330
  40.4 1.3 %triangle.5.near_ref = f32[1024,128]{1,0:T(8,128)S(1)} custom-call(bf16[32,32,128]{2,1,0:T(8,128)(2,1)S(1)} %collective-permute-done.8.right_ref, f32[2,1024,128]{2,1,0:T(8,128)S(1)} %panel.1.panel_ref, f32[1024,128]{1,0:T(8,128)S(1)} %triangle.4.refs_0_), custom_call_target="tpu_custom_call" | custom-call | bytes 1835008 | tf_op jit(solution)/shard_map/triangle/pallas_call | solution.py:340
  41.7 1.4 %collective-permute-done.6.right_ref = bf16[32,32,128]{2,1,0:T(8,128)(2,1)S(1)} collective-permute-done((bf16[32,32,128]{2,1,0:T(8,128)(2,1)S(1)}, bf16[32,32,128]{2,1,0:T(8,128)(2,1)S(1)}, u32[]{:S(2)}, u32[]{:S(2)}) %collective-permute-start.6) | collective-permute-done | bytes 262176 | tf_op jit(solution)/shard_map/ppermute | solution.py:334
  43.2 1.0 %last.3 = (f32[768,128]{1,0:T(8,128)S(1)}, bf16[768,128]{1,0:T(8,128)(2,1)S(1)}) custom-call(bf16[32,32,128]{2,1,0:T(8,128)(2,1)S(1)} %collective-permute-done.6.right_ref, f32[2,1024,128]{2,1,0:T(8,128)S(1)} %panel.1.panel_ref, f32[1024,128]{1,0:T(8,128)S(1)} %triangle.3.far_ref, f32[1024,128]{1,0:T(8,128)S(1)} %triangle.5.near_ref), custom_call_target="tpu_custom_call" | custom-call | flops 268435456 | bytes 2359296 | tf_op jit(solution)/shard_map/last/pallas_call | solution.py:340
  44.2 0.6 %collective-permute-start.11 = (bf16[768,128]{1,0:T(8,128)(2,1)S(1)}, bf16[768,128]{1,0:T(8,128)(2,1)S(1)}, u32[]{:S(2)}, u32[]{:S(2)}) collective-permute-start(bf16[768,128]{1,0:T(8,128)(2,1)S(1)} %get-tuple-element.30), channel_id=1, source_target_pairs={{0,2},{1,3},{2,0},{3,1},{4,6},{5,7},{6,4},{7,5},{8,10},{9,11},{10,... | collective-permute-start | bytes 589832 | tf_op jit(solution)/shard_map/ppermute | solution.py:305
  44.7 0.3 last.2
  45.2 0.7 %collective-permute-done.11.other_ref = bf16[768,128]{1,0:T(8,128)(2,1)S(1)} collective-permute-done((bf16[768,128]{1,0:T(8,128)(2,1)S(1)}, bf16[768,128]{1,0:T(8,128)(2,1)S(1)}, u32[]{:S(2)}, u32[]{:S(2)}) %collective-permute-start.11) | collective-permute-done | bytes 196640 | tf_op jit(solution)/shard_map/ppermute | solution.py:305
  45.8 0.4 final.2.refs_0_
  46.3 0.2 collective-permute-done.10.other_ref
  46.4 1.0 %final.3 = bf16[32,32,128]{2,1,0:T(8,128)(2,1)} custom-call(f32[256,128]{1,0:T(8,128)S(1)} %get-tuple-element.26.own_ref, bf16[256,128]{1,0:T(8,128)(2,1)S(1)} %collective-permute-done.10.other_ref, bf16[32,32,128]{2,1,0:T(8,128)(2,1)S(1)} %get-tuple-element.28.updated_ref, f32[1024,128]{1,0:T(8,128)S(1)} %gate.1.refs_2_.gate_ref, f32[1,128]{1,0:T(1,128)S(1)} %bitcast.12, ...), custom_call_target="tpu_custom_call" | custom-call | flops 268435456 | bytes 1213952 | tf_op jit(solution)/shard_map/final/pallas_call | solution.py:340
  (48 shorter events, 0.4 us)
Async XLA Ops:
  0.0 1.5 %copy-start.5 = (s32[128]{0:T(128)S(1)}, s32[128]{0:T(128)}, u32[]{:S(2)}) copy-start(s32[128]{0:T(128)} %param.22) | copy-start | bytes 1540
  0.0 1.1 %copy-start.8 = (bf16[32,32,256]{2,1,0:T(8,128)(2,1)S(1)}, bf16[32,32,256]{2,1,0:T(8,128)(2,1)}, u32[]{:S(2)}) copy-start(bf16[32,32,256]{2,1,0:T(8,128)(2,1)} %x_ref.1) | copy-start | bytes 1572868
  1.1 0.8 %copy-start.11 = (bf16[256,64]{0,1:T(8,128)(2,1)S(1)}, bf16[256,64]{0,1:T(8,128)(2,1)}, u32[]{:S(2)}) copy-start(bf16[256,64]{0,1:T(8,128)(2,1)} %param.26) | copy-start | bytes 98308
  1.1 0.8 %copy-start.13 = (s32[32,32]{1,0:T(8,128)S(1)}, s32[32,32]{1,0:T(8,128)}, u32[]{:S(2)}) copy-start(s32[32,32]{1,0:T(8,128)} %mask_ref.1) | copy-start | bytes 12292
  1.1 0.8 %copy-start.14 = (f32[256]{0:T(256)S(1)}, f32[256]{0:T(256)}, u32[]{:S(2)}) copy-start(f32[256]{0:T(256)} %param.24) | copy-start | bytes 3076
  1.1 0.8 %copy-start.15 = (f32[256]{0:T(256)S(1)}, f32[256]{0:T(256)}, u32[]{:S(2)}) copy-start(f32[256]{0:T(256)} %param.25) | copy-start | bytes 3076
  1.1 0.8 %copy-start.16 = (f32[64]{0:T(128)S(1)}, f32[64]{0:T(128)}, u32[]{:S(2)}) copy-start(f32[64]{0:T(128)} %param.27) | copy-start | bytes 772
  1.1 4.6 %copy-start.18 = (f32[640]{0:T(1024)S(1)}, f32[640]{0:T(1024)}, u32[]{:S(2)}) copy-start(f32[640]{0:T(1024)} %param.33) | copy-start | bytes 7684
  2.9 2.8 %collective-permute-start = (bf16[32,1152]{1,0:T(8,128)(2,1)S(1)}, bf16[32,1152]{1,0:T(8,128)(2,1)S(1)}, u32[]{:S(2)}, u32[]{:S(2)}) collective-permute-start(bf16[32,1152]{1,0:T(8,128)(2,1)S(1)} %get-tuple-element.18.refs_0_), channel_id=1, source_target_pairs={{0,2},{1,3},{2,0},{3,1},{4,6},{5,7},{6,4},{7,5},{8,10},{9,11},{10,... | collective-permute-start | bytes 221192 | tf_op jit(solution)/shard_map/ppermute | solution.py:305
  3.0 8.3 %collective-permute-start.3 = (bf16[32,1152]{1,0:T(8,128)(2,1)S(1)}, bf16[32,1152]{1,0:T(8,128)(2,1)S(1)}, u32[]{:S(2)}, u32[]{:S(2)}) collective-permute-start(bf16[32,1152]{1,0:T(8,128)(2,1)S(1)} %get-tuple-element.21.refs_0_), channel_id=1, source_target_pairs={{0,1},{1,0},{2,3},{3,2},{4,5},{5,4},{6,7},{7,6},{8,9},{9,8},{10,11... | collective-permute-start | bytes 221192 | tf_op jit(solution)/shard_map/ppermute | solution.py:310
  5.8 5.7 %copy-start.9 = (bf16[32,32,128]{2,1,0:T(8,128)(2,1)S(1)}, bf16[32,32,128]{2,1,0:T(8,128)(2,1)}, u32[]{:S(2)}) copy-start(bf16[32,32,128]{2,1,0:T(8,128)(2,1)} %pair_ref.1) | copy-start | bytes 786436
  5.8 5.7 %copy-start.10 = (bf16[1024,128]{1,0:T(8,128)(2,1)S(1)}, bf16[1024,128]{1,0:T(8,128)(2,1)}, u32[]{:S(2)}) copy-start(bf16[1024,128]{1,0:T(8,128)(2,1)} %w_ref.6) | copy-start | bytes 786436
  5.8 5.7 %copy-start.12 = (bf16[66,128]{1,0:T(8,128)(2,1)S(1)}, bf16[66,128]{1,0:T(8,128)(2,1)}, u32[]{:S(2)}) copy-start(bf16[66,128]{1,0:T(8,128)(2,1)} %table_ref.1) | copy-start | bytes 50692
  5.8 5.7 %copy-start.17 = (s32[128]{0:T(128)S(1)}, s32[128]{0:T(128)}, u32[]{:S(2)}) copy-start(s32[128]{0:T(128)} %param.23) | copy-start | bytes 1540
  5.8 7.6 %collective-permute-start.2 = (bf16[2,32,1152]{2,1,0:T(8,128)(2,1)S(1)}, bf16[2,32,1152]{2,1,0:T(8,128)(2,1)S(1)}, u32[]{:S(2)}, u32[]{:S(2)}) collective-permute-start(bf16[2,32,1152]{2,1,0:T(8,128)(2,1)S(1)} %join.2._), channel_id=1, source_target_pairs={{0,4},{1,0},{2,12},{3,8},{4,5},{5,1},{6,13},{7,9},{8,6},{9,2},{10,... | collective-permute-start | bytes 442376 | tf_op jit(solution)/shard_map/ppermute | solution.py:316
  9.4 8.9 %collective-permute-start.1 = (bf16[2,32,1152]{2,1,0:T(8,128)(2,1)S(1)}, bf16[2,32,1152]{2,1,0:T(8,128)(2,1)S(1)}, u32[]{:S(2)}, u32[]{:S(2)}) collective-permute-start(bf16[2,32,1152]{2,1,0:T(8,128)(2,1)S(1)} %join.2._), channel_id=1, source_target_pairs={{0,0},{1,4},{2,8},{3,12},{4,1},{5,5},{6,9},{7,13},{8,2},{9,6},{10,... | collective-permute-start | bytes 442376 | tf_op jit(solution)/shard_map/ppermute | solution.py:316
  11.3 7.5 %collective-permute-start.4 = (bf16[2,32,1152]{2,1,0:T(8,128)(2,1)S(1)}, bf16[2,32,1152]{2,1,0:T(8,128)(2,1)S(1)}, u32[]{:S(2)}, u32[]{:S(2)}) collective-permute-start(bf16[2,32,1152]{2,1,0:T(8,128)(2,1)S(1)} %join.3.own_ref), channel_id=1, source_target_pairs={{0,2},{1,3},{2,0},{3,1},{4,6},{5,7},{6,4},{7,5},{8,10},{9,11},{10,... | collective-permute-start | bytes 442376 | tf_op jit(solution)/shard_map/ppermute | solution.py:305
  12.6 6.2 %copy-start = (bf16[128,640]{1,0:T(8,128)(2,1)S(1)}, bf16[128,640]{1,0:T(8,128)(2,1)}, u32[]{:S(2)}) copy-start(bf16[128,640]{1,0:T(8,128)(2,1)} %w_ref.9) | copy-start | bytes 491524
  12.6 6.2 %copy-start.6 = (f32[128]{0:T(128)S(1)}, f32[128]{0:T(128)}, u32[]{:S(2)}) copy-start(f32[128]{0:T(128)} %param.30) | copy-start | bytes 1540
  12.7 6.2 %copy-start.7 = (f32[128]{0:T(128)S(1)}, f32[128]{0:T(128)}, u32[]{:S(2)}) copy-start(f32[128]{0:T(128)} %param.31) | copy-start | bytes 1540
  21.6 12.8 %collective-permute-start.5 = (bf16[32,32,128]{2,1,0:T(8,128)(2,1)S(1)}, bf16[32,32,128]{2,1,0:T(8,128)(2,1)S(1)}, u32[]{:S(2)}, u32[]{:S(2)}) collective-permute-start(bf16[32,32,128]{2,1,0:T(8,128)(2,1)S(1)} %get-tuple-element.24), channel_id=1, source_target_pairs={{8,0},{13,1},{11,2},{14,3},{9,4},{12,5},{10,6},{15,7},{0,8},{5,9},... | collective-permute-start | bytes 786440 | tf_op jit(solution)/shard_map/ppermute | solution.py:330
  23.8 11.1 %collective-permute-start.7 = (bf16[32,32,128]{2,1,0:T(8,128)(2,1)S(1)}, bf16[32,32,128]{2,1,0:T(8,128)(2,1)S(1)}, u32[]{:S(2)}, u32[]{:S(2)}) collective-permute-start(bf16[32,32,128]{2,1,0:T(8,128)(2,1)S(1)} %left.1.refs_0_), channel_id=1, source_target_pairs={{0,1},{1,0},{2,3},{3,2},{4,5},{5,4},{6,7},{7,6},{8,9},{9,8},{10,11... | collective-permute-start | bytes 786440 | tf_op jit(solution)/shard_map/ppermute | solution.py:310
  23.9 12.4 %collective-permute-start.9 = (bf16[32,32,128]{2,1,0:T(8,128)(2,1)S(1)}, bf16[32,32,128]{2,1,0:T(8,128)(2,1)S(1)}, u32[]{:S(2)}, u32[]{:S(2)}) collective-permute-start(bf16[32,32,128]{2,1,0:T(8,128)(2,1)S(1)} %get-tuple-element.24), channel_id=1, source_target_pairs={{0,0},{4,1},{2,2},{6,3},{1,4},{5,5},{3,6},{7,7},{8,8},{12,9},{10,1... | collective-permute-start | bytes 786440 | tf_op jit(solution)/shard_map/ppermute | solution.py:330
  24.6 15.9 %collective-permute-start.8 = (bf16[32,32,128]{2,1,0:T(8,128)(2,1)S(1)}, bf16[32,32,128]{2,1,0:T(8,128)(2,1)S(1)}, u32[]{:S(2)}, u32[]{:S(2)}) collective-permute-start(bf16[32,32,128]{2,1,0:T(8,128)(2,1)S(1)} %get-tuple-element.24), channel_id=1, source_target_pairs={{1,0},{5,1},{3,2},{7,3},{0,4},{4,5},{2,6},{6,7},{9,8},{13,9},{11,1... | collective-permute-start | bytes 786440 | tf_op jit(solution)/shard_map/ppermute | solution.py:330
  34.4 8.7 %collective-permute-start.6 = (bf16[32,32,128]{2,1,0:T(8,128)(2,1)S(1)}, bf16[32,32,128]{2,1,0:T(8,128)(2,1)S(1)}, u32[]{:S(2)}, u32[]{:S(2)}) collective-permute-start(bf16[32,32,128]{2,1,0:T(8,128)(2,1)S(1)} %collective-permute-done.5.right_ref), channel_id=1, source_target_pairs={{0,4},{4,0},{8,12},{12,8},{1,5},{5,1},{9,13},{13,9},{2,6},{6,2},{1... | collective-permute-start | bytes 786440 | tf_op jit(solution)/shard_map/ppermute | solution.py:334
  36.2 9.6 %copy-start.1 = (bf16[128,128]{1,0:T(8,128)(2,1)S(1)}, bf16[128,128]{1,0:T(8,128)(2,1)}, u32[]{:S(2)}) copy-start(bf16[128,128]{1,0:T(8,128)(2,1)} %w_ref.11) | copy-start | bytes 98308
  36.2 9.6 %copy-start.2 = (f32[128]{0:T(128)S(1)}, f32[128]{0:T(128)}, u32[]{:S(2)}) copy-start(f32[128]{0:T(128)} %param.34) | copy-start | bytes 1540
  36.2 9.6 %copy-start.3 = (f32[128]{0:T(128)S(1)}, f32[128]{0:T(128)}, u32[]{:S(2)}) copy-start(f32[128]{0:T(128)} %param.35) | copy-start | bytes 1540
  36.2 9.6 %copy-start.4 = (f32[128]{0:T(128)S(1)}, f32[128]{0:T(128)}, u32[]{:S(2)}) copy-start(f32[128]{0:T(128)} %param.37) | copy-start | bytes 1540
  44.2 1.6 %collective-permute-start.11 = (bf16[768,128]{1,0:T(8,128)(2,1)S(1)}, bf16[768,128]{1,0:T(8,128)(2,1)S(1)}, u32[]{:S(2)}, u32[]{:S(2)}) collective-permute-start(bf16[768,128]{1,0:T(8,128)(2,1)S(1)} %get-tuple-element.30), channel_id=1, source_target_pairs={{0,2},{1,3},{2,0},{3,1},{4,6},{5,7},{6,4},{7,5},{8,10},{9,11},{10,... | collective-permute-start | bytes 589832 | tf_op jit(solution)/shard_map/ppermute | solution.py:305
  45.1 1.3 %collective-permute-start.10 = (bf16[256,128]{1,0:T(8,128)(2,1)S(1)}, bf16[256,128]{1,0:T(8,128)(2,1)S(1)}, u32[]{:S(2)}, u32[]{:S(2)}) collective-permute-start(bf16[256,128]{1,0:T(8,128)(2,1)S(1)} %get-tuple-element.27), channel_id=1, source_target_pairs={{0,2},{1,3},{2,0},{3,1},{4,6},{5,7},{6,4},{7,5},{8,10},{9,11},{10,... | collective-permute-start | bytes 196616 | tf_op jit(solution)/shard_map/ppermute | solution.py:305

commit v20 on v19

--- a/solution.py
+++ b/solution.py
@@ -158,7 +158,7 @@
     counts = dot(live_ref[...], left[:, width:])
     inverse = 1.0 / jnp.maximum(counts, 1.0)
     wide = 2 * LANES
-    tall = 8
+    tall = half
     for first in range(0, width, wide):
         for d0 in range(0, half, tall):
             product = dot(turned_ref[d0 * cols:(d0 + tall) * cols, :], left[:, first:first + wide])

time: 47.8 us -> 47.8 us (level)
  no operation moved by 1% of the time
where the time goes in v20:
time: 47.8 us; the launch traced here: 47.4 us
  waiting for transfers between devices  16.8 us (35%)
  starting transfers between devices  15.6 us (33%)
  Pallas kernels  13.2 us (28%)
  local copies, waits for them, and re-layouts  1.48 us (3%)
    pallas_call x17, Pallas kernels, call(): pl.pallas_call(kernel, out_shape=outs, in_specs=[vmem] * len(args), out_s...  13.2 us
    ppermute x3, waiting for transfers between devices, send_same_core(): return lax.ppermute(block, GROUP, pairs)  8.88 us
    ppermute x3, starting transfers between devices, send_same_core(): return lax.ppermute(block, GROUP, pairs)  6.29 us
    ppermute x2, waiting for transfers between devices, send_turned(): lax.ppermute(block, GROUP, [(z * count + p, (p ^ m) * count + z) for z in...  5.66 us
    ppermute x2, starting transfers between devices, send_turned(): lax.ppermute(block, GROUP, [(z * count + p, (p ^ m) * count + z) for z in...  5.51 us
    ppermute x2, starting transfers between devices, send_chips(): lax.ppermute(block, 'seq', [(x, x ^ m) for x in range(chips)])  2.74 us
    unnamed x38, local copies, waits for them, and re-layouts  1.48 us
    ppermute x1, waiting for transfers between devices, pass_on(): return lax.ppermute(block, 'resi', [(z, z ^ 1) for z in range(count)])  1.45 us
  transfers between devices with their start and end apart: 12, of which 7 were waited for; matrix products, arithmetic and copies ran while one was open for 0% of the time, Pallas kernels for 15%

profile of v20, /device:TPU:1, one launch (start us, length us, event | category | flops | bytes accessed | tf_op | source)
XLA Modules:
  0.0 47.4 jit_solution(15538256789223939670)
XLA Ops:
  0.0 1.1 %copy-done.8 = bf16[32,32,256]{2,1,0:T(8,128)(2,1)S(1)} copy-done((bf16[32,32,256]{2,1,0:T(8,128)(2,1)S(1)}, bf16[32,32,256]{2,1,0:T(8,128)(2,1)}, u32[]{:S(2)}) %copy-start.8) | copy-done | bytes 524312
  1.1 0.4 norm.1.x_ref
  1.5 0.3 copy-done.11
  1.8 1.1 %pack.1 = (bf16[32,1152]{1,0:T(8,128)(2,1)S(1)}, bf16[32,1152]{1,0:T(8,128)(2,1)S(1)}) custom-call(f32[1024,256]{1,0:T(8,128)S(1)} %norm.1.x_ref, s32[32,32]{1,0:T(8,128)S(1)} %copy-done.13, s32[1,128]{1,0:T(1,128)S(1)} %bitcast.17, f32[1,256]{1,0:T(1,128)S(1)} %bitcast.23, f32[1,256]{1,0:T(1,128)S(1)} %bitcast.24, bf16[64,256]{1,0:T(8,128)(2,1)S(1)} %bitcast.22, ...), custom_call_target="tpu_custom_call" | custom-call | flops 1073741824 | bytes 1088256 | tf_op jit(solution)/shard_map/pack/pallas_call | solution.py:340
  2.9 0.1 collective-permute-start
  3.0 2.7 %collective-permute-start.3 = (bf16[32,1152]{1,0:T(8,128)(2,1)S(1)}, bf16[32,1152]{1,0:T(8,128)(2,1)S(1)}, u32[]{:S(2)}, u32[]{:S(2)}) collective-permute-start(bf16[32,1152]{1,0:T(8,128)(2,1)S(1)} %get-tuple-element.21.refs_0_), channel_id=1, source_target_pairs={{0,1},{1,0},{2,3},{3,2},{4,5},{5,4},{6,7},{7,6},{8,9},{9,8},{10,11... | collective-permute-start | bytes 221192 | tf_op jit(solution)/shard_map/ppermute | solution.py:310
  5.8 3.6 %collective-permute-start.2 = (bf16[2,32,1152]{2,1,0:T(8,128)(2,1)S(1)}, bf16[2,32,1152]{2,1,0:T(8,128)(2,1)S(1)}, u32[]{:S(2)}, u32[]{:S(2)}) collective-permute-start(bf16[2,32,1152]{2,1,0:T(8,128)(2,1)S(1)} %join.2._), channel_id=1, source_target_pairs={{0,4},{1,0},{2,12},{3,8},{4,5},{5,1},{6,13},{7,9},{8,6},{9,2},{10,... | collective-permute-start | bytes 442376 | tf_op jit(solution)/shard_map/ppermute | solution.py:316
  9.4 1.9 %collective-permute-start.1 = (bf16[2,32,1152]{2,1,0:T(8,128)(2,1)S(1)}, bf16[2,32,1152]{2,1,0:T(8,128)(2,1)S(1)}, u32[]{:S(2)}, u32[]{:S(2)}) collective-permute-start(bf16[2,32,1152]{2,1,0:T(8,128)(2,1)S(1)} %join.2._), channel_id=1, source_target_pairs={{0,0},{1,4},{2,8},{3,12},{4,1},{5,5},{6,9},{7,13},{8,2},{9,6},{10,... | collective-permute-start | bytes 442376 | tf_op jit(solution)/shard_map/ppermute | solution.py:316
  11.5 1.2 %base.1 = (f32[32,32,128]{2,1,0:T(8,128)S(1)}, bf16[4096,512]{1,0:T(8,128)(2,1)S(1)}) custom-call(bf16[32,32,128]{2,1,0:T(8,128)(2,1)S(1)} %copy-done.9, bf16[66,128]{1,0:T(8,128)(2,1)S(1)} %copy-done.12, s32[1,128]{1,0:T(1,128)S(1)} %bitcast.26, bf16[1024,128]{1,0:T(8,128)(2,1)S(1)} %copy-done.10, bf16[2,32,1152]{2,1,0:T(8,128)(2,1)S(1)} %join.2._), custom_call_target="tpu_custom_call" | custom-call | flops 1073741824 | bytes 689152 | tf_op jit(solution)/shard_map/base/pallas_call | solution.py:340
  12.7 0.8 %collective-permute-done.2.refs_1_ = bf16[2,32,1152]{2,1,0:T(8,128)(2,1)S(1)} collective-permute-done((bf16[2,32,1152]{2,1,0:T(8,128)(2,1)S(1)}, bf16[2,32,1152]{2,1,0:T(8,128)(2,1)S(1)}, u32[]{:S(2)}, u32[]{:S(2)}) %collective-permute-start.2) | collective-permute-done | bytes 147488 | tf_op jit(solution)/shard_map/ppermute | solution.py:316
  13.4 4.9 %collective-permute-done.1.refs_0_ = bf16[2,32,1152]{2,1,0:T(8,128)(2,1)S(1)} collective-permute-done((bf16[2,32,1152]{2,1,0:T(8,128)(2,1)S(1)}, bf16[2,32,1152]{2,1,0:T(8,128)(2,1)S(1)}, u32[]{:S(2)}, u32[]{:S(2)}) %collective-permute-start.1) | collective-permute-done | bytes 147488 | tf_op jit(solution)/shard_map/ppermute | solution.py:316
  18.3 0.5 turn.1
  18.8 2.8 %edges.1 = (bf16[32,32,128]{2,1,0:T(8,128)(2,1)S(1)}, bf16[32,32,128]{2,1,0:T(8,128)(2,1)S(1)}, bf16[1024,128]{1,0:T(8,128)(2,1)S(1)}) custom-call(bf16[1024,128]{1,0:T(8,128)(2,1)S(1)} %get-tuple-element.19.turned_ref, bf16[32,128]{1,0:T(8,128)(2,1)S(1)} %get-tuple-element.20.live_ref, bf16[2,32,1152]{2,1,0:T(8,128)(2,1)S(1)} %join.3.own_ref, ...), custom_call_target="tpu_custom_call" | custom-call | bytes 5451776 | tf_op jit(solution)/shard_map/edges/pallas_call | solution.py:340
  21.6 1.7 %collective-permute-start.5 = (bf16[32,32,128]{2,1,0:T(8,128)(2,1)S(1)}, bf16[32,32,128]{2,1,0:T(8,128)(2,1)S(1)}, u32[]{:S(2)}, u32[]{:S(2)}) collective-permute-start(bf16[32,32,128]{2,1,0:T(8,128)(2,1)S(1)} %get-tuple-element.24), channel_id=1, source_target_pairs={{8,0},{13,1},{11,2},{14,3},{9,4},{12,5},{10,6},{15,7},{0,8},{5,9},... | collective-permute-start | bytes 786440 | tf_op jit(solution)/shard_map/ppermute | solution.py:330
  23.4 0.4 left.1.refs_0_
  23.9 0.7 %collective-permute-start.9 = (bf16[32,32,128]{2,1,0:T(8,128)(2,1)S(1)}, bf16[32,32,128]{2,1,0:T(8,128)(2,1)S(1)}, u32[]{:S(2)}, u32[]{:S(2)}) collective-permute-start(bf16[32,32,128]{2,1,0:T(8,128)(2,1)S(1)} %get-tuple-element.24), channel_id=1, source_target_pairs={{0,0},{4,1},{2,2},{6,3},{1,4},{5,5},{3,6},{7,7},{8,8},{12,9},{10,1... | collective-permute-start | bytes 786440 | tf_op jit(solution)/shard_map/ppermute | solution.py:330
  24.5 3.9 %collective-permute-start.8 = (bf16[32,32,128]{2,1,0:T(8,128)(2,1)S(1)}, bf16[32,32,128]{2,1,0:T(8,128)(2,1)S(1)}, u32[]{:S(2)}, u32[]{:S(2)}) collective-permute-start(bf16[32,32,128]{2,1,0:T(8,128)(2,1)S(1)} %get-tuple-element.24), channel_id=1, source_target_pairs={{1,0},{5,1},{3,2},{7,3},{0,4},{4,5},{2,6},{6,7},{9,8},{13,9},{11,1... | collective-permute-start | bytes 786440 | tf_op jit(solution)/shard_map/ppermute | solution.py:330
  28.4 6.0 %collective-permute-done.5.right_ref = bf16[32,32,128]{2,1,0:T(8,128)(2,1)S(1)} collective-permute-done((bf16[32,32,128]{2,1,0:T(8,128)(2,1)S(1)}, bf16[32,32,128]{2,1,0:T(8,128)(2,1)S(1)}, u32[]{:S(2)}, u32[]{:S(2)}) %collective-permute-start.5) | collective-permute-done | bytes 262176 | tf_op jit(solution)/shard_map/ppermute | solution.py:330
  34.4 0.2 collective-permute-start.6
  34.6 0.2 gate.1.refs_2_.gate_ref
  34.9 1.3 %triangle.3.far_ref = f32[1024,128]{1,0:T(8,128)S(1)} custom-call(bf16[32,32,128]{2,1,0:T(8,128)(2,1)S(1)} %collective-permute-done.5.right_ref, f32[2,1024,128]{2,1,0:T(8,128)S(1)} %panel.1.panel_ref), custom_call_target="tpu_custom_call" | custom-call | bytes 1310720 | tf_op jit(solution)/shard_map/triangle/pallas_call | solution.py:340
  36.3 1.3 %triangle.4.refs_0_ = f32[1024,128]{1,0:T(8,128)S(1)} custom-call(bf16[32,32,128]{2,1,0:T(8,128)(2,1)S(1)} %collective-permute-done.9.right_ref, f32[2,1024,128]{2,1,0:T(8,128)S(1)} %panel.1.panel_ref), custom_call_target="tpu_custom_call" | custom-call | bytes 1310720 | tf_op jit(solution)/shard_map/triangle/pallas_call | solution.py:340
  37.5 2.9 %collective-permute-done.8.right_ref = bf16[32,32,128]{2,1,0:T(8,128)(2,1)S(1)} collective-permute-done((bf16[32,32,128]{2,1,0:T(8,128)(2,1)S(1)}, bf16[32,32,128]{2,1,0:T(8,128)(2,1)S(1)}, u32[]{:S(2)}, u32[]{:S(2)}) %collective-permute-start.8) | collective-permute-done | bytes 262176 | tf_op jit(solution)/shard_map/ppermute | solution.py:330
  40.4 1.3 %triangle.5.near_ref = f32[1024,128]{1,0:T(8,128)S(1)} custom-call(bf16[32,32,128]{2,1,0:T(8,128)(2,1)S(1)} %collective-permute-done.8.right_ref, f32[2,1024,128]{2,1,0:T(8,128)S(1)} %panel.1.panel_ref, f32[1024,128]{1,0:T(8,128)S(1)} %triangle.4.refs_0_), custom_call_target="tpu_custom_call" | custom-call | bytes 1835008 | tf_op jit(solution)/shard_map/triangle/pallas_call | solution.py:340
  41.7 1.4 %collective-permute-done.6.right_ref = bf16[32,32,128]{2,1,0:T(8,128)(2,1)S(1)} collective-permute-done((bf16[32,32,128]{2,1,0:T(8,128)(2,1)S(1)}, bf16[32,32,128]{2,1,0:T(8,128)(2,1)S(1)}, u32[]{:S(2)}, u32[]{:S(2)}) %collective-permute-start.6) | collective-permute-done | bytes 262176 | tf_op jit(solution)/shard_map/ppermute | solution.py:334
  43.2 1.0 %last.3 = (f32[768,128]{1,0:T(8,128)S(1)}, bf16[768,128]{1,0:T(8,128)(2,1)S(1)}) custom-call(bf16[32,32,128]{2,1,0:T(8,128)(2,1)S(1)} %collective-permute-done.6.right_ref, f32[2,1024,128]{2,1,0:T(8,128)S(1)} %panel.1.panel_ref, f32[1024,128]{1,0:T(8,128)S(1)} %triangle.3.far_ref, f32[1024,128]{1,0:T(8,128)S(1)} %triangle.5.near_ref), custom_call_target="tpu_custom_call" | custom-call | flops 268435456 | bytes 2359296 | tf_op jit(solution)/shard_map/last/pallas_call | solution.py:340
  44.2 0.6 %collective-permute-start.11 = (bf16[768,128]{1,0:T(8,128)(2,1)S(1)}, bf16[768,128]{1,0:T(8,128)(2,1)S(1)}, u32[]{:S(2)}, u32[]{:S(2)}) collective-permute-start(bf16[768,128]{1,0:T(8,128)(2,1)S(1)} %get-tuple-element.30), channel_id=1, source_target_pairs={{0,2},{1,3},{2,0},{3,1},{4,6},{5,7},{6,4},{7,5},{8,10},{9,11},{10,... | collective-permute-start | bytes 589832 | tf_op jit(solution)/shard_map/ppermute | solution.py:305
  44.7 0.3 last.2
  45.2 0.7 %collective-permute-done.11.other_ref = bf16[768,128]{1,0:T(8,128)(2,1)S(1)} collective-permute-done((bf16[768,128]{1,0:T(8,128)(2,1)S(1)}, bf16[768,128]{1,0:T(8,128)(2,1)S(1)}, u32[]{:S(2)}, u32[]{:S(2)}) %collective-permute-start.11) | collective-permute-done | bytes 196640 | tf_op jit(solution)/shard_map/ppermute | solution.py:305
  45.8 0.4 final.2.refs_0_
  46.2 0.2 collective-permute-done.10.other_ref
  46.4 1.0 %final.3 = bf16[32,32,128]{2,1,0:T(8,128)(2,1)} custom-call(f32[256,128]{1,0:T(8,128)S(1)} %get-tuple-element.26.own_ref, bf16[256,128]{1,0:T(8,128)(2,1)S(1)} %collective-permute-done.10.other_ref, bf16[32,32,128]{2,1,0:T(8,128)(2,1)S(1)} %get-tuple-element.28.updated_ref, f32[1024,128]{1,0:T(8,128)S(1)} %gate.1.refs_2_.gate_ref, f32[1,128]{1,0:T(1,128)S(1)} %bitcast.12, ...), custom_call_target="tpu_custom_call" | custom-call | flops 268435456 | bytes 1213952 | tf_op jit(solution)/shard_map/final/pallas_call | solution.py:340
  (48 shorter events, 0.4 us)
Async XLA Ops:
  0.0 1.5 %copy-start.5 = (s32[128]{0:T(128)S(1)}, s32[128]{0:T(128)}, u32[]{:S(2)}) copy-start(s32[128]{0:T(128)} %param.22) | copy-start | bytes 1540
  0.0 1.1 %copy-start.8 = (bf16[32,32,256]{2,1,0:T(8,128)(2,1)S(1)}, bf16[32,32,256]{2,1,0:T(8,128)(2,1)}, u32[]{:S(2)}) copy-start(bf16[32,32,256]{2,1,0:T(8,128)(2,1)} %x_ref.1) | copy-start | bytes 1572868
  1.1 0.8 %copy-start.11 = (bf16[256,64]{0,1:T(8,128)(2,1)S(1)}, bf16[256,64]{0,1:T(8,128)(2,1)}, u32[]{:S(2)}) copy-start(bf16[256,64]{0,1:T(8,128)(2,1)} %param.26) | copy-start | bytes 98308
  1.1 0.8 %copy-start.13 = (s32[32,32]{1,0:T(8,128)S(1)}, s32[32,32]{1,0:T(8,128)}, u32[]{:S(2)}) copy-start(s32[32,32]{1,0:T(8,128)} %mask_ref.1) | copy-start | bytes 12292
  1.1 0.8 %copy-start.14 = (f32[256]{0:T(256)S(1)}, f32[256]{0:T(256)}, u32[]{:S(2)}) copy-start(f32[256]{0:T(256)} %param.24) | copy-start | bytes 3076
  1.1 0.8 %copy-start.15 = (f32[256]{0:T(256)S(1)}, f32[256]{0:T(256)}, u32[]{:S(2)}) copy-start(f32[256]{0:T(256)} %param.25) | copy-start | bytes 3076
  1.1 0.8 %copy-start.16 = (f32[64]{0:T(128)S(1)}, f32[64]{0:T(128)}, u32[]{:S(2)}) copy-start(f32[64]{0:T(128)} %param.27) | copy-start | bytes 772
  1.1 4.6 %copy-start.18 = (f32[640]{0:T(1024)S(1)}, f32[640]{0:T(1024)}, u32[]{:S(2)}) copy-start(f32[640]{0:T(1024)} %param.33) | copy-start | bytes 7684
  2.9 2.8 %collective-permute-start = (bf16[32,1152]{1,0:T(8,128)(2,1)S(1)}, bf16[32,1152]{1,0:T(8,128)(2,1)S(1)}, u32[]{:S(2)}, u32[]{:S(2)}) collective-permute-start(bf16[32,1152]{1,0:T(8,128)(2,1)S(1)} %get-tuple-element.18.refs_0_), channel_id=1, source_target_pairs={{0,2},{1,3},{2,0},{3,1},{4,6},{5,7},{6,4},{7,5},{8,10},{9,11},{10,... | collective-permute-start | bytes 221192 | tf_op jit(solution)/shard_map/ppermute | solution.py:305
  3.0 8.3 %collective-permute-start.3 = (bf16[32,1152]{1,0:T(8,128)(2,1)S(1)}, bf16[32,1152]{1,0:T(8,128)(2,1)S(1)}, u32[]{:S(2)}, u32[]{:S(2)}) collective-permute-start(bf16[32,1152]{1,0:T(8,128)(2,1)S(1)} %get-tuple-element.21.refs_0_), channel_id=1, source_target_pairs={{0,1},{1,0},{2,3},{3,2},{4,5},{5,4},{6,7},{7,6},{8,9},{9,8},{10,11... | collective-permute-start | bytes 221192 | tf_op jit(solution)/shard_map/ppermute | solution.py:310
  5.8 5.7 %copy-start.9 = (bf16[32,32,128]{2,1,0:T(8,128)(2,1)S(1)}, bf16[32,32,128]{2,1,0:T(8,128)(2,1)}, u32[]{:S(2)}) copy-start(bf16[32,32,128]{2,1,0:T(8,128)(2,1)} %pair_ref.1) | copy-start | bytes 786436
  5.8 5.7 %copy-start.10 = (bf16[1024,128]{1,0:T(8,128)(2,1)S(1)}, bf16[1024,128]{1,0:T(8,128)(2,1)}, u32[]{:S(2)}) copy-start(bf16[1024,128]{1,0:T(8,128)(2,1)} %w_ref.6) | copy-start | bytes 786436
  5.8 5.7 %copy-start.12 = (bf16[66,128]{1,0:T(8,128)(2,1)S(1)}, bf16[66,128]{1,0:T(8,128)(2,1)}, u32[]{:S(2)}) copy-start(bf16[66,128]{1,0:T(8,128)(2,1)} %table_ref.1) | copy-start | bytes 50692
  5.8 5.7 %copy-start.17 = (s32[128]{0:T(128)S(1)}, s32[128]{0:T(128)}, u32[]{:S(2)}) copy-start(s32[128]{0:T(128)} %param.23) | copy-start | bytes 1540
  5.8 7.6 %collective-permute-start.2 = (bf16[2,32,1152]{2,1,0:T(8,128)(2,1)S(1)}, bf16[2,32,1152]{2,1,0:T(8,128)(2,1)S(1)}, u32[]{:S(2)}, u32[]{:S(2)}) collective-permute-start(bf16[2,32,1152]{2,1,0:T(8,128)(2,1)S(1)} %join.2._), channel_id=1, source_target_pairs={{0,4},{1,0},{2,12},{3,8},{4,5},{5,1},{6,13},{7,9},{8,6},{9,2},{10,... | collective-permute-start | bytes 442376 | tf_op jit(solution)/shard_map/ppermute | solution.py:316
  9.4 8.9 %collective-permute-start.1 = (bf16[2,32,1152]{2,1,0:T(8,128)(2,1)S(1)}, bf16[2,32,1152]{2,1,0:T(8,128)(2,1)S(1)}, u32[]{:S(2)}, u32[]{:S(2)}) collective-permute-start(bf16[2,32,1152]{2,1,0:T(8,128)(2,1)S(1)} %join.2._), channel_id=1, source_target_pairs={{0,0},{1,4},{2,8},{3,12},{4,1},{5,5},{6,9},{7,13},{8,2},{9,6},{10,... | collective-permute-start | bytes 442376 | tf_op jit(solution)/shard_map/ppermute | solution.py:316
  11.3 7.5 %collective-permute-start.4 = (bf16[2,32,1152]{2,1,0:T(8,128)(2,1)S(1)}, bf16[2,32,1152]{2,1,0:T(8,128)(2,1)S(1)}, u32[]{:S(2)}, u32[]{:S(2)}) collective-permute-start(bf16[2,32,1152]{2,1,0:T(8,128)(2,1)S(1)} %join.3.own_ref), channel_id=1, source_target_pairs={{0,2},{1,3},{2,0},{3,1},{4,6},{5,7},{6,4},{7,5},{8,10},{9,11},{10,... | collective-permute-start | bytes 442376 | tf_op jit(solution)/shard_map/ppermute | solution.py:305
  12.6 6.2 %copy-start = (bf16[128,640]{1,0:T(8,128)(2,1)S(1)}, bf16[128,640]{1,0:T(8,128)(2,1)}, u32[]{:S(2)}) copy-start(bf16[128,640]{1,0:T(8,128)(2,1)} %w_ref.9) | copy-start | bytes 491524
  12.6 6.2 %copy-start.6 = (f32[128]{0:T(128)S(1)}, f32[128]{0:T(128)}, u32[]{:S(2)}) copy-start(f32[128]{0:T(128)} %param.30) | copy-start | bytes 1540
  12.7 6.2 %copy-start.7 = (f32[128]{0:T(128)S(1)}, f32[128]{0:T(128)}, u32[]{:S(2)}) copy-start(f32[128]{0:T(128)} %param.31) | copy-start | bytes 1540
  21.6 12.8 %collective-permute-start.5 = (bf16[32,32,128]{2,1,0:T(8,128)(2,1)S(1)}, bf16[32,32,128]{2,1,0:T(8,128)(2,1)S(1)}, u32[]{:S(2)}, u32[]{:S(2)}) collective-permute-start(bf16[32,32,128]{2,1,0:T(8,128)(2,1)S(1)} %get-tuple-element.24), channel_id=1, source_target_pairs={{8,0},{13,1},{11,2},{14,3},{9,4},{12,5},{10,6},{15,7},{0,8},{5,9},... | collective-permute-start | bytes 786440 | tf_op jit(solution)/shard_map/ppermute | solution.py:330
  23.8 11.1 %collective-permute-start.7 = (bf16[32,32,128]{2,1,0:T(8,128)(2,1)S(1)}, bf16[32,32,128]{2,1,0:T(8,128)(2,1)S(1)}, u32[]{:S(2)}, u32[]{:S(2)}) collective-permute-start(bf16[32,32,128]{2,1,0:T(8,128)(2,1)S(1)} %left.1.refs_0_), channel_id=1, source_target_pairs={{0,1},{1,0},{2,3},{3,2},{4,5},{5,4},{6,7},{7,6},{8,9},{9,8},{10,11... | collective-permute-start | bytes 786440 | tf_op jit(solution)/shard_map/ppermute | solution.py:310
  23.9 12.4 %collective-permute-start.9 = (bf16[32,32,128]{2,1,0:T(8,128)(2,1)S(1)}, bf16[32,32,128]{2,1,0:T(8,128)(2,1)S(1)}, u32[]{:S(2)}, u32[]{:S(2)}) collective-permute-start(bf16[32,32,128]{2,1,0:T(8,128)(2,1)S(1)} %get-tuple-element.24), channel_id=1, source_target_pairs={{0,0},{4,1},{2,2},{6,3},{1,4},{5,5},{3,6},{7,7},{8,8},{12,9},{10,1... | collective-permute-start | bytes 786440 | tf_op jit(solution)/shard_map/ppermute | solution.py:330
  24.5 15.9 %collective-permute-start.8 = (bf16[32,32,128]{2,1,0:T(8,128)(2,1)S(1)}, bf16[32,32,128]{2,1,0:T(8,128)(2,1)S(1)}, u32[]{:S(2)}, u32[]{:S(2)}) collective-permute-start(bf16[32,32,128]{2,1,0:T(8,128)(2,1)S(1)} %get-tuple-element.24), channel_id=1, source_target_pairs={{1,0},{5,1},{3,2},{7,3},{0,4},{4,5},{2,6},{6,7},{9,8},{13,9},{11,1... | collective-permute-start | bytes 786440 | tf_op jit(solution)/shard_map/ppermute | solution.py:330
  34.4 8.7 %collective-permute-start.6 = (bf16[32,32,128]{2,1,0:T(8,128)(2,1)S(1)}, bf16[32,32,128]{2,1,0:T(8,128)(2,1)S(1)}, u32[]{:S(2)}, u32[]{:S(2)}) collective-permute-start(bf16[32,32,128]{2,1,0:T(8,128)(2,1)S(1)} %collective-permute-done.5.right_ref), channel_id=1, source_target_pairs={{0,4},{4,0},{8,12},{12,8},{1,5},{5,1},{9,13},{13,9},{2,6},{6,2},{1... | collective-permute-start | bytes 786440 | tf_op jit(solution)/shard_map/ppermute | solution.py:334
  36.2 9.6 %copy-start.1 = (bf16[128,128]{1,0:T(8,128)(2,1)S(1)}, bf16[128,128]{1,0:T(8,128)(2,1)}, u32[]{:S(2)}) copy-start(bf16[128,128]{1,0:T(8,128)(2,1)} %w_ref.11) | copy-start | bytes 98308
  36.2 9.6 %copy-start.2 = (f32[128]{0:T(128)S(1)}, f32[128]{0:T(128)}, u32[]{:S(2)}) copy-start(f32[128]{0:T(128)} %param.34) | copy-start | bytes 1540
  36.2 9.6 %copy-start.3 = (f32[128]{0:T(128)S(1)}, f32[128]{0:T(128)}, u32[]{:S(2)}) copy-start(f32[128]{0:T(128)} %param.35) | copy-start | bytes 1540
  36.2 9.6 %copy-start.4 = (f32[128]{0:T(128)S(1)}, f32[128]{0:T(128)}, u32[]{:S(2)}) copy-start(f32[128]{0:T(128)} %param.37) | copy-start | bytes 1540
  44.2 1.6 %collective-permute-start.11 = (bf16[768,128]{1,0:T(8,128)(2,1)S(1)}, bf16[768,128]{1,0:T(8,128)(2,1)S(1)}, u32[]{:S(2)}, u32[]{:S(2)}) collective-permute-start(bf16[768,128]{1,0:T(8,128)(2,1)S(1)} %get-tuple-element.30), channel_id=1, source_target_pairs={{0,2},{1,3},{2,0},{3,1},{4,6},{5,7},{6,4},{7,5},{8,10},{9,11},{10,... | collective-permute-start | bytes 589832 | tf_op jit(solution)/shard_map/ppermute | solution.py:305
  45.1 1.3 %collective-permute-start.10 = (bf16[256,128]{1,0:T(8,128)(2,1)S(1)}, bf16[256,128]{1,0:T(8,128)(2,1)S(1)}, u32[]{:S(2)}, u32[]{:S(2)}) collective-permute-start(bf16[256,128]{1,0:T(8,128)(2,1)S(1)} %get-tuple-element.27), channel_id=1, source_target_pairs={{0,2},{1,3},{2,0},{3,1},{4,6},{5,7},{6,4},{7,5},{8,10},{9,11},{10,... | collective-permute-start | bytes 196616 | tf_op jit(solution)/shard_map/ppermute | solution.py:305

commit v21 on v19

--- a/solution.py
+++ b/solution.py
@@ -129,7 +129,7 @@
     half = width // cols
     for step in range(pairs):
         for n in range(2):
-            rall[z ^ (step + n * pairs)] = rights[step][n]
+            rall[z ^ 1 ^ (step + n * pairs)] = rights[step][n]
     right = rall[...].reshape(total_seqs, -1)
     for at in range(0, width, LANES):
         for s in range(0, total_seqs, LANES):
@@ -315,7 +315,7 @@
     return [
         lax.ppermute(
             block, GROUP,
-            [(z * count + p, (p ^ m) * count + z) for z in range(count) for p in range(count)])
+            [(z * count + p, (p ^ m ^ 1) * count + z) for z in range(count) for p in range(count)])
         for m in range(steps)
     ]
 

time: 47.8 us -> 49.6 us (1.038)
  waiting for transfers between devices: 16.8 us -> 19 us
    ppermute x1, waiting for transfers between devices: 1.44 us -> 3.64 us  [pass_on(): return lax.ppermute(block, 'resi', [(z, z ^ 1) for z in range(count)])]
    ppermute x3, starting transfers between devices: 6.3 us -> 5.09 us  [send_same_core(): return lax.ppermute(block, GROUP, pairs)]
    ppermute x2, starting transfers between devices: 5.51 us -> 6.23 us  [send_turned(): lax.ppermute(block, GROUP, [(z * count + p, (p ^ m ^ 1) * count + z) for...]
  transfers between devices with their start and end apart: 12 -> 12, of which waited for: 7 -> 6; matrix products, arithmetic and copies ran while one was open for 0% -> 0% of each run, Pallas kernels for 15% -> 14%
where the time goes in v21:
time: 49.6 us; the launch traced here: 49.2 us
  waiting for transfers between devices  19 us (38%)
  starting transfers between devices  15.2 us (31%)
  Pallas kernels  13.2 us (27%)
  local copies, waits for them, and re-layouts  1.48 us (3%)
    pallas_call x17, Pallas kernels, call(): pl.pallas_call(kernel, out_shape=outs, in_specs=[vmem] * len(args), out_s...  13.2 us
    ppermute x3, waiting for transfers between devices, send_same_core(): return lax.ppermute(block, GROUP, pairs)  8.87 us
    ppermute x2, starting transfers between devices, send_turned(): lax.ppermute(block, GROUP, [(z * count + p, (p ^ m ^ 1) * count + z) for...  6.23 us
    ppermute x2, waiting for transfers between devices, send_turned(): lax.ppermute(block, GROUP, [(z * count + p, (p ^ m ^ 1) * count + z) for...  5.67 us
    ppermute x3, starting transfers between devices, send_same_core(): return lax.ppermute(block, GROUP, pairs)  5.09 us
    ppermute x1, waiting for transfers between devices, pass_on(): return lax.ppermute(block, 'resi', [(z, z ^ 1) for z in range(count)])  3.64 us
    ppermute x2, starting transfers between devices, send_chips(): lax.ppermute(block, 'seq', [(x, x ^ m) for x in range(chips)])  2.74 us
    unnamed x38, local copies, waits for them, and re-layouts  1.48 us
  transfers between devices with their start and end apart: 12, of which 6 were waited for; matrix products, arithmetic and copies ran while one was open for 0% of the time, Pallas kernels for 14%

profile of v21, /device:TPU:1, one launch (start us, length us, event | category | flops | bytes accessed | tf_op | source)
XLA Modules:
  0.0 49.2 jit_solution(12960816269821862295)
XLA Ops:
  0.0 1.1 %copy-done.8 = bf16[32,32,256]{2,1,0:T(8,128)(2,1)S(1)} copy-done((bf16[32,32,256]{2,1,0:T(8,128)(2,1)S(1)}, bf16[32,32,256]{2,1,0:T(8,128)(2,1)}, u32[]{:S(2)}) %copy-start.8) | copy-done | bytes 524312
  1.1 0.4 norm.1.x_ref
  1.5 0.3 copy-done.11
  1.8 1.1 %pack.1 = (bf16[32,1152]{1,0:T(8,128)(2,1)S(1)}, bf16[32,1152]{1,0:T(8,128)(2,1)S(1)}) custom-call(f32[1024,256]{1,0:T(8,128)S(1)} %norm.1.x_ref, s32[32,32]{1,0:T(8,128)S(1)} %copy-done.13, s32[1,128]{1,0:T(1,128)S(1)} %bitcast.17, f32[1,256]{1,0:T(1,128)S(1)} %bitcast.23, f32[1,256]{1,0:T(1,128)S(1)} %bitcast.24, bf16[64,256]{1,0:T(8,128)(2,1)S(1)} %bitcast.22, ...), custom_call_target="tpu_custom_call" | custom-call | flops 1073741824 | bytes 1088256 | tf_op jit(solution)/shard_map/pack/pallas_call | solution.py:340
  2.9 0.1 collective-permute-start
  3.0 2.7 %collective-permute-start.3 = (bf16[32,1152]{1,0:T(8,128)(2,1)S(1)}, bf16[32,1152]{1,0:T(8,128)(2,1)S(1)}, u32[]{:S(2)}, u32[]{:S(2)}) collective-permute-start(bf16[32,1152]{1,0:T(8,128)(2,1)S(1)} %get-tuple-element.21.refs_0_), channel_id=1, source_target_pairs={{0,1},{1,0},{2,3},{3,2},{4,5},{5,4},{6,7},{7,6},{8,9},{9,8},{10,11... | collective-permute-start | bytes 221192 | tf_op jit(solution)/shard_map/ppermute | solution.py:310
  5.8 4.6 %collective-permute-start.2 = (bf16[2,32,1152]{2,1,0:T(8,128)(2,1)S(1)}, bf16[2,32,1152]{2,1,0:T(8,128)(2,1)S(1)}, u32[]{:S(2)}, u32[]{:S(2)}) collective-permute-start(bf16[2,32,1152]{2,1,0:T(8,128)(2,1)S(1)} %join.2._), channel_id=1, source_target_pairs={{0,0},{1,4},{2,8},{3,12},{4,1},{5,5},{6,9},{7,13},{8,2},{9,6},{10,... | collective-permute-start | bytes 442376 | tf_op jit(solution)/shard_map/ppermute | solution.py:316
  10.4 1.7 %collective-permute-start.1 = (bf16[2,32,1152]{2,1,0:T(8,128)(2,1)S(1)}, bf16[2,32,1152]{2,1,0:T(8,128)(2,1)S(1)}, u32[]{:S(2)}, u32[]{:S(2)}) collective-permute-start(bf16[2,32,1152]{2,1,0:T(8,128)(2,1)S(1)} %join.2._), channel_id=1, source_target_pairs={{0,4},{1,0},{2,12},{3,8},{4,5},{5,1},{6,13},{7,9},{8,6},{9,2},{10,... | collective-permute-start | bytes 442376 | tf_op jit(solution)/shard_map/ppermute | solution.py:316
  12.2 1.2 %base.1 = (f32[32,32,128]{2,1,0:T(8,128)S(1)}, bf16[4096,512]{1,0:T(8,128)(2,1)S(1)}) custom-call(bf16[32,32,128]{2,1,0:T(8,128)(2,1)S(1)} %copy-done.9, bf16[66,128]{1,0:T(8,128)(2,1)S(1)} %copy-done.12, s32[1,128]{1,0:T(1,128)S(1)} %bitcast.26, bf16[1024,128]{1,0:T(8,128)(2,1)S(1)} %copy-done.10, bf16[2,32,1152]{2,1,0:T(8,128)(2,1)S(1)} %join.2._), custom_call_target="tpu_custom_call" | custom-call | flops 1073741824 | bytes 689152 | tf_op jit(solution)/shard_map/base/pallas_call | solution.py:340
  13.4 0.2 collective-permute-done.2.refs_1_
  13.6 5.4 %collective-permute-done.1.refs_0_ = bf16[2,32,1152]{2,1,0:T(8,128)(2,1)S(1)} collective-permute-done((bf16[2,32,1152]{2,1,0:T(8,128)(2,1)S(1)}, bf16[2,32,1152]{2,1,0:T(8,128)(2,1)S(1)}, u32[]{:S(2)}, u32[]{:S(2)}) %collective-permute-start.1) | collective-permute-done | bytes 147488 | tf_op jit(solution)/shard_map/ppermute | solution.py:316
  19.0 0.5 turn.1
  19.6 2.8 %edges.1 = (bf16[32,32,128]{2,1,0:T(8,128)(2,1)S(1)}, bf16[32,32,128]{2,1,0:T(8,128)(2,1)S(1)}, bf16[1024,128]{1,0:T(8,128)(2,1)S(1)}) custom-call(bf16[1024,128]{1,0:T(8,128)(2,1)S(1)} %get-tuple-element.19.turned_ref, bf16[32,128]{1,0:T(8,128)(2,1)S(1)} %get-tuple-element.20.live_ref, bf16[2,32,1152]{2,1,0:T(8,128)(2,1)S(1)} %join.3.own_ref, ...), custom_call_target="tpu_custom_call" | custom-call | bytes 5451776 | tf_op jit(solution)/shard_map/edges/pallas_call | solution.py:340
  22.4 0.5 %collective-permute-start.5 = (bf16[32,32,128]{2,1,0:T(8,128)(2,1)S(1)}, bf16[32,32,128]{2,1,0:T(8,128)(2,1)S(1)}, u32[]{:S(2)}, u32[]{:S(2)}) collective-permute-start(bf16[32,32,128]{2,1,0:T(8,128)(2,1)S(1)} %get-tuple-element.24), channel_id=1, source_target_pairs={{8,0},{13,1},{11,2},{14,3},{9,4},{12,5},{10,6},{15,7},{0,8},{5,9},... | collective-permute-start | bytes 786440 | tf_op jit(solution)/shard_map/ppermute | solution.py:330
  22.9 0.4 left.1.refs_0_
  23.4 0.7 %collective-permute-start.9 = (bf16[32,32,128]{2,1,0:T(8,128)(2,1)S(1)}, bf16[32,32,128]{2,1,0:T(8,128)(2,1)S(1)}, u32[]{:S(2)}, u32[]{:S(2)}) collective-permute-start(bf16[32,32,128]{2,1,0:T(8,128)(2,1)S(1)} %get-tuple-element.24), channel_id=1, source_target_pairs={{0,0},{4,1},{2,2},{6,3},{1,4},{5,5},{3,6},{7,7},{8,8},{12,9},{10,1... | collective-permute-start | bytes 786440 | tf_op jit(solution)/shard_map/ppermute | solution.py:330
  24.1 3.9 %collective-permute-start.8 = (bf16[32,32,128]{2,1,0:T(8,128)(2,1)S(1)}, bf16[32,32,128]{2,1,0:T(8,128)(2,1)S(1)}, u32[]{:S(2)}, u32[]{:S(2)}) collective-permute-start(bf16[32,32,128]{2,1,0:T(8,128)(2,1)S(1)} %get-tuple-element.24), channel_id=1, source_target_pairs={{1,0},{5,1},{3,2},{7,3},{0,4},{4,5},{2,6},{6,7},{9,8},{13,9},{11,1... | collective-permute-start | bytes 786440 | tf_op jit(solution)/shard_map/ppermute | solution.py:330
  28.0 8.9 %collective-permute-done.5.right_ref = bf16[32,32,128]{2,1,0:T(8,128)(2,1)S(1)} collective-permute-done((bf16[32,32,128]{2,1,0:T(8,128)(2,1)S(1)}, bf16[32,32,128]{2,1,0:T(8,128)(2,1)S(1)}, u32[]{:S(2)}, u32[]{:S(2)}) %collective-permute-start.5) | collective-permute-done | bytes 262176 | tf_op jit(solution)/shard_map/ppermute | solution.py:330
  36.8 0.2 gate.1.refs_2_.gate_ref
  37.1 0.1 panel.1.panel_ref
  37.2 1.3 %triangle.3.far_ref = f32[1024,128]{1,0:T(8,128)S(1)} custom-call(bf16[32,32,128]{2,1,0:T(8,128)(2,1)S(1)} %collective-permute-done.5.right_ref, f32[2,1024,128]{2,1,0:T(8,128)S(1)} %panel.1.panel_ref), custom_call_target="tpu_custom_call" | custom-call | bytes 1310720 | tf_op jit(solution)/shard_map/triangle/pallas_call | solution.py:340
  38.5 1.3 %triangle.4.refs_0_ = f32[1024,128]{1,0:T(8,128)S(1)} custom-call(bf16[32,32,128]{2,1,0:T(8,128)(2,1)S(1)} %collective-permute-done.9.right_ref, f32[2,1024,128]{2,1,0:T(8,128)S(1)} %panel.1.panel_ref), custom_call_target="tpu_custom_call" | custom-call | bytes 1310720 | tf_op jit(solution)/shard_map/triangle/pallas_call | solution.py:340
  39.8 1.3 %triangle.5.near_ref = f32[1024,128]{1,0:T(8,128)S(1)} custom-call(bf16[32,32,128]{2,1,0:T(8,128)(2,1)S(1)} %collective-permute-done.8.right_ref, f32[2,1024,128]{2,1,0:T(8,128)S(1)} %panel.1.panel_ref, f32[1024,128]{1,0:T(8,128)S(1)} %triangle.4.refs_0_), custom_call_target="tpu_custom_call" | custom-call | bytes 1835008 | tf_op jit(solution)/shard_map/triangle/pallas_call | solution.py:340
  41.1 3.6 %collective-permute-done.6.right_ref = bf16[32,32,128]{2,1,0:T(8,128)(2,1)S(1)} collective-permute-done((bf16[32,32,128]{2,1,0:T(8,128)(2,1)S(1)}, bf16[32,32,128]{2,1,0:T(8,128)(2,1)S(1)}, u32[]{:S(2)}, u32[]{:S(2)}) %collective-permute-start.6) | collective-permute-done | bytes 262176 | tf_op jit(solution)/shard_map/ppermute | solution.py:334
  44.7 1.0 %last.3 = (f32[768,128]{1,0:T(8,128)S(1)}, bf16[768,128]{1,0:T(8,128)(2,1)S(1)}) custom-call(bf16[32,32,128]{2,1,0:T(8,128)(2,1)S(1)} %collective-permute-done.6.right_ref, f32[2,1024,128]{2,1,0:T(8,128)S(1)} %panel.1.panel_ref, f32[1024,128]{1,0:T(8,128)S(1)} %triangle.3.far_ref, f32[1024,128]{1,0:T(8,128)S(1)} %triangle.5.near_ref), custom_call_target="tpu_custom_call" | custom-call | flops 268435456 | bytes 2359296 | tf_op jit(solution)/shard_map/last/pallas_call | solution.py:340
  45.7 0.9 %collective-permute-start.11 = (bf16[768,128]{1,0:T(8,128)(2,1)S(1)}, bf16[768,128]{1,0:T(8,128)(2,1)S(1)}, u32[]{:S(2)}, u32[]{:S(2)}) collective-permute-start(bf16[768,128]{1,0:T(8,128)(2,1)S(1)} %get-tuple-element.30), channel_id=1, source_target_pairs={{0,2},{1,3},{2,0},{3,1},{4,6},{5,7},{6,4},{7,5},{8,10},{9,11},{10,... | collective-permute-start | bytes 589832 | tf_op jit(solution)/shard_map/ppermute | solution.py:305
  46.6 0.3 last.2
  47.0 0.1 collective-permute-start.10
  47.0 0.7 %collective-permute-done.11.other_ref = bf16[768,128]{1,0:T(8,128)(2,1)S(1)} collective-permute-done((bf16[768,128]{1,0:T(8,128)(2,1)S(1)}, bf16[768,128]{1,0:T(8,128)(2,1)S(1)}, u32[]{:S(2)}, u32[]{:S(2)}) %collective-permute-start.11) | collective-permute-done | bytes 196640 | tf_op jit(solution)/shard_map/ppermute | solution.py:305
  47.7 0.4 final.2.refs_0_
  48.1 0.2 collective-permute-done.10.other_ref
  48.3 1.0 %final.3 = bf16[32,32,128]{2,1,0:T(8,128)(2,1)} custom-call(f32[256,128]{1,0:T(8,128)S(1)} %get-tuple-element.26.own_ref, bf16[256,128]{1,0:T(8,128)(2,1)S(1)} %collective-permute-done.10.other_ref, bf16[32,32,128]{2,1,0:T(8,128)(2,1)S(1)} %get-tuple-element.28.updated_ref, f32[1024,128]{1,0:T(8,128)S(1)} %gate.1.refs_2_.gate_ref, f32[1,128]{1,0:T(1,128)S(1)} %bitcast.12, ...), custom_call_target="tpu_custom_call" | custom-call | flops 268435456 | bytes 1213952 | tf_op jit(solution)/shard_map/final/pallas_call | solution.py:340
  (48 shorter events, 0.3 us)
Async XLA Ops:
  0.0 1.5 %copy-start.5 = (s32[128]{0:T(128)S(1)}, s32[128]{0:T(128)}, u32[]{:S(2)}) copy-start(s32[128]{0:T(128)} %param.22) | copy-start | bytes 1540
  0.0 1.1 %copy-start.8 = (bf16[32,32,256]{2,1,0:T(8,128)(2,1)S(1)}, bf16[32,32,256]{2,1,0:T(8,128)(2,1)}, u32[]{:S(2)}) copy-start(bf16[32,32,256]{2,1,0:T(8,128)(2,1)} %x_ref.1) | copy-start | bytes 1572868
  1.1 0.8 %copy-start.11 = (bf16[256,64]{0,1:T(8,128)(2,1)S(1)}, bf16[256,64]{0,1:T(8,128)(2,1)}, u32[]{:S(2)}) copy-start(bf16[256,64]{0,1:T(8,128)(2,1)} %param.26) | copy-start | bytes 98308
  1.1 0.8 %copy-start.13 = (s32[32,32]{1,0:T(8,128)S(1)}, s32[32,32]{1,0:T(8,128)}, u32[]{:S(2)}) copy-start(s32[32,32]{1,0:T(8,128)} %mask_ref.1) | copy-start | bytes 12292
  1.1 0.8 %copy-start.14 = (f32[256]{0:T(256)S(1)}, f32[256]{0:T(256)}, u32[]{:S(2)}) copy-start(f32[256]{0:T(256)} %param.24) | copy-start | bytes 3076
  1.1 0.8 %copy-start.15 = (f32[256]{0:T(256)S(1)}, f32[256]{0:T(256)}, u32[]{:S(2)}) copy-start(f32[256]{0:T(256)} %param.25) | copy-start | bytes 3076
  1.1 0.8 %copy-start.16 = (f32[64]{0:T(128)S(1)}, f32[64]{0:T(128)}, u32[]{:S(2)}) copy-start(f32[64]{0:T(128)} %param.27) | copy-start | bytes 772
  1.1 4.6 %copy-start.18 = (f32[640]{0:T(1024)S(1)}, f32[640]{0:T(1024)}, u32[]{:S(2)}) copy-start(f32[640]{0:T(1024)} %param.33) | copy-start | bytes 7684
  2.9 2.8 %collective-permute-start = (bf16[32,1152]{1,0:T(8,128)(2,1)S(1)}, bf16[32,1152]{1,0:T(8,128)(2,1)S(1)}, u32[]{:S(2)}, u32[]{:S(2)}) collective-permute-start(bf16[32,1152]{1,0:T(8,128)(2,1)S(1)} %get-tuple-element.18.refs_0_), channel_id=1, source_target_pairs={{0,2},{1,3},{2,0},{3,1},{4,6},{5,7},{6,4},{7,5},{8,10},{9,11},{10,... | collective-permute-start | bytes 221192 | tf_op jit(solution)/shard_map/ppermute | solution.py:305
  3.0 9.0 %collective-permute-start.3 = (bf16[32,1152]{1,0:T(8,128)(2,1)S(1)}, bf16[32,1152]{1,0:T(8,128)(2,1)S(1)}, u32[]{:S(2)}, u32[]{:S(2)}) collective-permute-start(bf16[32,1152]{1,0:T(8,128)(2,1)S(1)} %get-tuple-element.21.refs_0_), channel_id=1, source_target_pairs={{0,1},{1,0},{2,3},{3,2},{4,5},{5,4},{6,7},{7,6},{8,9},{9,8},{10,11... | collective-permute-start | bytes 221192 | tf_op jit(solution)/shard_map/ppermute | solution.py:310
  5.8 6.4 %copy-start.9 = (bf16[32,32,128]{2,1,0:T(8,128)(2,1)S(1)}, bf16[32,32,128]{2,1,0:T(8,128)(2,1)}, u32[]{:S(2)}) copy-start(bf16[32,32,128]{2,1,0:T(8,128)(2,1)} %pair_ref.1) | copy-start | bytes 786436
  5.8 6.4 %copy-start.10 = (bf16[1024,128]{1,0:T(8,128)(2,1)S(1)}, bf16[1024,128]{1,0:T(8,128)(2,1)}, u32[]{:S(2)}) copy-start(bf16[1024,128]{1,0:T(8,128)(2,1)} %w_ref.6) | copy-start | bytes 786436
  5.8 6.4 %copy-start.12 = (bf16[66,128]{1,0:T(8,128)(2,1)S(1)}, bf16[66,128]{1,0:T(8,128)(2,1)}, u32[]{:S(2)}) copy-start(bf16[66,128]{1,0:T(8,128)(2,1)} %table_ref.1) | copy-start | bytes 50692
  5.8 6.4 %copy-start.17 = (s32[128]{0:T(128)S(1)}, s32[128]{0:T(128)}, u32[]{:S(2)}) copy-start(s32[128]{0:T(128)} %param.23) | copy-start | bytes 1540
  5.8 7.8 %collective-permute-start.2 = (bf16[2,32,1152]{2,1,0:T(8,128)(2,1)S(1)}, bf16[2,32,1152]{2,1,0:T(8,128)(2,1)S(1)}, u32[]{:S(2)}, u32[]{:S(2)}) collective-permute-start(bf16[2,32,1152]{2,1,0:T(8,128)(2,1)S(1)} %join.2._), channel_id=1, source_target_pairs={{0,0},{1,4},{2,8},{3,12},{4,1},{5,5},{6,9},{7,13},{8,2},{9,6},{10,... | collective-permute-start | bytes 442376 | tf_op jit(solution)/shard_map/ppermute | solution.py:316
  10.4 8.7 %collective-permute-start.1 = (bf16[2,32,1152]{2,1,0:T(8,128)(2,1)S(1)}, bf16[2,32,1152]{2,1,0:T(8,128)(2,1)S(1)}, u32[]{:S(2)}, u32[]{:S(2)}) collective-permute-start(bf16[2,32,1152]{2,1,0:T(8,128)(2,1)S(1)} %join.2._), channel_id=1, source_target_pairs={{0,4},{1,0},{2,12},{3,8},{4,5},{5,1},{6,13},{7,9},{8,6},{9,2},{10,... | collective-permute-start | bytes 442376 | tf_op jit(solution)/shard_map/ppermute | solution.py:316
  12.1 7.5 %collective-permute-start.4 = (bf16[2,32,1152]{2,1,0:T(8,128)(2,1)S(1)}, bf16[2,32,1152]{2,1,0:T(8,128)(2,1)S(1)}, u32[]{:S(2)}, u32[]{:S(2)}) collective-permute-start(bf16[2,32,1152]{2,1,0:T(8,128)(2,1)S(1)} %join.3.own_ref), channel_id=1, source_target_pairs={{0,2},{1,3},{2,0},{3,1},{4,6},{5,7},{6,4},{7,5},{8,10},{9,11},{10,... | collective-permute-start | bytes 442376 | tf_op jit(solution)/shard_map/ppermute | solution.py:305
  13.3 6.2 %copy-start = (bf16[128,640]{1,0:T(8,128)(2,1)S(1)}, bf16[128,640]{1,0:T(8,128)(2,1)}, u32[]{:S(2)}) copy-start(bf16[128,640]{1,0:T(8,128)(2,1)} %w_ref.9) | copy-start | bytes 491524
  13.4 6.2 %copy-start.6 = (f32[128]{0:T(128)S(1)}, f32[128]{0:T(128)}, u32[]{:S(2)}) copy-start(f32[128]{0:T(128)} %param.30) | copy-start | bytes 1540
  13.4 6.2 %copy-start.7 = (f32[128]{0:T(128)S(1)}, f32[128]{0:T(128)}, u32[]{:S(2)}) copy-start(f32[128]{0:T(128)} %param.31) | copy-start | bytes 1540
  22.4 14.5 %collective-permute-start.5 = (bf16[32,32,128]{2,1,0:T(8,128)(2,1)S(1)}, bf16[32,32,128]{2,1,0:T(8,128)(2,1)S(1)}, u32[]{:S(2)}, u32[]{:S(2)}) collective-permute-start(bf16[32,32,128]{2,1,0:T(8,128)(2,1)S(1)} %get-tuple-element.24), channel_id=1, source_target_pairs={{8,0},{13,1},{11,2},{14,3},{9,4},{12,5},{10,6},{15,7},{0,8},{5,9},... | collective-permute-start | bytes 786440 | tf_op jit(solution)/shard_map/ppermute | solution.py:330
  23.3 13.8 %collective-permute-start.7 = (bf16[32,32,128]{2,1,0:T(8,128)(2,1)S(1)}, bf16[32,32,128]{2,1,0:T(8,128)(2,1)S(1)}, u32[]{:S(2)}, u32[]{:S(2)}) collective-permute-start(bf16[32,32,128]{2,1,0:T(8,128)(2,1)S(1)} %left.1.refs_0_), channel_id=1, source_target_pairs={{0,1},{1,0},{2,3},{3,2},{4,5},{5,4},{6,7},{7,6},{8,9},{9,8},{10,11... | collective-permute-start | bytes 786440 | tf_op jit(solution)/shard_map/ppermute | solution.py:310
  23.4 15.1 %collective-permute-start.9 = (bf16[32,32,128]{2,1,0:T(8,128)(2,1)S(1)}, bf16[32,32,128]{2,1,0:T(8,128)(2,1)S(1)}, u32[]{:S(2)}, u32[]{:S(2)}) collective-permute-start(bf16[32,32,128]{2,1,0:T(8,128)(2,1)S(1)} %get-tuple-element.24), channel_id=1, source_target_pairs={{0,0},{4,1},{2,2},{6,3},{1,4},{5,5},{3,6},{7,7},{8,8},{12,9},{10,1... | collective-permute-start | bytes 786440 | tf_op jit(solution)/shard_map/ppermute | solution.py:330
  24.1 15.7 %collective-permute-start.8 = (bf16[32,32,128]{2,1,0:T(8,128)(2,1)S(1)}, bf16[32,32,128]{2,1,0:T(8,128)(2,1)S(1)}, u32[]{:S(2)}, u32[]{:S(2)}) collective-permute-start(bf16[32,32,128]{2,1,0:T(8,128)(2,1)S(1)} %get-tuple-element.24), channel_id=1, source_target_pairs={{1,0},{5,1},{3,2},{7,3},{0,4},{4,5},{2,6},{6,7},{9,8},{13,9},{11,1... | collective-permute-start | bytes 786440 | tf_op jit(solution)/shard_map/ppermute | solution.py:330
  36.8 7.9 %collective-permute-start.6 = (bf16[32,32,128]{2,1,0:T(8,128)(2,1)S(1)}, bf16[32,32,128]{2,1,0:T(8,128)(2,1)S(1)}, u32[]{:S(2)}, u32[]{:S(2)}) collective-permute-start(bf16[32,32,128]{2,1,0:T(8,128)(2,1)S(1)} %collective-permute-done.5.right_ref), channel_id=1, source_target_pairs={{0,4},{4,0},{8,12},{12,8},{1,5},{5,1},{9,13},{13,9},{2,6},{6,2},{1... | collective-permute-start | bytes 786440 | tf_op jit(solution)/shard_map/ppermute | solution.py:334
  38.4 9.2 %copy-start.1 = (bf16[128,128]{1,0:T(8,128)(2,1)S(1)}, bf16[128,128]{1,0:T(8,128)(2,1)}, u32[]{:S(2)}) copy-start(bf16[128,128]{1,0:T(8,128)(2,1)} %w_ref.11) | copy-start | bytes 98308
  38.5 9.2 %copy-start.2 = (f32[128]{0:T(128)S(1)}, f32[128]{0:T(128)}, u32[]{:S(2)}) copy-start(f32[128]{0:T(128)} %param.34) | copy-start | bytes 1540
  38.5 9.2 %copy-start.3 = (f32[128]{0:T(128)S(1)}, f32[128]{0:T(128)}, u32[]{:S(2)}) copy-start(f32[128]{0:T(128)} %param.35) | copy-start | bytes 1540
  38.5 9.2 %copy-start.4 = (f32[128]{0:T(128)S(1)}, f32[128]{0:T(128)}, u32[]{:S(2)}) copy-start(f32[128]{0:T(128)} %param.37) | copy-start | bytes 1540
  45.7 2.0 %collective-permute-start.11 = (bf16[768,128]{1,0:T(8,128)(2,1)S(1)}, bf16[768,128]{1,0:T(8,128)(2,1)S(1)}, u32[]{:S(2)}, u32[]{:S(2)}) collective-permute-start(bf16[768,128]{1,0:T(8,128)(2,1)S(1)} %get-tuple-element.30), channel_id=1, source_target_pairs={{0,2},{1,3},{2,0},{3,1},{4,6},{5,7},{6,4},{7,5},{8,10},{9,11},{10,... | collective-permute-start | bytes 589832 | tf_op jit(solution)/shard_map/ppermute | solution.py:305
  47.0 1.3 %collective-permute-start.10 = (bf16[256,128]{1,0:T(8,128)(2,1)S(1)}, bf16[256,128]{1,0:T(8,128)(2,1)S(1)}, u32[]{:S(2)}, u32[]{:S(2)}) collective-permute-start(bf16[256,128]{1,0:T(8,128)(2,1)S(1)} %get-tuple-element.27), channel_id=1, source_target_pairs={{0,2},{1,3},{2,0},{3,1},{4,6},{5,7},{6,4},{7,5},{8,10},{9,11},{10,... | collective-permute-start | bytes 196616 | tf_op jit(solution)/shard_map/ppermute | solution.py:305

commit v22 on v19

--- a/solution.py
+++ b/solution.py
@@ -56,8 +56,10 @@
     bias = jnp.dot(jnp.broadcast_to(bias_ref[...], (8, 2 * half)), spread,
                    precision=lax.Precision.HIGHEST, preferred_element_type=F32)[0:1]
     mapped = dot(normed, wide)
-    lscr[...] = mapped[:, :LANES]
-    rscr[...] = mapped[:, LANES:]
+    pitch = rows + 1
+    for n in range(seqs):
+        lscr[n * pitch:n * pitch + rows, :] = mapped[n * rows:(n + 1) * rows, :LANES]
+        rscr[n * pitch:n * pitch + rows, :] = mapped[n * rows:(n + 1) * rows, LANES:]
     row_live = pick_rows(res_ref[...], row_start, rows)
     live = (mask_ref[...].astype(F32) * row_live).astype(BF16)
     width = rows * half
@@ -67,9 +69,9 @@
     for tile in range(width // LANES):
         at = slice(tile * LANES, (tile + 1) * LANES)
         for ref, scr, first in ((left_ref, lscr, 0), (right_ref, rscr, LANES)):
-            value = scr[pl.ds(tile * per, seqs, stride=rows), :]
+            value = scr[pl.ds(tile * per, seqs, stride=pitch), :]
             for k in range(1, per):
-                value = jnp.where(sub == k, scr[pl.ds(tile * per + k, seqs, stride=rows), :], value)
+                value = jnp.where(sub == k, scr[pl.ds(tile * per + k, seqs, stride=pitch), :], value)
             value = (value + bias[:, first:first + LANES]) * live_wide[:, at]
             ref[:, at] = value.astype(BF16)
     live_tile = dot(live, (iota((rows, LANES), 0) == iota((rows, LANES), 1)).astype(BF16))
@@ -127,16 +129,20 @@
     width, total_seqs = turned_ref.shape
     cols = live_ref.shape[0]
     half = width // cols
+    pitch = half + 1
     for step in range(pairs):
         for n in range(2):
             rall[z ^ (step + n * pairs)] = rights[step][n]
     right = rall[...].reshape(total_seqs, -1)
     for at in range(0, width, LANES):
         for s in range(0, total_seqs, LANES):
-            tscr[s // LANES, at:at + LANES, :] = right[s:s + LANES, at:at + LANES].astype(F32).T
+            block = right[s:s + LANES, at:at + LANES].astype(F32).T
+            for n in range(0, LANES, half):
+                first = (at + n) // half * pitch
+                tscr[s // LANES, first:first + half, :] = block[n:n + half]
     for d in range(half):
         for s in range(0, total_seqs, LANES):
-            turned = tscr[s // LANES, pl.ds(d, cols, stride=half), :]
+            turned = tscr[s // LANES, pl.ds(d, cols, stride=pitch), :]
             turned_ref[d * cols:(d + 1) * cols, s:s + LANES] = turned.astype(BF16)
     live_ref[...] = right[:, width:].astype(F32).T[0:cols].astype(BF16)
 
@@ -184,9 +190,10 @@
         right_edge = sigmoid(mixture[:, :channels]) * mixture[:, channels:]
         for ii in range(chunk):
             at = slice(ii * cols, (ii + 1) * cols)
-            escr[(i0 + ii) * cols:(i0 + ii + 1) * cols, :] = right_edge[at] * live[:, i0 + ii:i0 + ii + 1]
+            first = (i0 + ii) * (cols + 1)
+            escr[first:first + cols, :] = right_edge[at] * live[:, i0 + ii:i0 + ii + 1]
     for k in range(cols):
-        right_ref[k] = escr[pl.ds(k, rows, stride=cols), :].astype(BF16)
+        right_ref[k] = escr[pl.ds(k, rows, stride=cols + 1), :].astype(BF16)
 
 
 def left_kernel(normed_ref, res_ref, w_ref, bias_ref, left_ref):
@@ -387,7 +394,7 @@
                   flops=1 << 36, name="norm")
     left, right = call(
         pack_kernel, [pack, pack],
-        [pltpu.VMEM((seqs * rows, LANES), F32)] * 2,
+        [pltpu.VMEM((seqs * (rows + 1), LANES), F32)] * 2,
         [normed, sequence_pad_mask, residue, flat(homolog_standard_factor),
          flat(homolog_standard_offset), factor_mapping_matrices.T, flat(outer_side_biases)],
         flops=1 << 30, name="pack")
@@ -409,7 +416,7 @@
         functools.partial(turn_kernel, count),
         [shape((width, count * seqs), BF16), shape((cols, count * seqs), BF16)],
         [pltpu.VMEM((count,) + pack.shape, BF16),
-         pltpu.VMEM((count * seqs // LANES, width, LANES), F32)],
+         pltpu.VMEM((count * seqs // LANES, rows * (half + 1), LANES), F32)],
         rights, flops=1 << 36, name="turn")
     updated, right_edge, normed_pair = call(
         edges_kernel,
@@ -417,7 +424,7 @@
          shape((rows * cols, channels), BF16)],
         [pltpu.VMEM((count,) + pack.shape, BF16),
          pltpu.VMEM((rows // per * cols, half * LANES), BF16),
-         pltpu.VMEM((rows * cols, channels), F32)],
+         pltpu.VMEM((rows * (cols + 1), channels), F32)],
         [turned, live] + lefts + [
             base, block, residue, flat(pair_norm_gain), flat(pair_norm_bias),
             triangle_projection_weights, flat(triangle_projection_biases)],

time: 47.8 us -> 46.9 us (0.981)
  Pallas kernels: 13.2 us -> 12.3 us
    pallas_call x17, Pallas kernels: 13.2 us -> 12.3 us  [call(): pl.pallas_call(kernel, out_shape=outs, in_specs=[vmem] * len(args), out_s...]
  transfers between devices with their start and end apart: 12 -> 12, of which waited for: 7 -> 7; matrix products, arithmetic and copies ran while one was open for 0% -> 0% of each run, Pallas kernels for 15% -> 14%
where the time goes in v22:
time: 46.9 us; the launch traced here: 46.4 us
  waiting for transfers between devices  16.8 us (36%)
  starting transfers between devices  15.6 us (33%)
  Pallas kernels  12.3 us (26%)
  local copies, waits for them, and re-layouts  1.48 us (3%)
    pallas_call x17, Pallas kernels, call(): pl.pallas_call(kernel, out_shape=outs, in_specs=[vmem] * len(args), out_s...  12.3 us
    ppermute x3, waiting for transfers between devices, send_same_core(): return lax.ppermute(block, GROUP, pairs)  8.88 us
    ppermute x3, starting transfers between devices, send_same_core(): return lax.ppermute(block, GROUP, pairs)  6.29 us
    ppermute x2, waiting for transfers between devices, send_turned(): lax.ppermute(block, GROUP, [(z * count + p, (p ^ m) * count + z) for z in...  5.66 us
    ppermute x2, starting transfers between devices, send_turned(): lax.ppermute(block, GROUP, [(z * count + p, (p ^ m) * count + z) for z in...  5.51 us
    ppermute x2, starting transfers between devices, send_chips(): lax.ppermute(block, 'seq', [(x, x ^ m) for x in range(chips)])  2.74 us
    unnamed x38, local copies, waits for them, and re-layouts  1.48 us
    ppermute x1, waiting for transfers between devices, pass_on(): return lax.ppermute(block, 'resi', [(z, z ^ 1) for z in range(count)])  1.44 us
  transfers between devices with their start and end apart: 12, of which 7 were waited for; matrix products, arithmetic and copies ran while one was open for 0% of the time, Pallas kernels for 14%

profile of v22, /device:TPU:1, one launch (start us, length us, event | category | flops | bytes accessed | tf_op | source)
XLA Modules:
  0.0 46.4 jit_solution(12129955727073428791)
XLA Ops:
  0.0 1.1 %copy-done.8 = bf16[32,32,256]{2,1,0:T(8,128)(2,1)S(1)} copy-done((bf16[32,32,256]{2,1,0:T(8,128)(2,1)S(1)}, bf16[32,32,256]{2,1,0:T(8,128)(2,1)}, u32[]{:S(2)}) %copy-start.8) | copy-done | bytes 524312
  1.1 0.4 norm.1.x_ref
  1.5 0.3 copy-done.11
  1.8 0.7 %pack.1 = (bf16[32,1152]{1,0:T(8,128)(2,1)S(1)}, bf16[32,1152]{1,0:T(8,128)(2,1)S(1)}) custom-call(f32[1024,256]{1,0:T(8,128)S(1)} %norm.1.x_ref, s32[32,32]{1,0:T(8,128)S(1)} %copy-done.13, s32[1,128]{1,0:T(1,128)S(1)} %bitcast.17, f32[1,256]{1,0:T(1,128)S(1)} %bitcast.23, f32[1,256]{1,0:T(1,128)S(1)} %bitcast.24, bf16[64,256]{1,0:T(8,128)(2,1)S(1)} %bitcast.22, ...), custom_call_target="tpu_custom_call" | custom-call | flops 1073741824 | bytes 1088256 | tf_op jit(solution)/shard_map/pack/pallas_call | solution.py:347
  2.5 0.1 collective-permute-start
  2.6 2.7 %collective-permute-start.3 = (bf16[32,1152]{1,0:T(8,128)(2,1)S(1)}, bf16[32,1152]{1,0:T(8,128)(2,1)S(1)}, u32[]{:S(2)}, u32[]{:S(2)}) collective-permute-start(bf16[32,1152]{1,0:T(8,128)(2,1)S(1)} %get-tuple-element.21.refs_0_), channel_id=1, source_target_pairs={{0,1},{1,0},{2,3},{3,2},{4,5},{5,4},{6,7},{7,6},{8,9},{9,8},{10,11... | collective-permute-start | bytes 221192 | tf_op jit(solution)/shard_map/ppermute | solution.py:317
  5.4 3.6 %collective-permute-start.2 = (bf16[2,32,1152]{2,1,0:T(8,128)(2,1)S(1)}, bf16[2,32,1152]{2,1,0:T(8,128)(2,1)S(1)}, u32[]{:S(2)}, u32[]{:S(2)}) collective-permute-start(bf16[2,32,1152]{2,1,0:T(8,128)(2,1)S(1)} %join.2._), channel_id=1, source_target_pairs={{0,4},{1,0},{2,12},{3,8},{4,5},{5,1},{6,13},{7,9},{8,6},{9,2},{10,... | collective-permute-start | bytes 442376 | tf_op jit(solution)/shard_map/ppermute | solution.py:323
  9.0 1.9 %collective-permute-start.1 = (bf16[2,32,1152]{2,1,0:T(8,128)(2,1)S(1)}, bf16[2,32,1152]{2,1,0:T(8,128)(2,1)S(1)}, u32[]{:S(2)}, u32[]{:S(2)}) collective-permute-start(bf16[2,32,1152]{2,1,0:T(8,128)(2,1)S(1)} %join.2._), channel_id=1, source_target_pairs={{0,0},{1,4},{2,8},{3,12},{4,1},{5,5},{6,9},{7,13},{8,2},{9,6},{10,... | collective-permute-start | bytes 442376 | tf_op jit(solution)/shard_map/ppermute | solution.py:323
  11.0 1.2 %base.1 = (f32[32,32,128]{2,1,0:T(8,128)S(1)}, bf16[4096,512]{1,0:T(8,128)(2,1)S(1)}) custom-call(bf16[32,32,128]{2,1,0:T(8,128)(2,1)S(1)} %copy-done.9, bf16[66,128]{1,0:T(8,128)(2,1)S(1)} %copy-done.12, s32[1,128]{1,0:T(1,128)S(1)} %bitcast.26, bf16[1024,128]{1,0:T(8,128)(2,1)S(1)} %copy-done.10, bf16[2,32,1152]{2,1,0:T(8,128)(2,1)S(1)} %join.2._), custom_call_target="tpu_custom_call" | custom-call | flops 1073741824 | bytes 689152 | tf_op jit(solution)/shard_map/base/pallas_call | solution.py:347
  12.2 0.8 %collective-permute-done.2.refs_1_ = bf16[2,32,1152]{2,1,0:T(8,128)(2,1)S(1)} collective-permute-done((bf16[2,32,1152]{2,1,0:T(8,128)(2,1)S(1)}, bf16[2,32,1152]{2,1,0:T(8,128)(2,1)S(1)}, u32[]{:S(2)}, u32[]{:S(2)}) %collective-permute-start.2) | collective-permute-done | bytes 147488 | tf_op jit(solution)/shard_map/ppermute | solution.py:323
  13.0 4.9 %collective-permute-done.1.refs_0_ = bf16[2,32,1152]{2,1,0:T(8,128)(2,1)S(1)} collective-permute-done((bf16[2,32,1152]{2,1,0:T(8,128)(2,1)S(1)}, bf16[2,32,1152]{2,1,0:T(8,128)(2,1)S(1)}, u32[]{:S(2)}, u32[]{:S(2)}) %collective-permute-start.1) | collective-permute-done | bytes 147488 | tf_op jit(solution)/shard_map/ppermute | solution.py:323
  17.9 0.2 turn.1
  18.1 2.6 %edges.1 = (bf16[32,32,128]{2,1,0:T(8,128)(2,1)S(1)}, bf16[32,32,128]{2,1,0:T(8,128)(2,1)S(1)}, bf16[1024,128]{1,0:T(8,128)(2,1)S(1)}) custom-call(bf16[1024,128]{1,0:T(8,128)(2,1)S(1)} %get-tuple-element.19.turned_ref, bf16[32,128]{1,0:T(8,128)(2,1)S(1)} %get-tuple-element.20.live_ref, bf16[2,32,1152]{2,1,0:T(8,128)(2,1)S(1)} %join.3.own_ref, ...), custom_call_target="tpu_custom_call" | custom-call | bytes 5451776 | tf_op jit(solution)/shard_map/edges/pallas_call | solution.py:347
  20.7 1.7 %collective-permute-start.5 = (bf16[32,32,128]{2,1,0:T(8,128)(2,1)S(1)}, bf16[32,32,128]{2,1,0:T(8,128)(2,1)S(1)}, u32[]{:S(2)}, u32[]{:S(2)}) collective-permute-start(bf16[32,32,128]{2,1,0:T(8,128)(2,1)S(1)} %get-tuple-element.24), channel_id=1, source_target_pairs={{8,0},{13,1},{11,2},{14,3},{9,4},{12,5},{10,6},{15,7},{0,8},{5,9},... | collective-permute-start | bytes 786440 | tf_op jit(solution)/shard_map/ppermute | solution.py:337
  22.4 0.4 left.1.refs_0_
  22.9 0.7 %collective-permute-start.9 = (bf16[32,32,128]{2,1,0:T(8,128)(2,1)S(1)}, bf16[32,32,128]{2,1,0:T(8,128)(2,1)S(1)}, u32[]{:S(2)}, u32[]{:S(2)}) collective-permute-start(bf16[32,32,128]{2,1,0:T(8,128)(2,1)S(1)} %get-tuple-element.24), channel_id=1, source_target_pairs={{0,0},{4,1},{2,2},{6,3},{1,4},{5,5},{3,6},{7,7},{8,8},{12,9},{10,1... | collective-permute-start | bytes 786440 | tf_op jit(solution)/shard_map/ppermute | solution.py:337
  23.6 3.9 %collective-permute-start.8 = (bf16[32,32,128]{2,1,0:T(8,128)(2,1)S(1)}, bf16[32,32,128]{2,1,0:T(8,128)(2,1)S(1)}, u32[]{:S(2)}, u32[]{:S(2)}) collective-permute-start(bf16[32,32,128]{2,1,0:T(8,128)(2,1)S(1)} %get-tuple-element.24), channel_id=1, source_target_pairs={{1,0},{5,1},{3,2},{7,3},{0,4},{4,5},{2,6},{6,7},{9,8},{13,9},{11,1... | collective-permute-start | bytes 786440 | tf_op jit(solution)/shard_map/ppermute | solution.py:337
  27.5 6.0 %collective-permute-done.5.right_ref = bf16[32,32,128]{2,1,0:T(8,128)(2,1)S(1)} collective-permute-done((bf16[32,32,128]{2,1,0:T(8,128)(2,1)S(1)}, bf16[32,32,128]{2,1,0:T(8,128)(2,1)S(1)}, u32[]{:S(2)}, u32[]{:S(2)}) %collective-permute-start.5) | collective-permute-done | bytes 262176 | tf_op jit(solution)/shard_map/ppermute | solution.py:337
  33.5 0.2 collective-permute-start.6
  33.7 0.2 gate.1.refs_2_.gate_ref
  34.0 1.3 %triangle.3.far_ref = f32[1024,128]{1,0:T(8,128)S(1)} custom-call(bf16[32,32,128]{2,1,0:T(8,128)(2,1)S(1)} %collective-permute-done.5.right_ref, f32[2,1024,128]{2,1,0:T(8,128)S(1)} %panel.1.panel_ref), custom_call_target="tpu_custom_call" | custom-call | bytes 1310720 | tf_op jit(solution)/shard_map/triangle/pallas_call | solution.py:347
  35.3 1.3 %triangle.4.refs_0_ = f32[1024,128]{1,0:T(8,128)S(1)} custom-call(bf16[32,32,128]{2,1,0:T(8,128)(2,1)S(1)} %collective-permute-done.9.right_ref, f32[2,1024,128]{2,1,0:T(8,128)S(1)} %panel.1.panel_ref), custom_call_target="tpu_custom_call" | custom-call | bytes 1310720 | tf_op jit(solution)/shard_map/triangle/pallas_call | solution.py:347
  36.6 2.9 %collective-permute-done.8.right_ref = bf16[32,32,128]{2,1,0:T(8,128)(2,1)S(1)} collective-permute-done((bf16[32,32,128]{2,1,0:T(8,128)(2,1)S(1)}, bf16[32,32,128]{2,1,0:T(8,128)(2,1)S(1)}, u32[]{:S(2)}, u32[]{:S(2)}) %collective-permute-start.8) | collective-permute-done | bytes 262176 | tf_op jit(solution)/shard_map/ppermute | solution.py:337
  39.5 1.3 %triangle.5.near_ref = f32[1024,128]{1,0:T(8,128)S(1)} custom-call(bf16[32,32,128]{2,1,0:T(8,128)(2,1)S(1)} %collective-permute-done.8.right_ref, f32[2,1024,128]{2,1,0:T(8,128)S(1)} %panel.1.panel_ref, f32[1024,128]{1,0:T(8,128)S(1)} %triangle.4.refs_0_), custom_call_target="tpu_custom_call" | custom-call | bytes 1835008 | tf_op jit(solution)/shard_map/triangle/pallas_call | solution.py:347
  40.8 1.4 %collective-permute-done.6.right_ref = bf16[32,32,128]{2,1,0:T(8,128)(2,1)S(1)} collective-permute-done((bf16[32,32,128]{2,1,0:T(8,128)(2,1)S(1)}, bf16[32,32,128]{2,1,0:T(8,128)(2,1)S(1)}, u32[]{:S(2)}, u32[]{:S(2)}) %collective-permute-start.6) | collective-permute-done | bytes 262176 | tf_op jit(solution)/shard_map/ppermute | solution.py:341
  42.2 1.0 %last.3 = (f32[768,128]{1,0:T(8,128)S(1)}, bf16[768,128]{1,0:T(8,128)(2,1)S(1)}) custom-call(bf16[32,32,128]{2,1,0:T(8,128)(2,1)S(1)} %collective-permute-done.6.right_ref, f32[2,1024,128]{2,1,0:T(8,128)S(1)} %panel.1.panel_ref, f32[1024,128]{1,0:T(8,128)S(1)} %triangle.3.far_ref, f32[1024,128]{1,0:T(8,128)S(1)} %triangle.5.near_ref), custom_call_target="tpu_custom_call" | custom-call | flops 268435456 | bytes 2359296 | tf_op jit(solution)/shard_map/last/pallas_call | solution.py:347
  43.2 0.6 %collective-permute-start.11 = (bf16[768,128]{1,0:T(8,128)(2,1)S(1)}, bf16[768,128]{1,0:T(8,128)(2,1)S(1)}, u32[]{:S(2)}, u32[]{:S(2)}) collective-permute-start(bf16[768,128]{1,0:T(8,128)(2,1)S(1)} %get-tuple-element.30), channel_id=1, source_target_pairs={{0,2},{1,3},{2,0},{3,1},{4,6},{5,7},{6,4},{7,5},{8,10},{9,11},{10,... | collective-permute-start | bytes 589832 | tf_op jit(solution)/shard_map/ppermute | solution.py:312
  43.8 0.3 last.2
  44.2 0.7 %collective-permute-done.11.other_ref = bf16[768,128]{1,0:T(8,128)(2,1)S(1)} collective-permute-done((bf16[768,128]{1,0:T(8,128)(2,1)S(1)}, bf16[768,128]{1,0:T(8,128)(2,1)S(1)}, u32[]{:S(2)}, u32[]{:S(2)}) %collective-permute-start.11) | collective-permute-done | bytes 196640 | tf_op jit(solution)/shard_map/ppermute | solution.py:312
  44.9 0.4 final.2.refs_0_
  45.3 0.2 collective-permute-done.10.other_ref
  45.5 1.0 %final.3 = bf16[32,32,128]{2,1,0:T(8,128)(2,1)} custom-call(f32[256,128]{1,0:T(8,128)S(1)} %get-tuple-element.26.own_ref, bf16[256,128]{1,0:T(8,128)(2,1)S(1)} %collective-permute-done.10.other_ref, bf16[32,32,128]{2,1,0:T(8,128)(2,1)S(1)} %get-tuple-element.28.updated_ref, f32[1024,128]{1,0:T(8,128)S(1)} %gate.1.refs_2_.gate_ref, f32[1,128]{1,0:T(1,128)S(1)} %bitcast.12, ...), custom_call_target="tpu_custom_call" | custom-call | flops 268435456 | bytes 1213952 | tf_op jit(solution)/shard_map/final/pallas_call | solution.py:347
  (48 shorter events, 0.4 us)
Async XLA Ops:
  0.0 1.5 %copy-start.5 = (s32[128]{0:T(128)S(1)}, s32[128]{0:T(128)}, u32[]{:S(2)}) copy-start(s32[128]{0:T(128)} %param.22) | copy-start | bytes 1540
  0.0 1.1 %copy-start.8 = (bf16[32,32,256]{2,1,0:T(8,128)(2,1)S(1)}, bf16[32,32,256]{2,1,0:T(8,128)(2,1)}, u32[]{:S(2)}) copy-start(bf16[32,32,256]{2,1,0:T(8,128)(2,1)} %x_ref.1) | copy-start | bytes 1572868
  1.1 0.8 %copy-start.11 = (bf16[256,64]{0,1:T(8,128)(2,1)S(1)}, bf16[256,64]{0,1:T(8,128)(2,1)}, u32[]{:S(2)}) copy-start(bf16[256,64]{0,1:T(8,128)(2,1)} %param.26) | copy-start | bytes 98308
  1.1 0.8 %copy-start.13 = (s32[32,32]{1,0:T(8,128)S(1)}, s32[32,32]{1,0:T(8,128)}, u32[]{:S(2)}) copy-start(s32[32,32]{1,0:T(8,128)} %mask_ref.1) | copy-start | bytes 12292
  1.1 0.8 %copy-start.14 = (f32[256]{0:T(256)S(1)}, f32[256]{0:T(256)}, u32[]{:S(2)}) copy-start(f32[256]{0:T(256)} %param.24) | copy-start | bytes 3076
  1.1 0.8 %copy-start.15 = (f32[256]{0:T(256)S(1)}, f32[256]{0:T(256)}, u32[]{:S(2)}) copy-start(f32[256]{0:T(256)} %param.25) | copy-start | bytes 3076
  1.1 0.8 %copy-start.16 = (f32[64]{0:T(128)S(1)}, f32[64]{0:T(128)}, u32[]{:S(2)}) copy-start(f32[64]{0:T(128)} %param.27) | copy-start | bytes 772
  1.1 4.2 %copy-start.18 = (f32[640]{0:T(1024)S(1)}, f32[640]{0:T(1024)}, u32[]{:S(2)}) copy-start(f32[640]{0:T(1024)} %param.33) | copy-start | bytes 7684
  2.5 2.8 %collective-permute-start = (bf16[32,1152]{1,0:T(8,128)(2,1)S(1)}, bf16[32,1152]{1,0:T(8,128)(2,1)S(1)}, u32[]{:S(2)}, u32[]{:S(2)}) collective-permute-start(bf16[32,1152]{1,0:T(8,128)(2,1)S(1)} %get-tuple-element.18.refs_0_), channel_id=1, source_target_pairs={{0,2},{1,3},{2,0},{3,1},{4,6},{5,7},{6,4},{7,5},{8,10},{9,11},{10,... | collective-permute-start | bytes 221192 | tf_op jit(solution)/shard_map/ppermute | solution.py:312
  2.6 8.3 %collective-permute-start.3 = (bf16[32,1152]{1,0:T(8,128)(2,1)S(1)}, bf16[32,1152]{1,0:T(8,128)(2,1)S(1)}, u32[]{:S(2)}, u32[]{:S(2)}) collective-permute-start(bf16[32,1152]{1,0:T(8,128)(2,1)S(1)} %get-tuple-element.21.refs_0_), channel_id=1, source_target_pairs={{0,1},{1,0},{2,3},{3,2},{4,5},{5,4},{6,7},{7,6},{8,9},{9,8},{10,11... | collective-permute-start | bytes 221192 | tf_op jit(solution)/shard_map/ppermute | solution.py:317
  5.3 5.7 %copy-start.9 = (bf16[32,32,128]{2,1,0:T(8,128)(2,1)S(1)}, bf16[32,32,128]{2,1,0:T(8,128)(2,1)}, u32[]{:S(2)}) copy-start(bf16[32,32,128]{2,1,0:T(8,128)(2,1)} %pair_ref.1) | copy-start | bytes 786436
  5.3 5.7 %copy-start.10 = (bf16[1024,128]{1,0:T(8,128)(2,1)S(1)}, bf16[1024,128]{1,0:T(8,128)(2,1)}, u32[]{:S(2)}) copy-start(bf16[1024,128]{1,0:T(8,128)(2,1)} %w_ref.6) | copy-start | bytes 786436
  5.3 5.7 %copy-start.12 = (bf16[66,128]{1,0:T(8,128)(2,1)S(1)}, bf16[66,128]{1,0:T(8,128)(2,1)}, u32[]{:S(2)}) copy-start(bf16[66,128]{1,0:T(8,128)(2,1)} %table_ref.1) | copy-start | bytes 50692
  5.4 5.7 %copy-start.17 = (s32[128]{0:T(128)S(1)}, s32[128]{0:T(128)}, u32[]{:S(2)}) copy-start(s32[128]{0:T(128)} %param.23) | copy-start | bytes 1540
  5.4 7.6 %collective-permute-start.2 = (bf16[2,32,1152]{2,1,0:T(8,128)(2,1)S(1)}, bf16[2,32,1152]{2,1,0:T(8,128)(2,1)S(1)}, u32[]{:S(2)}, u32[]{:S(2)}) collective-permute-start(bf16[2,32,1152]{2,1,0:T(8,128)(2,1)S(1)} %join.2._), channel_id=1, source_target_pairs={{0,4},{1,0},{2,12},{3,8},{4,5},{5,1},{6,13},{7,9},{8,6},{9,2},{10,... | collective-permute-start | bytes 442376 | tf_op jit(solution)/shard_map/ppermute | solution.py:323
  9.0 8.9 %collective-permute-start.1 = (bf16[2,32,1152]{2,1,0:T(8,128)(2,1)S(1)}, bf16[2,32,1152]{2,1,0:T(8,128)(2,1)S(1)}, u32[]{:S(2)}, u32[]{:S(2)}) collective-permute-start(bf16[2,32,1152]{2,1,0:T(8,128)(2,1)S(1)} %join.2._), channel_id=1, source_target_pairs={{0,0},{1,4},{2,8},{3,12},{4,1},{5,5},{6,9},{7,13},{8,2},{9,6},{10,... | collective-permute-start | bytes 442376 | tf_op jit(solution)/shard_map/ppermute | solution.py:323
  10.9 7.2 %collective-permute-start.4 = (bf16[2,32,1152]{2,1,0:T(8,128)(2,1)S(1)}, bf16[2,32,1152]{2,1,0:T(8,128)(2,1)S(1)}, u32[]{:S(2)}, u32[]{:S(2)}) collective-permute-start(bf16[2,32,1152]{2,1,0:T(8,128)(2,1)S(1)} %join.3.own_ref), channel_id=1, source_target_pairs={{0,2},{1,3},{2,0},{3,1},{4,6},{5,7},{6,4},{7,5},{8,10},{9,11},{10,... | collective-permute-start | bytes 442376 | tf_op jit(solution)/shard_map/ppermute | solution.py:312
  12.2 5.9 %copy-start = (bf16[128,640]{1,0:T(8,128)(2,1)S(1)}, bf16[128,640]{1,0:T(8,128)(2,1)}, u32[]{:S(2)}) copy-start(bf16[128,640]{1,0:T(8,128)(2,1)} %w_ref.9) | copy-start | bytes 491524
  12.2 5.9 %copy-start.6 = (f32[128]{0:T(128)S(1)}, f32[128]{0:T(128)}, u32[]{:S(2)}) copy-start(f32[128]{0:T(128)} %param.30) | copy-start | bytes 1540
  12.2 5.9 %copy-start.7 = (f32[128]{0:T(128)S(1)}, f32[128]{0:T(128)}, u32[]{:S(2)}) copy-start(f32[128]{0:T(128)} %param.31) | copy-start | bytes 1540
  20.7 12.8 %collective-permute-start.5 = (bf16[32,32,128]{2,1,0:T(8,128)(2,1)S(1)}, bf16[32,32,128]{2,1,0:T(8,128)(2,1)S(1)}, u32[]{:S(2)}, u32[]{:S(2)}) collective-permute-start(bf16[32,32,128]{2,1,0:T(8,128)(2,1)S(1)} %get-tuple-element.24), channel_id=1, source_target_pairs={{8,0},{13,1},{11,2},{14,3},{9,4},{12,5},{10,6},{15,7},{0,8},{5,9},... | collective-permute-start | bytes 786440 | tf_op jit(solution)/shard_map/ppermute | solution.py:337
  22.8 11.1 %collective-permute-start.7 = (bf16[32,32,128]{2,1,0:T(8,128)(2,1)S(1)}, bf16[32,32,128]{2,1,0:T(8,128)(2,1)S(1)}, u32[]{:S(2)}, u32[]{:S(2)}) collective-permute-start(bf16[32,32,128]{2,1,0:T(8,128)(2,1)S(1)} %left.1.refs_0_), channel_id=1, source_target_pairs={{0,1},{1,0},{2,3},{3,2},{4,5},{5,4},{6,7},{7,6},{8,9},{9,8},{10,11... | collective-permute-start | bytes 786440 | tf_op jit(solution)/shard_map/ppermute | solution.py:317
  22.9 12.4 %collective-permute-start.9 = (bf16[32,32,128]{2,1,0:T(8,128)(2,1)S(1)}, bf16[32,32,128]{2,1,0:T(8,128)(2,1)S(1)}, u32[]{:S(2)}, u32[]{:S(2)}) collective-permute-start(bf16[32,32,128]{2,1,0:T(8,128)(2,1)S(1)} %get-tuple-element.24), channel_id=1, source_target_pairs={{0,0},{4,1},{2,2},{6,3},{1,4},{5,5},{3,6},{7,7},{8,8},{12,9},{10,1... | collective-permute-start | bytes 786440 | tf_op jit(solution)/shard_map/ppermute | solution.py:337
  23.6 15.9 %collective-permute-start.8 = (bf16[32,32,128]{2,1,0:T(8,128)(2,1)S(1)}, bf16[32,32,128]{2,1,0:T(8,128)(2,1)S(1)}, u32[]{:S(2)}, u32[]{:S(2)}) collective-permute-start(bf16[32,32,128]{2,1,0:T(8,128)(2,1)S(1)} %get-tuple-element.24), channel_id=1, source_target_pairs={{1,0},{5,1},{3,2},{7,3},{0,4},{4,5},{2,6},{6,7},{9,8},{13,9},{11,1... | collective-permute-start | bytes 786440 | tf_op jit(solution)/shard_map/ppermute | solution.py:337
  33.5 8.7 %collective-permute-start.6 = (bf16[32,32,128]{2,1,0:T(8,128)(2,1)S(1)}, bf16[32,32,128]{2,1,0:T(8,128)(2,1)S(1)}, u32[]{:S(2)}, u32[]{:S(2)}) collective-permute-start(bf16[32,32,128]{2,1,0:T(8,128)(2,1)S(1)} %collective-permute-done.5.right_ref), channel_id=1, source_target_pairs={{0,4},{4,0},{8,12},{12,8},{1,5},{5,1},{9,13},{13,9},{2,6},{6,2},{1... | collective-permute-start | bytes 786440 | tf_op jit(solution)/shard_map/ppermute | solution.py:341
  35.3 9.6 %copy-start.1 = (bf16[128,128]{1,0:T(8,128)(2,1)S(1)}, bf16[128,128]{1,0:T(8,128)(2,1)}, u32[]{:S(2)}) copy-start(bf16[128,128]{1,0:T(8,128)(2,1)} %w_ref.11) | copy-start | bytes 98308
  35.3 9.6 %copy-start.2 = (f32[128]{0:T(128)S(1)}, f32[128]{0:T(128)}, u32[]{:S(2)}) copy-start(f32[128]{0:T(128)} %param.34) | copy-start | bytes 1540
  35.3 9.6 %copy-start.3 = (f32[128]{0:T(128)S(1)}, f32[128]{0:T(128)}, u32[]{:S(2)}) copy-start(f32[128]{0:T(128)} %param.35) | copy-start | bytes 1540
  35.3 9.6 %copy-start.4 = (f32[128]{0:T(128)S(1)}, f32[128]{0:T(128)}, u32[]{:S(2)}) copy-start(f32[128]{0:T(128)} %param.37) | copy-start | bytes 1540
  43.2 1.7 %collective-permute-start.11 = (bf16[768,128]{1,0:T(8,128)(2,1)S(1)}, bf16[768,128]{1,0:T(8,128)(2,1)S(1)}, u32[]{:S(2)}, u32[]{:S(2)}) collective-permute-start(bf16[768,128]{1,0:T(8,128)(2,1)S(1)} %get-tuple-element.30), channel_id=1, source_target_pairs={{0,2},{1,3},{2,0},{3,1},{4,6},{5,7},{6,4},{7,5},{8,10},{9,11},{10,... | collective-permute-start | bytes 589832 | tf_op jit(solution)/shard_map/ppermute | solution.py:312
  44.1 1.3 %collective-permute-start.10 = (bf16[256,128]{1,0:T(8,128)(2,1)S(1)}, bf16[256,128]{1,0:T(8,128)(2,1)S(1)}, u32[]{:S(2)}, u32[]{:S(2)}) collective-permute-start(bf16[256,128]{1,0:T(8,128)(2,1)S(1)} %get-tuple-element.27), channel_id=1, source_target_pairs={{0,2},{1,3},{2,0},{3,1},{4,6},{5,7},{6,4},{7,5},{8,10},{9,11},{10,... | collective-permute-start | bytes 196616 | tf_op jit(solution)/shard_map/ppermute | solution.py:312

commit v23 on v22

--- a/solution.py
+++ b/solution.py
@@ -112,12 +112,14 @@
     for i in range(rows):
         one_hot = (lane == bins[:, i:i + 1]).astype(F32).astype(BF16)
         base_ref[i] = pair_ref[i].astype(F32) + dot(one_hot, table)
-    wscr[...] = w_ref[...].astype(F32)
     half = int(round(w_ref.shape[0] ** 0.5))
     per = LANES // half
+    for c in range(half):
+        first = c * (half + 1)
+        wscr[first:first + half, :] = w_ref[c * half:(c + 1) * half, :].astype(F32)
     block_ref[...] = jnp.zeros_like(block_ref)
     for d in range(half):
-        value = wscr[pl.ds(d, half, stride=half), :].astype(BF16)
+        value = wscr[pl.ds(d, half, stride=half + 1), :].astype(BF16)
         for k in range(per):
             block_ref[pl.ds(d * LANES + k * half, half), k * channels:(k + 1) * channels] = value
 
@@ -405,7 +407,7 @@
     base, block = call(
         base_kernel,
         [shape((rows, cols, channels), F32), shape((half * LANES, per * channels), BF16)],
-        [pltpu.VMEM((LANES, channels), F32), pltpu.VMEM((half * half, channels), F32)],
+        [pltpu.VMEM((LANES, channels), F32), pltpu.VMEM((half * (half + 1), channels), F32)],
         [pair_features, relative_position_table, chain, outer_pair_projection, pair],
         flops=1 << 30, name="base")
     rights = send_turned(pair, count, count // 2)

time: 46.9 us -> 46.9 us (level)
  no operation moved by 1% of the time
where the time goes in v23:
time: 46.9 us; the launch traced here: 46.4 us
  waiting for transfers between devices  17.1 us (36%)
  starting transfers between devices  15.6 us (33%)
  Pallas kernels  12 us (26%)
  local copies, waits for them, and re-layouts  1.48 us (3%)
    pallas_call x17, Pallas kernels, call(): pl.pallas_call(kernel, out_shape=outs, in_specs=[vmem] * len(args), out_s...  12 us
    ppermute x3, waiting for transfers between devices, send_same_core(): return lax.ppermute(block, GROUP, pairs)  8.88 us
    ppermute x3, starting transfers between devices, send_same_core(): return lax.ppermute(block, GROUP, pairs)  6.29 us
    ppermute x2, waiting for transfers between devices, send_turned(): lax.ppermute(block, GROUP, [(z * count + p, (p ^ m) * count + z) for z in...  5.94 us
    ppermute x2, starting transfers between devices, send_turned(): lax.ppermute(block, GROUP, [(z * count + p, (p ^ m) * count + z) for z in...  5.51 us
    ppermute x2, starting transfers between devices, send_chips(): lax.ppermute(block, 'seq', [(x, x ^ m) for x in range(chips)])  2.74 us
    unnamed x38, local copies, waits for them, and re-layouts  1.48 us
    ppermute x1, waiting for transfers between devices, pass_on(): return lax.ppermute(block, 'resi', [(z, z ^ 1) for z in range(count)])  1.44 us
  transfers between devices with their start and end apart: 12, of which 7 were waited for; matrix products, arithmetic and copies ran while one was open for 0% of the time, Pallas kernels for 14%

profile of v23, /device:TPU:1, one launch (start us, length us, event | category | flops | bytes accessed | tf_op | source)
XLA Modules:
  0.0 46.4 jit_solution(17170431408909164025)
XLA Ops:
  0.0 1.1 %copy-done.8 = bf16[32,32,256]{2,1,0:T(8,128)(2,1)S(1)} copy-done((bf16[32,32,256]{2,1,0:T(8,128)(2,1)S(1)}, bf16[32,32,256]{2,1,0:T(8,128)(2,1)}, u32[]{:S(2)}) %copy-start.8) | copy-done | bytes 524312
  1.1 0.4 norm.1.x_ref
  1.5 0.3 copy-done.11
  1.8 0.7 %pack.1 = (bf16[32,1152]{1,0:T(8,128)(2,1)S(1)}, bf16[32,1152]{1,0:T(8,128)(2,1)S(1)}) custom-call(f32[1024,256]{1,0:T(8,128)S(1)} %norm.1.x_ref, s32[32,32]{1,0:T(8,128)S(1)} %copy-done.13, s32[1,128]{1,0:T(1,128)S(1)} %bitcast.17, f32[1,256]{1,0:T(1,128)S(1)} %bitcast.23, f32[1,256]{1,0:T(1,128)S(1)} %bitcast.24, bf16[64,256]{1,0:T(8,128)(2,1)S(1)} %bitcast.22, ...), custom_call_target="tpu_custom_call" | custom-call | flops 1073741824 | bytes 1088256 | tf_op jit(solution)/shard_map/pack/pallas_call | solution.py:349
  2.5 0.1 collective-permute-start
  2.6 2.7 %collective-permute-start.3 = (bf16[32,1152]{1,0:T(8,128)(2,1)S(1)}, bf16[32,1152]{1,0:T(8,128)(2,1)S(1)}, u32[]{:S(2)}, u32[]{:S(2)}) collective-permute-start(bf16[32,1152]{1,0:T(8,128)(2,1)S(1)} %get-tuple-element.21.refs_0_), channel_id=1, source_target_pairs={{0,1},{1,0},{2,3},{3,2},{4,5},{5,4},{6,7},{7,6},{8,9},{9,8},{10,11... | collective-permute-start | bytes 221192 | tf_op jit(solution)/shard_map/ppermute | solution.py:319
  5.4 3.6 %collective-permute-start.2 = (bf16[2,32,1152]{2,1,0:T(8,128)(2,1)S(1)}, bf16[2,32,1152]{2,1,0:T(8,128)(2,1)S(1)}, u32[]{:S(2)}, u32[]{:S(2)}) collective-permute-start(bf16[2,32,1152]{2,1,0:T(8,128)(2,1)S(1)} %join.2._), channel_id=1, source_target_pairs={{0,4},{1,0},{2,12},{3,8},{4,5},{5,1},{6,13},{7,9},{8,6},{9,2},{10,... | collective-permute-start | bytes 442376 | tf_op jit(solution)/shard_map/ppermute | solution.py:325
  9.0 1.9 %collective-permute-start.1 = (bf16[2,32,1152]{2,1,0:T(8,128)(2,1)S(1)}, bf16[2,32,1152]{2,1,0:T(8,128)(2,1)S(1)}, u32[]{:S(2)}, u32[]{:S(2)}) collective-permute-start(bf16[2,32,1152]{2,1,0:T(8,128)(2,1)S(1)} %join.2._), channel_id=1, source_target_pairs={{0,0},{1,4},{2,8},{3,12},{4,1},{5,5},{6,9},{7,13},{8,2},{9,6},{10,... | collective-permute-start | bytes 442376 | tf_op jit(solution)/shard_map/ppermute | solution.py:325
  11.0 0.9 %base.1 = (f32[32,32,128]{2,1,0:T(8,128)S(1)}, bf16[4096,512]{1,0:T(8,128)(2,1)S(1)}) custom-call(bf16[32,32,128]{2,1,0:T(8,128)(2,1)S(1)} %copy-done.9, bf16[66,128]{1,0:T(8,128)(2,1)S(1)} %copy-done.12, s32[1,128]{1,0:T(1,128)S(1)} %bitcast.26, bf16[1024,128]{1,0:T(8,128)(2,1)S(1)} %copy-done.10, bf16[2,32,1152]{2,1,0:T(8,128)(2,1)S(1)} %join.2._), custom_call_target="tpu_custom_call" | custom-call | flops 1073741824 | bytes 689152 | tf_op jit(solution)/shard_map/base/pallas_call | solution.py:349
  12.0 1.0 %collective-permute-done.2.refs_1_ = bf16[2,32,1152]{2,1,0:T(8,128)(2,1)S(1)} collective-permute-done((bf16[2,32,1152]{2,1,0:T(8,128)(2,1)S(1)}, bf16[2,32,1152]{2,1,0:T(8,128)(2,1)S(1)}, u32[]{:S(2)}, u32[]{:S(2)}) %collective-permute-start.2) | collective-permute-done | bytes 147488 | tf_op jit(solution)/shard_map/ppermute | solution.py:325
  13.0 4.9 %collective-permute-done.1.refs_0_ = bf16[2,32,1152]{2,1,0:T(8,128)(2,1)S(1)} collective-permute-done((bf16[2,32,1152]{2,1,0:T(8,128)(2,1)S(1)}, bf16[2,32,1152]{2,1,0:T(8,128)(2,1)S(1)}, u32[]{:S(2)}, u32[]{:S(2)}) %collective-permute-start.1) | collective-permute-done | bytes 147488 | tf_op jit(solution)/shard_map/ppermute | solution.py:325
  17.9 0.2 turn.1
  18.1 2.6 %edges.1 = (bf16[32,32,128]{2,1,0:T(8,128)(2,1)S(1)}, bf16[32,32,128]{2,1,0:T(8,128)(2,1)S(1)}, bf16[1024,128]{1,0:T(8,128)(2,1)S(1)}) custom-call(bf16[1024,128]{1,0:T(8,128)(2,1)S(1)} %get-tuple-element.19.turned_ref, bf16[32,128]{1,0:T(8,128)(2,1)S(1)} %get-tuple-element.20.live_ref, bf16[2,32,1152]{2,1,0:T(8,128)(2,1)S(1)} %join.3.own_ref, ...), custom_call_target="tpu_custom_call" | custom-call | bytes 5451776 | tf_op jit(solution)/shard_map/edges/pallas_call | solution.py:349
  20.7 1.7 %collective-permute-start.5 = (bf16[32,32,128]{2,1,0:T(8,128)(2,1)S(1)}, bf16[32,32,128]{2,1,0:T(8,128)(2,1)S(1)}, u32[]{:S(2)}, u32[]{:S(2)}) collective-permute-start(bf16[32,32,128]{2,1,0:T(8,128)(2,1)S(1)} %get-tuple-element.24), channel_id=1, source_target_pairs={{8,0},{13,1},{11,2},{14,3},{9,4},{12,5},{10,6},{15,7},{0,8},{5,9},... | collective-permute-start | bytes 786440 | tf_op jit(solution)/shard_map/ppermute | solution.py:339
  22.4 0.4 left.1.refs_0_
  22.9 0.7 %collective-permute-start.9 = (bf16[32,32,128]{2,1,0:T(8,128)(2,1)S(1)}, bf16[32,32,128]{2,1,0:T(8,128)(2,1)S(1)}, u32[]{:S(2)}, u32[]{:S(2)}) collective-permute-start(bf16[32,32,128]{2,1,0:T(8,128)(2,1)S(1)} %get-tuple-element.24), channel_id=1, source_target_pairs={{0,0},{4,1},{2,2},{6,3},{1,4},{5,5},{3,6},{7,7},{8,8},{12,9},{10,1... | collective-permute-start | bytes 786440 | tf_op jit(solution)/shard_map/ppermute | solution.py:339
  23.6 3.9 %collective-permute-start.8 = (bf16[32,32,128]{2,1,0:T(8,128)(2,1)S(1)}, bf16[32,32,128]{2,1,0:T(8,128)(2,1)S(1)}, u32[]{:S(2)}, u32[]{:S(2)}) collective-permute-start(bf16[32,32,128]{2,1,0:T(8,128)(2,1)S(1)} %get-tuple-element.24), channel_id=1, source_target_pairs={{1,0},{5,1},{3,2},{7,3},{0,4},{4,5},{2,6},{6,7},{9,8},{13,9},{11,1... | collective-permute-start | bytes 786440 | tf_op jit(solution)/shard_map/ppermute | solution.py:339
  27.5 6.0 %collective-permute-done.5.right_ref = bf16[32,32,128]{2,1,0:T(8,128)(2,1)S(1)} collective-permute-done((bf16[32,32,128]{2,1,0:T(8,128)(2,1)S(1)}, bf16[32,32,128]{2,1,0:T(8,128)(2,1)S(1)}, u32[]{:S(2)}, u32[]{:S(2)}) %collective-permute-start.5) | collective-permute-done | bytes 262176 | tf_op jit(solution)/shard_map/ppermute | solution.py:339
  33.5 0.2 collective-permute-start.6
  33.7 0.2 gate.1.refs_2_.gate_ref
  34.0 1.3 %triangle.3.far_ref = f32[1024,128]{1,0:T(8,128)S(1)} custom-call(bf16[32,32,128]{2,1,0:T(8,128)(2,1)S(1)} %collective-permute-done.5.right_ref, f32[2,1024,128]{2,1,0:T(8,128)S(1)} %panel.1.panel_ref), custom_call_target="tpu_custom_call" | custom-call | bytes 1310720 | tf_op jit(solution)/shard_map/triangle/pallas_call | solution.py:349
  35.3 1.3 %triangle.4.refs_0_ = f32[1024,128]{1,0:T(8,128)S(1)} custom-call(bf16[32,32,128]{2,1,0:T(8,128)(2,1)S(1)} %collective-permute-done.9.right_ref, f32[2,1024,128]{2,1,0:T(8,128)S(1)} %panel.1.panel_ref), custom_call_target="tpu_custom_call" | custom-call | bytes 1310720 | tf_op jit(solution)/shard_map/triangle/pallas_call | solution.py:349
  36.6 2.9 %collective-permute-done.8.right_ref = bf16[32,32,128]{2,1,0:T(8,128)(2,1)S(1)} collective-permute-done((bf16[32,32,128]{2,1,0:T(8,128)(2,1)S(1)}, bf16[32,32,128]{2,1,0:T(8,128)(2,1)S(1)}, u32[]{:S(2)}, u32[]{:S(2)}) %collective-permute-start.8) | collective-permute-done | bytes 262176 | tf_op jit(solution)/shard_map/ppermute | solution.py:339
  39.5 1.3 %triangle.5.near_ref = f32[1024,128]{1,0:T(8,128)S(1)} custom-call(bf16[32,32,128]{2,1,0:T(8,128)(2,1)S(1)} %collective-permute-done.8.right_ref, f32[2,1024,128]{2,1,0:T(8,128)S(1)} %panel.1.panel_ref, f32[1024,128]{1,0:T(8,128)S(1)} %triangle.4.refs_0_), custom_call_target="tpu_custom_call" | custom-call | bytes 1835008 | tf_op jit(solution)/shard_map/triangle/pallas_call | solution.py:349
  40.8 1.4 %collective-permute-done.6.right_ref = bf16[32,32,128]{2,1,0:T(8,128)(2,1)S(1)} collective-permute-done((bf16[32,32,128]{2,1,0:T(8,128)(2,1)S(1)}, bf16[32,32,128]{2,1,0:T(8,128)(2,1)S(1)}, u32[]{:S(2)}, u32[]{:S(2)}) %collective-permute-start.6) | collective-permute-done | bytes 262176 | tf_op jit(solution)/shard_map/ppermute | solution.py:343
  42.2 1.0 %last.3 = (f32[768,128]{1,0:T(8,128)S(1)}, bf16[768,128]{1,0:T(8,128)(2,1)S(1)}) custom-call(bf16[32,32,128]{2,1,0:T(8,128)(2,1)S(1)} %collective-permute-done.6.right_ref, f32[2,1024,128]{2,1,0:T(8,128)S(1)} %panel.1.panel_ref, f32[1024,128]{1,0:T(8,128)S(1)} %triangle.3.far_ref, f32[1024,128]{1,0:T(8,128)S(1)} %triangle.5.near_ref), custom_call_target="tpu_custom_call" | custom-call | flops 268435456 | bytes 2359296 | tf_op jit(solution)/shard_map/last/pallas_call | solution.py:349
  43.2 0.6 %collective-permute-start.11 = (bf16[768,128]{1,0:T(8,128)(2,1)S(1)}, bf16[768,128]{1,0:T(8,128)(2,1)S(1)}, u32[]{:S(2)}, u32[]{:S(2)}) collective-permute-start(bf16[768,128]{1,0:T(8,128)(2,1)S(1)} %get-tuple-element.30), channel_id=1, source_target_pairs={{0,2},{1,3},{2,0},{3,1},{4,6},{5,7},{6,4},{7,5},{8,10},{9,11},{10,... | collective-permute-start | bytes 589832 | tf_op jit(solution)/shard_map/ppermute | solution.py:314
  43.8 0.3 last.2
  44.2 0.7 %collective-permute-done.11.other_ref = bf16[768,128]{1,0:T(8,128)(2,1)S(1)} collective-permute-done((bf16[768,128]{1,0:T(8,128)(2,1)S(1)}, bf16[768,128]{1,0:T(8,128)(2,1)S(1)}, u32[]{:S(2)}, u32[]{:S(2)}) %collective-permute-start.11) | collective-permute-done | bytes 196640 | tf_op jit(solution)/shard_map/ppermute | solution.py:314
  44.9 0.4 final.2.refs_0_
  45.3 0.2 collective-permute-done.10.other_ref
  45.5 1.0 %final.3 = bf16[32,32,128]{2,1,0:T(8,128)(2,1)} custom-call(f32[256,128]{1,0:T(8,128)S(1)} %get-tuple-element.26.own_ref, bf16[256,128]{1,0:T(8,128)(2,1)S(1)} %collective-permute-done.10.other_ref, bf16[32,32,128]{2,1,0:T(8,128)(2,1)S(1)} %get-tuple-element.28.updated_ref, f32[1024,128]{1,0:T(8,128)S(1)} %gate.1.refs_2_.gate_ref, f32[1,128]{1,0:T(1,128)S(1)} %bitcast.12, ...), custom_call_target="tpu_custom_call" | custom-call | flops 268435456 | bytes 1213952 | tf_op jit(solution)/shard_map/final/pallas_call | solution.py:349
  (48 shorter events, 0.4 us)
Async XLA Ops:
  0.0 1.5 %copy-start.5 = (s32[128]{0:T(128)S(1)}, s32[128]{0:T(128)}, u32[]{:S(2)}) copy-start(s32[128]{0:T(128)} %param.22) | copy-start | bytes 1540
  0.0 1.1 %copy-start.8 = (bf16[32,32,256]{2,1,0:T(8,128)(2,1)S(1)}, bf16[32,32,256]{2,1,0:T(8,128)(2,1)}, u32[]{:S(2)}) copy-start(bf16[32,32,256]{2,1,0:T(8,128)(2,1)} %x_ref.1) | copy-start | bytes 1572868
  1.1 0.8 %copy-start.11 = (bf16[256,64]{0,1:T(8,128)(2,1)S(1)}, bf16[256,64]{0,1:T(8,128)(2,1)}, u32[]{:S(2)}) copy-start(bf16[256,64]{0,1:T(8,128)(2,1)} %param.26) | copy-start | bytes 98308
  1.1 0.8 %copy-start.13 = (s32[32,32]{1,0:T(8,128)S(1)}, s32[32,32]{1,0:T(8,128)}, u32[]{:S(2)}) copy-start(s32[32,32]{1,0:T(8,128)} %mask_ref.1) | copy-start | bytes 12292
  1.1 0.8 %copy-start.14 = (f32[256]{0:T(256)S(1)}, f32[256]{0:T(256)}, u32[]{:S(2)}) copy-start(f32[256]{0:T(256)} %param.24) | copy-start | bytes 3076
  1.1 0.8 %copy-start.15 = (f32[256]{0:T(256)S(1)}, f32[256]{0:T(256)}, u32[]{:S(2)}) copy-start(f32[256]{0:T(256)} %param.25) | copy-start | bytes 3076
  1.1 0.8 %copy-start.16 = (f32[64]{0:T(128)S(1)}, f32[64]{0:T(128)}, u32[]{:S(2)}) copy-start(f32[64]{0:T(128)} %param.27) | copy-start | bytes 772
  1.1 4.2 %copy-start.18 = (f32[640]{0:T(1024)S(1)}, f32[640]{0:T(1024)}, u32[]{:S(2)}) copy-start(f32[640]{0:T(1024)} %param.33) | copy-start | bytes 7684
  2.5 2.8 %collective-permute-start = (bf16[32,1152]{1,0:T(8,128)(2,1)S(1)}, bf16[32,1152]{1,0:T(8,128)(2,1)S(1)}, u32[]{:S(2)}, u32[]{:S(2)}) collective-permute-start(bf16[32,1152]{1,0:T(8,128)(2,1)S(1)} %get-tuple-element.18.refs_0_), channel_id=1, source_target_pairs={{0,2},{1,3},{2,0},{3,1},{4,6},{5,7},{6,4},{7,5},{8,10},{9,11},{10,... | collective-permute-start | bytes 221192 | tf_op jit(solution)/shard_map/ppermute | solution.py:314
  2.6 8.3 %collective-permute-start.3 = (bf16[32,1152]{1,0:T(8,128)(2,1)S(1)}, bf16[32,1152]{1,0:T(8,128)(2,1)S(1)}, u32[]{:S(2)}, u32[]{:S(2)}) collective-permute-start(bf16[32,1152]{1,0:T(8,128)(2,1)S(1)} %get-tuple-element.21.refs_0_), channel_id=1, source_target_pairs={{0,1},{1,0},{2,3},{3,2},{4,5},{5,4},{6,7},{7,6},{8,9},{9,8},{10,11... | collective-permute-start | bytes 221192 | tf_op jit(solution)/shard_map/ppermute | solution.py:319
  5.3 5.7 %copy-start.9 = (bf16[32,32,128]{2,1,0:T(8,128)(2,1)S(1)}, bf16[32,32,128]{2,1,0:T(8,128)(2,1)}, u32[]{:S(2)}) copy-start(bf16[32,32,128]{2,1,0:T(8,128)(2,1)} %pair_ref.1) | copy-start | bytes 786436
  5.3 5.7 %copy-start.10 = (bf16[1024,128]{1,0:T(8,128)(2,1)S(1)}, bf16[1024,128]{1,0:T(8,128)(2,1)}, u32[]{:S(2)}) copy-start(bf16[1024,128]{1,0:T(8,128)(2,1)} %w_ref.6) | copy-start | bytes 786436
  5.3 5.7 %copy-start.12 = (bf16[66,128]{1,0:T(8,128)(2,1)S(1)}, bf16[66,128]{1,0:T(8,128)(2,1)}, u32[]{:S(2)}) copy-start(bf16[66,128]{1,0:T(8,128)(2,1)} %table_ref.1) | copy-start | bytes 50692
  5.4 5.7 %copy-start.17 = (s32[128]{0:T(128)S(1)}, s32[128]{0:T(128)}, u32[]{:S(2)}) copy-start(s32[128]{0:T(128)} %param.23) | copy-start | bytes 1540
  5.4 7.6 %collective-permute-start.2 = (bf16[2,32,1152]{2,1,0:T(8,128)(2,1)S(1)}, bf16[2,32,1152]{2,1,0:T(8,128)(2,1)S(1)}, u32[]{:S(2)}, u32[]{:S(2)}) collective-permute-start(bf16[2,32,1152]{2,1,0:T(8,128)(2,1)S(1)} %join.2._), channel_id=1, source_target_pairs={{0,4},{1,0},{2,12},{3,8},{4,5},{5,1},{6,13},{7,9},{8,6},{9,2},{10,... | collective-permute-start | bytes 442376 | tf_op jit(solution)/shard_map/ppermute | solution.py:325
  9.0 8.9 %collective-permute-start.1 = (bf16[2,32,1152]{2,1,0:T(8,128)(2,1)S(1)}, bf16[2,32,1152]{2,1,0:T(8,128)(2,1)S(1)}, u32[]{:S(2)}, u32[]{:S(2)}) collective-permute-start(bf16[2,32,1152]{2,1,0:T(8,128)(2,1)S(1)} %join.2._), channel_id=1, source_target_pairs={{0,0},{1,4},{2,8},{3,12},{4,1},{5,5},{6,9},{7,13},{8,2},{9,6},{10,... | collective-permute-start | bytes 442376 | tf_op jit(solution)/shard_map/ppermute | solution.py:325
  10.9 7.2 %collective-permute-start.4 = (bf16[2,32,1152]{2,1,0:T(8,128)(2,1)S(1)}, bf16[2,32,1152]{2,1,0:T(8,128)(2,1)S(1)}, u32[]{:S(2)}, u32[]{:S(2)}) collective-permute-start(bf16[2,32,1152]{2,1,0:T(8,128)(2,1)S(1)} %join.3.own_ref), channel_id=1, source_target_pairs={{0,2},{1,3},{2,0},{3,1},{4,6},{5,7},{6,4},{7,5},{8,10},{9,11},{10,... | collective-permute-start | bytes 442376 | tf_op jit(solution)/shard_map/ppermute | solution.py:314
  11.9 6.2 %copy-start = (bf16[128,640]{1,0:T(8,128)(2,1)S(1)}, bf16[128,640]{1,0:T(8,128)(2,1)}, u32[]{:S(2)}) copy-start(bf16[128,640]{1,0:T(8,128)(2,1)} %w_ref.9) | copy-start | bytes 491524
  11.9 6.2 %copy-start.6 = (f32[128]{0:T(128)S(1)}, f32[128]{0:T(128)}, u32[]{:S(2)}) copy-start(f32[128]{0:T(128)} %param.30) | copy-start | bytes 1540
  11.9 6.2 %copy-start.7 = (f32[128]{0:T(128)S(1)}, f32[128]{0:T(128)}, u32[]{:S(2)}) copy-start(f32[128]{0:T(128)} %param.31) | copy-start | bytes 1540
  20.7 12.8 %collective-permute-start.5 = (bf16[32,32,128]{2,1,0:T(8,128)(2,1)S(1)}, bf16[32,32,128]{2,1,0:T(8,128)(2,1)S(1)}, u32[]{:S(2)}, u32[]{:S(2)}) collective-permute-start(bf16[32,32,128]{2,1,0:T(8,128)(2,1)S(1)} %get-tuple-element.24), channel_id=1, source_target_pairs={{8,0},{13,1},{11,2},{14,3},{9,4},{12,5},{10,6},{15,7},{0,8},{5,9},... | collective-permute-start | bytes 786440 | tf_op jit(solution)/shard_map/ppermute | solution.py:339
  22.8 11.1 %collective-permute-start.7 = (bf16[32,32,128]{2,1,0:T(8,128)(2,1)S(1)}, bf16[32,32,128]{2,1,0:T(8,128)(2,1)S(1)}, u32[]{:S(2)}, u32[]{:S(2)}) collective-permute-start(bf16[32,32,128]{2,1,0:T(8,128)(2,1)S(1)} %left.1.refs_0_), channel_id=1, source_target_pairs={{0,1},{1,0},{2,3},{3,2},{4,5},{5,4},{6,7},{7,6},{8,9},{9,8},{10,11... | collective-permute-start | bytes 786440 | tf_op jit(solution)/shard_map/ppermute | solution.py:319
  22.9 12.4 %collective-permute-start.9 = (bf16[32,32,128]{2,1,0:T(8,128)(2,1)S(1)}, bf16[32,32,128]{2,1,0:T(8,128)(2,1)S(1)}, u32[]{:S(2)}, u32[]{:S(2)}) collective-permute-start(bf16[32,32,128]{2,1,0:T(8,128)(2,1)S(1)} %get-tuple-element.24), channel_id=1, source_target_pairs={{0,0},{4,1},{2,2},{6,3},{1,4},{5,5},{3,6},{7,7},{8,8},{12,9},{10,1... | collective-permute-start | bytes 786440 | tf_op jit(solution)/shard_map/ppermute | solution.py:339
  23.6 15.9 %collective-permute-start.8 = (bf16[32,32,128]{2,1,0:T(8,128)(2,1)S(1)}, bf16[32,32,128]{2,1,0:T(8,128)(2,1)S(1)}, u32[]{:S(2)}, u32[]{:S(2)}) collective-permute-start(bf16[32,32,128]{2,1,0:T(8,128)(2,1)S(1)} %get-tuple-element.24), channel_id=1, source_target_pairs={{1,0},{5,1},{3,2},{7,3},{0,4},{4,5},{2,6},{6,7},{9,8},{13,9},{11,1... | collective-permute-start | bytes 786440 | tf_op jit(solution)/shard_map/ppermute | solution.py:339
  33.5 8.7 %collective-permute-start.6 = (bf16[32,32,128]{2,1,0:T(8,128)(2,1)S(1)}, bf16[32,32,128]{2,1,0:T(8,128)(2,1)S(1)}, u32[]{:S(2)}, u32[]{:S(2)}) collective-permute-start(bf16[32,32,128]{2,1,0:T(8,128)(2,1)S(1)} %collective-permute-done.5.right_ref), channel_id=1, source_target_pairs={{0,4},{4,0},{8,12},{12,8},{1,5},{5,1},{9,13},{13,9},{2,6},{6,2},{1... | collective-permute-start | bytes 786440 | tf_op jit(solution)/shard_map/ppermute | solution.py:343
  35.3 9.6 %copy-start.1 = (bf16[128,128]{1,0:T(8,128)(2,1)S(1)}, bf16[128,128]{1,0:T(8,128)(2,1)}, u32[]{:S(2)}) copy-start(bf16[128,128]{1,0:T(8,128)(2,1)} %w_ref.11) | copy-start | bytes 98308
  35.3 9.6 %copy-start.2 = (f32[128]{0:T(128)S(1)}, f32[128]{0:T(128)}, u32[]{:S(2)}) copy-start(f32[128]{0:T(128)} %param.34) | copy-start | bytes 1540
  35.3 9.6 %copy-start.3 = (f32[128]{0:T(128)S(1)}, f32[128]{0:T(128)}, u32[]{:S(2)}) copy-start(f32[128]{0:T(128)} %param.35) | copy-start | bytes 1540
  35.3 9.6 %copy-start.4 = (f32[128]{0:T(128)S(1)}, f32[128]{0:T(128)}, u32[]{:S(2)}) copy-start(f32[128]{0:T(128)} %param.37) | copy-start | bytes 1540
  43.2 1.7 %collective-permute-start.11 = (bf16[768,128]{1,0:T(8,128)(2,1)S(1)}, bf16[768,128]{1,0:T(8,128)(2,1)S(1)}, u32[]{:S(2)}, u32[]{:S(2)}) collective-permute-start(bf16[768,128]{1,0:T(8,128)(2,1)S(1)} %get-tuple-element.30), channel_id=1, source_target_pairs={{0,2},{1,3},{2,0},{3,1},{4,6},{5,7},{6,4},{7,5},{8,10},{9,11},{10,... | collective-permute-start | bytes 589832 | tf_op jit(solution)/shard_map/ppermute | solution.py:314
  44.1 1.3 %collective-permute-start.10 = (bf16[256,128]{1,0:T(8,128)(2,1)S(1)}, bf16[256,128]{1,0:T(8,128)(2,1)S(1)}, u32[]{:S(2)}, u32[]{:S(2)}) collective-permute-start(bf16[256,128]{1,0:T(8,128)(2,1)S(1)} %get-tuple-element.27), channel_id=1, source_target_pairs={{0,2},{1,3},{2,0},{3,1},{4,6},{5,7},{6,4},{7,5},{8,10},{9,11},{10,... | collective-permute-start | bytes 196616 | tf_op jit(solution)/shard_map/ppermute | solution.py:314
